TPU v7x, 32 devices: a whole 2x2x4 slice. The times are simulated.
32 devices in a mesh: replica: 4 (over y, core), section: 2 (over x), tensor: 4 (over z).
Axes of the slice: x: 2, y: 2, z: 4, core: 2. Of those that a mesh axis runs over, the one named last changes fastest.
Arguments:
- inputs: bfloat16 [4, 4, 128, 12288], P('replica', None, 'tensor'), may hold values from -0.375 to 0.375
- cotangent: bfloat16 [4, 4, 128, 12288], P('replica', None, 'tensor'), may hold values from -36 to 36
- micro_counts: int32 [4], replicated, may hold values from 1 to 4
- bounds: int32 [4, 3], replicated, may hold values from 0 to 2, as said below
- holder_down: bfloat16 [4, 2, 2, 64, 12288], P('replica', 'section'), may hold values from -0.25 to 0.25, as said below
- holder_up: bfloat16 [4, 2, 2, 64, 12288], P('replica', 'section'), may hold values from -0.25 to 0.25, as said below
- master_down: float32 [2, 64, 12288], P('section', None, ('replica', 'tensor')), may hold values from -0.25 to 0.25
- master_up: float32 [2, 64, 12288], P('section', None, ('replica', 'tensor')), may hold values from -0.25 to 0.25
- moment_down: float32 [2, 64, 12288], P('section', None, ('replica', 'tensor')), may hold values from -4 to 4
- moment_up: float32 [2, 64, 12288], P('section', None, ('replica', 'tensor')), may hold values from -4 to 4
- second_down: float32 [2, 64, 12288], P('section', None, ('replica', 'tensor')), may hold values from 0.01 to 1
- second_up: float32 [2, 64, 12288], P('section', None, ('replica', 'tensor')), may hold values from 0.01 to 1
Outputs:
- new_holder_down: bfloat16 [4, 2, 2, 64, 12288], P('replica', 'section')
- new_holder_up: bfloat16 [4, 2, 2, 64, 12288], P('replica', 'section')
- new_master_down: float32 [2, 64, 12288], P('section', None, ('replica', 'tensor'))
- new_master_up: float32 [2, 64, 12288], P('section', None, ('replica', 'tensor'))
- new_moment_down: float32 [2, 64, 12288], P('section', None, ('replica', 'tensor'))
- new_moment_up: float32 [2, 64, 12288], P('section', None, ('replica', 'tensor'))
- new_second_down: float32 [2, 64, 12288], P('section', None, ('replica', 'tensor'))
- new_second_up: float32 [2, 64, 12288], P('section', None, ('replica', 'tensor'))
Inputs may be any that keep to these rules, and one draw needn't show every extreme that they name: `bounds`: each row starts at 0, never falls and ends at 2; the sections that hold layers come first, 1 to 2 of them and at least one, and their layer counts differ by at most one; a layer l held by section s satisfies s <= l <= s + 1; a section holds at most 2 layers, and some section of replica 0 holds exactly 2. `holder_down`: each used slot holds master_down's layer that lives there by bounds, rounded to bfloat16; unused slots are zeros. `holder_up`: each used slot holds master_up's layer that lives there by bounds, rounded to bfloat16; unused slots are zeros.
All inputs are finite; a program needn't handle non-finite values.
Results may differ from a plain program's by a relative error of at most 0.006.
Values may be sent and summed in bfloat16 or wider, within the bound.
No kernel may reach another device: no remote copies, remote signals or barrier semaphores. Data moves between devices by JAX's collectives and lax.ppermute only.
A program may use at most 192 MiB of HBM per device.

v0:
```python
import functools
import math

import jax
import jax.numpy as jnp
from jax import lax
from jax.experimental import pallas as pl
from jax.experimental.pallas import tpu as pltpu
from jax.sharding import PartitionSpec as P

norm_eps = 1e-06
learn_rate = 0.01
beta_one = 0.9
beta_two = 0.95
decay_rate = 0.1
adam_eps = 1e-08
first_fix = 0.9999734386011124
second_fix = 0.9940794707796659

f32 = jnp.float32
bf16 = jnp.bfloat16
exact = lax.Precision.HIGHEST
in_smem = pl.BlockSpec(memory_space=pltpu.SMEM)
in_vmem = pl.BlockSpec(memory_space=pltpu.VMEM)
anywhere = pl.BlockSpec(memory_space=pl.ANY)


def held_layers(bounds):
    at_row = lax.axis_index("replica")
    at_column = lax.axis_index("section")
    return bounds[at_row, at_column], bounds[at_row, at_column + 1]


def counted_rows(counts, tokens, per_micro):
    rows = lax.broadcasted_iota(jnp.int32, (tokens, 1), 0)
    return rows < counts[lax.axis_index("replica")] * per_micro


def dot_last(x, y, precision=None):
    return lax.dot_general(
        x, y, (((1,), (1,)), ((), ())), preferred_element_type=f32, precision=precision
    )


def dot_first(x, y, precision=None):
    return lax.dot_general(
        x, y, (((0,), (0,)), ((), ())), preferred_element_type=f32, precision=precision
    )


def row_sum(x):
    return jnp.sum(x, axis=-1, keepdims=True)


def project_kernel(layers, per_micro, bounds, counts, h_ref, g_ref, down_ref, up_ref, out_ref, sq_ref, acc_h, acc_g):
    step = pl.program_id(0)
    slots, ranks, width = down_ref.shape

    @pl.when(step == 0)
    def _():
        acc_h[...] = jnp.zeros_like(acc_h)
        acc_g[...] = jnp.zeros_like(acc_g)
        sq_ref[...] = jnp.zeros_like(sq_ref)

    h = h_ref[...]
    ups = up_ref[...].reshape(slots * ranks, width)
    both = jnp.concatenate([down_ref[...].reshape(slots * ranks, width), ups], axis=0)
    acc_h[...] += dot_last(h, both)
    acc_g[...] += dot_last(g_ref[...], ups)
    wide = h.astype(f32)
    sq_ref[...] += row_sum(wide * wide)

    @pl.when(step == pl.num_programs(0) - 1)
    def _():
        first, after = held_layers(bounds)
        ph = acc_h[...]
        pg = jnp.where(counted_rows(counts, h_ref.shape[0], per_micro), acc_g[...], 0.0)
        pieces = []
        for slot in range(slots):
            lo, hi = slot * ranks, (slot + 1) * ranks
            pieces.append(
                jnp.concatenate(
                    [ph[:, lo:hi], ph[:, slots * ranks + lo : slots * ranks + hi], pg[:, lo:hi]],
                    axis=1,
                )
            )
        for layer in range(layers):
            total = jnp.zeros_like(pieces[0])
            for slot in range(slots):
                here = (first + slot == layer) & (layer < after)
                total = jnp.where(here, pieces[slot], total)
            out_ref[:, layer * 3 * ranks : (layer + 1) * 3 * ranks] = total


def project(bounds, counts, hidden, cot, downs, ups, layers, per_micro):
    tokens, features = hidden.shape
    slots, ranks, _ = downs.shape
    width = features // 8
    kernel = functools.partial(project_kernel, layers, per_micro)
    return pl.pallas_call(
        kernel,
        grid_spec=pltpu.PrefetchScalarGridSpec(
            num_scalar_prefetch=2,
            grid=(features // width,),
            in_specs=[
                pl.BlockSpec((tokens, width), lambda i, *_: (0, i)),
                pl.BlockSpec((tokens, width), lambda i, *_: (0, i)),
                pl.BlockSpec((slots, ranks, width), lambda i, *_: (0, 0, i)),
                pl.BlockSpec((slots, ranks, width), lambda i, *_: (0, 0, i)),
            ],
            out_specs=[
                pl.BlockSpec((tokens, layers * 3 * ranks), lambda i, *_: (0, 0)),
                pl.BlockSpec((tokens, 128), lambda i, *_: (0, 0)),
            ],
            scratch_shapes=[
                pltpu.VMEM((tokens, 2 * slots * ranks), f32),
                pltpu.VMEM((tokens, slots * ranks), f32),
            ],
        ),
        out_shape=[
            jax.ShapeDtypeStruct((tokens, layers * 3 * ranks), f32),
            jax.ShapeDtypeStruct((tokens, 128), f32),
        ],
        cost_estimate=pl.CostEstimate(
            flops=6 * tokens * slots * ranks * features,
            bytes_accessed=4 * (tokens + slots * ranks) * features,
            transcendentals=0,
        ),
        name="project",
    )(bounds, counts, hidden, cot, downs, ups)


def gram_kernel(sections, *refs):
    around = refs[:sections]
    gram_ref, right_ref = refs[sections:]
    section_at = lax.axis_index("section")
    ranks = around[0].shape[0] // 2
    layers = []
    for layer in range(sections):
        distance = lax.rem(layer - section_at + sections, sections)
        chosen = around[0][...]
        for step in range(1, sections):
            chosen = jnp.where(distance == step, around[step][...], chosen)
        layers.append(chosen)
    lefts = [chosen[ranks:] for chosen in layers[:-1]]
    right = jnp.concatenate([chosen[:ranks] for chosen in layers[1:]] + lefts, axis=0)
    right_ref[...] = right
    gram_ref[...] = dot_last(jnp.concatenate(lefts, axis=0), right)


def gram(around):
    sections = len(around)
    ranks = around[0].shape[0] // 2
    columns = around[0].shape[1]
    before = (sections - 1) * ranks
    return pl.pallas_call(
        functools.partial(gram_kernel, sections),
        in_specs=[in_vmem] * sections,
        out_specs=[in_vmem] * 2,
        out_shape=[
            jax.ShapeDtypeStruct((before, 2 * before), f32),
            jax.ShapeDtypeStruct((2 * before, columns), bf16),
        ],
        name="gram",
    )(*around)


def chain_kernel(sections, parts, features, per_micro, counts, *refs):
    projections = refs[:sections]
    sq_ref = refs[sections]
    grams = refs[sections + 1 : sections + 1 + parts]
    down_ref, up_ref, mixed_ref = refs[sections + 1 + parts :]
    layers = sections
    section_at = lax.axis_index("section")
    tokens = sq_ref.shape[0]
    total = projections[0][...]
    for other in projections[1:]:
        total = total + other[...]
    table = grams[0][...]
    for other in grams[1:]:
        table = table + other[...]
    ranks = total.shape[1] // (3 * layers)
    scale_d = 1.0 / math.sqrt(features)
    scale_r = 1.0 / math.sqrt(ranks)

    def part(layer, which):
        at_column = (3 * layer + which) * ranks
        return total[:, at_column : at_column + ranks]

    def up_down(i, layer):
        return table[i * ranks : (i + 1) * ranks, (layer - 1) * ranks : layer * ranks]

    def up_up(i, j):
        at_column = (layers - 1 + j) * ranks
        return table[i * ranks : (i + 1) * ranks, at_column : at_column + ranks]

    def times(x, y):
        return jnp.dot(x, y, preferred_element_type=f32, precision=exact)

    square = sq_ref[:, 0:1]
    inverses, inners, actives, sigmoids = [], [], [], []
    on_up = [[part(l, 1) for l in range(layers - 1)]]
    for layer in range(layers):
        inverse = lax.rsqrt(jnp.maximum(square, 0.0) * (1.0 / features) + norm_eps)
        on_down = part(layer, 0)
        for i in range(layer):
            on_down = on_down + scale_r * times(actives[i], up_down(i, layer))
        inner = on_down * (inverse * scale_d)
        sigmoid = jax.nn.sigmoid(inner)
        active = (inner * sigmoid).astype(bf16).astype(f32)
        inverses.append(inverse)
        inners.append(inner)
        sigmoids.append(sigmoid)
        actives.append(active)
        if layer < layers - 1:
            now = on_up[-1]
            grown = [now[l] + scale_r * times(active, up_up(layer, l)) for l in range(layers - 1)]
            square = square + scale_r * row_sum(active * (now[layer] + grown[layer]))
            on_up.append(grown)
    scaled = [None] * layers
    kappas = [None] * layers
    for layer in reversed(range(layers)):
        incoming = part(layer, 2)
        for k in range(layer + 1, layers):
            incoming = incoming + scale_d * dot_last(scaled[k], up_down(layer, k), exact)
            incoming = incoming - kappas[k] * on_up[k][layer]
        sigmoid, inner = sigmoids[layer], inners[layer]
        slope = sigmoid * (1.0 + inner * (1.0 - sigmoid))
        error = incoming * scale_r * slope
        scaled[layer] = error * inverses[layer]
        kappas[layer] = (
            inverses[layer] * inverses[layer] * (row_sum(error * inner) * (1.0 / features))
        )

    def owned(values):
        chosen = values[0]
        for layer in range(1, layers):
            chosen = jnp.where(section_at == layer, values[layer], chosen)
        return chosen

    own_error = owned(scaled)
    own_active = owned(actives)
    counted = counted_rows(counts, tokens, per_micro)
    later = jnp.zeros_like(square)
    for k in range(1, layers):
        later = later + jnp.where(k > section_at, kappas[k], 0.0)
    down_ref[...] = (own_error * scale_d).T.astype(bf16)
    on_hidden = -scale_r * later * own_active
    on_cot = jnp.where(counted, own_active * scale_r, 0.0)
    up_ref[...] = jnp.concatenate([on_hidden.T, on_cot.T], axis=1).astype(bf16)
    both = scale_d * scale_r
    for k in range(1, layers):
        cut = slice((k - 1) * ranks, k * ranks)
        across = dot_first(own_active, scaled[k], exact) * both
        mixed_ref[:ranks, cut] = jnp.zeros_like(across)
        mixed_ref[ranks:, cut] = jnp.where(k > section_at, across, 0.0)
    for i in range(layers - 1):
        cut = slice((layers - 1 + i) * ranks, (layers + i) * ranks)
        after = jnp.zeros_like(square)
        for k in range(i + 1, layers):
            after = after + jnp.where(k > section_at, kappas[k], 0.0)
        across = dot_first(own_error, actives[i], exact) * both
        mixed_ref[:ranks, cut] = jnp.where(i < section_at, across, 0.0)
        across = dot_first(own_active, after * actives[i], exact)
        mixed_ref[ranks:, cut] = across * (-scale_r * scale_r)


def chain(counts, projections, square, grams, features, per_micro):
    sections = len(projections)
    tokens, wide = projections[0].shape
    ranks = wide // (3 * sections)
    inputs = [*projections, square, *grams]
    kernel = functools.partial(chain_kernel, sections, len(grams), features, per_micro)
    return pl.pallas_call(
        kernel,
        in_specs=[in_smem] + [in_vmem] * len(inputs),
        out_specs=[in_vmem] * 3,
        out_shape=[
            jax.ShapeDtypeStruct((ranks, tokens), bf16),
            jax.ShapeDtypeStruct((ranks, 2 * tokens), bf16),
            jax.ShapeDtypeStruct((2 * ranks, 2 * (sections - 1) * ranks), f32),
        ],
        name="chain",
    )(counts, *inputs)


def gradient_kernel(tensors, factor_ref, *refs):
    tokens, out_ref = refs[:-1], refs[-1]
    columns = tokens[0].shape[1] // tensors
    tensor_at = lax.axis_index("tensor")
    for owner in range(tensors):
        cut = pl.ds(owner * columns, columns)
        stacked = jnp.concatenate([ref[:, cut] for ref in tokens], axis=0)
        block = jnp.dot(factor_ref[...], stacked, preferred_element_type=f32)
        out_ref[0, tensor_at ^ owner] = block.astype(bf16)


def gradient(factors, sources, first, replicas, tensors):
    tokens, features = sources[0].shape
    width = features // replicas
    rows, depth = factors.shape

    def chosen(i):
        return (0, lax.axis_index("replica") ^ (first + 2 * i))

    return pl.pallas_call(
        functools.partial(gradient_kernel, tensors),
        grid=(replicas // 2,),
        in_specs=[pl.BlockSpec(factors.shape, lambda i: (0, 0))]
        + [pl.BlockSpec((tokens, width), chosen)] * len(sources),
        out_specs=pl.BlockSpec((1, tensors, rows, width // tensors), lambda i: (i, 0, 0, 0)),
        out_shape=jax.ShapeDtypeStruct((replicas // 2, tensors, rows, width // tensors), bf16),
        cost_estimate=pl.CostEstimate(
            flops=rows * depth * features,
            bytes_accessed=(depth + rows) * features,
            transcendentals=0,
        ),
        name="gradient",
    )(factors, *sources)


def update_kernel(count, *refs):
    pieces = refs[:count]
    mixes = refs[count : -8]
    right_ref, master_ref, moment_ref, second_ref = refs[-8:-4]
    new_master, new_moment, new_second, share_ref = refs[-4:]
    mixed = mixes[0][...]
    for other in mixes[1:]:
        mixed = mixed + other[...]
    grad = jnp.dot(mixed, right_ref[...].astype(f32), preferred_element_type=f32, precision=exact)
    for piece in pieces:
        grad = grad + piece[...].reshape(grad.shape).astype(f32)
    moment = beta_one * moment_ref[0] + (1.0 - beta_one) * grad
    second = beta_two * second_ref[0] + (1.0 - beta_two) * grad * grad
    master = master_ref[0]
    master = master - learn_rate * (
        moment / first_fix / (jnp.sqrt(second / second_fix) + adam_eps) + decay_rate * master
    )
    new_master[0] = master
    new_moment[0] = moment
    new_second[0] = second
    share_ref[...] = master.astype(bf16)


def update(pieces, mixes, which, right, state):
    _, ranks, columns = state[0].shape
    width = columns // 2

    def leading(piece):
        lead = piece.ndim - 2
        return pl.BlockSpec((1,) * lead + (ranks, width), lambda i: (0,) * lead + (0, i))

    own = pl.BlockSpec((1, ranks, width), lambda i: (0, 0, i))
    return pl.pallas_call(
        functools.partial(update_kernel, len(pieces)),
        grid=(columns // width,),
        in_specs=[leading(piece) for piece in pieces]
        + [pl.BlockSpec((ranks, mixed.shape[1]), lambda i: (which, 0)) for mixed in mixes]
        + [pl.BlockSpec((right.shape[0], width), lambda i: (0, i))]
        + [own] * 3,
        out_specs=[own] * 3 + [pl.BlockSpec((ranks, width), lambda i: (0, i))],
        out_shape=[jax.ShapeDtypeStruct(state[0].shape, f32)] * 3
        + [jax.ShapeDtypeStruct((ranks, columns), bf16)],
        name="update",
    )(*pieces, *mixes, right, *state)


def place_kernel(orders, bounds, *refs):
    groups = len(orders)
    window = (refs[:groups], refs[groups : 2 * groups])
    out_ref, zeros, sem = refs[2 * groups :]
    slots = out_ref.shape[0]
    tensors, _, columns = window[0][0].shape
    first, after = held_layers(bounds)
    replica_at = lax.axis_index("replica")
    section_at = lax.axis_index("section")
    tensor_at = lax.axis_index("tensor")
    zeros[...] = jnp.zeros_like(zeros)

    def move(slot, distance, go):
        for group, order in enumerate(orders):
            for hop in range(tensors):
                owner = (replica_at ^ order) * tensors + (tensor_at ^ hop)
                cut = pl.ds(pl.multiple_of(owner * columns, columns), columns)
                source = zeros if distance is None else window[distance][group].at[hop]
                go(pltpu.make_async_copy(source, out_ref.at[slot, :, cut], sem))

    for act in (lambda copy: copy.start(), lambda copy: copy.wait()):
        for slot in range(slots):
            layer = first + slot
            present = layer < after
            for distance in range(2):

                @pl.when(present & (layer - section_at == distance))
                def _():
                    move(slot, distance, act)

            @pl.when(jnp.logical_not(present))
            def _():
                move(slot, None, act)


def place(bounds, own, following, orders, slots, features):
    _, ranks, columns = own[0].shape
    return pl.pallas_call(
        functools.partial(place_kernel, orders),
        in_specs=[in_smem] + [anywhere] * (len(own) + len(following)),
        out_specs=anywhere,
        out_shape=jax.ShapeDtypeStruct((slots, ranks, features), bf16),
        scratch_shapes=[pltpu.VMEM((ranks, columns), bf16), pltpu.SemaphoreType.DMA],
        name="place",
    )(bounds, *own, *following)


def swapped(block, axis, distance):
    route = [(i, i ^ distance) for i in range(lax.axis_size(axis))]
    return lax.ppermute(block, axis, route)


def swaps(block, axis):
    return [swapped(block, axis, k) for k in range(1, lax.axis_size(axis))]


def from_next(block, distance=1):
    size = lax.axis_size("section")
    route = [((i + distance) % size, i) for i in range(size)]
    return lax.ppermute(block, "section", route)


def following_layer(block):
    size = lax.axis_size("section")
    return lax.ppermute(block, "section", [(i + 1, i) for i in range(size - 1)])


def summed(*blocks):
    total = blocks[0].astype(f32)
    for block in blocks[1:]:
        total = total + block.astype(f32)
    return total.astype(bf16)


def reduced(factors, sources, replicas, tensors):
    sent = gradient(factors, sources, 1, replicas, tensors)
    near = swapped(sent, "replica", 1)
    kept = gradient(factors, sources, 0, replicas, tensors)
    across = swapped(summed(kept[1], near[1]), "replica", 2)
    along = [
        swapped(summed(kept[0, k], near[0, k], across[k]), "tensor", k) for k in range(1, tensors)
    ]
    return [kept, near, across, *along]


def gathered(share):
    own_line = jnp.stack([share] + swaps(share, "tensor"))
    half = own_line.shape[0] // 2
    next_line = following_layer(own_line)
    own_far = swapped(own_line, "replica", 2)
    next_far = jnp.concatenate(
        [following_layer(own_far[:half]), swapped(next_line[half:], "replica", 2)], axis=0
    )
    return [
        [own_line, own_far, swapped(own_line, "replica", 1), swapped(own_far, "replica", 1)],
        [next_line, next_far, swapped(next_line, "replica", 1), swapped(next_far, "replica", 1)],
    ]


def on_device(
    inputs,
    cotangent,
    micro_counts,
    bounds,
    holder_down,
    holder_up,
    master_down,
    master_up,
    moment_down,
    moment_up,
    second_down,
    second_up,
):
    sections = lax.axis_size("section")
    replicas = lax.axis_size("replica")
    tensors = lax.axis_size("tensor")
    assert replicas == 4 and tensors == 4
    _, micros, per_micro, features = inputs.shape
    slots = holder_down.shape[2]
    hidden = inputs.reshape(micros * per_micro, features)
    cot = cotangent.reshape(micros * per_micro, features)

    owned = jnp.concatenate([master_down[0], master_up[0]], axis=0).astype(bf16)
    around = [owned] + [from_next(owned, d) for d in range(1, sections)]
    table, right = gram(around)
    table = table + sum(swaps(table, "replica"))
    tables = [table] + swaps(table, "tensor")

    projected, square = project(
        bounds, micro_counts, hidden, cot, holder_down[0, 0], holder_up[0, 0], sections, per_micro
    )
    projections = [projected] + [from_next(projected, d) for d in range(1, sections)]
    factors_down, factors_up, mixed = chain(
        micro_counts, projections, square, tables, features, per_micro
    )

    pieces_down = reduced(factors_down, [hidden], replicas, tensors)
    pieces_up = reduced(factors_up, [hidden, cot], replicas, tensors)
    mixed = mixed + sum(swaps(mixed, "replica"))
    mixes = [mixed] + swaps(mixed, "tensor")
    down = update(pieces_down, mixes, 0, right, [master_down, moment_down, second_down])
    up = update(pieces_up, mixes, 1, right, [master_up, moment_up, second_up])
    new_down, new_up = (
        place(bounds, *gathered(made[3]), (0, 2, 1, 3), slots, features)[None, None]
        for made in (down, up)
    )
    return (new_down, new_up, down[0], up[0], down[1], up[1], down[2], up[2])


def solution(mesh):
    held = P("replica", "section", None, None, None)
    owned = P("section", None, ("replica", "tensor"))
    tokens = P("replica", None, "tensor", None)
    return jax.shard_map(
        on_device,
        mesh=mesh,
        in_specs=(tokens, tokens, P(), P(), held, held) + (owned,) * 6,
        out_specs=(held, held) + (owned,) * 6,
        check_vma=False,
    )
```

profile of v0, /device:TPU:0, one launch (start us, length us, event | category | flops | bytes accessed | tf_op | source)
XLA Modules:
  0.0 339.9 jit_solution(17206037532796024999)
XLA Ops:
  0.6 1.0 convert_bitcast_fusion
  1.7 3.0 collective-permute-start.1
  4.7 4.9 %collective-permute-done.1.refs_1_ = bf16[128,768]{1,0:T(8,128)(2,1)S(1)} collective-permute-done((bf16[128,768]{1,0:T(8,128)(2,1)S(1)}, bf16[128,768]{1,0:T(8,128)(2,1)S(1)}, u32[]{:S(2)}, u32[]{:S(2)}) %collective-permute-start.1) | collective-permute-done | bytes 196640 | tf_op jit(solution)/shard_map/ppermute | solution.py:427
  10.3 1.8 gram.1
  12.5 1.5 collective-permute-start.3
  14.1 10.2 %project.1 = (f32[128,384]{1,0:T(8,128)}, f32[128,128]{1,0:T(8,128)}) custom-call(s32[4,3]{1,0:T(4,128)} %bounds.5, s32[4]{0:T(128)} %counts.3, bf16[128,12288]{1,0:T(8,128)(2,1)} %bitcast.64, bf16[128,12288]{1,0:T(8,128)(2,1)} %bitcast.69, bf16[2,64,12288]{2,1,0:T(8,128)(2,1)} %bitcast.74, bf16[2,64,12288]{2,1,0:T(8,128)(2,1)} %bitcast.75), custom_call_target="tpu_custom_call" | custom-call | flops 1207959552 | bytes 12582912 | tf_op jit(solution)/shard_map/project/pallas_call | solution.py:100
  24.2 1.7 collective-permute-start
  26.0 3.7 %collective-permute-start.7 = (f32[64,128]{1,0:T(8,128)S(1)}, f32[64,128]{1,0:T(8,128)S(1)}, u32[]{:S(2)}, u32[]{:S(2)}) collective-permute-start(f32[64,128]{1,0:T(8,128)S(1)} %add_add_fusion.1.refs_3_), channel_id=1, source_target_pairs={{0,3},{1,2},{2,1},{3,0},{4,7},{5,6},{6,5},{7,4},{8,11},{9,10},{10,... | collective-permute-start | bytes 98312 | tf_op jit(solution)/shard_map/ppermute | solution.py:417
  30.4 1.2 collective-permute-done.refs_1_
  31.8 2.7 collective-permute-done.6.refs_5_
  35.1 3.3 chain.1
  38.4 3.0 gradient.7
  41.4 2.5 gradient.5
  44.4 1.2 collective-permute-start.15
  46.2 2.4 gradient.4.refs_0_
  48.7 3.1 gradient.6.refs_0_
  51.8 1.4 fusion.1
  53.1 1.6 collective-permute-start.31
  55.4 1.5 collective-permute-start.18
  57.6 7.5 %collective-permute-done.31.refs_2_ = bf16[4,64,768]{2,1,0:T(8,128)(2,1)S(1)} collective-permute-done((bf16[4,64,768]{2,1,0:T(8,128)(2,1)S(1)}, bf16[4,64,768]{2,1,0:T(8,128)(2,1)S(1)}, u32[]{:S(2)}, u32[]{:S(2)}) %collective-permute-start.31) | collective-permute-done | bytes 393248 | tf_op jit(solution)/shard_map/ppermute | solution.py:417
  65.1 1.2 fusion.2
  66.4 1.5 collective-permute-start.34
  68.5 4.5 %collective-permute-done.9.refs_2_ = bf16[4,64,768]{2,1,0:T(8,128)(2,1)S(1)} collective-permute-done((bf16[4,64,768]{2,1,0:T(8,128)(2,1)S(1)}, bf16[4,64,768]{2,1,0:T(8,128)(2,1)S(1)}, u32[]{:S(2)}, u32[]{:S(2)}) %collective-permute-start.9) | collective-permute-done | bytes 393248 | tf_op jit(solution)/shard_map/ppermute | solution.py:417
  73.8 3.4 %collective-permute-start.12 = (bf16[64,768]{1,0:T(8,128)(2,1)}, bf16[64,768]{1,0:T(8,128)(2,1)S(1)}, u32[]{:S(2)}, u32[]{:S(2)}) collective-permute-start(bf16[64,768]{1,0:T(8,128)(2,1)} %get-tuple-element.41), channel_id=1, source_target_pairs={{0,3},{1,2},{2,1},{3,0},{4,7},{5,6},{6,5},{7,4},{8,11},{9,10},{10,... | collective-permute-start | bytes 294920 | tf_op jit(solution)/shard_map/ppermute | solution.py:417
  77.3 5.0 %collective-permute-done.16.refs_7_ = f32[128,128]{1,0:T(8,128)S(1)} collective-permute-done((f32[128,128]{1,0:T(8,128)S(1)}, f32[128,128]{1,0:T(8,128)S(1)}, u32[]{:S(2)}, u32[]{:S(2)}) %collective-permute-start.16) | collective-permute-done | bytes 65568 | tf_op jit(solution)/shard_map/ppermute | solution.py:417
  83.1 2.0 collective-permute-start.10
  85.7 2.7 update.3
  88.5 1.7 collective-permute-start.37
  90.2 2.8 collective-permute-start.35
  94.2 2.7 update.2
  97.0 1.7 collective-permute-start.21
  98.6 2.8 collective-permute-start.19
  101.7 1.6 collective-permute-start.38
  103.8 3.1 collective-permute-done.20
  106.9 0.9 pad_maximum_fusion.refs_0_
  107.9 1.6 collective-permute-start.22
  109.5 1.3 collective-permute-start.41
  110.7 1.3 collective-permute-start.25
  112.1 1.3 collective-permute-start.42
  113.4 4.6 %collective-permute-done.22.refs_1_ = bf16[4,64,768]{2,1,0:T(8,128)(2,1)S(1)} collective-permute-done((bf16[4,64,768]{2,1,0:T(8,128)(2,1)S(1)}, bf16[4,64,768]{2,1,0:T(8,128)(2,1)S(1)}, u32[]{:S(2)}, u32[]{:S(2)}) %collective-permute-start.22) | collective-permute-done | bytes 393248 | tf_op jit(solution)/shard_map/ppermute | solution.py:417
  118.0 1.3 collective-permute-start.26
  119.4 4.0 %collective-permute-done.41.refs_4_ = bf16[4,64,768]{2,1,0:T(8,128)(2,1)S(1)} collective-permute-done((bf16[4,64,768]{2,1,0:T(8,128)(2,1)S(1)}, bf16[4,64,768]{2,1,0:T(8,128)(2,1)S(1)}, u32[]{:S(2)}, u32[]{:S(2)}) %collective-permute-start.41) | collective-permute-done | bytes 393248 | tf_op jit(solution)/shard_map/ppermute | solution.py:432
  124.0 7.8 %collective-permute-done.25.refs_4_ = bf16[4,64,768]{2,1,0:T(8,128)(2,1)S(1)} collective-permute-done((bf16[4,64,768]{2,1,0:T(8,128)(2,1)S(1)}, bf16[4,64,768]{2,1,0:T(8,128)(2,1)S(1)}, u32[]{:S(2)}, u32[]{:S(2)}) %collective-permute-start.25) | collective-permute-done | bytes 393248 | tf_op jit(solution)/shard_map/ppermute | solution.py:432
  131.8 3.8 %collective-permute-done.42 = bf16[2,64,768]{2,1,0:T(8,128)(2,1)S(1)} collective-permute-done((bf16[2,64,768]{2,1,0:T(8,128)(2,1)S(1)}, bf16[2,64,768]{2,1,0:T(8,128)(2,1)S(1)}, u32[]{:S(2)}, u32[]{:S(2)}) %collective-permute-start.42) | collective-permute-done | bytes 196640 | tf_op jit(solution)/shard_map/ppermute | solution.py:432
  135.6 2.1 collective-permute-done.26
  138.3 5.0 %collective-permute-done.27 = bf16[2,64,768]{2,1,0:T(8,128)(2,1)S(1)} collective-permute-done((bf16[2,64,768]{2,1,0:T(8,128)(2,1)S(1)}, bf16[2,64,768]{2,1,0:T(8,128)(2,1)S(1)}, u32[]{:S(2)}, u32[]{:S(2)}) %collective-permute-start.27) | collective-permute-done | bytes 196640 | tf_op jit(solution)/shard_map/ppermute | solution.py:417
  145.6 97.1 %place.3 = bf16[2,64,12288]{2,1,0:T(8,128)(2,1)} custom-call(s32[4,3]{1,0:T(4,128)} %bounds.5, bf16[4,64,768]{2,1,0:T(8,128)(2,1)} %copy-done.4, bf16[4,64,768]{2,1,0:T(8,128)(2,1)} %copy-done.8, bf16[4,64,768]{2,1,0:T(8,128)(2,1)} %copy-done.15, bf16[4,64,768]{2,1,0:T(8,128)(2,1)} %copy-done.17, bf16[4,64,768]{2,1,0:T(8,128)(2,1)} %copy-done.10, ...), custom_call_target="tpu_custom_call" | custom-call | tf_op jit(solution)/shard_map/place/pallas_call | solution.py:405
  242.8 97.1 %place.2 = bf16[2,64,12288]{2,1,0:T(8,128)(2,1)} custom-call(s32[4,3]{1,0:T(4,128)} %bounds.5, bf16[4,64,768]{2,1,0:T(8,128)(2,1)} %copy-done.3, bf16[4,64,768]{2,1,0:T(8,128)(2,1)} %copy-done.7, bf16[4,64,768]{2,1,0:T(8,128)(2,1)} %collective-permute-done.23.refs_2_, bf16[4,64,768]{2,1,0:T(8,128)(2,1)} %collective-permute-done.24.refs_3_, ...), custom_call_target="tpu_custom_call" | custom-call | tf_op jit(solution)/shard_map/place/pallas_call | solution.py:405
  (143 shorter events, 13.6 us)
Async XLA Ops:
  1.7 7.9 %collective-permute-start.1 = (bf16[128,768]{1,0:T(8,128)(2,1)S(1)}, bf16[128,768]{1,0:T(8,128)(2,1)S(1)}, u32[]{:S(2)}, u32[]{:S(2)}) collective-permute-start(bf16[128,768]{1,0:T(8,128)(2,1)S(1)} %pad_maximum_fusion.2.refs_0_), channel_id=1, source_target_pairs={{4,0},{0,4},{5,1},{1,5},{6,2},{2,6},{7,3},{3,7},{12,8},{8,12},{13,... | collective-permute-start | bytes 589832 | tf_op jit(solution)/shard_map/ppermute | solution.py:427
  12.1 13.8 %collective-permute-start.4 = (f32[64,128]{1,0:T(8,128)}, f32[64,128]{1,0:T(8,128)S(1)}, u32[]{:S(2)}, u32[]{:S(2)}) collective-permute-start(f32[64,128]{1,0:T(8,128)} %get-tuple-element.25), channel_id=1, source_target_pairs={{0,24},{8,16},{16,8},{24,0},{1,25},{9,17},{17,9},{25,1},{2,26},{10... | collective-permute-start | bytes 98312 | tf_op jit(solution)/shard_map/ppermute | solution.py:417
  12.5 13.4 %collective-permute-start.3 = (f32[64,128]{1,0:T(8,128)}, f32[64,128]{1,0:T(8,128)S(1)}, u32[]{:S(2)}, u32[]{:S(2)}) collective-permute-start(f32[64,128]{1,0:T(8,128)} %get-tuple-element.25), channel_id=1, source_target_pairs={{0,16},{8,24},{16,0},{24,8},{1,17},{9,25},{17,1},{25,9},{2,18},{10... | collective-permute-start | bytes 98312 | tf_op jit(solution)/shard_map/ppermute | solution.py:417
  14.0 12.0 %collective-permute-start.2 = (f32[64,128]{1,0:T(8,128)}, f32[64,128]{1,0:T(8,128)S(1)}, u32[]{:S(2)}, u32[]{:S(2)}) collective-permute-start(f32[64,128]{1,0:T(8,128)} %get-tuple-element.25), channel_id=1, source_target_pairs={{0,8},{8,0},{16,24},{24,16},{1,9},{9,1},{17,25},{25,17},{2,10},{10... | collective-permute-start | bytes 98312 | tf_op jit(solution)/shard_map/ppermute | solution.py:417
  24.2 7.5 %collective-permute-start = (f32[128,384]{1,0:T(8,128)}, f32[128,384]{1,0:T(8,128)S(1)}, u32[]{:S(2)}, u32[]{:S(2)}) collective-permute-start(f32[128,384]{1,0:T(8,128)} %get-tuple-element.23.refs_0_), channel_id=1, source_target_pairs={{4,0},{0,4},{5,1},{1,5},{6,2},{2,6},{7,3},{3,7},{12,8},{8,12},{13,... | collective-permute-start | bytes 589832 | tf_op jit(solution)/shard_map/ppermute | solution.py:427
  26.0 5.8 %collective-permute-start.7 = (f32[64,128]{1,0:T(8,128)S(1)}, f32[64,128]{1,0:T(8,128)S(1)}, u32[]{:S(2)}, u32[]{:S(2)}) collective-permute-start(f32[64,128]{1,0:T(8,128)S(1)} %add_add_fusion.1.refs_3_), channel_id=1, source_target_pairs={{0,3},{1,2},{2,1},{3,0},{4,7},{5,6},{6,5},{7,4},{8,11},{9,10},{10,... | collective-permute-start | bytes 98312 | tf_op jit(solution)/shard_map/ppermute | solution.py:417
  29.6 4.8 %collective-permute-start.6 = (f32[64,128]{1,0:T(8,128)S(1)}, f32[64,128]{1,0:T(8,128)S(1)}, u32[]{:S(2)}, u32[]{:S(2)}) collective-permute-start(f32[64,128]{1,0:T(8,128)S(1)} %add_add_fusion.1.refs_3_), channel_id=1, source_target_pairs={{0,2},{1,3},{2,0},{3,1},{4,6},{5,7},{6,4},{7,5},{8,10},{9,11},{10,... | collective-permute-start | bytes 98312 | tf_op jit(solution)/shard_map/ppermute | solution.py:417
  29.6 4.8 %collective-permute-start.5 = (f32[64,128]{1,0:T(8,128)S(1)}, f32[64,128]{1,0:T(8,128)S(1)}, u32[]{:S(2)}, u32[]{:S(2)}) collective-permute-start(f32[64,128]{1,0:T(8,128)S(1)} %add_add_fusion.1.refs_3_), channel_id=1, source_target_pairs={{0,1},{1,0},{2,3},{3,2},{4,5},{5,4},{6,7},{7,6},{8,9},{9,8},{10,11... | collective-permute-start | bytes 98312 | tf_op jit(solution)/shard_map/ppermute | solution.py:417
  41.4 10.4 %collective-permute-start.30 = (bf16[2,4,64,768]{3,2,1,0:T(8,128)(2,1)}, bf16[2,4,64,768]{3,2,1,0:T(8,128)(2,1)S(1)}, u32[]{:S(2)}, u32[]{:S(2)}) collective-permute-start(bf16[2,4,64,768]{3,2,1,0:T(8,128)(2,1)} %gradient.7), channel_id=1, source_target_pairs={{0,8},{8,0},{16,24},{24,16},{1,9},{9,1},{17,25},{25,17},{2,10},{10... | collective-permute-start | bytes 2359304 | tf_op jit(solution)/shard_map/ppermute | solution.py:417
  43.9 10.8 %collective-permute-start.8 = (bf16[2,4,64,768]{3,2,1,0:T(8,128)(2,1)}, bf16[2,4,64,768]{3,2,1,0:T(8,128)(2,1)S(1)}, u32[]{:S(2)}, u32[]{:S(2)}) collective-permute-start(bf16[2,4,64,768]{3,2,1,0:T(8,128)(2,1)} %gradient.5), channel_id=1, source_target_pairs={{0,8},{8,0},{16,24},{24,16},{1,9},{9,1},{17,25},{25,17},{2,10},{10... | collective-permute-start | bytes 2359304 | tf_op jit(solution)/shard_map/ppermute | solution.py:417
  44.4 11.0 %collective-permute-start.15 = (f32[128,128]{1,0:T(8,128)S(1)}, f32[128,128]{1,0:T(8,128)S(1)}, u32[]{:S(2)}, u32[]{:S(2)}) collective-permute-start(f32[128,128]{1,0:T(8,128)S(1)} %copy-done.30), channel_id=1, source_target_pairs={{0,24},{8,16},{16,8},{24,0},{1,25},{9,17},{17,9},{25,1},{2,26},{10... | collective-permute-start | bytes 196616 | tf_op jit(solution)/shard_map/ppermute | solution.py:417
  45.5 9.9 %collective-permute-start.14 = (f32[128,128]{1,0:T(8,128)S(1)}, f32[128,128]{1,0:T(8,128)S(1)}, u32[]{:S(2)}, u32[]{:S(2)}) collective-permute-start(f32[128,128]{1,0:T(8,128)S(1)} %copy-done.30), channel_id=1, source_target_pairs={{0,16},{8,24},{16,0},{24,8},{1,17},{9,25},{17,1},{25,9},{2,18},{10... | collective-permute-start | bytes 196616 | tf_op jit(solution)/shard_map/ppermute | solution.py:417
  46.0 9.4 %collective-permute-start.13 = (f32[128,128]{1,0:T(8,128)S(1)}, f32[128,128]{1,0:T(8,128)S(1)}, u32[]{:S(2)}, u32[]{:S(2)}) collective-permute-start(f32[128,128]{1,0:T(8,128)S(1)} %copy-done.30), channel_id=1, source_target_pairs={{0,8},{8,0},{16,24},{24,16},{1,9},{9,1},{17,25},{25,17},{2,10},{10... | collective-permute-start | bytes 196616 | tf_op jit(solution)/shard_map/ppermute | solution.py:417
  53.1 12.0 %collective-permute-start.31 = (bf16[4,64,768]{2,1,0:T(8,128)(2,1)S(1)}, bf16[4,64,768]{2,1,0:T(8,128)(2,1)S(1)}, u32[]{:S(2)}, u32[]{:S(2)}) collective-permute-start(bf16[4,64,768]{2,1,0:T(8,128)(2,1)S(1)} %fusion.1), channel_id=1, source_target_pairs={{0,16},{8,24},{16,0},{24,8},{1,17},{9,25},{17,1},{25,9},{2,18},{10... | collective-permute-start | bytes 1179656 | tf_op jit(solution)/shard_map/ppermute | solution.py:417
  54.8 18.2 %collective-permute-start.9 = (bf16[4,64,768]{2,1,0:T(8,128)(2,1)S(1)}, bf16[4,64,768]{2,1,0:T(8,128)(2,1)S(1)}, u32[]{:S(2)}, u32[]{:S(2)}) collective-permute-start(bf16[4,64,768]{2,1,0:T(8,128)(2,1)S(1)} %fusion), channel_id=1, source_target_pairs={{0,16},{8,24},{16,0},{24,8},{1,17},{9,25},{17,1},{25,9},{2,18},{10... | collective-permute-start | bytes 1179656 | tf_op jit(solution)/shard_map/ppermute | solution.py:417
  55.4 18.4 %collective-permute-start.18 = (f32[128,128]{1,0:T(8,128)S(1)}, f32[128,128]{1,0:T(8,128)S(1)}, u32[]{:S(2)}, u32[]{:S(2)}) collective-permute-start(f32[128,128]{1,0:T(8,128)S(1)} %add_add_fusion.refs_6_), channel_id=1, source_target_pairs={{0,3},{1,2},{2,1},{3,0},{4,7},{5,6},{6,5},{7,4},{8,11},{9,10},{10,... | collective-permute-start | bytes 196616 | tf_op jit(solution)/shard_map/ppermute | solution.py:417
  57.0 20.3 %collective-permute-start.17 = (f32[128,128]{1,0:T(8,128)S(1)}, f32[128,128]{1,0:T(8,128)S(1)}, u32[]{:S(2)}, u32[]{:S(2)}) collective-permute-start(f32[128,128]{1,0:T(8,128)S(1)} %add_add_fusion.refs_6_), channel_id=1, source_target_pairs={{0,2},{1,3},{2,0},{3,1},{4,6},{5,7},{6,4},{7,5},{8,10},{9,11},{10,... | collective-permute-start | bytes 196616 | tf_op jit(solution)/shard_map/ppermute | solution.py:417
  66.4 16.7 %collective-permute-start.34 = (bf16[64,768]{1,0:T(8,128)(2,1)S(1)}, bf16[64,768]{1,0:T(8,128)(2,1)S(1)}, u32[]{:S(2)}, u32[]{:S(2)}) collective-permute-start(bf16[64,768]{1,0:T(8,128)(2,1)S(1)} %get-tuple-element.38), channel_id=1, source_target_pairs={{0,3},{1,2},{2,1},{3,0},{4,7},{5,6},{6,5},{7,4},{8,11},{9,10},{10,... | collective-permute-start | bytes 294920 | tf_op jit(solution)/shard_map/ppermute | solution.py:417
  67.9 17.2 %collective-permute-start.33 = (bf16[64,768]{1,0:T(8,128)(2,1)S(1)}, bf16[64,768]{1,0:T(8,128)(2,1)S(1)}, u32[]{:S(2)}, u32[]{:S(2)}) collective-permute-start(bf16[64,768]{1,0:T(8,128)(2,1)S(1)} %get-tuple-element.39), channel_id=1, source_target_pairs={{0,2},{1,3},{2,0},{3,1},{4,6},{5,7},{6,4},{7,5},{8,10},{9,11},{10,... | collective-permute-start | bytes 294920 | tf_op jit(solution)/shard_map/ppermute | solution.py:417
  73.0 12.1 %collective-permute-start.32 = (bf16[64,768]{1,0:T(8,128)(2,1)S(1)}, bf16[64,768]{1,0:T(8,128)(2,1)}, u32[]{:S(2)}, u32[]{:S(2)}) collective-permute-start(bf16[64,768]{1,0:T(8,128)(2,1)S(1)} %get-tuple-element.40), channel_id=1, source_target_pairs={{0,1},{1,0},{2,3},{3,2},{4,5},{5,4},{6,7},{7,6},{8,9},{9,8},{10,11... | collective-permute-start | bytes 294920 | tf_op jit(solution)/shard_map/ppermute | solution.py:417
  73.8 16.3 %collective-permute-start.12 = (bf16[64,768]{1,0:T(8,128)(2,1)}, bf16[64,768]{1,0:T(8,128)(2,1)S(1)}, u32[]{:S(2)}, u32[]{:S(2)}) collective-permute-start(bf16[64,768]{1,0:T(8,128)(2,1)} %get-tuple-element.41), channel_id=1, source_target_pairs={{0,3},{1,2},{2,1},{3,0},{4,7},{5,6},{6,5},{7,4},{8,11},{9,10},{10,... | collective-permute-start | bytes 294920 | tf_op jit(solution)/shard_map/ppermute | solution.py:417
  77.2 5.0 %collective-permute-start.16 = (f32[128,128]{1,0:T(8,128)S(1)}, f32[128,128]{1,0:T(8,128)S(1)}, u32[]{:S(2)}, u32[]{:S(2)}) collective-permute-start(f32[128,128]{1,0:T(8,128)S(1)} %add_add_fusion.refs_6_), channel_id=1, source_target_pairs={{0,1},{1,0},{2,3},{3,2},{4,5},{5,4},{6,7},{7,6},{8,9},{9,8},{10,11... | collective-permute-start | bytes 196616 | tf_op jit(solution)/shard_map/ppermute | solution.py:417
  82.3 10.7 %collective-permute-start.11 = (bf16[64,768]{1,0:T(8,128)(2,1)}, bf16[64,768]{1,0:T(8,128)(2,1)S(1)}, u32[]{:S(2)}, u32[]{:S(2)}) collective-permute-start(bf16[64,768]{1,0:T(8,128)(2,1)} %get-tuple-element.42), channel_id=1, source_target_pairs={{0,2},{1,3},{2,0},{3,1},{4,6},{5,7},{6,4},{7,5},{8,10},{9,11},{10,... | collective-permute-start | bytes 294920 | tf_op jit(solution)/shard_map/ppermute | solution.py:417
  83.1 9.8 %collective-permute-start.10 = (bf16[64,768]{1,0:T(8,128)(2,1)}, bf16[64,768]{1,0:T(8,128)(2,1)S(1)}, u32[]{:S(2)}, u32[]{:S(2)}) collective-permute-start(bf16[64,768]{1,0:T(8,128)(2,1)} %get-tuple-element.43), channel_id=1, source_target_pairs={{0,1},{1,0},{2,3},{3,2},{4,5},{5,4},{6,7},{7,6},{8,9},{9,8},{10,11... | collective-permute-start | bytes 294920 | tf_op jit(solution)/shard_map/ppermute | solution.py:417
  88.5 10.1 %collective-permute-start.37 = (bf16[64,768]{1,0:T(8,128)(2,1)}, bf16[64,768]{1,0:T(8,128)(2,1)S(1)}, u32[]{:S(2)}, u32[]{:S(2)}) collective-permute-start(bf16[64,768]{1,0:T(8,128)(2,1)} %get-tuple-element.31), channel_id=1, source_target_pairs={{0,3},{1,2},{2,1},{3,0},{4,7},{5,6},{6,5},{7,4},{8,11},{9,10},{10,... | collective-permute-start | bytes 294920 | tf_op jit(solution)/shard_map/ppermute | solution.py:417
  90.1 11.5 %collective-permute-start.36 = (bf16[64,768]{1,0:T(8,128)(2,1)}, bf16[64,768]{1,0:T(8,128)(2,1)S(1)}, u32[]{:S(2)}, u32[]{:S(2)}) collective-permute-start(bf16[64,768]{1,0:T(8,128)(2,1)} %get-tuple-element.31), channel_id=1, source_target_pairs={{0,2},{1,3},{2,0},{3,1},{4,6},{5,7},{6,4},{7,5},{8,10},{9,11},{10,... | collective-permute-start | bytes 294920 | tf_op jit(solution)/shard_map/ppermute | solution.py:417
  90.2 11.5 %collective-permute-start.35 = (bf16[64,768]{1,0:T(8,128)(2,1)}, bf16[64,768]{1,0:T(8,128)(2,1)S(1)}, u32[]{:S(2)}, u32[]{:S(2)}) collective-permute-start(bf16[64,768]{1,0:T(8,128)(2,1)} %get-tuple-element.31), channel_id=1, source_target_pairs={{0,1},{1,0},{2,3},{3,2},{4,5},{5,4},{6,7},{7,6},{8,9},{9,8},{10,11... | collective-permute-start | bytes 294920 | tf_op jit(solution)/shard_map/ppermute | solution.py:417
  97.0 6.8 %collective-permute-start.21 = (bf16[64,768]{1,0:T(8,128)(2,1)}, bf16[64,768]{1,0:T(8,128)(2,1)S(1)}, u32[]{:S(2)}, u32[]{:S(2)}) collective-permute-start(bf16[64,768]{1,0:T(8,128)(2,1)} %get-tuple-element.29), channel_id=1, source_target_pairs={{0,3},{1,2},{2,1},{3,0},{4,7},{5,6},{6,5},{7,4},{8,11},{9,10},{10,... | collective-permute-start | bytes 294920 | tf_op jit(solution)/shard_map/ppermute | solution.py:417
  98.6 8.3 %collective-permute-start.20 = (bf16[64,768]{1,0:T(8,128)(2,1)}, bf16[64,768]{1,0:T(8,128)(2,1)S(1)}, u32[]{:S(2)}, u32[]{:S(2)}) collective-permute-start(bf16[64,768]{1,0:T(8,128)(2,1)} %get-tuple-element.29), channel_id=1, source_target_pairs={{0,2},{1,3},{2,0},{3,1},{4,6},{5,7},{6,4},{7,5},{8,10},{9,11},{10,... | collective-permute-start | bytes 294920 | tf_op jit(solution)/shard_map/ppermute | solution.py:417
  98.6 8.3 %collective-permute-start.19 = (bf16[64,768]{1,0:T(8,128)(2,1)}, bf16[64,768]{1,0:T(8,128)(2,1)S(1)}, u32[]{:S(2)}, u32[]{:S(2)}) collective-permute-start(bf16[64,768]{1,0:T(8,128)(2,1)} %get-tuple-element.29), channel_id=1, source_target_pairs={{0,1},{1,0},{2,3},{3,2},{4,5},{5,4},{6,7},{7,6},{8,9},{9,8},{10,11... | collective-permute-start | bytes 294920 | tf_op jit(solution)/shard_map/ppermute | solution.py:417
  101.7 10.3 %collective-permute-start.38 = (bf16[4,64,768]{2,1,0:T(8,128)(2,1)S(1)}, bf16[4,64,768]{2,1,0:T(8,128)(2,1)S(1)}, u32[]{:S(2)}, u32[]{:S(2)}) collective-permute-start(bf16[4,64,768]{2,1,0:T(8,128)(2,1)S(1)} %pad_maximum_fusion.1.refs_0_), channel_id=1, source_target_pairs={{0,16},{8,24},{16,0},{24,8},{1,17},{9,25},{17,1},{25,9},{2,18},{10... | collective-permute-start | bytes 1179656 | tf_op jit(solution)/shard_map/ppermute | solution.py:417
  107.9 134.8 %copy-start.3 = (bf16[4,64,768]{2,1,0:T(8,128)(2,1)}, bf16[4,64,768]{2,1,0:T(8,128)(2,1)S(1)}, u32[]{:S(2)}) copy-start(bf16[4,64,768]{2,1,0:T(8,128)(2,1)S(1)} %pad_maximum_fusion.refs_0_) | copy-start | bytes 1179652
  107.9 10.1 %collective-permute-start.22 = (bf16[4,64,768]{2,1,0:T(8,128)(2,1)S(1)}, bf16[4,64,768]{2,1,0:T(8,128)(2,1)S(1)}, u32[]{:S(2)}, u32[]{:S(2)}) collective-permute-start(bf16[4,64,768]{2,1,0:T(8,128)(2,1)S(1)} %pad_maximum_fusion.refs_0_), channel_id=1, source_target_pairs={{0,16},{8,24},{16,0},{24,8},{1,17},{9,25},{17,1},{25,9},{2,18},{10... | collective-permute-start | bytes 1179656 | tf_op jit(solution)/shard_map/ppermute | solution.py:417
  109.5 13.9 %collective-permute-start.41 = (bf16[4,64,768]{2,1,0:T(8,128)(2,1)S(1)}, bf16[4,64,768]{2,1,0:T(8,128)(2,1)S(1)}, u32[]{:S(2)}, u32[]{:S(2)}) collective-permute-start(bf16[4,64,768]{2,1,0:T(8,128)(2,1)S(1)} %pad_maximum_fusion.1.refs_0_), channel_id=1, source_target_pairs={{4,0},{5,1},{6,2},{7,3},{12,8},{13,9},{14,10},{15,11},{20,16},{21,... | collective-permute-start | bytes 1179656 | tf_op jit(solution)/shard_map/ppermute | solution.py:432
  110.7 21.1 %collective-permute-start.25 = (bf16[4,64,768]{2,1,0:T(8,128)(2,1)S(1)}, bf16[4,64,768]{2,1,0:T(8,128)(2,1)S(1)}, u32[]{:S(2)}, u32[]{:S(2)}) collective-permute-start(bf16[4,64,768]{2,1,0:T(8,128)(2,1)S(1)} %pad_maximum_fusion.refs_0_), channel_id=1, source_target_pairs={{4,0},{5,1},{6,2},{7,3},{12,8},{13,9},{14,10},{15,11},{20,16},{21,... | collective-permute-start | bytes 1179656 | tf_op jit(solution)/shard_map/ppermute | solution.py:432
  112.1 23.5 %collective-permute-start.42 = (bf16[2,64,768]{2,1,0:T(8,128)(2,1)S(1)}, bf16[2,64,768]{2,1,0:T(8,128)(2,1)S(1)}, u32[]{:S(2)}, u32[]{:S(2)}) collective-permute-start(bf16[2,64,768]{2,1,0:T(8,128)(2,1)S(1)} %slice.128), channel_id=1, source_target_pairs={{4,0},{5,1},{6,2},{7,3},{12,8},{13,9},{14,10},{15,11},{20,16},{21,... | collective-permute-start | bytes 589832 | tf_op jit(solution)/shard_map/ppermute | solution.py:432
  118.0 124.7 %copy-start.7 = (bf16[4,64,768]{2,1,0:T(8,128)(2,1)}, bf16[4,64,768]{2,1,0:T(8,128)(2,1)S(1)}, u32[]{:S(2)}) copy-start(bf16[4,64,768]{2,1,0:T(8,128)(2,1)S(1)} %collective-permute-done.22.refs_1_) | copy-start | bytes 1179652
  118.0 19.7 %collective-permute-start.26 = (bf16[2,64,768]{2,1,0:T(8,128)(2,1)S(1)}, bf16[2,64,768]{2,1,0:T(8,128)(2,1)S(1)}, u32[]{:S(2)}, u32[]{:S(2)}) collective-permute-start(bf16[2,64,768]{2,1,0:T(8,128)(2,1)S(1)} %slice.115), channel_id=1, source_target_pairs={{4,0},{5,1},{6,2},{7,3},{12,8},{13,9},{14,10},{15,11},{20,16},{21,... | collective-permute-start | bytes 589832 | tf_op jit(solution)/shard_map/ppermute | solution.py:432
  119.3 24.1 %collective-permute-start.39 = (bf16[4,64,768]{2,1,0:T(8,128)(2,1)S(1)}, bf16[4,64,768]{2,1,0:T(8,128)(2,1)S(1)}, u32[]{:S(2)}, u32[]{:S(2)}) collective-permute-start(bf16[4,64,768]{2,1,0:T(8,128)(2,1)S(1)} %pad_maximum_fusion.1.refs_0_), channel_id=1, source_target_pairs={{0,8},{8,0},{16,24},{24,16},{1,9},{9,1},{17,25},{25,17},{2,10},{10... | collective-permute-start | bytes 1179656 | tf_op jit(solution)/shard_map/ppermute | solution.py:417
  123.4 14.8 %collective-permute-start.43 = (bf16[2,64,768]{2,1,0:T(8,128)(2,1)S(1)}, bf16[2,64,768]{2,1,0:T(8,128)(2,1)S(1)}, u32[]{:S(2)}, u32[]{:S(2)}) collective-permute-start(bf16[2,64,768]{2,1,0:T(8,128)(2,1)S(1)} %slice.129), channel_id=1, source_target_pairs={{0,16},{8,24},{16,0},{24,8},{1,17},{9,25},{17,1},{25,9},{2,18},{10... | collective-permute-start | bytes 589832 | tf_op jit(solution)/shard_map/ppermute | solution.py:417
  131.8 12.2 %collective-permute-start.44 = (bf16[4,64,768]{2,1,0:T(8,128)(2,1)S(1)}, bf16[4,64,768]{2,1,0:T(8,128)(2,1)S(1)}, u32[]{:S(2)}, u32[]{:S(2)}) collective-permute-start(bf16[4,64,768]{2,1,0:T(8,128)(2,1)S(1)} %collective-permute-done.41.refs_4_), channel_id=1, source_target_pairs={{0,8},{8,0},{16,24},{24,16},{1,9},{9,1},{17,25},{25,17},{2,10},{10... | collective-permute-start | bytes 1179656 | tf_op jit(solution)/shard_map/ppermute | solution.py:417
  135.6 8.5 %collective-permute-start.40 = (bf16[4,64,768]{2,1,0:T(8,128)(2,1)S(1)}, bf16[4,64,768]{2,1,0:T(8,128)(2,1)S(1)}, u32[]{:S(2)}, u32[]{:S(2)}) collective-permute-start(bf16[4,64,768]{2,1,0:T(8,128)(2,1)S(1)} %collective-permute-done.38.refs_1_), channel_id=1, source_target_pairs={{0,8},{8,0},{16,24},{24,16},{1,9},{9,1},{17,25},{25,17},{2,10},{10... | collective-permute-start | bytes 1179656 | tf_op jit(solution)/shard_map/ppermute | solution.py:417
  137.7 5.7 %collective-permute-start.27 = (bf16[2,64,768]{2,1,0:T(8,128)(2,1)S(1)}, bf16[2,64,768]{2,1,0:T(8,128)(2,1)S(1)}, u32[]{:S(2)}, u32[]{:S(2)}) collective-permute-start(bf16[2,64,768]{2,1,0:T(8,128)(2,1)S(1)} %slice.116), channel_id=1, source_target_pairs={{0,16},{8,24},{16,0},{24,8},{1,17},{9,25},{17,1},{25,9},{2,18},{10... | collective-permute-start | bytes 589832 | tf_op jit(solution)/shard_map/ppermute | solution.py:417
  138.2 104.5 %collective-permute-start.23 = (bf16[4,64,768]{2,1,0:T(8,128)(2,1)S(1)}, bf16[4,64,768]{2,1,0:T(8,128)(2,1)}, u32[]{:S(2)}, u32[]{:S(2)}) collective-permute-start(bf16[4,64,768]{2,1,0:T(8,128)(2,1)S(1)} %pad_maximum_fusion.refs_0_), channel_id=1, source_target_pairs={{0,8},{8,0},{16,24},{24,16},{1,9},{9,1},{17,25},{25,17},{2,10},{10... | collective-permute-start | bytes 1179656 | tf_op jit(solution)/shard_map/ppermute | solution.py:417
  143.4 2.2 collective-permute-start.45
  143.4 99.3 %collective-permute-start.28 = (bf16[4,64,768]{2,1,0:T(8,128)(2,1)S(1)}, bf16[4,64,768]{2,1,0:T(8,128)(2,1)}, u32[]{:S(2)}, u32[]{:S(2)}) collective-permute-start(bf16[4,64,768]{2,1,0:T(8,128)(2,1)S(1)} %collective-permute-done.25.refs_4_), channel_id=1, source_target_pairs={{0,8},{8,0},{16,24},{24,16},{1,9},{9,1},{17,25},{25,17},{2,10},{10... | collective-permute-start | bytes 1179656 | tf_op jit(solution)/shard_map/ppermute | solution.py:417
  144.0 98.8 %collective-permute-start.24 = (bf16[4,64,768]{2,1,0:T(8,128)(2,1)S(1)}, bf16[4,64,768]{2,1,0:T(8,128)(2,1)}, u32[]{:S(2)}, u32[]{:S(2)}) collective-permute-start(bf16[4,64,768]{2,1,0:T(8,128)(2,1)S(1)} %collective-permute-done.22.refs_1_), channel_id=1, source_target_pairs={{0,8},{8,0},{16,24},{24,16},{1,9},{9,1},{17,25},{25,17},{2,10},{10... | collective-permute-start | bytes 1179656 | tf_op jit(solution)/shard_map/ppermute | solution.py:417
  144.8 98.0 %collective-permute-start.29 = (bf16[4,64,768]{2,1,0:T(8,128)(2,1)S(1)}, bf16[4,64,768]{2,1,0:T(8,128)(2,1)}, u32[]{:S(2)}, u32[]{:S(2)}) collective-permute-start(bf16[4,64,768]{2,1,0:T(8,128)(2,1)S(1)} %constant_dynamic-update-slice_fusion.refs_5_), channel_id=1, source_target_pairs={{0,8},{8,0},{16,24},{24,16},{1,9},{9,1},{17,25},{25,17},{2,10},{10... | collective-permute-start | bytes 1179656 | tf_op jit(solution)/shard_map/ppermute | solution.py:417
  (33 other events, 544.0 us)
where the time goes:
time: 341 us; the launch traced here: 340 us
  Pallas kernels  226 us (66%)
  waiting for transfers between devices  57.2 us (17%)
  starting transfers between devices  45.4 us (13%)
  other arithmetic  5.6 us (2%)
  local copies, waits for them, and re-layouts  4.56 us (1%)
    pallas_call x2, Pallas kernels, place(): pl.pallas_call(functools.partial(place_kernel, orders), in_specs=[in_smem...  194 us
    ppermute x40, starting transfers between devices, swapped(): return lax.ppermute(block, axis, route)  35.5 us
    ppermute x40, waiting for transfers between devices, swapped(): return lax.ppermute(block, axis, route)  33.3 us
    ppermute x4, waiting for transfers between devices, following_layer(): return lax.ppermute(block, 'section', [(i + 1, i) for i in range(size - 1)])  17.7 us
    pallas_call x4, Pallas kernels, gradient(): pl.pallas_call(functools.partial(gradient_kernel, tensors), grid=(replica...  11.1 us
    pallas_call x1, Pallas kernels, project(): pl.pallas_call(kernel, grid_spec=pltpu.PrefetchScalarGridSpec(num_scalar_...  10.2 us
  transfers between devices with their start and end apart: 46, of which 16 were waited for; matrix products, arithmetic and copies ran while one was open for 1% of the time, Pallas kernels for 36%

commit v1 on v0

v1 whole, which is shorter than its diff:
```python
import functools
import math

import jax
import jax.numpy as jnp
from jax import lax
from jax.experimental import pallas as pl
from jax.experimental.pallas import tpu as pltpu
from jax.sharding import PartitionSpec as P

norm_eps = 1e-06
learn_rate = 0.01
beta_one = 0.9
beta_two = 0.95
decay_rate = 0.1
adam_eps = 1e-08
first_fix = 0.9999734386011124
second_fix = 0.9940794707796659

f32 = jnp.float32
bf16 = jnp.bfloat16
exact = lax.Precision.HIGHEST
in_smem = pl.BlockSpec(memory_space=pltpu.SMEM)
in_vmem = pl.BlockSpec(memory_space=pltpu.VMEM)
in_hbm = pl.BlockSpec(memory_space=pltpu.HBM)
limited = pltpu.CompilerParams(vmem_limit_bytes=16 * 1024 * 1024)


def held_layers(bounds):
    at_row = lax.axis_index("replica")
    at_column = lax.axis_index("section")
    return bounds[at_row, at_column], bounds[at_row, at_column + 1]


def counted_rows(counts, tokens, per_micro):
    rows = lax.broadcasted_iota(jnp.int32, (tokens, 1), 0)
    return rows < counts[lax.axis_index("replica")] * per_micro


def dot_last(x, y, precision=None):
    return lax.dot_general(
        x, y, (((1,), (1,)), ((), ())), preferred_element_type=f32, precision=precision
    )


def dot_first(x, y, precision=None):
    return lax.dot_general(
        x, y, (((0,), (0,)), ((), ())), preferred_element_type=f32, precision=precision
    )


def row_sum(x):
    return jnp.sum(x, axis=-1, keepdims=True)


def project_kernel(layers, per_micro, steps, bounds, counts, h_in, g_in, down_in, up_in, *refs):
    out_ref, sq_ref, h_ref, g_ref, weights, sems = refs
    slots, ranks, features = down_in.shape
    tokens = h_ref.shape[0]
    width = features // steps
    copies = []
    for step in range(steps):
        cut = pl.ds(step * width, width)
        moves = [
            (h_in.at[:, cut], h_ref.at[:, cut]),
            (g_in.at[:, cut], g_ref.at[:, cut]),
        ]
        for slot in range(slots):
            for which, source in enumerate((down_in, up_in)):
                rows = pl.ds((which * slots + slot) * ranks, ranks)
                moves.append((source.at[slot, :, cut], weights.at[rows, cut]))
        copies.append(
            [
                pltpu.make_async_copy(source, target, sems.at[step, i])
                for i, (source, target) in enumerate(moves)
            ]
        )
        for copy in copies[-1]:
            copy.start()
    ph = jnp.zeros((tokens, 2 * slots * ranks), f32)
    pg = jnp.zeros((tokens, slots * ranks), f32)
    square = jnp.zeros((tokens, 128), f32)
    for step in range(steps):
        for copy in copies[step]:
            copy.wait()
        cut = pl.ds(step * width, width)
        h = h_ref[:, cut]
        w = weights[:, cut]
        ph = ph + dot_last(h, w)
        pg = pg + dot_last(g_ref[:, cut], w[slots * ranks :])
        wide = h.astype(f32)
        wide = wide * wide
        for lane in range(0, width, 128):
            square = square + wide[:, lane : lane + 128]
    sq_ref[...] = jnp.broadcast_to(row_sum(square), square.shape)
    first, after = held_layers(bounds)
    pg = jnp.where(counted_rows(counts, tokens, per_micro), pg, 0.0)
    pieces = []
    for slot in range(slots):
        lo, hi = slot * ranks, (slot + 1) * ranks
        pieces.append(
            jnp.concatenate(
                [ph[:, lo:hi], ph[:, slots * ranks + lo : slots * ranks + hi], pg[:, lo:hi]],
                axis=1,
            )
        )
    for layer in range(layers):
        total = jnp.zeros_like(pieces[0])
        for slot in range(slots):
            here = (first + slot == layer) & (layer < after)
            total = jnp.where(here, pieces[slot], total)
        out_ref[:, layer * 3 * ranks : (layer + 1) * 3 * ranks] = total


def project(bounds, counts, hidden, cot, downs, ups, layers, per_micro):
    tokens, features = hidden.shape
    slots, ranks, _ = downs.shape
    steps = 8
    kernel = functools.partial(project_kernel, layers, per_micro, steps)
    return pl.pallas_call(
        kernel,
        in_specs=[in_smem] * 2 + [in_hbm] * 4,
        out_specs=[in_vmem] * 4,
        out_shape=[
            jax.ShapeDtypeStruct((tokens, layers * 3 * ranks), f32),
            jax.ShapeDtypeStruct((tokens, 128), f32),
            jax.ShapeDtypeStruct((tokens, features), bf16),
            jax.ShapeDtypeStruct((tokens, features), bf16),
        ],
        scratch_shapes=[
            pltpu.VMEM((2 * slots * ranks, features), bf16),
            pltpu.SemaphoreType.DMA((steps, 2 + 2 * slots)),
        ],
        compiler_params=limited,
        cost_estimate=pl.CostEstimate(
            flops=6 * tokens * slots * ranks * features,
            bytes_accessed=4 * (tokens + slots * ranks) * features,
            transcendentals=0,
        ),
        name="project",
    )(bounds, counts, hidden, cot, downs, ups)


def gram_kernel(sections, *refs):
    around = refs[:sections]
    gram_ref, right_ref = refs[sections:]
    section_at = lax.axis_index("section")
    ranks = around[0].shape[0] // 2
    layers = []
    for layer in range(sections):
        distance = lax.rem(layer - section_at + sections, sections)
        chosen = around[0][...]
        for step in range(1, sections):
            chosen = jnp.where(distance == step, around[step][...], chosen)
        layers.append(chosen)
    lefts = [chosen[ranks:] for chosen in layers[:-1]]
    right = jnp.concatenate([chosen[:ranks] for chosen in layers[1:]] + lefts, axis=0)
    right_ref[...] = right
    gram_ref[...] = dot_last(jnp.concatenate(lefts, axis=0), right)


def gram(around):
    sections = len(around)
    ranks = around[0].shape[0] // 2
    columns = around[0].shape[1]
    before = (sections - 1) * ranks
    return pl.pallas_call(
        functools.partial(gram_kernel, sections),
        in_specs=[in_vmem] * sections,
        out_specs=[in_vmem] * 2,
        out_shape=[
            jax.ShapeDtypeStruct((before, 2 * before), f32),
            jax.ShapeDtypeStruct((2 * before, columns), bf16),
        ],
        compiler_params=limited,
        name="gram",
    )(*around)


def chain_kernel(sections, parts, features, per_micro, counts, *refs):
    projections = refs[:sections]
    sq_ref = refs[sections]
    grams = refs[sections + 1 : sections + 1 + parts]
    factor_ref, mixed_ref = refs[sections + 1 + parts :]
    layers = sections
    section_at = lax.axis_index("section")
    tokens = sq_ref.shape[0]
    total = projections[0][...]
    for other in projections[1:]:
        total = total + other[...]
    table = grams[0][...]
    for other in grams[1:]:
        table = table + other[...]
    ranks = total.shape[1] // (3 * layers)
    scale_d = 1.0 / math.sqrt(features)
    scale_r = 1.0 / math.sqrt(ranks)

    def part(layer, which):
        at_column = (3 * layer + which) * ranks
        return total[:, at_column : at_column + ranks]

    def up_down(i, layer):
        return table[i * ranks : (i + 1) * ranks, (layer - 1) * ranks : layer * ranks]

    def up_up(i, j):
        at_column = (layers - 1 + j) * ranks
        return table[i * ranks : (i + 1) * ranks, at_column : at_column + ranks]

    def times(x, y):
        return jnp.dot(x, y, preferred_element_type=f32, precision=exact)

    square = sq_ref[:, 0:1]
    inverses, inners, actives, sigmoids = [], [], [], []
    on_up = [[part(l, 1) for l in range(layers - 1)]]
    for layer in range(layers):
        inverse = lax.rsqrt(jnp.maximum(square, 0.0) * (1.0 / features) + norm_eps)
        on_down = part(layer, 0)
        for i in range(layer):
            on_down = on_down + scale_r * times(actives[i], up_down(i, layer))
        inner = on_down * (inverse * scale_d)
        sigmoid = jax.nn.sigmoid(inner)
        active = (inner * sigmoid).astype(bf16).astype(f32)
        inverses.append(inverse)
        inners.append(inner)
        sigmoids.append(sigmoid)
        actives.append(active)
        if layer < layers - 1:
            now = on_up[-1]
            grown = [now[l] + scale_r * times(active, up_up(layer, l)) for l in range(layers - 1)]
            square = square + scale_r * row_sum(active * (now[layer] + grown[layer]))
            on_up.append(grown)
    scaled = [None] * layers
    kappas = [None] * layers
    for layer in reversed(range(layers)):
        incoming = part(layer, 2)
        for k in range(layer + 1, layers):
            incoming = incoming + scale_d * dot_last(scaled[k], up_down(layer, k), exact)
            incoming = incoming - kappas[k] * on_up[k][layer]
        sigmoid, inner = sigmoids[layer], inners[layer]
        slope = sigmoid * (1.0 + inner * (1.0 - sigmoid))
        error = incoming * scale_r * slope
        scaled[layer] = error * inverses[layer]
        kappas[layer] = (
            inverses[layer] * inverses[layer] * (row_sum(error * inner) * (1.0 / features))
        )

    def owned(values):
        chosen = values[0]
        for layer in range(1, layers):
            chosen = jnp.where(section_at == layer, values[layer], chosen)
        return chosen

    own_error = owned(scaled)
    own_active = owned(actives)
    counted = counted_rows(counts, tokens, per_micro)
    later = jnp.zeros_like(square)
    for k in range(1, layers):
        later = later + jnp.where(k > section_at, kappas[k], 0.0)
    on_hidden = jnp.concatenate([own_error * scale_d, -scale_r * later * own_active], axis=1)
    on_cot = jnp.concatenate(
        [jnp.zeros_like(own_active), jnp.where(counted, own_active * scale_r, 0.0)], axis=1
    )
    factor_ref[...] = jnp.concatenate([on_hidden.T, on_cot.T], axis=1).astype(bf16)
    both = scale_d * scale_r
    for k in range(1, layers):
        cut = slice((k - 1) * ranks, k * ranks)
        across = dot_first(own_active, scaled[k], exact) * both
        mixed_ref[:ranks, cut] = jnp.zeros_like(across)
        mixed_ref[ranks:, cut] = jnp.where(k > section_at, across, 0.0)
    for i in range(layers - 1):
        cut = slice((layers - 1 + i) * ranks, (layers + i) * ranks)
        after = jnp.zeros_like(square)
        for k in range(i + 1, layers):
            after = after + jnp.where(k > section_at, kappas[k], 0.0)
        across = dot_first(own_error, actives[i], exact) * both
        mixed_ref[:ranks, cut] = jnp.where(i < section_at, across, 0.0)
        across = dot_first(own_active, after * actives[i], exact)
        mixed_ref[ranks:, cut] = across * (-scale_r * scale_r)


def chain(counts, projections, square, grams, features, per_micro):
    sections = len(projections)
    tokens, wide = projections[0].shape
    ranks = wide // (3 * sections)
    inputs = [*projections, square, *grams]
    kernel = functools.partial(chain_kernel, sections, len(grams), features, per_micro)
    return pl.pallas_call(
        kernel,
        in_specs=[in_smem] + [in_vmem] * len(inputs),
        out_specs=[in_vmem] * 2,
        out_shape=[
            jax.ShapeDtypeStruct((2 * ranks, 2 * tokens), bf16),
            jax.ShapeDtypeStruct((2 * ranks, 2 * (sections - 1) * ranks), f32),
        ],
        compiler_params=limited,
        name="chain",
    )(counts, *inputs)


def gradient_kernel(first, factor_ref, h_ref, g_ref, out_ref):
    groups, tensors, _, columns = out_ref.shape
    replica_at = lax.axis_index("replica")
    tensor_at = lax.axis_index("tensor")
    factors = factor_ref[...]
    for group in range(groups):
        for hop in range(tensors):
            owner = (replica_at ^ (first + 2 * group)) * tensors + (tensor_at ^ hop)
            cut = pl.ds(pl.multiple_of(owner * columns, columns), columns)
            stacked = jnp.concatenate([h_ref[:, cut], g_ref[:, cut]], axis=0)
            block = jnp.dot(factors, stacked, preferred_element_type=f32)
            out_ref[group, hop] = block.astype(bf16)


def gradient(factors, hidden, cot, first, replicas, tensors):
    tokens, features = hidden.shape
    rows = factors.shape[0]
    shape = (replicas // 2, tensors, rows, features // (replicas * tensors))
    return pl.pallas_call(
        functools.partial(gradient_kernel, first),
        in_specs=[in_vmem] * 3,
        out_specs=in_vmem,
        out_shape=jax.ShapeDtypeStruct(shape, bf16),
        compiler_params=limited,
        cost_estimate=pl.CostEstimate(
            flops=2 * rows * tokens * features,
            bytes_accessed=(2 * tokens + rows) * features,
            transcendentals=0,
        ),
        name="gradient",
    )(factors, hidden, cot)


def update_kernel(count, *refs):
    pieces = refs[:count]
    mixed_ref, other_ref, right_ref = refs[count : count + 3]
    state_in = refs[count + 3 : count + 9]
    outs = refs[count + 9 : count + 15]
    share_ref, state, sems = refs[count + 15 :]
    copies = [
        pltpu.make_async_copy(source.at[0], state.at[i], sems.at[i])
        for i, source in enumerate(state_in)
    ]
    for copy in copies:
        copy.start()
    mixed = mixed_ref[...] + other_ref[...]
    grad = jnp.dot(mixed, right_ref[...].astype(f32), preferred_element_type=f32, precision=exact)
    for piece in pieces:
        grad = grad + piece[...].reshape(grad.shape).astype(f32)
    for copy in copies:
        copy.wait()
    ranks = grad.shape[0] // 2
    for which in range(2):
        rows = slice(which * ranks, (which + 1) * ranks)
        own = grad[rows]
        master, moment, second = (state[2 * kind + which] for kind in range(3))
        moment = beta_one * moment + (1.0 - beta_one) * own
        second = beta_two * second + (1.0 - beta_two) * own * own
        master = master - learn_rate * (
            moment / first_fix / (jnp.sqrt(second / second_fix) + adam_eps) + decay_rate * master
        )
        share_ref[rows] = master.astype(bf16)
        outs[which][0] = master
        outs[2 + which][0] = moment
        outs[4 + which][0] = second


def update(pieces, mixed, other, right, state):
    _, ranks, columns = state[0].shape

    def leading(piece):
        lead = piece.ndim - 2
        return pl.BlockSpec((1,) * lead + piece.shape[-2:], lambda i: (0,) * piece.ndim)

    whole = [leading(array) for array in (*pieces, mixed, other, right)]
    return pl.pallas_call(
        functools.partial(update_kernel, len(pieces)),
        grid=(1,),
        in_specs=whole + [in_hbm] * 6,
        out_specs=[leading(array) for array in state]
        + [pl.BlockSpec((2 * ranks, columns), lambda i: (0, 0))],
        out_shape=[jax.ShapeDtypeStruct(array.shape, f32) for array in state]
        + [jax.ShapeDtypeStruct((2 * ranks, columns), bf16)],
        scratch_shapes=[
            pltpu.VMEM((6, ranks, columns), f32),
            pltpu.SemaphoreType.DMA((6,)),
        ],
        compiler_params=limited,
        name="update",
    )(*pieces, mixed, other, right, *state)


def place_kernel(layout, bounds, *refs):
    sources = refs[: len(layout)]
    outs = refs[len(layout) : len(layout) + 2]
    zeros, sem = refs[len(layout) + 2 :]
    slots, ranks, features = outs[0].shape
    columns = zeros.shape[1]
    tensors = lax.axis_size("tensor")
    first, after = held_layers(bounds)
    replica_at = lax.axis_index("replica")
    section_at = lax.axis_index("section")
    tensor_at = lax.axis_index("tensor")
    zeros[...] = jnp.zeros_like(zeros)

    def fill(slot, distance, go):
        for (window, rows, owners), source in zip(layout, sources):
            if window != distance:
                continue
            for i, (order, hop) in enumerate(owners):
                owner = (replica_at ^ order) * tensors + (tensor_at ^ hop)
                cut = pl.ds(pl.multiple_of(owner * columns, columns), columns)
                for at, which in enumerate(rows):
                    block = source.at[i, pl.ds(at * ranks, ranks), :]
                    go(pltpu.make_async_copy(block, outs[which].at[slot, :, cut], sem))

    def clear(slot, go):
        for out in outs:
            for block in range(features // columns):
                cut = pl.ds(block * columns, columns)
                go(pltpu.make_async_copy(zeros, out.at[slot, :, cut], sem))

    for act in (lambda copy: copy.start(), lambda copy: copy.wait()):
        for slot in range(slots):
            layer = first + slot
            present = layer < after
            for distance in range(2):

                @pl.when(present & (layer - section_at == distance))
                def _():
                    fill(slot, distance, act)

            @pl.when(jnp.logical_not(present))
            def _():
                clear(slot, act)


def place(bounds, pieces, slots, ranks, features):
    layout = [piece[:3] for piece in pieces]
    arrays = [piece[3] for piece in pieces]
    columns = arrays[0].shape[-1]
    return pl.pallas_call(
        functools.partial(place_kernel, layout),
        in_specs=[in_smem] + [in_vmem] * len(arrays),
        out_specs=[in_hbm] * 2,
        out_shape=[jax.ShapeDtypeStruct((slots, ranks, features), bf16)] * 2,
        scratch_shapes=[pltpu.VMEM((ranks, columns), bf16), pltpu.SemaphoreType.DMA],
        compiler_params=limited,
        name="place",
    )(bounds, *arrays)


def swapped(block, axis, distance):
    route = [(i, i ^ distance) for i in range(lax.axis_size(axis))]
    return lax.ppermute(block, axis, route)


def swaps(block, axis):
    return [swapped(block, axis, k) for k in range(1, lax.axis_size(axis))]


def from_next(block, distance=1):
    size = lax.axis_size("section")
    route = [((i + distance) % size, i) for i in range(size)]
    return lax.ppermute(block, "section", route)


def following_layer(block):
    size = lax.axis_size("section")
    return lax.ppermute(block, "section", [(i + 1, i) for i in range(size - 1)])


def summed(*blocks):
    total = blocks[0].astype(f32)
    for block in blocks[1:]:
        total = total + block.astype(f32)
    return total.astype(bf16)


def reduced(factors, hidden, cot, replicas, tensors):
    sent = gradient(factors, hidden, cot, 1, replicas, tensors)
    near = swapped(sent, "replica", 1)
    kept = gradient(factors, hidden, cot, 0, replicas, tensors)
    across = swapped(summed(kept[1, 1:], near[1, 1:]), "replica", 2)
    last = swapped(summed(kept[1, 0], near[1, 0]), "replica", 2)
    along = [
        swapped(summed(kept[0, k], near[0, k], across[k - 1]), "tensor", k)
        for k in range(1, tensors)
    ]
    return [kept, near, last, *along]


def gathered(share):
    ranks = share.shape[0] // 2
    far_one = swapped(share, "replica", 2)
    next_one = following_layer(share)
    line = jnp.stack(swaps(share, "tensor"))
    next_far_one = following_layer(far_one)
    far_line = swapped(line, "replica", 2)
    next_line = following_layer(line)
    near = jnp.concatenate([share[None], far_one[None], line])
    next_near = jnp.concatenate([next_one[None], next_far_one[None], next_line])
    next_far_down = following_layer(far_line[:, :ranks])
    next_far_up = swapped(next_line[:, ranks:], "replica", 2)
    hops = range(1, lax.axis_size("tensor"))
    near_owners = [(0, 0), (2, 0)] + [(0, hop) for hop in hops]
    far_owners = [(2, hop) for hop in hops]
    pieces = []
    for window, rows, owners, block in (
        (0, (0, 1), near_owners, near),
        (1, (0, 1), near_owners, next_near),
        (0, (0, 1), far_owners, far_line),
        (1, (0,), far_owners, next_far_down),
        (1, (1,), far_owners, next_far_up),
    ):
        other = [(order ^ 1, hop) for order, hop in owners]
        pieces.append((window, rows, owners, block))
        pieces.append((window, rows, other, swapped(block, "replica", 1)))
    return pieces


def on_device(
    inputs,
    cotangent,
    micro_counts,
    bounds,
    holder_down,
    holder_up,
    master_down,
    master_up,
    moment_down,
    moment_up,
    second_down,
    second_up,
):
    sections = lax.axis_size("section")
    replicas = lax.axis_size("replica")
    tensors = lax.axis_size("tensor")
    assert replicas == 4 and tensors == 4
    _, micros, per_micro, features = inputs.shape
    slots = holder_down.shape[2]
    hidden = inputs.reshape(micros * per_micro, features)
    cot = cotangent.reshape(micros * per_micro, features)

    projected, square, hidden, cot = project(
        bounds, micro_counts, hidden, cot, holder_down[0, 0], holder_up[0, 0], sections, per_micro
    )
    owned = jnp.concatenate([master_down[0], master_up[0]], axis=0).astype(bf16)
    around = [from_next(owned, d) for d in range(1, sections)]
    around, projected = lax.optimization_barrier((around, projected))
    table, right = gram([owned, *around])
    projections = [projected] + [from_next(projected, d) for d in range(1, sections)]
    table = table + sum(swaps(table, "replica"))
    tables = [table] + swaps(table, "tensor")
    factors, mixed = chain(micro_counts, projections, square, tables, features, per_micro)

    pieces = reduced(factors, hidden, cot, replicas, tensors)
    for axis, distance in (("tensor", 1), ("tensor", 2), ("replica", 1)):
        mixed = mixed + swapped(mixed, axis, distance)
    other = swapped(mixed, "replica", 2)
    state = [master_down, master_up, moment_down, moment_up, second_down, second_up]
    updated = update(pieces, mixed, other, right, state)
    placed = place(bounds, gathered(updated[6]), slots, holder_down.shape[3], features)
    return (placed[0][None, None], placed[1][None, None], *updated[:6])


def solution(mesh):
    held = P("replica", "section", None, None, None)
    owned = P("section", None, ("replica", "tensor"))
    tokens = P("replica", None, "tensor", None)
    return jax.shard_map(
        on_device,
        mesh=mesh,
        in_specs=(tokens, tokens, P(), P(), held, held) + (owned,) * 6,
        out_specs=(held, held) + (owned,) * 6,
        check_vma=False,
    )
```

time: 341 us -> 136 us (0.40)
  Pallas kernels: 226 us -> 17.3 us
  waiting for transfers between devices: 57.2 us -> 74.1 us
  starting transfers between devices: 45.4 us -> 33 us
  local copies, waits for them, and re-layouts: 4.56 us -> 9.05 us
  other arithmetic: 5.6 us -> 1.66 us
    pallas_call x9 -> x5, Pallas kernels: 221 us -> 15 us  [the longest x1 7.29 us: project(): pl.pallas_call(kernel, in_specs=[in_smem] * 2 + [in_hbm] * 4, out_specs=[...]
    ppermute x40 -> x27, waiting for transfers between devices: 33.3 us -> 49.1 us  [swapped(): return lax.ppermute(block, axis, route)]
    ppermute x40 -> x27, starting transfers between devices: 35.5 us -> 24.5 us  [swapped(): return lax.ppermute(block, axis, route)]
    ppermute x4, waiting for transfers between devices: 17.7 us -> 25 us  [following_layer(): return lax.ppermute(block, 'section', [(i + 1, i) for i in range(size - 1)])]
    ppermute x2, waiting for transfers between devices: 6.14 us -> 0.01 us  [from_next(): return lax.ppermute(block, 'section', route)]
    unnamed x72 -> x32, local copies, waits for them, and re-layouts: 4.48 us -> 9 us
  transfers between devices with their start and end apart: 46 -> 33, of which waited for: 16 -> 16; matrix products, arithmetic and copies ran while one was open for 1% -> 0% of each run, Pallas kernels for 36% -> 6%
where the time goes in v1:
time: 136 us
  waiting for transfers between devices  74.1 us (54%)
  starting transfers between devices  33 us (24%)
  Pallas kernels  17.3 us (13%)
  local copies, waits for them, and re-layouts  9.05 us (7%)
  other arithmetic  1.66 us (1%)
    ppermute x27, waiting for transfers between devices, swapped(): return lax.ppermute(block, axis, route)  49.1 us
    ppermute x4, waiting for transfers between devices, following_layer(): return lax.ppermute(block, 'section', [(i + 1, i) for i in range(size - 1)])  25 us
    ppermute x27, starting transfers between devices, swapped(): return lax.ppermute(block, axis, route)  24.5 us
    unnamed x32, local copies, waits for them, and re-layouts  9 us
    pallas_call x1, Pallas kernels, project(): pl.pallas_call(kernel, in_specs=[in_smem] * 2 + [in_hbm] * 4, out_specs=[...  7.29 us
    ppermute x4, starting transfers between devices, following_layer(): return lax.ppermute(block, 'section', [(i + 1, i) for i in range(size - 1)])  5.16 us
    ppermute x2, starting transfers between devices, from_next(): return lax.ppermute(block, 'section', route)  3.31 us
    pallas_call x1, Pallas kernels, update(): pl.pallas_call(functools.partial(update_kernel, len(pieces)), grid=(1,),...  3.31 us
  transfers between devices with their start and end apart: 33, of which 16 were waited for; matrix products, arithmetic and copies ran while one was open for 0% of the time, Pallas kernels for 6%

profile of v1, /device:TPU:0, one launch (start us, length us, event | category | flops | bytes accessed | tf_op | source)
XLA Modules:
  0.0 136.1 jit_solution(17928938062010395359)
XLA Ops:
  0.6 1.0 convert_bitcast_fusion
  1.7 3.0 %collective-permute-start = (bf16[128,768]{1,0:T(8,128)(2,1)S(1)}, bf16[128,768]{1,0:T(8,128)(2,1)S(1)}, u32[]{:S(2)}, u32[]{:S(2)}) collective-permute-start(bf16[128,768]{1,0:T(8,128)(2,1)S(1)} %pad_maximum_fusion.2.refs_0_), channel_id=1, source_target_pairs={{4,0},{0,4},{5,1},{1,5},{6,2},{2,6},{7,3},{3,7},{12,8},{8,12},{13,... | collective-permute-start | bytes 589832 | tf_op jit(solution)/shard_map/ppermute | solution.py:464
  4.7 1.9 %copy-done = bf16[1,4,32,12288]{3,2,1,0:T(8,128)(2,1)S(1)} copy-done((bf16[1,4,32,12288]{3,2,1,0:T(8,128)(2,1)S(1)}, bf16[1,4,32,12288]{3,2,1,0:T(8,128)(2,1)}, u32[]{:S(2)}) %copy-start) | copy-done | bytes 3145752
  6.6 1.9 %copy-done.1 = bf16[1,4,32,12288]{3,2,1,0:T(8,128)(2,1)S(1)} copy-done((bf16[1,4,32,12288]{3,2,1,0:T(8,128)(2,1)S(1)}, bf16[1,4,32,12288]{3,2,1,0:T(8,128)(2,1)}, u32[]{:S(2)}) %copy-start.1) | copy-done | bytes 3145752
  8.5 1.9 %copy-done.2 = bf16[1,1,2,64,12288]{4,3,2,1,0:T(8,128)(2,1)S(1)} copy-done((bf16[1,1,2,64,12288]{4,3,2,1,0:T(8,128)(2,1)S(1)}, bf16[1,1,2,64,12288]{4,3,2,1,0:T(8,128)(2,1)}, u32[]{:S(2)}) %copy-start.2) | copy-done | bytes 3145752
  10.4 1.9 %copy-done.3 = bf16[1,1,2,64,12288]{4,3,2,1,0:T(8,128)(2,1)S(1)} copy-done((bf16[1,1,2,64,12288]{4,3,2,1,0:T(8,128)(2,1)S(1)}, bf16[1,1,2,64,12288]{4,3,2,1,0:T(8,128)(2,1)}, u32[]{:S(2)}) %copy-start.3) | copy-done | bytes 3145752
  12.3 0.7 copy-done.10
  13.0 0.7 copy-done.12
  13.6 7.3 %project.1 = (f32[128,384]{1,0:T(8,128)S(1)}, f32[128,128]{1,0:T(8,128)S(1)}, bf16[128,12288]{1,0:T(8,128)(2,1)S(1)}, bf16[128,12288]{1,0:T(8,128)(2,1)S(1)}) custom-call(s32[4,3]{1,0:T(4,128)S(1)} %copy-done.10, s32[4]{0:T(128)S(1)} %copy-done.12, bf16[128,12288]{1,0:T(8,128)(2,1)S(1)} %bitcast.47, bf16[128,12288]{1,0:T(8,128)(2,1)S(1)} %bitcast.48, ...), custom_call_target="tpu_custom_call" | custom-call | flops 1207959552 | bytes 12582912 | tf_op jit(solution)/shard_map/project/pallas_call | solution.py:120
  21.1 0.7 collective-permute-start.4
  21.8 0.9 collective-permute-start.3
  23.3 1.4 %collective-permute-done.4 = f32[64,128]{1,0:T(8,128)S(1)} collective-permute-done((f32[64,128]{1,0:T(8,128)S(1)}, f32[64,128]{1,0:T(8,128)S(1)}, u32[]{:S(2)}, u32[]{:S(2)}) %collective-permute-start.4) | collective-permute-done | bytes 32800 | tf_op jit(solution)/shard_map/ppermute | solution.py:454
  24.8 1.3 collective-permute-done.3
  26.1 3.7 %collective-permute-start.7 = (f32[64,128]{1,0:T(8,128)S(1)}, f32[64,128]{1,0:T(8,128)S(1)}, u32[]{:S(2)}, u32[]{:S(2)}) collective-permute-start(f32[64,128]{1,0:T(8,128)S(1)} %add_add_fusion.refs_3_), channel_id=1, source_target_pairs={{0,3},{1,2},{2,1},{3,0},{4,7},{5,6},{6,5},{7,4},{8,11},{9,10},{10,... | collective-permute-start | bytes 98312 | tf_op jit(solution)/shard_map/ppermute | solution.py:454
  29.8 0.8 collective-permute-start.5
  30.6 1.3 collective-permute-done.7.refs_6_
  31.9 2.7 %collective-permute-done.6.refs_5_ = f32[64,128]{1,0:T(8,128)S(1)} collective-permute-done((f32[64,128]{1,0:T(8,128)S(1)}, f32[64,128]{1,0:T(8,128)S(1)}, u32[]{:S(2)}, u32[]{:S(2)}) %collective-permute-start.6) | collective-permute-done | bytes 32800 | tf_op jit(solution)/shard_map/ppermute | solution.py:454
  34.6 2.1 %chain.1 = (bf16[128,256]{1,0:T(8,128)(2,1)S(1)}, f32[128,128]{1,0:T(8,128)S(1)}) custom-call(s32[4]{0:T(128)S(1)} %copy-done.13, f32[128,384]{1,0:T(8,128)S(1)} %get-tuple-element.28.refs_0_, f32[128,384]{1,0:T(8,128)S(1)} %collective-permute-done.1.refs_1_, f32[128,128]{1,0:T(8,128)S(1)} %get-tuple-element.29.refs_2_, f32[64,128]{1,0:T(8,128)S(1)} %add_add_fusion.refs_3_, ...), custom_call_target="tpu_custom_call" | custom-call | tf_op jit(solution)/shard_map/chain/pallas_call | solution.py:287
  37.4 0.6 gradient.2.refs_0_
  38.0 2.8 %collective-permute-done.8.refs_1_ = bf16[2,4,128,768]{3,2,1,0:T(8,128)(2,1)S(1)} collective-permute-done((bf16[2,4,128,768]{3,2,1,0:T(8,128)(2,1)S(1)}, bf16[2,4,128,768]{3,2,1,0:T(8,128)(2,1)S(1)}, u32[]{:S(2)}, u32[]{:S(2)}) %collective-permute-start.8) | collective-permute-done | bytes 1572896 | tf_op jit(solution)/shard_map/ppermute | solution.py:454
  40.9 0.8 collective-permute-start.10
  41.7 4.3 %collective-permute-done.14 = f32[128,128]{1,0:T(8,128)S(1)} collective-permute-done((f32[128,128]{1,0:T(8,128)S(1)}, f32[128,128]{1,0:T(8,128)S(1)}, u32[]{:S(2)}, u32[]{:S(2)}) %collective-permute-start.14) | collective-permute-done | bytes 65568 | tf_op jit(solution)/shard_map/ppermute | solution.py:454
  46.1 2.1 %collective-permute-start.15 = (f32[128,128]{1,0:T(8,128)S(1)}, f32[128,128]{1,0:T(8,128)S(1)}, u32[]{:S(2)}, u32[]{:S(2)}) collective-permute-start(f32[128,128]{1,0:T(8,128)S(1)} %add.67), channel_id=1, source_target_pairs={{0,2},{1,3},{2,0},{3,1},{4,6},{5,7},{6,4},{7,5},{8,10},{9,11},{10,... | collective-permute-start | bytes 196616 | tf_op jit(solution)/shard_map/ppermute | solution.py:454
  48.2 1.4 %collective-permute-start.9 = (bf16[128,768]{1,0:T(8,128)(2,1)S(1)}, bf16[128,768]{1,0:T(8,128)(2,1)S(1)}, u32[]{:S(2)}, u32[]{:S(2)}) collective-permute-start(bf16[128,768]{1,0:T(8,128)(2,1)S(1)} %fusion.4), channel_id=1, source_target_pairs={{0,16},{8,24},{16,0},{24,8},{1,17},{9,25},{17,1},{25,9},{2,18},{10... | collective-permute-start | bytes 589832 | tf_op jit(solution)/shard_map/ppermute | solution.py:454
  49.6 7.6 %collective-permute-done.10 = bf16[3,128,768]{2,1,0:T(8,128)(2,1)S(1)} collective-permute-done((bf16[3,128,768]{2,1,0:T(8,128)(2,1)S(1)}, bf16[3,128,768]{2,1,0:T(8,128)(2,1)S(1)}, u32[]{:S(2)}, u32[]{:S(2)}) %collective-permute-start.10) | collective-permute-done | bytes 589856 | tf_op jit(solution)/shard_map/ppermute | solution.py:454
  57.4 1.5 %collective-permute-start.13 = (bf16[128,768]{1,0:T(8,128)(2,1)S(1)}, bf16[128,768]{1,0:T(8,128)(2,1)S(1)}, u32[]{:S(2)}, u32[]{:S(2)}) collective-permute-start(bf16[128,768]{1,0:T(8,128)(2,1)S(1)} %get-tuple-element.46), channel_id=1, source_target_pairs={{0,3},{1,2},{2,1},{3,0},{4,7},{5,6},{6,5},{7,4},{8,11},{9,10},{10,... | collective-permute-start | bytes 589832 | tf_op jit(solution)/shard_map/ppermute | solution.py:454
  58.9 0.6 collective-permute-start.12
  59.5 2.3 %collective-permute-start.11 = (bf16[128,768]{1,0:T(8,128)(2,1)S(1)}, bf16[128,768]{1,0:T(8,128)(2,1)S(1)}, u32[]{:S(2)}, u32[]{:S(2)}) collective-permute-start(bf16[128,768]{1,0:T(8,128)(2,1)S(1)} %get-tuple-element.48), channel_id=1, source_target_pairs={{0,1},{1,0},{2,3},{3,2},{4,5},{5,4},{6,7},{7,6},{8,9},{9,8},{10,11... | collective-permute-start | bytes 589832 | tf_op jit(solution)/shard_map/ppermute | solution.py:454
  61.9 1.2 collective-permute-done.16
  63.2 0.8 collective-permute-start.17
  64.0 3.6 %collective-permute-done.17.refs_7_ = f32[128,128]{1,0:T(8,128)S(1)} collective-permute-done((f32[128,128]{1,0:T(8,128)S(1)}, f32[128,128]{1,0:T(8,128)S(1)}, u32[]{:S(2)}, u32[]{:S(2)}) %collective-permute-start.17) | collective-permute-done | bytes 65568 | tf_op jit(solution)/shard_map/ppermute | solution.py:454
  67.5 8.2 %collective-permute-done.12.refs_4_ = bf16[128,768]{1,0:T(8,128)(2,1)S(1)} collective-permute-done((bf16[128,768]{1,0:T(8,128)(2,1)S(1)}, bf16[128,768]{1,0:T(8,128)(2,1)S(1)}, u32[]{:S(2)}, u32[]{:S(2)}) %collective-permute-start.12) | collective-permute-done | bytes 196640 | tf_op jit(solution)/shard_map/ppermute | solution.py:454
  75.7 3.3 %update.1 = (f32[1,64,768]{2,1,0:T(8,128)}, f32[1,64,768]{2,1,0:T(8,128)}, f32[1,64,768]{2,1,0:T(8,128)}, f32[1,64,768]{2,1,0:T(8,128)}, f32[1,64,768]{2,1,0:T(8...) custom-call(bf16[2,4,128,768]{3,2,1,0:T(8,128)(2,1)S(1)} %gradient.2.refs_0_, ...), custom_call_target="tpu_custom_call" | custom-call | tf_op jit(solution)/shard_map/update/pallas_call | solution.py:375
  79.0 1.3 collective-permute-start.23
  80.3 2.7 %collective-permute-start.21 = (bf16[128,768]{1,0:T(8,128)(2,1)S(1)}, bf16[128,768]{1,0:T(8,128)(2,1)S(1)}, u32[]{:S(2)}, u32[]{:S(2)}) collective-permute-start(bf16[128,768]{1,0:T(8,128)(2,1)S(1)} %get-tuple-element.37), channel_id=1, source_target_pairs={{0,3},{1,2},{2,1},{3,0},{4,7},{5,6},{6,5},{7,4},{8,11},{9,10},{10,... | collective-permute-start | bytes 589832 | tf_op jit(solution)/shard_map/ppermute | solution.py:454
  83.1 1.7 %collective-permute-start.19 = (bf16[128,768]{1,0:T(8,128)(2,1)S(1)}, bf16[128,768]{1,0:T(8,128)(2,1)S(1)}, u32[]{:S(2)}, u32[]{:S(2)}) collective-permute-start(bf16[128,768]{1,0:T(8,128)(2,1)S(1)} %get-tuple-element.37), channel_id=1, source_target_pairs={{0,1},{1,0},{2,3},{3,2},{4,5},{5,4},{6,7},{7,6},{8,9},{9,8},{10,11... | collective-permute-start | bytes 589832 | tf_op jit(solution)/shard_map/ppermute | solution.py:454
  84.8 0.7 collective-permute-start.18
  85.5 4.5 %collective-permute-done.21 = bf16[128,768]{1,0:T(8,128)(2,1)S(1)} collective-permute-done((bf16[128,768]{1,0:T(8,128)(2,1)S(1)}, bf16[128,768]{1,0:T(8,128)(2,1)S(1)}, u32[]{:S(2)}, u32[]{:S(2)}) %collective-permute-start.21) | collective-permute-done | bytes 196640 | tf_op jit(solution)/shard_map/ppermute | solution.py:454
  90.1 8.7 %collective-permute-done.20 = bf16[128,768]{1,0:T(8,128)(2,1)S(1)} collective-permute-done((bf16[128,768]{1,0:T(8,128)(2,1)S(1)}, bf16[128,768]{1,0:T(8,128)(2,1)S(1)}, u32[]{:S(2)}, u32[]{:S(2)}) %collective-permute-start.20) | collective-permute-done | bytes 196640 | tf_op jit(solution)/shard_map/ppermute | solution.py:454
  98.8 0.8 collective-permute-start.27
  99.6 1.3 collective-permute-start.25
  100.9 1.3 collective-permute-start.24
  102.4 17.0 %collective-permute-done.24 = bf16[128,768]{1,0:T(8,128)(2,1)S(1)} collective-permute-done((bf16[128,768]{1,0:T(8,128)(2,1)S(1)}, bf16[128,768]{1,0:T(8,128)(2,1)S(1)}, u32[]{:S(2)}, u32[]{:S(2)}) %collective-permute-start.24) | collective-permute-done | bytes 196640 | tf_op jit(solution)/shard_map/ppermute | solution.py:469
  119.5 1.3 collective-permute-start.29
  121.4 1.4 %collective-permute-start.31 = (bf16[3,64,768]{2,1,0:T(8,128)(2,1)S(1)}, bf16[3,64,768]{2,1,0:T(8,128)(2,1)S(1)}, u32[]{:S(2)}, u32[]{:S(2)}) collective-permute-start(bf16[3,64,768]{2,1,0:T(8,128)(2,1)S(1)} %slice.74), channel_id=1, source_target_pairs={{0,16},{8,24},{16,0},{24,8},{1,17},{9,25},{17,1},{25,9},{2,18},{10... | collective-permute-start | bytes 884744 | tf_op jit(solution)/shard_map/ppermute | solution.py:454
  122.8 8.0 %collective-permute-done.29.refs_6_ = bf16[3,64,768]{2,1,0:T(8,128)(2,1)S(1)} collective-permute-done((bf16[3,64,768]{2,1,0:T(8,128)(2,1)S(1)}, bf16[3,64,768]{2,1,0:T(8,128)(2,1)S(1)}, u32[]{:S(2)}, u32[]{:S(2)}) %collective-permute-start.29) | collective-permute-done | bytes 294944 | tf_op jit(solution)/shard_map/ppermute | solution.py:469
  131.4 1.1 collective-permute-done.30.refs_7_
  132.9 3.2 %place.1 = (bf16[2,64,12288]{2,1,0:T(8,128)(2,1)}, bf16[2,64,12288]{2,1,0:T(8,128)(2,1)}) custom-call(s32[4,3]{1,0:T(4,128)S(1)} %copy-done.11, bf16[5,128,768]{2,1,0:T(8,128)(2,1)S(1)} %constant_dynamic-update-slice_fusion.refs_0_, bf16[5,128,768]{2,1,0:T(8,128)(2,1)S(1)} %collective-permute-done.22.refs_1_, ...), custom_call_target="tpu_custom_call" | custom-call | tf_op jit(solution)/shard_map/place/pallas_call | solution.py:441
  (71 shorter events, 4.0 us)
Async XLA Ops:
  1.7 19.2 %collective-permute-start = (bf16[128,768]{1,0:T(8,128)(2,1)S(1)}, bf16[128,768]{1,0:T(8,128)(2,1)S(1)}, u32[]{:S(2)}, u32[]{:S(2)}) collective-permute-start(bf16[128,768]{1,0:T(8,128)(2,1)S(1)} %pad_maximum_fusion.2.refs_0_), channel_id=1, source_target_pairs={{4,0},{0,4},{5,1},{1,5},{6,2},{2,6},{7,3},{3,7},{12,8},{8,12},{13,... | collective-permute-start | bytes 589832 | tf_op jit(solution)/shard_map/ppermute | solution.py:464
  4.7 1.9 %copy-start = (bf16[1,4,32,12288]{3,2,1,0:T(8,128)(2,1)S(1)}, bf16[1,4,32,12288]{3,2,1,0:T(8,128)(2,1)}, u32[]{:S(2)}) copy-start(bf16[1,4,32,12288]{3,2,1,0:T(8,128)(2,1)} %param.12) | copy-start | bytes 9437188
  6.6 1.9 %copy-start.1 = (bf16[1,4,32,12288]{3,2,1,0:T(8,128)(2,1)S(1)}, bf16[1,4,32,12288]{3,2,1,0:T(8,128)(2,1)}, u32[]{:S(2)}) copy-start(bf16[1,4,32,12288]{3,2,1,0:T(8,128)(2,1)} %param.13) | copy-start | bytes 9437188
  8.5 1.9 %copy-start.2 = (bf16[1,1,2,64,12288]{4,3,2,1,0:T(8,128)(2,1)S(1)}, bf16[1,1,2,64,12288]{4,3,2,1,0:T(8,128)(2,1)}, u32[]{:S(2)}) copy-start(bf16[1,1,2,64,12288]{4,3,2,1,0:T(8,128)(2,1)} %param.16) | copy-start | bytes 9437188
  10.4 1.9 %copy-start.3 = (bf16[1,1,2,64,12288]{4,3,2,1,0:T(8,128)(2,1)S(1)}, bf16[1,1,2,64,12288]{4,3,2,1,0:T(8,128)(2,1)}, u32[]{:S(2)}) copy-start(bf16[1,1,2,64,12288]{4,3,2,1,0:T(8,128)(2,1)} %param.17) | copy-start | bytes 9437188
  12.3 0.7 copy-start.10
  13.0 0.7 copy-start.12
  13.6 21.0 %copy-start.13 = (s32[4]{0:T(128)S(1)}, s32[4]{0:T(128)}, u32[]{:S(2)}) copy-start(s32[4]{0:T(128)} %counts.3) | copy-start | bytes 52
  21.1 3.7 %collective-permute-start.4 = (f32[64,128]{1,0:T(8,128)S(1)}, f32[64,128]{1,0:T(8,128)S(1)}, u32[]{:S(2)}, u32[]{:S(2)}) collective-permute-start(f32[64,128]{1,0:T(8,128)S(1)} %get-tuple-element.31), channel_id=1, source_target_pairs={{0,24},{8,16},{16,8},{24,0},{1,25},{9,17},{17,9},{25,1},{2,26},{10... | collective-permute-start | bytes 98312 | tf_op jit(solution)/shard_map/ppermute | solution.py:454
  21.8 4.3 %collective-permute-start.3 = (f32[64,128]{1,0:T(8,128)S(1)}, f32[64,128]{1,0:T(8,128)S(1)}, u32[]{:S(2)}, u32[]{:S(2)}) collective-permute-start(f32[64,128]{1,0:T(8,128)S(1)} %get-tuple-element.31), channel_id=1, source_target_pairs={{0,16},{8,24},{16,0},{24,8},{1,17},{9,25},{17,1},{25,9},{2,18},{10... | collective-permute-start | bytes 98312 | tf_op jit(solution)/shard_map/ppermute | solution.py:454
  22.8 3.3 %collective-permute-start.2 = (f32[64,128]{1,0:T(8,128)S(1)}, f32[64,128]{1,0:T(8,128)S(1)}, u32[]{:S(2)}, u32[]{:S(2)}) collective-permute-start(f32[64,128]{1,0:T(8,128)S(1)} %get-tuple-element.31), channel_id=1, source_target_pairs={{0,8},{8,0},{16,24},{24,16},{1,9},{9,1},{17,25},{25,17},{2,10},{10... | collective-permute-start | bytes 98312 | tf_op jit(solution)/shard_map/ppermute | solution.py:454
  23.0 11.6 %collective-permute-start.1 = (f32[128,384]{1,0:T(8,128)S(1)}, f32[128,384]{1,0:T(8,128)S(1)}, u32[]{:S(2)}, u32[]{:S(2)}) collective-permute-start(f32[128,384]{1,0:T(8,128)S(1)} %get-tuple-element.28.refs_0_), channel_id=1, source_target_pairs={{4,0},{0,4},{5,1},{1,5},{6,2},{2,6},{7,3},{3,7},{12,8},{8,12},{13,... | collective-permute-start | bytes 589832 | tf_op jit(solution)/shard_map/ppermute | solution.py:464
  26.1 5.8 %collective-permute-start.7 = (f32[64,128]{1,0:T(8,128)S(1)}, f32[64,128]{1,0:T(8,128)S(1)}, u32[]{:S(2)}, u32[]{:S(2)}) collective-permute-start(f32[64,128]{1,0:T(8,128)S(1)} %add_add_fusion.refs_3_), channel_id=1, source_target_pairs={{0,3},{1,2},{2,1},{3,0},{4,7},{5,6},{6,5},{7,4},{8,11},{9,10},{10,... | collective-permute-start | bytes 98312 | tf_op jit(solution)/shard_map/ppermute | solution.py:454
  29.8 4.8 %collective-permute-start.6 = (f32[64,128]{1,0:T(8,128)S(1)}, f32[64,128]{1,0:T(8,128)S(1)}, u32[]{:S(2)}, u32[]{:S(2)}) collective-permute-start(f32[64,128]{1,0:T(8,128)S(1)} %add_add_fusion.refs_3_), channel_id=1, source_target_pairs={{0,2},{1,3},{2,0},{3,1},{4,6},{5,7},{6,4},{7,5},{8,10},{9,11},{10,... | collective-permute-start | bytes 98312 | tf_op jit(solution)/shard_map/ppermute | solution.py:454
  29.8 4.8 %collective-permute-start.5 = (f32[64,128]{1,0:T(8,128)S(1)}, f32[64,128]{1,0:T(8,128)S(1)}, u32[]{:S(2)}, u32[]{:S(2)}) collective-permute-start(f32[64,128]{1,0:T(8,128)S(1)} %add_add_fusion.refs_3_), channel_id=1, source_target_pairs={{0,1},{1,0},{2,3},{3,2},{4,5},{5,4},{6,7},{7,6},{8,9},{9,8},{10,11... | collective-permute-start | bytes 98312 | tf_op jit(solution)/shard_map/ppermute | solution.py:454
  37.3 3.5 %collective-permute-start.8 = (bf16[2,4,128,768]{3,2,1,0:T(8,128)(2,1)S(1)}, bf16[2,4,128,768]{3,2,1,0:T(8,128)(2,1)S(1)}, u32[]{:S(2)}, u32[]{:S(2)}) collective-permute-start(bf16[2,4,128,768]{3,2,1,0:T(8,128)(2,1)S(1)} %gradient.3), channel_id=1, source_target_pairs={{0,8},{8,0},{16,24},{24,16},{1,9},{9,1},{17,25},{25,17},{2,10},{10... | collective-permute-start | bytes 4718600 | tf_op jit(solution)/shard_map/ppermute | solution.py:454
  40.9 16.2 %collective-permute-start.10 = (bf16[3,128,768]{2,1,0:T(8,128)(2,1)S(1)}, bf16[3,128,768]{2,1,0:T(8,128)(2,1)S(1)}, u32[]{:S(2)}, u32[]{:S(2)}) collective-permute-start(bf16[3,128,768]{2,1,0:T(8,128)(2,1)S(1)} %fusion), channel_id=1, source_target_pairs={{0,16},{8,24},{16,0},{24,8},{1,17},{9,25},{17,1},{25,9},{2,18},{10... | collective-permute-start | bytes 1769480 | tf_op jit(solution)/shard_map/ppermute | solution.py:454
  41.7 4.3 %collective-permute-start.14 = (f32[128,128]{1,0:T(8,128)S(1)}, f32[128,128]{1,0:T(8,128)S(1)}, u32[]{:S(2)}, u32[]{:S(2)}) collective-permute-start(f32[128,128]{1,0:T(8,128)S(1)} %get-tuple-element.35), channel_id=1, source_target_pairs={{0,1},{1,0},{2,3},{3,2},{4,5},{5,4},{6,7},{7,6},{8,9},{9,8},{10,11... | collective-permute-start | bytes 196616 | tf_op jit(solution)/shard_map/ppermute | solution.py:454
  46.0 29.7 %copy-start.4 = (f32[1,64,768]{2,1,0:T(8,128)S(1)}, f32[1,64,768]{2,1,0:T(8,128)}, u32[]{:S(2)}) copy-start(f32[1,64,768]{2,1,0:T(8,128)} %refs_10_.1) | copy-start | bytes 589828
  46.0 29.7 %copy-start.5 = (f32[1,64,768]{2,1,0:T(8,128)S(1)}, f32[1,64,768]{2,1,0:T(8,128)}, u32[]{:S(2)}) copy-start(f32[1,64,768]{2,1,0:T(8,128)} %refs_9_.1) | copy-start | bytes 589828
  46.0 29.7 %copy-start.6 = (f32[1,64,768]{2,1,0:T(8,128)S(1)}, f32[1,64,768]{2,1,0:T(8,128)}, u32[]{:S(2)}) copy-start(f32[1,64,768]{2,1,0:T(8,128)} %refs_11_.1) | copy-start | bytes 589828
  46.0 29.7 %copy-start.7 = (f32[1,64,768]{2,1,0:T(8,128)S(1)}, f32[1,64,768]{2,1,0:T(8,128)}, u32[]{:S(2)}) copy-start(f32[1,64,768]{2,1,0:T(8,128)} %refs_12_.1) | copy-start | bytes 589828
  46.0 29.7 %copy-start.8 = (f32[1,64,768]{2,1,0:T(8,128)S(1)}, f32[1,64,768]{2,1,0:T(8,128)}, u32[]{:S(2)}) copy-start(f32[1,64,768]{2,1,0:T(8,128)} %refs_13_.1) | copy-start | bytes 589828
  46.0 29.7 %copy-start.9 = (f32[1,64,768]{2,1,0:T(8,128)S(1)}, f32[1,64,768]{2,1,0:T(8,128)}, u32[]{:S(2)}) copy-start(f32[1,64,768]{2,1,0:T(8,128)} %refs_14_.1) | copy-start | bytes 589828
  46.1 15.8 %collective-permute-start.15 = (f32[128,128]{1,0:T(8,128)S(1)}, f32[128,128]{1,0:T(8,128)S(1)}, u32[]{:S(2)}, u32[]{:S(2)}) collective-permute-start(f32[128,128]{1,0:T(8,128)S(1)} %add.67), channel_id=1, source_target_pairs={{0,2},{1,3},{2,0},{3,1},{4,6},{5,7},{6,4},{7,5},{8,10},{9,11},{10,... | collective-permute-start | bytes 196616 | tf_op jit(solution)/shard_map/ppermute | solution.py:454
  48.2 19.3 %collective-permute-start.9 = (bf16[128,768]{1,0:T(8,128)(2,1)S(1)}, bf16[128,768]{1,0:T(8,128)(2,1)S(1)}, u32[]{:S(2)}, u32[]{:S(2)}) collective-permute-start(bf16[128,768]{1,0:T(8,128)(2,1)S(1)} %fusion.4), channel_id=1, source_target_pairs={{0,16},{8,24},{16,0},{24,8},{1,17},{9,25},{17,1},{25,9},{2,18},{10... | collective-permute-start | bytes 589832 | tf_op jit(solution)/shard_map/ppermute | solution.py:454
  57.4 10.1 %collective-permute-start.13 = (bf16[128,768]{1,0:T(8,128)(2,1)S(1)}, bf16[128,768]{1,0:T(8,128)(2,1)S(1)}, u32[]{:S(2)}, u32[]{:S(2)}) collective-permute-start(bf16[128,768]{1,0:T(8,128)(2,1)S(1)} %get-tuple-element.46), channel_id=1, source_target_pairs={{0,3},{1,2},{2,1},{3,0},{4,7},{5,6},{6,5},{7,4},{8,11},{9,10},{10,... | collective-permute-start | bytes 589832 | tf_op jit(solution)/shard_map/ppermute | solution.py:454
  58.9 16.8 %collective-permute-start.12 = (bf16[128,768]{1,0:T(8,128)(2,1)S(1)}, bf16[128,768]{1,0:T(8,128)(2,1)S(1)}, u32[]{:S(2)}, u32[]{:S(2)}) collective-permute-start(bf16[128,768]{1,0:T(8,128)(2,1)S(1)} %get-tuple-element.47), channel_id=1, source_target_pairs={{0,2},{1,3},{2,0},{3,1},{4,6},{5,7},{6,4},{7,5},{8,10},{9,11},{10,... | collective-permute-start | bytes 589832 | tf_op jit(solution)/shard_map/ppermute | solution.py:454
  59.5 16.1 %collective-permute-start.11 = (bf16[128,768]{1,0:T(8,128)(2,1)S(1)}, bf16[128,768]{1,0:T(8,128)(2,1)S(1)}, u32[]{:S(2)}, u32[]{:S(2)}) collective-permute-start(bf16[128,768]{1,0:T(8,128)(2,1)S(1)} %get-tuple-element.48), channel_id=1, source_target_pairs={{0,1},{1,0},{2,3},{3,2},{4,5},{5,4},{6,7},{7,6},{8,9},{9,8},{10,11... | collective-permute-start | bytes 589832 | tf_op jit(solution)/shard_map/ppermute | solution.py:454
  61.9 1.3 collective-permute-start.16
  63.2 4.3 %collective-permute-start.17 = (f32[128,128]{1,0:T(8,128)S(1)}, f32[128,128]{1,0:T(8,128)S(1)}, u32[]{:S(2)}, u32[]{:S(2)}) collective-permute-start(f32[128,128]{1,0:T(8,128)S(1)} %add.69.refs_6_), channel_id=1, source_target_pairs={{0,16},{8,24},{16,0},{24,8},{1,17},{9,25},{17,1},{25,9},{2,18},{10... | collective-permute-start | bytes 196616 | tf_op jit(solution)/shard_map/ppermute | solution.py:454
  79.0 23.3 %collective-permute-start.23 = (bf16[128,768]{1,0:T(8,128)(2,1)S(1)}, bf16[128,768]{1,0:T(8,128)(2,1)S(1)}, u32[]{:S(2)}, u32[]{:S(2)}) collective-permute-start(bf16[128,768]{1,0:T(8,128)(2,1)S(1)} %get-tuple-element.37), channel_id=1, source_target_pairs={{4,0},{5,1},{6,2},{7,3},{12,8},{13,9},{14,10},{15,11},{20,16},{21,... | collective-permute-start | bytes 589832 | tf_op jit(solution)/shard_map/ppermute | solution.py:469
  80.3 9.7 %collective-permute-start.21 = (bf16[128,768]{1,0:T(8,128)(2,1)S(1)}, bf16[128,768]{1,0:T(8,128)(2,1)S(1)}, u32[]{:S(2)}, u32[]{:S(2)}) collective-permute-start(bf16[128,768]{1,0:T(8,128)(2,1)S(1)} %get-tuple-element.37), channel_id=1, source_target_pairs={{0,3},{1,2},{2,1},{3,0},{4,7},{5,6},{6,5},{7,4},{8,11},{9,10},{10,... | collective-permute-start | bytes 589832 | tf_op jit(solution)/shard_map/ppermute | solution.py:454
  83.1 15.7 %collective-permute-start.20 = (bf16[128,768]{1,0:T(8,128)(2,1)S(1)}, bf16[128,768]{1,0:T(8,128)(2,1)S(1)}, u32[]{:S(2)}, u32[]{:S(2)}) collective-permute-start(bf16[128,768]{1,0:T(8,128)(2,1)S(1)} %get-tuple-element.37), channel_id=1, source_target_pairs={{0,2},{1,3},{2,0},{3,1},{4,6},{5,7},{6,4},{7,5},{8,10},{9,11},{10,... | collective-permute-start | bytes 589832 | tf_op jit(solution)/shard_map/ppermute | solution.py:454
  83.1 15.7 %collective-permute-start.19 = (bf16[128,768]{1,0:T(8,128)(2,1)S(1)}, bf16[128,768]{1,0:T(8,128)(2,1)S(1)}, u32[]{:S(2)}, u32[]{:S(2)}) collective-permute-start(bf16[128,768]{1,0:T(8,128)(2,1)S(1)} %get-tuple-element.37), channel_id=1, source_target_pairs={{0,1},{1,0},{2,3},{3,2},{4,5},{5,4},{6,7},{7,6},{8,9},{9,8},{10,11... | collective-permute-start | bytes 589832 | tf_op jit(solution)/shard_map/ppermute | solution.py:454
  84.8 16.1 %collective-permute-start.18 = (bf16[128,768]{1,0:T(8,128)(2,1)S(1)}, bf16[128,768]{1,0:T(8,128)(2,1)S(1)}, u32[]{:S(2)}, u32[]{:S(2)}) collective-permute-start(bf16[128,768]{1,0:T(8,128)(2,1)S(1)} %get-tuple-element.37), channel_id=1, source_target_pairs={{0,16},{8,24},{16,0},{24,8},{1,17},{9,25},{17,1},{25,9},{2,18},{10... | collective-permute-start | bytes 589832 | tf_op jit(solution)/shard_map/ppermute | solution.py:454
  98.8 20.7 %collective-permute-start.27 = (bf16[3,128,768]{2,1,0:T(8,128)(2,1)S(1)}, bf16[3,128,768]{2,1,0:T(8,128)(2,1)S(1)}, u32[]{:S(2)}, u32[]{:S(2)}) collective-permute-start(bf16[3,128,768]{2,1,0:T(8,128)(2,1)S(1)} %pad_maximum_fusion.1), channel_id=1, source_target_pairs={{0,16},{8,24},{16,0},{24,8},{1,17},{9,25},{17,1},{25,9},{2,18},{10... | collective-permute-start | bytes 1769480 | tf_op jit(solution)/shard_map/ppermute | solution.py:454
  99.6 19.8 %collective-permute-start.25 = (bf16[3,128,768]{2,1,0:T(8,128)(2,1)S(1)}, bf16[3,128,768]{2,1,0:T(8,128)(2,1)S(1)}, u32[]{:S(2)}, u32[]{:S(2)}) collective-permute-start(bf16[3,128,768]{2,1,0:T(8,128)(2,1)S(1)} %pad_maximum_fusion.1), channel_id=1, source_target_pairs={{4,0},{5,1},{6,2},{7,3},{12,8},{13,9},{14,10},{15,11},{20,16},{21,... | collective-permute-start | bytes 1769480 | tf_op jit(solution)/shard_map/ppermute | solution.py:469
  100.9 18.5 %collective-permute-start.24 = (bf16[128,768]{1,0:T(8,128)(2,1)S(1)}, bf16[128,768]{1,0:T(8,128)(2,1)S(1)}, u32[]{:S(2)}, u32[]{:S(2)}) collective-permute-start(bf16[128,768]{1,0:T(8,128)(2,1)S(1)} %collective-permute-done.18), channel_id=1, source_target_pairs={{4,0},{5,1},{6,2},{7,3},{12,8},{13,9},{14,10},{15,11},{20,16},{21,... | collective-permute-start | bytes 589832 | tf_op jit(solution)/shard_map/ppermute | solution.py:469
  102.3 29.1 %collective-permute-start.22 = (bf16[5,128,768]{2,1,0:T(8,128)(2,1)S(1)}, bf16[5,128,768]{2,1,0:T(8,128)(2,1)S(1)}, u32[]{:S(2)}, u32[]{:S(2)}) collective-permute-start(bf16[5,128,768]{2,1,0:T(8,128)(2,1)S(1)} %constant_dynamic-update-slice_fusion.refs_0_), channel_id=1, source_target_pairs={{0,8},{8,0},{16,24},{24,16},{1,9},{9,1},{17,25},{25,17},{2,10},{10... | collective-permute-start | bytes 2949128 | tf_op jit(solution)/shard_map/ppermute | solution.py:454
  119.3 13.5 %copy-start.11 = (s32[4,3]{1,0:T(4,128)S(1)}, s32[4,3]{1,0:T(4,128)}, u32[]{:S(2)}) copy-start(s32[4,3]{1,0:T(4,128)} %bounds.3) | copy-start | bytes 148
  119.4 13.4 %collective-permute-start.26 = (bf16[5,128,768]{2,1,0:T(8,128)(2,1)S(1)}, bf16[5,128,768]{2,1,0:T(8,128)(2,1)S(1)}, u32[]{:S(2)}, u32[]{:S(2)}) collective-permute-start(bf16[5,128,768]{2,1,0:T(8,128)(2,1)S(1)} %pad_maximum_fusion.refs_2_), channel_id=1, source_target_pairs={{0,8},{8,0},{16,24},{24,16},{1,9},{9,1},{17,25},{25,17},{2,10},{10... | collective-permute-start | bytes 2949128 | tf_op jit(solution)/shard_map/ppermute | solution.py:454
  119.5 11.3 %collective-permute-start.29 = (bf16[3,64,768]{2,1,0:T(8,128)(2,1)S(1)}, bf16[3,64,768]{2,1,0:T(8,128)(2,1)S(1)}, u32[]{:S(2)}, u32[]{:S(2)}) collective-permute-start(bf16[3,64,768]{2,1,0:T(8,128)(2,1)S(1)} %slice.73), channel_id=1, source_target_pairs={{4,0},{5,1},{6,2},{7,3},{12,8},{13,9},{14,10},{15,11},{20,16},{21,... | collective-permute-start | bytes 884744 | tf_op jit(solution)/shard_map/ppermute | solution.py:469
  120.8 10.5 %collective-permute-start.28 = (bf16[3,128,768]{2,1,0:T(8,128)(2,1)S(1)}, bf16[3,128,768]{2,1,0:T(8,128)(2,1)S(1)}, u32[]{:S(2)}, u32[]{:S(2)}) collective-permute-start(bf16[3,128,768]{2,1,0:T(8,128)(2,1)S(1)} %collective-permute-done.27.refs_4_), channel_id=1, source_target_pairs={{0,8},{8,0},{16,24},{24,16},{1,9},{9,1},{17,25},{25,17},{2,10},{10... | collective-permute-start | bytes 1769480 | tf_op jit(solution)/shard_map/ppermute | solution.py:454
  121.4 9.4 %collective-permute-start.31 = (bf16[3,64,768]{2,1,0:T(8,128)(2,1)S(1)}, bf16[3,64,768]{2,1,0:T(8,128)(2,1)S(1)}, u32[]{:S(2)}, u32[]{:S(2)}) collective-permute-start(bf16[3,64,768]{2,1,0:T(8,128)(2,1)S(1)} %slice.74), channel_id=1, source_target_pairs={{0,16},{8,24},{16,0},{24,8},{1,17},{9,25},{17,1},{25,9},{2,18},{10... | collective-permute-start | bytes 884744 | tf_op jit(solution)/shard_map/ppermute | solution.py:454
  130.8 1.6 %collective-permute-start.30 = (bf16[3,64,768]{2,1,0:T(8,128)(2,1)S(1)}, bf16[3,64,768]{2,1,0:T(8,128)(2,1)S(1)}, u32[]{:S(2)}, u32[]{:S(2)}) collective-permute-start(bf16[3,64,768]{2,1,0:T(8,128)(2,1)S(1)} %collective-permute-done.29.refs_6_), channel_id=1, source_target_pairs={{0,8},{8,0},{16,24},{24,16},{1,9},{9,1},{17,25},{25,17},{2,10},{10... | collective-permute-start | bytes 884744 | tf_op jit(solution)/shard_map/ppermute | solution.py:454
  130.8 2.0 %collective-permute-start.32 = (bf16[3,64,768]{2,1,0:T(8,128)(2,1)S(1)}, bf16[3,64,768]{2,1,0:T(8,128)(2,1)S(1)}, u32[]{:S(2)}, u32[]{:S(2)}) collective-permute-start(bf16[3,64,768]{2,1,0:T(8,128)(2,1)S(1)} %collective-permute-done.31.refs_8_), channel_id=1, source_target_pairs={{0,8},{8,0},{16,24},{24,16},{1,9},{9,1},{17,25},{25,17},{2,10},{10... | collective-permute-start | bytes 884744 | tf_op jit(solution)/shard_map/ppermute | solution.py:454

commit v2 on v1

--- a/solution.py
+++ b/solution.py
@@ -53,22 +53,30 @@
     return jnp.sum(x, axis=-1, keepdims=True)
 
 
-def project_kernel(layers, per_micro, steps, bounds, counts, h_in, g_in, down_in, up_in, *refs):
-    out_ref, sq_ref, h_ref, g_ref, weights, sems = refs
+def store_by_layer(out_ref, bounds, layers, pieces):
+    first, after = held_layers(bounds)
+    columns = pieces[0].shape[1]
+    for layer in range(layers):
+        total = jnp.zeros_like(pieces[0])
+        for slot, piece in enumerate(pieces):
+            here = (first + slot == layer) & (layer < after)
+            total = jnp.where(here, piece, total)
+        out_ref[:, layer * columns : (layer + 1) * columns] = total
+
+
+def project_kernel(layers, steps, bounds, h_in, down_in, up_in, *refs):
+    out_ref, sq_ref, h_ref, up_ref, down_ref, sems = refs
     slots, ranks, features = down_in.shape
     tokens = h_ref.shape[0]
     width = features // steps
     copies = []
     for step in range(steps):
         cut = pl.ds(step * width, width)
-        moves = [
-            (h_in.at[:, cut], h_ref.at[:, cut]),
-            (g_in.at[:, cut], g_ref.at[:, cut]),
-        ]
+        moves = [(h_in.at[:, cut], h_ref.at[:, cut])]
         for slot in range(slots):
-            for which, source in enumerate((down_in, up_in)):
-                rows = pl.ds((which * slots + slot) * ranks, ranks)
-                moves.append((source.at[slot, :, cut], weights.at[rows, cut]))
+            rows = pl.ds(slot * ranks, ranks)
+            moves.append((down_in.at[slot, :, cut], down_ref.at[rows, cut]))
+            moves.append((up_in.at[slot, :, cut], up_ref.at[rows, cut]))
         copies.append(
             [
                 pltpu.make_async_copy(source, target, sems.at[step, i])
@@ -78,67 +86,78 @@
         for copy in copies[-1]:
             copy.start()
     ph = jnp.zeros((tokens, 2 * slots * ranks), f32)
-    pg = jnp.zeros((tokens, slots * ranks), f32)
     square = jnp.zeros((tokens, 128), f32)
     for step in range(steps):
         for copy in copies[step]:
             copy.wait()
         cut = pl.ds(step * width, width)
         h = h_ref[:, cut]
-        w = weights[:, cut]
-        ph = ph + dot_last(h, w)
-        pg = pg + dot_last(g_ref[:, cut], w[slots * ranks :])
+        ph = ph + dot_last(h, jnp.concatenate([down_ref[:, cut], up_ref[:, cut]], axis=0))
         wide = h.astype(f32)
         wide = wide * wide
         for lane in range(0, width, 128):
             square = square + wide[:, lane : lane + 128]
     sq_ref[...] = jnp.broadcast_to(row_sum(square), square.shape)
-    first, after = held_layers(bounds)
-    pg = jnp.where(counted_rows(counts, tokens, per_micro), pg, 0.0)
     pieces = []
     for slot in range(slots):
         lo, hi = slot * ranks, (slot + 1) * ranks
-        pieces.append(
-            jnp.concatenate(
-                [ph[:, lo:hi], ph[:, slots * ranks + lo : slots * ranks + hi], pg[:, lo:hi]],
-                axis=1,
-            )
-        )
-    for layer in range(layers):
-        total = jnp.zeros_like(pieces[0])
-        for slot in range(slots):
-            here = (first + slot == layer) & (layer < after)
-            total = jnp.where(here, pieces[slot], total)
-        out_ref[:, layer * 3 * ranks : (layer + 1) * 3 * ranks] = total
-
-
-def project(bounds, counts, hidden, cot, downs, ups, layers, per_micro):
+        up = slots * ranks
+        pieces.append(jnp.concatenate([ph[:, lo:hi], ph[:, up + lo : up + hi]], axis=1))
+    store_by_layer(out_ref, bounds, layers, pieces)
+
+
+def project(bounds, hidden, downs, ups, layers):
     tokens, features = hidden.shape
     slots, ranks, _ = downs.shape
     steps = 8
-    kernel = functools.partial(project_kernel, layers, per_micro, steps)
-    return pl.pallas_call(
-        kernel,
-        in_specs=[in_smem] * 2 + [in_hbm] * 4,
+    sources = [pltpu.with_memory_space_constraint(x, pltpu.HBM) for x in (hidden, downs, ups)]
+    return pl.pallas_call(
+        functools.partial(project_kernel, layers, steps),
+        in_specs=[in_smem] + [in_hbm] * 3,
         out_specs=[in_vmem] * 4,
         out_shape=[
-            jax.ShapeDtypeStruct((tokens, layers * 3 * ranks), f32),
+            jax.ShapeDtypeStruct((tokens, layers * 2 * ranks), f32),
             jax.ShapeDtypeStruct((tokens, 128), f32),
             jax.ShapeDtypeStruct((tokens, features), bf16),
-            jax.ShapeDtypeStruct((tokens, features), bf16),
+            jax.ShapeDtypeStruct((slots * ranks, features), bf16),
         ],
         scratch_shapes=[
-            pltpu.VMEM((2 * slots * ranks, features), bf16),
-            pltpu.SemaphoreType.DMA((steps, 2 + 2 * slots)),
+            pltpu.VMEM((slots * ranks, features), bf16),
+            pltpu.SemaphoreType.DMA((steps, 1 + 2 * slots)),
         ],
         compiler_params=limited,
         cost_estimate=pl.CostEstimate(
-            flops=6 * tokens * slots * ranks * features,
-            bytes_accessed=4 * (tokens + slots * ranks) * features,
+            flops=4 * tokens * slots * ranks * features,
+            bytes_accessed=2 * (tokens + 2 * slots * ranks) * features,
             transcendentals=0,
         ),
         name="project",
-    )(bounds, counts, hidden, cot, downs, ups)
+    )(bounds, *sources)
+
+
+def project_back_kernel(layers, ranks, per_micro, bounds, counts, g_ref, up_ref, out_ref):
+    pg = dot_last(g_ref[...], up_ref[...])
+    pg = jnp.where(counted_rows(counts, pg.shape[0], per_micro), pg, 0.0)
+    slots = pg.shape[1] // ranks
+    pieces = [pg[:, slot * ranks : (slot + 1) * ranks] for slot in range(slots)]
+    store_by_layer(out_ref, bounds, layers, pieces)
+
+
+def project_back(bounds, counts, cot, ups, layers, ranks, per_micro):
+    tokens, features = cot.shape
+    return pl.pallas_call(
+        functools.partial(project_back_kernel, layers, ranks, per_micro),
+        in_specs=[in_smem] * 2 + [in_vmem] * 2,
+        out_specs=in_vmem,
+        out_shape=jax.ShapeDtypeStruct((tokens, layers * ranks), f32),
+        compiler_params=limited,
+        cost_estimate=pl.CostEstimate(
+            flops=2 * tokens * ups.shape[0] * features,
+            bytes_accessed=2 * (tokens + ups.shape[0]) * features,
+            transcendentals=0,
+        ),
+        name="project_back",
+    )(bounds, counts, cot, ups)
 
 
 def gram_kernel(sections, *refs):
@@ -178,26 +197,27 @@
 
 
 def chain_kernel(sections, parts, features, per_micro, counts, *refs):
-    projections = refs[:sections]
-    sq_ref = refs[sections]
-    grams = refs[sections + 1 : sections + 1 + parts]
-    factor_ref, mixed_ref = refs[sections + 1 + parts :]
+    on_hidden, on_cot, grams = refs[:sections], refs[sections : 2 * sections], refs[2 * sections :]
+    sq_ref = grams[parts]
+    factor_ref, mixed_ref = grams[parts + 1 :]
     layers = sections
     section_at = lax.axis_index("section")
     tokens = sq_ref.shape[0]
-    total = projections[0][...]
-    for other in projections[1:]:
-        total = total + other[...]
-    table = grams[0][...]
-    for other in grams[1:]:
-        table = table + other[...]
-    ranks = total.shape[1] // (3 * layers)
+
+    def total(arrays):
+        result = arrays[0][...]
+        for other in arrays[1:]:
+            result = result + other[...]
+        return result
+
+    by_hidden, by_cot, table = total(on_hidden), total(on_cot), total(grams[:parts])
+    ranks = by_cot.shape[1] // layers
     scale_d = 1.0 / math.sqrt(features)
     scale_r = 1.0 / math.sqrt(ranks)
 
     def part(layer, which):
-        at_column = (3 * layer + which) * ranks
-        return total[:, at_column : at_column + ranks]
+        source, block = (by_cot, layer) if which == 2 else (by_hidden, 2 * layer + which)
+        return source[:, block * ranks : (block + 1) * ranks]
 
     def up_down(i, layer):
         return table[i * ranks : (i + 1) * ranks, (layer - 1) * ranks : layer * ranks]
@@ -278,11 +298,11 @@
         mixed_ref[ranks:, cut] = across * (-scale_r * scale_r)
 
 
-def chain(counts, projections, square, grams, features, per_micro):
-    sections = len(projections)
-    tokens, wide = projections[0].shape
-    ranks = wide // (3 * sections)
-    inputs = [*projections, square, *grams]
+def chain(counts, on_hidden, on_cot, grams, square, features, per_micro):
+    sections = len(on_cot)
+    tokens, wide = on_cot[0].shape
+    ranks = wide // sections
+    inputs = [*on_hidden, *on_cot, *grams, square]
     kernel = functools.partial(chain_kernel, sections, len(grams), features, per_micro)
     return pl.pallas_call(
         kernel,
@@ -333,26 +353,19 @@
 def update_kernel(count, *refs):
     pieces = refs[:count]
     mixed_ref, other_ref, right_ref = refs[count : count + 3]
-    state_in = refs[count + 3 : count + 9]
+    state = refs[count + 3 : count + 9]
     outs = refs[count + 9 : count + 15]
-    share_ref, state, sems = refs[count + 15 :]
-    copies = [
-        pltpu.make_async_copy(source.at[0], state.at[i], sems.at[i])
-        for i, source in enumerate(state_in)
-    ]
-    for copy in copies:
-        copy.start()
+    share_ref = refs[count + 15]
     mixed = mixed_ref[...] + other_ref[...]
     grad = jnp.dot(mixed, right_ref[...].astype(f32), preferred_element_type=f32, precision=exact)
     for piece in pieces:
-        grad = grad + piece[...].reshape(grad.shape).astype(f32)
-    for copy in copies:
-        copy.wait()
+        block = piece[(0,) * (len(piece.shape) - 2)] if len(piece.shape) > 2 else piece[...]
+        grad = grad + block.astype(f32)
     ranks = grad.shape[0] // 2
     for which in range(2):
         rows = slice(which * ranks, (which + 1) * ranks)
         own = grad[rows]
-        master, moment, second = (state[2 * kind + which] for kind in range(3))
+        master, moment, second = (state[2 * kind + which][0] for kind in range(3))
         moment = beta_one * moment + (1.0 - beta_one) * own
         second = beta_two * second + (1.0 - beta_two) * own * own
         master = master - learn_rate * (
@@ -366,33 +379,21 @@
 
 def update(pieces, mixed, other, right, state):
     _, ranks, columns = state[0].shape
-
-    def leading(piece):
-        lead = piece.ndim - 2
-        return pl.BlockSpec((1,) * lead + piece.shape[-2:], lambda i: (0,) * piece.ndim)
-
-    whole = [leading(array) for array in (*pieces, mixed, other, right)]
     return pl.pallas_call(
         functools.partial(update_kernel, len(pieces)),
-        grid=(1,),
-        in_specs=whole + [in_hbm] * 6,
-        out_specs=[leading(array) for array in state]
-        + [pl.BlockSpec((2 * ranks, columns), lambda i: (0, 0))],
+        in_specs=[in_vmem] * (len(pieces) + 9),
+        out_specs=[in_vmem] * 7,
         out_shape=[jax.ShapeDtypeStruct(array.shape, f32) for array in state]
         + [jax.ShapeDtypeStruct((2 * ranks, columns), bf16)],
-        scratch_shapes=[
-            pltpu.VMEM((6, ranks, columns), f32),
-            pltpu.SemaphoreType.DMA((6,)),
-        ],
         compiler_params=limited,
         name="update",
     )(*pieces, mixed, other, right, *state)
 
 
-def place_kernel(layout, bounds, *refs):
+def place_kernel(layout, start, bounds, *refs):
     sources = refs[: len(layout)]
-    outs = refs[len(layout) : len(layout) + 2]
-    zeros, sem = refs[len(layout) + 2 :]
+    outs = refs[-4:-2]
+    zeros, sem = refs[-2:]
     slots, ranks, features = outs[0].shape
     columns = zeros.shape[1]
     tensors = lax.axis_size("tensor")
@@ -429,24 +430,32 @@
                 def _():
                     fill(slot, distance, act)
 
-            @pl.when(jnp.logical_not(present))
-            def _():
-                clear(slot, act)
-
-
-def place(bounds, pieces, slots, ranks, features):
+            if start:
+
+                @pl.when(jnp.logical_not(present))
+                def _():
+                    clear(slot, act)
+
+
+def place(bounds, pieces, before, slots, ranks, features):
     layout = [piece[:3] for piece in pieces]
     arrays = [piece[3] for piece in pieces]
     columns = arrays[0].shape[-1]
     return pl.pallas_call(
-        functools.partial(place_kernel, layout),
-        in_specs=[in_smem] + [in_vmem] * len(arrays),
+        functools.partial(place_kernel, layout, not before),
+        in_specs=[in_smem] + [in_vmem] * len(arrays) + [in_hbm] * len(before),
         out_specs=[in_hbm] * 2,
         out_shape=[jax.ShapeDtypeStruct((slots, ranks, features), bf16)] * 2,
         scratch_shapes=[pltpu.VMEM((ranks, columns), bf16), pltpu.SemaphoreType.DMA],
-        compiler_params=limited,
+        input_output_aliases={1 + len(arrays) + i: i for i in range(len(before))},
+        compiler_params=limited,
+        cost_estimate=pl.CostEstimate(
+            flops=0,
+            bytes_accessed=4 * sum(array.size for array in arrays),
+            transcendentals=0,
+        ),
         name="place",
-    )(bounds, *arrays)
+    )(bounds, *arrays, *before)
 
 
 def swapped(block, axis, distance):
@@ -481,7 +490,8 @@
     near = swapped(sent, "replica", 1)
     kept = gradient(factors, hidden, cot, 0, replicas, tensors)
     across = swapped(summed(kept[1, 1:], near[1, 1:]), "replica", 2)
-    last = swapped(summed(kept[1, 0], near[1, 0]), "replica", 2)
+    across, last = lax.optimization_barrier((across, summed(kept[1, 0], near[1, 0])))
+    last = swapped(last, "replica", 2)
     along = [
         swapped(summed(kept[0, k], near[0, k], across[k - 1]), "tensor", k)
         for k in range(1, tensors)
@@ -489,12 +499,16 @@
     return [kept, near, last, *along]
 
 
-def gathered(share):
+def spread(share, bounds, slots, features):
     ranks = share.shape[0] // 2
+    along = swaps(share, "tensor")
     far_one = swapped(share, "replica", 2)
     next_one = following_layer(share)
-    line = jnp.stack(swaps(share, "tensor"))
     next_far_one = following_layer(far_one)
+    along, far_one, next_one, next_far_one = lax.optimization_barrier(
+        (along, far_one, next_one, next_far_one)
+    )
+    line = jnp.stack(along)
     far_line = swapped(line, "replica", 2)
     next_line = following_layer(line)
     near = jnp.concatenate([share[None], far_one[None], line])
@@ -504,18 +518,22 @@
     hops = range(1, lax.axis_size("tensor"))
     near_owners = [(0, 0), (2, 0)] + [(0, hop) for hop in hops]
     far_owners = [(2, hop) for hop in hops]
-    pieces = []
-    for window, rows, owners, block in (
-        (0, (0, 1), near_owners, near),
-        (1, (0, 1), near_owners, next_near),
-        (0, (0, 1), far_owners, far_line),
-        (1, (0,), far_owners, next_far_down),
-        (1, (1,), far_owners, next_far_up),
+    placed = []
+    for group in (
+        (
+            (0, (0, 1), near_owners, near),
+            (0, (0, 1), far_owners, far_line),
+            (1, (0, 1), near_owners, next_near),
+        ),
+        ((1, (0,), far_owners, next_far_down), (1, (1,), far_owners, next_far_up)),
     ):
-        other = [(order ^ 1, hop) for order, hop in owners]
-        pieces.append((window, rows, owners, block))
-        pieces.append((window, rows, other, swapped(block, "replica", 1)))
-    return pieces
+        pieces = []
+        for window, rows, owners, block in group:
+            other = [(order ^ 1, hop) for order, hop in owners]
+            pieces.append((window, rows, owners, block))
+            pieces.append((window, rows, other, swapped(block, "replica", 1)))
+        placed = place(bounds, pieces, placed, slots, ranks, features)
+    return placed
 
 
 def on_device(
@@ -541,17 +559,22 @@
     hidden = inputs.reshape(micros * per_micro, features)
     cot = cotangent.reshape(micros * per_micro, features)
 
-    projected, square, hidden, cot = project(
-        bounds, micro_counts, hidden, cot, holder_down[0, 0], holder_up[0, 0], sections, per_micro
-    )
     owned = jnp.concatenate([master_down[0], master_up[0]], axis=0).astype(bf16)
     around = [from_next(owned, d) for d in range(1, sections)]
-    around, projected = lax.optimization_barrier((around, projected))
+    by_hidden, square, hidden, ups = project(
+        bounds, hidden, holder_down[0, 0], holder_up[0, 0], sections
+    )
+    around, by_hidden = lax.optimization_barrier((around, by_hidden))
     table, right = gram([owned, *around])
-    projections = [projected] + [from_next(projected, d) for d in range(1, sections)]
+    on_hidden = [by_hidden] + [from_next(by_hidden, d) for d in range(1, sections)]
+    table, ups = lax.optimization_barrier((table, ups))
+    by_cot = project_back(
+        bounds, micro_counts, cot, ups, sections, holder_down.shape[3], per_micro
+    )
+    on_cot = [by_cot] + [from_next(by_cot, d) for d in range(1, sections)]
     table = table + sum(swaps(table, "replica"))
     tables = [table] + swaps(table, "tensor")
-    factors, mixed = chain(micro_counts, projections, square, tables, features, per_micro)
+    factors, mixed = chain(micro_counts, on_hidden, on_cot, tables, square, features, per_micro)
 
     pieces = reduced(factors, hidden, cot, replicas, tensors)
     for axis, distance in (("tensor", 1), ("tensor", 2), ("replica", 1)):
@@ -559,7 +582,7 @@
     other = swapped(mixed, "replica", 2)
     state = [master_down, master_up, moment_down, moment_up, second_down, second_up]
     updated = update(pieces, mixed, other, right, state)
-    placed = place(bounds, gathered(updated[6]), slots, holder_down.shape[3], features)
+    placed = spread(updated[6], bounds, slots, features)
     return (placed[0][None, None], placed[1][None, None], *updated[:6])
 
 

time: 136 us -> 124 us (0.912)
  local copies, waits for them, and re-layouts: 9.05 us -> 0.85 us
  waiting for transfers between devices: 74.1 us -> 66.3 us
  starting transfers between devices: 33 us -> 35.7 us
    ppermute x4, waiting for transfers between devices: 25 us -> 16.1 us  [following_layer(): return lax.ppermute(block, 'section', [(i + 1, i) for i in range(size - 1)])]
    unnamed x32 -> x24, local copies, waits for them, and re-layouts: 9 us -> 0.79 us
    ppermute x2 -> x3, starting transfers between devices: 3.31 us -> 5.09 us  [from_next(): return lax.ppermute(block, 'section', route)]
    pallas_call x3 -> x5, Pallas kernels: 13.8 us -> 14.7 us  [the longest x1 6.74 us: project(): pl.pallas_call(functools.partial(project_kernel, layers, steps), in_specs...]
  transfers between devices with their start and end apart: 33 -> 34, of which waited for: 16 -> 14; matrix products, arithmetic and copies ran while one was open for 0% -> 0% of each run, Pallas kernels for 6% -> 10%
where the time goes in v2:
time: 124 us
  waiting for transfers between devices  66.3 us (53%)
  starting transfers between devices  35.7 us (29%)
  Pallas kernels  18.2 us (15%)
  other arithmetic  1.65 us (1%)
    ppermute x27, waiting for transfers between devices, swapped(): return lax.ppermute(block, axis, route)  50.2 us
    ppermute x27, starting transfers between devices, swapped(): return lax.ppermute(block, axis, route)  25.5 us
    ppermute x4, waiting for transfers between devices, following_layer(): return lax.ppermute(block, 'section', [(i + 1, i) for i in range(size - 1)])  16.1 us
    pallas_call x1, Pallas kernels, project(): pl.pallas_call(functools.partial(project_kernel, layers, steps), in_specs...  6.74 us
    ppermute x4, starting transfers between devices, following_layer(): return lax.ppermute(block, 'section', [(i + 1, i) for i in range(size - 1)])  5.15 us
    ppermute x3, starting transfers between devices, from_next(): return lax.ppermute(block, 'section', route)  5.09 us
    pallas_call x2, Pallas kernels, place(): pl.pallas_call(functools.partial(place_kernel, layout, not before), in_sp...  4.48 us
  transfers between devices with their start and end apart: 34, of which 14 were waited for; matrix products, arithmetic and copies ran while one was open for 0% of the time, Pallas kernels for 10%

profile of v2, /device:TPU:0, one launch (start us, length us, event | category | flops | bytes accessed | tf_op | source)
XLA Modules:
  0.0 123.8 jit_solution(8210616762683343138)
XLA Ops:
  0.6 1.0 convert_bitcast_fusion
  1.7 3.0 %collective-permute-start = (bf16[128,768]{1,0:T(8,128)(2,1)S(1)}, bf16[128,768]{1,0:T(8,128)(2,1)S(1)}, u32[]{:S(2)}, u32[]{:S(2)}) collective-permute-start(bf16[128,768]{1,0:T(8,128)(2,1)S(1)} %pad_maximum_fusion.2.refs_0_), channel_id=1, source_target_pairs={{4,0},{0,4},{5,1},{1,5},{6,2},{2,6},{7,3},{3,7},{12,8},{8,12},{13,... | collective-permute-start | bytes 589832 | tf_op jit(solution)/shard_map/ppermute | solution.py:473
  4.7 0.7 copy-done.7
  5.4 6.7 %project.1 = (f32[128,256]{1,0:T(8,128)S(1)}, f32[128,128]{1,0:T(8,128)S(1)}, bf16[128,12288]{1,0:T(8,128)(2,1)S(1)}, bf16[128,12288]{1,0:T(8,128)(2,1)S(1)}) custom-call(s32[4,3]{1,0:T(4,128)S(1)} %copy-done.7, bf16[128,12288]{1,0:T(8,128)(2,1)} %bitcast.44, bf16[2,64,12288]{2,1,0:T(8,128)(2,1)} %bitcast.45, bf16[2,64,12288]{2,1,0:T(8,128)(2,1)} %bitcast.46), custom_call_target="tpu_custom_call" | custom-call | flops 805306368 | bytes 9437184 | tf_op jit(solution)/shard_map/project/pallas_call | solution.py:114
  12.3 0.7 collective-permute-start.5
  13.1 0.9 collective-permute-start.4
  14.3 1.7 %project_back.1.refs_2_ = f32[128,128]{1,0:T(8,128)S(1)} custom-call(s32[4,3]{1,0:T(4,128)S(1)} %copy-done.7, s32[4]{0:T(128)S(1)} %copy-done.9, bf16[128,12288]{1,0:T(8,128)(2,1)S(1)} %bitcast.41, bf16[128,12288]{1,0:T(8,128)(2,1)S(1)} %get-tuple-element.44.up_ref), custom_call_target="tpu_custom_call" | custom-call | flops 402653184 | bytes 6291456 | tf_op jit(solution)/shard_map/project_back/pallas_call | solution.py:148
  16.0 0.4 collective-permute-start.2
  16.3 1.7 %collective-permute-start.1 = (f32[128,256]{1,0:T(8,128)S(1)}, f32[128,256]{1,0:T(8,128)S(1)}, u32[]{:S(2)}, u32[]{:S(2)}) collective-permute-start(f32[128,256]{1,0:T(8,128)S(1)} %get-tuple-element.40.refs_0_), channel_id=1, source_target_pairs={{4,0},{0,4},{5,1},{1,5},{6,2},{2,6},{7,3},{3,7},{12,8},{8,12},{13,... | collective-permute-start | bytes 393224 | tf_op jit(solution)/shard_map/ppermute | solution.py:473
  18.1 3.7 %collective-permute-start.8 = (f32[64,128]{1,0:T(8,128)S(1)}, f32[64,128]{1,0:T(8,128)S(1)}, u32[]{:S(2)}, u32[]{:S(2)}) collective-permute-start(f32[64,128]{1,0:T(8,128)S(1)} %add_add_fusion.refs_4_), channel_id=1, source_target_pairs={{0,3},{1,2},{2,1},{3,0},{4,7},{5,6},{6,5},{7,4},{8,11},{9,10},{10,... | collective-permute-start | bytes 98312 | tf_op jit(solution)/shard_map/ppermute | solution.py:463
  21.8 0.8 collective-permute-start.6
  22.5 1.5 %collective-permute-done.8.refs_7_ = f32[64,128]{1,0:T(8,128)S(1)} collective-permute-done((f32[64,128]{1,0:T(8,128)S(1)}, f32[64,128]{1,0:T(8,128)S(1)}, u32[]{:S(2)}, u32[]{:S(2)}) %collective-permute-start.8) | collective-permute-done | bytes 32800 | tf_op jit(solution)/shard_map/ppermute | solution.py:463
  24.1 2.5 %collective-permute-done.7.refs_6_ = f32[64,128]{1,0:T(8,128)S(1)} collective-permute-done((f32[64,128]{1,0:T(8,128)S(1)}, f32[64,128]{1,0:T(8,128)S(1)}, u32[]{:S(2)}, u32[]{:S(2)}) %collective-permute-start.7) | collective-permute-done | bytes 32800 | tf_op jit(solution)/shard_map/ppermute | solution.py:463
  26.6 2.1 %chain.1 = (bf16[128,256]{1,0:T(8,128)(2,1)S(1)}, f32[128,128]{1,0:T(8,128)S(1)}) custom-call(s32[4]{0:T(128)S(1)} %copy-done.9, f32[128,256]{1,0:T(8,128)S(1)} %get-tuple-element.40.refs_0_, f32[128,256]{1,0:T(8,128)S(1)} %collective-permute-done.1.refs_1_, f32[128,128]{1,0:T(8,128)S(1)} %project_back.1.refs_2_, ...), custom_call_target="tpu_custom_call" | custom-call | tf_op jit(solution)/shard_map/chain/pallas_call | solution.py:307
  28.7 0.6 gradient.3
  29.4 0.6 gradient.2.refs_0_
  30.0 2.8 %collective-permute-done.9.refs_1_ = bf16[2,4,128,768]{3,2,1,0:T(8,128)(2,1)S(1)} collective-permute-done((bf16[2,4,128,768]{3,2,1,0:T(8,128)(2,1)S(1)}, bf16[2,4,128,768]{3,2,1,0:T(8,128)(2,1)S(1)}, u32[]{:S(2)}, u32[]{:S(2)}) %collective-permute-start.9) | collective-permute-done | bytes 1572896 | tf_op jit(solution)/shard_map/ppermute | solution.py:463
  32.9 1.6 %collective-permute-start.10 = (bf16[3,128,768]{2,1,0:T(8,128)(2,1)S(1)}, bf16[3,128,768]{2,1,0:T(8,128)(2,1)S(1)}, u32[]{:S(2)}, u32[]{:S(2)}) collective-permute-start(bf16[3,128,768]{2,1,0:T(8,128)(2,1)S(1)} %fusion), channel_id=1, source_target_pairs={{0,16},{8,24},{16,0},{24,8},{1,17},{9,25},{17,1},{25,9},{2,18},{10... | collective-permute-start | bytes 1769480 | tf_op jit(solution)/shard_map/ppermute | solution.py:463
  34.5 4.3 %collective-permute-done.15 = f32[128,128]{1,0:T(8,128)S(1)} collective-permute-done((f32[128,128]{1,0:T(8,128)S(1)}, f32[128,128]{1,0:T(8,128)S(1)}, u32[]{:S(2)}, u32[]{:S(2)}) %collective-permute-start.15) | collective-permute-done | bytes 65568 | tf_op jit(solution)/shard_map/ppermute | solution.py:463
  38.9 2.1 %collective-permute-start.16 = (f32[128,128]{1,0:T(8,128)S(1)}, f32[128,128]{1,0:T(8,128)S(1)}, u32[]{:S(2)}, u32[]{:S(2)}) collective-permute-start(f32[128,128]{1,0:T(8,128)S(1)} %add.67), channel_id=1, source_target_pairs={{0,2},{1,3},{2,0},{3,1},{4,6},{5,7},{6,4},{7,5},{8,10},{9,11},{10,... | collective-permute-start | bytes 196616 | tf_op jit(solution)/shard_map/ppermute | solution.py:463
  41.0 7.4 %collective-permute-done.10 = bf16[3,128,768]{2,1,0:T(8,128)(2,1)S(1)} collective-permute-done((bf16[3,128,768]{2,1,0:T(8,128)(2,1)S(1)}, bf16[3,128,768]{2,1,0:T(8,128)(2,1)S(1)}, u32[]{:S(2)}, u32[]{:S(2)}) %collective-permute-start.10) | collective-permute-done | bytes 589856 | tf_op jit(solution)/shard_map/ppermute | solution.py:463
  48.4 1.5 %collective-permute-start.11 = (bf16[128,768]{1,0:T(8,128)(2,1)S(1)}, bf16[128,768]{1,0:T(8,128)(2,1)S(1)}, u32[]{:S(2)}, u32[]{:S(2)}) collective-permute-start(bf16[128,768]{1,0:T(8,128)(2,1)S(1)} %fusion.4), channel_id=1, source_target_pairs={{0,16},{8,24},{16,0},{24,8},{1,17},{9,25},{17,1},{25,9},{2,18},{10... | collective-permute-start | bytes 589832 | tf_op jit(solution)/shard_map/ppermute | solution.py:463
  50.1 1.5 %collective-permute-start.14 = (bf16[128,768]{1,0:T(8,128)(2,1)S(1)}, bf16[128,768]{1,0:T(8,128)(2,1)S(1)}, u32[]{:S(2)}, u32[]{:S(2)}) collective-permute-start(bf16[128,768]{1,0:T(8,128)(2,1)S(1)} %get-tuple-element.70), channel_id=1, source_target_pairs={{0,3},{1,2},{2,1},{3,0},{4,7},{5,6},{6,5},{7,4},{8,11},{9,10},{10,... | collective-permute-start | bytes 589832 | tf_op jit(solution)/shard_map/ppermute | solution.py:463
  51.6 0.6 collective-permute-start.13
  52.3 2.3 %collective-permute-start.12 = (bf16[128,768]{1,0:T(8,128)(2,1)S(1)}, bf16[128,768]{1,0:T(8,128)(2,1)S(1)}, u32[]{:S(2)}, u32[]{:S(2)}) collective-permute-start(bf16[128,768]{1,0:T(8,128)(2,1)S(1)} %get-tuple-element.72), channel_id=1, source_target_pairs={{0,1},{1,0},{2,3},{3,2},{4,5},{5,4},{6,7},{7,6},{8,9},{9,8},{10,11... | collective-permute-start | bytes 589832 | tf_op jit(solution)/shard_map/ppermute | solution.py:463
  54.7 1.2 %collective-permute-done.17 = f32[128,128]{1,0:T(8,128)S(1)} collective-permute-done((f32[128,128]{1,0:T(8,128)S(1)}, f32[128,128]{1,0:T(8,128)S(1)}, u32[]{:S(2)}, u32[]{:S(2)}) %collective-permute-start.17) | collective-permute-done | bytes 65568 | tf_op jit(solution)/shard_map/ppermute | solution.py:463
  55.9 0.6 collective-permute-start.18
  56.5 3.8 %collective-permute-done.18.refs_7_ = f32[128,128]{1,0:T(8,128)S(1)} collective-permute-done((f32[128,128]{1,0:T(8,128)S(1)}, f32[128,128]{1,0:T(8,128)S(1)}, u32[]{:S(2)}, u32[]{:S(2)}) %collective-permute-start.18) | collective-permute-done | bytes 65568 | tf_op jit(solution)/shard_map/ppermute | solution.py:463
  60.2 8.7 %collective-permute-done.13.refs_4_ = bf16[128,768]{1,0:T(8,128)(2,1)S(1)} collective-permute-done((bf16[128,768]{1,0:T(8,128)(2,1)S(1)}, bf16[128,768]{1,0:T(8,128)(2,1)S(1)}, u32[]{:S(2)}, u32[]{:S(2)}) %collective-permute-start.13) | collective-permute-done | bytes 196640 | tf_op jit(solution)/shard_map/ppermute | solution.py:463
  69.0 1.8 %update.1 = (f32[1,64,768]{2,1,0:T(8,128)}, f32[1,64,768]{2,1,0:T(8,128)}, f32[1,64,768]{2,1,0:T(8,128)}, f32[1,64,768]{2,1,0:T(8,128)}, f32[1,64,768]{2,1,0:T(8...) custom-call(bf16[2,4,128,768]{3,2,1,0:T(8,128)(2,1)S(1)} %gradient.2.refs_0_, ...), custom_call_target="tpu_custom_call" | custom-call | tf_op jit(solution)/shard_map/update/pallas_call | solution.py:382
  70.8 0.5 collective-permute-start.22
  71.3 1.3 %collective-permute-start.23 = (bf16[128,768]{1,0:T(8,128)(2,1)S(1)}, bf16[128,768]{1,0:T(8,128)(2,1)S(1)}, u32[]{:S(2)}, u32[]{:S(2)}) collective-permute-start(bf16[128,768]{1,0:T(8,128)(2,1)S(1)} %get-tuple-element.53), channel_id=1, source_target_pairs={{4,0},{5,1},{6,2},{7,3},{12,8},{13,9},{14,10},{15,11},{20,16},{21,... | collective-permute-start | bytes 589832 | tf_op jit(solution)/shard_map/ppermute | solution.py:478
  72.6 2.7 %collective-permute-start.21 = (bf16[128,768]{1,0:T(8,128)(2,1)S(1)}, bf16[128,768]{1,0:T(8,128)(2,1)S(1)}, u32[]{:S(2)}, u32[]{:S(2)}) collective-permute-start(bf16[128,768]{1,0:T(8,128)(2,1)S(1)} %get-tuple-element.53), channel_id=1, source_target_pairs={{0,3},{1,2},{2,1},{3,0},{4,7},{5,6},{6,5},{7,4},{8,11},{9,10},{10,... | collective-permute-start | bytes 589832 | tf_op jit(solution)/shard_map/ppermute | solution.py:463
  75.3 1.7 %collective-permute-start.19 = (bf16[128,768]{1,0:T(8,128)(2,1)S(1)}, bf16[128,768]{1,0:T(8,128)(2,1)S(1)}, u32[]{:S(2)}, u32[]{:S(2)}) collective-permute-start(bf16[128,768]{1,0:T(8,128)(2,1)S(1)} %get-tuple-element.53), channel_id=1, source_target_pairs={{0,1},{1,0},{2,3},{3,2},{4,5},{5,4},{6,7},{7,6},{8,9},{9,8},{10,11... | collective-permute-start | bytes 589832 | tf_op jit(solution)/shard_map/ppermute | solution.py:463
  77.0 1.3 %collective-permute-start.24 = (bf16[128,768]{1,0:T(8,128)(2,1)S(1)}, bf16[128,768]{1,0:T(8,128)(2,1)S(1)}, u32[]{:S(2)}, u32[]{:S(2)}) collective-permute-start(bf16[128,768]{1,0:T(8,128)(2,1)S(1)} %collective-permute-done.22), channel_id=1, source_target_pairs={{4,0},{5,1},{6,2},{7,3},{12,8},{13,9},{14,10},{15,11},{20,16},{21,... | collective-permute-start | bytes 589832 | tf_op jit(solution)/shard_map/ppermute | solution.py:478
  78.3 0.5 collective-permute-done.23
  78.8 3.4 %collective-permute-done.21 = bf16[128,768]{1,0:T(8,128)(2,1)S(1)} collective-permute-done((bf16[128,768]{1,0:T(8,128)(2,1)S(1)}, bf16[128,768]{1,0:T(8,128)(2,1)S(1)}, u32[]{:S(2)}, u32[]{:S(2)}) %collective-permute-start.21) | collective-permute-done | bytes 196640 | tf_op jit(solution)/shard_map/ppermute | solution.py:463
  82.3 8.4 %collective-permute-done.20 = bf16[128,768]{1,0:T(8,128)(2,1)S(1)} collective-permute-done((bf16[128,768]{1,0:T(8,128)(2,1)S(1)}, bf16[128,768]{1,0:T(8,128)(2,1)S(1)}, u32[]{:S(2)}, u32[]{:S(2)}) %collective-permute-start.20) | collective-permute-done | bytes 196640 | tf_op jit(solution)/shard_map/ppermute | solution.py:463
  90.8 1.3 %collective-permute-start.28 = (bf16[3,128,768]{2,1,0:T(8,128)(2,1)S(1)}, bf16[3,128,768]{2,1,0:T(8,128)(2,1)S(1)}, u32[]{:S(2)}, u32[]{:S(2)}) collective-permute-start(bf16[3,128,768]{2,1,0:T(8,128)(2,1)S(1)} %pad_maximum_fusion.1), channel_id=1, source_target_pairs={{4,0},{5,1},{6,2},{7,3},{12,8},{13,9},{14,10},{15,11},{20,16},{21,... | collective-permute-start | bytes 1769480 | tf_op jit(solution)/shard_map/ppermute | solution.py:478
  92.1 1.6 %collective-permute-start.25 = (bf16[3,128,768]{2,1,0:T(8,128)(2,1)S(1)}, bf16[3,128,768]{2,1,0:T(8,128)(2,1)S(1)}, u32[]{:S(2)}, u32[]{:S(2)}) collective-permute-start(bf16[3,128,768]{2,1,0:T(8,128)(2,1)S(1)} %pad_maximum_fusion.1), channel_id=1, source_target_pairs={{0,16},{8,24},{16,0},{24,8},{1,17},{9,25},{17,1},{25,9},{2,18},{10... | collective-permute-start | bytes 1769480 | tf_op jit(solution)/shard_map/ppermute | solution.py:463
  93.8 12.5 %collective-permute-done.28 = bf16[3,128,768]{2,1,0:T(8,128)(2,1)S(1)} collective-permute-done((bf16[3,128,768]{2,1,0:T(8,128)(2,1)S(1)}, bf16[3,128,768]{2,1,0:T(8,128)(2,1)S(1)}, u32[]{:S(2)}, u32[]{:S(2)}) %collective-permute-start.28) | collective-permute-done | bytes 589856 | tf_op jit(solution)/shard_map/ppermute | solution.py:478
  106.5 0.6 collective-permute-start.32
  107.1 1.5 %collective-permute-start.29 = (bf16[3,64,768]{2,1,0:T(8,128)(2,1)S(1)}, bf16[3,64,768]{2,1,0:T(8,128)(2,1)S(1)}, u32[]{:S(2)}, u32[]{:S(2)}) collective-permute-start(bf16[3,64,768]{2,1,0:T(8,128)(2,1)S(1)} %slice.71), channel_id=1, source_target_pairs={{0,16},{8,24},{16,0},{24,8},{1,17},{9,25},{17,1},{25,9},{2,18},{10... | collective-permute-start | bytes 884744 | tf_op jit(solution)/shard_map/ppermute | solution.py:463
  108.6 1.3 %collective-permute-start.26 = (bf16[3,64,768]{2,1,0:T(8,128)(2,1)S(1)}, bf16[3,64,768]{2,1,0:T(8,128)(2,1)S(1)}, u32[]{:S(2)}, u32[]{:S(2)}) collective-permute-start(bf16[3,64,768]{2,1,0:T(8,128)(2,1)S(1)} %slice.70), channel_id=1, source_target_pairs={{4,0},{5,1},{6,2},{7,3},{12,8},{13,9},{14,10},{15,11},{20,16},{21,... | collective-permute-start | bytes 884744 | tf_op jit(solution)/shard_map/ppermute | solution.py:478
  109.9 6.2 %collective-permute-done.29.refs_2_ = bf16[3,64,768]{2,1,0:T(8,128)(2,1)S(1)} collective-permute-done((bf16[3,64,768]{2,1,0:T(8,128)(2,1)S(1)}, bf16[3,64,768]{2,1,0:T(8,128)(2,1)S(1)}, u32[]{:S(2)}, u32[]{:S(2)}) %collective-permute-start.29) | collective-permute-done | bytes 294944 | tf_op jit(solution)/shard_map/ppermute | solution.py:463
  116.1 3.2 %collective-permute-done.26.refs_0_ = bf16[3,64,768]{2,1,0:T(8,128)(2,1)S(1)} collective-permute-done((bf16[3,64,768]{2,1,0:T(8,128)(2,1)S(1)}, bf16[3,64,768]{2,1,0:T(8,128)(2,1)S(1)}, u32[]{:S(2)}, u32[]{:S(2)}) %collective-permute-start.26) | collective-permute-done | bytes 294944 | tf_op jit(solution)/shard_map/ppermute | solution.py:478
  119.3 2.9 %place.2 = (bf16[2,64,12288]{2,1,0:T(8,128)(2,1)}, bf16[2,64,12288]{2,1,0:T(8,128)(2,1)}) custom-call(s32[4,3]{1,0:T(4,128)S(1)} %copy-done.8, bf16[5,128,768]{2,1,0:T(8,128)(2,1)S(1)} %constant_dynamic-update-slice_fusion.refs_0_, bf16[5,128,768]{2,1,0:T(8,128)(2,1)S(1)} %collective-permute-done.31.refs_1_, ...), custom_call_target="tpu_custom_call" | custom-call | bytes 10223616 | tf_op jit(solution)/shard_map/place/pallas_call | solution.py:444
  122.1 1.6 %place.3 = (bf16[2,64,12288]{2,1,0:T(8,128)(2,1)}, bf16[2,64,12288]{2,1,0:T(8,128)(2,1)}) custom-call(s32[4,3]{1,0:T(4,128)S(1)} %copy-done.8, bf16[3,64,768]{2,1,0:T(8,128)(2,1)S(1)} %collective-permute-done.26.refs_0_, bf16[3,64,768]{2,1,0:T(8,128)(2,1)S(1)} %collective-permute-done.27.refs_1_, ...), custom_call_target="tpu_custom_call", output_to_operand_aliasing={{0}: (5, {}), {1}: (6, {})} | custom-call | bytes 2359296 | tf_op jit(solution)/shard_map/place/pallas_call | solution.py:444
  (67 shorter events, 1.6 us)
Async XLA Ops:
  1.7 10.4 %collective-permute-start = (bf16[128,768]{1,0:T(8,128)(2,1)S(1)}, bf16[128,768]{1,0:T(8,128)(2,1)S(1)}, u32[]{:S(2)}, u32[]{:S(2)}) collective-permute-start(bf16[128,768]{1,0:T(8,128)(2,1)S(1)} %pad_maximum_fusion.2.refs_0_), channel_id=1, source_target_pairs={{4,0},{0,4},{5,1},{1,5},{6,2},{2,6},{7,3},{3,7},{12,8},{8,12},{13,... | collective-permute-start | bytes 589832 | tf_op jit(solution)/shard_map/ppermute | solution.py:473
  4.7 0.7 copy-start.7
  5.4 8.9 %copy-start = (bf16[1,4,32,12288]{3,2,1,0:T(8,128)(2,1)S(1)}, bf16[1,4,32,12288]{3,2,1,0:T(8,128)(2,1)}, u32[]{:S(2)}) copy-start(bf16[1,4,32,12288]{3,2,1,0:T(8,128)(2,1)} %param.13) | copy-start | bytes 9437188
  5.4 8.9 %copy-start.9 = (s32[4]{0:T(128)S(1)}, s32[4]{0:T(128)}, u32[]{:S(2)}) copy-start(s32[4]{0:T(128)} %counts.3) | copy-start | bytes 52
  12.3 5.7 %collective-permute-start.5 = (f32[64,128]{1,0:T(8,128)S(1)}, f32[64,128]{1,0:T(8,128)S(1)}, u32[]{:S(2)}, u32[]{:S(2)}) collective-permute-start(f32[64,128]{1,0:T(8,128)S(1)} %get-tuple-element.45), channel_id=1, source_target_pairs={{0,24},{8,16},{16,8},{24,0},{1,25},{9,17},{17,9},{25,1},{2,26},{10... | collective-permute-start | bytes 98312 | tf_op jit(solution)/shard_map/ppermute | solution.py:463
  13.1 5.0 %collective-permute-start.4 = (f32[64,128]{1,0:T(8,128)S(1)}, f32[64,128]{1,0:T(8,128)S(1)}, u32[]{:S(2)}, u32[]{:S(2)}) collective-permute-start(f32[64,128]{1,0:T(8,128)S(1)} %get-tuple-element.45), channel_id=1, source_target_pairs={{0,16},{8,24},{16,0},{24,8},{1,17},{9,25},{17,1},{25,9},{2,18},{10... | collective-permute-start | bytes 98312 | tf_op jit(solution)/shard_map/ppermute | solution.py:463
  14.0 4.1 %collective-permute-start.3 = (f32[64,128]{1,0:T(8,128)S(1)}, f32[64,128]{1,0:T(8,128)S(1)}, u32[]{:S(2)}, u32[]{:S(2)}) collective-permute-start(f32[64,128]{1,0:T(8,128)S(1)} %get-tuple-element.45), channel_id=1, source_target_pairs={{0,8},{8,0},{16,24},{24,16},{1,9},{9,1},{17,25},{25,17},{2,10},{10... | collective-permute-start | bytes 98312 | tf_op jit(solution)/shard_map/ppermute | solution.py:463
  16.0 10.6 %collective-permute-start.2 = (f32[128,128]{1,0:T(8,128)S(1)}, f32[128,128]{1,0:T(8,128)S(1)}, u32[]{:S(2)}, u32[]{:S(2)}) collective-permute-start(f32[128,128]{1,0:T(8,128)S(1)} %project_back.1.refs_2_), channel_id=1, source_target_pairs={{4,0},{0,4},{5,1},{1,5},{6,2},{2,6},{7,3},{3,7},{12,8},{8,12},{13,... | collective-permute-start | bytes 196616 | tf_op jit(solution)/shard_map/ppermute | solution.py:473
  16.3 10.2 %collective-permute-start.1 = (f32[128,256]{1,0:T(8,128)S(1)}, f32[128,256]{1,0:T(8,128)S(1)}, u32[]{:S(2)}, u32[]{:S(2)}) collective-permute-start(f32[128,256]{1,0:T(8,128)S(1)} %get-tuple-element.40.refs_0_), channel_id=1, source_target_pairs={{4,0},{0,4},{5,1},{1,5},{6,2},{2,6},{7,3},{3,7},{12,8},{8,12},{13,... | collective-permute-start | bytes 393224 | tf_op jit(solution)/shard_map/ppermute | solution.py:473
  18.1 6.0 %collective-permute-start.8 = (f32[64,128]{1,0:T(8,128)S(1)}, f32[64,128]{1,0:T(8,128)S(1)}, u32[]{:S(2)}, u32[]{:S(2)}) collective-permute-start(f32[64,128]{1,0:T(8,128)S(1)} %add_add_fusion.refs_4_), channel_id=1, source_target_pairs={{0,3},{1,2},{2,1},{3,0},{4,7},{5,6},{6,5},{7,4},{8,11},{9,10},{10,... | collective-permute-start | bytes 98312 | tf_op jit(solution)/shard_map/ppermute | solution.py:463
  21.7 4.8 %collective-permute-start.7 = (f32[64,128]{1,0:T(8,128)S(1)}, f32[64,128]{1,0:T(8,128)S(1)}, u32[]{:S(2)}, u32[]{:S(2)}) collective-permute-start(f32[64,128]{1,0:T(8,128)S(1)} %add_add_fusion.refs_4_), channel_id=1, source_target_pairs={{0,2},{1,3},{2,0},{3,1},{4,6},{5,7},{6,4},{7,5},{8,10},{9,11},{10,... | collective-permute-start | bytes 98312 | tf_op jit(solution)/shard_map/ppermute | solution.py:463
  21.8 4.8 %collective-permute-start.6 = (f32[64,128]{1,0:T(8,128)S(1)}, f32[64,128]{1,0:T(8,128)S(1)}, u32[]{:S(2)}, u32[]{:S(2)}) collective-permute-start(f32[64,128]{1,0:T(8,128)S(1)} %add_add_fusion.refs_4_), channel_id=1, source_target_pairs={{0,1},{1,0},{2,3},{3,2},{4,5},{5,4},{6,7},{7,6},{8,9},{9,8},{10,11... | collective-permute-start | bytes 98312 | tf_op jit(solution)/shard_map/ppermute | solution.py:463
  29.3 3.5 %collective-permute-start.9 = (bf16[2,4,128,768]{3,2,1,0:T(8,128)(2,1)S(1)}, bf16[2,4,128,768]{3,2,1,0:T(8,128)(2,1)S(1)}, u32[]{:S(2)}, u32[]{:S(2)}) collective-permute-start(bf16[2,4,128,768]{3,2,1,0:T(8,128)(2,1)S(1)} %gradient.3), channel_id=1, source_target_pairs={{0,8},{8,0},{16,24},{24,16},{1,9},{9,1},{17,25},{25,17},{2,10},{10... | collective-permute-start | bytes 4718600 | tf_op jit(solution)/shard_map/ppermute | solution.py:463
  32.9 15.4 %collective-permute-start.10 = (bf16[3,128,768]{2,1,0:T(8,128)(2,1)S(1)}, bf16[3,128,768]{2,1,0:T(8,128)(2,1)S(1)}, u32[]{:S(2)}, u32[]{:S(2)}) collective-permute-start(bf16[3,128,768]{2,1,0:T(8,128)(2,1)S(1)} %fusion), channel_id=1, source_target_pairs={{0,16},{8,24},{16,0},{24,8},{1,17},{9,25},{17,1},{25,9},{2,18},{10... | collective-permute-start | bytes 1769480 | tf_op jit(solution)/shard_map/ppermute | solution.py:463
  34.5 4.3 %collective-permute-start.15 = (f32[128,128]{1,0:T(8,128)S(1)}, f32[128,128]{1,0:T(8,128)S(1)}, u32[]{:S(2)}, u32[]{:S(2)}) collective-permute-start(f32[128,128]{1,0:T(8,128)S(1)} %get-tuple-element.51), channel_id=1, source_target_pairs={{0,1},{1,0},{2,3},{3,2},{4,5},{5,4},{6,7},{7,6},{8,9},{9,8},{10,11... | collective-permute-start | bytes 196616 | tf_op jit(solution)/shard_map/ppermute | solution.py:463
  38.8 30.1 %copy-start.1 = (f32[1,64,768]{2,1,0:T(8,128)S(1)}, f32[1,64,768]{2,1,0:T(8,128)}, u32[]{:S(2)}) copy-start(f32[1,64,768]{2,1,0:T(8,128)} %refs_10_.1) | copy-start | bytes 589828
  38.8 30.1 %copy-start.2 = (f32[1,64,768]{2,1,0:T(8,128)S(1)}, f32[1,64,768]{2,1,0:T(8,128)}, u32[]{:S(2)}) copy-start(f32[1,64,768]{2,1,0:T(8,128)} %refs_9_.1) | copy-start | bytes 589828
  38.8 30.1 %copy-start.3 = (f32[1,64,768]{2,1,0:T(8,128)S(1)}, f32[1,64,768]{2,1,0:T(8,128)}, u32[]{:S(2)}) copy-start(f32[1,64,768]{2,1,0:T(8,128)} %refs_11_.1) | copy-start | bytes 589828
  38.8 30.1 %copy-start.4 = (f32[1,64,768]{2,1,0:T(8,128)S(1)}, f32[1,64,768]{2,1,0:T(8,128)}, u32[]{:S(2)}) copy-start(f32[1,64,768]{2,1,0:T(8,128)} %refs_12_.1) | copy-start | bytes 589828
  38.8 30.1 %copy-start.5 = (f32[1,64,768]{2,1,0:T(8,128)S(1)}, f32[1,64,768]{2,1,0:T(8,128)}, u32[]{:S(2)}) copy-start(f32[1,64,768]{2,1,0:T(8,128)} %refs_13_.1) | copy-start | bytes 589828
  38.9 30.1 %copy-start.6 = (f32[1,64,768]{2,1,0:T(8,128)S(1)}, f32[1,64,768]{2,1,0:T(8,128)}, u32[]{:S(2)}) copy-start(f32[1,64,768]{2,1,0:T(8,128)} %refs_14_.1) | copy-start | bytes 589828
  38.9 15.7 %collective-permute-start.16 = (f32[128,128]{1,0:T(8,128)S(1)}, f32[128,128]{1,0:T(8,128)S(1)}, u32[]{:S(2)}, u32[]{:S(2)}) collective-permute-start(f32[128,128]{1,0:T(8,128)S(1)} %add.67), channel_id=1, source_target_pairs={{0,2},{1,3},{2,0},{3,1},{4,6},{5,7},{6,4},{7,5},{8,10},{9,11},{10,... | collective-permute-start | bytes 196616 | tf_op jit(solution)/shard_map/ppermute | solution.py:463
  48.4 11.9 %collective-permute-start.11 = (bf16[128,768]{1,0:T(8,128)(2,1)S(1)}, bf16[128,768]{1,0:T(8,128)(2,1)S(1)}, u32[]{:S(2)}, u32[]{:S(2)}) collective-permute-start(bf16[128,768]{1,0:T(8,128)(2,1)S(1)} %fusion.4), channel_id=1, source_target_pairs={{0,16},{8,24},{16,0},{24,8},{1,17},{9,25},{17,1},{25,9},{2,18},{10... | collective-permute-start | bytes 589832 | tf_op jit(solution)/shard_map/ppermute | solution.py:463
  50.1 10.1 %collective-permute-start.14 = (bf16[128,768]{1,0:T(8,128)(2,1)S(1)}, bf16[128,768]{1,0:T(8,128)(2,1)S(1)}, u32[]{:S(2)}, u32[]{:S(2)}) collective-permute-start(bf16[128,768]{1,0:T(8,128)(2,1)S(1)} %get-tuple-element.70), channel_id=1, source_target_pairs={{0,3},{1,2},{2,1},{3,0},{4,7},{5,6},{6,5},{7,4},{8,11},{9,10},{10,... | collective-permute-start | bytes 589832 | tf_op jit(solution)/shard_map/ppermute | solution.py:463
  51.6 17.3 %collective-permute-start.13 = (bf16[128,768]{1,0:T(8,128)(2,1)S(1)}, bf16[128,768]{1,0:T(8,128)(2,1)S(1)}, u32[]{:S(2)}, u32[]{:S(2)}) collective-permute-start(bf16[128,768]{1,0:T(8,128)(2,1)S(1)} %get-tuple-element.71), channel_id=1, source_target_pairs={{0,2},{1,3},{2,0},{3,1},{4,6},{5,7},{6,4},{7,5},{8,10},{9,11},{10,... | collective-permute-start | bytes 589832 | tf_op jit(solution)/shard_map/ppermute | solution.py:463
  52.3 16.7 %collective-permute-start.12 = (bf16[128,768]{1,0:T(8,128)(2,1)S(1)}, bf16[128,768]{1,0:T(8,128)(2,1)S(1)}, u32[]{:S(2)}, u32[]{:S(2)}) collective-permute-start(bf16[128,768]{1,0:T(8,128)(2,1)S(1)} %get-tuple-element.72), channel_id=1, source_target_pairs={{0,1},{1,0},{2,3},{3,2},{4,5},{5,4},{6,7},{7,6},{8,9},{9,8},{10,11... | collective-permute-start | bytes 589832 | tf_op jit(solution)/shard_map/ppermute | solution.py:463
  54.6 1.3 %collective-permute-start.17 = (f32[128,128]{1,0:T(8,128)S(1)}, f32[128,128]{1,0:T(8,128)S(1)}, u32[]{:S(2)}, u32[]{:S(2)}) collective-permute-start(f32[128,128]{1,0:T(8,128)S(1)} %add.68), channel_id=1, source_target_pairs={{0,8},{8,0},{16,24},{24,16},{1,9},{9,1},{17,25},{25,17},{2,10},{10... | collective-permute-start | bytes 196616 | tf_op jit(solution)/shard_map/ppermute | solution.py:463
  55.9 4.3 %collective-permute-start.18 = (f32[128,128]{1,0:T(8,128)S(1)}, f32[128,128]{1,0:T(8,128)S(1)}, u32[]{:S(2)}, u32[]{:S(2)}) collective-permute-start(f32[128,128]{1,0:T(8,128)S(1)} %add.69.refs_6_), channel_id=1, source_target_pairs={{0,16},{8,24},{16,0},{24,8},{1,17},{9,25},{17,1},{25,9},{2,18},{10... | collective-permute-start | bytes 196616 | tf_op jit(solution)/shard_map/ppermute | solution.py:463
  70.8 6.3 %collective-permute-start.22 = (bf16[128,768]{1,0:T(8,128)(2,1)S(1)}, bf16[128,768]{1,0:T(8,128)(2,1)S(1)}, u32[]{:S(2)}, u32[]{:S(2)}) collective-permute-start(bf16[128,768]{1,0:T(8,128)(2,1)S(1)} %get-tuple-element.53), channel_id=1, source_target_pairs={{0,16},{8,24},{16,0},{24,8},{1,17},{9,25},{17,1},{25,9},{2,18},{10... | collective-permute-start | bytes 589832 | tf_op jit(solution)/shard_map/ppermute | solution.py:463
  71.3 7.6 %collective-permute-start.23 = (bf16[128,768]{1,0:T(8,128)(2,1)S(1)}, bf16[128,768]{1,0:T(8,128)(2,1)S(1)}, u32[]{:S(2)}, u32[]{:S(2)}) collective-permute-start(bf16[128,768]{1,0:T(8,128)(2,1)S(1)} %get-tuple-element.53), channel_id=1, source_target_pairs={{4,0},{5,1},{6,2},{7,3},{12,8},{13,9},{14,10},{15,11},{20,16},{21,... | collective-permute-start | bytes 589832 | tf_op jit(solution)/shard_map/ppermute | solution.py:478
  72.6 9.7 %collective-permute-start.21 = (bf16[128,768]{1,0:T(8,128)(2,1)S(1)}, bf16[128,768]{1,0:T(8,128)(2,1)S(1)}, u32[]{:S(2)}, u32[]{:S(2)}) collective-permute-start(bf16[128,768]{1,0:T(8,128)(2,1)S(1)} %get-tuple-element.53), channel_id=1, source_target_pairs={{0,3},{1,2},{2,1},{3,0},{4,7},{5,6},{6,5},{7,4},{8,11},{9,10},{10,... | collective-permute-start | bytes 589832 | tf_op jit(solution)/shard_map/ppermute | solution.py:463
  75.3 15.4 %collective-permute-start.20 = (bf16[128,768]{1,0:T(8,128)(2,1)S(1)}, bf16[128,768]{1,0:T(8,128)(2,1)S(1)}, u32[]{:S(2)}, u32[]{:S(2)}) collective-permute-start(bf16[128,768]{1,0:T(8,128)(2,1)S(1)} %get-tuple-element.53), channel_id=1, source_target_pairs={{0,2},{1,3},{2,0},{3,1},{4,6},{5,7},{6,4},{7,5},{8,10},{9,11},{10,... | collective-permute-start | bytes 589832 | tf_op jit(solution)/shard_map/ppermute | solution.py:463
  75.3 15.4 %collective-permute-start.19 = (bf16[128,768]{1,0:T(8,128)(2,1)S(1)}, bf16[128,768]{1,0:T(8,128)(2,1)S(1)}, u32[]{:S(2)}, u32[]{:S(2)}) collective-permute-start(bf16[128,768]{1,0:T(8,128)(2,1)S(1)} %get-tuple-element.53), channel_id=1, source_target_pairs={{0,1},{1,0},{2,3},{3,2},{4,5},{5,4},{6,7},{7,6},{8,9},{9,8},{10,11... | collective-permute-start | bytes 589832 | tf_op jit(solution)/shard_map/ppermute | solution.py:463
  77.0 13.7 %collective-permute-start.24 = (bf16[128,768]{1,0:T(8,128)(2,1)S(1)}, bf16[128,768]{1,0:T(8,128)(2,1)S(1)}, u32[]{:S(2)}, u32[]{:S(2)}) collective-permute-start(bf16[128,768]{1,0:T(8,128)(2,1)S(1)} %collective-permute-done.22), channel_id=1, source_target_pairs={{4,0},{5,1},{6,2},{7,3},{12,8},{13,9},{14,10},{15,11},{20,16},{21,... | collective-permute-start | bytes 589832 | tf_op jit(solution)/shard_map/ppermute | solution.py:478
  90.8 15.5 %collective-permute-start.28 = (bf16[3,128,768]{2,1,0:T(8,128)(2,1)S(1)}, bf16[3,128,768]{2,1,0:T(8,128)(2,1)S(1)}, u32[]{:S(2)}, u32[]{:S(2)}) collective-permute-start(bf16[3,128,768]{2,1,0:T(8,128)(2,1)S(1)} %pad_maximum_fusion.1), channel_id=1, source_target_pairs={{4,0},{5,1},{6,2},{7,3},{12,8},{13,9},{14,10},{15,11},{20,16},{21,... | collective-permute-start | bytes 1769480 | tf_op jit(solution)/shard_map/ppermute | solution.py:478
  92.1 14.4 %collective-permute-start.25 = (bf16[3,128,768]{2,1,0:T(8,128)(2,1)S(1)}, bf16[3,128,768]{2,1,0:T(8,128)(2,1)S(1)}, u32[]{:S(2)}, u32[]{:S(2)}) collective-permute-start(bf16[3,128,768]{2,1,0:T(8,128)(2,1)S(1)} %pad_maximum_fusion.1), channel_id=1, source_target_pairs={{0,16},{8,24},{16,0},{24,8},{1,17},{9,25},{17,1},{25,9},{2,18},{10... | collective-permute-start | bytes 1769480 | tf_op jit(solution)/shard_map/ppermute | solution.py:463
  93.7 25.5 %collective-permute-start.31 = (bf16[5,128,768]{2,1,0:T(8,128)(2,1)S(1)}, bf16[5,128,768]{2,1,0:T(8,128)(2,1)S(1)}, u32[]{:S(2)}, u32[]{:S(2)}) collective-permute-start(bf16[5,128,768]{2,1,0:T(8,128)(2,1)S(1)} %constant_dynamic-update-slice_fusion.refs_0_), channel_id=1, source_target_pairs={{0,8},{8,0},{16,24},{24,16},{1,9},{9,1},{17,25},{25,17},{2,10},{10... | collective-permute-start | bytes 2949128 | tf_op jit(solution)/shard_map/ppermute | solution.py:463
  106.3 12.9 %copy-start.8 = (s32[4,3]{1,0:T(4,128)S(1)}, s32[4,3]{1,0:T(4,128)}, u32[]{:S(2)}) copy-start(s32[4,3]{1,0:T(4,128)} %bounds.7) | copy-start | bytes 148
  106.4 12.8 %collective-permute-start.33 = (bf16[5,128,768]{2,1,0:T(8,128)(2,1)S(1)}, bf16[5,128,768]{2,1,0:T(8,128)(2,1)S(1)}, u32[]{:S(2)}, u32[]{:S(2)}) collective-permute-start(bf16[5,128,768]{2,1,0:T(8,128)(2,1)S(1)} %pad_maximum_fusion.refs_4_), channel_id=1, source_target_pairs={{0,8},{8,0},{16,24},{24,16},{1,9},{9,1},{17,25},{25,17},{2,10},{10... | collective-permute-start | bytes 2949128 | tf_op jit(solution)/shard_map/ppermute | solution.py:463
  106.5 12.7 %collective-permute-start.32 = (bf16[3,128,768]{2,1,0:T(8,128)(2,1)S(1)}, bf16[3,128,768]{2,1,0:T(8,128)(2,1)S(1)}, u32[]{:S(2)}, u32[]{:S(2)}) collective-permute-start(bf16[3,128,768]{2,1,0:T(8,128)(2,1)S(1)} %collective-permute-done.25.refs_2_), channel_id=1, source_target_pairs={{0,8},{8,0},{16,24},{24,16},{1,9},{9,1},{17,25},{25,17},{2,10},{10... | collective-permute-start | bytes 1769480 | tf_op jit(solution)/shard_map/ppermute | solution.py:463
  107.1 9.0 %collective-permute-start.29 = (bf16[3,64,768]{2,1,0:T(8,128)(2,1)S(1)}, bf16[3,64,768]{2,1,0:T(8,128)(2,1)S(1)}, u32[]{:S(2)}, u32[]{:S(2)}) collective-permute-start(bf16[3,64,768]{2,1,0:T(8,128)(2,1)S(1)} %slice.71), channel_id=1, source_target_pairs={{0,16},{8,24},{16,0},{24,8},{1,17},{9,25},{17,1},{25,9},{2,18},{10... | collective-permute-start | bytes 884744 | tf_op jit(solution)/shard_map/ppermute | solution.py:463
  108.6 10.6 %collective-permute-start.26 = (bf16[3,64,768]{2,1,0:T(8,128)(2,1)S(1)}, bf16[3,64,768]{2,1,0:T(8,128)(2,1)S(1)}, u32[]{:S(2)}, u32[]{:S(2)}) collective-permute-start(bf16[3,64,768]{2,1,0:T(8,128)(2,1)S(1)} %slice.70), channel_id=1, source_target_pairs={{4,0},{5,1},{6,2},{7,3},{12,8},{13,9},{14,10},{15,11},{20,16},{21,... | collective-permute-start | bytes 884744 | tf_op jit(solution)/shard_map/ppermute | solution.py:478
  116.1 6.1 %collective-permute-start.30 = (bf16[3,64,768]{2,1,0:T(8,128)(2,1)S(1)}, bf16[3,64,768]{2,1,0:T(8,128)(2,1)S(1)}, u32[]{:S(2)}, u32[]{:S(2)}) collective-permute-start(bf16[3,64,768]{2,1,0:T(8,128)(2,1)S(1)} %collective-permute-done.29.refs_2_), channel_id=1, source_target_pairs={{0,8},{8,0},{16,24},{24,16},{1,9},{9,1},{17,25},{25,17},{2,10},{10... | collective-permute-start | bytes 884744 | tf_op jit(solution)/shard_map/ppermute | solution.py:463
  119.2 2.9 %collective-permute-start.27 = (bf16[3,64,768]{2,1,0:T(8,128)(2,1)S(1)}, bf16[3,64,768]{2,1,0:T(8,128)(2,1)S(1)}, u32[]{:S(2)}, u32[]{:S(2)}) collective-permute-start(bf16[3,64,768]{2,1,0:T(8,128)(2,1)S(1)} %collective-permute-done.26.refs_0_), channel_id=1, source_target_pairs={{0,8},{8,0},{16,24},{24,16},{1,9},{9,1},{17,25},{25,17},{2,10},{10... | collective-permute-start | bytes 884744 | tf_op jit(solution)/shard_map/ppermute | solution.py:463

commit v3 on v2

--- a/solution.py
+++ b/solution.py
@@ -53,18 +53,7 @@
     return jnp.sum(x, axis=-1, keepdims=True)
 
 
-def store_by_layer(out_ref, bounds, layers, pieces):
-    first, after = held_layers(bounds)
-    columns = pieces[0].shape[1]
-    for layer in range(layers):
-        total = jnp.zeros_like(pieces[0])
-        for slot, piece in enumerate(pieces):
-            here = (first + slot == layer) & (layer < after)
-            total = jnp.where(here, piece, total)
-        out_ref[:, layer * columns : (layer + 1) * columns] = total
-
-
-def project_kernel(layers, steps, bounds, h_in, down_in, up_in, *refs):
+def project_kernel(steps, h_in, down_in, up_in, *refs):
     out_ref, sq_ref, h_ref, up_ref, down_ref, sems = refs
     slots, ranks, features = down_in.shape
     tokens = h_ref.shape[0]
@@ -98,25 +87,20 @@
         for lane in range(0, width, 128):
             square = square + wide[:, lane : lane + 128]
     sq_ref[...] = jnp.broadcast_to(row_sum(square), square.shape)
-    pieces = []
-    for slot in range(slots):
-        lo, hi = slot * ranks, (slot + 1) * ranks
-        up = slots * ranks
-        pieces.append(jnp.concatenate([ph[:, lo:hi], ph[:, up + lo : up + hi]], axis=1))
-    store_by_layer(out_ref, bounds, layers, pieces)
-
-
-def project(bounds, hidden, downs, ups, layers):
+    out_ref[...] = ph
+
+
+def project(hidden, downs, ups):
     tokens, features = hidden.shape
     slots, ranks, _ = downs.shape
     steps = 8
     sources = [pltpu.with_memory_space_constraint(x, pltpu.HBM) for x in (hidden, downs, ups)]
     return pl.pallas_call(
-        functools.partial(project_kernel, layers, steps),
-        in_specs=[in_smem] + [in_hbm] * 3,
+        functools.partial(project_kernel, steps),
+        in_specs=[in_hbm] * 3,
         out_specs=[in_vmem] * 4,
         out_shape=[
-            jax.ShapeDtypeStruct((tokens, layers * 2 * ranks), f32),
+            jax.ShapeDtypeStruct((tokens, 2 * slots * ranks), f32),
             jax.ShapeDtypeStruct((tokens, 128), f32),
             jax.ShapeDtypeStruct((tokens, features), bf16),
             jax.ShapeDtypeStruct((slots * ranks, features), bf16),
@@ -132,24 +116,25 @@
             transcendentals=0,
         ),
         name="project",
-    )(bounds, *sources)
-
-
-def project_back_kernel(layers, ranks, per_micro, bounds, counts, g_ref, up_ref, out_ref):
+    )(*sources)
+
+
+def project_back_kernel(per_micro, counts, by_hidden, g_ref, up_ref, out_ref):
     pg = dot_last(g_ref[...], up_ref[...])
     pg = jnp.where(counted_rows(counts, pg.shape[0], per_micro), pg, 0.0)
-    slots = pg.shape[1] // ranks
-    pieces = [pg[:, slot * ranks : (slot + 1) * ranks] for slot in range(slots)]
-    store_by_layer(out_ref, bounds, layers, pieces)
-
-
-def project_back(bounds, counts, cot, ups, layers, ranks, per_micro):
+    ahead = by_hidden.shape[1]
+    out_ref[:, :ahead] = by_hidden[...]
+    out_ref[:, ahead:] = pg
+
+
+def project_back(counts, by_hidden, cot, ups, per_micro):
     tokens, features = cot.shape
+    columns = by_hidden.shape[1] + ups.shape[0]
     return pl.pallas_call(
-        functools.partial(project_back_kernel, layers, ranks, per_micro),
-        in_specs=[in_smem] * 2 + [in_vmem] * 2,
+        functools.partial(project_back_kernel, per_micro),
+        in_specs=[in_smem] + [in_vmem] * 3,
         out_specs=in_vmem,
-        out_shape=jax.ShapeDtypeStruct((tokens, layers * ranks), f32),
+        out_shape=jax.ShapeDtypeStruct((tokens, columns), f32),
         compiler_params=limited,
         cost_estimate=pl.CostEstimate(
             flops=2 * tokens * ups.shape[0] * features,
@@ -157,7 +142,7 @@
             transcendentals=0,
         ),
         name="project_back",
-    )(bounds, counts, cot, ups)
+    )(counts, by_hidden, cot, ups)
 
 
 def gram_kernel(sections, *refs):
@@ -196,28 +181,33 @@
     )(*around)
 
 
-def chain_kernel(sections, parts, features, per_micro, counts, *refs):
-    on_hidden, on_cot, grams = refs[:sections], refs[sections : 2 * sections], refs[2 * sections :]
-    sq_ref = grams[parts]
-    factor_ref, mixed_ref = grams[parts + 1 :]
+def chain_kernel(sections, slots, features, per_micro, bounds, counts, *refs):
+    projections, grams = refs[:sections], refs[sections:-3]
+    sq_ref, factor_ref, mixed_ref = refs[-3:]
     layers = sections
+    replica_at = lax.axis_index("replica")
     section_at = lax.axis_index("section")
     tokens = sq_ref.shape[0]
-
-    def total(arrays):
-        result = arrays[0][...]
-        for other in arrays[1:]:
-            result = result + other[...]
-        return result
-
-    by_hidden, by_cot, table = total(on_hidden), total(on_cot), total(grams[:parts])
-    ranks = by_cot.shape[1] // layers
+    table = grams[0][...]
+    for other in grams[1:]:
+        table = table + other[...]
+    ranks = projections[0].shape[1] // (3 * slots)
+    parts = [[jnp.zeros((tokens, ranks), f32)] * 3 for _ in range(layers)]
+    for distance, source in enumerate(projections):
+        section = lax.rem(section_at + distance, sections)
+        first, after = bounds[replica_at, section], bounds[replica_at, section + 1]
+        for slot in range(slots):
+            for which in range(3):
+                block = which * slots + slot
+                piece = source[:, block * ranks : (block + 1) * ranks]
+                for layer in range(layers):
+                    here = (first + slot == layer) & (layer < after)
+                    parts[layer][which] = jnp.where(here, piece, parts[layer][which])
     scale_d = 1.0 / math.sqrt(features)
     scale_r = 1.0 / math.sqrt(ranks)
 
     def part(layer, which):
-        source, block = (by_cot, layer) if which == 2 else (by_hidden, 2 * layer + which)
-        return source[:, block * ranks : (block + 1) * ranks]
+        return parts[layer][which]
 
     def up_down(i, layer):
         return table[i * ranks : (i + 1) * ranks, (layer - 1) * ranks : layer * ranks]
@@ -298,15 +288,15 @@
         mixed_ref[ranks:, cut] = across * (-scale_r * scale_r)
 
 
-def chain(counts, on_hidden, on_cot, grams, square, features, per_micro):
-    sections = len(on_cot)
-    tokens, wide = on_cot[0].shape
-    ranks = wide // sections
-    inputs = [*on_hidden, *on_cot, *grams, square]
-    kernel = functools.partial(chain_kernel, sections, len(grams), features, per_micro)
+def chain(bounds, counts, projections, grams, square, slots, features, per_micro):
+    sections = len(projections)
+    tokens, wide = projections[0].shape
+    ranks = wide // (3 * slots)
+    inputs = [*projections, *grams, square]
+    kernel = functools.partial(chain_kernel, sections, slots, features, per_micro)
     return pl.pallas_call(
         kernel,
-        in_specs=[in_smem] + [in_vmem] * len(inputs),
+        in_specs=[in_smem] * 2 + [in_vmem] * len(inputs),
         out_specs=[in_vmem] * 2,
         out_shape=[
             jax.ShapeDtypeStruct((2 * ranks, 2 * tokens), bf16),
@@ -314,32 +304,34 @@
         ],
         compiler_params=limited,
         name="chain",
-    )(counts, *inputs)
+    )(bounds, counts, *inputs)
 
 
 def gradient_kernel(first, factor_ref, h_ref, g_ref, out_ref):
-    groups, tensors, _, columns = out_ref.shape
+    _, _, ranks, columns = out_ref.shape
     replica_at = lax.axis_index("replica")
     tensor_at = lax.axis_index("tensor")
+    tensors = lax.axis_size("tensor")
     factors = factor_ref[...]
-    for group in range(groups):
-        for hop in range(tensors):
-            owner = (replica_at ^ (first + 2 * group)) * tensors + (tensor_at ^ hop)
+    for far in range(2):
+        for hop in range(4):
+            owner = (replica_at ^ (first + 2 * far)) * tensors + (tensor_at ^ hop)
             cut = pl.ds(pl.multiple_of(owner * columns, columns), columns)
             stacked = jnp.concatenate([h_ref[:, cut], g_ref[:, cut]], axis=0)
-            block = jnp.dot(factors, stacked, preferred_element_type=f32)
-            out_ref[group, hop] = block.astype(bf16)
-
-
-def gradient(factors, hidden, cot, first, replicas, tensors):
+            block = jnp.dot(factors, stacked, preferred_element_type=f32).astype(bf16)
+            low, high = hop % 2, hop // 2
+            out_ref[0, 4 * far + 2 * low + high] = block[:ranks]
+            out_ref[1, 4 * low + 2 * far + high] = block[ranks:]
+
+
+def gradient(factors, hidden, cot, first, columns):
     tokens, features = hidden.shape
     rows = factors.shape[0]
-    shape = (replicas // 2, tensors, rows, features // (replicas * tensors))
     return pl.pallas_call(
         functools.partial(gradient_kernel, first),
         in_specs=[in_vmem] * 3,
         out_specs=in_vmem,
-        out_shape=jax.ShapeDtypeStruct(shape, bf16),
+        out_shape=jax.ShapeDtypeStruct((2, 8, rows // 2, columns), bf16),
         compiler_params=limited,
         cost_estimate=pl.CostEstimate(
             flops=2 * rows * tokens * features,
@@ -350,44 +342,44 @@
     )(factors, hidden, cot)
 
 
-def update_kernel(count, *refs):
-    pieces = refs[:count]
-    mixed_ref, other_ref, right_ref = refs[count : count + 3]
-    state = refs[count + 3 : count + 9]
-    outs = refs[count + 9 : count + 15]
-    share_ref = refs[count + 15]
+def update_kernel(kept, near, downs, ups, *refs):
+    last, mixed_ref, other_ref, right_ref = refs[:4]
+    state, outs, share_ref = refs[4:10], refs[10:16], refs[16]
     mixed = mixed_ref[...] + other_ref[...]
-    grad = jnp.dot(mixed, right_ref[...].astype(f32), preferred_element_type=f32, precision=exact)
-    for piece in pieces:
-        block = piece[(0,) * (len(piece.shape) - 2)] if len(piece.shape) > 2 else piece[...]
-        grad = grad + block.astype(f32)
-    ranks = grad.shape[0] // 2
-    for which in range(2):
-        rows = slice(which * ranks, (which + 1) * ranks)
-        own = grad[rows]
+    right = right_ref[...].astype(f32)
+    small = jnp.dot(mixed, right, preferred_element_type=f32, precision=exact)
+    ranks = small.shape[0] // 2
+    for which, steps in enumerate((downs, ups)):
+        own = small[which * ranks : (which + 1) * ranks]
+        for block in (kept[which, 0], near[which, 0], *(step[0] for step in steps), last[which]):
+            own = own + block.astype(f32)
         master, moment, second = (state[2 * kind + which][0] for kind in range(3))
         moment = beta_one * moment + (1.0 - beta_one) * own
         second = beta_two * second + (1.0 - beta_two) * own * own
         master = master - learn_rate * (
             moment / first_fix / (jnp.sqrt(second / second_fix) + adam_eps) + decay_rate * master
         )
-        share_ref[rows] = master.astype(bf16)
+        share_ref[which] = master.astype(bf16)
         outs[which][0] = master
         outs[2 + which][0] = moment
         outs[4 + which][0] = second
 
 
-def update(pieces, mixed, other, right, state):
+def update(kept, near, downs, ups, last, mixed, other, right, state):
     _, ranks, columns = state[0].shape
+
+    def kernel(kept, near, down_one, down_two, up_one, up_two, *refs):
+        update_kernel(kept, near, (down_one, down_two), (up_one, up_two), *refs)
+
     return pl.pallas_call(
-        functools.partial(update_kernel, len(pieces)),
-        in_specs=[in_vmem] * (len(pieces) + 9),
+        kernel,
+        in_specs=[in_vmem] * 16,
         out_specs=[in_vmem] * 7,
         out_shape=[jax.ShapeDtypeStruct(array.shape, f32) for array in state]
-        + [jax.ShapeDtypeStruct((2 * ranks, columns), bf16)],
+        + [jax.ShapeDtypeStruct((2, ranks, columns), bf16)],
         compiler_params=limited,
         name="update",
-    )(*pieces, mixed, other, right, *state)
+    )(kept, near, *downs, *ups, last, mixed, other, right, *state)
 
 
 def place_kernel(layout, start, bounds, *refs):
@@ -404,15 +396,13 @@
     zeros[...] = jnp.zeros_like(zeros)
 
     def fill(slot, distance, go):
-        for (window, rows, owners), source in zip(layout, sources):
+        for (window, blocks), source in zip(layout, sources):
             if window != distance:
                 continue
-            for i, (order, hop) in enumerate(owners):
+            for i, (which, order, hop) in enumerate(blocks):
                 owner = (replica_at ^ order) * tensors + (tensor_at ^ hop)
                 cut = pl.ds(pl.multiple_of(owner * columns, columns), columns)
-                for at, which in enumerate(rows):
-                    block = source.at[i, pl.ds(at * ranks, ranks), :]
-                    go(pltpu.make_async_copy(block, outs[which].at[slot, :, cut], sem))
+                go(pltpu.make_async_copy(source.at[i], outs[which].at[slot, :, cut], sem))
 
     def clear(slot, go):
         for out in outs:
@@ -438,8 +428,8 @@
 
 
 def place(bounds, pieces, before, slots, ranks, features):
-    layout = [piece[:3] for piece in pieces]
-    arrays = [piece[3] for piece in pieces]
+    layout = [piece[:2] for piece in pieces]
+    arrays = [piece[2] for piece in pieces]
     columns = arrays[0].shape[-1]
     return pl.pallas_call(
         functools.partial(place_kernel, layout, not before),
@@ -485,55 +475,90 @@
     return total.astype(bf16)
 
 
-def reduced(factors, hidden, cot, replicas, tensors):
-    sent = gradient(factors, hidden, cot, 1, replicas, tensors)
+def reduced(factors, hidden, cot, columns, mixed):
+    sent = gradient(factors, hidden, cot, 1, columns)
     near = swapped(sent, "replica", 1)
-    kept = gradient(factors, hidden, cot, 0, replicas, tensors)
-    across = swapped(summed(kept[1, 1:], near[1, 1:]), "replica", 2)
-    across, last = lax.optimization_barrier((across, summed(kept[1, 0], near[1, 0])))
-    last = swapped(last, "replica", 2)
-    along = [
-        swapped(summed(kept[0, k], near[0, k], across[k - 1]), "tensor", k)
-        for k in range(1, tensors)
+    kept = gradient(factors, hidden, cot, 0, columns)
+    mixed = mixed + swapped(mixed, "tensor", 1)
+
+    def part(which, cut, *steps):
+        return summed(kept[which, cut], near[which, cut], *steps)
+
+    high, low = slice(4, 8), slice(2, 4)
+    down_one, up_one, mixed = lax.optimization_barrier((part(0, high), part(1, high), mixed))
+    down_one = swapped(down_one, "replica", 2)
+    up_one = swapped(up_one, "tensor", 1)
+    down_two = swapped(part(0, low, down_one[2:]), "tensor", 1)
+    up_two = swapped(part(1, low, up_one[2:]), "replica", 2)
+    last = jnp.stack([part(0, 1, down_one[1], down_two[1]), part(1, 1, up_one[1], up_two[1])])
+    last = swapped(last, "tensor", 2)
+    return (kept, near, (down_one, down_two), (up_one, up_two), last), mixed
+
+
+def crossed(piece, axis, distance):
+    window, blocks, array = piece
+    blocks = [
+        (which, order ^ distance, hop) if axis == "replica" else (which, order, hop ^ distance)
+        for which, order, hop in blocks
     ]
-    return [kept, near, last, *along]
+    return (window, blocks, swapped(array, axis, distance))
+
+
+def fetched(piece):
+    _, blocks, array = piece
+    return (1, blocks, following_layer(array))
+
+
+def picked(piece, cut):
+    return (piece[0], piece[1][cut], piece[2][cut])
+
+
+def joined(*pieces):
+    blocks = [block for piece in pieces for block in piece[1]]
+    return (pieces[0][0], blocks, jnp.concatenate([piece[2] for piece in pieces]))
+
+
+def ordered(*pieces):
+    arrays = lax.optimization_barrier(tuple(piece[2] for piece in pieces))
+    return [(*piece[:2], array) for piece, array in zip(pieces, arrays)]
 
 
 def spread(share, bounds, slots, features):
-    ranks = share.shape[0] // 2
-    along = swaps(share, "tensor")
-    far_one = swapped(share, "replica", 2)
-    next_one = following_layer(share)
-    next_far_one = following_layer(far_one)
-    along, far_one, next_one, next_far_one = lax.optimization_barrier(
-        (along, far_one, next_one, next_far_one)
+    ranks = share.shape[1]
+    own = (0, [(0, 0, 0), (1, 0, 0)], share)
+    one = crossed(own, "tensor", 2)
+    next_own = fetched(own)
+    both = joined(picked(own, slice(0, 1)), picked(one, slice(0, 1)))
+    both_up = joined(picked(own, slice(1, 2)), picked(one, slice(1, 2)))
+    down_two = crossed(both, "tensor", 1)
+    up_two = crossed(both_up, "replica", 2)
+    next_one = fetched(one)
+    two = joined(down_two, up_two)
+    down_three = crossed(joined(both, down_two), "replica", 2)
+    up_three = crossed(joined(both_up, up_two), "tensor", 1)
+    next_two = fetched(two)
+    last, first = slice(3, 4), slice(0, 1)
+    next_end = fetched(joined(picked(down_three, last), picked(up_three, last)))
+    next_near = joined(next_own, next_one, next_two)
+    down_end = crossed(
+        joined(picked(next_own, first), picked(next_one, first), picked(next_two, first)),
+        "replica",
+        2,
     )
-    line = jnp.stack(along)
-    far_line = swapped(line, "replica", 2)
-    next_line = following_layer(line)
-    near = jnp.concatenate([share[None], far_one[None], line])
-    next_near = jnp.concatenate([next_one[None], next_far_one[None], next_line])
-    next_far_down = following_layer(far_line[:, :ranks])
-    next_far_up = swapped(next_line[:, ranks:], "replica", 2)
-    hops = range(1, lax.axis_size("tensor"))
-    near_owners = [(0, 0), (2, 0)] + [(0, hop) for hop in hops]
-    far_owners = [(2, hop) for hop in hops]
-    placed = []
-    for group in (
-        (
-            (0, (0, 1), near_owners, near),
-            (0, (0, 1), far_owners, far_line),
-            (1, (0, 1), near_owners, next_near),
-        ),
-        ((1, (0,), far_owners, next_far_down), (1, (1,), far_owners, next_far_up)),
-    ):
-        pieces = []
-        for window, rows, owners, block in group:
-            other = [(order ^ 1, hop) for order, hop in owners]
-            pieces.append((window, rows, owners, block))
-            pieces.append((window, rows, other, swapped(block, "replica", 1)))
-        placed = place(bounds, pieces, placed, slots, ranks, features)
-    return placed
+    second = slice(1, 2)
+    up_end = crossed(
+        joined(picked(next_own, second), picked(next_one, second), picked(next_two, slice(2, 3))),
+        "tensor",
+        1,
+    )
+    near = joined(own, one)
+    early = [near, two, down_three, up_three, next_near]
+    early += [crossed(piece, "replica", 1) for piece in early]
+    placed = place(bounds, early, [], slots, ranks, features)
+    end = joined(down_end, up_end, next_end)
+    end_array, *placed = lax.optimization_barrier((end[2], *placed))
+    end = (*end[:2], end_array)
+    return place(bounds, [end, crossed(end, "replica", 1)], placed, slots, ranks, features)
 
 
 def on_device(
@@ -561,27 +586,25 @@
 
     owned = jnp.concatenate([master_down[0], master_up[0]], axis=0).astype(bf16)
     around = [from_next(owned, d) for d in range(1, sections)]
-    by_hidden, square, hidden, ups = project(
-        bounds, hidden, holder_down[0, 0], holder_up[0, 0], sections
-    )
+    by_hidden, square, hidden, ups = project(hidden, holder_down[0, 0], holder_up[0, 0])
     around, by_hidden = lax.optimization_barrier((around, by_hidden))
     table, right = gram([owned, *around])
-    on_hidden = [by_hidden] + [from_next(by_hidden, d) for d in range(1, sections)]
     table, ups = lax.optimization_barrier((table, ups))
-    by_cot = project_back(
-        bounds, micro_counts, cot, ups, sections, holder_down.shape[3], per_micro
+    projected = project_back(micro_counts, by_hidden, cot, ups, per_micro)
+    table = table + sum(swaps(table, "replica"))
+    projections = [projected] + [from_next(projected, d) for d in range(1, sections)]
+    table = table + swapped(table, "tensor", 1)
+    tables = [table, swapped(table, "tensor", 2)]
+    factors, mixed = chain(
+        bounds, micro_counts, projections, tables, square, slots, features, per_micro
     )
-    on_cot = [by_cot] + [from_next(by_cot, d) for d in range(1, sections)]
-    table = table + sum(swaps(table, "replica"))
-    tables = [table] + swaps(table, "tensor")
-    factors, mixed = chain(micro_counts, on_hidden, on_cot, tables, square, features, per_micro)
-
-    pieces = reduced(factors, hidden, cot, replicas, tensors)
-    for axis, distance in (("tensor", 1), ("tensor", 2), ("replica", 1)):
+
+    parts, mixed = reduced(factors, hidden, cot, master_down.shape[2], mixed)
+    for axis, distance in (("tensor", 2), ("replica", 1)):
         mixed = mixed + swapped(mixed, axis, distance)
     other = swapped(mixed, "replica", 2)
     state = [master_down, master_up, moment_down, moment_up, second_down, second_up]
-    updated = update(pieces, mixed, other, right, state)
+    updated = update(*parts, mixed, other, right, state)
     placed = spread(updated[6], bounds, slots, features)
     return (placed[0][None, None], placed[1][None, None], *updated[:6])
 

time: 124 us -> 114 us (0.919)
  waiting for transfers between devices: 66.3 us -> 58.1 us
    ppermute x27 -> x28, waiting for transfers between devices: 50.2 us -> 42.7 us  [swapped(): return lax.ppermute(block, axis, route)]
    ppermute x3 -> x2, starting transfers between devices: 5.09 us -> 3.69 us  [from_next(): return lax.ppermute(block, 'section', route)]
    ppermute x27 -> x28, starting transfers between devices: 25.5 us -> 25.8 us  [swapped(): return lax.ppermute(block, axis, route)]
  transfers between devices with their start and end apart: 34 -> 34, of which waited for: 14 -> 18; matrix products, arithmetic and copies ran while one was open for 0% -> 1% of each run, Pallas kernels for 10% -> 7%
where the time goes in v3:
time: 114 us; the launch traced here: 113 us
  waiting for transfers between devices  58.1 us (51%)
  starting transfers between devices  34.6 us (30%)
  Pallas kernels  17.5 us (15%)
  other arithmetic  1.86 us (2%)
    ppermute x28, waiting for transfers between devices, swapped(): return lax.ppermute(block, axis, route)  42.7 us
    ppermute x28, starting transfers between devices, swapped(): return lax.ppermute(block, axis, route)  25.8 us
    ppermute x4, waiting for transfers between devices, following_layer(): return lax.ppermute(block, 'section', [(i + 1, i) for i in range(size - 1)])  15.4 us
    pallas_call x1, Pallas kernels, project(): pl.pallas_call(functools.partial(project_kernel, steps), in_specs=[in_hbm...  5.99 us
    ppermute x4, starting transfers between devices, following_layer(): return lax.ppermute(block, 'section', [(i + 1, i) for i in range(size - 1)])  5.16 us
    pallas_call x2, Pallas kernels, place(): pl.pallas_call(functools.partial(place_kernel, layout, not before), in_sp...  4.46 us
    ppermute x2, starting transfers between devices, from_next(): return lax.ppermute(block, 'section', route)  3.69 us
    pallas_call x1, Pallas kernels, chain(): pl.pallas_call(kernel, in_specs=[in_smem] * 2 + [in_vmem] * len(inputs),...  2.33 us
  transfers between devices with their start and end apart: 34, of which 18 were waited for; matrix products, arithmetic and copies ran while one was open for 1% of the time, Pallas kernels for 7%

profile of v3, /device:TPU:0, one launch (start us, length us, event | category | flops | bytes accessed | tf_op | source)
XLA Modules:
  0.0 113.4 jit_solution(11812284603956521631)
XLA Ops:
  0.6 1.0 convert_bitcast_fusion
  1.7 3.0 %collective-permute-start = (bf16[128,768]{1,0:T(8,128)(2,1)S(1)}, bf16[128,768]{1,0:T(8,128)(2,1)S(1)}, u32[]{:S(2)}, u32[]{:S(2)}) collective-permute-start(bf16[128,768]{1,0:T(8,128)(2,1)S(1)} %pad_maximum_fusion.5.refs_0_), channel_id=1, source_target_pairs={{4,0},{0,4},{5,1},{1,5},{6,2},{2,6},{7,3},{3,7},{12,8},{8,12},{13,... | collective-permute-start | bytes 589832 | tf_op jit(solution)/shard_map/ppermute | solution.py:463
  4.7 6.0 %project.1 = (f32[128,256]{1,0:T(8,128)S(1)}, f32[128,128]{1,0:T(8,128)S(1)}, bf16[128,12288]{1,0:T(8,128)(2,1)S(1)}, bf16[128,12288]{1,0:T(8,128)(2,1)S(1)}) custom-call(bf16[128,12288]{1,0:T(8,128)(2,1)} %bitcast.39, bf16[2,64,12288]{2,1,0:T(8,128)(2,1)} %bitcast.40, bf16[2,64,12288]{2,1,0:T(8,128)(2,1)} %bitcast.41), custom_call_target="tpu_custom_call" | custom-call | flops 805306368 | bytes 9437184 | tf_op jit(solution)/shard_map/project/pallas_call | solution.py:98
  10.9 0.7 collective-permute-start.4
  11.7 0.9 collective-permute-start.3
  12.8 1.5 %project_back.1.refs_0_ = f32[128,384]{1,0:T(8,128)S(1)} custom-call(s32[4]{0:T(128)S(1)} %copy-done.8, f32[128,256]{1,0:T(8,128)S(1)} %get-tuple-element.38.by_hidden, bf16[128,12288]{1,0:T(8,128)(2,1)S(1)} %bitcast.34, bf16[128,12288]{1,0:T(8,128)(2,1)S(1)} %get-tuple-element.42.up_ref), custom_call_target="tpu_custom_call" | custom-call | flops 402653184 | bytes 6291456 | tf_op jit(solution)/shard_map/project_back/pallas_call | solution.py:133
  14.4 0.7 collective-permute-start.1
  15.1 0.8 collective-permute-done.3
  15.9 1.6 %collective-permute-start.5 = (f32[64,128]{1,0:T(8,128)S(1)}, f32[64,128]{1,0:T(8,128)S(1)}, u32[]{:S(2)}, u32[]{:S(2)}) collective-permute-start(f32[64,128]{1,0:T(8,128)S(1)} %add_add_fusion), channel_id=1, source_target_pairs={{0,1},{1,0},{2,3},{3,2},{4,5},{5,4},{6,7},{7,6},{8,9},{9,8},{10,11... | collective-permute-start | bytes 98312 | tf_op jit(solution)/shard_map/ppermute | solution.py:453
  17.6 2.3 %collective-permute-done.5 = f32[64,128]{1,0:T(8,128)S(1)} collective-permute-done((f32[64,128]{1,0:T(8,128)S(1)}, f32[64,128]{1,0:T(8,128)S(1)}, u32[]{:S(2)}, u32[]{:S(2)}) %collective-permute-start.5) | collective-permute-done | bytes 32800 | tf_op jit(solution)/shard_map/ppermute | solution.py:453
  19.9 2.6 %collective-permute-start.6 = (f32[64,128]{1,0:T(8,128)S(1)}, f32[64,128]{1,0:T(8,128)S(1)}, u32[]{:S(2)}, u32[]{:S(2)}) collective-permute-start(f32[64,128]{1,0:T(8,128)S(1)} %add.92.refs_2_), channel_id=1, source_target_pairs={{0,2},{1,3},{2,0},{3,1},{4,6},{5,7},{6,4},{7,5},{8,10},{9,11},{10,... | collective-permute-start | bytes 98312 | tf_op jit(solution)/shard_map/ppermute | solution.py:453
  22.5 2.2 %collective-permute-done.6.refs_3_ = f32[64,128]{1,0:T(8,128)S(1)} collective-permute-done((f32[64,128]{1,0:T(8,128)S(1)}, f32[64,128]{1,0:T(8,128)S(1)}, u32[]{:S(2)}, u32[]{:S(2)}) %collective-permute-start.6) | collective-permute-done | bytes 32800 | tf_op jit(solution)/shard_map/ppermute | solution.py:453
  24.7 2.3 %chain.1 = (bf16[128,256]{1,0:T(8,128)(2,1)S(1)}, f32[128,128]{1,0:T(8,128)S(1)}) custom-call(s32[4,3]{1,0:T(4,128)S(1)} %copy-done.7, s32[4]{0:T(128)S(1)} %copy-done.8, f32[128,384]{1,0:T(8,128)S(1)} %project_back.1.refs_0_, f32[128,384]{1,0:T(8,128)S(1)} %collective-permute-done.1.refs_1_, f32[64,128]{1,0:T(8,128)S(1)} %add.92.refs_2_, ...), custom_call_target="tpu_custom_call" | custom-call | tf_op jit(solution)/shard_map/chain/pallas_call | solution.py:297
  27.1 0.6 gradient.3
  27.8 1.6 %collective-permute-start.8 = (f32[128,128]{1,0:T(8,128)S(1)}, f32[128,128]{1,0:T(8,128)S(1)}, u32[]{:S(2)}, u32[]{:S(2)}) collective-permute-start(f32[128,128]{1,0:T(8,128)S(1)} %get-tuple-element.47), channel_id=1, source_target_pairs={{0,1},{1,0},{2,3},{3,2},{4,5},{5,4},{6,7},{7,6},{8,9},{9,8},{10,11... | collective-permute-start | bytes 196616 | tf_op jit(solution)/shard_map/ppermute | solution.py:453
  29.4 0.6 gradient.2.kept
  30.1 2.2 %collective-permute-done.8 = f32[128,128]{1,0:T(8,128)S(1)} collective-permute-done((f32[128,128]{1,0:T(8,128)S(1)}, f32[128,128]{1,0:T(8,128)S(1)}, u32[]{:S(2)}, u32[]{:S(2)}) %collective-permute-start.8) | collective-permute-done | bytes 65568 | tf_op jit(solution)/shard_map/ppermute | solution.py:453
  32.5 0.8 collective-permute-start.9
  33.3 1.6 %collective-permute-start.11 = (bf16[4,64,768]{2,1,0:T(8,128)(2,1)S(1)}, bf16[4,64,768]{2,1,0:T(8,128)(2,1)S(1)}, u32[]{:S(2)}, u32[]{:S(2)}) collective-permute-start(bf16[4,64,768]{2,1,0:T(8,128)(2,1)S(1)} %get-tuple-element.49), channel_id=1, source_target_pairs={{0,1},{1,0},{2,3},{3,2},{4,5},{5,4},{6,7},{7,6},{8,9},{9,8},{10,11... | collective-permute-start | bytes 1179656 | tf_op jit(solution)/shard_map/ppermute | solution.py:453
  34.8 8.4 %collective-permute-done.9.down_one = bf16[4,64,768]{2,1,0:T(8,128)(2,1)S(1)} collective-permute-done((bf16[4,64,768]{2,1,0:T(8,128)(2,1)S(1)}, bf16[4,64,768]{2,1,0:T(8,128)(2,1)S(1)}, u32[]{:S(2)}, u32[]{:S(2)}) %collective-permute-start.9) | collective-permute-done | bytes 393248 | tf_op jit(solution)/shard_map/ppermute | solution.py:453
  43.8 1.4 %collective-permute-start.12 = (bf16[2,64,768]{2,1,0:T(8,128)(2,1)S(1)}, bf16[2,64,768]{2,1,0:T(8,128)(2,1)S(1)}, u32[]{:S(2)}, u32[]{:S(2)}) collective-permute-start(bf16[2,64,768]{2,1,0:T(8,128)(2,1)S(1)} %get-tuple-element.68), channel_id=1, source_target_pairs={{0,16},{8,24},{16,0},{24,8},{1,17},{9,25},{17,1},{25,9},{2,18},{10... | collective-permute-start | bytes 589832 | tf_op jit(solution)/shard_map/ppermute | solution.py:453
  45.2 1.6 %collective-permute-start.10 = (bf16[2,64,768]{2,1,0:T(8,128)(2,1)S(1)}, bf16[2,64,768]{2,1,0:T(8,128)(2,1)S(1)}, u32[]{:S(2)}, u32[]{:S(2)}) collective-permute-start(bf16[2,64,768]{2,1,0:T(8,128)(2,1)S(1)} %get-tuple-element.69), channel_id=1, source_target_pairs={{0,1},{1,0},{2,3},{3,2},{4,5},{5,4},{6,7},{7,6},{8,9},{9,8},{10,11... | collective-permute-start | bytes 589832 | tf_op jit(solution)/shard_map/ppermute | solution.py:453
  46.8 2.8 %collective-permute-start.14 = (f32[128,128]{1,0:T(8,128)S(1)}, f32[128,128]{1,0:T(8,128)S(1)}, u32[]{:S(2)}, u32[]{:S(2)}) collective-permute-start(f32[128,128]{1,0:T(8,128)S(1)} %add.95), channel_id=1, source_target_pairs={{0,2},{1,3},{2,0},{3,1},{4,6},{5,7},{6,4},{7,5},{8,10},{9,11},{10,... | collective-permute-start | bytes 196616 | tf_op jit(solution)/shard_map/ppermute | solution.py:453
  49.6 1.6 %collective-permute-done.10.down_two = bf16[2,64,768]{2,1,0:T(8,128)(2,1)S(1)} collective-permute-done((bf16[2,64,768]{2,1,0:T(8,128)(2,1)S(1)}, bf16[2,64,768]{2,1,0:T(8,128)(2,1)S(1)}, u32[]{:S(2)}, u32[]{:S(2)}) %collective-permute-start.10) | collective-permute-done | bytes 196640 | tf_op jit(solution)/shard_map/ppermute | solution.py:453
  51.3 2.5 %collective-permute-start.13 = (bf16[2,64,768]{2,1,0:T(8,128)(2,1)S(1)}, bf16[2,64,768]{2,1,0:T(8,128)(2,1)S(1)}, u32[]{:S(2)}, u32[]{:S(2)}) collective-permute-start(bf16[2,64,768]{2,1,0:T(8,128)(2,1)S(1)} %pad_maximum_fusion.6), channel_id=1, source_target_pairs={{0,2},{1,3},{2,0},{3,1},{4,6},{5,7},{6,4},{7,5},{8,10},{9,11},{10,... | collective-permute-start | bytes 589832 | tf_op jit(solution)/shard_map/ppermute | solution.py:453
  53.9 1.2 %collective-permute-done.15 = f32[128,128]{1,0:T(8,128)S(1)} collective-permute-done((f32[128,128]{1,0:T(8,128)S(1)}, f32[128,128]{1,0:T(8,128)S(1)}, u32[]{:S(2)}, u32[]{:S(2)}) %collective-permute-start.15) | collective-permute-done | bytes 65568 | tf_op jit(solution)/shard_map/ppermute | solution.py:453
  55.2 0.8 collective-permute-start.16
  55.9 3.6 %collective-permute-done.16.refs_2_ = f32[128,128]{1,0:T(8,128)S(1)} collective-permute-done((f32[128,128]{1,0:T(8,128)S(1)}, f32[128,128]{1,0:T(8,128)S(1)}, u32[]{:S(2)}, u32[]{:S(2)}) %collective-permute-start.16) | collective-permute-done | bytes 65568 | tf_op jit(solution)/shard_map/ppermute | solution.py:453
  59.5 1.6 %collective-permute-done.13.refs_0_ = bf16[2,64,768]{2,1,0:T(8,128)(2,1)S(1)} collective-permute-done((bf16[2,64,768]{2,1,0:T(8,128)(2,1)S(1)}, bf16[2,64,768]{2,1,0:T(8,128)(2,1)S(1)}, u32[]{:S(2)}, u32[]{:S(2)}) %collective-permute-start.13) | collective-permute-done | bytes 196640 | tf_op jit(solution)/shard_map/ppermute | solution.py:453
  61.1 1.8 %update.1 = (f32[1,64,768]{2,1,0:T(8,128)}, f32[1,64,768]{2,1,0:T(8,128)}, f32[1,64,768]{2,1,0:T(8,128)}, f32[1,64,768]{2,1,0:T(8,128)}, f32[1,64,768]{2,1,0:T(8...) custom-call(bf16[2,8,64,768]{3,2,1,0:T(8,128)(2,1)S(1)} %gradient.2.kept, ...), custom_call_target="tpu_custom_call" | custom-call | tf_op jit(solution)/shard_map/update/pallas_call | solution.py:374
  62.9 1.3 %collective-permute-start.17 = (bf16[2,64,768]{2,1,0:T(8,128)(2,1)S(1)}, bf16[2,64,768]{2,1,0:T(8,128)(2,1)S(1)}, u32[]{:S(2)}, u32[]{:S(2)}) collective-permute-start(bf16[2,64,768]{2,1,0:T(8,128)(2,1)S(1)} %get-tuple-element.52), channel_id=1, source_target_pairs={{4,0},{5,1},{6,2},{7,3},{12,8},{13,9},{14,10},{15,11},{20,16},{21,... | collective-permute-start | bytes 589832 | tf_op jit(solution)/shard_map/ppermute | solution.py:468
  64.2 9.5 %collective-permute-done.18 = bf16[2,64,768]{2,1,0:T(8,128)(2,1)S(1)} collective-permute-done((bf16[2,64,768]{2,1,0:T(8,128)(2,1)S(1)}, bf16[2,64,768]{2,1,0:T(8,128)(2,1)S(1)}, u32[]{:S(2)}, u32[]{:S(2)}) %collective-permute-start.18) | collective-permute-done | bytes 196640 | tf_op jit(solution)/shard_map/ppermute | solution.py:453
  73.8 0.8 collective-permute-start.21
  74.6 1.3 %collective-permute-start.19 = (bf16[2,64,768]{2,1,0:T(8,128)(2,1)S(1)}, bf16[2,64,768]{2,1,0:T(8,128)(2,1)S(1)}, u32[]{:S(2)}, u32[]{:S(2)}) collective-permute-start(bf16[2,64,768]{2,1,0:T(8,128)(2,1)S(1)} %collective-permute-done.18), channel_id=1, source_target_pairs={{4,0},{5,1},{6,2},{7,3},{12,8},{13,9},{14,10},{15,11},{20,16},{21,... | collective-permute-start | bytes 589832 | tf_op jit(solution)/shard_map/ppermute | solution.py:468
  76.0 4.7 %collective-permute-done.20 = bf16[2,64,768]{2,1,0:T(8,128)(2,1)S(1)} collective-permute-done((bf16[2,64,768]{2,1,0:T(8,128)(2,1)S(1)}, bf16[2,64,768]{2,1,0:T(8,128)(2,1)S(1)}, u32[]{:S(2)}, u32[]{:S(2)}) %collective-permute-start.20) | collective-permute-done | bytes 196640 | tf_op jit(solution)/shard_map/ppermute | solution.py:453
  80.8 1.3 %collective-permute-start.22 = (bf16[4,64,768]{2,1,0:T(8,128)(2,1)S(1)}, bf16[4,64,768]{2,1,0:T(8,128)(2,1)S(1)}, u32[]{:S(2)}, u32[]{:S(2)}) collective-permute-start(bf16[4,64,768]{2,1,0:T(8,128)(2,1)S(1)} %constant_dynamic-update-slice_fusion.refs_1_), channel_id=1, source_target_pairs={{4,0},{5,1},{6,2},{7,3},{12,8},{13,9},{14,10},{15,11},{20,16},{21,... | collective-permute-start | bytes 1179656 | tf_op jit(solution)/shard_map/ppermute | solution.py:468
  82.1 1.4 %collective-permute-start.25 = (bf16[4,64,768]{2,1,0:T(8,128)(2,1)S(1)}, bf16[4,64,768]{2,1,0:T(8,128)(2,1)S(1)}, u32[]{:S(2)}, u32[]{:S(2)}) collective-permute-start(bf16[4,64,768]{2,1,0:T(8,128)(2,1)S(1)} %pad_maximum_fusion.1), channel_id=1, source_target_pairs={{0,16},{8,24},{16,0},{24,8},{1,17},{9,25},{17,1},{25,9},{2,18},{10... | collective-permute-start | bytes 1179656 | tf_op jit(solution)/shard_map/ppermute | solution.py:453
  84.0 8.1 %collective-permute-done.22 = bf16[4,64,768]{2,1,0:T(8,128)(2,1)S(1)} collective-permute-done((bf16[4,64,768]{2,1,0:T(8,128)(2,1)S(1)}, bf16[4,64,768]{2,1,0:T(8,128)(2,1)S(1)}, u32[]{:S(2)}, u32[]{:S(2)}) %collective-permute-start.22) | collective-permute-done | bytes 393248 | tf_op jit(solution)/shard_map/ppermute | solution.py:468
  92.1 0.8 collective-permute-start.24
  93.0 1.4 %collective-permute-start.23 = (bf16[3,64,768]{2,1,0:T(8,128)(2,1)S(1)}, bf16[3,64,768]{2,1,0:T(8,128)(2,1)S(1)}, u32[]{:S(2)}, u32[]{:S(2)}) collective-permute-start(bf16[3,64,768]{2,1,0:T(8,128)(2,1)S(1)} %pad_maximum_fusion.3), channel_id=1, source_target_pairs={{0,16},{8,24},{16,0},{24,8},{1,17},{9,25},{17,1},{25,9},{2,18},{10... | collective-permute-start | bytes 884744 | tf_op jit(solution)/shard_map/ppermute | solution.py:453
  94.5 1.3 %collective-permute-start.27 = (bf16[2,64,768]{2,1,0:T(8,128)(2,1)S(1)}, bf16[2,64,768]{2,1,0:T(8,128)(2,1)S(1)}, u32[]{:S(2)}, u32[]{:S(2)}) collective-permute-start(bf16[2,64,768]{2,1,0:T(8,128)(2,1)S(1)} %pad_maximum_fusion.9), channel_id=1, source_target_pairs={{4,0},{5,1},{6,2},{7,3},{12,8},{13,9},{14,10},{15,11},{20,16},{21,... | collective-permute-start | bytes 589832 | tf_op jit(solution)/shard_map/ppermute | solution.py:468
  96.2 7.3 %collective-permute-done.27 = bf16[2,64,768]{2,1,0:T(8,128)(2,1)S(1)} collective-permute-done((bf16[2,64,768]{2,1,0:T(8,128)(2,1)S(1)}, bf16[2,64,768]{2,1,0:T(8,128)(2,1)S(1)}, u32[]{:S(2)}, u32[]{:S(2)}) %collective-permute-start.27) | collective-permute-done | bytes 196640 | tf_op jit(solution)/shard_map/ppermute | solution.py:468
  104.1 1.0 collective-permute-done.29.refs_6_
  105.2 0.6 collective-permute-done.30.refs_7_
  106.3 2.7 %place.2 = (bf16[2,64,12288]{2,1,0:T(8,128)(2,1)}, bf16[2,64,12288]{2,1,0:T(8,128)(2,1)}) custom-call(s32[4,3]{1,0:T(4,128)S(1)} %copy-done.7, bf16[4,64,768]{2,1,0:T(8,128)(2,1)S(1)} %constant_dynamic-update-slice_fusion.2.refs_0_, bf16[4,64,768]{2,1,0:T(8,128)(2,1)S(1)} %constant_dynamic-update-slice_fusion.refs_1_, ...), custom_call_target="tpu_custom_call" | custom-call | bytes 9437184 | tf_op jit(solution)/shard_map/place/pallas_call | solution.py:434
  109.0 0.7 collective-permute-start.33
  109.7 1.9 %collective-permute-done.33.refs_1_ = bf16[8,64,768]{2,1,0:T(8,128)(2,1)S(1)} collective-permute-done((bf16[8,64,768]{2,1,0:T(8,128)(2,1)S(1)}, bf16[8,64,768]{2,1,0:T(8,128)(2,1)S(1)}, u32[]{:S(2)}, u32[]{:S(2)}) %collective-permute-start.33) | collective-permute-done | bytes 786464 | tf_op jit(solution)/shard_map/ppermute | solution.py:453
  111.6 1.7 %place.3 = (bf16[2,64,12288]{2,1,0:T(8,128)(2,1)}, bf16[2,64,12288]{2,1,0:T(8,128)(2,1)}) custom-call(s32[4,3]{1,0:T(4,128)S(1)} %copy-done.7, bf16[8,64,768]{2,1,0:T(8,128)(2,1)S(1)} %pad_maximum_fusion.refs_0_, bf16[8,64,768]{2,1,0:T(8,128)(2,1)S(1)} %collective-permute-done.33.refs_1_, ...), custom_call_target="tpu_custom_call", output_to_operand_aliasing={{0}: (3, {}), {1}: (4, {})} | custom-call | bytes 3145728 | tf_op jit(solution)/shard_map/place/pallas_call | solution.py:434
  (80 shorter events, 4.0 us)
Async XLA Ops:
  1.7 9.0 %collective-permute-start = (bf16[128,768]{1,0:T(8,128)(2,1)S(1)}, bf16[128,768]{1,0:T(8,128)(2,1)S(1)}, u32[]{:S(2)}, u32[]{:S(2)}) collective-permute-start(bf16[128,768]{1,0:T(8,128)(2,1)S(1)} %pad_maximum_fusion.5.refs_0_), channel_id=1, source_target_pairs={{4,0},{0,4},{5,1},{1,5},{6,2},{2,6},{7,3},{3,7},{12,8},{8,12},{13,... | collective-permute-start | bytes 589832 | tf_op jit(solution)/shard_map/ppermute | solution.py:463
  4.7 8.1 %copy-start = (bf16[1,4,32,12288]{3,2,1,0:T(8,128)(2,1)S(1)}, bf16[1,4,32,12288]{3,2,1,0:T(8,128)(2,1)}, u32[]{:S(2)}) copy-start(bf16[1,4,32,12288]{3,2,1,0:T(8,128)(2,1)} %param.13) | copy-start | bytes 9437188
  4.7 8.1 %copy-start.8 = (s32[4]{0:T(128)S(1)}, s32[4]{0:T(128)}, u32[]{:S(2)}) copy-start(s32[4]{0:T(128)} %counts.3) | copy-start | bytes 52
  10.9 4.1 %collective-permute-start.4 = (f32[64,128]{1,0:T(8,128)S(1)}, f32[64,128]{1,0:T(8,128)S(1)}, u32[]{:S(2)}, u32[]{:S(2)}) collective-permute-start(f32[64,128]{1,0:T(8,128)S(1)} %get-tuple-element.43), channel_id=1, source_target_pairs={{0,24},{8,16},{16,8},{24,0},{1,25},{9,17},{17,9},{25,1},{2,26},{10... | collective-permute-start | bytes 98312 | tf_op jit(solution)/shard_map/ppermute | solution.py:453
  11.7 4.2 %collective-permute-start.3 = (f32[64,128]{1,0:T(8,128)S(1)}, f32[64,128]{1,0:T(8,128)S(1)}, u32[]{:S(2)}, u32[]{:S(2)}) collective-permute-start(f32[64,128]{1,0:T(8,128)S(1)} %get-tuple-element.43), channel_id=1, source_target_pairs={{0,16},{8,24},{16,0},{24,8},{1,17},{9,25},{17,1},{25,9},{2,18},{10... | collective-permute-start | bytes 98312 | tf_op jit(solution)/shard_map/ppermute | solution.py:453
  12.6 3.3 %collective-permute-start.2 = (f32[64,128]{1,0:T(8,128)S(1)}, f32[64,128]{1,0:T(8,128)S(1)}, u32[]{:S(2)}, u32[]{:S(2)}) collective-permute-start(f32[64,128]{1,0:T(8,128)S(1)} %get-tuple-element.43), channel_id=1, source_target_pairs={{0,8},{8,0},{16,24},{24,16},{1,9},{9,1},{17,25},{25,17},{2,10},{10... | collective-permute-start | bytes 98312 | tf_op jit(solution)/shard_map/ppermute | solution.py:453
  12.8 11.9 %copy-start.7 = (s32[4,3]{1,0:T(4,128)S(1)}, s32[4,3]{1,0:T(4,128)}, u32[]{:S(2)}) copy-start(s32[4,3]{1,0:T(4,128)} %bounds.5) | copy-start | bytes 148
  14.4 10.4 %collective-permute-start.1 = (f32[128,384]{1,0:T(8,128)S(1)}, f32[128,384]{1,0:T(8,128)S(1)}, u32[]{:S(2)}, u32[]{:S(2)}) collective-permute-start(f32[128,384]{1,0:T(8,128)S(1)} %project_back.1.refs_0_), channel_id=1, source_target_pairs={{4,0},{0,4},{5,1},{1,5},{6,2},{2,6},{7,3},{3,7},{12,8},{8,12},{13,... | collective-permute-start | bytes 589832 | tf_op jit(solution)/shard_map/ppermute | solution.py:463
  15.9 4.0 %collective-permute-start.5 = (f32[64,128]{1,0:T(8,128)S(1)}, f32[64,128]{1,0:T(8,128)S(1)}, u32[]{:S(2)}, u32[]{:S(2)}) collective-permute-start(f32[64,128]{1,0:T(8,128)S(1)} %add_add_fusion), channel_id=1, source_target_pairs={{0,1},{1,0},{2,3},{3,2},{4,5},{5,4},{6,7},{7,6},{8,9},{9,8},{10,11... | collective-permute-start | bytes 98312 | tf_op jit(solution)/shard_map/ppermute | solution.py:453
  19.9 4.8 %collective-permute-start.6 = (f32[64,128]{1,0:T(8,128)S(1)}, f32[64,128]{1,0:T(8,128)S(1)}, u32[]{:S(2)}, u32[]{:S(2)}) collective-permute-start(f32[64,128]{1,0:T(8,128)S(1)} %add.92.refs_2_), channel_id=1, source_target_pairs={{0,2},{1,3},{2,0},{3,1},{4,6},{5,7},{6,4},{7,5},{8,10},{9,11},{10,... | collective-permute-start | bytes 98312 | tf_op jit(solution)/shard_map/ppermute | solution.py:453
  27.7 4.6 %collective-permute-start.7 = (bf16[2,8,64,768]{3,2,1,0:T(8,128)(2,1)S(1)}, bf16[2,8,64,768]{3,2,1,0:T(8,128)(2,1)S(1)}, u32[]{:S(2)}, u32[]{:S(2)}) collective-permute-start(bf16[2,8,64,768]{3,2,1,0:T(8,128)(2,1)S(1)} %gradient.3), channel_id=1, source_target_pairs={{0,8},{8,0},{16,24},{24,16},{1,9},{9,1},{17,25},{25,17},{2,10},{10... | collective-permute-start | bytes 4718600 | tf_op jit(solution)/shard_map/ppermute | solution.py:453
  27.8 4.5 %collective-permute-start.8 = (f32[128,128]{1,0:T(8,128)S(1)}, f32[128,128]{1,0:T(8,128)S(1)}, u32[]{:S(2)}, u32[]{:S(2)}) collective-permute-start(f32[128,128]{1,0:T(8,128)S(1)} %get-tuple-element.47), channel_id=1, source_target_pairs={{0,1},{1,0},{2,3},{3,2},{4,5},{5,4},{6,7},{7,6},{8,9},{9,8},{10,11... | collective-permute-start | bytes 196616 | tf_op jit(solution)/shard_map/ppermute | solution.py:453
  30.0 31.1 %copy-start.1 = (f32[1,64,768]{2,1,0:T(8,128)S(1)}, f32[1,64,768]{2,1,0:T(8,128)}, u32[]{:S(2)}) copy-start(f32[1,64,768]{2,1,0:T(8,128)} %refs_5_.1) | copy-start | bytes 589828
  30.0 31.1 %copy-start.2 = (f32[1,64,768]{2,1,0:T(8,128)S(1)}, f32[1,64,768]{2,1,0:T(8,128)}, u32[]{:S(2)}) copy-start(f32[1,64,768]{2,1,0:T(8,128)} %refs_4_.1) | copy-start | bytes 589828
  30.0 31.1 %copy-start.3 = (f32[1,64,768]{2,1,0:T(8,128)S(1)}, f32[1,64,768]{2,1,0:T(8,128)}, u32[]{:S(2)}) copy-start(f32[1,64,768]{2,1,0:T(8,128)} %refs_6_.1) | copy-start | bytes 589828
  30.0 31.1 %copy-start.4 = (f32[1,64,768]{2,1,0:T(8,128)S(1)}, f32[1,64,768]{2,1,0:T(8,128)}, u32[]{:S(2)}) copy-start(f32[1,64,768]{2,1,0:T(8,128)} %refs_7_.1) | copy-start | bytes 589828
  30.0 31.1 %copy-start.5 = (f32[1,64,768]{2,1,0:T(8,128)S(1)}, f32[1,64,768]{2,1,0:T(8,128)}, u32[]{:S(2)}) copy-start(f32[1,64,768]{2,1,0:T(8,128)} %refs_8_.1) | copy-start | bytes 589828
  30.1 31.1 %copy-start.6 = (f32[1,64,768]{2,1,0:T(8,128)S(1)}, f32[1,64,768]{2,1,0:T(8,128)}, u32[]{:S(2)}) copy-start(f32[1,64,768]{2,1,0:T(8,128)} %refs_9_.1) | copy-start | bytes 589828
  32.5 10.7 %collective-permute-start.9 = (bf16[4,64,768]{2,1,0:T(8,128)(2,1)S(1)}, bf16[4,64,768]{2,1,0:T(8,128)(2,1)S(1)}, u32[]{:S(2)}, u32[]{:S(2)}) collective-permute-start(bf16[4,64,768]{2,1,0:T(8,128)(2,1)S(1)} %get-tuple-element.48), channel_id=1, source_target_pairs={{0,16},{8,24},{16,0},{24,8},{1,17},{9,25},{17,1},{25,9},{2,18},{10... | collective-permute-start | bytes 1179656 | tf_op jit(solution)/shard_map/ppermute | solution.py:453
  33.3 10.4 %collective-permute-start.11 = (bf16[4,64,768]{2,1,0:T(8,128)(2,1)S(1)}, bf16[4,64,768]{2,1,0:T(8,128)(2,1)S(1)}, u32[]{:S(2)}, u32[]{:S(2)}) collective-permute-start(bf16[4,64,768]{2,1,0:T(8,128)(2,1)S(1)} %get-tuple-element.49), channel_id=1, source_target_pairs={{0,1},{1,0},{2,3},{3,2},{4,5},{5,4},{6,7},{7,6},{8,9},{9,8},{10,11... | collective-permute-start | bytes 1179656 | tf_op jit(solution)/shard_map/ppermute | solution.py:453
  43.8 5.8 %collective-permute-start.12 = (bf16[2,64,768]{2,1,0:T(8,128)(2,1)S(1)}, bf16[2,64,768]{2,1,0:T(8,128)(2,1)S(1)}, u32[]{:S(2)}, u32[]{:S(2)}) collective-permute-start(bf16[2,64,768]{2,1,0:T(8,128)(2,1)S(1)} %get-tuple-element.68), channel_id=1, source_target_pairs={{0,16},{8,24},{16,0},{24,8},{1,17},{9,25},{17,1},{25,9},{2,18},{10... | collective-permute-start | bytes 589832 | tf_op jit(solution)/shard_map/ppermute | solution.py:453
  45.2 6.0 %collective-permute-start.10 = (bf16[2,64,768]{2,1,0:T(8,128)(2,1)S(1)}, bf16[2,64,768]{2,1,0:T(8,128)(2,1)S(1)}, u32[]{:S(2)}, u32[]{:S(2)}) collective-permute-start(bf16[2,64,768]{2,1,0:T(8,128)(2,1)S(1)} %get-tuple-element.69), channel_id=1, source_target_pairs={{0,1},{1,0},{2,3},{3,2},{4,5},{5,4},{6,7},{7,6},{8,9},{9,8},{10,11... | collective-permute-start | bytes 589832 | tf_op jit(solution)/shard_map/ppermute | solution.py:453
  46.8 7.0 %collective-permute-start.14 = (f32[128,128]{1,0:T(8,128)S(1)}, f32[128,128]{1,0:T(8,128)S(1)}, u32[]{:S(2)}, u32[]{:S(2)}) collective-permute-start(f32[128,128]{1,0:T(8,128)S(1)} %add.95), channel_id=1, source_target_pairs={{0,2},{1,3},{2,0},{3,1},{4,6},{5,7},{6,4},{7,5},{8,10},{9,11},{10,... | collective-permute-start | bytes 196616 | tf_op jit(solution)/shard_map/ppermute | solution.py:453
  51.3 9.8 %collective-permute-start.13 = (bf16[2,64,768]{2,1,0:T(8,128)(2,1)S(1)}, bf16[2,64,768]{2,1,0:T(8,128)(2,1)S(1)}, u32[]{:S(2)}, u32[]{:S(2)}) collective-permute-start(bf16[2,64,768]{2,1,0:T(8,128)(2,1)S(1)} %pad_maximum_fusion.6), channel_id=1, source_target_pairs={{0,2},{1,3},{2,0},{3,1},{4,6},{5,7},{6,4},{7,5},{8,10},{9,11},{10,... | collective-permute-start | bytes 589832 | tf_op jit(solution)/shard_map/ppermute | solution.py:453
  53.8 1.3 %collective-permute-start.15 = (f32[128,128]{1,0:T(8,128)S(1)}, f32[128,128]{1,0:T(8,128)S(1)}, u32[]{:S(2)}, u32[]{:S(2)}) collective-permute-start(f32[128,128]{1,0:T(8,128)S(1)} %add.110), channel_id=1, source_target_pairs={{0,8},{8,0},{16,24},{24,16},{1,9},{9,1},{17,25},{25,17},{2,10},{10... | collective-permute-start | bytes 196616 | tf_op jit(solution)/shard_map/ppermute | solution.py:453
  55.2 4.3 %collective-permute-start.16 = (f32[128,128]{1,0:T(8,128)S(1)}, f32[128,128]{1,0:T(8,128)S(1)}, u32[]{:S(2)}, u32[]{:S(2)}) collective-permute-start(f32[128,128]{1,0:T(8,128)S(1)} %add.111.refs_1_), channel_id=1, source_target_pairs={{0,16},{8,24},{16,0},{24,8},{1,17},{9,25},{17,1},{25,9},{2,18},{10... | collective-permute-start | bytes 196616 | tf_op jit(solution)/shard_map/ppermute | solution.py:453
  62.9 10.8 %collective-permute-start.18 = (bf16[2,64,768]{2,1,0:T(8,128)(2,1)S(1)}, bf16[2,64,768]{2,1,0:T(8,128)(2,1)S(1)}, u32[]{:S(2)}, u32[]{:S(2)}) collective-permute-start(bf16[2,64,768]{2,1,0:T(8,128)(2,1)S(1)} %get-tuple-element.52), channel_id=1, source_target_pairs={{0,2},{1,3},{2,0},{3,1},{4,6},{5,7},{6,4},{7,5},{8,10},{9,11},{10,... | collective-permute-start | bytes 589832 | tf_op jit(solution)/shard_map/ppermute | solution.py:453
  62.9 13.0 %collective-permute-start.17 = (bf16[2,64,768]{2,1,0:T(8,128)(2,1)S(1)}, bf16[2,64,768]{2,1,0:T(8,128)(2,1)S(1)}, u32[]{:S(2)}, u32[]{:S(2)}) collective-permute-start(bf16[2,64,768]{2,1,0:T(8,128)(2,1)S(1)} %get-tuple-element.52), channel_id=1, source_target_pairs={{4,0},{5,1},{6,2},{7,3},{12,8},{13,9},{14,10},{15,11},{20,16},{21,... | collective-permute-start | bytes 589832 | tf_op jit(solution)/shard_map/ppermute | solution.py:468
  73.8 7.0 %collective-permute-start.21 = (bf16[2,64,768]{2,1,0:T(8,128)(2,1)S(1)}, bf16[2,64,768]{2,1,0:T(8,128)(2,1)S(1)}, u32[]{:S(2)}, u32[]{:S(2)}) collective-permute-start(bf16[2,64,768]{2,1,0:T(8,128)(2,1)S(1)} %pad_maximum_fusion.8), channel_id=1, source_target_pairs={{0,16},{8,24},{16,0},{24,8},{1,17},{9,25},{17,1},{25,9},{2,18},{10... | collective-permute-start | bytes 589832 | tf_op jit(solution)/shard_map/ppermute | solution.py:453
  74.5 6.2 %collective-permute-start.20 = (bf16[2,64,768]{2,1,0:T(8,128)(2,1)S(1)}, bf16[2,64,768]{2,1,0:T(8,128)(2,1)S(1)}, u32[]{:S(2)}, u32[]{:S(2)}) collective-permute-start(bf16[2,64,768]{2,1,0:T(8,128)(2,1)S(1)} %pad_maximum_fusion.7), channel_id=1, source_target_pairs={{0,1},{1,0},{2,3},{3,2},{4,5},{5,4},{6,7},{7,6},{8,9},{9,8},{10,11... | collective-permute-start | bytes 589832 | tf_op jit(solution)/shard_map/ppermute | solution.py:453
  74.6 9.3 %collective-permute-start.19 = (bf16[2,64,768]{2,1,0:T(8,128)(2,1)S(1)}, bf16[2,64,768]{2,1,0:T(8,128)(2,1)S(1)}, u32[]{:S(2)}, u32[]{:S(2)}) collective-permute-start(bf16[2,64,768]{2,1,0:T(8,128)(2,1)S(1)} %collective-permute-done.18), channel_id=1, source_target_pairs={{4,0},{5,1},{6,2},{7,3},{12,8},{13,9},{14,10},{15,11},{20,16},{21,... | collective-permute-start | bytes 589832 | tf_op jit(solution)/shard_map/ppermute | solution.py:468
  80.8 11.3 %collective-permute-start.22 = (bf16[4,64,768]{2,1,0:T(8,128)(2,1)S(1)}, bf16[4,64,768]{2,1,0:T(8,128)(2,1)S(1)}, u32[]{:S(2)}, u32[]{:S(2)}) collective-permute-start(bf16[4,64,768]{2,1,0:T(8,128)(2,1)S(1)} %constant_dynamic-update-slice_fusion.refs_1_), channel_id=1, source_target_pairs={{4,0},{5,1},{6,2},{7,3},{12,8},{13,9},{14,10},{15,11},{20,16},{21,... | collective-permute-start | bytes 1179656 | tf_op jit(solution)/shard_map/ppermute | solution.py:468
  82.1 12.4 %collective-permute-start.25 = (bf16[4,64,768]{2,1,0:T(8,128)(2,1)S(1)}, bf16[4,64,768]{2,1,0:T(8,128)(2,1)S(1)}, u32[]{:S(2)}, u32[]{:S(2)}) collective-permute-start(bf16[4,64,768]{2,1,0:T(8,128)(2,1)S(1)} %pad_maximum_fusion.1), channel_id=1, source_target_pairs={{0,16},{8,24},{16,0},{24,8},{1,17},{9,25},{17,1},{25,9},{2,18},{10... | collective-permute-start | bytes 1179656 | tf_op jit(solution)/shard_map/ppermute | solution.py:453
  83.6 10.9 %collective-permute-start.26 = (bf16[4,64,768]{2,1,0:T(8,128)(2,1)S(1)}, bf16[4,64,768]{2,1,0:T(8,128)(2,1)S(1)}, u32[]{:S(2)}, u32[]{:S(2)}) collective-permute-start(bf16[4,64,768]{2,1,0:T(8,128)(2,1)S(1)} %pad_maximum_fusion.2), channel_id=1, source_target_pairs={{0,1},{1,0},{2,3},{3,2},{4,5},{5,4},{6,7},{7,6},{8,9},{9,8},{10,11... | collective-permute-start | bytes 1179656 | tf_op jit(solution)/shard_map/ppermute | solution.py:453
  92.1 11.3 %collective-permute-start.24 = (bf16[3,64,768]{2,1,0:T(8,128)(2,1)S(1)}, bf16[3,64,768]{2,1,0:T(8,128)(2,1)S(1)}, u32[]{:S(2)}, u32[]{:S(2)}) collective-permute-start(bf16[3,64,768]{2,1,0:T(8,128)(2,1)S(1)} %pad_maximum_fusion.4), channel_id=1, source_target_pairs={{0,1},{1,0},{2,3},{3,2},{4,5},{5,4},{6,7},{7,6},{8,9},{9,8},{10,11... | collective-permute-start | bytes 884744 | tf_op jit(solution)/shard_map/ppermute | solution.py:453
  92.9 13.4 %collective-permute-start.32 = (bf16[8,64,768]{2,1,0:T(8,128)(2,1)S(1)}, bf16[8,64,768]{2,1,0:T(8,128)(2,1)S(1)}, u32[]{:S(2)}, u32[]{:S(2)}) collective-permute-start(bf16[8,64,768]{2,1,0:T(8,128)(2,1)S(1)} %constant_dynamic-update-slice_fusion.4.refs_4_), channel_id=1, source_target_pairs={{0,8},{8,0},{16,24},{24,16},{1,9},{9,1},{17,25},{25,17},{2,10},{10... | collective-permute-start | bytes 2359304 | tf_op jit(solution)/shard_map/ppermute | solution.py:453
  93.0 10.9 %collective-permute-start.23 = (bf16[3,64,768]{2,1,0:T(8,128)(2,1)S(1)}, bf16[3,64,768]{2,1,0:T(8,128)(2,1)S(1)}, u32[]{:S(2)}, u32[]{:S(2)}) collective-permute-start(bf16[3,64,768]{2,1,0:T(8,128)(2,1)S(1)} %pad_maximum_fusion.3), channel_id=1, source_target_pairs={{0,16},{8,24},{16,0},{24,8},{1,17},{9,25},{17,1},{25,9},{2,18},{10... | collective-permute-start | bytes 884744 | tf_op jit(solution)/shard_map/ppermute | solution.py:453
  94.5 8.9 %collective-permute-start.27 = (bf16[2,64,768]{2,1,0:T(8,128)(2,1)S(1)}, bf16[2,64,768]{2,1,0:T(8,128)(2,1)S(1)}, u32[]{:S(2)}, u32[]{:S(2)}) collective-permute-start(bf16[2,64,768]{2,1,0:T(8,128)(2,1)S(1)} %pad_maximum_fusion.9), channel_id=1, source_target_pairs={{4,0},{5,1},{6,2},{7,3},{12,8},{13,9},{14,10},{15,11},{20,16},{21,... | collective-permute-start | bytes 589832 | tf_op jit(solution)/shard_map/ppermute | solution.py:468
  95.9 8.3 %collective-permute-start.28 = (bf16[4,64,768]{2,1,0:T(8,128)(2,1)S(1)}, bf16[4,64,768]{2,1,0:T(8,128)(2,1)S(1)}, u32[]{:S(2)}, u32[]{:S(2)}) collective-permute-start(bf16[4,64,768]{2,1,0:T(8,128)(2,1)S(1)} %constant_dynamic-update-slice_fusion.2.refs_0_), channel_id=1, source_target_pairs={{0,8},{8,0},{16,24},{24,16},{1,9},{9,1},{17,25},{25,17},{2,10},{10... | collective-permute-start | bytes 1179656 | tf_op jit(solution)/shard_map/ppermute | solution.py:453
  103.4 1.7 %collective-permute-start.29 = (bf16[4,64,768]{2,1,0:T(8,128)(2,1)S(1)}, bf16[4,64,768]{2,1,0:T(8,128)(2,1)S(1)}, u32[]{:S(2)}, u32[]{:S(2)}) collective-permute-start(bf16[4,64,768]{2,1,0:T(8,128)(2,1)S(1)} %constant_dynamic-update-slice_fusion.refs_1_), channel_id=1, source_target_pairs={{0,8},{8,0},{16,24},{24,16},{1,9},{9,1},{17,25},{25,17},{2,10},{10... | collective-permute-start | bytes 1179656 | tf_op jit(solution)/shard_map/ppermute | solution.py:453
  103.5 2.3 %collective-permute-start.30 = (bf16[4,64,768]{2,1,0:T(8,128)(2,1)S(1)}, bf16[4,64,768]{2,1,0:T(8,128)(2,1)S(1)}, u32[]{:S(2)}, u32[]{:S(2)}) collective-permute-start(bf16[4,64,768]{2,1,0:T(8,128)(2,1)S(1)} %collective-permute-done.25.refs_2_), channel_id=1, source_target_pairs={{0,8},{8,0},{16,24},{24,16},{1,9},{9,1},{17,25},{25,17},{2,10},{10... | collective-permute-start | bytes 1179656 | tf_op jit(solution)/shard_map/ppermute | solution.py:453
  104.0 2.3 %collective-permute-start.31 = (bf16[4,64,768]{2,1,0:T(8,128)(2,1)S(1)}, bf16[4,64,768]{2,1,0:T(8,128)(2,1)S(1)}, u32[]{:S(2)}, u32[]{:S(2)}) collective-permute-start(bf16[4,64,768]{2,1,0:T(8,128)(2,1)S(1)} %collective-permute-done.26.refs_3_), channel_id=1, source_target_pairs={{0,8},{8,0},{16,24},{24,16},{1,9},{9,1},{17,25},{25,17},{2,10},{10... | collective-permute-start | bytes 1179656 | tf_op jit(solution)/shard_map/ppermute | solution.py:453
  109.0 2.6 %collective-permute-start.33 = (bf16[8,64,768]{2,1,0:T(8,128)(2,1)S(1)}, bf16[8,64,768]{2,1,0:T(8,128)(2,1)S(1)}, u32[]{:S(2)}, u32[]{:S(2)}) collective-permute-start(bf16[8,64,768]{2,1,0:T(8,128)(2,1)S(1)} %pad_maximum_fusion.refs_0_), channel_id=1, source_target_pairs={{0,8},{8,0},{16,24},{24,16},{1,9},{9,1},{17,25},{25,17},{2,10},{10... | collective-permute-start | bytes 2359304 | tf_op jit(solution)/shard_map/ppermute | solution.py:453

commit v4 on v3

--- a/solution.py
+++ b/solution.py
@@ -475,24 +475,38 @@
     return total.astype(bf16)
 
 
-def reduced(factors, hidden, cot, columns, mixed):
+def reduced(factors, hidden, cot, columns):
     sent = gradient(factors, hidden, cot, 1, columns)
     near = swapped(sent, "replica", 1)
     kept = gradient(factors, hidden, cot, 0, columns)
-    mixed = mixed + swapped(mixed, "tensor", 1)
 
     def part(which, cut, *steps):
         return summed(kept[which, cut], near[which, cut], *steps)
 
     high, low = slice(4, 8), slice(2, 4)
-    down_one, up_one, mixed = lax.optimization_barrier((part(0, high), part(1, high), mixed))
-    down_one = swapped(down_one, "replica", 2)
-    up_one = swapped(up_one, "tensor", 1)
+    down_one = swapped(part(0, high), "replica", 2)
+    up_one = swapped(part(1, high), "tensor", 1)
     down_two = swapped(part(0, low, down_one[2:]), "tensor", 1)
     up_two = swapped(part(1, low, up_one[2:]), "replica", 2)
     last = jnp.stack([part(0, 1, down_one[1], down_two[1]), part(1, 1, up_one[1], up_two[1])])
     last = swapped(last, "tensor", 2)
-    return (kept, near, (down_one, down_two), (up_one, up_two), last), mixed
+    return (kept, near, (down_one, down_two), (up_one, up_two), last)
+
+
+def swapped_before_last(block, axis, distance):
+    size, sections = lax.axis_size(axis), lax.axis_size("section")
+    ahead = axis == "replica"
+    axes = (axis, "section") if ahead else ("section", axis)
+
+    def place_of(i, section):
+        return i * sections + section if ahead else section * size + i
+
+    route = [
+        (place_of(i, section), place_of(i ^ distance, section))
+        for i in range(size)
+        for section in range(sections - 1)
+    ]
+    return lax.ppermute(block, axes, route)
 
 
 def crossed(piece, axis, distance):
@@ -501,7 +515,8 @@
         (which, order ^ distance, hop) if axis == "replica" else (which, order, hop ^ distance)
         for which, order, hop in blocks
     ]
-    return (window, blocks, swapped(array, axis, distance))
+    swap = swapped if window == 0 else swapped_before_last
+    return (window, blocks, swap(array, axis, distance))
 
 
 def fetched(piece):
@@ -516,11 +531,6 @@
 def joined(*pieces):
     blocks = [block for piece in pieces for block in piece[1]]
     return (pieces[0][0], blocks, jnp.concatenate([piece[2] for piece in pieces]))
-
-
-def ordered(*pieces):
-    arrays = lax.optimization_barrier(tuple(piece[2] for piece in pieces))
-    return [(*piece[:2], array) for piece, array in zip(pieces, arrays)]
 
 
 def spread(share, bounds, slots, features):
@@ -528,37 +538,33 @@
     own = (0, [(0, 0, 0), (1, 0, 0)], share)
     one = crossed(own, "tensor", 2)
     next_own = fetched(own)
-    both = joined(picked(own, slice(0, 1)), picked(one, slice(0, 1)))
-    both_up = joined(picked(own, slice(1, 2)), picked(one, slice(1, 2)))
-    down_two = crossed(both, "tensor", 1)
-    up_two = crossed(both_up, "replica", 2)
+    downs = joined(picked(own, slice(0, 1)), picked(one, slice(0, 1)))
+    ups = joined(picked(own, slice(1, 2)), picked(one, slice(1, 2)))
+    down_two = crossed(downs, "tensor", 1)
+    up_two = crossed(ups, "replica", 2)
     next_one = fetched(one)
     two = joined(down_two, up_two)
-    down_three = crossed(joined(both, down_two), "replica", 2)
-    up_three = crossed(joined(both_up, up_two), "tensor", 1)
+    down_three = crossed(joined(downs, down_two), "replica", 2)
+    up_three = crossed(joined(ups, up_two), "tensor", 1)
     next_two = fetched(two)
-    last, first = slice(3, 4), slice(0, 1)
+    near = joined(own, one, two)
+    near_core = crossed(near, "replica", 1)
+    last, first, second = slice(3, 4), slice(0, 1), slice(1, 2)
     next_end = fetched(joined(picked(down_three, last), picked(up_three, last)))
     next_near = joined(next_own, next_one, next_two)
-    down_end = crossed(
-        joined(picked(next_own, first), picked(next_one, first), picked(next_two, first)),
-        "replica",
-        2,
+    down_end = joined(*(picked(piece, first) for piece in (next_own, next_one, next_two)))
+    up_end = joined(
+        picked(next_own, second), picked(next_one, second), picked(next_two, slice(2, 3))
     )
-    second = slice(1, 2)
-    up_end = crossed(
-        joined(picked(next_own, second), picked(next_one, second), picked(next_two, slice(2, 3))),
-        "tensor",
-        1,
-    )
-    near = joined(own, one)
-    early = [near, two, down_three, up_three, next_near]
-    early += [crossed(piece, "replica", 1) for piece in early]
-    placed = place(bounds, early, [], slots, ranks, features)
-    end = joined(down_end, up_end, next_end)
-    end_array, *placed = lax.optimization_barrier((end[2], *placed))
-    end = (*end[:2], end_array)
-    return place(bounds, [end, crossed(end, "replica", 1)], placed, slots, ranks, features)
+    end = joined(crossed(down_end, "replica", 2), crossed(up_end, "tensor", 1), next_end)
+    placed = place(bounds, [near, near_core], [], slots, ranks, features)
+    far = joined(down_three, up_three)
+    far_array, *placed = lax.optimization_barrier((far[2], *placed))
+    far = (*far[:2], far_array)
+    for group in ((far, next_near), (end,)):
+        pieces = [*group, *(crossed(piece, "replica", 1) for piece in group)]
+        placed = place(bounds, pieces, placed, slots, ranks, features)
+    return placed
 
 
 def on_device(
@@ -599,8 +605,8 @@
         bounds, micro_counts, projections, tables, square, slots, features, per_micro
     )
 
-    parts, mixed = reduced(factors, hidden, cot, master_down.shape[2], mixed)
-    for axis, distance in (("tensor", 2), ("replica", 1)):
+    parts = reduced(factors, hidden, cot, master_down.shape[2])
+    for axis, distance in (("replica", 1), ("tensor", 1), ("tensor", 2)):
         mixed = mixed + swapped(mixed, axis, distance)
     other = swapped(mixed, "replica", 2)
     state = [master_down, master_up, moment_down, moment_up, second_down, second_up]

time: 114 us -> 117 us (1.026)
  starting transfers between devices: 34.6 us -> 39.2 us
  waiting for transfers between devices: 58.1 us -> 55.1 us
  Pallas kernels: 17.5 us -> 18.7 us
    ppermute x0 -> x4, starting transfers between devices: none -> 10.4 us  [swapped_before_last(): return lax.ppermute(block, axes, route)]
    ppermute x4, waiting for transfers between devices: 15.4 us -> 8.4 us  [following_layer(): return lax.ppermute(block, 'section', [(i + 1, i) for i in range(size - 1)])]
    ppermute x28 -> x22, starting transfers between devices: 25.8 us -> 20 us  [swapped(): return lax.ppermute(block, axis, route)]
    ppermute x0 -> x4, waiting for transfers between devices: none -> 2.06 us  [swapped_before_last(): return lax.ppermute(block, axes, route)]
    ppermute x28 -> x22, waiting for transfers between devices: 42.7 us -> 44.6 us  [swapped(): return lax.ppermute(block, axis, route)]
    pallas_call x2 -> x3, Pallas kernels: 4.46 us -> 5.69 us  [place(): pl.pallas_call(functools.partial(place_kernel, layout, not before), in_sp...]
  transfers between devices with their start and end apart: 34 -> 32, of which waited for: 18 -> 17; matrix products, arithmetic and copies ran while one was open for 1% -> 1% of each run, Pallas kernels for 7% -> 10%
where the time goes in v4:
time: 117 us; the launch traced here: 116 us
  waiting for transfers between devices  55.1 us (47%)
  starting transfers between devices  39.2 us (34%)
  Pallas kernels  18.7 us (16%)
  other arithmetic  1.86 us (2%)
  between operations  1.19 us (1%)
    ppermute x22, waiting for transfers between devices, swapped(): return lax.ppermute(block, axis, route)  44.6 us
    ppermute x22, starting transfers between devices, swapped(): return lax.ppermute(block, axis, route)  20 us
    ppermute x4, starting transfers between devices, swapped_before_last(): return lax.ppermute(block, axes, route)  10.4 us
    ppermute x4, waiting for transfers between devices, following_layer(): return lax.ppermute(block, 'section', [(i + 1, i) for i in range(size - 1)])  8.4 us
    pallas_call x1, Pallas kernels, project(): pl.pallas_call(functools.partial(project_kernel, steps), in_specs=[in_hbm...  5.99 us
    pallas_call x3, Pallas kernels, place(): pl.pallas_call(functools.partial(place_kernel, layout, not before), in_sp...  5.69 us
    ppermute x4, starting transfers between devices, following_layer(): return lax.ppermute(block, 'section', [(i + 1, i) for i in range(size - 1)])  5.15 us
    ppermute x2, starting transfers between devices, from_next(): return lax.ppermute(block, 'section', route)  3.69 us
  transfers between devices with their start and end apart: 32, of which 17 were waited for; matrix products, arithmetic and copies ran while one was open for 1% of the time, Pallas kernels for 10%

profile of v4, /device:TPU:0, one launch (start us, length us, event | category | flops | bytes accessed | tf_op | source)
XLA Modules:
  0.0 116.4 jit_solution(7928112139334552816)
XLA Ops:
  0.6 1.0 convert_bitcast_fusion
  1.7 3.0 %collective-permute-start = (bf16[128,768]{1,0:T(8,128)(2,1)S(1)}, bf16[128,768]{1,0:T(8,128)(2,1)S(1)}, u32[]{:S(2)}, u32[]{:S(2)}) collective-permute-start(bf16[128,768]{1,0:T(8,128)(2,1)S(1)} %pad_maximum_fusion.6.refs_0_), channel_id=1, source_target_pairs={{4,0},{0,4},{5,1},{1,5},{6,2},{2,6},{7,3},{3,7},{12,8},{8,12},{13,... | collective-permute-start | bytes 589832 | tf_op jit(solution)/shard_map/ppermute | solution.py:463
  4.7 6.0 %project.1 = (f32[128,256]{1,0:T(8,128)S(1)}, f32[128,128]{1,0:T(8,128)S(1)}, bf16[128,12288]{1,0:T(8,128)(2,1)S(1)}, bf16[128,12288]{1,0:T(8,128)(2,1)S(1)}) custom-call(bf16[128,12288]{1,0:T(8,128)(2,1)} %bitcast.39, bf16[2,64,12288]{2,1,0:T(8,128)(2,1)} %bitcast.40, bf16[2,64,12288]{2,1,0:T(8,128)(2,1)} %bitcast.41), custom_call_target="tpu_custom_call" | custom-call | flops 805306368 | bytes 9437184 | tf_op jit(solution)/shard_map/project/pallas_call | solution.py:98
  10.9 0.7 collective-permute-start.4
  11.7 0.9 collective-permute-start.3
  12.8 1.5 %project_back.1.refs_0_ = f32[128,384]{1,0:T(8,128)S(1)} custom-call(s32[4]{0:T(128)S(1)} %copy-done.8, f32[128,256]{1,0:T(8,128)S(1)} %get-tuple-element.37.by_hidden, bf16[128,12288]{1,0:T(8,128)(2,1)S(1)} %bitcast.34, bf16[128,12288]{1,0:T(8,128)(2,1)S(1)} %get-tuple-element.41.up_ref), custom_call_target="tpu_custom_call" | custom-call | flops 402653184 | bytes 6291456 | tf_op jit(solution)/shard_map/project_back/pallas_call | solution.py:133
  14.4 0.7 collective-permute-start.1
  15.1 0.8 collective-permute-done.3
  15.9 1.6 %collective-permute-start.5 = (f32[64,128]{1,0:T(8,128)S(1)}, f32[64,128]{1,0:T(8,128)S(1)}, u32[]{:S(2)}, u32[]{:S(2)}) collective-permute-start(f32[64,128]{1,0:T(8,128)S(1)} %add_add_fusion), channel_id=1, source_target_pairs={{0,1},{1,0},{2,3},{3,2},{4,5},{5,4},{6,7},{7,6},{8,9},{9,8},{10,11... | collective-permute-start | bytes 98312 | tf_op jit(solution)/shard_map/ppermute | solution.py:453
  17.6 2.3 %collective-permute-done.5 = f32[64,128]{1,0:T(8,128)S(1)} collective-permute-done((f32[64,128]{1,0:T(8,128)S(1)}, f32[64,128]{1,0:T(8,128)S(1)}, u32[]{:S(2)}, u32[]{:S(2)}) %collective-permute-start.5) | collective-permute-done | bytes 32800 | tf_op jit(solution)/shard_map/ppermute | solution.py:453
  19.9 2.6 %collective-permute-start.6 = (f32[64,128]{1,0:T(8,128)S(1)}, f32[64,128]{1,0:T(8,128)S(1)}, u32[]{:S(2)}, u32[]{:S(2)}) collective-permute-start(f32[64,128]{1,0:T(8,128)S(1)} %add.92.refs_2_), channel_id=1, source_target_pairs={{0,2},{1,3},{2,0},{3,1},{4,6},{5,7},{6,4},{7,5},{8,10},{9,11},{10,... | collective-permute-start | bytes 98312 | tf_op jit(solution)/shard_map/ppermute | solution.py:453
  22.5 2.2 %collective-permute-done.6.refs_3_ = f32[64,128]{1,0:T(8,128)S(1)} collective-permute-done((f32[64,128]{1,0:T(8,128)S(1)}, f32[64,128]{1,0:T(8,128)S(1)}, u32[]{:S(2)}, u32[]{:S(2)}) %collective-permute-start.6) | collective-permute-done | bytes 32800 | tf_op jit(solution)/shard_map/ppermute | solution.py:453
  24.7 2.3 %chain.1 = (bf16[128,256]{1,0:T(8,128)(2,1)S(1)}, f32[128,128]{1,0:T(8,128)S(1)}) custom-call(s32[4,3]{1,0:T(4,128)S(1)} %copy-done.7, s32[4]{0:T(128)S(1)} %copy-done.8, f32[128,384]{1,0:T(8,128)S(1)} %project_back.1.refs_0_, f32[128,384]{1,0:T(8,128)S(1)} %collective-permute-done.1.refs_1_, f32[64,128]{1,0:T(8,128)S(1)} %add.92.refs_2_, ...), custom_call_target="tpu_custom_call" | custom-call | tf_op jit(solution)/shard_map/chain/pallas_call | solution.py:297
  27.1 0.6 gradient.3
  28.4 2.7 %collective-permute-done.7.near = bf16[2,8,64,768]{3,2,1,0:T(8,128)(2,1)S(1)} collective-permute-done((bf16[2,8,64,768]{3,2,1,0:T(8,128)(2,1)S(1)}, bf16[2,8,64,768]{3,2,1,0:T(8,128)(2,1)S(1)}, u32[]{:S(2)}, u32[]{:S(2)}) %collective-permute-start.7) | collective-permute-done | bytes 1572896 | tf_op jit(solution)/shard_map/ppermute | solution.py:453
  31.3 1.6 %collective-permute-start.10 = (bf16[4,64,768]{2,1,0:T(8,128)(2,1)S(1)}, bf16[4,64,768]{2,1,0:T(8,128)(2,1)S(1)}, u32[]{:S(2)}, u32[]{:S(2)}) collective-permute-start(bf16[4,64,768]{2,1,0:T(8,128)(2,1)S(1)} %get-tuple-element.68), channel_id=1, source_target_pairs={{0,1},{1,0},{2,3},{3,2},{4,5},{5,4},{6,7},{7,6},{8,9},{9,8},{10,11... | collective-permute-start | bytes 1179656 | tf_op jit(solution)/shard_map/ppermute | solution.py:453
  33.0 0.7 collective-permute-start.8
  33.7 8.9 %collective-permute-done.10.up_one = bf16[4,64,768]{2,1,0:T(8,128)(2,1)S(1)} collective-permute-done((bf16[4,64,768]{2,1,0:T(8,128)(2,1)S(1)}, bf16[4,64,768]{2,1,0:T(8,128)(2,1)S(1)}, u32[]{:S(2)}, u32[]{:S(2)}) %collective-permute-start.10) | collective-permute-done | bytes 393248 | tf_op jit(solution)/shard_map/ppermute | solution.py:453
  42.6 1.3 %collective-permute-done.8.down_one = bf16[4,64,768]{2,1,0:T(8,128)(2,1)S(1)} collective-permute-done((bf16[4,64,768]{2,1,0:T(8,128)(2,1)S(1)}, bf16[4,64,768]{2,1,0:T(8,128)(2,1)S(1)}, u32[]{:S(2)}, u32[]{:S(2)}) %collective-permute-start.8) | collective-permute-done | bytes 393248 | tf_op jit(solution)/shard_map/ppermute | solution.py:453
  44.0 0.8 collective-permute-start.11
  45.2 1.3 %collective-permute-done.13 = f32[128,128]{1,0:T(8,128)S(1)} collective-permute-done((f32[128,128]{1,0:T(8,128)S(1)}, f32[128,128]{1,0:T(8,128)S(1)}, u32[]{:S(2)}, u32[]{:S(2)}) %collective-permute-start.13) | collective-permute-done | bytes 65568 | tf_op jit(solution)/shard_map/ppermute | solution.py:453
  46.5 1.6 %collective-permute-start.14 = (f32[128,128]{1,0:T(8,128)S(1)}, f32[128,128]{1,0:T(8,128)S(1)}, u32[]{:S(2)}, u32[]{:S(2)}) collective-permute-start(f32[128,128]{1,0:T(8,128)S(1)} %add.109), channel_id=1, source_target_pairs={{0,1},{1,0},{2,3},{3,2},{4,5},{5,4},{6,7},{7,6},{8,9},{9,8},{10,11... | collective-permute-start | bytes 196616 | tf_op jit(solution)/shard_map/ppermute | solution.py:453
  48.1 1.7 %collective-permute-done.11.up_two = bf16[2,64,768]{2,1,0:T(8,128)(2,1)S(1)} collective-permute-done((bf16[2,64,768]{2,1,0:T(8,128)(2,1)S(1)}, bf16[2,64,768]{2,1,0:T(8,128)(2,1)S(1)}, u32[]{:S(2)}, u32[]{:S(2)}) %collective-permute-start.11) | collective-permute-done | bytes 196640 | tf_op jit(solution)/shard_map/ppermute | solution.py:453
  49.9 1.3 %collective-permute-done.9.down_two = bf16[2,64,768]{2,1,0:T(8,128)(2,1)S(1)} collective-permute-done((bf16[2,64,768]{2,1,0:T(8,128)(2,1)S(1)}, bf16[2,64,768]{2,1,0:T(8,128)(2,1)S(1)}, u32[]{:S(2)}, u32[]{:S(2)}) %collective-permute-start.9) | collective-permute-done | bytes 196640 | tf_op jit(solution)/shard_map/ppermute | solution.py:453
  51.3 3.4 %collective-permute-start.12 = (bf16[2,64,768]{2,1,0:T(8,128)(2,1)S(1)}, bf16[2,64,768]{2,1,0:T(8,128)(2,1)S(1)}, u32[]{:S(2)}, u32[]{:S(2)}) collective-permute-start(bf16[2,64,768]{2,1,0:T(8,128)(2,1)S(1)} %pad_maximum_fusion.7), channel_id=1, source_target_pairs={{0,2},{1,3},{2,0},{3,1},{4,6},{5,7},{6,4},{7,5},{8,10},{9,11},{10,... | collective-permute-start | bytes 589832 | tf_op jit(solution)/shard_map/ppermute | solution.py:453
  54.7 1.3 %collective-permute-start.15 = (f32[128,128]{1,0:T(8,128)S(1)}, f32[128,128]{1,0:T(8,128)S(1)}, u32[]{:S(2)}, u32[]{:S(2)}) collective-permute-start(f32[128,128]{1,0:T(8,128)S(1)} %add.110), channel_id=1, source_target_pairs={{0,2},{1,3},{2,0},{3,1},{4,6},{5,7},{6,4},{7,5},{8,10},{9,11},{10,... | collective-permute-start | bytes 196616 | tf_op jit(solution)/shard_map/ppermute | solution.py:453
  56.0 7.4 %collective-permute-done.15 = f32[128,128]{1,0:T(8,128)S(1)} collective-permute-done((f32[128,128]{1,0:T(8,128)S(1)}, f32[128,128]{1,0:T(8,128)S(1)}, u32[]{:S(2)}, u32[]{:S(2)}) %collective-permute-start.15) | collective-permute-done | bytes 65568 | tf_op jit(solution)/shard_map/ppermute | solution.py:453
  63.4 1.4 %collective-permute-start.16 = (f32[128,128]{1,0:T(8,128)S(1)}, f32[128,128]{1,0:T(8,128)S(1)}, u32[]{:S(2)}, u32[]{:S(2)}) collective-permute-start(f32[128,128]{1,0:T(8,128)S(1)} %add.111.refs_1_), channel_id=1, source_target_pairs={{0,16},{8,24},{16,0},{24,8},{1,17},{9,25},{17,1},{25,9},{2,18},{10... | collective-permute-start | bytes 196616 | tf_op jit(solution)/shard_map/ppermute | solution.py:453
  64.8 3.0 %collective-permute-done.16.refs_2_ = f32[128,128]{1,0:T(8,128)S(1)} collective-permute-done((f32[128,128]{1,0:T(8,128)S(1)}, f32[128,128]{1,0:T(8,128)S(1)}, u32[]{:S(2)}, u32[]{:S(2)}) %collective-permute-start.16) | collective-permute-done | bytes 65568 | tf_op jit(solution)/shard_map/ppermute | solution.py:453
  67.8 1.8 %update.1 = (f32[1,64,768]{2,1,0:T(8,128)}, f32[1,64,768]{2,1,0:T(8,128)}, f32[1,64,768]{2,1,0:T(8,128)}, f32[1,64,768]{2,1,0:T(8,128)}, f32[1,64,768]{2,1,0:T(8...) custom-call(bf16[2,8,64,768]{3,2,1,0:T(8,128)(2,1)S(1)} %gradient.2.kept, ...), custom_call_target="tpu_custom_call" | custom-call | tf_op jit(solution)/shard_map/update/pallas_call | solution.py:374
  69.6 1.3 %collective-permute-start.17 = (bf16[2,64,768]{2,1,0:T(8,128)(2,1)S(1)}, bf16[2,64,768]{2,1,0:T(8,128)(2,1)S(1)}, u32[]{:S(2)}, u32[]{:S(2)}) collective-permute-start(bf16[2,64,768]{2,1,0:T(8,128)(2,1)S(1)} %get-tuple-element.48), channel_id=1, source_target_pairs={{4,0},{5,1},{6,2},{7,3},{12,8},{13,9},{14,10},{15,11},{20,16},{21,... | collective-permute-start | bytes 589832 | tf_op jit(solution)/shard_map/ppermute | solution.py:468
  70.9 7.4 %collective-permute-done.18 = bf16[2,64,768]{2,1,0:T(8,128)(2,1)S(1)} collective-permute-done((bf16[2,64,768]{2,1,0:T(8,128)(2,1)S(1)}, bf16[2,64,768]{2,1,0:T(8,128)(2,1)S(1)}, u32[]{:S(2)}, u32[]{:S(2)}) %collective-permute-start.18) | collective-permute-done | bytes 196640 | tf_op jit(solution)/shard_map/ppermute | solution.py:453
  78.4 1.4 %collective-permute-start.21 = (bf16[2,64,768]{2,1,0:T(8,128)(2,1)S(1)}, bf16[2,64,768]{2,1,0:T(8,128)(2,1)S(1)}, u32[]{:S(2)}, u32[]{:S(2)}) collective-permute-start(bf16[2,64,768]{2,1,0:T(8,128)(2,1)S(1)} %pad_maximum_fusion.9), channel_id=1, source_target_pairs={{0,16},{8,24},{16,0},{24,8},{1,17},{9,25},{17,1},{25,9},{2,18},{10... | collective-permute-start | bytes 589832 | tf_op jit(solution)/shard_map/ppermute | solution.py:453
  79.9 1.3 %collective-permute-start.19 = (bf16[2,64,768]{2,1,0:T(8,128)(2,1)S(1)}, bf16[2,64,768]{2,1,0:T(8,128)(2,1)S(1)}, u32[]{:S(2)}, u32[]{:S(2)}) collective-permute-start(bf16[2,64,768]{2,1,0:T(8,128)(2,1)S(1)} %collective-permute-done.18), channel_id=1, source_target_pairs={{4,0},{5,1},{6,2},{7,3},{12,8},{13,9},{14,10},{15,11},{20,16},{21,... | collective-permute-start | bytes 589832 | tf_op jit(solution)/shard_map/ppermute | solution.py:468
  81.3 2.9 %collective-permute-done.21 = bf16[2,64,768]{2,1,0:T(8,128)(2,1)S(1)} collective-permute-done((bf16[2,64,768]{2,1,0:T(8,128)(2,1)S(1)}, bf16[2,64,768]{2,1,0:T(8,128)(2,1)S(1)}, u32[]{:S(2)}, u32[]{:S(2)}) %collective-permute-start.21) | collective-permute-done | bytes 196640 | tf_op jit(solution)/shard_map/ppermute | solution.py:453
  84.2 1.4 %collective-permute-done.20 = bf16[2,64,768]{2,1,0:T(8,128)(2,1)S(1)} collective-permute-done((bf16[2,64,768]{2,1,0:T(8,128)(2,1)S(1)}, bf16[2,64,768]{2,1,0:T(8,128)(2,1)S(1)}, u32[]{:S(2)}, u32[]{:S(2)}) %collective-permute-start.20) | collective-permute-done | bytes 196640 | tf_op jit(solution)/shard_map/ppermute | solution.py:453
  85.7 0.8 collective-permute-start.25
  86.5 1.3 %collective-permute-start.22 = (bf16[4,64,768]{2,1,0:T(8,128)(2,1)S(1)}, bf16[4,64,768]{2,1,0:T(8,128)(2,1)S(1)}, u32[]{:S(2)}, u32[]{:S(2)}) collective-permute-start(bf16[4,64,768]{2,1,0:T(8,128)(2,1)S(1)} %get-tuple-element.73), channel_id=1, source_target_pairs={{4,0},{5,1},{6,2},{7,3},{12,8},{13,9},{14,10},{15,11},{20,16},{21,... | collective-permute-start | bytes 1179656 | tf_op jit(solution)/shard_map/ppermute | solution.py:468
  88.0 8.1 %collective-permute-done.22 = bf16[4,64,768]{2,1,0:T(8,128)(2,1)S(1)} collective-permute-done((bf16[4,64,768]{2,1,0:T(8,128)(2,1)S(1)}, bf16[4,64,768]{2,1,0:T(8,128)(2,1)S(1)}, u32[]{:S(2)}, u32[]{:S(2)}) %collective-permute-start.22) | collective-permute-done | bytes 393248 | tf_op jit(solution)/shard_map/ppermute | solution.py:468
  96.2 3.2 %collective-permute-start.23 = (bf16[3,64,768]{2,1,0:T(8,128)(2,1)S(1)}, bf16[3,64,768]{2,1,0:T(8,128)(2,1)S(1)}, u32[]{:S(2)}, u32[]{:S(2)}) collective-permute-start(bf16[3,64,768]{2,1,0:T(8,128)(2,1)S(1)} %pad_maximum_fusion.4), channel_id=1, source_target_pairs={{0,16},{8,24},{16,0},{24,8},{1,17},{9,25},{17,1},{25,9},{2,18},{10... | collective-permute-start | bytes 884744 | tf_op jit(solution)/shard_map/ppermute | solution.py:509
  99.5 3.1 %collective-permute-start.24 = (bf16[3,64,768]{2,1,0:T(8,128)(2,1)S(1)}, bf16[3,64,768]{2,1,0:T(8,128)(2,1)S(1)}, u32[]{:S(2)}, u32[]{:S(2)}) collective-permute-start(bf16[3,64,768]{2,1,0:T(8,128)(2,1)S(1)} %pad_maximum_fusion.5), channel_id=1, source_target_pairs={{0,1},{1,0},{2,3},{3,2},{8,9},{9,8},{10,11},{11,10},{16,17},{17,16... | collective-permute-start | bytes 884744 | tf_op jit(solution)/shard_map/ppermute | solution.py:509
  102.6 1.3 %collective-permute-start.27 = (bf16[2,64,768]{2,1,0:T(8,128)(2,1)S(1)}, bf16[2,64,768]{2,1,0:T(8,128)(2,1)S(1)}, u32[]{:S(2)}, u32[]{:S(2)}) collective-permute-start(bf16[2,64,768]{2,1,0:T(8,128)(2,1)S(1)} %pad_maximum_fusion.10), channel_id=1, source_target_pairs={{4,0},{5,1},{6,2},{7,3},{12,8},{13,9},{14,10},{15,11},{20,16},{21,... | collective-permute-start | bytes 589832 | tf_op jit(solution)/shard_map/ppermute | solution.py:468
  104.0 1.9 %collective-permute-start.31 = (bf16[8,64,768]{2,1,0:T(8,128)(2,1)S(1)}, bf16[8,64,768]{2,1,0:T(8,128)(2,1)S(1)}, u32[]{:S(2)}, u32[]{:S(2)}) collective-permute-start(bf16[8,64,768]{2,1,0:T(8,128)(2,1)S(1)} %constant_dynamic-update-slice_fusion.7.refs_1_), channel_id=1, source_target_pairs={{0,8},{8,0},{16,24},{24,16},{1,9},{9,1},{17,25},{25,17},{2,10},{10... | collective-permute-start | bytes 2359304 | tf_op jit(solution)/shard_map/ppermute | solution.py:509
  106.0 2.1 %collective-permute-done.24 = bf16[3,64,768]{2,1,0:T(8,128)(2,1)S(1)} collective-permute-done((bf16[3,64,768]{2,1,0:T(8,128)(2,1)S(1)}, bf16[3,64,768]{2,1,0:T(8,128)(2,1)S(1)}, u32[]{:S(2)}, u32[]{:S(2)}) %collective-permute-start.24) | collective-permute-done | bytes 294944 | tf_op jit(solution)/shard_map/ppermute | solution.py:509
  108.1 1.7 %place.3 = (bf16[2,64,12288]{2,1,0:T(8,128)(2,1)}, bf16[2,64,12288]{2,1,0:T(8,128)(2,1)}) custom-call(s32[4,3]{1,0:T(4,128)S(1)} %copy-done.7, bf16[8,64,768]{2,1,0:T(8,128)(2,1)S(1)} %constant_dynamic-update-slice_fusion.3.refs_0_, bf16[8,64,768]{2,1,0:T(8,128)(2,1)S(1)} %collective-permute-done.29.refs_1_), custom_call_target="tpu_custom_call" | custom-call | bytes 3145728 | tf_op jit(solution)/shard_map/place/pallas_call | solution.py:434
  110.2 2.1 %collective-permute-start.28 = (bf16[8,64,768]{2,1,0:T(8,128)(2,1)S(1)}, bf16[8,64,768]{2,1,0:T(8,128)(2,1)S(1)}, u32[]{:S(2)}, u32[]{:S(2)}) collective-permute-start(bf16[8,64,768]{2,1,0:T(8,128)(2,1)S(1)} %constant_dynamic-update-slice_fusion.refs_0_), channel_id=1, source_target_pairs={{0,8},{8,0},{16,24},{24,16},{1,9},{9,1},{17,25},{25,17},{2,10},{10... | collective-permute-start | bytes 2359304 | tf_op jit(solution)/shard_map/ppermute | solution.py:509
  112.4 2.2 %place.4 = (bf16[2,64,12288]{2,1,0:T(8,128)(2,1)}, bf16[2,64,12288]{2,1,0:T(8,128)(2,1)}) custom-call(s32[4,3]{1,0:T(4,128)S(1)} %copy-done.7, bf16[8,64,768]{2,1,0:T(8,128)(2,1)S(1)} %pad_maximum_fusion.refs_0_, bf16[8,64,768]{2,1,0:T(8,128)(2,1)S(1)} %constant_dynamic-update-slice_fusion.7.refs_1_, ...), custom_call_target="tpu_custom_call", output_to_operand_aliasing={{0}: (5, {}), {1}: (6, {})} | custom-call | bytes 6291456 | tf_op jit(solution)/shard_map/place/pallas_call | solution.py:434
  114.6 1.7 %place.5 = (bf16[2,64,12288]{2,1,0:T(8,128)(2,1)}, bf16[2,64,12288]{2,1,0:T(8,128)(2,1)}) custom-call(s32[4,3]{1,0:T(4,128)S(1)} %copy-done.7, bf16[8,64,768]{2,1,0:T(8,128)(2,1)S(1)} %constant_dynamic-update-slice_fusion.refs_0_, bf16[8,64,768]{2,1,0:T(8,128)(2,1)S(1)} %collective-permute-done.28.refs_1_, ...), custom_call_target="tpu_custom_call", output_to_operand_aliasing={{0}: (3, {}), {1}: (4, {})} | custom-call | bytes 3145728 | tf_op jit(solution)/shard_map/place/pallas_call | solution.py:434
  (79 shorter events, 3.3 us)
Async XLA Ops:
  1.7 9.0 %collective-permute-start = (bf16[128,768]{1,0:T(8,128)(2,1)S(1)}, bf16[128,768]{1,0:T(8,128)(2,1)S(1)}, u32[]{:S(2)}, u32[]{:S(2)}) collective-permute-start(bf16[128,768]{1,0:T(8,128)(2,1)S(1)} %pad_maximum_fusion.6.refs_0_), channel_id=1, source_target_pairs={{4,0},{0,4},{5,1},{1,5},{6,2},{2,6},{7,3},{3,7},{12,8},{8,12},{13,... | collective-permute-start | bytes 589832 | tf_op jit(solution)/shard_map/ppermute | solution.py:463
  4.7 8.1 %copy-start = (bf16[1,4,32,12288]{3,2,1,0:T(8,128)(2,1)S(1)}, bf16[1,4,32,12288]{3,2,1,0:T(8,128)(2,1)}, u32[]{:S(2)}) copy-start(bf16[1,4,32,12288]{3,2,1,0:T(8,128)(2,1)} %param.13) | copy-start | bytes 9437188
  4.7 8.1 %copy-start.8 = (s32[4]{0:T(128)S(1)}, s32[4]{0:T(128)}, u32[]{:S(2)}) copy-start(s32[4]{0:T(128)} %counts.3) | copy-start | bytes 52
  10.9 4.1 %collective-permute-start.4 = (f32[64,128]{1,0:T(8,128)S(1)}, f32[64,128]{1,0:T(8,128)S(1)}, u32[]{:S(2)}, u32[]{:S(2)}) collective-permute-start(f32[64,128]{1,0:T(8,128)S(1)} %get-tuple-element.42), channel_id=1, source_target_pairs={{0,24},{8,16},{16,8},{24,0},{1,25},{9,17},{17,9},{25,1},{2,26},{10... | collective-permute-start | bytes 98312 | tf_op jit(solution)/shard_map/ppermute | solution.py:453
  11.7 4.2 %collective-permute-start.3 = (f32[64,128]{1,0:T(8,128)S(1)}, f32[64,128]{1,0:T(8,128)S(1)}, u32[]{:S(2)}, u32[]{:S(2)}) collective-permute-start(f32[64,128]{1,0:T(8,128)S(1)} %get-tuple-element.42), channel_id=1, source_target_pairs={{0,16},{8,24},{16,0},{24,8},{1,17},{9,25},{17,1},{25,9},{2,18},{10... | collective-permute-start | bytes 98312 | tf_op jit(solution)/shard_map/ppermute | solution.py:453
  12.6 3.3 %collective-permute-start.2 = (f32[64,128]{1,0:T(8,128)S(1)}, f32[64,128]{1,0:T(8,128)S(1)}, u32[]{:S(2)}, u32[]{:S(2)}) collective-permute-start(f32[64,128]{1,0:T(8,128)S(1)} %get-tuple-element.42), channel_id=1, source_target_pairs={{0,8},{8,0},{16,24},{24,16},{1,9},{9,1},{17,25},{25,17},{2,10},{10... | collective-permute-start | bytes 98312 | tf_op jit(solution)/shard_map/ppermute | solution.py:453
  12.8 11.9 %copy-start.7 = (s32[4,3]{1,0:T(4,128)S(1)}, s32[4,3]{1,0:T(4,128)}, u32[]{:S(2)}) copy-start(s32[4,3]{1,0:T(4,128)} %bounds.7) | copy-start | bytes 148
  14.4 10.4 %collective-permute-start.1 = (f32[128,384]{1,0:T(8,128)S(1)}, f32[128,384]{1,0:T(8,128)S(1)}, u32[]{:S(2)}, u32[]{:S(2)}) collective-permute-start(f32[128,384]{1,0:T(8,128)S(1)} %project_back.1.refs_0_), channel_id=1, source_target_pairs={{4,0},{0,4},{5,1},{1,5},{6,2},{2,6},{7,3},{3,7},{12,8},{8,12},{13,... | collective-permute-start | bytes 589832 | tf_op jit(solution)/shard_map/ppermute | solution.py:463
  15.9 4.0 %collective-permute-start.5 = (f32[64,128]{1,0:T(8,128)S(1)}, f32[64,128]{1,0:T(8,128)S(1)}, u32[]{:S(2)}, u32[]{:S(2)}) collective-permute-start(f32[64,128]{1,0:T(8,128)S(1)} %add_add_fusion), channel_id=1, source_target_pairs={{0,1},{1,0},{2,3},{3,2},{4,5},{5,4},{6,7},{7,6},{8,9},{9,8},{10,11... | collective-permute-start | bytes 98312 | tf_op jit(solution)/shard_map/ppermute | solution.py:453
  19.9 4.8 %collective-permute-start.6 = (f32[64,128]{1,0:T(8,128)S(1)}, f32[64,128]{1,0:T(8,128)S(1)}, u32[]{:S(2)}, u32[]{:S(2)}) collective-permute-start(f32[64,128]{1,0:T(8,128)S(1)} %add.92.refs_2_), channel_id=1, source_target_pairs={{0,2},{1,3},{2,0},{3,1},{4,6},{5,7},{6,4},{7,5},{8,10},{9,11},{10,... | collective-permute-start | bytes 98312 | tf_op jit(solution)/shard_map/ppermute | solution.py:453
  27.7 3.5 %collective-permute-start.7 = (bf16[2,8,64,768]{3,2,1,0:T(8,128)(2,1)S(1)}, bf16[2,8,64,768]{3,2,1,0:T(8,128)(2,1)S(1)}, u32[]{:S(2)}, u32[]{:S(2)}) collective-permute-start(bf16[2,8,64,768]{3,2,1,0:T(8,128)(2,1)S(1)} %gradient.3), channel_id=1, source_target_pairs={{0,8},{8,0},{16,24},{24,16},{1,9},{9,1},{17,25},{25,17},{2,10},{10... | collective-permute-start | bytes 4718600 | tf_op jit(solution)/shard_map/ppermute | solution.py:453
  28.4 39.4 %copy-start.1 = (f32[1,64,768]{2,1,0:T(8,128)S(1)}, f32[1,64,768]{2,1,0:T(8,128)}, u32[]{:S(2)}) copy-start(f32[1,64,768]{2,1,0:T(8,128)} %refs_5_.1) | copy-start | bytes 589828
  28.4 39.4 %copy-start.2 = (f32[1,64,768]{2,1,0:T(8,128)S(1)}, f32[1,64,768]{2,1,0:T(8,128)}, u32[]{:S(2)}) copy-start(f32[1,64,768]{2,1,0:T(8,128)} %refs_4_.1) | copy-start | bytes 589828
  28.4 39.4 %copy-start.3 = (f32[1,64,768]{2,1,0:T(8,128)S(1)}, f32[1,64,768]{2,1,0:T(8,128)}, u32[]{:S(2)}) copy-start(f32[1,64,768]{2,1,0:T(8,128)} %refs_6_.1) | copy-start | bytes 589828
  28.4 39.4 %copy-start.4 = (f32[1,64,768]{2,1,0:T(8,128)S(1)}, f32[1,64,768]{2,1,0:T(8,128)}, u32[]{:S(2)}) copy-start(f32[1,64,768]{2,1,0:T(8,128)} %refs_7_.1) | copy-start | bytes 589828
  28.4 39.4 %copy-start.5 = (f32[1,64,768]{2,1,0:T(8,128)S(1)}, f32[1,64,768]{2,1,0:T(8,128)}, u32[]{:S(2)}) copy-start(f32[1,64,768]{2,1,0:T(8,128)} %refs_8_.1) | copy-start | bytes 589828
  28.4 39.4 %copy-start.6 = (f32[1,64,768]{2,1,0:T(8,128)S(1)}, f32[1,64,768]{2,1,0:T(8,128)}, u32[]{:S(2)}) copy-start(f32[1,64,768]{2,1,0:T(8,128)} %refs_9_.1) | copy-start | bytes 589828
  31.3 11.2 %collective-permute-start.10 = (bf16[4,64,768]{2,1,0:T(8,128)(2,1)S(1)}, bf16[4,64,768]{2,1,0:T(8,128)(2,1)S(1)}, u32[]{:S(2)}, u32[]{:S(2)}) collective-permute-start(bf16[4,64,768]{2,1,0:T(8,128)(2,1)S(1)} %get-tuple-element.68), channel_id=1, source_target_pairs={{0,1},{1,0},{2,3},{3,2},{4,5},{5,4},{6,7},{7,6},{8,9},{9,8},{10,11... | collective-permute-start | bytes 1179656 | tf_op jit(solution)/shard_map/ppermute | solution.py:453
  33.0 10.9 %collective-permute-start.8 = (bf16[4,64,768]{2,1,0:T(8,128)(2,1)S(1)}, bf16[4,64,768]{2,1,0:T(8,128)(2,1)S(1)}, u32[]{:S(2)}, u32[]{:S(2)}) collective-permute-start(bf16[4,64,768]{2,1,0:T(8,128)(2,1)S(1)} %get-tuple-element.69), channel_id=1, source_target_pairs={{0,16},{8,24},{16,0},{24,8},{1,17},{9,25},{17,1},{25,9},{2,18},{10... | collective-permute-start | bytes 1179656 | tf_op jit(solution)/shard_map/ppermute | solution.py:453
  44.0 5.9 %collective-permute-start.11 = (bf16[2,64,768]{2,1,0:T(8,128)(2,1)S(1)}, bf16[2,64,768]{2,1,0:T(8,128)(2,1)S(1)}, u32[]{:S(2)}, u32[]{:S(2)}) collective-permute-start(bf16[2,64,768]{2,1,0:T(8,128)(2,1)S(1)} %get-tuple-element.66), channel_id=1, source_target_pairs={{0,16},{8,24},{16,0},{24,8},{1,17},{9,25},{17,1},{25,9},{2,18},{10... | collective-permute-start | bytes 589832 | tf_op jit(solution)/shard_map/ppermute | solution.py:453
  44.8 6.4 %collective-permute-start.9 = (bf16[2,64,768]{2,1,0:T(8,128)(2,1)S(1)}, bf16[2,64,768]{2,1,0:T(8,128)(2,1)S(1)}, u32[]{:S(2)}, u32[]{:S(2)}) collective-permute-start(bf16[2,64,768]{2,1,0:T(8,128)(2,1)S(1)} %get-tuple-element.67), channel_id=1, source_target_pairs={{0,1},{1,0},{2,3},{3,2},{4,5},{5,4},{6,7},{7,6},{8,9},{9,8},{10,11... | collective-permute-start | bytes 589832 | tf_op jit(solution)/shard_map/ppermute | solution.py:453
  45.2 1.3 %collective-permute-start.13 = (f32[128,128]{1,0:T(8,128)S(1)}, f32[128,128]{1,0:T(8,128)S(1)}, u32[]{:S(2)}, u32[]{:S(2)}) collective-permute-start(f32[128,128]{1,0:T(8,128)S(1)} %get-tuple-element.46), channel_id=1, source_target_pairs={{0,8},{8,0},{16,24},{24,16},{1,9},{9,1},{17,25},{25,17},{2,10},{10... | collective-permute-start | bytes 196616 | tf_op jit(solution)/shard_map/ppermute | solution.py:453
  46.5 8.2 %collective-permute-start.14 = (f32[128,128]{1,0:T(8,128)S(1)}, f32[128,128]{1,0:T(8,128)S(1)}, u32[]{:S(2)}, u32[]{:S(2)}) collective-permute-start(f32[128,128]{1,0:T(8,128)S(1)} %add.109), channel_id=1, source_target_pairs={{0,1},{1,0},{2,3},{3,2},{4,5},{5,4},{6,7},{7,6},{8,9},{9,8},{10,11... | collective-permute-start | bytes 196616 | tf_op jit(solution)/shard_map/ppermute | solution.py:453
  51.3 16.5 %collective-permute-start.12 = (bf16[2,64,768]{2,1,0:T(8,128)(2,1)S(1)}, bf16[2,64,768]{2,1,0:T(8,128)(2,1)S(1)}, u32[]{:S(2)}, u32[]{:S(2)}) collective-permute-start(bf16[2,64,768]{2,1,0:T(8,128)(2,1)S(1)} %pad_maximum_fusion.7), channel_id=1, source_target_pairs={{0,2},{1,3},{2,0},{3,1},{4,6},{5,7},{6,4},{7,5},{8,10},{9,11},{10,... | collective-permute-start | bytes 589832 | tf_op jit(solution)/shard_map/ppermute | solution.py:453
  54.7 8.7 %collective-permute-start.15 = (f32[128,128]{1,0:T(8,128)S(1)}, f32[128,128]{1,0:T(8,128)S(1)}, u32[]{:S(2)}, u32[]{:S(2)}) collective-permute-start(f32[128,128]{1,0:T(8,128)S(1)} %add.110), channel_id=1, source_target_pairs={{0,2},{1,3},{2,0},{3,1},{4,6},{5,7},{6,4},{7,5},{8,10},{9,11},{10,... | collective-permute-start | bytes 196616 | tf_op jit(solution)/shard_map/ppermute | solution.py:453
  63.4 4.3 %collective-permute-start.16 = (f32[128,128]{1,0:T(8,128)S(1)}, f32[128,128]{1,0:T(8,128)S(1)}, u32[]{:S(2)}, u32[]{:S(2)}) collective-permute-start(f32[128,128]{1,0:T(8,128)S(1)} %add.111.refs_1_), channel_id=1, source_target_pairs={{0,16},{8,24},{16,0},{24,8},{1,17},{9,25},{17,1},{25,9},{2,18},{10... | collective-permute-start | bytes 196616 | tf_op jit(solution)/shard_map/ppermute | solution.py:453
  69.6 8.8 %collective-permute-start.18 = (bf16[2,64,768]{2,1,0:T(8,128)(2,1)S(1)}, bf16[2,64,768]{2,1,0:T(8,128)(2,1)S(1)}, u32[]{:S(2)}, u32[]{:S(2)}) collective-permute-start(bf16[2,64,768]{2,1,0:T(8,128)(2,1)S(1)} %get-tuple-element.48), channel_id=1, source_target_pairs={{0,2},{1,3},{2,0},{3,1},{4,6},{5,7},{6,4},{7,5},{8,10},{9,11},{10,... | collective-permute-start | bytes 589832 | tf_op jit(solution)/shard_map/ppermute | solution.py:453
  69.6 11.6 %collective-permute-start.17 = (bf16[2,64,768]{2,1,0:T(8,128)(2,1)S(1)}, bf16[2,64,768]{2,1,0:T(8,128)(2,1)S(1)}, u32[]{:S(2)}, u32[]{:S(2)}) collective-permute-start(bf16[2,64,768]{2,1,0:T(8,128)(2,1)S(1)} %get-tuple-element.48), channel_id=1, source_target_pairs={{4,0},{5,1},{6,2},{7,3},{12,8},{13,9},{14,10},{15,11},{20,16},{21,... | collective-permute-start | bytes 589832 | tf_op jit(solution)/shard_map/ppermute | solution.py:468
  78.4 5.7 %collective-permute-start.21 = (bf16[2,64,768]{2,1,0:T(8,128)(2,1)S(1)}, bf16[2,64,768]{2,1,0:T(8,128)(2,1)S(1)}, u32[]{:S(2)}, u32[]{:S(2)}) collective-permute-start(bf16[2,64,768]{2,1,0:T(8,128)(2,1)S(1)} %pad_maximum_fusion.9), channel_id=1, source_target_pairs={{0,16},{8,24},{16,0},{24,8},{1,17},{9,25},{17,1},{25,9},{2,18},{10... | collective-permute-start | bytes 589832 | tf_op jit(solution)/shard_map/ppermute | solution.py:453
  79.8 5.7 %collective-permute-start.20 = (bf16[2,64,768]{2,1,0:T(8,128)(2,1)S(1)}, bf16[2,64,768]{2,1,0:T(8,128)(2,1)S(1)}, u32[]{:S(2)}, u32[]{:S(2)}) collective-permute-start(bf16[2,64,768]{2,1,0:T(8,128)(2,1)S(1)} %pad_maximum_fusion.8), channel_id=1, source_target_pairs={{0,1},{1,0},{2,3},{3,2},{4,5},{5,4},{6,7},{7,6},{8,9},{9,8},{10,11... | collective-permute-start | bytes 589832 | tf_op jit(solution)/shard_map/ppermute | solution.py:453
  79.9 8.0 %collective-permute-start.19 = (bf16[2,64,768]{2,1,0:T(8,128)(2,1)S(1)}, bf16[2,64,768]{2,1,0:T(8,128)(2,1)S(1)}, u32[]{:S(2)}, u32[]{:S(2)}) collective-permute-start(bf16[2,64,768]{2,1,0:T(8,128)(2,1)S(1)} %collective-permute-done.18), channel_id=1, source_target_pairs={{4,0},{5,1},{6,2},{7,3},{12,8},{13,9},{14,10},{15,11},{20,16},{21,... | collective-permute-start | bytes 589832 | tf_op jit(solution)/shard_map/ppermute | solution.py:468
  85.7 16.9 %collective-permute-start.25 = (bf16[4,64,768]{2,1,0:T(8,128)(2,1)S(1)}, bf16[4,64,768]{2,1,0:T(8,128)(2,1)S(1)}, u32[]{:S(2)}, u32[]{:S(2)}) collective-permute-start(bf16[4,64,768]{2,1,0:T(8,128)(2,1)S(1)} %get-tuple-element.72), channel_id=1, source_target_pairs={{0,16},{8,24},{16,0},{24,8},{1,17},{9,25},{17,1},{25,9},{2,18},{10... | collective-permute-start | bytes 1179656 | tf_op jit(solution)/shard_map/ppermute | solution.py:453
  86.5 9.7 %collective-permute-start.22 = (bf16[4,64,768]{2,1,0:T(8,128)(2,1)S(1)}, bf16[4,64,768]{2,1,0:T(8,128)(2,1)S(1)}, u32[]{:S(2)}, u32[]{:S(2)}) collective-permute-start(bf16[4,64,768]{2,1,0:T(8,128)(2,1)S(1)} %get-tuple-element.73), channel_id=1, source_target_pairs={{4,0},{5,1},{6,2},{7,3},{12,8},{13,9},{14,10},{15,11},{20,16},{21,... | collective-permute-start | bytes 1179656 | tf_op jit(solution)/shard_map/ppermute | solution.py:468
  87.7 14.8 %collective-permute-start.26 = (bf16[4,64,768]{2,1,0:T(8,128)(2,1)S(1)}, bf16[4,64,768]{2,1,0:T(8,128)(2,1)S(1)}, u32[]{:S(2)}, u32[]{:S(2)}) collective-permute-start(bf16[4,64,768]{2,1,0:T(8,128)(2,1)S(1)} %get-tuple-element.74), channel_id=1, source_target_pairs={{0,1},{1,0},{2,3},{3,2},{4,5},{5,4},{6,7},{7,6},{8,9},{9,8},{10,11... | collective-permute-start | bytes 1179656 | tf_op jit(solution)/shard_map/ppermute | solution.py:453
  87.9 20.2 %collective-permute-start.29 = (bf16[8,64,768]{2,1,0:T(8,128)(2,1)S(1)}, bf16[8,64,768]{2,1,0:T(8,128)(2,1)S(1)}, u32[]{:S(2)}, u32[]{:S(2)}) collective-permute-start(bf16[8,64,768]{2,1,0:T(8,128)(2,1)S(1)} %constant_dynamic-update-slice_fusion.3.refs_0_), channel_id=1, source_target_pairs={{0,8},{8,0},{16,24},{24,16},{1,9},{9,1},{17,25},{25,17},{2,10},{10... | collective-permute-start | bytes 2359304 | tf_op jit(solution)/shard_map/ppermute | solution.py:453
  96.2 9.8 %collective-permute-start.23 = (bf16[3,64,768]{2,1,0:T(8,128)(2,1)S(1)}, bf16[3,64,768]{2,1,0:T(8,128)(2,1)S(1)}, u32[]{:S(2)}, u32[]{:S(2)}) collective-permute-start(bf16[3,64,768]{2,1,0:T(8,128)(2,1)S(1)} %pad_maximum_fusion.4), channel_id=1, source_target_pairs={{0,16},{8,24},{16,0},{24,8},{1,17},{9,25},{17,1},{25,9},{2,18},{10... | collective-permute-start | bytes 884744 | tf_op jit(solution)/shard_map/ppermute | solution.py:509
  99.5 8.6 %collective-permute-start.24 = (bf16[3,64,768]{2,1,0:T(8,128)(2,1)S(1)}, bf16[3,64,768]{2,1,0:T(8,128)(2,1)S(1)}, u32[]{:S(2)}, u32[]{:S(2)}) collective-permute-start(bf16[3,64,768]{2,1,0:T(8,128)(2,1)S(1)} %pad_maximum_fusion.5), channel_id=1, source_target_pairs={{0,1},{1,0},{2,3},{3,2},{8,9},{9,8},{10,11},{11,10},{16,17},{17,16... | collective-permute-start | bytes 884744 | tf_op jit(solution)/shard_map/ppermute | solution.py:509
  102.6 7.6 %collective-permute-start.27 = (bf16[2,64,768]{2,1,0:T(8,128)(2,1)S(1)}, bf16[2,64,768]{2,1,0:T(8,128)(2,1)S(1)}, u32[]{:S(2)}, u32[]{:S(2)}) collective-permute-start(bf16[2,64,768]{2,1,0:T(8,128)(2,1)S(1)} %pad_maximum_fusion.10), channel_id=1, source_target_pairs={{4,0},{5,1},{6,2},{7,3},{12,8},{13,9},{14,10},{15,11},{20,16},{21,... | collective-permute-start | bytes 589832 | tf_op jit(solution)/shard_map/ppermute | solution.py:468
  104.0 8.4 %collective-permute-start.31 = (bf16[8,64,768]{2,1,0:T(8,128)(2,1)S(1)}, bf16[8,64,768]{2,1,0:T(8,128)(2,1)S(1)}, u32[]{:S(2)}, u32[]{:S(2)}) collective-permute-start(bf16[8,64,768]{2,1,0:T(8,128)(2,1)S(1)} %constant_dynamic-update-slice_fusion.7.refs_1_), channel_id=1, source_target_pairs={{0,8},{8,0},{16,24},{24,16},{1,9},{9,1},{17,25},{25,17},{2,10},{10... | collective-permute-start | bytes 2359304 | tf_op jit(solution)/shard_map/ppermute | solution.py:509
  109.8 2.5 %collective-permute-start.30 = (bf16[8,64,768]{2,1,0:T(8,128)(2,1)S(1)}, bf16[8,64,768]{2,1,0:T(8,128)(2,1)S(1)}, u32[]{:S(2)}, u32[]{:S(2)}) collective-permute-start(bf16[8,64,768]{2,1,0:T(8,128)(2,1)S(1)} %pad_maximum_fusion.refs_0_), channel_id=1, source_target_pairs={{0,8},{8,0},{16,24},{24,16},{1,9},{9,1},{17,25},{25,17},{2,10},{10... | collective-permute-start | bytes 2359304 | tf_op jit(solution)/shard_map/ppermute | solution.py:453
  110.2 4.4 %collective-permute-start.28 = (bf16[8,64,768]{2,1,0:T(8,128)(2,1)S(1)}, bf16[8,64,768]{2,1,0:T(8,128)(2,1)S(1)}, u32[]{:S(2)}, u32[]{:S(2)}) collective-permute-start(bf16[8,64,768]{2,1,0:T(8,128)(2,1)S(1)} %constant_dynamic-update-slice_fusion.refs_0_), channel_id=1, source_target_pairs={{0,8},{8,0},{16,24},{24,16},{1,9},{9,1},{17,25},{25,17},{2,10},{10... | collective-permute-start | bytes 2359304 | tf_op jit(solution)/shard_map/ppermute | solution.py:509

commit v5 on v4

--- a/solution.py
+++ b/solution.py
@@ -53,18 +53,15 @@
     return jnp.sum(x, axis=-1, keepdims=True)
 
 
-def project_kernel(steps, h_in, down_in, up_in, *refs):
-    out_ref, sq_ref, h_ref, up_ref, down_ref, sems = refs
-    slots, ranks, features = down_in.shape
-    tokens = h_ref.shape[0]
+def project_back_kernel(steps, g_in, up_in, out_ref, g_ref, up_ref, sems):
+    slots, ranks, features = up_in.shape
     width = features // steps
     copies = []
     for step in range(steps):
         cut = pl.ds(step * width, width)
-        moves = [(h_in.at[:, cut], h_ref.at[:, cut])]
+        moves = [(g_in.at[:, cut], g_ref.at[:, cut])]
         for slot in range(slots):
             rows = pl.ds(slot * ranks, ranks)
-            moves.append((down_in.at[slot, :, cut], down_ref.at[rows, cut]))
             moves.append((up_in.at[slot, :, cut], up_ref.at[rows, cut]))
         copies.append(
             [
@@ -74,75 +71,96 @@
         )
         for copy in copies[-1]:
             copy.start()
-    ph = jnp.zeros((tokens, 2 * slots * ranks), f32)
-    square = jnp.zeros((tokens, 128), f32)
+    total = jnp.zeros(out_ref.shape, f32)
     for step in range(steps):
         for copy in copies[step]:
             copy.wait()
         cut = pl.ds(step * width, width)
-        h = h_ref[:, cut]
-        ph = ph + dot_last(h, jnp.concatenate([down_ref[:, cut], up_ref[:, cut]], axis=0))
-        wide = h.astype(f32)
-        wide = wide * wide
-        for lane in range(0, width, 128):
-            square = square + wide[:, lane : lane + 128]
-    sq_ref[...] = jnp.broadcast_to(row_sum(square), square.shape)
-    out_ref[...] = ph
-
-
-def project(hidden, downs, ups):
-    tokens, features = hidden.shape
-    slots, ranks, _ = downs.shape
+        total = total + dot_last(g_ref[:, cut], up_ref[:, cut])
+    out_ref[...] = total
+
+
+def project_back(cot, ups):
+    tokens, features = cot.shape
+    slots, ranks, _ = ups.shape
     steps = 8
-    sources = [pltpu.with_memory_space_constraint(x, pltpu.HBM) for x in (hidden, downs, ups)]
-    return pl.pallas_call(
-        functools.partial(project_kernel, steps),
-        in_specs=[in_hbm] * 3,
-        out_specs=[in_vmem] * 4,
+    sources = [pltpu.with_memory_space_constraint(x, pltpu.HBM) for x in (cot, ups)]
+    return pl.pallas_call(
+        functools.partial(project_back_kernel, steps),
+        in_specs=[in_hbm] * 2,
+        out_specs=[in_vmem] * 3,
         out_shape=[
-            jax.ShapeDtypeStruct((tokens, 2 * slots * ranks), f32),
-            jax.ShapeDtypeStruct((tokens, 128), f32),
+            jax.ShapeDtypeStruct((tokens, slots * ranks), f32),
             jax.ShapeDtypeStruct((tokens, features), bf16),
             jax.ShapeDtypeStruct((slots * ranks, features), bf16),
         ],
-        scratch_shapes=[
-            pltpu.VMEM((slots * ranks, features), bf16),
-            pltpu.SemaphoreType.DMA((steps, 1 + 2 * slots)),
-        ],
+        scratch_shapes=[pltpu.SemaphoreType.DMA((steps, 1 + slots))],
         compiler_params=limited,
         cost_estimate=pl.CostEstimate(
-            flops=4 * tokens * slots * ranks * features,
-            bytes_accessed=2 * (tokens + 2 * slots * ranks) * features,
-            transcendentals=0,
-        ),
-        name="project",
-    )(*sources)
-
-
-def project_back_kernel(per_micro, counts, by_hidden, g_ref, up_ref, out_ref):
-    pg = dot_last(g_ref[...], up_ref[...])
-    pg = jnp.where(counted_rows(counts, pg.shape[0], per_micro), pg, 0.0)
-    ahead = by_hidden.shape[1]
-    out_ref[:, :ahead] = by_hidden[...]
-    out_ref[:, ahead:] = pg
-
-
-def project_back(counts, by_hidden, cot, ups, per_micro):
-    tokens, features = cot.shape
-    columns = by_hidden.shape[1] + ups.shape[0]
-    return pl.pallas_call(
-        functools.partial(project_back_kernel, per_micro),
-        in_specs=[in_smem] + [in_vmem] * 3,
-        out_specs=in_vmem,
-        out_shape=jax.ShapeDtypeStruct((tokens, columns), f32),
-        compiler_params=limited,
-        cost_estimate=pl.CostEstimate(
-            flops=2 * tokens * ups.shape[0] * features,
-            bytes_accessed=2 * (tokens + ups.shape[0]) * features,
+            flops=2 * tokens * slots * ranks * features,
+            bytes_accessed=2 * (tokens + slots * ranks) * features,
             transcendentals=0,
         ),
         name="project_back",
-    )(counts, by_hidden, cot, ups)
+    )(*sources)
+
+
+def project_down_kernel(h_ref, down_ref, out_ref, sq_ref):
+    slots, ranks, features = down_ref.shape
+    tokens = h_ref.shape[0]
+    out_ref[...] = dot_last(h_ref[...], down_ref[...].reshape(slots * ranks, features))
+    square = jnp.zeros((tokens, 128), f32)
+    for lane in range(0, features, 128):
+        wide = h_ref[:, lane : lane + 128].astype(f32)
+        square = square + wide * wide
+    sq_ref[...] = jnp.broadcast_to(row_sum(square), square.shape)
+
+
+def project_down(hidden, downs):
+    tokens, features = hidden.shape
+    slots, ranks, _ = downs.shape
+    return pl.pallas_call(
+        project_down_kernel,
+        in_specs=[in_vmem] * 2,
+        out_specs=[in_vmem] * 2,
+        out_shape=[
+            jax.ShapeDtypeStruct((tokens, slots * ranks), f32),
+            jax.ShapeDtypeStruct((tokens, 128), f32),
+        ],
+        compiler_params=limited,
+        cost_estimate=pl.CostEstimate(
+            flops=2 * tokens * slots * ranks * features,
+            bytes_accessed=2 * (tokens + slots * ranks) * features,
+            transcendentals=0,
+        ),
+        name="project_down",
+    )(hidden, downs)
+
+
+def project_up_kernel(per_micro, counts, h_ref, up_ref, by_down, by_cot, out_ref):
+    tokens, columns = by_down.shape
+    out_ref[:, :columns] = by_down[...]
+    out_ref[:, columns : 2 * columns] = dot_last(h_ref[...], up_ref[...])
+    counted = counted_rows(counts, tokens, per_micro)
+    out_ref[:, 2 * columns :] = jnp.where(counted, by_cot[...], 0.0)
+
+
+def project_up(counts, hidden, ups, by_down, by_cot, per_micro):
+    tokens, features = hidden.shape
+    columns = ups.shape[0]
+    return pl.pallas_call(
+        functools.partial(project_up_kernel, per_micro),
+        in_specs=[in_smem] + [in_vmem] * 4,
+        out_specs=in_vmem,
+        out_shape=jax.ShapeDtypeStruct((tokens, 3 * columns), f32),
+        compiler_params=limited,
+        cost_estimate=pl.CostEstimate(
+            flops=2 * tokens * columns * features,
+            bytes_accessed=2 * (tokens + columns) * features,
+            transcendentals=0,
+        ),
+        name="project_up",
+    )(counts, hidden, ups, by_down, by_cot)
 
 
 def gram_kernel(sections, *refs):
@@ -475,7 +493,7 @@
     return total.astype(bf16)
 
 
-def reduced(factors, hidden, cot, columns):
+def reduced(factors, hidden, cot, columns, mixed):
     sent = gradient(factors, hidden, cot, 1, columns)
     near = swapped(sent, "replica", 1)
     kept = gradient(factors, hidden, cot, 0, columns)
@@ -484,29 +502,22 @@
         return summed(kept[which, cut], near[which, cut], *steps)
 
     high, low = slice(4, 8), slice(2, 4)
+    def added(axis, distance):
+        return mixed + swapped(mixed, axis, distance)
+
     down_one = swapped(part(0, high), "replica", 2)
     up_one = swapped(part(1, high), "tensor", 1)
+    mixed = added("replica", 1)
+    mixed = added("tensor", 2)
+    down_one, up_one, mixed = lax.optimization_barrier((down_one, up_one, mixed))
     down_two = swapped(part(0, low, down_one[2:]), "tensor", 1)
     up_two = swapped(part(1, low, up_one[2:]), "replica", 2)
+    mixed = added("tensor", 1)
+    down_two, up_two, mixed = lax.optimization_barrier((down_two, up_two, mixed))
     last = jnp.stack([part(0, 1, down_one[1], down_two[1]), part(1, 1, up_one[1], up_two[1])])
     last = swapped(last, "tensor", 2)
-    return (kept, near, (down_one, down_two), (up_one, up_two), last)
-
-
-def swapped_before_last(block, axis, distance):
-    size, sections = lax.axis_size(axis), lax.axis_size("section")
-    ahead = axis == "replica"
-    axes = (axis, "section") if ahead else ("section", axis)
-
-    def place_of(i, section):
-        return i * sections + section if ahead else section * size + i
-
-    route = [
-        (place_of(i, section), place_of(i ^ distance, section))
-        for i in range(size)
-        for section in range(sections - 1)
-    ]
-    return lax.ppermute(block, axes, route)
+    other = swapped(mixed, "replica", 2)
+    return (kept, near, (down_one, down_two), (up_one, up_two), last, mixed, other)
 
 
 def crossed(piece, axis, distance):
@@ -515,8 +526,7 @@
         (which, order ^ distance, hop) if axis == "replica" else (which, order, hop ^ distance)
         for which, order, hop in blocks
     ]
-    swap = swapped if window == 0 else swapped_before_last
-    return (window, blocks, swap(array, axis, distance))
+    return (window, blocks, swapped(array, axis, distance))
 
 
 def fetched(piece):
@@ -547,6 +557,11 @@
     down_three = crossed(joined(downs, down_two), "replica", 2)
     up_three = crossed(joined(ups, up_two), "tensor", 1)
     next_two = fetched(two)
+    down_far, up_far, next_far = lax.optimization_barrier(
+        (down_three[2], up_three[2], next_two[2])
+    )
+    down_three, up_three = (*down_three[:2], down_far), (*up_three[:2], up_far)
+    next_two = (*next_two[:2], next_far)
     near = joined(own, one, two)
     near_core = crossed(near, "replica", 1)
     last, first, second = slice(3, 4), slice(0, 1), slice(1, 2)
@@ -592,12 +607,14 @@
 
     owned = jnp.concatenate([master_down[0], master_up[0]], axis=0).astype(bf16)
     around = [from_next(owned, d) for d in range(1, sections)]
-    by_hidden, square, hidden, ups = project(hidden, holder_down[0, 0], holder_up[0, 0])
-    around, by_hidden = lax.optimization_barrier((around, by_hidden))
+    by_cot, cot, ups = project_back(cot, holder_up[0, 0])
+    around, by_cot = lax.optimization_barrier((around, by_cot))
     table, right = gram([owned, *around])
-    table, ups = lax.optimization_barrier((table, ups))
-    projected = project_back(micro_counts, by_hidden, cot, ups, per_micro)
+    table, hidden = lax.optimization_barrier((table, hidden))
+    by_down, square = project_down(hidden, holder_down[0, 0])
     table = table + sum(swaps(table, "replica"))
+    table, by_down = lax.optimization_barrier((table, by_down))
+    projected = project_up(micro_counts, hidden, ups, by_down, by_cot, per_micro)
     projections = [projected] + [from_next(projected, d) for d in range(1, sections)]
     table = table + swapped(table, "tensor", 1)
     tables = [table, swapped(table, "tensor", 2)]
@@ -605,12 +622,9 @@
         bounds, micro_counts, projections, tables, square, slots, features, per_micro
     )
 
-    parts = reduced(factors, hidden, cot, master_down.shape[2])
-    for axis, distance in (("replica", 1), ("tensor", 1), ("tensor", 2)):
-        mixed = mixed + swapped(mixed, axis, distance)
-    other = swapped(mixed, "replica", 2)
+    parts = reduced(factors, hidden, cot, master_down.shape[2], mixed)
     state = [master_down, master_up, moment_down, moment_up, second_down, second_up]
-    updated = update(*parts, mixed, other, right, state)
+    updated = update(*parts, right, state)
     placed = spread(updated[6], bounds, slots, features)
     return (placed[0][None, None], placed[1][None, None], *updated[:6])
 

time: 117 us -> 113 us (0.966)
  starting transfers between devices: 39.2 us -> 34.8 us
  waiting for transfers between devices: 55.1 us -> 57 us
    ppermute x4 -> x0, starting transfers between devices: 10.4 us -> none  [swapped_before_last(): return lax.ppermute(block, axes, route)]
    ppermute x22 -> x26, starting transfers between devices: 20 us -> 25.1 us  [swapped(): return lax.ppermute(block, axis, route)]
    ppermute x22 -> x26, waiting for transfers between devices: 44.6 us -> 47.4 us  [swapped(): return lax.ppermute(block, axis, route)]
    ppermute x4 -> x0, waiting for transfers between devices: 2.06 us -> none  [swapped_before_last(): return lax.ppermute(block, axes, route)]
    pallas_call x2 -> x3, Pallas kernels: 7.51 us -> 6.83 us  [the longest x1 3.85 us: project_back(): pl.pallas_call(functools.partial(project_back_kernel, steps), in_specs=[i...]
  transfers between devices with their start and end apart: 32 -> 32, of which waited for: 17 -> 19; matrix products, arithmetic and copies ran while one was open for 1% -> 1% of each run, Pallas kernels for 10% -> 9%
where the time goes in v5:
time: 113 us
  waiting for transfers between devices  57 us (50%)
  starting transfers between devices  34.8 us (31%)
  Pallas kernels  18 us (16%)
  other arithmetic  1.87 us (2%)
    ppermute x26, waiting for transfers between devices, swapped(): return lax.ppermute(block, axis, route)  47.4 us
    ppermute x26, starting transfers between devices, swapped(): return lax.ppermute(block, axis, route)  25.1 us
    ppermute x4, waiting for transfers between devices, following_layer(): return lax.ppermute(block, 'section', [(i + 1, i) for i in range(size - 1)])  8.55 us
    pallas_call x3, Pallas kernels, place(): pl.pallas_call(functools.partial(place_kernel, layout, not before), in_sp...  5.68 us
    ppermute x4, starting transfers between devices, following_layer(): return lax.ppermute(block, 'section', [(i + 1, i) for i in range(size - 1)])  5.15 us
    ppermute x2, starting transfers between devices, from_next(): return lax.ppermute(block, 'section', route)  4.61 us
    pallas_call x1, Pallas kernels, project_back(): pl.pallas_call(functools.partial(project_back_kernel, steps), in_specs=[i...  3.85 us
    pallas_call x1, Pallas kernels, chain(): pl.pallas_call(kernel, in_specs=[in_smem] * 2 + [in_vmem] * len(inputs),...  2.33 us
  transfers between devices with their start and end apart: 32, of which 19 were waited for; matrix products, arithmetic and copies ran while one was open for 1% of the time, Pallas kernels for 9%

profile of v5, /device:TPU:0, one launch (start us, length us, event | category | flops | bytes accessed | tf_op | source)
XLA Modules:
  0.0 113.2 jit_solution(2681558953281191973)
XLA Ops:
  0.6 1.0 convert_bitcast_fusion
  1.7 3.0 %collective-permute-start = (bf16[128,768]{1,0:T(8,128)(2,1)S(1)}, bf16[128,768]{1,0:T(8,128)(2,1)S(1)}, u32[]{:S(2)}, u32[]{:S(2)}) collective-permute-start(bf16[128,768]{1,0:T(8,128)(2,1)S(1)} %pad_maximum_fusion.6.refs_0_), channel_id=1, source_target_pairs={{4,0},{0,4},{5,1},{1,5},{6,2},{2,6},{7,3},{3,7},{12,8},{8,12},{13,... | collective-permute-start | bytes 589832 | tf_op jit(solution)/shard_map/ppermute | solution.py:481
  4.7 3.9 %project_back.1 = (f32[128,128]{1,0:T(8,128)S(1)}, bf16[128,12288]{1,0:T(8,128)(2,1)S(1)}, bf16[128,12288]{1,0:T(8,128)(2,1)S(1)}) custom-call(bf16[128,12288]{1,0:T(8,128)(2,1)} %bitcast.41, bf16[2,64,12288]{2,1,0:T(8,128)(2,1)} %bitcast.42), custom_call_target="tpu_custom_call" | custom-call | flops 402653184 | bytes 6291456 | tf_op jit(solution)/shard_map/project_back/pallas_call | solution.py:88
  8.6 1.0 collective-permute-done.refs_1_
  10.2 1.5 %collective-permute-start.2 = (f32[64,128]{1,0:T(8,128)S(1)}, f32[64,128]{1,0:T(8,128)S(1)}, u32[]{:S(2)}, u32[]{:S(2)}) collective-permute-start(f32[64,128]{1,0:T(8,128)S(1)} %get-tuple-element.53), channel_id=1, source_target_pairs={{0,16},{8,24},{16,0},{24,8},{1,17},{9,25},{17,1},{25,9},{2,18},{10... | collective-permute-start | bytes 98312 | tf_op jit(solution)/shard_map/ppermute | solution.py:471
  11.8 1.5 %project_down.1 = (f32[128,128]{1,0:T(8,128)S(1)}, f32[128,128]{1,0:T(8,128)S(1)}) custom-call(bf16[128,12288]{1,0:T(8,128)(2,1)S(1)} %bitcast.34, bf16[2,64,12288]{2,1,0:T(8,128)(2,1)S(1)} %bitcast.38), custom_call_target="tpu_custom_call" | custom-call | flops 402653184 | bytes 6291456 | tf_op jit(solution)/shard_map/project_down/pallas_call | solution.py:122
  13.2 0.9 collective-permute-done.2
  14.1 1.5 %project_up.1.refs_0_ = f32[128,384]{1,0:T(8,128)S(1)} custom-call(s32[4]{0:T(128)S(1)} %copy-done.9, bf16[128,12288]{1,0:T(8,128)(2,1)S(1)} %bitcast.35, bf16[128,12288]{1,0:T(8,128)(2,1)S(1)} %get-tuple-element.52.up_ref, f32[128,128]{1,0:T(8,128)S(1)} %get-tuple-element.55.by_down, f32[128,128]{1,0:T(8,128)S(1)} %get-tuple-element.56.by_cot), custom_call_target="tpu_custom_call" | custom-call | flops 402653184 | bytes 6291456 | tf_op jit(solution)/shard_map/project_up/pallas_call | solution.py:151
  15.7 1.6 %collective-permute-start.4 = (f32[128,384]{1,0:T(8,128)S(1)}, f32[128,384]{1,0:T(8,128)S(1)}, u32[]{:S(2)}, u32[]{:S(2)}) collective-permute-start(f32[128,384]{1,0:T(8,128)S(1)} %project_up.1.refs_0_), channel_id=1, source_target_pairs={{4,0},{0,4},{5,1},{1,5},{6,2},{2,6},{7,3},{3,7},{12,8},{8,12},{13,... | collective-permute-start | bytes 589832 | tf_op jit(solution)/shard_map/ppermute | solution.py:481
  17.3 1.6 %collective-permute-start.5 = (f32[64,128]{1,0:T(8,128)S(1)}, f32[64,128]{1,0:T(8,128)S(1)}, u32[]{:S(2)}, u32[]{:S(2)}) collective-permute-start(f32[64,128]{1,0:T(8,128)S(1)} %add_add_fusion), channel_id=1, source_target_pairs={{0,1},{1,0},{2,3},{3,2},{4,5},{5,4},{6,7},{7,6},{8,9},{9,8},{10,11... | collective-permute-start | bytes 98312 | tf_op jit(solution)/shard_map/ppermute | solution.py:471
  18.9 2.3 %collective-permute-done.5 = f32[64,128]{1,0:T(8,128)S(1)} collective-permute-done((f32[64,128]{1,0:T(8,128)S(1)}, f32[64,128]{1,0:T(8,128)S(1)}, u32[]{:S(2)}, u32[]{:S(2)}) %collective-permute-start.5) | collective-permute-done | bytes 32800 | tf_op jit(solution)/shard_map/ppermute | solution.py:471
  21.2 2.6 %collective-permute-start.6 = (f32[64,128]{1,0:T(8,128)S(1)}, f32[64,128]{1,0:T(8,128)S(1)}, u32[]{:S(2)}, u32[]{:S(2)}) collective-permute-start(f32[64,128]{1,0:T(8,128)S(1)} %add.92.refs_2_), channel_id=1, source_target_pairs={{0,2},{1,3},{2,0},{3,1},{4,6},{5,7},{6,4},{7,5},{8,10},{9,11},{10,... | collective-permute-start | bytes 98312 | tf_op jit(solution)/shard_map/ppermute | solution.py:471
  23.8 2.2 %collective-permute-done.6.refs_3_ = f32[64,128]{1,0:T(8,128)S(1)} collective-permute-done((f32[64,128]{1,0:T(8,128)S(1)}, f32[64,128]{1,0:T(8,128)S(1)}, u32[]{:S(2)}, u32[]{:S(2)}) %collective-permute-start.6) | collective-permute-done | bytes 32800 | tf_op jit(solution)/shard_map/ppermute | solution.py:471
  26.0 2.3 %chain.1 = (bf16[128,256]{1,0:T(8,128)(2,1)S(1)}, f32[128,128]{1,0:T(8,128)S(1)}) custom-call(s32[4,3]{1,0:T(4,128)S(1)} %copy-done.8, s32[4]{0:T(128)S(1)} %copy-done.9, f32[128,384]{1,0:T(8,128)S(1)} %project_up.1.refs_0_, f32[128,384]{1,0:T(8,128)S(1)} %collective-permute-done.4.refs_1_, f32[64,128]{1,0:T(8,128)S(1)} %add.92.refs_2_, ...), custom_call_target="tpu_custom_call" | custom-call | tf_op jit(solution)/shard_map/chain/pallas_call | solution.py:315
  28.4 0.6 gradient.3
  29.0 0.6 gradient.2.kept
  29.7 2.7 %collective-permute-done.7.near = bf16[2,8,64,768]{3,2,1,0:T(8,128)(2,1)S(1)} collective-permute-done((bf16[2,8,64,768]{3,2,1,0:T(8,128)(2,1)S(1)}, bf16[2,8,64,768]{3,2,1,0:T(8,128)(2,1)S(1)}, u32[]{:S(2)}, u32[]{:S(2)}) %collective-permute-start.7) | collective-permute-done | bytes 1572896 | tf_op jit(solution)/shard_map/ppermute | solution.py:471
  32.6 1.6 %collective-permute-start.9 = (bf16[4,64,768]{2,1,0:T(8,128)(2,1)S(1)}, bf16[4,64,768]{2,1,0:T(8,128)(2,1)S(1)}, u32[]{:S(2)}, u32[]{:S(2)}) collective-permute-start(bf16[4,64,768]{2,1,0:T(8,128)(2,1)S(1)} %get-tuple-element.92), channel_id=1, source_target_pairs={{0,1},{1,0},{2,3},{3,2},{4,5},{5,4},{6,7},{7,6},{8,9},{9,8},{10,11... | collective-permute-start | bytes 1179656 | tf_op jit(solution)/shard_map/ppermute | solution.py:471
  34.3 1.5 %collective-permute-start.8 = (bf16[4,64,768]{2,1,0:T(8,128)(2,1)S(1)}, bf16[4,64,768]{2,1,0:T(8,128)(2,1)S(1)}, u32[]{:S(2)}, u32[]{:S(2)}) collective-permute-start(bf16[4,64,768]{2,1,0:T(8,128)(2,1)S(1)} %get-tuple-element.93), channel_id=1, source_target_pairs={{0,16},{8,24},{16,0},{24,8},{1,17},{9,25},{17,1},{25,9},{2,18},{10... | collective-permute-start | bytes 1179656 | tf_op jit(solution)/shard_map/ppermute | solution.py:471
  35.8 1.3 %collective-permute-done.10 = f32[128,128]{1,0:T(8,128)S(1)} collective-permute-done((f32[128,128]{1,0:T(8,128)S(1)}, f32[128,128]{1,0:T(8,128)S(1)}, u32[]{:S(2)}, u32[]{:S(2)}) %collective-permute-start.10) | collective-permute-done | bytes 65568 | tf_op jit(solution)/shard_map/ppermute | solution.py:471
  37.0 2.9 %collective-permute-start.11 = (f32[128,128]{1,0:T(8,128)S(1)}, f32[128,128]{1,0:T(8,128)S(1)}, u32[]{:S(2)}, u32[]{:S(2)}) collective-permute-start(f32[128,128]{1,0:T(8,128)S(1)} %add.95), channel_id=1, source_target_pairs={{0,2},{1,3},{2,0},{3,1},{4,6},{5,7},{6,4},{7,5},{8,10},{9,11},{10,... | collective-permute-start | bytes 196616 | tf_op jit(solution)/shard_map/ppermute | solution.py:471
  39.9 4.4 %collective-permute-done.11 = f32[128,128]{1,0:T(8,128)S(1)} collective-permute-done((f32[128,128]{1,0:T(8,128)S(1)}, f32[128,128]{1,0:T(8,128)S(1)}, u32[]{:S(2)}, u32[]{:S(2)}) %collective-permute-start.11) | collective-permute-done | bytes 65568 | tf_op jit(solution)/shard_map/ppermute | solution.py:471
  44.4 0.9 collective-permute-done.9.up_one
  45.4 1.6 %collective-permute-start.13 = (bf16[2,64,768]{2,1,0:T(8,128)(2,1)S(1)}, bf16[2,64,768]{2,1,0:T(8,128)(2,1)S(1)}, u32[]{:S(2)}, u32[]{:S(2)}) collective-permute-start(bf16[2,64,768]{2,1,0:T(8,128)(2,1)S(1)} %get-tuple-element.90), channel_id=1, source_target_pairs={{0,16},{8,24},{16,0},{24,8},{1,17},{9,25},{17,1},{25,9},{2,18},{10... | collective-permute-start | bytes 589832 | tf_op jit(solution)/shard_map/ppermute | solution.py:471
  47.0 2.7 %collective-permute-start.12 = (bf16[2,64,768]{2,1,0:T(8,128)(2,1)S(1)}, bf16[2,64,768]{2,1,0:T(8,128)(2,1)S(1)}, u32[]{:S(2)}, u32[]{:S(2)}) collective-permute-start(bf16[2,64,768]{2,1,0:T(8,128)(2,1)S(1)} %get-tuple-element.91), channel_id=1, source_target_pairs={{0,1},{1,0},{2,3},{3,2},{4,5},{5,4},{6,7},{7,6},{8,9},{9,8},{10,11... | collective-permute-start | bytes 589832 | tf_op jit(solution)/shard_map/ppermute | solution.py:471
  49.7 5.2 %collective-permute-done.14 = f32[128,128]{1,0:T(8,128)S(1)} collective-permute-done((f32[128,128]{1,0:T(8,128)S(1)}, f32[128,128]{1,0:T(8,128)S(1)}, u32[]{:S(2)}, u32[]{:S(2)}) %collective-permute-start.14) | collective-permute-done | bytes 65568 | tf_op jit(solution)/shard_map/ppermute | solution.py:471
  55.1 2.0 %collective-permute-start.15 = (bf16[2,64,768]{2,1,0:T(8,128)(2,1)S(1)}, bf16[2,64,768]{2,1,0:T(8,128)(2,1)S(1)}, u32[]{:S(2)}, u32[]{:S(2)}) collective-permute-start(bf16[2,64,768]{2,1,0:T(8,128)(2,1)S(1)} %pad_maximum_fusion.7), channel_id=1, source_target_pairs={{0,2},{1,3},{2,0},{3,1},{4,6},{5,7},{6,4},{7,5},{8,10},{9,11},{10,... | collective-permute-start | bytes 589832 | tf_op jit(solution)/shard_map/ppermute | solution.py:471
  57.6 3.7 %collective-permute-done.16.refs_2_ = f32[128,128]{1,0:T(8,128)S(1)} collective-permute-done((f32[128,128]{1,0:T(8,128)S(1)}, f32[128,128]{1,0:T(8,128)S(1)}, u32[]{:S(2)}, u32[]{:S(2)}) %collective-permute-start.16) | collective-permute-done | bytes 65568 | tf_op jit(solution)/shard_map/ppermute | solution.py:471
  61.4 3.9 %collective-permute-done.15.refs_0_ = bf16[2,64,768]{2,1,0:T(8,128)(2,1)S(1)} collective-permute-done((bf16[2,64,768]{2,1,0:T(8,128)(2,1)S(1)}, bf16[2,64,768]{2,1,0:T(8,128)(2,1)S(1)}, u32[]{:S(2)}, u32[]{:S(2)}) %collective-permute-start.15) | collective-permute-done | bytes 196640 | tf_op jit(solution)/shard_map/ppermute | solution.py:471
  65.3 1.8 %update.1 = (f32[1,64,768]{2,1,0:T(8,128)}, f32[1,64,768]{2,1,0:T(8,128)}, f32[1,64,768]{2,1,0:T(8,128)}, f32[1,64,768]{2,1,0:T(8,128)}, f32[1,64,768]{2,1,0:T(8...) custom-call(bf16[2,8,64,768]{3,2,1,0:T(8,128)(2,1)S(1)} %gradient.2.kept, ...), custom_call_target="tpu_custom_call" | custom-call | tf_op jit(solution)/shard_map/update/pallas_call | solution.py:392
  67.1 1.3 %collective-permute-start.17 = (bf16[2,64,768]{2,1,0:T(8,128)(2,1)S(1)}, bf16[2,64,768]{2,1,0:T(8,128)(2,1)S(1)}, u32[]{:S(2)}, u32[]{:S(2)}) collective-permute-start(bf16[2,64,768]{2,1,0:T(8,128)(2,1)S(1)} %get-tuple-element.69), channel_id=1, source_target_pairs={{4,0},{5,1},{6,2},{7,3},{12,8},{13,9},{14,10},{15,11},{20,16},{21,... | collective-permute-start | bytes 589832 | tf_op jit(solution)/shard_map/ppermute | solution.py:486
  68.4 9.6 %collective-permute-done.18 = bf16[2,64,768]{2,1,0:T(8,128)(2,1)S(1)} collective-permute-done((bf16[2,64,768]{2,1,0:T(8,128)(2,1)S(1)}, bf16[2,64,768]{2,1,0:T(8,128)(2,1)S(1)}, u32[]{:S(2)}, u32[]{:S(2)}) %collective-permute-start.18) | collective-permute-done | bytes 196640 | tf_op jit(solution)/shard_map/ppermute | solution.py:471
  78.2 0.6 collective-permute-start.22
  78.7 1.3 %collective-permute-start.19 = (bf16[2,64,768]{2,1,0:T(8,128)(2,1)S(1)}, bf16[2,64,768]{2,1,0:T(8,128)(2,1)S(1)}, u32[]{:S(2)}, u32[]{:S(2)}) collective-permute-start(bf16[2,64,768]{2,1,0:T(8,128)(2,1)S(1)} %collective-permute-done.18), channel_id=1, source_target_pairs={{4,0},{5,1},{6,2},{7,3},{12,8},{13,9},{14,10},{15,11},{20,16},{21,... | collective-permute-start | bytes 589832 | tf_op jit(solution)/shard_map/ppermute | solution.py:486
  80.1 4.6 %collective-permute-done.20 = bf16[2,64,768]{2,1,0:T(8,128)(2,1)S(1)} collective-permute-done((bf16[2,64,768]{2,1,0:T(8,128)(2,1)S(1)}, bf16[2,64,768]{2,1,0:T(8,128)(2,1)S(1)}, u32[]{:S(2)}, u32[]{:S(2)}) %collective-permute-start.20) | collective-permute-done | bytes 196640 | tf_op jit(solution)/shard_map/ppermute | solution.py:471
  85.0 1.3 %collective-permute-start.24 = (bf16[4,64,768]{2,1,0:T(8,128)(2,1)S(1)}, bf16[4,64,768]{2,1,0:T(8,128)(2,1)S(1)}, u32[]{:S(2)}, u32[]{:S(2)}) collective-permute-start(bf16[4,64,768]{2,1,0:T(8,128)(2,1)S(1)} %get-tuple-element.100), channel_id=1, source_target_pairs={{4,0},{5,1},{6,2},{7,3},{12,8},{13,9},{14,10},{15,11},{20,16},{21,... | collective-permute-start | bytes 1179656 | tf_op jit(solution)/shard_map/ppermute | solution.py:486
  86.3 0.5 collective-permute-start.21
  86.8 1.7 %collective-permute-start.23 = (bf16[4,64,768]{2,1,0:T(8,128)(2,1)S(1)}, bf16[4,64,768]{2,1,0:T(8,128)(2,1)S(1)}, u32[]{:S(2)}, u32[]{:S(2)}) collective-permute-start(bf16[4,64,768]{2,1,0:T(8,128)(2,1)S(1)} %get-tuple-element.102), channel_id=1, source_target_pairs={{0,1},{1,0},{2,3},{3,2},{4,5},{5,4},{6,7},{7,6},{8,9},{9,8},{10,11... | collective-permute-start | bytes 1179656 | tf_op jit(solution)/shard_map/ppermute | solution.py:471
  88.7 8.1 %collective-permute-done.24 = bf16[4,64,768]{2,1,0:T(8,128)(2,1)S(1)} collective-permute-done((bf16[4,64,768]{2,1,0:T(8,128)(2,1)S(1)}, bf16[4,64,768]{2,1,0:T(8,128)(2,1)S(1)}, u32[]{:S(2)}, u32[]{:S(2)}) %collective-permute-start.24) | collective-permute-done | bytes 393248 | tf_op jit(solution)/shard_map/ppermute | solution.py:486
  96.9 1.3 %collective-permute-start.25 = (bf16[3,64,768]{2,1,0:T(8,128)(2,1)S(1)}, bf16[3,64,768]{2,1,0:T(8,128)(2,1)S(1)}, u32[]{:S(2)}, u32[]{:S(2)}) collective-permute-start(bf16[3,64,768]{2,1,0:T(8,128)(2,1)S(1)} %pad_maximum_fusion.4), channel_id=1, source_target_pairs={{0,16},{8,24},{16,0},{24,8},{1,17},{9,25},{17,1},{25,9},{2,18},{10... | collective-permute-start | bytes 884744 | tf_op jit(solution)/shard_map/ppermute | solution.py:471
  98.3 1.5 %collective-permute-start.26 = (bf16[3,64,768]{2,1,0:T(8,128)(2,1)S(1)}, bf16[3,64,768]{2,1,0:T(8,128)(2,1)S(1)}, u32[]{:S(2)}, u32[]{:S(2)}) collective-permute-start(bf16[3,64,768]{2,1,0:T(8,128)(2,1)S(1)} %pad_maximum_fusion.5), channel_id=1, source_target_pairs={{0,1},{1,0},{2,3},{3,2},{4,5},{5,4},{6,7},{7,6},{8,9},{9,8},{10,11... | collective-permute-start | bytes 884744 | tf_op jit(solution)/shard_map/ppermute | solution.py:471
  99.8 1.3 %collective-permute-start.27 = (bf16[2,64,768]{2,1,0:T(8,128)(2,1)S(1)}, bf16[2,64,768]{2,1,0:T(8,128)(2,1)S(1)}, u32[]{:S(2)}, u32[]{:S(2)}) collective-permute-start(bf16[2,64,768]{2,1,0:T(8,128)(2,1)S(1)} %pad_maximum_fusion.10), channel_id=1, source_target_pairs={{4,0},{5,1},{6,2},{7,3},{12,8},{13,9},{14,10},{15,11},{20,16},{21,... | collective-permute-start | bytes 589832 | tf_op jit(solution)/shard_map/ppermute | solution.py:486
  101.2 2.6 %collective-permute-done.25 = bf16[3,64,768]{2,1,0:T(8,128)(2,1)S(1)} collective-permute-done((bf16[3,64,768]{2,1,0:T(8,128)(2,1)S(1)}, bf16[3,64,768]{2,1,0:T(8,128)(2,1)S(1)}, u32[]{:S(2)}, u32[]{:S(2)}) %collective-permute-start.25) | collective-permute-done | bytes 294944 | tf_op jit(solution)/shard_map/ppermute | solution.py:471
  103.9 1.2 %collective-permute-done.26 = bf16[3,64,768]{2,1,0:T(8,128)(2,1)S(1)} collective-permute-done((bf16[3,64,768]{2,1,0:T(8,128)(2,1)S(1)}, bf16[3,64,768]{2,1,0:T(8,128)(2,1)S(1)}, u32[]{:S(2)}, u32[]{:S(2)}) %collective-permute-start.26) | collective-permute-done | bytes 294944 | tf_op jit(solution)/shard_map/ppermute | solution.py:471
  105.1 1.7 %place.3 = (bf16[2,64,12288]{2,1,0:T(8,128)(2,1)}, bf16[2,64,12288]{2,1,0:T(8,128)(2,1)}) custom-call(s32[4,3]{1,0:T(4,128)S(1)} %copy-done.8, bf16[8,64,768]{2,1,0:T(8,128)(2,1)S(1)} %constant_dynamic-update-slice_fusion.3.refs_0_, bf16[8,64,768]{2,1,0:T(8,128)(2,1)S(1)} %collective-permute-done.29.refs_1_), custom_call_target="tpu_custom_call" | custom-call | bytes 3145728 | tf_op jit(solution)/shard_map/place/pallas_call | solution.py:452
  107.5 1.7 %collective-permute-done.30.refs_2_ = bf16[8,64,768]{2,1,0:T(8,128)(2,1)S(1)} collective-permute-done((bf16[8,64,768]{2,1,0:T(8,128)(2,1)S(1)}, bf16[8,64,768]{2,1,0:T(8,128)(2,1)S(1)}, u32[]{:S(2)}, u32[]{:S(2)}) %collective-permute-start.30) | collective-permute-done | bytes 786464 | tf_op jit(solution)/shard_map/ppermute | solution.py:471
  109.2 2.2 %place.4 = (bf16[2,64,12288]{2,1,0:T(8,128)(2,1)}, bf16[2,64,12288]{2,1,0:T(8,128)(2,1)}) custom-call(s32[4,3]{1,0:T(4,128)S(1)} %copy-done.8, bf16[8,64,768]{2,1,0:T(8,128)(2,1)S(1)} %pad_maximum_fusion.refs_0_, bf16[8,64,768]{2,1,0:T(8,128)(2,1)S(1)} %constant_dynamic-update-slice_fusion.7.refs_1_, ...), custom_call_target="tpu_custom_call", output_to_operand_aliasing={{0}: (5, {}), {1}: (6, {})} | custom-call | bytes 6291456 | tf_op jit(solution)/shard_map/place/pallas_call | solution.py:452
  111.4 1.7 %place.5 = (bf16[2,64,12288]{2,1,0:T(8,128)(2,1)}, bf16[2,64,12288]{2,1,0:T(8,128)(2,1)}) custom-call(s32[4,3]{1,0:T(4,128)S(1)} %copy-done.8, bf16[8,64,768]{2,1,0:T(8,128)(2,1)S(1)} %constant_dynamic-update-slice_fusion.refs_0_, bf16[8,64,768]{2,1,0:T(8,128)(2,1)S(1)} %collective-permute-done.28.refs_1_, ...), custom_call_target="tpu_custom_call", output_to_operand_aliasing={{0}: (3, {}), {1}: (4, {})} | custom-call | bytes 3145728 | tf_op jit(solution)/shard_map/place/pallas_call | solution.py:452
  (82 shorter events, 3.4 us)
Async XLA Ops:
  1.7 7.9 %collective-permute-start = (bf16[128,768]{1,0:T(8,128)(2,1)S(1)}, bf16[128,768]{1,0:T(8,128)(2,1)S(1)}, u32[]{:S(2)}, u32[]{:S(2)}) collective-permute-start(bf16[128,768]{1,0:T(8,128)(2,1)S(1)} %pad_maximum_fusion.6.refs_0_), channel_id=1, source_target_pairs={{4,0},{0,4},{5,1},{1,5},{6,2},{2,6},{7,3},{3,7},{12,8},{8,12},{13,... | collective-permute-start | bytes 589832 | tf_op jit(solution)/shard_map/ppermute | solution.py:481
  4.7 7.0 %copy-start = (bf16[1,4,32,12288]{3,2,1,0:T(8,128)(2,1)S(1)}, bf16[1,4,32,12288]{3,2,1,0:T(8,128)(2,1)}, u32[]{:S(2)}) copy-start(bf16[1,4,32,12288]{3,2,1,0:T(8,128)(2,1)} %param.12) | copy-start | bytes 9437188
  4.7 7.0 %copy-start.1 = (bf16[1,1,2,64,12288]{4,3,2,1,0:T(8,128)(2,1)S(1)}, bf16[1,1,2,64,12288]{4,3,2,1,0:T(8,128)(2,1)}, u32[]{:S(2)}) copy-start(bf16[1,1,2,64,12288]{4,3,2,1,0:T(8,128)(2,1)} %param.16) | copy-start | bytes 9437188
  9.8 3.4 %collective-permute-start.3 = (f32[64,128]{1,0:T(8,128)S(1)}, f32[64,128]{1,0:T(8,128)S(1)}, u32[]{:S(2)}, u32[]{:S(2)}) collective-permute-start(f32[64,128]{1,0:T(8,128)S(1)} %get-tuple-element.53), channel_id=1, source_target_pairs={{0,24},{8,16},{16,8},{24,0},{1,25},{9,17},{17,9},{25,1},{2,26},{10... | collective-permute-start | bytes 98312 | tf_op jit(solution)/shard_map/ppermute | solution.py:471
  10.2 3.9 %collective-permute-start.2 = (f32[64,128]{1,0:T(8,128)S(1)}, f32[64,128]{1,0:T(8,128)S(1)}, u32[]{:S(2)}, u32[]{:S(2)}) collective-permute-start(f32[64,128]{1,0:T(8,128)S(1)} %get-tuple-element.53), channel_id=1, source_target_pairs={{0,16},{8,24},{16,0},{24,8},{1,17},{9,25},{17,1},{25,9},{2,18},{10... | collective-permute-start | bytes 98312 | tf_op jit(solution)/shard_map/ppermute | solution.py:471
  11.7 2.4 %collective-permute-start.1 = (f32[64,128]{1,0:T(8,128)S(1)}, f32[64,128]{1,0:T(8,128)S(1)}, u32[]{:S(2)}, u32[]{:S(2)}) collective-permute-start(f32[64,128]{1,0:T(8,128)S(1)} %get-tuple-element.53), channel_id=1, source_target_pairs={{0,8},{8,0},{16,24},{24,16},{1,9},{9,1},{17,25},{25,17},{2,10},{10... | collective-permute-start | bytes 98312 | tf_op jit(solution)/shard_map/ppermute | solution.py:471
  11.8 2.4 %copy-start.9 = (s32[4]{0:T(128)S(1)}, s32[4]{0:T(128)}, u32[]{:S(2)}) copy-start(s32[4]{0:T(128)} %counts.3) | copy-start | bytes 52
  14.1 11.9 %copy-start.8 = (s32[4,3]{1,0:T(4,128)S(1)}, s32[4,3]{1,0:T(4,128)}, u32[]{:S(2)}) copy-start(s32[4,3]{1,0:T(4,128)} %bounds.7) | copy-start | bytes 148
  15.7 10.3 %collective-permute-start.4 = (f32[128,384]{1,0:T(8,128)S(1)}, f32[128,384]{1,0:T(8,128)S(1)}, u32[]{:S(2)}, u32[]{:S(2)}) collective-permute-start(f32[128,384]{1,0:T(8,128)S(1)} %project_up.1.refs_0_), channel_id=1, source_target_pairs={{4,0},{0,4},{5,1},{1,5},{6,2},{2,6},{7,3},{3,7},{12,8},{8,12},{13,... | collective-permute-start | bytes 589832 | tf_op jit(solution)/shard_map/ppermute | solution.py:481
  17.3 3.9 %collective-permute-start.5 = (f32[64,128]{1,0:T(8,128)S(1)}, f32[64,128]{1,0:T(8,128)S(1)}, u32[]{:S(2)}, u32[]{:S(2)}) collective-permute-start(f32[64,128]{1,0:T(8,128)S(1)} %add_add_fusion), channel_id=1, source_target_pairs={{0,1},{1,0},{2,3},{3,2},{4,5},{5,4},{6,7},{7,6},{8,9},{9,8},{10,11... | collective-permute-start | bytes 98312 | tf_op jit(solution)/shard_map/ppermute | solution.py:471
  21.2 4.8 %collective-permute-start.6 = (f32[64,128]{1,0:T(8,128)S(1)}, f32[64,128]{1,0:T(8,128)S(1)}, u32[]{:S(2)}, u32[]{:S(2)}) collective-permute-start(f32[64,128]{1,0:T(8,128)S(1)} %add.92.refs_2_), channel_id=1, source_target_pairs={{0,2},{1,3},{2,0},{3,1},{4,6},{5,7},{6,4},{7,5},{8,10},{9,11},{10,... | collective-permute-start | bytes 98312 | tf_op jit(solution)/shard_map/ppermute | solution.py:471
  29.0 3.5 %collective-permute-start.7 = (bf16[2,8,64,768]{3,2,1,0:T(8,128)(2,1)S(1)}, bf16[2,8,64,768]{3,2,1,0:T(8,128)(2,1)S(1)}, u32[]{:S(2)}, u32[]{:S(2)}) collective-permute-start(bf16[2,8,64,768]{3,2,1,0:T(8,128)(2,1)S(1)} %gradient.3), channel_id=1, source_target_pairs={{0,8},{8,0},{16,24},{24,16},{1,9},{9,1},{17,25},{25,17},{2,10},{10... | collective-permute-start | bytes 4718600 | tf_op jit(solution)/shard_map/ppermute | solution.py:471
  29.7 35.6 %copy-start.2 = (f32[1,64,768]{2,1,0:T(8,128)S(1)}, f32[1,64,768]{2,1,0:T(8,128)}, u32[]{:S(2)}) copy-start(f32[1,64,768]{2,1,0:T(8,128)} %refs_5_.1) | copy-start | bytes 589828
  29.7 35.6 %copy-start.3 = (f32[1,64,768]{2,1,0:T(8,128)S(1)}, f32[1,64,768]{2,1,0:T(8,128)}, u32[]{:S(2)}) copy-start(f32[1,64,768]{2,1,0:T(8,128)} %refs_4_.1) | copy-start | bytes 589828
  29.7 35.6 %copy-start.4 = (f32[1,64,768]{2,1,0:T(8,128)S(1)}, f32[1,64,768]{2,1,0:T(8,128)}, u32[]{:S(2)}) copy-start(f32[1,64,768]{2,1,0:T(8,128)} %refs_6_.1) | copy-start | bytes 589828
  29.7 35.6 %copy-start.5 = (f32[1,64,768]{2,1,0:T(8,128)S(1)}, f32[1,64,768]{2,1,0:T(8,128)}, u32[]{:S(2)}) copy-start(f32[1,64,768]{2,1,0:T(8,128)} %refs_7_.1) | copy-start | bytes 589828
  29.7 35.6 %copy-start.6 = (f32[1,64,768]{2,1,0:T(8,128)S(1)}, f32[1,64,768]{2,1,0:T(8,128)}, u32[]{:S(2)}) copy-start(f32[1,64,768]{2,1,0:T(8,128)} %refs_8_.1) | copy-start | bytes 589828
  29.7 35.6 %copy-start.7 = (f32[1,64,768]{2,1,0:T(8,128)S(1)}, f32[1,64,768]{2,1,0:T(8,128)}, u32[]{:S(2)}) copy-start(f32[1,64,768]{2,1,0:T(8,128)} %refs_9_.1) | copy-start | bytes 589828
  32.6 12.6 %collective-permute-start.9 = (bf16[4,64,768]{2,1,0:T(8,128)(2,1)S(1)}, bf16[4,64,768]{2,1,0:T(8,128)(2,1)S(1)}, u32[]{:S(2)}, u32[]{:S(2)}) collective-permute-start(bf16[4,64,768]{2,1,0:T(8,128)(2,1)S(1)} %get-tuple-element.92), channel_id=1, source_target_pairs={{0,1},{1,0},{2,3},{3,2},{4,5},{5,4},{6,7},{7,6},{8,9},{9,8},{10,11... | collective-permute-start | bytes 1179656 | tf_op jit(solution)/shard_map/ppermute | solution.py:471
  34.3 11.0 %collective-permute-start.8 = (bf16[4,64,768]{2,1,0:T(8,128)(2,1)S(1)}, bf16[4,64,768]{2,1,0:T(8,128)(2,1)S(1)}, u32[]{:S(2)}, u32[]{:S(2)}) collective-permute-start(bf16[4,64,768]{2,1,0:T(8,128)(2,1)S(1)} %get-tuple-element.93), channel_id=1, source_target_pairs={{0,16},{8,24},{16,0},{24,8},{1,17},{9,25},{17,1},{25,9},{2,18},{10... | collective-permute-start | bytes 1179656 | tf_op jit(solution)/shard_map/ppermute | solution.py:471
  35.8 1.3 %collective-permute-start.10 = (f32[128,128]{1,0:T(8,128)S(1)}, f32[128,128]{1,0:T(8,128)S(1)}, u32[]{:S(2)}, u32[]{:S(2)}) collective-permute-start(f32[128,128]{1,0:T(8,128)S(1)} %get-tuple-element.61), channel_id=1, source_target_pairs={{0,8},{8,0},{16,24},{24,16},{1,9},{9,1},{17,25},{25,17},{2,10},{10... | collective-permute-start | bytes 196616 | tf_op jit(solution)/shard_map/ppermute | solution.py:471
  37.0 7.3 %collective-permute-start.11 = (f32[128,128]{1,0:T(8,128)S(1)}, f32[128,128]{1,0:T(8,128)S(1)}, u32[]{:S(2)}, u32[]{:S(2)}) collective-permute-start(f32[128,128]{1,0:T(8,128)S(1)} %add.95), channel_id=1, source_target_pairs={{0,2},{1,3},{2,0},{3,1},{4,6},{5,7},{6,4},{7,5},{8,10},{9,11},{10,... | collective-permute-start | bytes 196616 | tf_op jit(solution)/shard_map/ppermute | solution.py:471
  45.4 9.5 %collective-permute-start.13 = (bf16[2,64,768]{2,1,0:T(8,128)(2,1)S(1)}, bf16[2,64,768]{2,1,0:T(8,128)(2,1)S(1)}, u32[]{:S(2)}, u32[]{:S(2)}) collective-permute-start(bf16[2,64,768]{2,1,0:T(8,128)(2,1)S(1)} %get-tuple-element.90), channel_id=1, source_target_pairs={{0,16},{8,24},{16,0},{24,8},{1,17},{9,25},{17,1},{25,9},{2,18},{10... | collective-permute-start | bytes 589832 | tf_op jit(solution)/shard_map/ppermute | solution.py:471
  47.0 8.0 %collective-permute-start.12 = (bf16[2,64,768]{2,1,0:T(8,128)(2,1)S(1)}, bf16[2,64,768]{2,1,0:T(8,128)(2,1)S(1)}, u32[]{:S(2)}, u32[]{:S(2)}) collective-permute-start(bf16[2,64,768]{2,1,0:T(8,128)(2,1)S(1)} %get-tuple-element.91), channel_id=1, source_target_pairs={{0,1},{1,0},{2,3},{3,2},{4,5},{5,4},{6,7},{7,6},{8,9},{9,8},{10,11... | collective-permute-start | bytes 589832 | tf_op jit(solution)/shard_map/ppermute | solution.py:471
  49.7 5.3 %collective-permute-start.14 = (f32[128,128]{1,0:T(8,128)S(1)}, f32[128,128]{1,0:T(8,128)S(1)}, u32[]{:S(2)}, u32[]{:S(2)}) collective-permute-start(f32[128,128]{1,0:T(8,128)S(1)} %add.96), channel_id=1, source_target_pairs={{0,1},{1,0},{2,3},{3,2},{4,5},{5,4},{6,7},{7,6},{8,9},{9,8},{10,11... | collective-permute-start | bytes 196616 | tf_op jit(solution)/shard_map/ppermute | solution.py:471
  55.1 10.1 %collective-permute-start.15 = (bf16[2,64,768]{2,1,0:T(8,128)(2,1)S(1)}, bf16[2,64,768]{2,1,0:T(8,128)(2,1)S(1)}, u32[]{:S(2)}, u32[]{:S(2)}) collective-permute-start(bf16[2,64,768]{2,1,0:T(8,128)(2,1)S(1)} %pad_maximum_fusion.7), channel_id=1, source_target_pairs={{0,2},{1,3},{2,0},{3,1},{4,6},{5,7},{6,4},{7,5},{8,10},{9,11},{10,... | collective-permute-start | bytes 589832 | tf_op jit(solution)/shard_map/ppermute | solution.py:471
  57.1 4.3 %collective-permute-start.16 = (f32[128,128]{1,0:T(8,128)S(1)}, f32[128,128]{1,0:T(8,128)S(1)}, u32[]{:S(2)}, u32[]{:S(2)}) collective-permute-start(f32[128,128]{1,0:T(8,128)S(1)} %add.103.refs_1_), channel_id=1, source_target_pairs={{0,16},{8,24},{16,0},{24,8},{1,17},{9,25},{17,1},{25,9},{2,18},{10... | collective-permute-start | bytes 196616 | tf_op jit(solution)/shard_map/ppermute | solution.py:471
  67.1 11.0 %collective-permute-start.18 = (bf16[2,64,768]{2,1,0:T(8,128)(2,1)S(1)}, bf16[2,64,768]{2,1,0:T(8,128)(2,1)S(1)}, u32[]{:S(2)}, u32[]{:S(2)}) collective-permute-start(bf16[2,64,768]{2,1,0:T(8,128)(2,1)S(1)} %get-tuple-element.69), channel_id=1, source_target_pairs={{0,2},{1,3},{2,0},{3,1},{4,6},{5,7},{6,4},{7,5},{8,10},{9,11},{10,... | collective-permute-start | bytes 589832 | tf_op jit(solution)/shard_map/ppermute | solution.py:471
  67.1 13.0 %collective-permute-start.17 = (bf16[2,64,768]{2,1,0:T(8,128)(2,1)S(1)}, bf16[2,64,768]{2,1,0:T(8,128)(2,1)S(1)}, u32[]{:S(2)}, u32[]{:S(2)}) collective-permute-start(bf16[2,64,768]{2,1,0:T(8,128)(2,1)S(1)} %get-tuple-element.69), channel_id=1, source_target_pairs={{4,0},{5,1},{6,2},{7,3},{12,8},{13,9},{14,10},{15,11},{20,16},{21,... | collective-permute-start | bytes 589832 | tf_op jit(solution)/shard_map/ppermute | solution.py:486
  78.1 6.7 %collective-permute-start.20 = (bf16[2,64,768]{2,1,0:T(8,128)(2,1)S(1)}, bf16[2,64,768]{2,1,0:T(8,128)(2,1)S(1)}, u32[]{:S(2)}, u32[]{:S(2)}) collective-permute-start(bf16[2,64,768]{2,1,0:T(8,128)(2,1)S(1)} %pad_maximum_fusion.8), channel_id=1, source_target_pairs={{0,1},{1,0},{2,3},{3,2},{4,5},{5,4},{6,7},{7,6},{8,9},{9,8},{10,11... | collective-permute-start | bytes 589832 | tf_op jit(solution)/shard_map/ppermute | solution.py:471
  78.2 6.7 %collective-permute-start.22 = (bf16[2,64,768]{2,1,0:T(8,128)(2,1)S(1)}, bf16[2,64,768]{2,1,0:T(8,128)(2,1)S(1)}, u32[]{:S(2)}, u32[]{:S(2)}) collective-permute-start(bf16[2,64,768]{2,1,0:T(8,128)(2,1)S(1)} %pad_maximum_fusion.9), channel_id=1, source_target_pairs={{0,16},{8,24},{16,0},{24,8},{1,17},{9,25},{17,1},{25,9},{2,18},{10... | collective-permute-start | bytes 589832 | tf_op jit(solution)/shard_map/ppermute | solution.py:471
  78.7 9.9 %collective-permute-start.19 = (bf16[2,64,768]{2,1,0:T(8,128)(2,1)S(1)}, bf16[2,64,768]{2,1,0:T(8,128)(2,1)S(1)}, u32[]{:S(2)}, u32[]{:S(2)}) collective-permute-start(bf16[2,64,768]{2,1,0:T(8,128)(2,1)S(1)} %collective-permute-done.18), channel_id=1, source_target_pairs={{4,0},{5,1},{6,2},{7,3},{12,8},{13,9},{14,10},{15,11},{20,16},{21,... | collective-permute-start | bytes 589832 | tf_op jit(solution)/shard_map/ppermute | solution.py:486
  85.0 11.8 %collective-permute-start.24 = (bf16[4,64,768]{2,1,0:T(8,128)(2,1)S(1)}, bf16[4,64,768]{2,1,0:T(8,128)(2,1)S(1)}, u32[]{:S(2)}, u32[]{:S(2)}) collective-permute-start(bf16[4,64,768]{2,1,0:T(8,128)(2,1)S(1)} %get-tuple-element.100), channel_id=1, source_target_pairs={{4,0},{5,1},{6,2},{7,3},{12,8},{13,9},{14,10},{15,11},{20,16},{21,... | collective-permute-start | bytes 1179656 | tf_op jit(solution)/shard_map/ppermute | solution.py:486
  86.3 10.5 %collective-permute-start.21 = (bf16[4,64,768]{2,1,0:T(8,128)(2,1)S(1)}, bf16[4,64,768]{2,1,0:T(8,128)(2,1)S(1)}, u32[]{:S(2)}, u32[]{:S(2)}) collective-permute-start(bf16[4,64,768]{2,1,0:T(8,128)(2,1)S(1)} %get-tuple-element.101), channel_id=1, source_target_pairs={{0,16},{8,24},{16,0},{24,8},{1,17},{9,25},{17,1},{25,9},{2,18},{10... | collective-permute-start | bytes 1179656 | tf_op jit(solution)/shard_map/ppermute | solution.py:471
  86.8 10.0 %collective-permute-start.23 = (bf16[4,64,768]{2,1,0:T(8,128)(2,1)S(1)}, bf16[4,64,768]{2,1,0:T(8,128)(2,1)S(1)}, u32[]{:S(2)}, u32[]{:S(2)}) collective-permute-start(bf16[4,64,768]{2,1,0:T(8,128)(2,1)S(1)} %get-tuple-element.102), channel_id=1, source_target_pairs={{0,1},{1,0},{2,3},{3,2},{4,5},{5,4},{6,7},{7,6},{8,9},{9,8},{10,11... | collective-permute-start | bytes 1179656 | tf_op jit(solution)/shard_map/ppermute | solution.py:471
  88.6 16.5 %collective-permute-start.29 = (bf16[8,64,768]{2,1,0:T(8,128)(2,1)S(1)}, bf16[8,64,768]{2,1,0:T(8,128)(2,1)S(1)}, u32[]{:S(2)}, u32[]{:S(2)}) collective-permute-start(bf16[8,64,768]{2,1,0:T(8,128)(2,1)S(1)} %constant_dynamic-update-slice_fusion.3.refs_0_), channel_id=1, source_target_pairs={{0,8},{8,0},{16,24},{24,16},{1,9},{9,1},{17,25},{25,17},{2,10},{10... | collective-permute-start | bytes 2359304 | tf_op jit(solution)/shard_map/ppermute | solution.py:471
  96.9 7.0 %collective-permute-start.25 = (bf16[3,64,768]{2,1,0:T(8,128)(2,1)S(1)}, bf16[3,64,768]{2,1,0:T(8,128)(2,1)S(1)}, u32[]{:S(2)}, u32[]{:S(2)}) collective-permute-start(bf16[3,64,768]{2,1,0:T(8,128)(2,1)S(1)} %pad_maximum_fusion.4), channel_id=1, source_target_pairs={{0,16},{8,24},{16,0},{24,8},{1,17},{9,25},{17,1},{25,9},{2,18},{10... | collective-permute-start | bytes 884744 | tf_op jit(solution)/shard_map/ppermute | solution.py:471
  98.3 6.8 %collective-permute-start.26 = (bf16[3,64,768]{2,1,0:T(8,128)(2,1)S(1)}, bf16[3,64,768]{2,1,0:T(8,128)(2,1)S(1)}, u32[]{:S(2)}, u32[]{:S(2)}) collective-permute-start(bf16[3,64,768]{2,1,0:T(8,128)(2,1)S(1)} %pad_maximum_fusion.5), channel_id=1, source_target_pairs={{0,1},{1,0},{2,3},{3,2},{4,5},{5,4},{6,7},{7,6},{8,9},{9,8},{10,11... | collective-permute-start | bytes 884744 | tf_op jit(solution)/shard_map/ppermute | solution.py:471
  99.8 7.6 %collective-permute-start.27 = (bf16[2,64,768]{2,1,0:T(8,128)(2,1)S(1)}, bf16[2,64,768]{2,1,0:T(8,128)(2,1)S(1)}, u32[]{:S(2)}, u32[]{:S(2)}) collective-permute-start(bf16[2,64,768]{2,1,0:T(8,128)(2,1)S(1)} %pad_maximum_fusion.10), channel_id=1, source_target_pairs={{4,0},{5,1},{6,2},{7,3},{12,8},{13,9},{14,10},{15,11},{20,16},{21,... | collective-permute-start | bytes 589832 | tf_op jit(solution)/shard_map/ppermute | solution.py:486
  101.1 6.4 %collective-permute-start.31 = (bf16[8,64,768]{2,1,0:T(8,128)(2,1)S(1)}, bf16[8,64,768]{2,1,0:T(8,128)(2,1)S(1)}, u32[]{:S(2)}, u32[]{:S(2)}) collective-permute-start(bf16[8,64,768]{2,1,0:T(8,128)(2,1)S(1)} %constant_dynamic-update-slice_fusion.7.refs_1_), channel_id=1, source_target_pairs={{0,8},{8,0},{16,24},{24,16},{1,9},{9,1},{17,25},{25,17},{2,10},{10... | collective-permute-start | bytes 2359304 | tf_op jit(solution)/shard_map/ppermute | solution.py:471
  106.8 2.4 %collective-permute-start.30 = (bf16[8,64,768]{2,1,0:T(8,128)(2,1)S(1)}, bf16[8,64,768]{2,1,0:T(8,128)(2,1)S(1)}, u32[]{:S(2)}, u32[]{:S(2)}) collective-permute-start(bf16[8,64,768]{2,1,0:T(8,128)(2,1)S(1)} %pad_maximum_fusion.refs_0_), channel_id=1, source_target_pairs={{0,8},{8,0},{16,24},{24,16},{1,9},{9,1},{17,25},{25,17},{2,10},{10... | collective-permute-start | bytes 2359304 | tf_op jit(solution)/shard_map/ppermute | solution.py:471
  107.4 4.1 %collective-permute-start.28 = (bf16[8,64,768]{2,1,0:T(8,128)(2,1)S(1)}, bf16[8,64,768]{2,1,0:T(8,128)(2,1)S(1)}, u32[]{:S(2)}, u32[]{:S(2)}) collective-permute-start(bf16[8,64,768]{2,1,0:T(8,128)(2,1)S(1)} %constant_dynamic-update-slice_fusion.refs_0_), channel_id=1, source_target_pairs={{0,8},{8,0},{16,24},{24,16},{1,9},{9,1},{17,25},{25,17},{2,10},{10... | collective-permute-start | bytes 2359304 | tf_op jit(solution)/shard_map/ppermute | solution.py:471

commit v6 on v4

--- a/solution.py
+++ b/solution.py
@@ -307,35 +307,40 @@
     )(bounds, counts, *inputs)
 
 
-def gradient_kernel(first, factor_ref, h_ref, g_ref, out_ref):
+def gradient_kernel(first, lead, factor_ref, h_ref, g_ref, out_ref):
     _, _, ranks, columns = out_ref.shape
+    tokens = h_ref.shape[0]
     replica_at = lax.axis_index("replica")
     tensor_at = lax.axis_index("tensor")
     tensors = lax.axis_size("tensor")
-    factors = factor_ref[...]
-    for far in range(2):
-        for hop in range(4):
-            owner = (replica_at ^ (first + 2 * far)) * tensors + (tensor_at ^ hop)
-            cut = pl.ds(pl.multiple_of(owner * columns, columns), columns)
-            stacked = jnp.concatenate([h_ref[:, cut], g_ref[:, cut]], axis=0)
-            block = jnp.dot(factors, stacked, preferred_element_type=f32).astype(bf16)
-            low, high = hop % 2, hop // 2
-            out_ref[0, 4 * far + 2 * low + high] = block[:ranks]
-            out_ref[1, 4 * low + 2 * far + high] = block[ranks:]
-
-
-def gradient(factors, hidden, cot, first, columns):
+    down = factor_ref[:ranks, :tokens]
+    up = factor_ref[ranks:]
+    for middle in range(2):
+        for high in range(2):
+            for which, (far, low) in enumerate(((lead, middle), (middle, lead))):
+                hop = low + 2 * high
+                owner = (replica_at ^ (first + 2 * far)) * tensors + (tensor_at ^ hop)
+                cut = pl.ds(pl.multiple_of(owner * columns, columns), columns)
+                if which == 0:
+                    block = jnp.dot(down, h_ref[:, cut], preferred_element_type=f32)
+                else:
+                    stacked = jnp.concatenate([h_ref[:, cut], g_ref[:, cut]], axis=0)
+                    block = jnp.dot(up, stacked, preferred_element_type=f32)
+                out_ref[which, 2 * middle + high] = block.astype(bf16)
+
+
+def gradient(factors, hidden, cot, first, lead, columns):
     tokens, features = hidden.shape
     rows = factors.shape[0]
     return pl.pallas_call(
-        functools.partial(gradient_kernel, first),
+        functools.partial(gradient_kernel, first, lead),
         in_specs=[in_vmem] * 3,
         out_specs=in_vmem,
-        out_shape=jax.ShapeDtypeStruct((2, 8, rows // 2, columns), bf16),
+        out_shape=jax.ShapeDtypeStruct((2, 4, rows // 2, columns), bf16),
         compiler_params=limited,
         cost_estimate=pl.CostEstimate(
-            flops=2 * rows * tokens * features,
-            bytes_accessed=(2 * tokens + rows) * features,
+            flops=rows * tokens * features,
+            bytes_accessed=(tokens + rows // 2) * features,
             transcendentals=0,
         ),
         name="gradient",
@@ -396,10 +401,10 @@
     zeros[...] = jnp.zeros_like(zeros)
 
     def fill(slot, distance, go):
-        for (window, blocks), source in zip(layout, sources):
-            if window != distance:
-                continue
-            for i, (which, order, hop) in enumerate(blocks):
+        for blocks, source in zip(layout, sources):
+            for i, (window, which, order, hop) in enumerate(blocks):
+                if window != distance:
+                    continue
                 owner = (replica_at ^ order) * tensors + (tensor_at ^ hop)
                 cut = pl.ds(pl.multiple_of(owner * columns, columns), columns)
                 go(pltpu.make_async_copy(source.at[i], outs[which].at[slot, :, cut], sem))
@@ -428,8 +433,8 @@
 
 
 def place(bounds, pieces, before, slots, ranks, features):
-    layout = [piece[:2] for piece in pieces]
-    arrays = [piece[2] for piece in pieces]
+    layout = [blocks for blocks, _ in pieces]
+    arrays = [array for _, array in pieces]
     columns = arrays[0].shape[-1]
     return pl.pallas_call(
         functools.partial(place_kernel, layout, not before),
@@ -475,71 +480,68 @@
     return total.astype(bf16)
 
 
-def reduced(factors, hidden, cot, columns):
-    sent = gradient(factors, hidden, cot, 1, columns)
-    near = swapped(sent, "replica", 1)
-    kept = gradient(factors, hidden, cot, 0, columns)
+def reduced(factors, hidden, cot, columns, mixed):
+    def halves(lead, factors):
+        sent = gradient(factors, hidden, cot, 1, lead, columns)
+        return swapped(sent, "replica", 1), gradient(factors, hidden, cot, 0, lead, columns)
+
+    near, kept = halves(1, factors)
+    mixed = mixed + swapped(mixed, "tensor", 1)
+    down_one = summed(kept[0], near[0])
+    up_one = summed(kept[1], near[1])
+    down_one, up_one, mixed, factors = lax.optimization_barrier(
+        (down_one, up_one, mixed, factors)
+    )
+    down_one = swapped(down_one, "replica", 2)
+    up_one = swapped(up_one, "tensor", 1)
+    near, kept = halves(0, factors)
 
     def part(which, cut, *steps):
         return summed(kept[which, cut], near[which, cut], *steps)
 
-    high, low = slice(4, 8), slice(2, 4)
-    down_one = swapped(part(0, high), "replica", 2)
-    up_one = swapped(part(1, high), "tensor", 1)
+    low = slice(2, 4)
     down_two = swapped(part(0, low, down_one[2:]), "tensor", 1)
     up_two = swapped(part(1, low, up_one[2:]), "replica", 2)
     last = jnp.stack([part(0, 1, down_one[1], down_two[1]), part(1, 1, up_one[1], up_two[1])])
     last = swapped(last, "tensor", 2)
-    return (kept, near, (down_one, down_two), (up_one, up_two), last)
-
-
-def swapped_before_last(block, axis, distance):
-    size, sections = lax.axis_size(axis), lax.axis_size("section")
-    ahead = axis == "replica"
-    axes = (axis, "section") if ahead else ("section", axis)
-
-    def place_of(i, section):
-        return i * sections + section if ahead else section * size + i
-
-    route = [
-        (place_of(i, section), place_of(i ^ distance, section))
-        for i in range(size)
-        for section in range(sections - 1)
+    for axis, distance in (("tensor", 2), ("replica", 1)):
+        mixed = mixed + swapped(mixed, axis, distance)
+    other = swapped(mixed, "replica", 2)
+    return (kept, near, (down_one, down_two), (up_one, up_two), last, mixed, other)
+
+
+def crossed(piece, axis, distance):
+    blocks, array = piece
+    blocks = [
+        (window, which, order ^ distance, hop)
+        if axis == "replica"
+        else (window, which, order, hop ^ distance)
+        for window, which, order, hop in blocks
     ]
-    return lax.ppermute(block, axes, route)
-
-
-def crossed(piece, axis, distance):
-    window, blocks, array = piece
-    blocks = [
-        (which, order ^ distance, hop) if axis == "replica" else (which, order, hop ^ distance)
-        for which, order, hop in blocks
-    ]
-    swap = swapped if window == 0 else swapped_before_last
-    return (window, blocks, swap(array, axis, distance))
+    return blocks, swapped(array, axis, distance)
 
 
 def fetched(piece):
-    _, blocks, array = piece
-    return (1, blocks, following_layer(array))
-
-
-def picked(piece, cut):
-    return (piece[0], piece[1][cut], piece[2][cut])
+    blocks, array = piece
+    return [(1, *block[1:]) for block in blocks], following_layer(array)
+
+
+def picked(piece, at):
+    return piece[0][at : at + 1], piece[1][at : at + 1]
 
 
 def joined(*pieces):
-    blocks = [block for piece in pieces for block in piece[1]]
-    return (pieces[0][0], blocks, jnp.concatenate([piece[2] for piece in pieces]))
+    blocks = [block for piece in pieces for block in piece[0]]
+    return blocks, jnp.concatenate([array for _, array in pieces])
 
 
 def spread(share, bounds, slots, features):
     ranks = share.shape[1]
-    own = (0, [(0, 0, 0), (1, 0, 0)], share)
+    own = ([(0, 0, 0, 0), (0, 1, 0, 0)], share)
     one = crossed(own, "tensor", 2)
     next_own = fetched(own)
-    downs = joined(picked(own, slice(0, 1)), picked(one, slice(0, 1)))
-    ups = joined(picked(own, slice(1, 2)), picked(one, slice(1, 2)))
+    downs = joined(picked(own, 0), picked(one, 0))
+    ups = joined(picked(own, 1), picked(one, 1))
     down_two = crossed(downs, "tensor", 1)
     up_two = crossed(ups, "replica", 2)
     next_one = fetched(one)
@@ -547,23 +549,22 @@
     down_three = crossed(joined(downs, down_two), "replica", 2)
     up_three = crossed(joined(ups, up_two), "tensor", 1)
     next_two = fetched(two)
+    next_end = fetched(joined(picked(down_three, 3), picked(up_three, 3)))
+    _, _, next_array = lax.optimization_barrier((down_three[1], up_three[1], next_two[1]))
+    next_two = (next_two[0], next_array)
+    down_end = joined(picked(next_own, 0), picked(next_one, 0), picked(next_two, 0))
+    up_end = joined(picked(next_own, 1), picked(next_one, 1), picked(next_two, 2))
+    end = joined(crossed(down_end, "replica", 2), crossed(up_end, "tensor", 1), next_end)
     near = joined(own, one, two)
-    near_core = crossed(near, "replica", 1)
-    last, first, second = slice(3, 4), slice(0, 1), slice(1, 2)
-    next_end = fetched(joined(picked(down_three, last), picked(up_three, last)))
+    far = joined(down_three, up_three)
     next_near = joined(next_own, next_one, next_two)
-    down_end = joined(*(picked(piece, first) for piece in (next_own, next_one, next_two)))
-    up_end = joined(
-        picked(next_own, second), picked(next_one, second), picked(next_two, slice(2, 3))
-    )
-    end = joined(crossed(down_end, "replica", 2), crossed(up_end, "tensor", 1), next_end)
-    placed = place(bounds, [near, near_core], [], slots, ranks, features)
-    far = joined(down_three, up_three)
-    far_array, *placed = lax.optimization_barrier((far[2], *placed))
-    far = (*far[:2], far_array)
-    for group in ((far, next_near), (end,)):
-        pieces = [*group, *(crossed(piece, "replica", 1) for piece in group)]
-        placed = place(bounds, pieces, placed, slots, ranks, features)
+    near_core, far_core, next_core, end_core = (
+        crossed(piece, "replica", 1) for piece in (near, far, next_near, end)
+    )
+    placed = place(
+        bounds, [near, near_core, far, far_core, next_near, next_core], [], slots, ranks, features
+    )
+    placed = place(bounds, [end, end_core], placed, slots, ranks, features)
     return placed
 
 
@@ -605,12 +606,9 @@
         bounds, micro_counts, projections, tables, square, slots, features, per_micro
     )
 
-    parts = reduced(factors, hidden, cot, master_down.shape[2])
-    for axis, distance in (("replica", 1), ("tensor", 1), ("tensor", 2)):
-        mixed = mixed + swapped(mixed, axis, distance)
-    other = swapped(mixed, "replica", 2)
+    parts = reduced(factors, hidden, cot, master_down.shape[2], mixed)
     state = [master_down, master_up, moment_down, moment_up, second_down, second_up]
-    updated = update(*parts, mixed, other, right, state)
+    updated = update(*parts, right, state)
     placed = spread(updated[6], bounds, slots, features)
     return (placed[0][None, None], placed[1][None, None], *updated[:6])
 

time: 117 us -> 109 us (0.932)
  waiting for transfers between devices: 55.1 us -> 50.8 us
  starting transfers between devices: 39.2 us -> 35.3 us
    ppermute x4 -> x0, starting transfers between devices: 10.4 us -> none  [swapped_before_last(): return lax.ppermute(block, axes, route)]
    ppermute x22 -> x27, starting transfers between devices: 20 us -> 26.5 us  [swapped(): return lax.ppermute(block, axis, route)]
    ppermute x4 -> x0, waiting for transfers between devices: 2.06 us -> none  [swapped_before_last(): return lax.ppermute(block, axes, route)]
    ppermute x4, waiting for transfers between devices: 8.4 us -> 6.65 us  [following_layer(): return lax.ppermute(block, 'section', [(i + 1, i) for i in range(size - 1)])]
    pallas_call x3 -> x2, Pallas kernels: 5.69 us -> 4.47 us  [place(): pl.pallas_call(functools.partial(place_kernel, layout, not before), in_sp...]
    ppermute x22 -> x27, waiting for transfers between devices: 44.6 us -> 44.2 us  [swapped(): return lax.ppermute(block, axis, route)]
  transfers between devices with their start and end apart: 32 -> 33, of which waited for: 17 -> 18; matrix products, arithmetic and copies ran while one was open for 1% -> 1% of each run, Pallas kernels for 10% -> 10%
where the time goes in v6:
time: 109 us; the launch traced here: 108 us
  waiting for transfers between devices  50.8 us (47%)
  starting transfers between devices  35.3 us (32%)
  Pallas kernels  18.2 us (17%)
  other arithmetic  1.8 us (2%)
  between operations  1.17 us (1%)
    ppermute x27, waiting for transfers between devices, swapped(): return lax.ppermute(block, axis, route)  44.2 us
    ppermute x27, starting transfers between devices, swapped(): return lax.ppermute(block, axis, route)  26.5 us
    ppermute x4, waiting for transfers between devices, following_layer(): return lax.ppermute(block, 'section', [(i + 1, i) for i in range(size - 1)])  6.65 us
    pallas_call x1, Pallas kernels, project(): pl.pallas_call(functools.partial(project_kernel, steps), in_specs=[in_hbm...  5.99 us
    ppermute x4, starting transfers between devices, following_layer(): return lax.ppermute(block, 'section', [(i + 1, i) for i in range(size - 1)])  5.15 us
    pallas_call x2, Pallas kernels, place(): pl.pallas_call(functools.partial(place_kernel, layout, not before), in_sp...  4.47 us
    ppermute x2, starting transfers between devices, from_next(): return lax.ppermute(block, 'section', route)  3.69 us
    pallas_call x1, Pallas kernels, chain(): pl.pallas_call(kernel, in_specs=[in_smem] * 2 + [in_vmem] * len(inputs),...  2.33 us
  transfers between devices with their start and end apart: 33, of which 18 were waited for; matrix products, arithmetic and copies ran while one was open for 1% of the time, Pallas kernels for 10%

profile of v6, /device:TPU:0, one launch (start us, length us, event | category | flops | bytes accessed | tf_op | source)
XLA Modules:
  0.0 107.7 jit_solution(16942533604294059225)
XLA Ops:
  0.6 1.0 convert_bitcast_fusion
  1.7 3.0 %collective-permute-start = (bf16[128,768]{1,0:T(8,128)(2,1)S(1)}, bf16[128,768]{1,0:T(8,128)(2,1)S(1)}, u32[]{:S(2)}, u32[]{:S(2)}) collective-permute-start(bf16[128,768]{1,0:T(8,128)(2,1)S(1)} %pad_maximum_fusion.5.refs_0_), channel_id=1, source_target_pairs={{4,0},{0,4},{5,1},{1,5},{6,2},{2,6},{7,3},{3,7},{12,8},{8,12},{13,... | collective-permute-start | bytes 589832 | tf_op jit(solution)/shard_map/ppermute | solution.py:468
  4.7 6.0 %project.1 = (f32[128,256]{1,0:T(8,128)S(1)}, f32[128,128]{1,0:T(8,128)S(1)}, bf16[128,12288]{1,0:T(8,128)(2,1)S(1)}, bf16[128,12288]{1,0:T(8,128)(2,1)S(1)}) custom-call(bf16[128,12288]{1,0:T(8,128)(2,1)} %bitcast.41, bf16[2,64,12288]{2,1,0:T(8,128)(2,1)} %bitcast.42, bf16[2,64,12288]{2,1,0:T(8,128)(2,1)} %bitcast.43), custom_call_target="tpu_custom_call" | custom-call | flops 805306368 | bytes 9437184 | tf_op jit(solution)/shard_map/project/pallas_call | solution.py:98
  10.9 0.7 collective-permute-start.4
  11.7 0.9 collective-permute-start.3
  12.8 1.5 %project_back.1.refs_0_ = f32[128,384]{1,0:T(8,128)S(1)} custom-call(s32[4]{0:T(128)S(1)} %copy-done.8, f32[128,256]{1,0:T(8,128)S(1)} %get-tuple-element.37.by_hidden, bf16[128,12288]{1,0:T(8,128)(2,1)S(1)} %bitcast.34, bf16[128,12288]{1,0:T(8,128)(2,1)S(1)} %get-tuple-element.41.up_ref), custom_call_target="tpu_custom_call" | custom-call | flops 402653184 | bytes 6291456 | tf_op jit(solution)/shard_map/project_back/pallas_call | solution.py:133
  14.4 0.7 collective-permute-start.1
  15.1 0.8 collective-permute-done.3
  15.9 1.6 %collective-permute-start.5 = (f32[64,128]{1,0:T(8,128)S(1)}, f32[64,128]{1,0:T(8,128)S(1)}, u32[]{:S(2)}, u32[]{:S(2)}) collective-permute-start(f32[64,128]{1,0:T(8,128)S(1)} %add_add_fusion), channel_id=1, source_target_pairs={{0,1},{1,0},{2,3},{3,2},{4,5},{5,4},{6,7},{7,6},{8,9},{9,8},{10,11... | collective-permute-start | bytes 98312 | tf_op jit(solution)/shard_map/ppermute | solution.py:458
  17.6 2.3 %collective-permute-done.5 = f32[64,128]{1,0:T(8,128)S(1)} collective-permute-done((f32[64,128]{1,0:T(8,128)S(1)}, f32[64,128]{1,0:T(8,128)S(1)}, u32[]{:S(2)}, u32[]{:S(2)}) %collective-permute-start.5) | collective-permute-done | bytes 32800 | tf_op jit(solution)/shard_map/ppermute | solution.py:458
  19.9 2.6 %collective-permute-start.6 = (f32[64,128]{1,0:T(8,128)S(1)}, f32[64,128]{1,0:T(8,128)S(1)}, u32[]{:S(2)}, u32[]{:S(2)}) collective-permute-start(f32[64,128]{1,0:T(8,128)S(1)} %add.92.refs_2_), channel_id=1, source_target_pairs={{0,2},{1,3},{2,0},{3,1},{4,6},{5,7},{6,4},{7,5},{8,10},{9,11},{10,... | collective-permute-start | bytes 98312 | tf_op jit(solution)/shard_map/ppermute | solution.py:458
  22.5 2.2 %collective-permute-done.6.refs_3_ = f32[64,128]{1,0:T(8,128)S(1)} collective-permute-done((f32[64,128]{1,0:T(8,128)S(1)}, f32[64,128]{1,0:T(8,128)S(1)}, u32[]{:S(2)}, u32[]{:S(2)}) %collective-permute-start.6) | collective-permute-done | bytes 32800 | tf_op jit(solution)/shard_map/ppermute | solution.py:458
  24.7 2.3 %chain.1 = (bf16[128,256]{1,0:T(8,128)(2,1)S(1)}, f32[128,128]{1,0:T(8,128)S(1)}) custom-call(s32[4,3]{1,0:T(4,128)S(1)} %copy-done.7, s32[4]{0:T(128)S(1)} %copy-done.8, f32[128,384]{1,0:T(8,128)S(1)} %project_back.1.refs_0_, f32[128,384]{1,0:T(8,128)S(1)} %collective-permute-done.1.refs_1_, f32[64,128]{1,0:T(8,128)S(1)} %add.92.refs_2_, ...), custom_call_target="tpu_custom_call" | custom-call | tf_op jit(solution)/shard_map/chain/pallas_call | solution.py:297
  27.1 0.5 gradient.5
  27.6 1.6 %collective-permute-start.8 = (f32[128,128]{1,0:T(8,128)S(1)}, f32[128,128]{1,0:T(8,128)S(1)}, u32[]{:S(2)}, u32[]{:S(2)}) collective-permute-start(f32[128,128]{1,0:T(8,128)S(1)} %get-tuple-element.46), channel_id=1, source_target_pairs={{0,1},{1,0},{2,3},{3,2},{4,5},{5,4},{6,7},{7,6},{8,9},{9,8},{10,11... | collective-permute-start | bytes 196616 | tf_op jit(solution)/shard_map/ppermute | solution.py:458
  29.8 2.4 %collective-permute-done.8 = f32[128,128]{1,0:T(8,128)S(1)} collective-permute-done((f32[128,128]{1,0:T(8,128)S(1)}, f32[128,128]{1,0:T(8,128)S(1)}, u32[]{:S(2)}, u32[]{:S(2)}) %collective-permute-start.8) | collective-permute-done | bytes 65568 | tf_op jit(solution)/shard_map/ppermute | solution.py:458
  32.4 0.5 gradient.7
  33.0 0.8 collective-permute-start.10
  33.7 1.6 %collective-permute-start.12 = (bf16[4,64,768]{2,1,0:T(8,128)(2,1)S(1)}, bf16[4,64,768]{2,1,0:T(8,128)(2,1)S(1)}, u32[]{:S(2)}, u32[]{:S(2)}) collective-permute-start(bf16[4,64,768]{2,1,0:T(8,128)(2,1)S(1)} %get-tuple-element.49), channel_id=1, source_target_pairs={{0,1},{1,0},{2,3},{3,2},{4,5},{5,4},{6,7},{7,6},{8,9},{9,8},{10,11... | collective-permute-start | bytes 1179656 | tf_op jit(solution)/shard_map/ppermute | solution.py:458
  35.3 0.5 gradient.6.kept
  35.9 8.6 %collective-permute-done.10.down_one = bf16[4,64,768]{2,1,0:T(8,128)(2,1)S(1)} collective-permute-done((bf16[4,64,768]{2,1,0:T(8,128)(2,1)S(1)}, bf16[4,64,768]{2,1,0:T(8,128)(2,1)S(1)}, u32[]{:S(2)}, u32[]{:S(2)}) %collective-permute-start.10) | collective-permute-done | bytes 393248 | tf_op jit(solution)/shard_map/ppermute | solution.py:458
  45.1 1.4 %collective-permute-start.13 = (bf16[2,64,768]{2,1,0:T(8,128)(2,1)S(1)}, bf16[2,64,768]{2,1,0:T(8,128)(2,1)S(1)}, u32[]{:S(2)}, u32[]{:S(2)}) collective-permute-start(bf16[2,64,768]{2,1,0:T(8,128)(2,1)S(1)} %get-tuple-element.66), channel_id=1, source_target_pairs={{0,16},{8,24},{16,0},{24,8},{1,17},{9,25},{17,1},{25,9},{2,18},{10... | collective-permute-start | bytes 589832 | tf_op jit(solution)/shard_map/ppermute | solution.py:458
  46.5 1.6 %collective-permute-start.11 = (bf16[2,64,768]{2,1,0:T(8,128)(2,1)S(1)}, bf16[2,64,768]{2,1,0:T(8,128)(2,1)S(1)}, u32[]{:S(2)}, u32[]{:S(2)}) collective-permute-start(bf16[2,64,768]{2,1,0:T(8,128)(2,1)S(1)} %get-tuple-element.67), channel_id=1, source_target_pairs={{0,1},{1,0},{2,3},{3,2},{4,5},{5,4},{6,7},{7,6},{8,9},{9,8},{10,11... | collective-permute-start | bytes 589832 | tf_op jit(solution)/shard_map/ppermute | solution.py:458
  48.0 2.8 %collective-permute-start.15 = (f32[128,128]{1,0:T(8,128)S(1)}, f32[128,128]{1,0:T(8,128)S(1)}, u32[]{:S(2)}, u32[]{:S(2)}) collective-permute-start(f32[128,128]{1,0:T(8,128)S(1)} %add.95), channel_id=1, source_target_pairs={{0,2},{1,3},{2,0},{3,1},{4,6},{5,7},{6,4},{7,5},{8,10},{9,11},{10,... | collective-permute-start | bytes 196616 | tf_op jit(solution)/shard_map/ppermute | solution.py:458
  51.3 2.3 %collective-permute-done.11.down_two = bf16[2,64,768]{2,1,0:T(8,128)(2,1)S(1)} collective-permute-done((bf16[2,64,768]{2,1,0:T(8,128)(2,1)S(1)}, bf16[2,64,768]{2,1,0:T(8,128)(2,1)S(1)}, u32[]{:S(2)}, u32[]{:S(2)}) %collective-permute-start.11) | collective-permute-done | bytes 196640 | tf_op jit(solution)/shard_map/ppermute | solution.py:458
  53.7 2.2 %collective-permute-start.14 = (bf16[2,64,768]{2,1,0:T(8,128)(2,1)S(1)}, bf16[2,64,768]{2,1,0:T(8,128)(2,1)S(1)}, u32[]{:S(2)}, u32[]{:S(2)}) collective-permute-start(bf16[2,64,768]{2,1,0:T(8,128)(2,1)S(1)} %pad_maximum_fusion.6), channel_id=1, source_target_pairs={{0,2},{1,3},{2,0},{3,1},{4,6},{5,7},{6,4},{7,5},{8,10},{9,11},{10,... | collective-permute-start | bytes 589832 | tf_op jit(solution)/shard_map/ppermute | solution.py:458
  56.0 1.2 %collective-permute-done.16 = f32[128,128]{1,0:T(8,128)S(1)} collective-permute-done((f32[128,128]{1,0:T(8,128)S(1)}, f32[128,128]{1,0:T(8,128)S(1)}, u32[]{:S(2)}, u32[]{:S(2)}) %collective-permute-start.16) | collective-permute-done | bytes 65568 | tf_op jit(solution)/shard_map/ppermute | solution.py:458
  57.3 0.8 collective-permute-start.17
  58.0 3.6 %collective-permute-done.17.refs_2_ = f32[128,128]{1,0:T(8,128)S(1)} collective-permute-done((f32[128,128]{1,0:T(8,128)S(1)}, f32[128,128]{1,0:T(8,128)S(1)}, u32[]{:S(2)}, u32[]{:S(2)}) %collective-permute-start.17) | collective-permute-done | bytes 65568 | tf_op jit(solution)/shard_map/ppermute | solution.py:458
  61.6 2.4 %collective-permute-done.14.refs_0_ = bf16[2,64,768]{2,1,0:T(8,128)(2,1)S(1)} collective-permute-done((bf16[2,64,768]{2,1,0:T(8,128)(2,1)S(1)}, bf16[2,64,768]{2,1,0:T(8,128)(2,1)S(1)}, u32[]{:S(2)}, u32[]{:S(2)}) %collective-permute-start.14) | collective-permute-done | bytes 196640 | tf_op jit(solution)/shard_map/ppermute | solution.py:458
  64.0 1.8 %update.1 = (f32[1,64,768]{2,1,0:T(8,128)}, f32[1,64,768]{2,1,0:T(8,128)}, f32[1,64,768]{2,1,0:T(8,128)}, f32[1,64,768]{2,1,0:T(8,128)}, f32[1,64,768]{2,1,0:T(8...) custom-call(bf16[2,4,64,768]{3,2,1,0:T(8,128)(2,1)S(1)} %gradient.6.kept, ...), custom_call_target="tpu_custom_call" | custom-call | tf_op jit(solution)/shard_map/update/pallas_call | solution.py:379
  65.8 1.3 %collective-permute-start.18 = (bf16[2,64,768]{2,1,0:T(8,128)(2,1)S(1)}, bf16[2,64,768]{2,1,0:T(8,128)(2,1)S(1)}, u32[]{:S(2)}, u32[]{:S(2)}) collective-permute-start(bf16[2,64,768]{2,1,0:T(8,128)(2,1)S(1)} %get-tuple-element.52), channel_id=1, source_target_pairs={{4,0},{5,1},{6,2},{7,3},{12,8},{13,9},{14,10},{15,11},{20,16},{21,... | collective-permute-start | bytes 589832 | tf_op jit(solution)/shard_map/ppermute | solution.py:473
  67.2 8.6 %collective-permute-done.19 = bf16[2,64,768]{2,1,0:T(8,128)(2,1)S(1)} collective-permute-done((bf16[2,64,768]{2,1,0:T(8,128)(2,1)S(1)}, bf16[2,64,768]{2,1,0:T(8,128)(2,1)S(1)}, u32[]{:S(2)}, u32[]{:S(2)}) %collective-permute-start.19) | collective-permute-done | bytes 196640 | tf_op jit(solution)/shard_map/ppermute | solution.py:458
  76.0 0.8 collective-permute-start.23
  76.7 1.3 %collective-permute-start.20 = (bf16[2,64,768]{2,1,0:T(8,128)(2,1)S(1)}, bf16[2,64,768]{2,1,0:T(8,128)(2,1)S(1)}, u32[]{:S(2)}, u32[]{:S(2)}) collective-permute-start(bf16[2,64,768]{2,1,0:T(8,128)(2,1)S(1)} %collective-permute-done.19), channel_id=1, source_target_pairs={{4,0},{5,1},{6,2},{7,3},{12,8},{13,9},{14,10},{15,11},{20,16},{21,... | collective-permute-start | bytes 589832 | tf_op jit(solution)/shard_map/ppermute | solution.py:473
  78.1 3.5 %collective-permute-done.21 = bf16[2,64,768]{2,1,0:T(8,128)(2,1)S(1)} collective-permute-done((bf16[2,64,768]{2,1,0:T(8,128)(2,1)S(1)}, bf16[2,64,768]{2,1,0:T(8,128)(2,1)S(1)}, u32[]{:S(2)}, u32[]{:S(2)}) %collective-permute-start.21) | collective-permute-done | bytes 196640 | tf_op jit(solution)/shard_map/ppermute | solution.py:458
  81.8 1.3 %collective-permute-start.25 = (bf16[4,64,768]{2,1,0:T(8,128)(2,1)S(1)}, bf16[4,64,768]{2,1,0:T(8,128)(2,1)S(1)}, u32[]{:S(2)}, u32[]{:S(2)}) collective-permute-start(bf16[4,64,768]{2,1,0:T(8,128)(2,1)S(1)} %get-tuple-element.76), channel_id=1, source_target_pairs={{4,0},{5,1},{6,2},{7,3},{12,8},{13,9},{14,10},{15,11},{20,16},{21,... | collective-permute-start | bytes 1179656 | tf_op jit(solution)/shard_map/ppermute | solution.py:473
  83.1 0.8 collective-permute-start.22
  83.9 2.0 %collective-permute-start.24 = (bf16[4,64,768]{2,1,0:T(8,128)(2,1)S(1)}, bf16[4,64,768]{2,1,0:T(8,128)(2,1)S(1)}, u32[]{:S(2)}, u32[]{:S(2)}) collective-permute-start(bf16[4,64,768]{2,1,0:T(8,128)(2,1)S(1)} %get-tuple-element.78), channel_id=1, source_target_pairs={{0,1},{1,0},{2,3},{3,2},{4,5},{5,4},{6,7},{7,6},{8,9},{9,8},{10,11... | collective-permute-start | bytes 1179656 | tf_op jit(solution)/shard_map/ppermute | solution.py:458
  86.1 6.6 %collective-permute-done.25 = bf16[4,64,768]{2,1,0:T(8,128)(2,1)S(1)} collective-permute-done((bf16[4,64,768]{2,1,0:T(8,128)(2,1)S(1)}, bf16[4,64,768]{2,1,0:T(8,128)(2,1)S(1)}, u32[]{:S(2)}, u32[]{:S(2)}) %collective-permute-start.25) | collective-permute-done | bytes 393248 | tf_op jit(solution)/shard_map/ppermute | solution.py:473
  92.8 1.3 %collective-permute-start.28 = (bf16[2,64,768]{2,1,0:T(8,128)(2,1)S(1)}, bf16[2,64,768]{2,1,0:T(8,128)(2,1)S(1)}, u32[]{:S(2)}, u32[]{:S(2)}) collective-permute-start(bf16[2,64,768]{2,1,0:T(8,128)(2,1)S(1)} %pad_maximum_fusion.9), channel_id=1, source_target_pairs={{4,0},{5,1},{6,2},{7,3},{12,8},{13,9},{14,10},{15,11},{20,16},{21,... | collective-permute-start | bytes 589832 | tf_op jit(solution)/shard_map/ppermute | solution.py:473
  94.2 1.4 %collective-permute-start.26 = (bf16[3,64,768]{2,1,0:T(8,128)(2,1)S(1)}, bf16[3,64,768]{2,1,0:T(8,128)(2,1)S(1)}, u32[]{:S(2)}, u32[]{:S(2)}) collective-permute-start(bf16[3,64,768]{2,1,0:T(8,128)(2,1)S(1)} %pad_maximum_fusion.3), channel_id=1, source_target_pairs={{0,16},{8,24},{16,0},{24,8},{1,17},{9,25},{17,1},{25,9},{2,18},{10... | collective-permute-start | bytes 884744 | tf_op jit(solution)/shard_map/ppermute | solution.py:458
  95.6 2.1 %collective-permute-start.27 = (bf16[3,64,768]{2,1,0:T(8,128)(2,1)S(1)}, bf16[3,64,768]{2,1,0:T(8,128)(2,1)S(1)}, u32[]{:S(2)}, u32[]{:S(2)}) collective-permute-start(bf16[3,64,768]{2,1,0:T(8,128)(2,1)S(1)} %pad_maximum_fusion.4), channel_id=1, source_target_pairs={{0,1},{1,0},{2,3},{3,2},{4,5},{5,4},{6,7},{7,6},{8,9},{9,8},{10,11... | collective-permute-start | bytes 884744 | tf_op jit(solution)/shard_map/ppermute | solution.py:458
  97.8 3.1 %collective-permute-done.26 = bf16[3,64,768]{2,1,0:T(8,128)(2,1)S(1)} collective-permute-done((bf16[3,64,768]{2,1,0:T(8,128)(2,1)S(1)}, bf16[3,64,768]{2,1,0:T(8,128)(2,1)S(1)}, u32[]{:S(2)}, u32[]{:S(2)}) %collective-permute-start.26) | collective-permute-done | bytes 294944 | tf_op jit(solution)/shard_map/ppermute | solution.py:458
  101.0 1.4 %collective-permute-done.27 = bf16[3,64,768]{2,1,0:T(8,128)(2,1)S(1)} collective-permute-done((bf16[3,64,768]{2,1,0:T(8,128)(2,1)S(1)}, bf16[3,64,768]{2,1,0:T(8,128)(2,1)S(1)}, u32[]{:S(2)}, u32[]{:S(2)}) %collective-permute-start.27) | collective-permute-done | bytes 294944 | tf_op jit(solution)/shard_map/ppermute | solution.py:458
  102.5 0.7 collective-permute-done.32.refs_5_
  103.2 2.7 %place.2 = (bf16[2,64,12288]{2,1,0:T(8,128)(2,1)}, bf16[2,64,12288]{2,1,0:T(8,128)(2,1)}) custom-call(s32[4,3]{1,0:T(4,128)S(1)} %copy-done.7, bf16[8,64,768]{2,1,0:T(8,128)(2,1)S(1)} %constant_dynamic-update-slice_fusion.3.refs_0_, bf16[8,64,768]{2,1,0:T(8,128)(2,1)S(1)} %collective-permute-done.30.refs_1_, ...), custom_call_target="tpu_custom_call" | custom-call | bytes 9437184 | tf_op jit(solution)/shard_map/place/pallas_call | solution.py:439
  106.0 1.7 %place.3 = (bf16[2,64,12288]{2,1,0:T(8,128)(2,1)}, bf16[2,64,12288]{2,1,0:T(8,128)(2,1)}) custom-call(s32[4,3]{1,0:T(4,128)S(1)} %copy-done.7, bf16[8,64,768]{2,1,0:T(8,128)(2,1)S(1)} %constant_dynamic-update-slice_fusion.refs_0_, bf16[8,64,768]{2,1,0:T(8,128)(2,1)S(1)} %collective-permute-done.29.refs_1_, ...), custom_call_target="tpu_custom_call", output_to_operand_aliasing={{0}: (3, {}), {1}: (4, {})} | custom-call | bytes 3145728 | tf_op jit(solution)/shard_map/place/pallas_call | solution.py:439
  (83 shorter events, 3.6 us)
Async XLA Ops:
  1.7 9.0 %collective-permute-start = (bf16[128,768]{1,0:T(8,128)(2,1)S(1)}, bf16[128,768]{1,0:T(8,128)(2,1)S(1)}, u32[]{:S(2)}, u32[]{:S(2)}) collective-permute-start(bf16[128,768]{1,0:T(8,128)(2,1)S(1)} %pad_maximum_fusion.5.refs_0_), channel_id=1, source_target_pairs={{4,0},{0,4},{5,1},{1,5},{6,2},{2,6},{7,3},{3,7},{12,8},{8,12},{13,... | collective-permute-start | bytes 589832 | tf_op jit(solution)/shard_map/ppermute | solution.py:468
  4.7 8.1 %copy-start = (bf16[1,4,32,12288]{3,2,1,0:T(8,128)(2,1)S(1)}, bf16[1,4,32,12288]{3,2,1,0:T(8,128)(2,1)}, u32[]{:S(2)}) copy-start(bf16[1,4,32,12288]{3,2,1,0:T(8,128)(2,1)} %param.13) | copy-start | bytes 9437188
  4.7 8.1 %copy-start.8 = (s32[4]{0:T(128)S(1)}, s32[4]{0:T(128)}, u32[]{:S(2)}) copy-start(s32[4]{0:T(128)} %counts.3) | copy-start | bytes 52
  10.9 4.1 %collective-permute-start.4 = (f32[64,128]{1,0:T(8,128)S(1)}, f32[64,128]{1,0:T(8,128)S(1)}, u32[]{:S(2)}, u32[]{:S(2)}) collective-permute-start(f32[64,128]{1,0:T(8,128)S(1)} %get-tuple-element.42), channel_id=1, source_target_pairs={{0,24},{8,16},{16,8},{24,0},{1,25},{9,17},{17,9},{25,1},{2,26},{10... | collective-permute-start | bytes 98312 | tf_op jit(solution)/shard_map/ppermute | solution.py:458
  11.7 4.2 %collective-permute-start.3 = (f32[64,128]{1,0:T(8,128)S(1)}, f32[64,128]{1,0:T(8,128)S(1)}, u32[]{:S(2)}, u32[]{:S(2)}) collective-permute-start(f32[64,128]{1,0:T(8,128)S(1)} %get-tuple-element.42), channel_id=1, source_target_pairs={{0,16},{8,24},{16,0},{24,8},{1,17},{9,25},{17,1},{25,9},{2,18},{10... | collective-permute-start | bytes 98312 | tf_op jit(solution)/shard_map/ppermute | solution.py:458
  12.6 3.3 %collective-permute-start.2 = (f32[64,128]{1,0:T(8,128)S(1)}, f32[64,128]{1,0:T(8,128)S(1)}, u32[]{:S(2)}, u32[]{:S(2)}) collective-permute-start(f32[64,128]{1,0:T(8,128)S(1)} %get-tuple-element.42), channel_id=1, source_target_pairs={{0,8},{8,0},{16,24},{24,16},{1,9},{9,1},{17,25},{25,17},{2,10},{10... | collective-permute-start | bytes 98312 | tf_op jit(solution)/shard_map/ppermute | solution.py:458
  12.8 11.9 %copy-start.7 = (s32[4,3]{1,0:T(4,128)S(1)}, s32[4,3]{1,0:T(4,128)}, u32[]{:S(2)}) copy-start(s32[4,3]{1,0:T(4,128)} %bounds.5) | copy-start | bytes 148
  14.4 10.4 %collective-permute-start.1 = (f32[128,384]{1,0:T(8,128)S(1)}, f32[128,384]{1,0:T(8,128)S(1)}, u32[]{:S(2)}, u32[]{:S(2)}) collective-permute-start(f32[128,384]{1,0:T(8,128)S(1)} %project_back.1.refs_0_), channel_id=1, source_target_pairs={{4,0},{0,4},{5,1},{1,5},{6,2},{2,6},{7,3},{3,7},{12,8},{8,12},{13,... | collective-permute-start | bytes 589832 | tf_op jit(solution)/shard_map/ppermute | solution.py:468
  15.9 4.0 %collective-permute-start.5 = (f32[64,128]{1,0:T(8,128)S(1)}, f32[64,128]{1,0:T(8,128)S(1)}, u32[]{:S(2)}, u32[]{:S(2)}) collective-permute-start(f32[64,128]{1,0:T(8,128)S(1)} %add_add_fusion), channel_id=1, source_target_pairs={{0,1},{1,0},{2,3},{3,2},{4,5},{5,4},{6,7},{7,6},{8,9},{9,8},{10,11... | collective-permute-start | bytes 98312 | tf_op jit(solution)/shard_map/ppermute | solution.py:458
  19.9 4.8 %collective-permute-start.6 = (f32[64,128]{1,0:T(8,128)S(1)}, f32[64,128]{1,0:T(8,128)S(1)}, u32[]{:S(2)}, u32[]{:S(2)}) collective-permute-start(f32[64,128]{1,0:T(8,128)S(1)} %add.92.refs_2_), channel_id=1, source_target_pairs={{0,2},{1,3},{2,0},{3,1},{4,6},{5,7},{6,4},{7,5},{8,10},{9,11},{10,... | collective-permute-start | bytes 98312 | tf_op jit(solution)/shard_map/ppermute | solution.py:458
  27.6 4.6 %collective-permute-start.7 = (bf16[2,4,64,768]{3,2,1,0:T(8,128)(2,1)S(1)}, bf16[2,4,64,768]{3,2,1,0:T(8,128)(2,1)S(1)}, u32[]{:S(2)}, u32[]{:S(2)}) collective-permute-start(bf16[2,4,64,768]{3,2,1,0:T(8,128)(2,1)S(1)} %gradient.5), channel_id=1, source_target_pairs={{0,8},{8,0},{16,24},{24,16},{1,9},{9,1},{17,25},{25,17},{2,10},{10... | collective-permute-start | bytes 2359304 | tf_op jit(solution)/shard_map/ppermute | solution.py:458
  27.6 4.5 %collective-permute-start.8 = (f32[128,128]{1,0:T(8,128)S(1)}, f32[128,128]{1,0:T(8,128)S(1)}, u32[]{:S(2)}, u32[]{:S(2)}) collective-permute-start(f32[128,128]{1,0:T(8,128)S(1)} %get-tuple-element.46), channel_id=1, source_target_pairs={{0,1},{1,0},{2,3},{3,2},{4,5},{5,4},{6,7},{7,6},{8,9},{9,8},{10,11... | collective-permute-start | bytes 196616 | tf_op jit(solution)/shard_map/ppermute | solution.py:458
  32.9 12.1 %collective-permute-start.9 = (bf16[2,4,64,768]{3,2,1,0:T(8,128)(2,1)S(1)}, bf16[2,4,64,768]{3,2,1,0:T(8,128)(2,1)S(1)}, u32[]{:S(2)}, u32[]{:S(2)}) collective-permute-start(bf16[2,4,64,768]{3,2,1,0:T(8,128)(2,1)S(1)} %gradient.7), channel_id=1, source_target_pairs={{0,8},{8,0},{16,24},{24,16},{1,9},{9,1},{17,25},{25,17},{2,10},{10... | collective-permute-start | bytes 2359304 | tf_op jit(solution)/shard_map/ppermute | solution.py:458
  33.0 11.5 %collective-permute-start.10 = (bf16[4,64,768]{2,1,0:T(8,128)(2,1)S(1)}, bf16[4,64,768]{2,1,0:T(8,128)(2,1)S(1)}, u32[]{:S(2)}, u32[]{:S(2)}) collective-permute-start(bf16[4,64,768]{2,1,0:T(8,128)(2,1)S(1)} %get-tuple-element.48), channel_id=1, source_target_pairs={{0,16},{8,24},{16,0},{24,8},{1,17},{9,25},{17,1},{25,9},{2,18},{10... | collective-permute-start | bytes 1179656 | tf_op jit(solution)/shard_map/ppermute | solution.py:458
  33.7 11.2 %collective-permute-start.12 = (bf16[4,64,768]{2,1,0:T(8,128)(2,1)S(1)}, bf16[4,64,768]{2,1,0:T(8,128)(2,1)S(1)}, u32[]{:S(2)}, u32[]{:S(2)}) collective-permute-start(bf16[4,64,768]{2,1,0:T(8,128)(2,1)S(1)} %get-tuple-element.49), channel_id=1, source_target_pairs={{0,1},{1,0},{2,3},{3,2},{4,5},{5,4},{6,7},{7,6},{8,9},{9,8},{10,11... | collective-permute-start | bytes 1179656 | tf_op jit(solution)/shard_map/ppermute | solution.py:458
  35.8 28.2 %copy-start.1 = (f32[1,64,768]{2,1,0:T(8,128)S(1)}, f32[1,64,768]{2,1,0:T(8,128)}, u32[]{:S(2)}) copy-start(f32[1,64,768]{2,1,0:T(8,128)} %refs_5_.1) | copy-start | bytes 589828
  35.8 28.2 %copy-start.2 = (f32[1,64,768]{2,1,0:T(8,128)S(1)}, f32[1,64,768]{2,1,0:T(8,128)}, u32[]{:S(2)}) copy-start(f32[1,64,768]{2,1,0:T(8,128)} %refs_4_.1) | copy-start | bytes 589828
  35.8 28.2 %copy-start.3 = (f32[1,64,768]{2,1,0:T(8,128)S(1)}, f32[1,64,768]{2,1,0:T(8,128)}, u32[]{:S(2)}) copy-start(f32[1,64,768]{2,1,0:T(8,128)} %refs_6_.1) | copy-start | bytes 589828
  35.9 28.2 %copy-start.4 = (f32[1,64,768]{2,1,0:T(8,128)S(1)}, f32[1,64,768]{2,1,0:T(8,128)}, u32[]{:S(2)}) copy-start(f32[1,64,768]{2,1,0:T(8,128)} %refs_7_.1) | copy-start | bytes 589828
  35.9 28.2 %copy-start.5 = (f32[1,64,768]{2,1,0:T(8,128)S(1)}, f32[1,64,768]{2,1,0:T(8,128)}, u32[]{:S(2)}) copy-start(f32[1,64,768]{2,1,0:T(8,128)} %refs_8_.1) | copy-start | bytes 589828
  35.9 28.1 %copy-start.6 = (f32[1,64,768]{2,1,0:T(8,128)S(1)}, f32[1,64,768]{2,1,0:T(8,128)}, u32[]{:S(2)}) copy-start(f32[1,64,768]{2,1,0:T(8,128)} %refs_9_.1) | copy-start | bytes 589828
  45.1 6.2 %collective-permute-start.13 = (bf16[2,64,768]{2,1,0:T(8,128)(2,1)S(1)}, bf16[2,64,768]{2,1,0:T(8,128)(2,1)S(1)}, u32[]{:S(2)}, u32[]{:S(2)}) collective-permute-start(bf16[2,64,768]{2,1,0:T(8,128)(2,1)S(1)} %get-tuple-element.66), channel_id=1, source_target_pairs={{0,16},{8,24},{16,0},{24,8},{1,17},{9,25},{17,1},{25,9},{2,18},{10... | collective-permute-start | bytes 589832 | tf_op jit(solution)/shard_map/ppermute | solution.py:458
  46.5 7.1 %collective-permute-start.11 = (bf16[2,64,768]{2,1,0:T(8,128)(2,1)S(1)}, bf16[2,64,768]{2,1,0:T(8,128)(2,1)S(1)}, u32[]{:S(2)}, u32[]{:S(2)}) collective-permute-start(bf16[2,64,768]{2,1,0:T(8,128)(2,1)S(1)} %get-tuple-element.67), channel_id=1, source_target_pairs={{0,1},{1,0},{2,3},{3,2},{4,5},{5,4},{6,7},{7,6},{8,9},{9,8},{10,11... | collective-permute-start | bytes 589832 | tf_op jit(solution)/shard_map/ppermute | solution.py:458
  48.0 7.9 %collective-permute-start.15 = (f32[128,128]{1,0:T(8,128)S(1)}, f32[128,128]{1,0:T(8,128)S(1)}, u32[]{:S(2)}, u32[]{:S(2)}) collective-permute-start(f32[128,128]{1,0:T(8,128)S(1)} %add.95), channel_id=1, source_target_pairs={{0,2},{1,3},{2,0},{3,1},{4,6},{5,7},{6,4},{7,5},{8,10},{9,11},{10,... | collective-permute-start | bytes 196616 | tf_op jit(solution)/shard_map/ppermute | solution.py:458
  53.7 10.3 %collective-permute-start.14 = (bf16[2,64,768]{2,1,0:T(8,128)(2,1)S(1)}, bf16[2,64,768]{2,1,0:T(8,128)(2,1)S(1)}, u32[]{:S(2)}, u32[]{:S(2)}) collective-permute-start(bf16[2,64,768]{2,1,0:T(8,128)(2,1)S(1)} %pad_maximum_fusion.6), channel_id=1, source_target_pairs={{0,2},{1,3},{2,0},{3,1},{4,6},{5,7},{6,4},{7,5},{8,10},{9,11},{10,... | collective-permute-start | bytes 589832 | tf_op jit(solution)/shard_map/ppermute | solution.py:458
  55.9 1.3 %collective-permute-start.16 = (f32[128,128]{1,0:T(8,128)S(1)}, f32[128,128]{1,0:T(8,128)S(1)}, u32[]{:S(2)}, u32[]{:S(2)}) collective-permute-start(f32[128,128]{1,0:T(8,128)S(1)} %add.110), channel_id=1, source_target_pairs={{0,8},{8,0},{16,24},{24,16},{1,9},{9,1},{17,25},{25,17},{2,10},{10... | collective-permute-start | bytes 196616 | tf_op jit(solution)/shard_map/ppermute | solution.py:458
  57.3 4.3 %collective-permute-start.17 = (f32[128,128]{1,0:T(8,128)S(1)}, f32[128,128]{1,0:T(8,128)S(1)}, u32[]{:S(2)}, u32[]{:S(2)}) collective-permute-start(f32[128,128]{1,0:T(8,128)S(1)} %add.111.refs_1_), channel_id=1, source_target_pairs={{0,16},{8,24},{16,0},{24,8},{1,17},{9,25},{17,1},{25,9},{2,18},{10... | collective-permute-start | bytes 196616 | tf_op jit(solution)/shard_map/ppermute | solution.py:458
  65.8 10.0 %collective-permute-start.19 = (bf16[2,64,768]{2,1,0:T(8,128)(2,1)S(1)}, bf16[2,64,768]{2,1,0:T(8,128)(2,1)S(1)}, u32[]{:S(2)}, u32[]{:S(2)}) collective-permute-start(bf16[2,64,768]{2,1,0:T(8,128)(2,1)S(1)} %get-tuple-element.52), channel_id=1, source_target_pairs={{0,2},{1,3},{2,0},{3,1},{4,6},{5,7},{6,4},{7,5},{8,10},{9,11},{10,... | collective-permute-start | bytes 589832 | tf_op jit(solution)/shard_map/ppermute | solution.py:458
  65.8 12.2 %collective-permute-start.18 = (bf16[2,64,768]{2,1,0:T(8,128)(2,1)S(1)}, bf16[2,64,768]{2,1,0:T(8,128)(2,1)S(1)}, u32[]{:S(2)}, u32[]{:S(2)}) collective-permute-start(bf16[2,64,768]{2,1,0:T(8,128)(2,1)S(1)} %get-tuple-element.52), channel_id=1, source_target_pairs={{4,0},{5,1},{6,2},{7,3},{12,8},{13,9},{14,10},{15,11},{20,16},{21,... | collective-permute-start | bytes 589832 | tf_op jit(solution)/shard_map/ppermute | solution.py:473
  75.9 5.7 %collective-permute-start.21 = (bf16[2,64,768]{2,1,0:T(8,128)(2,1)S(1)}, bf16[2,64,768]{2,1,0:T(8,128)(2,1)S(1)}, u32[]{:S(2)}, u32[]{:S(2)}) collective-permute-start(bf16[2,64,768]{2,1,0:T(8,128)(2,1)S(1)} %pad_maximum_fusion.7), channel_id=1, source_target_pairs={{0,1},{1,0},{2,3},{3,2},{4,5},{5,4},{6,7},{7,6},{8,9},{9,8},{10,11... | collective-permute-start | bytes 589832 | tf_op jit(solution)/shard_map/ppermute | solution.py:458
  76.0 5.7 %collective-permute-start.23 = (bf16[2,64,768]{2,1,0:T(8,128)(2,1)S(1)}, bf16[2,64,768]{2,1,0:T(8,128)(2,1)S(1)}, u32[]{:S(2)}, u32[]{:S(2)}) collective-permute-start(bf16[2,64,768]{2,1,0:T(8,128)(2,1)S(1)} %pad_maximum_fusion.8), channel_id=1, source_target_pairs={{0,16},{8,24},{16,0},{24,8},{1,17},{9,25},{17,1},{25,9},{2,18},{10... | collective-permute-start | bytes 589832 | tf_op jit(solution)/shard_map/ppermute | solution.py:458
  76.7 9.3 %collective-permute-start.20 = (bf16[2,64,768]{2,1,0:T(8,128)(2,1)S(1)}, bf16[2,64,768]{2,1,0:T(8,128)(2,1)S(1)}, u32[]{:S(2)}, u32[]{:S(2)}) collective-permute-start(bf16[2,64,768]{2,1,0:T(8,128)(2,1)S(1)} %collective-permute-done.19), channel_id=1, source_target_pairs={{4,0},{5,1},{6,2},{7,3},{12,8},{13,9},{14,10},{15,11},{20,16},{21,... | collective-permute-start | bytes 589832 | tf_op jit(solution)/shard_map/ppermute | solution.py:473
  81.8 10.9 %collective-permute-start.25 = (bf16[4,64,768]{2,1,0:T(8,128)(2,1)S(1)}, bf16[4,64,768]{2,1,0:T(8,128)(2,1)S(1)}, u32[]{:S(2)}, u32[]{:S(2)}) collective-permute-start(bf16[4,64,768]{2,1,0:T(8,128)(2,1)S(1)} %get-tuple-element.76), channel_id=1, source_target_pairs={{4,0},{5,1},{6,2},{7,3},{12,8},{13,9},{14,10},{15,11},{20,16},{21,... | collective-permute-start | bytes 1179656 | tf_op jit(solution)/shard_map/ppermute | solution.py:473
  83.1 9.6 %collective-permute-start.22 = (bf16[4,64,768]{2,1,0:T(8,128)(2,1)S(1)}, bf16[4,64,768]{2,1,0:T(8,128)(2,1)S(1)}, u32[]{:S(2)}, u32[]{:S(2)}) collective-permute-start(bf16[4,64,768]{2,1,0:T(8,128)(2,1)S(1)} %get-tuple-element.77), channel_id=1, source_target_pairs={{0,16},{8,24},{16,0},{24,8},{1,17},{9,25},{17,1},{25,9},{2,18},{10... | collective-permute-start | bytes 1179656 | tf_op jit(solution)/shard_map/ppermute | solution.py:458
  83.9 8.8 %collective-permute-start.24 = (bf16[4,64,768]{2,1,0:T(8,128)(2,1)S(1)}, bf16[4,64,768]{2,1,0:T(8,128)(2,1)S(1)}, u32[]{:S(2)}, u32[]{:S(2)}) collective-permute-start(bf16[4,64,768]{2,1,0:T(8,128)(2,1)S(1)} %get-tuple-element.78), channel_id=1, source_target_pairs={{0,1},{1,0},{2,3},{3,2},{4,5},{5,4},{6,7},{7,6},{8,9},{9,8},{10,11... | collective-permute-start | bytes 1179656 | tf_op jit(solution)/shard_map/ppermute | solution.py:458
  85.9 16.6 %collective-permute-start.30 = (bf16[8,64,768]{2,1,0:T(8,128)(2,1)S(1)}, bf16[8,64,768]{2,1,0:T(8,128)(2,1)S(1)}, u32[]{:S(2)}, u32[]{:S(2)}) collective-permute-start(bf16[8,64,768]{2,1,0:T(8,128)(2,1)S(1)} %constant_dynamic-update-slice_fusion.3.refs_0_), channel_id=1, source_target_pairs={{0,8},{8,0},{16,24},{24,16},{1,9},{9,1},{17,25},{25,17},{2,10},{10... | collective-permute-start | bytes 2359304 | tf_op jit(solution)/shard_map/ppermute | solution.py:458
  92.8 9.6 %collective-permute-start.28 = (bf16[2,64,768]{2,1,0:T(8,128)(2,1)S(1)}, bf16[2,64,768]{2,1,0:T(8,128)(2,1)S(1)}, u32[]{:S(2)}, u32[]{:S(2)}) collective-permute-start(bf16[2,64,768]{2,1,0:T(8,128)(2,1)S(1)} %pad_maximum_fusion.9), channel_id=1, source_target_pairs={{4,0},{5,1},{6,2},{7,3},{12,8},{13,9},{14,10},{15,11},{20,16},{21,... | collective-permute-start | bytes 589832 | tf_op jit(solution)/shard_map/ppermute | solution.py:473
  94.2 6.8 %collective-permute-start.26 = (bf16[3,64,768]{2,1,0:T(8,128)(2,1)S(1)}, bf16[3,64,768]{2,1,0:T(8,128)(2,1)S(1)}, u32[]{:S(2)}, u32[]{:S(2)}) collective-permute-start(bf16[3,64,768]{2,1,0:T(8,128)(2,1)S(1)} %pad_maximum_fusion.3), channel_id=1, source_target_pairs={{0,16},{8,24},{16,0},{24,8},{1,17},{9,25},{17,1},{25,9},{2,18},{10... | collective-permute-start | bytes 884744 | tf_op jit(solution)/shard_map/ppermute | solution.py:458
  95.6 6.8 %collective-permute-start.27 = (bf16[3,64,768]{2,1,0:T(8,128)(2,1)S(1)}, bf16[3,64,768]{2,1,0:T(8,128)(2,1)S(1)}, u32[]{:S(2)}, u32[]{:S(2)}) collective-permute-start(bf16[3,64,768]{2,1,0:T(8,128)(2,1)S(1)} %pad_maximum_fusion.4), channel_id=1, source_target_pairs={{0,1},{1,0},{2,3},{3,2},{4,5},{5,4},{6,7},{7,6},{8,9},{9,8},{10,11... | collective-permute-start | bytes 884744 | tf_op jit(solution)/shard_map/ppermute | solution.py:458
  97.7 4.8 %collective-permute-start.31 = (bf16[8,64,768]{2,1,0:T(8,128)(2,1)S(1)}, bf16[8,64,768]{2,1,0:T(8,128)(2,1)S(1)}, u32[]{:S(2)}, u32[]{:S(2)}) collective-permute-start(bf16[8,64,768]{2,1,0:T(8,128)(2,1)S(1)} %constant_dynamic-update-slice_fusion.7.refs_2_), channel_id=1, source_target_pairs={{0,8},{8,0},{16,24},{24,16},{1,9},{9,1},{17,25},{25,17},{2,10},{10... | collective-permute-start | bytes 2359304 | tf_op jit(solution)/shard_map/ppermute | solution.py:458
  100.9 2.3 %collective-permute-start.32 = (bf16[8,64,768]{2,1,0:T(8,128)(2,1)S(1)}, bf16[8,64,768]{2,1,0:T(8,128)(2,1)S(1)}, u32[]{:S(2)}, u32[]{:S(2)}) collective-permute-start(bf16[8,64,768]{2,1,0:T(8,128)(2,1)S(1)} %constant_dynamic-update-slice_fusion.9.refs_4_), channel_id=1, source_target_pairs={{0,8},{8,0},{16,24},{24,16},{1,9},{9,1},{17,25},{25,17},{2,10},{10... | collective-permute-start | bytes 2359304 | tf_op jit(solution)/shard_map/ppermute | solution.py:458
  102.4 3.6 %collective-permute-start.29 = (bf16[8,64,768]{2,1,0:T(8,128)(2,1)S(1)}, bf16[8,64,768]{2,1,0:T(8,128)(2,1)S(1)}, u32[]{:S(2)}, u32[]{:S(2)}) collective-permute-start(bf16[8,64,768]{2,1,0:T(8,128)(2,1)S(1)} %constant_dynamic-update-slice_fusion.refs_0_), channel_id=1, source_target_pairs={{0,8},{8,0},{16,24},{24,16},{1,9},{9,1},{17,25},{25,17},{2,10},{10... | collective-permute-start | bytes 2359304 | tf_op jit(solution)/shard_map/ppermute | solution.py:458

commit v7 on v6

--- a/solution.py
+++ b/solution.py
@@ -274,7 +274,7 @@
     both = scale_d * scale_r
     for k in range(1, layers):
         cut = slice((k - 1) * ranks, k * ranks)
-        across = dot_first(own_active, scaled[k], exact) * both
+        across = dot_first(own_active.astype(bf16), scaled[k].astype(bf16)) * both
         mixed_ref[:ranks, cut] = jnp.zeros_like(across)
         mixed_ref[ranks:, cut] = jnp.where(k > section_at, across, 0.0)
     for i in range(layers - 1):
@@ -282,9 +282,9 @@
         after = jnp.zeros_like(square)
         for k in range(i + 1, layers):
             after = after + jnp.where(k > section_at, kappas[k], 0.0)
-        across = dot_first(own_error, actives[i], exact) * both
+        across = dot_first(own_error.astype(bf16), actives[i].astype(bf16)) * both
         mixed_ref[:ranks, cut] = jnp.where(i < section_at, across, 0.0)
-        across = dot_first(own_active, after * actives[i], exact)
+        across = dot_first(own_active.astype(bf16), (after * actives[i]).astype(bf16))
         mixed_ref[ranks:, cut] = across * (-scale_r * scale_r)
 
 
@@ -350,7 +350,7 @@
 def update_kernel(kept, near, downs, ups, *refs):
     last, mixed_ref, other_ref, right_ref = refs[:4]
     state, outs, share_ref = refs[4:10], refs[10:16], refs[16]
-    mixed = mixed_ref[...] + other_ref[...]
+    mixed = mixed_ref[...] + other_ref[...].astype(f32)
     right = right_ref[...].astype(f32)
     small = jnp.dot(mixed, right, preferred_element_type=f32, precision=exact)
     ranks = small.shape[0] // 2
@@ -481,32 +481,30 @@
 
 
 def reduced(factors, hidden, cot, columns, mixed):
-    def halves(lead, factors):
+    def halves(lead):
         sent = gradient(factors, hidden, cot, 1, lead, columns)
         return swapped(sent, "replica", 1), gradient(factors, hidden, cot, 0, lead, columns)
 
-    near, kept = halves(1, factors)
-    mixed = mixed + swapped(mixed, "tensor", 1)
-    down_one = summed(kept[0], near[0])
-    up_one = summed(kept[1], near[1])
-    down_one, up_one, mixed, factors = lax.optimization_barrier(
-        (down_one, up_one, mixed, factors)
-    )
-    down_one = swapped(down_one, "replica", 2)
-    up_one = swapped(up_one, "tensor", 1)
-    near, kept = halves(0, factors)
-
     def part(which, cut, *steps):
         return summed(kept[which, cut], near[which, cut], *steps)
 
-    low = slice(2, 4)
+    def added(axis, distance):
+        return mixed + swapped(mixed.astype(bf16), axis, distance).astype(f32)
+
+    near, kept = halves(1)
+    whole, low = slice(0, 4), slice(2, 4)
+    down_one = swapped(part(0, whole), "replica", 2)
+    up_one = swapped(part(1, whole), "tensor", 1)
+    near, kept = halves(0)
+    mixed = added("replica", 1)
+    mixed = added("tensor", 1)
+    down_one, up_one, mixed = lax.optimization_barrier((down_one, up_one, mixed))
     down_two = swapped(part(0, low, down_one[2:]), "tensor", 1)
     up_two = swapped(part(1, low, up_one[2:]), "replica", 2)
     last = jnp.stack([part(0, 1, down_one[1], down_two[1]), part(1, 1, up_one[1], up_two[1])])
     last = swapped(last, "tensor", 2)
-    for axis, distance in (("tensor", 2), ("replica", 1)):
-        mixed = mixed + swapped(mixed, axis, distance)
-    other = swapped(mixed, "replica", 2)
+    mixed = added("tensor", 2)
+    other = swapped(mixed.astype(bf16), "replica", 2)
     return (kept, near, (down_one, down_two), (up_one, up_two), last, mixed, other)
 
 

time: 109 us -> 106 us (0.972)
  transfers between devices with their start and end apart: 33 -> 33, of which waited for: 18 -> 18; matrix products, arithmetic and copies ran while one was open for 1% -> 1% of each run, Pallas kernels for 10% -> 11%
where the time goes in v7:
time: 106 us
  waiting for transfers between devices  50 us (47%)
  starting transfers between devices  34.3 us (32%)
  Pallas kernels  18.1 us (17%)
  other arithmetic  1.82 us (2%)
  between operations  1.15 us (1%)
    ppermute x27, waiting for transfers between devices, swapped(): return lax.ppermute(block, axis, route)  43.1 us
    ppermute x27, starting transfers between devices, swapped(): return lax.ppermute(block, axis, route)  25.5 us
    ppermute x4, waiting for transfers between devices, following_layer(): return lax.ppermute(block, 'section', [(i + 1, i) for i in range(size - 1)])  6.85 us
    pallas_call x1, Pallas kernels, project(): pl.pallas_call(functools.partial(project_kernel, steps), in_specs=[in_hbm...  5.99 us
    ppermute x4, starting transfers between devices, following_layer(): return lax.ppermute(block, 'section', [(i + 1, i) for i in range(size - 1)])  5.15 us
    pallas_call x2, Pallas kernels, place(): pl.pallas_call(functools.partial(place_kernel, layout, not before), in_sp...  4.47 us
    ppermute x2, starting transfers between devices, from_next(): return lax.ppermute(block, 'section', route)  3.69 us
    pallas_call x1, Pallas kernels, chain(): pl.pallas_call(kernel, in_specs=[in_smem] * 2 + [in_vmem] * len(inputs),...  2.19 us
  transfers between devices with their start and end apart: 33, of which 18 were waited for; matrix products, arithmetic and copies ran while one was open for 1% of the time, Pallas kernels for 11%

profile of v7, /device:TPU:0, one launch (start us, length us, event | category | flops | bytes accessed | tf_op | source)
XLA Modules:
  0.0 105.7 jit_solution(5270862704921735644)
XLA Ops:
  0.6 1.0 convert_bitcast_fusion
  1.7 3.0 %collective-permute-start = (bf16[128,768]{1,0:T(8,128)(2,1)S(1)}, bf16[128,768]{1,0:T(8,128)(2,1)S(1)}, u32[]{:S(2)}, u32[]{:S(2)}) collective-permute-start(bf16[128,768]{1,0:T(8,128)(2,1)S(1)} %pad_maximum_fusion.5.refs_0_), channel_id=1, source_target_pairs={{4,0},{0,4},{5,1},{1,5},{6,2},{2,6},{7,3},{3,7},{12,8},{8,12},{13,... | collective-permute-start | bytes 589832 | tf_op jit(solution)/shard_map/ppermute | solution.py:468
  4.7 6.0 %project.1 = (f32[128,256]{1,0:T(8,128)S(1)}, f32[128,128]{1,0:T(8,128)S(1)}, bf16[128,12288]{1,0:T(8,128)(2,1)S(1)}, bf16[128,12288]{1,0:T(8,128)(2,1)S(1)}) custom-call(bf16[128,12288]{1,0:T(8,128)(2,1)} %bitcast.41, bf16[2,64,12288]{2,1,0:T(8,128)(2,1)} %bitcast.42, bf16[2,64,12288]{2,1,0:T(8,128)(2,1)} %bitcast.43), custom_call_target="tpu_custom_call" | custom-call | flops 805306368 | bytes 9437184 | tf_op jit(solution)/shard_map/project/pallas_call | solution.py:98
  10.9 0.7 collective-permute-start.4
  11.7 0.9 collective-permute-start.3
  12.8 1.5 %project_back.1.refs_0_ = f32[128,384]{1,0:T(8,128)S(1)} custom-call(s32[4]{0:T(128)S(1)} %copy-done.8, f32[128,256]{1,0:T(8,128)S(1)} %get-tuple-element.36.by_hidden, bf16[128,12288]{1,0:T(8,128)(2,1)S(1)} %bitcast.34, bf16[128,12288]{1,0:T(8,128)(2,1)S(1)} %get-tuple-element.40.up_ref), custom_call_target="tpu_custom_call" | custom-call | flops 402653184 | bytes 6291456 | tf_op jit(solution)/shard_map/project_back/pallas_call | solution.py:133
  14.4 0.7 collective-permute-start.1
  15.1 0.8 collective-permute-done.3
  15.9 1.6 %collective-permute-start.5 = (f32[64,128]{1,0:T(8,128)S(1)}, f32[64,128]{1,0:T(8,128)S(1)}, u32[]{:S(2)}, u32[]{:S(2)}) collective-permute-start(f32[64,128]{1,0:T(8,128)S(1)} %add_add_fusion), channel_id=1, source_target_pairs={{0,1},{1,0},{2,3},{3,2},{4,5},{5,4},{6,7},{7,6},{8,9},{9,8},{10,11... | collective-permute-start | bytes 98312 | tf_op jit(solution)/shard_map/ppermute | solution.py:458
  17.6 2.3 %collective-permute-done.5 = f32[64,128]{1,0:T(8,128)S(1)} collective-permute-done((f32[64,128]{1,0:T(8,128)S(1)}, f32[64,128]{1,0:T(8,128)S(1)}, u32[]{:S(2)}, u32[]{:S(2)}) %collective-permute-start.5) | collective-permute-done | bytes 32800 | tf_op jit(solution)/shard_map/ppermute | solution.py:458
  19.9 2.6 %collective-permute-start.6 = (f32[64,128]{1,0:T(8,128)S(1)}, f32[64,128]{1,0:T(8,128)S(1)}, u32[]{:S(2)}, u32[]{:S(2)}) collective-permute-start(f32[64,128]{1,0:T(8,128)S(1)} %add.92.refs_2_), channel_id=1, source_target_pairs={{0,2},{1,3},{2,0},{3,1},{4,6},{5,7},{6,4},{7,5},{8,10},{9,11},{10,... | collective-permute-start | bytes 98312 | tf_op jit(solution)/shard_map/ppermute | solution.py:458
  22.5 2.2 %collective-permute-done.6.refs_3_ = f32[64,128]{1,0:T(8,128)S(1)} collective-permute-done((f32[64,128]{1,0:T(8,128)S(1)}, f32[64,128]{1,0:T(8,128)S(1)}, u32[]{:S(2)}, u32[]{:S(2)}) %collective-permute-start.6) | collective-permute-done | bytes 32800 | tf_op jit(solution)/shard_map/ppermute | solution.py:458
  24.7 2.2 %chain.1 = (bf16[128,256]{1,0:T(8,128)(2,1)S(1)}, f32[128,128]{1,0:T(8,128)S(1)}) custom-call(s32[4,3]{1,0:T(4,128)S(1)} %copy-done.7, s32[4]{0:T(128)S(1)} %copy-done.8, f32[128,384]{1,0:T(8,128)S(1)} %project_back.1.refs_0_, f32[128,384]{1,0:T(8,128)S(1)} %collective-permute-done.1.refs_1_, f32[64,128]{1,0:T(8,128)S(1)} %add.92.refs_2_, ...), custom_call_target="tpu_custom_call" | custom-call | tf_op jit(solution)/shard_map/chain/pallas_call | solution.py:297
  28.0 0.5 collective-permute-start.7
  29.2 0.6 collective-permute-done.8
  30.0 1.6 %collective-permute-start.10 = (bf16[4,64,768]{2,1,0:T(8,128)(2,1)S(1)}, bf16[4,64,768]{2,1,0:T(8,128)(2,1)S(1)}, u32[]{:S(2)}, u32[]{:S(2)}) collective-permute-start(bf16[4,64,768]{2,1,0:T(8,128)(2,1)S(1)} %get-tuple-element.68), channel_id=1, source_target_pairs={{0,1},{1,0},{2,3},{3,2},{4,5},{5,4},{6,7},{7,6},{8,9},{9,8},{10,11... | collective-permute-start | bytes 1179656 | tf_op jit(solution)/shard_map/ppermute | solution.py:458
  31.6 0.7 collective-permute-start.9
  32.4 0.5 collective-permute-start.12
  33.4 8.5 %collective-permute-done.12 = bf16[128,128]{1,0:T(8,128)(2,1)S(1)} collective-permute-done((bf16[128,128]{1,0:T(8,128)(2,1)S(1)}, bf16[128,128]{1,0:T(8,128)(2,1)S(1)}, u32[]{:S(2)}, u32[]{:S(2)}) %collective-permute-start.12) | collective-permute-done | bytes 32800 | tf_op jit(solution)/shard_map/ppermute | solution.py:458
  41.9 0.6 collective-permute-done.9.down_one
  42.6 0.8 collective-permute-start.14
  43.4 1.0 collective-permute-start.13
  44.5 2.8 %collective-permute-start.16 = (bf16[128,128]{1,0:T(8,128)(2,1)S(1)}, bf16[128,128]{1,0:T(8,128)(2,1)S(1)}, u32[]{:S(2)}, u32[]{:S(2)}) collective-permute-start(bf16[128,128]{1,0:T(8,128)(2,1)S(1)} %convert_element_type.176), channel_id=1, source_target_pairs={{0,2},{1,3},{2,0},{3,1},{4,6},{5,7},{6,4},{7,5},{8,10},{9,11},{10,... | collective-permute-start | bytes 98312 | tf_op jit(solution)/shard_map/ppermute | solution.py:458
  47.3 1.2 %collective-permute-done.14.up_two = bf16[2,64,768]{2,1,0:T(8,128)(2,1)S(1)} collective-permute-done((bf16[2,64,768]{2,1,0:T(8,128)(2,1)S(1)}, bf16[2,64,768]{2,1,0:T(8,128)(2,1)S(1)}, u32[]{:S(2)}, u32[]{:S(2)}) %collective-permute-start.14) | collective-permute-done | bytes 196640 | tf_op jit(solution)/shard_map/ppermute | solution.py:458
  48.5 1.2 %collective-permute-done.13.down_two = bf16[2,64,768]{2,1,0:T(8,128)(2,1)S(1)} collective-permute-done((bf16[2,64,768]{2,1,0:T(8,128)(2,1)S(1)}, bf16[2,64,768]{2,1,0:T(8,128)(2,1)S(1)}, u32[]{:S(2)}, u32[]{:S(2)}) %collective-permute-start.13) | collective-permute-done | bytes 196640 | tf_op jit(solution)/shard_map/ppermute | solution.py:458
  49.8 2.5 %collective-permute-start.15 = (bf16[2,64,768]{2,1,0:T(8,128)(2,1)S(1)}, bf16[2,64,768]{2,1,0:T(8,128)(2,1)S(1)}, u32[]{:S(2)}, u32[]{:S(2)}) collective-permute-start(bf16[2,64,768]{2,1,0:T(8,128)(2,1)S(1)} %pad_maximum_fusion.6), channel_id=1, source_target_pairs={{0,2},{1,3},{2,0},{3,1},{4,6},{5,7},{6,4},{7,5},{8,10},{9,11},{10,... | collective-permute-start | bytes 589832 | tf_op jit(solution)/shard_map/ppermute | solution.py:458
  52.3 1.4 %collective-permute-start.17 = (bf16[128,128]{1,0:T(8,128)(2,1)S(1)}, bf16[128,128]{1,0:T(8,128)(2,1)S(1)}, u32[]{:S(2)}, u32[]{:S(2)}) collective-permute-start(bf16[128,128]{1,0:T(8,128)(2,1)S(1)} %get-tuple-element.62), channel_id=1, source_target_pairs={{0,16},{8,24},{16,0},{24,8},{1,17},{9,25},{17,1},{25,9},{2,18},{10... | collective-permute-start | bytes 98312 | tf_op jit(solution)/shard_map/ppermute | solution.py:458
  53.7 2.6 %collective-permute-done.17.refs_2_ = bf16[128,128]{1,0:T(8,128)(2,1)S(1)} collective-permute-done((bf16[128,128]{1,0:T(8,128)(2,1)S(1)}, bf16[128,128]{1,0:T(8,128)(2,1)S(1)}, u32[]{:S(2)}, u32[]{:S(2)}) %collective-permute-start.17) | collective-permute-done | bytes 32800 | tf_op jit(solution)/shard_map/ppermute | solution.py:458
  56.3 3.3 %collective-permute-done.15.refs_0_ = bf16[2,64,768]{2,1,0:T(8,128)(2,1)S(1)} collective-permute-done((bf16[2,64,768]{2,1,0:T(8,128)(2,1)S(1)}, bf16[2,64,768]{2,1,0:T(8,128)(2,1)S(1)}, u32[]{:S(2)}, u32[]{:S(2)}) %collective-permute-start.15) | collective-permute-done | bytes 196640 | tf_op jit(solution)/shard_map/ppermute | solution.py:458
  59.6 1.8 %update.1 = (f32[1,64,768]{2,1,0:T(8,128)}, f32[1,64,768]{2,1,0:T(8,128)}, f32[1,64,768]{2,1,0:T(8,128)}, f32[1,64,768]{2,1,0:T(8,128)}, f32[1,64,768]{2,1,0:T(8...) custom-call(bf16[2,4,64,768]{3,2,1,0:T(8,128)(2,1)S(1)} %gradient.4.kept, ...), custom_call_target="tpu_custom_call" | custom-call | tf_op jit(solution)/shard_map/update/pallas_call | solution.py:379
  61.4 1.3 %collective-permute-start.18 = (bf16[2,64,768]{2,1,0:T(8,128)(2,1)S(1)}, bf16[2,64,768]{2,1,0:T(8,128)(2,1)S(1)}, u32[]{:S(2)}, u32[]{:S(2)}) collective-permute-start(bf16[2,64,768]{2,1,0:T(8,128)(2,1)S(1)} %get-tuple-element.50), channel_id=1, source_target_pairs={{4,0},{5,1},{6,2},{7,3},{12,8},{13,9},{14,10},{15,11},{20,16},{21,... | collective-permute-start | bytes 589832 | tf_op jit(solution)/shard_map/ppermute | solution.py:473
  62.8 9.4 %collective-permute-done.19 = bf16[2,64,768]{2,1,0:T(8,128)(2,1)S(1)} collective-permute-done((bf16[2,64,768]{2,1,0:T(8,128)(2,1)S(1)}, bf16[2,64,768]{2,1,0:T(8,128)(2,1)S(1)}, u32[]{:S(2)}, u32[]{:S(2)}) %collective-permute-start.19) | collective-permute-done | bytes 196640 | tf_op jit(solution)/shard_map/ppermute | solution.py:458
  72.3 1.4 %collective-permute-start.23 = (bf16[2,64,768]{2,1,0:T(8,128)(2,1)S(1)}, bf16[2,64,768]{2,1,0:T(8,128)(2,1)S(1)}, u32[]{:S(2)}, u32[]{:S(2)}) collective-permute-start(bf16[2,64,768]{2,1,0:T(8,128)(2,1)S(1)} %pad_maximum_fusion.8), channel_id=1, source_target_pairs={{0,16},{8,24},{16,0},{24,8},{1,17},{9,25},{17,1},{25,9},{2,18},{10... | collective-permute-start | bytes 589832 | tf_op jit(solution)/shard_map/ppermute | solution.py:458
  73.7 1.3 %collective-permute-start.20 = (bf16[2,64,768]{2,1,0:T(8,128)(2,1)S(1)}, bf16[2,64,768]{2,1,0:T(8,128)(2,1)S(1)}, u32[]{:S(2)}, u32[]{:S(2)}) collective-permute-start(bf16[2,64,768]{2,1,0:T(8,128)(2,1)S(1)} %collective-permute-done.19), channel_id=1, source_target_pairs={{4,0},{5,1},{6,2},{7,3},{12,8},{13,9},{14,10},{15,11},{20,16},{21,... | collective-permute-start | bytes 589832 | tf_op jit(solution)/shard_map/ppermute | solution.py:473
  75.1 3.5 %collective-permute-done.21 = bf16[2,64,768]{2,1,0:T(8,128)(2,1)S(1)} collective-permute-done((bf16[2,64,768]{2,1,0:T(8,128)(2,1)S(1)}, bf16[2,64,768]{2,1,0:T(8,128)(2,1)S(1)}, u32[]{:S(2)}, u32[]{:S(2)}) %collective-permute-start.21) | collective-permute-done | bytes 196640 | tf_op jit(solution)/shard_map/ppermute | solution.py:458
  78.8 1.3 %collective-permute-start.25 = (bf16[4,64,768]{2,1,0:T(8,128)(2,1)S(1)}, bf16[4,64,768]{2,1,0:T(8,128)(2,1)S(1)}, u32[]{:S(2)}, u32[]{:S(2)}) collective-permute-start(bf16[4,64,768]{2,1,0:T(8,128)(2,1)S(1)} %get-tuple-element.76), channel_id=1, source_target_pairs={{4,0},{5,1},{6,2},{7,3},{12,8},{13,9},{14,10},{15,11},{20,16},{21,... | collective-permute-start | bytes 1179656 | tf_op jit(solution)/shard_map/ppermute | solution.py:473
  80.1 1.4 %collective-permute-start.22 = (bf16[4,64,768]{2,1,0:T(8,128)(2,1)S(1)}, bf16[4,64,768]{2,1,0:T(8,128)(2,1)S(1)}, u32[]{:S(2)}, u32[]{:S(2)}) collective-permute-start(bf16[4,64,768]{2,1,0:T(8,128)(2,1)S(1)} %get-tuple-element.77), channel_id=1, source_target_pairs={{0,16},{8,24},{16,0},{24,8},{1,17},{9,25},{17,1},{25,9},{2,18},{10... | collective-permute-start | bytes 1179656 | tf_op jit(solution)/shard_map/ppermute | solution.py:458
  81.5 1.7 %collective-permute-start.24 = (bf16[4,64,768]{2,1,0:T(8,128)(2,1)S(1)}, bf16[4,64,768]{2,1,0:T(8,128)(2,1)S(1)}, u32[]{:S(2)}, u32[]{:S(2)}) collective-permute-start(bf16[4,64,768]{2,1,0:T(8,128)(2,1)S(1)} %get-tuple-element.78), channel_id=1, source_target_pairs={{0,1},{1,0},{2,3},{3,2},{4,5},{5,4},{6,7},{7,6},{8,9},{9,8},{10,11... | collective-permute-start | bytes 1179656 | tf_op jit(solution)/shard_map/ppermute | solution.py:458
  83.4 6.8 %collective-permute-done.25 = bf16[4,64,768]{2,1,0:T(8,128)(2,1)S(1)} collective-permute-done((bf16[4,64,768]{2,1,0:T(8,128)(2,1)S(1)}, bf16[4,64,768]{2,1,0:T(8,128)(2,1)S(1)}, u32[]{:S(2)}, u32[]{:S(2)}) %collective-permute-start.25) | collective-permute-done | bytes 393248 | tf_op jit(solution)/shard_map/ppermute | solution.py:473
  90.2 0.5 collective-permute-done.24
  90.8 1.3 %collective-permute-start.28 = (bf16[2,64,768]{2,1,0:T(8,128)(2,1)S(1)}, bf16[2,64,768]{2,1,0:T(8,128)(2,1)S(1)}, u32[]{:S(2)}, u32[]{:S(2)}) collective-permute-start(bf16[2,64,768]{2,1,0:T(8,128)(2,1)S(1)} %pad_maximum_fusion.9), channel_id=1, source_target_pairs={{4,0},{5,1},{6,2},{7,3},{12,8},{13,9},{14,10},{15,11},{20,16},{21,... | collective-permute-start | bytes 589832 | tf_op jit(solution)/shard_map/ppermute | solution.py:473
  92.2 0.9 collective-permute-start.26
  93.1 1.5 %collective-permute-start.27 = (bf16[3,64,768]{2,1,0:T(8,128)(2,1)S(1)}, bf16[3,64,768]{2,1,0:T(8,128)(2,1)S(1)}, u32[]{:S(2)}, u32[]{:S(2)}) collective-permute-start(bf16[3,64,768]{2,1,0:T(8,128)(2,1)S(1)} %pad_maximum_fusion.4), channel_id=1, source_target_pairs={{0,1},{1,0},{2,3},{3,2},{4,5},{5,4},{6,7},{7,6},{8,9},{9,8},{10,11... | collective-permute-start | bytes 884744 | tf_op jit(solution)/shard_map/ppermute | solution.py:458
  94.8 4.2 %collective-permute-done.26 = bf16[3,64,768]{2,1,0:T(8,128)(2,1)S(1)} collective-permute-done((bf16[3,64,768]{2,1,0:T(8,128)(2,1)S(1)}, bf16[3,64,768]{2,1,0:T(8,128)(2,1)S(1)}, u32[]{:S(2)}, u32[]{:S(2)}) %collective-permute-start.26) | collective-permute-done | bytes 294944 | tf_op jit(solution)/shard_map/ppermute | solution.py:458
  99.0 0.9 collective-permute-done.27
  100.0 1.2 %collective-permute-done.32.refs_5_ = bf16[8,64,768]{2,1,0:T(8,128)(2,1)S(1)} collective-permute-done((bf16[8,64,768]{2,1,0:T(8,128)(2,1)S(1)}, bf16[8,64,768]{2,1,0:T(8,128)(2,1)S(1)}, u32[]{:S(2)}, u32[]{:S(2)}) %collective-permute-start.32) | collective-permute-done | bytes 786464 | tf_op jit(solution)/shard_map/ppermute | solution.py:458
  101.2 2.7 %place.2 = (bf16[2,64,12288]{2,1,0:T(8,128)(2,1)}, bf16[2,64,12288]{2,1,0:T(8,128)(2,1)}) custom-call(s32[4,3]{1,0:T(4,128)S(1)} %copy-done.7, bf16[8,64,768]{2,1,0:T(8,128)(2,1)S(1)} %constant_dynamic-update-slice_fusion.3.refs_0_, bf16[8,64,768]{2,1,0:T(8,128)(2,1)S(1)} %collective-permute-done.30.refs_1_, ...), custom_call_target="tpu_custom_call" | custom-call | bytes 9437184 | tf_op jit(solution)/shard_map/place/pallas_call | solution.py:439
  104.0 1.7 %place.3 = (bf16[2,64,12288]{2,1,0:T(8,128)(2,1)}, bf16[2,64,12288]{2,1,0:T(8,128)(2,1)}) custom-call(s32[4,3]{1,0:T(4,128)S(1)} %copy-done.7, bf16[8,64,768]{2,1,0:T(8,128)(2,1)S(1)} %constant_dynamic-update-slice_fusion.refs_0_, bf16[8,64,768]{2,1,0:T(8,128)(2,1)S(1)} %collective-permute-done.29.refs_1_, ...), custom_call_target="tpu_custom_call", output_to_operand_aliasing={{0}: (3, {}), {1}: (4, {})} | custom-call | bytes 3145728 | tf_op jit(solution)/shard_map/place/pallas_call | solution.py:439
  (85 shorter events, 4.2 us)
Async XLA Ops:
  1.7 9.0 %collective-permute-start = (bf16[128,768]{1,0:T(8,128)(2,1)S(1)}, bf16[128,768]{1,0:T(8,128)(2,1)S(1)}, u32[]{:S(2)}, u32[]{:S(2)}) collective-permute-start(bf16[128,768]{1,0:T(8,128)(2,1)S(1)} %pad_maximum_fusion.5.refs_0_), channel_id=1, source_target_pairs={{4,0},{0,4},{5,1},{1,5},{6,2},{2,6},{7,3},{3,7},{12,8},{8,12},{13,... | collective-permute-start | bytes 589832 | tf_op jit(solution)/shard_map/ppermute | solution.py:468
  4.7 8.1 %copy-start = (bf16[1,4,32,12288]{3,2,1,0:T(8,128)(2,1)S(1)}, bf16[1,4,32,12288]{3,2,1,0:T(8,128)(2,1)}, u32[]{:S(2)}) copy-start(bf16[1,4,32,12288]{3,2,1,0:T(8,128)(2,1)} %param.13) | copy-start | bytes 9437188
  4.7 8.1 %copy-start.8 = (s32[4]{0:T(128)S(1)}, s32[4]{0:T(128)}, u32[]{:S(2)}) copy-start(s32[4]{0:T(128)} %counts.3) | copy-start | bytes 52
  10.9 4.1 %collective-permute-start.4 = (f32[64,128]{1,0:T(8,128)S(1)}, f32[64,128]{1,0:T(8,128)S(1)}, u32[]{:S(2)}, u32[]{:S(2)}) collective-permute-start(f32[64,128]{1,0:T(8,128)S(1)} %get-tuple-element.41), channel_id=1, source_target_pairs={{0,24},{8,16},{16,8},{24,0},{1,25},{9,17},{17,9},{25,1},{2,26},{10... | collective-permute-start | bytes 98312 | tf_op jit(solution)/shard_map/ppermute | solution.py:458
  11.7 4.2 %collective-permute-start.3 = (f32[64,128]{1,0:T(8,128)S(1)}, f32[64,128]{1,0:T(8,128)S(1)}, u32[]{:S(2)}, u32[]{:S(2)}) collective-permute-start(f32[64,128]{1,0:T(8,128)S(1)} %get-tuple-element.41), channel_id=1, source_target_pairs={{0,16},{8,24},{16,0},{24,8},{1,17},{9,25},{17,1},{25,9},{2,18},{10... | collective-permute-start | bytes 98312 | tf_op jit(solution)/shard_map/ppermute | solution.py:458
  12.6 3.3 %collective-permute-start.2 = (f32[64,128]{1,0:T(8,128)S(1)}, f32[64,128]{1,0:T(8,128)S(1)}, u32[]{:S(2)}, u32[]{:S(2)}) collective-permute-start(f32[64,128]{1,0:T(8,128)S(1)} %get-tuple-element.41), channel_id=1, source_target_pairs={{0,8},{8,0},{16,24},{24,16},{1,9},{9,1},{17,25},{25,17},{2,10},{10... | collective-permute-start | bytes 98312 | tf_op jit(solution)/shard_map/ppermute | solution.py:458
  12.8 11.9 %copy-start.7 = (s32[4,3]{1,0:T(4,128)S(1)}, s32[4,3]{1,0:T(4,128)}, u32[]{:S(2)}) copy-start(s32[4,3]{1,0:T(4,128)} %bounds.5) | copy-start | bytes 148
  14.4 10.4 %collective-permute-start.1 = (f32[128,384]{1,0:T(8,128)S(1)}, f32[128,384]{1,0:T(8,128)S(1)}, u32[]{:S(2)}, u32[]{:S(2)}) collective-permute-start(f32[128,384]{1,0:T(8,128)S(1)} %project_back.1.refs_0_), channel_id=1, source_target_pairs={{4,0},{0,4},{5,1},{1,5},{6,2},{2,6},{7,3},{3,7},{12,8},{8,12},{13,... | collective-permute-start | bytes 589832 | tf_op jit(solution)/shard_map/ppermute | solution.py:468
  15.9 4.0 %collective-permute-start.5 = (f32[64,128]{1,0:T(8,128)S(1)}, f32[64,128]{1,0:T(8,128)S(1)}, u32[]{:S(2)}, u32[]{:S(2)}) collective-permute-start(f32[64,128]{1,0:T(8,128)S(1)} %add_add_fusion), channel_id=1, source_target_pairs={{0,1},{1,0},{2,3},{3,2},{4,5},{5,4},{6,7},{7,6},{8,9},{9,8},{10,11... | collective-permute-start | bytes 98312 | tf_op jit(solution)/shard_map/ppermute | solution.py:458
  19.9 4.8 %collective-permute-start.6 = (f32[64,128]{1,0:T(8,128)S(1)}, f32[64,128]{1,0:T(8,128)S(1)}, u32[]{:S(2)}, u32[]{:S(2)}) collective-permute-start(f32[64,128]{1,0:T(8,128)S(1)} %add.92.refs_2_), channel_id=1, source_target_pairs={{0,2},{1,3},{2,0},{3,1},{4,6},{5,7},{6,4},{7,5},{8,10},{9,11},{10,... | collective-permute-start | bytes 98312 | tf_op jit(solution)/shard_map/ppermute | solution.py:458
  27.4 2.4 %collective-permute-start.8 = (bf16[2,4,64,768]{3,2,1,0:T(8,128)(2,1)S(1)}, bf16[2,4,64,768]{3,2,1,0:T(8,128)(2,1)S(1)}, u32[]{:S(2)}, u32[]{:S(2)}) collective-permute-start(bf16[2,4,64,768]{3,2,1,0:T(8,128)(2,1)S(1)} %gradient.7), channel_id=1, source_target_pairs={{0,8},{8,0},{16,24},{24,16},{1,9},{9,1},{17,25},{25,17},{2,10},{10... | collective-permute-start | bytes 2359304 | tf_op jit(solution)/shard_map/ppermute | solution.py:458
  28.0 14.5 %collective-permute-start.7 = (bf16[2,4,64,768]{3,2,1,0:T(8,128)(2,1)S(1)}, bf16[2,4,64,768]{3,2,1,0:T(8,128)(2,1)S(1)}, u32[]{:S(2)}, u32[]{:S(2)}) collective-permute-start(bf16[2,4,64,768]{3,2,1,0:T(8,128)(2,1)S(1)} %gradient.5), channel_id=1, source_target_pairs={{0,8},{8,0},{16,24},{24,16},{1,9},{9,1},{17,25},{25,17},{2,10},{10... | collective-permute-start | bytes 2359304 | tf_op jit(solution)/shard_map/ppermute | solution.py:458
  28.6 3.8 %collective-permute-start.11 = (bf16[128,128]{1,0:T(8,128)(2,1)S(1)}, bf16[128,128]{1,0:T(8,128)(2,1)S(1)}, u32[]{:S(2)}, u32[]{:S(2)}) collective-permute-start(bf16[128,128]{1,0:T(8,128)(2,1)S(1)} %convert_element_type.154), channel_id=1, source_target_pairs={{0,8},{8,0},{16,24},{24,16},{1,9},{9,1},{17,25},{25,17},{2,10},{10... | collective-permute-start | bytes 98312 | tf_op jit(solution)/shard_map/ppermute | solution.py:458
  30.0 11.9 %collective-permute-start.10 = (bf16[4,64,768]{2,1,0:T(8,128)(2,1)S(1)}, bf16[4,64,768]{2,1,0:T(8,128)(2,1)S(1)}, u32[]{:S(2)}, u32[]{:S(2)}) collective-permute-start(bf16[4,64,768]{2,1,0:T(8,128)(2,1)S(1)} %get-tuple-element.68), channel_id=1, source_target_pairs={{0,1},{1,0},{2,3},{3,2},{4,5},{5,4},{6,7},{7,6},{8,9},{9,8},{10,11... | collective-permute-start | bytes 1179656 | tf_op jit(solution)/shard_map/ppermute | solution.py:458
  31.6 10.9 %collective-permute-start.9 = (bf16[4,64,768]{2,1,0:T(8,128)(2,1)S(1)}, bf16[4,64,768]{2,1,0:T(8,128)(2,1)S(1)}, u32[]{:S(2)}, u32[]{:S(2)}) collective-permute-start(bf16[4,64,768]{2,1,0:T(8,128)(2,1)S(1)} %get-tuple-element.69), channel_id=1, source_target_pairs={{0,16},{8,24},{16,0},{24,8},{1,17},{9,25},{17,1},{25,9},{2,18},{10... | collective-permute-start | bytes 1179656 | tf_op jit(solution)/shard_map/ppermute | solution.py:458
  32.4 9.5 %collective-permute-start.12 = (bf16[128,128]{1,0:T(8,128)(2,1)S(1)}, bf16[128,128]{1,0:T(8,128)(2,1)S(1)}, u32[]{:S(2)}, u32[]{:S(2)}) collective-permute-start(bf16[128,128]{1,0:T(8,128)(2,1)S(1)} %fusion.8), channel_id=1, source_target_pairs={{0,1},{1,0},{2,3},{3,2},{4,5},{5,4},{6,7},{7,6},{8,9},{9,8},{10,11... | collective-permute-start | bytes 98312 | tf_op jit(solution)/shard_map/ppermute | solution.py:458
  33.4 26.2 %copy-start.1 = (f32[1,64,768]{2,1,0:T(8,128)S(1)}, f32[1,64,768]{2,1,0:T(8,128)}, u32[]{:S(2)}) copy-start(f32[1,64,768]{2,1,0:T(8,128)} %refs_5_.1) | copy-start | bytes 589828
  33.4 26.2 %copy-start.2 = (f32[1,64,768]{2,1,0:T(8,128)S(1)}, f32[1,64,768]{2,1,0:T(8,128)}, u32[]{:S(2)}) copy-start(f32[1,64,768]{2,1,0:T(8,128)} %refs_4_.1) | copy-start | bytes 589828
  33.4 26.2 %copy-start.3 = (f32[1,64,768]{2,1,0:T(8,128)S(1)}, f32[1,64,768]{2,1,0:T(8,128)}, u32[]{:S(2)}) copy-start(f32[1,64,768]{2,1,0:T(8,128)} %refs_6_.1) | copy-start | bytes 589828
  33.4 26.2 %copy-start.4 = (f32[1,64,768]{2,1,0:T(8,128)S(1)}, f32[1,64,768]{2,1,0:T(8,128)}, u32[]{:S(2)}) copy-start(f32[1,64,768]{2,1,0:T(8,128)} %refs_7_.1) | copy-start | bytes 589828
  33.4 26.2 %copy-start.5 = (f32[1,64,768]{2,1,0:T(8,128)S(1)}, f32[1,64,768]{2,1,0:T(8,128)}, u32[]{:S(2)}) copy-start(f32[1,64,768]{2,1,0:T(8,128)} %refs_8_.1) | copy-start | bytes 589828
  33.4 26.2 %copy-start.6 = (f32[1,64,768]{2,1,0:T(8,128)S(1)}, f32[1,64,768]{2,1,0:T(8,128)}, u32[]{:S(2)}) copy-start(f32[1,64,768]{2,1,0:T(8,128)} %refs_9_.1) | copy-start | bytes 589828
  42.6 5.9 %collective-permute-start.14 = (bf16[2,64,768]{2,1,0:T(8,128)(2,1)S(1)}, bf16[2,64,768]{2,1,0:T(8,128)(2,1)S(1)}, u32[]{:S(2)}, u32[]{:S(2)}) collective-permute-start(bf16[2,64,768]{2,1,0:T(8,128)(2,1)S(1)} %get-tuple-element.66), channel_id=1, source_target_pairs={{0,16},{8,24},{16,0},{24,8},{1,17},{9,25},{17,1},{25,9},{2,18},{10... | collective-permute-start | bytes 589832 | tf_op jit(solution)/shard_map/ppermute | solution.py:458
  43.4 6.3 %collective-permute-start.13 = (bf16[2,64,768]{2,1,0:T(8,128)(2,1)S(1)}, bf16[2,64,768]{2,1,0:T(8,128)(2,1)S(1)}, u32[]{:S(2)}, u32[]{:S(2)}) collective-permute-start(bf16[2,64,768]{2,1,0:T(8,128)(2,1)S(1)} %get-tuple-element.67), channel_id=1, source_target_pairs={{0,1},{1,0},{2,3},{3,2},{4,5},{5,4},{6,7},{7,6},{8,9},{9,8},{10,11... | collective-permute-start | bytes 589832 | tf_op jit(solution)/shard_map/ppermute | solution.py:458
  44.5 7.8 %collective-permute-start.16 = (bf16[128,128]{1,0:T(8,128)(2,1)S(1)}, bf16[128,128]{1,0:T(8,128)(2,1)S(1)}, u32[]{:S(2)}, u32[]{:S(2)}) collective-permute-start(bf16[128,128]{1,0:T(8,128)(2,1)S(1)} %convert_element_type.176), channel_id=1, source_target_pairs={{0,2},{1,3},{2,0},{3,1},{4,6},{5,7},{6,4},{7,5},{8,10},{9,11},{10,... | collective-permute-start | bytes 98312 | tf_op jit(solution)/shard_map/ppermute | solution.py:458
  49.8 9.8 %collective-permute-start.15 = (bf16[2,64,768]{2,1,0:T(8,128)(2,1)S(1)}, bf16[2,64,768]{2,1,0:T(8,128)(2,1)S(1)}, u32[]{:S(2)}, u32[]{:S(2)}) collective-permute-start(bf16[2,64,768]{2,1,0:T(8,128)(2,1)S(1)} %pad_maximum_fusion.6), channel_id=1, source_target_pairs={{0,2},{1,3},{2,0},{3,1},{4,6},{5,7},{6,4},{7,5},{8,10},{9,11},{10,... | collective-permute-start | bytes 589832 | tf_op jit(solution)/shard_map/ppermute | solution.py:458
  52.3 4.0 %collective-permute-start.17 = (bf16[128,128]{1,0:T(8,128)(2,1)S(1)}, bf16[128,128]{1,0:T(8,128)(2,1)S(1)}, u32[]{:S(2)}, u32[]{:S(2)}) collective-permute-start(bf16[128,128]{1,0:T(8,128)(2,1)S(1)} %get-tuple-element.62), channel_id=1, source_target_pairs={{0,16},{8,24},{16,0},{24,8},{1,17},{9,25},{17,1},{25,9},{2,18},{10... | collective-permute-start | bytes 98312 | tf_op jit(solution)/shard_map/ppermute | solution.py:458
  61.4 10.7 %collective-permute-start.19 = (bf16[2,64,768]{2,1,0:T(8,128)(2,1)S(1)}, bf16[2,64,768]{2,1,0:T(8,128)(2,1)S(1)}, u32[]{:S(2)}, u32[]{:S(2)}) collective-permute-start(bf16[2,64,768]{2,1,0:T(8,128)(2,1)S(1)} %get-tuple-element.50), channel_id=1, source_target_pairs={{0,2},{1,3},{2,0},{3,1},{4,6},{5,7},{6,4},{7,5},{8,10},{9,11},{10,... | collective-permute-start | bytes 589832 | tf_op jit(solution)/shard_map/ppermute | solution.py:458
  61.4 13.6 %collective-permute-start.18 = (bf16[2,64,768]{2,1,0:T(8,128)(2,1)S(1)}, bf16[2,64,768]{2,1,0:T(8,128)(2,1)S(1)}, u32[]{:S(2)}, u32[]{:S(2)}) collective-permute-start(bf16[2,64,768]{2,1,0:T(8,128)(2,1)S(1)} %get-tuple-element.50), channel_id=1, source_target_pairs={{4,0},{5,1},{6,2},{7,3},{12,8},{13,9},{14,10},{15,11},{20,16},{21,... | collective-permute-start | bytes 589832 | tf_op jit(solution)/shard_map/ppermute | solution.py:473
  72.2 6.3 %collective-permute-start.21 = (bf16[2,64,768]{2,1,0:T(8,128)(2,1)S(1)}, bf16[2,64,768]{2,1,0:T(8,128)(2,1)S(1)}, u32[]{:S(2)}, u32[]{:S(2)}) collective-permute-start(bf16[2,64,768]{2,1,0:T(8,128)(2,1)S(1)} %pad_maximum_fusion.7), channel_id=1, source_target_pairs={{0,1},{1,0},{2,3},{3,2},{4,5},{5,4},{6,7},{7,6},{8,9},{9,8},{10,11... | collective-permute-start | bytes 589832 | tf_op jit(solution)/shard_map/ppermute | solution.py:458
  72.3 6.3 %collective-permute-start.23 = (bf16[2,64,768]{2,1,0:T(8,128)(2,1)S(1)}, bf16[2,64,768]{2,1,0:T(8,128)(2,1)S(1)}, u32[]{:S(2)}, u32[]{:S(2)}) collective-permute-start(bf16[2,64,768]{2,1,0:T(8,128)(2,1)S(1)} %pad_maximum_fusion.8), channel_id=1, source_target_pairs={{0,16},{8,24},{16,0},{24,8},{1,17},{9,25},{17,1},{25,9},{2,18},{10... | collective-permute-start | bytes 589832 | tf_op jit(solution)/shard_map/ppermute | solution.py:458
  73.7 9.6 %collective-permute-start.20 = (bf16[2,64,768]{2,1,0:T(8,128)(2,1)S(1)}, bf16[2,64,768]{2,1,0:T(8,128)(2,1)S(1)}, u32[]{:S(2)}, u32[]{:S(2)}) collective-permute-start(bf16[2,64,768]{2,1,0:T(8,128)(2,1)S(1)} %collective-permute-done.19), channel_id=1, source_target_pairs={{4,0},{5,1},{6,2},{7,3},{12,8},{13,9},{14,10},{15,11},{20,16},{21,... | collective-permute-start | bytes 589832 | tf_op jit(solution)/shard_map/ppermute | solution.py:473
  78.8 11.5 %collective-permute-start.25 = (bf16[4,64,768]{2,1,0:T(8,128)(2,1)S(1)}, bf16[4,64,768]{2,1,0:T(8,128)(2,1)S(1)}, u32[]{:S(2)}, u32[]{:S(2)}) collective-permute-start(bf16[4,64,768]{2,1,0:T(8,128)(2,1)S(1)} %get-tuple-element.76), channel_id=1, source_target_pairs={{4,0},{5,1},{6,2},{7,3},{12,8},{13,9},{14,10},{15,11},{20,16},{21,... | collective-permute-start | bytes 1179656 | tf_op jit(solution)/shard_map/ppermute | solution.py:473
  80.1 10.2 %collective-permute-start.22 = (bf16[4,64,768]{2,1,0:T(8,128)(2,1)S(1)}, bf16[4,64,768]{2,1,0:T(8,128)(2,1)S(1)}, u32[]{:S(2)}, u32[]{:S(2)}) collective-permute-start(bf16[4,64,768]{2,1,0:T(8,128)(2,1)S(1)} %get-tuple-element.77), channel_id=1, source_target_pairs={{0,16},{8,24},{16,0},{24,8},{1,17},{9,25},{17,1},{25,9},{2,18},{10... | collective-permute-start | bytes 1179656 | tf_op jit(solution)/shard_map/ppermute | solution.py:458
  81.5 9.3 %collective-permute-start.24 = (bf16[4,64,768]{2,1,0:T(8,128)(2,1)S(1)}, bf16[4,64,768]{2,1,0:T(8,128)(2,1)S(1)}, u32[]{:S(2)}, u32[]{:S(2)}) collective-permute-start(bf16[4,64,768]{2,1,0:T(8,128)(2,1)S(1)} %get-tuple-element.78), channel_id=1, source_target_pairs={{0,1},{1,0},{2,3},{3,2},{4,5},{5,4},{6,7},{7,6},{8,9},{9,8},{10,11... | collective-permute-start | bytes 1179656 | tf_op jit(solution)/shard_map/ppermute | solution.py:458
  83.2 16.8 %collective-permute-start.30 = (bf16[8,64,768]{2,1,0:T(8,128)(2,1)S(1)}, bf16[8,64,768]{2,1,0:T(8,128)(2,1)S(1)}, u32[]{:S(2)}, u32[]{:S(2)}) collective-permute-start(bf16[8,64,768]{2,1,0:T(8,128)(2,1)S(1)} %constant_dynamic-update-slice_fusion.3.refs_0_), channel_id=1, source_target_pairs={{0,8},{8,0},{16,24},{24,16},{1,9},{9,1},{17,25},{25,17},{2,10},{10... | collective-permute-start | bytes 2359304 | tf_op jit(solution)/shard_map/ppermute | solution.py:458
  90.8 9.1 %collective-permute-start.28 = (bf16[2,64,768]{2,1,0:T(8,128)(2,1)S(1)}, bf16[2,64,768]{2,1,0:T(8,128)(2,1)S(1)}, u32[]{:S(2)}, u32[]{:S(2)}) collective-permute-start(bf16[2,64,768]{2,1,0:T(8,128)(2,1)S(1)} %pad_maximum_fusion.9), channel_id=1, source_target_pairs={{4,0},{5,1},{6,2},{7,3},{12,8},{13,9},{14,10},{15,11},{20,16},{21,... | collective-permute-start | bytes 589832 | tf_op jit(solution)/shard_map/ppermute | solution.py:473
  92.2 6.8 %collective-permute-start.26 = (bf16[3,64,768]{2,1,0:T(8,128)(2,1)S(1)}, bf16[3,64,768]{2,1,0:T(8,128)(2,1)S(1)}, u32[]{:S(2)}, u32[]{:S(2)}) collective-permute-start(bf16[3,64,768]{2,1,0:T(8,128)(2,1)S(1)} %pad_maximum_fusion.3), channel_id=1, source_target_pairs={{0,16},{8,24},{16,0},{24,8},{1,17},{9,25},{17,1},{25,9},{2,18},{10... | collective-permute-start | bytes 884744 | tf_op jit(solution)/shard_map/ppermute | solution.py:458
  93.1 6.8 %collective-permute-start.27 = (bf16[3,64,768]{2,1,0:T(8,128)(2,1)S(1)}, bf16[3,64,768]{2,1,0:T(8,128)(2,1)S(1)}, u32[]{:S(2)}, u32[]{:S(2)}) collective-permute-start(bf16[3,64,768]{2,1,0:T(8,128)(2,1)S(1)} %pad_maximum_fusion.4), channel_id=1, source_target_pairs={{0,1},{1,0},{2,3},{3,2},{4,5},{5,4},{6,7},{7,6},{8,9},{9,8},{10,11... | collective-permute-start | bytes 884744 | tf_op jit(solution)/shard_map/ppermute | solution.py:458
  94.7 5.4 %collective-permute-start.31 = (bf16[8,64,768]{2,1,0:T(8,128)(2,1)S(1)}, bf16[8,64,768]{2,1,0:T(8,128)(2,1)S(1)}, u32[]{:S(2)}, u32[]{:S(2)}) collective-permute-start(bf16[8,64,768]{2,1,0:T(8,128)(2,1)S(1)} %constant_dynamic-update-slice_fusion.7.refs_2_), channel_id=1, source_target_pairs={{0,8},{8,0},{16,24},{24,16},{1,9},{9,1},{17,25},{25,17},{2,10},{10... | collective-permute-start | bytes 2359304 | tf_op jit(solution)/shard_map/ppermute | solution.py:458
  99.0 2.3 %collective-permute-start.32 = (bf16[8,64,768]{2,1,0:T(8,128)(2,1)S(1)}, bf16[8,64,768]{2,1,0:T(8,128)(2,1)S(1)}, u32[]{:S(2)}, u32[]{:S(2)}) collective-permute-start(bf16[8,64,768]{2,1,0:T(8,128)(2,1)S(1)} %constant_dynamic-update-slice_fusion.9.refs_4_), channel_id=1, source_target_pairs={{0,8},{8,0},{16,24},{24,16},{1,9},{9,1},{17,25},{25,17},{2,10},{10... | collective-permute-start | bytes 2359304 | tf_op jit(solution)/shard_map/ppermute | solution.py:458
  99.9 4.1 %collective-permute-start.29 = (bf16[8,64,768]{2,1,0:T(8,128)(2,1)S(1)}, bf16[8,64,768]{2,1,0:T(8,128)(2,1)S(1)}, u32[]{:S(2)}, u32[]{:S(2)}) collective-permute-start(bf16[8,64,768]{2,1,0:T(8,128)(2,1)S(1)} %constant_dynamic-update-slice_fusion.refs_0_), channel_id=1, source_target_pairs={{0,8},{8,0},{16,24},{24,16},{1,9},{9,1},{17,25},{25,17},{2,10},{10... | collective-permute-start | bytes 2359304 | tf_op jit(solution)/shard_map/ppermute | solution.py:458

commit v8 on v7

--- a/solution.py
+++ b/solution.py
@@ -20,21 +20,21 @@
 f32 = jnp.float32
 bf16 = jnp.bfloat16
 exact = lax.Precision.HIGHEST
-in_smem = pl.BlockSpec(memory_space=pltpu.SMEM)
 in_vmem = pl.BlockSpec(memory_space=pltpu.VMEM)
 in_hbm = pl.BlockSpec(memory_space=pltpu.HBM)
 limited = pltpu.CompilerParams(vmem_limit_bytes=16 * 1024 * 1024)
 
 
-def held_layers(bounds):
-    at_row = lax.axis_index("replica")
-    at_column = lax.axis_index("section")
-    return bounds[at_row, at_column], bounds[at_row, at_column + 1]
+def entry(ref, row, column):
+    values = ref[...].astype(f32)
+    rows = lax.broadcasted_iota(jnp.int32, values.shape, 0)
+    columns = lax.broadcasted_iota(jnp.int32, values.shape, 1)
+    return jnp.sum(jnp.where((rows == row) & (columns == column), values, 0.0)).astype(jnp.int32)
 
 
 def counted_rows(counts, tokens, per_micro):
     rows = lax.broadcasted_iota(jnp.int32, (tokens, 1), 0)
-    return rows < counts[lax.axis_index("replica")] * per_micro
+    return rows < entry(counts, 0, lax.axis_index("replica")) * per_micro
 
 
 def dot_last(x, y, precision=None):
@@ -132,7 +132,7 @@
     columns = by_hidden.shape[1] + ups.shape[0]
     return pl.pallas_call(
         functools.partial(project_back_kernel, per_micro),
-        in_specs=[in_smem] + [in_vmem] * 3,
+        in_specs=[in_vmem] * 4,
         out_specs=in_vmem,
         out_shape=jax.ShapeDtypeStruct((tokens, columns), f32),
         compiler_params=limited,
@@ -195,7 +195,8 @@
     parts = [[jnp.zeros((tokens, ranks), f32)] * 3 for _ in range(layers)]
     for distance, source in enumerate(projections):
         section = lax.rem(section_at + distance, sections)
-        first, after = bounds[replica_at, section], bounds[replica_at, section + 1]
+        first = entry(bounds, replica_at, section)
+        after = entry(bounds, replica_at, section + 1)
         for slot in range(slots):
             for which in range(3):
                 block = which * slots + slot
@@ -296,7 +297,7 @@
     kernel = functools.partial(chain_kernel, sections, slots, features, per_micro)
     return pl.pallas_call(
         kernel,
-        in_specs=[in_smem] * 2 + [in_vmem] * len(inputs),
+        in_specs=[in_vmem] * (2 + len(inputs)),
         out_specs=[in_vmem] * 2,
         out_shape=[
             jax.ShapeDtypeStruct((2 * ranks, 2 * tokens), bf16),
@@ -347,44 +348,38 @@
     )(factors, hidden, cot)
 
 
-def update_kernel(kept, near, downs, ups, *refs):
-    last, mixed_ref, other_ref, right_ref = refs[:4]
-    state, outs, share_ref = refs[4:10], refs[10:16], refs[16]
-    mixed = mixed_ref[...] + other_ref[...].astype(f32)
+def update_kernel(which, kept, near, one, two, last, mixed_ref, other_ref, right_ref, *refs):
+    master_ref, moment_ref, second_ref, new_master, new_moment, new_second, share_ref = refs
+    ranks = last.shape[0]
+    rows = slice(which * ranks, (which + 1) * ranks)
+    mixed = mixed_ref[rows] + other_ref[rows].astype(f32)
     right = right_ref[...].astype(f32)
-    small = jnp.dot(mixed, right, preferred_element_type=f32, precision=exact)
-    ranks = small.shape[0] // 2
-    for which, steps in enumerate((downs, ups)):
-        own = small[which * ranks : (which + 1) * ranks]
-        for block in (kept[which, 0], near[which, 0], *(step[0] for step in steps), last[which]):
-            own = own + block.astype(f32)
-        master, moment, second = (state[2 * kind + which][0] for kind in range(3))
-        moment = beta_one * moment + (1.0 - beta_one) * own
-        second = beta_two * second + (1.0 - beta_two) * own * own
-        master = master - learn_rate * (
-            moment / first_fix / (jnp.sqrt(second / second_fix) + adam_eps) + decay_rate * master
-        )
-        share_ref[which] = master.astype(bf16)
-        outs[which][0] = master
-        outs[2 + which][0] = moment
-        outs[4 + which][0] = second
-
-
-def update(kept, near, downs, ups, last, mixed, other, right, state):
-    _, ranks, columns = state[0].shape
-
-    def kernel(kept, near, down_one, down_two, up_one, up_two, *refs):
-        update_kernel(kept, near, (down_one, down_two), (up_one, up_two), *refs)
-
+    own = jnp.dot(mixed, right, preferred_element_type=f32, precision=exact)
+    for block in (kept[which, 0], near[which, 0], one[0], two[0], last[...]):
+        own = own + block.astype(f32)
+    moment = beta_one * moment_ref[0] + (1.0 - beta_one) * own
+    second = beta_two * second_ref[0] + (1.0 - beta_two) * own * own
+    master = master_ref[0]
+    master = master - learn_rate * (
+        moment / first_fix / (jnp.sqrt(second / second_fix) + adam_eps) + decay_rate * master
+    )
+    share_ref[0] = master.astype(bf16)
+    new_master[0] = master
+    new_moment[0] = moment
+    new_second[0] = second
+
+
+def update(which, parts, right, state):
+    inputs = [*parts, right, *state]
     return pl.pallas_call(
-        kernel,
-        in_specs=[in_vmem] * 16,
-        out_specs=[in_vmem] * 7,
+        functools.partial(update_kernel, which),
+        in_specs=[in_vmem] * len(inputs),
+        out_specs=[in_vmem] * 4,
         out_shape=[jax.ShapeDtypeStruct(array.shape, f32) for array in state]
-        + [jax.ShapeDtypeStruct((2, ranks, columns), bf16)],
+        + [jax.ShapeDtypeStruct(state[0].shape, bf16)],
         compiler_params=limited,
         name="update",
-    )(kept, near, *downs, *ups, last, mixed, other, right, *state)
+    )(*inputs)
 
 
 def place_kernel(layout, start, bounds, *refs):
@@ -394,10 +389,11 @@
     slots, ranks, features = outs[0].shape
     columns = zeros.shape[1]
     tensors = lax.axis_size("tensor")
-    first, after = held_layers(bounds)
     replica_at = lax.axis_index("replica")
     section_at = lax.axis_index("section")
     tensor_at = lax.axis_index("tensor")
+    first = entry(bounds, replica_at, section_at)
+    after = entry(bounds, replica_at, section_at + 1)
     zeros[...] = jnp.zeros_like(zeros)
 
     def fill(slot, distance, go):
@@ -438,7 +434,7 @@
     columns = arrays[0].shape[-1]
     return pl.pallas_call(
         functools.partial(place_kernel, layout, not before),
-        in_specs=[in_smem] + [in_vmem] * len(arrays) + [in_hbm] * len(before),
+        in_specs=[in_vmem] * (1 + len(arrays)) + [in_hbm] * len(before),
         out_specs=[in_hbm] * 2,
         out_shape=[jax.ShapeDtypeStruct((slots, ranks, features), bf16)] * 2,
         scratch_shapes=[pltpu.VMEM((ranks, columns), bf16), pltpu.SemaphoreType.DMA],
@@ -501,11 +497,13 @@
     down_one, up_one, mixed = lax.optimization_barrier((down_one, up_one, mixed))
     down_two = swapped(part(0, low, down_one[2:]), "tensor", 1)
     up_two = swapped(part(1, low, up_one[2:]), "replica", 2)
-    last = jnp.stack([part(0, 1, down_one[1], down_two[1]), part(1, 1, up_one[1], up_two[1])])
-    last = swapped(last, "tensor", 2)
+    down_last = swapped(part(0, 1, down_one[1], down_two[1]), "tensor", 2)
+    kept, near = lax.optimization_barrier((kept, near))
+    up_last = swapped(part(1, 1, up_one[1], up_two[1]), "tensor", 2)
     mixed = added("tensor", 2)
     other = swapped(mixed.astype(bf16), "replica", 2)
-    return (kept, near, (down_one, down_two), (up_one, up_two), last, mixed, other)
+    down = (kept, near, down_one, down_two, down_last, mixed, other)
+    return down, (kept, near, up_one, up_two, up_last, mixed, other)
 
 
 def crossed(piece, axis, distance):
@@ -533,17 +531,23 @@
     return blocks, jnp.concatenate([array for _, array in pieces])
 
 
-def spread(share, bounds, slots, features):
-    ranks = share.shape[1]
-    own = ([(0, 0, 0, 0), (0, 1, 0, 0)], share)
-    one = crossed(own, "tensor", 2)
+def spread(down, up, bounds, slots, features):
+    ranks = down.shape[1]
+    down_own, up_own = ([(0, 0, 0, 0)], down), ([(0, 1, 0, 0)], up)
+    down_one = crossed(down_own, "tensor", 2)
+    up_one = crossed(up_own, "tensor", 2)
+    downs, ups = joined(down_own, down_one), joined(up_own, up_one)
+    owns = lax.optimization_barrier((down, up))
+    own = joined((down_own[0], owns[0]), (up_own[0], owns[1]))
     next_own = fetched(own)
-    downs = joined(picked(own, 0), picked(one, 0))
-    ups = joined(picked(own, 1), picked(one, 1))
+    *ones, next_array = lax.optimization_barrier((down_one[1], up_one[1], next_own[1]))
+    one = joined((down_one[0], ones[0]), (up_one[0], ones[1]))
+    next_own = (next_own[0], next_array)
     down_two = crossed(downs, "tensor", 1)
     up_two = crossed(ups, "replica", 2)
     next_one = fetched(one)
-    two = joined(down_two, up_two)
+    twos = lax.optimization_barrier((down_two[1], up_two[1]))
+    two = joined((down_two[0], twos[0]), (up_two[0], twos[1]))
     down_three = crossed(joined(downs, down_two), "replica", 2)
     up_three = crossed(joined(ups, up_two), "tensor", 1)
     next_two = fetched(two)
@@ -585,6 +589,7 @@
     tensors = lax.axis_size("tensor")
     assert replicas == 4 and tensors == 4
     _, micros, per_micro, features = inputs.shape
+    micro_counts = micro_counts[None]
     slots = holder_down.shape[2]
     hidden = inputs.reshape(micros * per_micro, features)
     cot = cotangent.reshape(micros * per_micro, features)
@@ -604,11 +609,20 @@
         bounds, micro_counts, projections, tables, square, slots, features, per_micro
     )
 
-    parts = reduced(factors, hidden, cot, master_down.shape[2], mixed)
-    state = [master_down, master_up, moment_down, moment_up, second_down, second_up]
-    updated = update(*parts, right, state)
-    placed = spread(updated[6], bounds, slots, features)
-    return (placed[0][None, None], placed[1][None, None], *updated[:6])
+    down_parts, up_parts = reduced(factors, hidden, cot, master_down.shape[2], mixed)
+    down = update(0, down_parts, right, [master_down, moment_down, second_down])
+    up = update(1, up_parts, right, [master_up, moment_up, second_up])
+    placed = spread(down[3], up[3], bounds, slots, features)
+    return (
+        placed[0][None, None],
+        placed[1][None, None],
+        down[0],
+        up[0],
+        down[1],
+        up[1],
+        down[2],
+        up[2],
+    )
 
 
 def solution(mesh):

time: 106 us -> 105 us (level)
  starting transfers between devices: 34.3 us -> 43.2 us
  waiting for transfers between devices: 50 us -> 41.2 us
  Pallas kernels: 18.1 us -> 16.9 us
    ppermute x27 -> x29, starting transfers between devices: 25.5 us -> 34.3 us  [swapped(): return lax.ppermute(block, axis, route)]
    ppermute x27 -> x29, waiting for transfers between devices: 43.1 us -> 36.6 us  [swapped(): return lax.ppermute(block, axis, route)]
    ppermute x4, waiting for transfers between devices: 6.85 us -> 4.58 us  [following_layer(): return lax.ppermute(block, 'section', [(i + 1, i) for i in range(size - 1)])]
    pallas_call x2 -> x3, Pallas kernels: 3.97 us -> 4.23 us  [the longest x2 2.51 us: update(): pl.pallas_call(functools.partial(update_kernel, which), in_specs=[in_vmem...]
  transfers between devices with their start and end apart: 33 -> 35, of which waited for: 18 -> 21; matrix products, arithmetic and copies ran while one was open for 1% -> 1% of each run, Pallas kernels for 11% -> 13%
where the time goes in v8:
time: 105 us
  starting transfers between devices  43.2 us (41%)
  waiting for transfers between devices  41.2 us (39%)
  Pallas kernels  16.9 us (16%)
  other arithmetic  1.84 us (2%)
  between operations  1.1 us (1%)
    ppermute x29, waiting for transfers between devices, swapped(): return lax.ppermute(block, axis, route)  36.6 us
    ppermute x29, starting transfers between devices, swapped(): return lax.ppermute(block, axis, route)  34.3 us
    pallas_call x1, Pallas kernels, project(): pl.pallas_call(functools.partial(project_kernel, steps), in_specs=[in_hbm...  5.99 us
    ppermute x4, starting transfers between devices, following_layer(): return lax.ppermute(block, 'section', [(i + 1, i) for i in range(size - 1)])  5.17 us
    ppermute x4, waiting for transfers between devices, following_layer(): return lax.ppermute(block, 'section', [(i + 1, i) for i in range(size - 1)])  4.58 us
    ppermute x2, starting transfers between devices, from_next(): return lax.ppermute(block, 'section', route)  3.69 us
    pallas_call x2, Pallas kernels, place(): pl.pallas_call(functools.partial(place_kernel, layout, not before), in_sp...  3.56 us
    pallas_call x2, Pallas kernels, update(): pl.pallas_call(functools.partial(update_kernel, which), in_specs=[in_vmem...  2.51 us
  transfers between devices with their start and end apart: 35, of which 21 were waited for; matrix products, arithmetic and copies ran while one was open for 1% of the time, Pallas kernels for 13%

profile of v8, /device:TPU:0, one launch (start us, length us, event | category | flops | bytes accessed | tf_op | source)
XLA Modules:
  0.0 104.5 jit_solution(972103811055069366)
XLA Ops:
  0.6 1.0 %convert_bitcast_fusion = (bf16[64,768]{1,0:T(8,128)(2,1)S(1)}, bf16[64,768]{1,0:T(8,128)(2,1)S(1)}) fusion(f32[1,64,768]{2,1,0:T(8,128)} %refs_0_.3, f32[1,64,768]{2,1,0:T(8,128)} %refs_0_.2), kind=kLoop, calls=%fused_computation.27 | loop fusion | flops 98304 | bytes 589824 | tf_op jit(solution)/shard_map/squeeze | solution.py:597
  1.7 3.0 %collective-permute-start = (bf16[128,768]{1,0:T(8,128)(2,1)S(1)}, bf16[128,768]{1,0:T(8,128)(2,1)S(1)}, u32[]{:S(2)}, u32[]{:S(2)}) collective-permute-start(bf16[128,768]{1,0:T(8,128)(2,1)S(1)} %pad_maximum_fusion.5.refs_0_), channel_id=1, source_target_pairs={{4,0},{0,4},{5,1},{1,5},{6,2},{2,6},{7,3},{3,7},{12,8},{8,12},{13,... | collective-permute-start | bytes 589832 | tf_op jit(solution)/shard_map/ppermute | solution.py:464
  4.7 6.0 %project.1 = (f32[128,256]{1,0:T(8,128)S(1)}, f32[128,128]{1,0:T(8,128)S(1)}, bf16[128,12288]{1,0:T(8,128)(2,1)S(1)}, bf16[128,12288]{1,0:T(8,128)(2,1)S(1)}) custom-call(bf16[128,12288]{1,0:T(8,128)(2,1)} %bitcast.52, bf16[2,64,12288]{2,1,0:T(8,128)(2,1)} %bitcast.53, bf16[2,64,12288]{2,1,0:T(8,128)(2,1)} %bitcast.54), custom_call_target="tpu_custom_call" | custom-call | flops 805306368 | bytes 9437184 | tf_op jit(solution)/shard_map/project/pallas_call | solution.py:98
  10.9 0.7 collective-permute-start.4
  11.7 0.9 collective-permute-start.3
  12.8 1.0 project_back.1.refs_0_
  13.8 0.7 collective-permute-start.1
  14.6 1.3 %collective-permute-done.3 = f32[64,128]{1,0:T(8,128)S(1)} collective-permute-done((f32[64,128]{1,0:T(8,128)S(1)}, f32[64,128]{1,0:T(8,128)S(1)}, u32[]{:S(2)}, u32[]{:S(2)}) %collective-permute-start.3) | collective-permute-done | bytes 32800 | tf_op jit(solution)/shard_map/ppermute | solution.py:454
  15.9 1.6 %collective-permute-start.5 = (f32[64,128]{1,0:T(8,128)S(1)}, f32[64,128]{1,0:T(8,128)S(1)}, u32[]{:S(2)}, u32[]{:S(2)}) collective-permute-start(f32[64,128]{1,0:T(8,128)S(1)} %add_add_fusion), channel_id=1, source_target_pairs={{0,1},{1,0},{2,3},{3,2},{4,5},{5,4},{6,7},{7,6},{8,9},{9,8},{10,11... | collective-permute-start | bytes 98312 | tf_op jit(solution)/shard_map/ppermute | solution.py:454
  17.6 2.3 %collective-permute-done.5 = f32[64,128]{1,0:T(8,128)S(1)} collective-permute-done((f32[64,128]{1,0:T(8,128)S(1)}, f32[64,128]{1,0:T(8,128)S(1)}, u32[]{:S(2)}, u32[]{:S(2)}) %collective-permute-start.5) | collective-permute-done | bytes 32800 | tf_op jit(solution)/shard_map/ppermute | solution.py:454
  19.9 2.6 %collective-permute-start.6 = (f32[64,128]{1,0:T(8,128)S(1)}, f32[64,128]{1,0:T(8,128)S(1)}, u32[]{:S(2)}, u32[]{:S(2)}) collective-permute-start(f32[64,128]{1,0:T(8,128)S(1)} %add.74.refs_2_), channel_id=1, source_target_pairs={{0,2},{1,3},{2,0},{3,1},{4,6},{5,7},{6,4},{7,5},{8,10},{9,11},{10,... | collective-permute-start | bytes 98312 | tf_op jit(solution)/shard_map/ppermute | solution.py:454
  22.5 2.2 %collective-permute-done.6.refs_3_ = f32[64,128]{1,0:T(8,128)S(1)} collective-permute-done((f32[64,128]{1,0:T(8,128)S(1)}, f32[64,128]{1,0:T(8,128)S(1)}, u32[]{:S(2)}, u32[]{:S(2)}) %collective-permute-start.6) | collective-permute-done | bytes 32800 | tf_op jit(solution)/shard_map/ppermute | solution.py:454
  24.7 1.7 %chain.1 = (bf16[128,256]{1,0:T(8,128)(2,1)S(1)}, f32[128,128]{1,0:T(8,128)S(1)}) custom-call(s32[4,3]{1,0:T(4,128)S(1)} %copy-done.7, s32[1,4]{1,0:T(1,128)S(1)} %bitcast.49, f32[128,384]{1,0:T(8,128)S(1)} %project_back.1.refs_0_, f32[128,384]{1,0:T(8,128)S(1)} %collective-permute-done.1.refs_1_, f32[64,128]{1,0:T(8,128)S(1)} %add.74.refs_2_, ...), custom_call_target="tpu_custom_call" | custom-call | tf_op jit(solution)/shard_map/chain/pallas_call | solution.py:298
  27.0 0.5 gradient.5
  27.6 0.5 collective-permute-start.7
  28.7 0.6 collective-permute-done.8
  29.5 1.6 %collective-permute-start.10 = (bf16[4,64,768]{2,1,0:T(8,128)(2,1)S(1)}, bf16[4,64,768]{2,1,0:T(8,128)(2,1)S(1)}, u32[]{:S(2)}, u32[]{:S(2)}) collective-permute-start(bf16[4,64,768]{2,1,0:T(8,128)(2,1)S(1)} %get-tuple-element.86), channel_id=1, source_target_pairs={{0,1},{1,0},{2,3},{3,2},{4,5},{5,4},{6,7},{7,6},{8,9},{9,8},{10,11... | collective-permute-start | bytes 1179656 | tf_op jit(solution)/shard_map/ppermute | solution.py:454
  31.1 0.7 collective-permute-start.9
  31.9 0.5 collective-permute-start.12
  33.0 8.5 %collective-permute-done.12 = bf16[128,128]{1,0:T(8,128)(2,1)S(1)} collective-permute-done((bf16[128,128]{1,0:T(8,128)(2,1)S(1)}, bf16[128,128]{1,0:T(8,128)(2,1)S(1)}, u32[]{:S(2)}, u32[]{:S(2)}) %collective-permute-start.12) | collective-permute-done | bytes 32800 | tf_op jit(solution)/shard_map/ppermute | solution.py:454
  41.4 0.6 collective-permute-done.9.one
  42.2 0.8 collective-permute-start.18
  43.0 2.8 %collective-permute-start.15 = (bf16[128,128]{1,0:T(8,128)(2,1)S(1)}, bf16[128,128]{1,0:T(8,128)(2,1)S(1)}, u32[]{:S(2)}, u32[]{:S(2)}) collective-permute-start(bf16[128,128]{1,0:T(8,128)(2,1)S(1)} %convert_element_type.147), channel_id=1, source_target_pairs={{0,2},{1,3},{2,0},{3,1},{4,6},{5,7},{6,4},{7,5},{8,10},{9,11},{10,... | collective-permute-start | bytes 98312 | tf_op jit(solution)/shard_map/ppermute | solution.py:454
  45.8 1.0 collective-permute-start.13
  46.8 1.2 %collective-permute-done.18.two = bf16[2,64,768]{2,1,0:T(8,128)(2,1)S(1)} collective-permute-done((bf16[2,64,768]{2,1,0:T(8,128)(2,1)S(1)}, bf16[2,64,768]{2,1,0:T(8,128)(2,1)S(1)}, u32[]{:S(2)}, u32[]{:S(2)}) %collective-permute-start.18) | collective-permute-done | bytes 196640 | tf_op jit(solution)/shard_map/ppermute | solution.py:454
  48.1 2.9 %collective-permute-start.19 = (bf16[64,768]{1,0:T(8,128)(2,1)S(1)}, bf16[64,768]{1,0:T(8,128)(2,1)S(1)}, u32[]{:S(2)}, u32[]{:S(2)}) collective-permute-start(bf16[64,768]{1,0:T(8,128)(2,1)S(1)} %fusion.4), channel_id=1, source_target_pairs={{0,2},{1,3},{2,0},{3,1},{4,6},{5,7},{6,4},{7,5},{8,10},{9,11},{10,... | collective-permute-start | bytes 294920 | tf_op jit(solution)/shard_map/ppermute | solution.py:454
  51.0 1.5 %collective-permute-done.13.two = bf16[2,64,768]{2,1,0:T(8,128)(2,1)S(1)} collective-permute-done((bf16[2,64,768]{2,1,0:T(8,128)(2,1)S(1)}, bf16[2,64,768]{2,1,0:T(8,128)(2,1)S(1)}, u32[]{:S(2)}, u32[]{:S(2)}) %collective-permute-start.13) | collective-permute-done | bytes 196640 | tf_op jit(solution)/shard_map/ppermute | solution.py:454
  52.7 2.0 %collective-permute-start.16 = (bf16[128,128]{1,0:T(8,128)(2,1)S(1)}, bf16[128,128]{1,0:T(8,128)(2,1)S(1)}, u32[]{:S(2)}, u32[]{:S(2)}) collective-permute-start(bf16[128,128]{1,0:T(8,128)(2,1)S(1)} %get-tuple-element.82), channel_id=1, source_target_pairs={{0,16},{8,24},{16,0},{24,8},{1,17},{9,25},{17,1},{25,9},{2,18},{10... | collective-permute-start | bytes 98312 | tf_op jit(solution)/shard_map/ppermute | solution.py:454
  54.7 2.0 %collective-permute-done.16.other_ref = bf16[128,128]{1,0:T(8,128)(2,1)S(1)} collective-permute-done((bf16[128,128]{1,0:T(8,128)(2,1)S(1)}, bf16[128,128]{1,0:T(8,128)(2,1)S(1)}, u32[]{:S(2)}, u32[]{:S(2)}) %collective-permute-start.16) | collective-permute-done | bytes 32800 | tf_op jit(solution)/shard_map/ppermute | solution.py:454
  56.7 1.3 %update.3 = (f32[1,64,768]{2,1,0:T(8,128)}, f32[1,64,768]{2,1,0:T(8,128)}, f32[1,64,768]{2,1,0:T(8,128)}, bf16[1,64,768]{2,1,0:T(8,128)(2,1)S(1)}) custom-call(bf16[2,4,64,768]{3,2,1,0:T(8,128)(2,1)S(1)} %gradient.4.kept, bf16[2,4,64,768]{3,2,1,0:T(8,128)(2,1)S(1)} %collective-permute-done.7.near, bf16[4,64,768]{2,1,0:T(8,128)(2,1)S(1)} %collective-permute-done.10.one, ...), custom_call_target="tpu_custom_call" | custom-call | tf_op jit(solution)/shard_map/update/pallas_call | solution.py:374
  58.0 2.8 %collective-permute-start.20 = (bf16[1,64,768]{2,1,0:T(8,128)(2,1)S(1)}, bf16[1,64,768]{2,1,0:T(8,128)(2,1)S(1)}, u32[]{:S(2)}, u32[]{:S(2)}) collective-permute-start(bf16[1,64,768]{2,1,0:T(8,128)(2,1)S(1)} %get-tuple-element.65), channel_id=1, source_target_pairs={{0,2},{1,3},{2,0},{3,1},{4,6},{5,7},{6,4},{7,5},{8,10},{9,11},{10,... | collective-permute-start | bytes 294920 | tf_op jit(solution)/shard_map/ppermute | solution.py:454
  60.9 1.3 %update.2 = (f32[1,64,768]{2,1,0:T(8,128)}, f32[1,64,768]{2,1,0:T(8,128)}, f32[1,64,768]{2,1,0:T(8,128)}, bf16[1,64,768]{2,1,0:T(8,128)(2,1)S(1)}) custom-call(bf16[2,4,64,768]{3,2,1,0:T(8,128)(2,1)S(1)} %gradient.4.kept, bf16[2,4,64,768]{3,2,1,0:T(8,128)(2,1)S(1)} %collective-permute-done.7.near, bf16[4,64,768]{2,1,0:T(8,128)(2,1)S(1)} %collective-permute-done.9.one, ...), custom_call_target="tpu_custom_call" | custom-call | tf_op jit(solution)/shard_map/update/pallas_call | solution.py:374
  62.2 1.3 %collective-permute-start.21 = (bf16[2,64,768]{2,1,0:T(8,128)(2,1)S(1)}, bf16[2,64,768]{2,1,0:T(8,128)(2,1)S(1)}, u32[]{:S(2)}, u32[]{:S(2)}) collective-permute-start(bf16[2,64,768]{2,1,0:T(8,128)(2,1)S(1)} %pad_maximum_fusion.6), channel_id=1, source_target_pairs={{4,0},{5,1},{6,2},{7,3},{12,8},{13,9},{14,10},{15,11},{20,16},{21,... | collective-permute-start | bytes 589832 | tf_op jit(solution)/shard_map/ppermute | solution.py:469
  63.7 3.7 %collective-permute-start.25 = (bf16[2,64,768]{2,1,0:T(8,128)(2,1)S(1)}, bf16[2,64,768]{2,1,0:T(8,128)(2,1)S(1)}, u32[]{:S(2)}, u32[]{:S(2)}) collective-permute-start(bf16[2,64,768]{2,1,0:T(8,128)(2,1)S(1)} %pad_maximum_fusion.9), channel_id=1, source_target_pairs={{0,16},{8,24},{16,0},{24,8},{1,17},{9,25},{17,1},{25,9},{2,18},{10... | collective-permute-start | bytes 589832 | tf_op jit(solution)/shard_map/ppermute | solution.py:454
  67.7 3.1 %collective-permute-start.23 = (bf16[2,64,768]{2,1,0:T(8,128)(2,1)S(1)}, bf16[2,64,768]{2,1,0:T(8,128)(2,1)S(1)}, u32[]{:S(2)}, u32[]{:S(2)}) collective-permute-start(bf16[2,64,768]{2,1,0:T(8,128)(2,1)S(1)} %pad_maximum_fusion.8), channel_id=1, source_target_pairs={{0,1},{1,0},{2,3},{3,2},{4,5},{5,4},{6,7},{7,6},{8,9},{9,8},{10,11... | collective-permute-start | bytes 589832 | tf_op jit(solution)/shard_map/ppermute | solution.py:454
  70.8 1.3 %collective-permute-start.22 = (bf16[2,64,768]{2,1,0:T(8,128)(2,1)S(1)}, bf16[2,64,768]{2,1,0:T(8,128)(2,1)S(1)}, u32[]{:S(2)}, u32[]{:S(2)}) collective-permute-start(bf16[2,64,768]{2,1,0:T(8,128)(2,1)S(1)} %pad_maximum_fusion.7), channel_id=1, source_target_pairs={{4,0},{5,1},{6,2},{7,3},{12,8},{13,9},{14,10},{15,11},{20,16},{21,... | collective-permute-start | bytes 589832 | tf_op jit(solution)/shard_map/ppermute | solution.py:469
  72.2 3.4 %collective-permute-done.23 = bf16[2,64,768]{2,1,0:T(8,128)(2,1)S(1)} collective-permute-done((bf16[2,64,768]{2,1,0:T(8,128)(2,1)S(1)}, bf16[2,64,768]{2,1,0:T(8,128)(2,1)S(1)}, u32[]{:S(2)}, u32[]{:S(2)}) %collective-permute-start.23) | collective-permute-done | bytes 196640 | tf_op jit(solution)/shard_map/ppermute | solution.py:454
  75.6 2.4 %collective-permute-start.26 = (bf16[4,64,768]{2,1,0:T(8,128)(2,1)S(1)}, bf16[4,64,768]{2,1,0:T(8,128)(2,1)S(1)}, u32[]{:S(2)}, u32[]{:S(2)}) collective-permute-start(bf16[4,64,768]{2,1,0:T(8,128)(2,1)S(1)} %pad_maximum_fusion.1), channel_id=1, source_target_pairs={{0,1},{1,0},{2,3},{3,2},{4,5},{5,4},{6,7},{7,6},{8,9},{9,8},{10,11... | collective-permute-start | bytes 1179656 | tf_op jit(solution)/shard_map/ppermute | solution.py:454
  78.1 1.9 %collective-permute-start.24 = (bf16[4,64,768]{2,1,0:T(8,128)(2,1)S(1)}, bf16[4,64,768]{2,1,0:T(8,128)(2,1)S(1)}, u32[]{:S(2)}, u32[]{:S(2)}) collective-permute-start(bf16[4,64,768]{2,1,0:T(8,128)(2,1)S(1)} %pad_maximum_fusion), channel_id=1, source_target_pairs={{0,16},{8,24},{16,0},{24,8},{1,17},{9,25},{17,1},{25,9},{2,18},{10... | collective-permute-start | bytes 1179656 | tf_op jit(solution)/shard_map/ppermute | solution.py:454
  80.0 1.3 %collective-permute-start.27 = (bf16[4,64,768]{2,1,0:T(8,128)(2,1)S(1)}, bf16[4,64,768]{2,1,0:T(8,128)(2,1)S(1)}, u32[]{:S(2)}, u32[]{:S(2)}) collective-permute-start(bf16[4,64,768]{2,1,0:T(8,128)(2,1)S(1)} %pad_maximum_fusion.2), channel_id=1, source_target_pairs={{4,0},{5,1},{6,2},{7,3},{12,8},{13,9},{14,10},{15,11},{20,16},{21,... | collective-permute-start | bytes 1179656 | tf_op jit(solution)/shard_map/ppermute | solution.py:469
  81.5 2.3 %collective-permute-done.26 = bf16[4,64,768]{2,1,0:T(8,128)(2,1)S(1)} collective-permute-done((bf16[4,64,768]{2,1,0:T(8,128)(2,1)S(1)}, bf16[4,64,768]{2,1,0:T(8,128)(2,1)S(1)}, u32[]{:S(2)}, u32[]{:S(2)}) %collective-permute-start.26) | collective-permute-done | bytes 393248 | tf_op jit(solution)/shard_map/ppermute | solution.py:454
  83.8 2.1 %collective-permute-done.24 = bf16[4,64,768]{2,1,0:T(8,128)(2,1)S(1)} collective-permute-done((bf16[4,64,768]{2,1,0:T(8,128)(2,1)S(1)}, bf16[4,64,768]{2,1,0:T(8,128)(2,1)S(1)}, u32[]{:S(2)}, u32[]{:S(2)}) %collective-permute-start.24) | collective-permute-done | bytes 393248 | tf_op jit(solution)/shard_map/ppermute | solution.py:454
  86.0 1.3 %collective-permute-start.30 = (bf16[2,64,768]{2,1,0:T(8,128)(2,1)S(1)}, bf16[2,64,768]{2,1,0:T(8,128)(2,1)S(1)}, u32[]{:S(2)}, u32[]{:S(2)}) collective-permute-start(bf16[2,64,768]{2,1,0:T(8,128)(2,1)S(1)} %pad_maximum_fusion.10), channel_id=1, source_target_pairs={{4,0},{5,1},{6,2},{7,3},{12,8},{13,9},{14,10},{15,11},{20,16},{21,... | collective-permute-start | bytes 589832 | tf_op jit(solution)/shard_map/ppermute | solution.py:469
  87.3 4.6 %collective-permute-done.27 = bf16[4,64,768]{2,1,0:T(8,128)(2,1)S(1)} collective-permute-done((bf16[4,64,768]{2,1,0:T(8,128)(2,1)S(1)}, bf16[4,64,768]{2,1,0:T(8,128)(2,1)S(1)}, u32[]{:S(2)}, u32[]{:S(2)}) %collective-permute-start.27) | collective-permute-done | bytes 393248 | tf_op jit(solution)/shard_map/ppermute | solution.py:469
  92.6 6.1 %collective-permute-done.28 = bf16[3,64,768]{2,1,0:T(8,128)(2,1)S(1)} collective-permute-done((bf16[3,64,768]{2,1,0:T(8,128)(2,1)S(1)}, bf16[3,64,768]{2,1,0:T(8,128)(2,1)S(1)}, u32[]{:S(2)}, u32[]{:S(2)}) %collective-permute-start.28) | collective-permute-done | bytes 294944 | tf_op jit(solution)/shard_map/ppermute | solution.py:454
  99.4 1.6 %collective-permute-done.34.refs_5_ = bf16[8,64,768]{2,1,0:T(8,128)(2,1)S(1)} collective-permute-done((bf16[8,64,768]{2,1,0:T(8,128)(2,1)S(1)}, bf16[8,64,768]{2,1,0:T(8,128)(2,1)S(1)}, u32[]{:S(2)}, u32[]{:S(2)}) %collective-permute-start.34) | collective-permute-done | bytes 786464 | tf_op jit(solution)/shard_map/ppermute | solution.py:454
  101.0 2.3 %place.2 = (bf16[2,64,12288]{2,1,0:T(8,128)(2,1)}, bf16[2,64,12288]{2,1,0:T(8,128)(2,1)}) custom-call(s32[4,3]{1,0:T(4,128)S(1)} %copy-done.7, bf16[8,64,768]{2,1,0:T(8,128)(2,1)S(1)} %constant_dynamic-update-slice_fusion.3.refs_0_, bf16[8,64,768]{2,1,0:T(8,128)(2,1)S(1)} %collective-permute-done.32.refs_1_, ...), custom_call_target="tpu_custom_call" | custom-call | bytes 9437184 | tf_op jit(solution)/shard_map/place/pallas_call | solution.py:435
  103.3 1.3 %place.3 = (bf16[2,64,12288]{2,1,0:T(8,128)(2,1)}, bf16[2,64,12288]{2,1,0:T(8,128)(2,1)}) custom-call(s32[4,3]{1,0:T(4,128)S(1)} %copy-done.7, bf16[8,64,768]{2,1,0:T(8,128)(2,1)S(1)} %constant_dynamic-update-slice_fusion.refs_0_, bf16[8,64,768]{2,1,0:T(8,128)(2,1)S(1)} %collective-permute-done.31.refs_1_, ...), custom_call_target="tpu_custom_call", output_to_operand_aliasing={{0}: (3, {}), {1}: (4, {})} | custom-call | bytes 3145728 | tf_op jit(solution)/shard_map/place/pallas_call | solution.py:435
  (94 shorter events, 5.3 us)
Async XLA Ops:
  1.7 9.0 %collective-permute-start = (bf16[128,768]{1,0:T(8,128)(2,1)S(1)}, bf16[128,768]{1,0:T(8,128)(2,1)S(1)}, u32[]{:S(2)}, u32[]{:S(2)}) collective-permute-start(bf16[128,768]{1,0:T(8,128)(2,1)S(1)} %pad_maximum_fusion.5.refs_0_), channel_id=1, source_target_pairs={{4,0},{0,4},{5,1},{1,5},{6,2},{2,6},{7,3},{3,7},{12,8},{8,12},{13,... | collective-permute-start | bytes 589832 | tf_op jit(solution)/shard_map/ppermute | solution.py:464
  4.7 8.1 %copy-start = (bf16[1,4,32,12288]{3,2,1,0:T(8,128)(2,1)S(1)}, bf16[1,4,32,12288]{3,2,1,0:T(8,128)(2,1)}, u32[]{:S(2)}) copy-start(bf16[1,4,32,12288]{3,2,1,0:T(8,128)(2,1)} %param.13) | copy-start | bytes 9437188
  4.7 8.1 %copy-start.8 = (s32[4]{0:T(128)S(1)}, s32[4]{0:T(128)}, u32[]{:S(2)}) copy-start(s32[4]{0:T(128)} %param.14) | copy-start | bytes 52
  10.9 3.7 %collective-permute-start.4 = (f32[64,128]{1,0:T(8,128)S(1)}, f32[64,128]{1,0:T(8,128)S(1)}, u32[]{:S(2)}, u32[]{:S(2)}) collective-permute-start(f32[64,128]{1,0:T(8,128)S(1)} %get-tuple-element.51), channel_id=1, source_target_pairs={{0,24},{8,16},{16,8},{24,0},{1,25},{9,17},{17,9},{25,1},{2,26},{10... | collective-permute-start | bytes 98312 | tf_op jit(solution)/shard_map/ppermute | solution.py:454
  11.7 4.2 %collective-permute-start.3 = (f32[64,128]{1,0:T(8,128)S(1)}, f32[64,128]{1,0:T(8,128)S(1)}, u32[]{:S(2)}, u32[]{:S(2)}) collective-permute-start(f32[64,128]{1,0:T(8,128)S(1)} %get-tuple-element.51), channel_id=1, source_target_pairs={{0,16},{8,24},{16,0},{24,8},{1,17},{9,25},{17,1},{25,9},{2,18},{10... | collective-permute-start | bytes 98312 | tf_op jit(solution)/shard_map/ppermute | solution.py:454
  12.6 3.3 %collective-permute-start.2 = (f32[64,128]{1,0:T(8,128)S(1)}, f32[64,128]{1,0:T(8,128)S(1)}, u32[]{:S(2)}, u32[]{:S(2)}) collective-permute-start(f32[64,128]{1,0:T(8,128)S(1)} %get-tuple-element.51), channel_id=1, source_target_pairs={{0,8},{8,0},{16,24},{24,16},{1,9},{9,1},{17,25},{25,17},{2,10},{10... | collective-permute-start | bytes 98312 | tf_op jit(solution)/shard_map/ppermute | solution.py:454
  12.8 11.9 %copy-start.7 = (s32[4,3]{1,0:T(4,128)S(1)}, s32[4,3]{1,0:T(4,128)}, u32[]{:S(2)}) copy-start(s32[4,3]{1,0:T(4,128)} %bounds.5) | copy-start | bytes 148
  13.8 10.9 %collective-permute-start.1 = (f32[128,384]{1,0:T(8,128)S(1)}, f32[128,384]{1,0:T(8,128)S(1)}, u32[]{:S(2)}, u32[]{:S(2)}) collective-permute-start(f32[128,384]{1,0:T(8,128)S(1)} %project_back.1.refs_0_), channel_id=1, source_target_pairs={{4,0},{0,4},{5,1},{1,5},{6,2},{2,6},{7,3},{3,7},{12,8},{8,12},{13,... | collective-permute-start | bytes 589832 | tf_op jit(solution)/shard_map/ppermute | solution.py:464
  15.9 4.0 %collective-permute-start.5 = (f32[64,128]{1,0:T(8,128)S(1)}, f32[64,128]{1,0:T(8,128)S(1)}, u32[]{:S(2)}, u32[]{:S(2)}) collective-permute-start(f32[64,128]{1,0:T(8,128)S(1)} %add_add_fusion), channel_id=1, source_target_pairs={{0,1},{1,0},{2,3},{3,2},{4,5},{5,4},{6,7},{7,6},{8,9},{9,8},{10,11... | collective-permute-start | bytes 98312 | tf_op jit(solution)/shard_map/ppermute | solution.py:454
  19.9 4.8 %collective-permute-start.6 = (f32[64,128]{1,0:T(8,128)S(1)}, f32[64,128]{1,0:T(8,128)S(1)}, u32[]{:S(2)}, u32[]{:S(2)}) collective-permute-start(f32[64,128]{1,0:T(8,128)S(1)} %add.74.refs_2_), channel_id=1, source_target_pairs={{0,2},{1,3},{2,0},{3,1},{4,6},{5,7},{6,4},{7,5},{8,10},{9,11},{10,... | collective-permute-start | bytes 98312 | tf_op jit(solution)/shard_map/ppermute | solution.py:454
  27.0 2.4 %collective-permute-start.8 = (bf16[2,4,64,768]{3,2,1,0:T(8,128)(2,1)S(1)}, bf16[2,4,64,768]{3,2,1,0:T(8,128)(2,1)S(1)}, u32[]{:S(2)}, u32[]{:S(2)}) collective-permute-start(bf16[2,4,64,768]{3,2,1,0:T(8,128)(2,1)S(1)} %gradient.7), channel_id=1, source_target_pairs={{0,8},{8,0},{16,24},{24,16},{1,9},{9,1},{17,25},{25,17},{2,10},{10... | collective-permute-start | bytes 2359304 | tf_op jit(solution)/shard_map/ppermute | solution.py:454
  27.6 14.5 %collective-permute-start.7 = (bf16[2,4,64,768]{3,2,1,0:T(8,128)(2,1)S(1)}, bf16[2,4,64,768]{3,2,1,0:T(8,128)(2,1)S(1)}, u32[]{:S(2)}, u32[]{:S(2)}) collective-permute-start(bf16[2,4,64,768]{3,2,1,0:T(8,128)(2,1)S(1)} %gradient.5), channel_id=1, source_target_pairs={{0,8},{8,0},{16,24},{24,16},{1,9},{9,1},{17,25},{25,17},{2,10},{10... | collective-permute-start | bytes 2359304 | tf_op jit(solution)/shard_map/ppermute | solution.py:454
  28.1 3.8 %collective-permute-start.11 = (bf16[128,128]{1,0:T(8,128)(2,1)S(1)}, bf16[128,128]{1,0:T(8,128)(2,1)S(1)}, u32[]{:S(2)}, u32[]{:S(2)}) collective-permute-start(bf16[128,128]{1,0:T(8,128)(2,1)S(1)} %convert_element_type.132), channel_id=1, source_target_pairs={{0,8},{8,0},{16,24},{24,16},{1,9},{9,1},{17,25},{25,17},{2,10},{10... | collective-permute-start | bytes 98312 | tf_op jit(solution)/shard_map/ppermute | solution.py:454
  29.5 11.9 %collective-permute-start.10 = (bf16[4,64,768]{2,1,0:T(8,128)(2,1)S(1)}, bf16[4,64,768]{2,1,0:T(8,128)(2,1)S(1)}, u32[]{:S(2)}, u32[]{:S(2)}) collective-permute-start(bf16[4,64,768]{2,1,0:T(8,128)(2,1)S(1)} %get-tuple-element.86), channel_id=1, source_target_pairs={{0,1},{1,0},{2,3},{3,2},{4,5},{5,4},{6,7},{7,6},{8,9},{9,8},{10,11... | collective-permute-start | bytes 1179656 | tf_op jit(solution)/shard_map/ppermute | solution.py:454
  31.1 10.9 %collective-permute-start.9 = (bf16[4,64,768]{2,1,0:T(8,128)(2,1)S(1)}, bf16[4,64,768]{2,1,0:T(8,128)(2,1)S(1)}, u32[]{:S(2)}, u32[]{:S(2)}) collective-permute-start(bf16[4,64,768]{2,1,0:T(8,128)(2,1)S(1)} %get-tuple-element.87), channel_id=1, source_target_pairs={{0,16},{8,24},{16,0},{24,8},{1,17},{9,25},{17,1},{25,9},{2,18},{10... | collective-permute-start | bytes 1179656 | tf_op jit(solution)/shard_map/ppermute | solution.py:454
  31.9 9.5 %collective-permute-start.12 = (bf16[128,128]{1,0:T(8,128)(2,1)S(1)}, bf16[128,128]{1,0:T(8,128)(2,1)S(1)}, u32[]{:S(2)}, u32[]{:S(2)}) collective-permute-start(bf16[128,128]{1,0:T(8,128)(2,1)S(1)} %fusion.6), channel_id=1, source_target_pairs={{0,1},{1,0},{2,3},{3,2},{4,5},{5,4},{6,7},{7,6},{8,9},{9,8},{10,11... | collective-permute-start | bytes 98312 | tf_op jit(solution)/shard_map/ppermute | solution.py:454
  32.9 23.8 %copy-start.1 = (f32[1,64,768]{2,1,0:T(8,128)S(1)}, f32[1,64,768]{2,1,0:T(8,128)}, u32[]{:S(2)}) copy-start(f32[1,64,768]{2,1,0:T(8,128)} %refs_0_.3) | copy-start | bytes 589828
  32.9 23.8 %copy-start.3 = (f32[1,64,768]{2,1,0:T(8,128)S(1)}, f32[1,64,768]{2,1,0:T(8,128)}, u32[]{:S(2)}) copy-start(f32[1,64,768]{2,1,0:T(8,128)} %refs_1_.3) | copy-start | bytes 589828
  32.9 23.8 %copy-start.4 = (f32[1,64,768]{2,1,0:T(8,128)S(1)}, f32[1,64,768]{2,1,0:T(8,128)}, u32[]{:S(2)}) copy-start(f32[1,64,768]{2,1,0:T(8,128)} %refs_2_.3) | copy-start | bytes 589828
  32.9 28.0 %copy-start.2 = (f32[1,64,768]{2,1,0:T(8,128)S(1)}, f32[1,64,768]{2,1,0:T(8,128)}, u32[]{:S(2)}) copy-start(f32[1,64,768]{2,1,0:T(8,128)} %refs_0_.2) | copy-start | bytes 589828
  32.9 28.0 %copy-start.5 = (f32[1,64,768]{2,1,0:T(8,128)S(1)}, f32[1,64,768]{2,1,0:T(8,128)}, u32[]{:S(2)}) copy-start(f32[1,64,768]{2,1,0:T(8,128)} %refs_1_.2) | copy-start | bytes 589828
  33.0 28.0 %copy-start.6 = (f32[1,64,768]{2,1,0:T(8,128)S(1)}, f32[1,64,768]{2,1,0:T(8,128)}, u32[]{:S(2)}) copy-start(f32[1,64,768]{2,1,0:T(8,128)} %refs_2_.2) | copy-start | bytes 589828
  42.2 5.9 %collective-permute-start.18 = (bf16[2,64,768]{2,1,0:T(8,128)(2,1)S(1)}, bf16[2,64,768]{2,1,0:T(8,128)(2,1)S(1)}, u32[]{:S(2)}, u32[]{:S(2)}) collective-permute-start(bf16[2,64,768]{2,1,0:T(8,128)(2,1)S(1)} %get-tuple-element.84), channel_id=1, source_target_pairs={{0,16},{8,24},{16,0},{24,8},{1,17},{9,25},{17,1},{25,9},{2,18},{10... | collective-permute-start | bytes 589832 | tf_op jit(solution)/shard_map/ppermute | solution.py:454
  43.0 9.7 %collective-permute-start.15 = (bf16[128,128]{1,0:T(8,128)(2,1)S(1)}, bf16[128,128]{1,0:T(8,128)(2,1)S(1)}, u32[]{:S(2)}, u32[]{:S(2)}) collective-permute-start(bf16[128,128]{1,0:T(8,128)(2,1)S(1)} %convert_element_type.147), channel_id=1, source_target_pairs={{0,2},{1,3},{2,0},{3,1},{4,6},{5,7},{6,4},{7,5},{8,10},{9,11},{10,... | collective-permute-start | bytes 98312 | tf_op jit(solution)/shard_map/ppermute | solution.py:454
  45.8 6.7 %collective-permute-start.13 = (bf16[2,64,768]{2,1,0:T(8,128)(2,1)S(1)}, bf16[2,64,768]{2,1,0:T(8,128)(2,1)S(1)}, u32[]{:S(2)}, u32[]{:S(2)}) collective-permute-start(bf16[2,64,768]{2,1,0:T(8,128)(2,1)S(1)} %get-tuple-element.85), channel_id=1, source_target_pairs={{0,1},{1,0},{2,3},{3,2},{4,5},{5,4},{6,7},{7,6},{8,9},{9,8},{10,11... | collective-permute-start | bytes 589832 | tf_op jit(solution)/shard_map/ppermute | solution.py:454
  48.1 8.7 %collective-permute-start.19 = (bf16[64,768]{1,0:T(8,128)(2,1)S(1)}, bf16[64,768]{1,0:T(8,128)(2,1)S(1)}, u32[]{:S(2)}, u32[]{:S(2)}) collective-permute-start(bf16[64,768]{1,0:T(8,128)(2,1)S(1)} %fusion.4), channel_id=1, source_target_pairs={{0,2},{1,3},{2,0},{3,1},{4,6},{5,7},{6,4},{7,5},{8,10},{9,11},{10,... | collective-permute-start | bytes 294920 | tf_op jit(solution)/shard_map/ppermute | solution.py:454
  52.6 8.3 %collective-permute-start.14 = (bf16[64,768]{1,0:T(8,128)(2,1)S(1)}, bf16[64,768]{1,0:T(8,128)(2,1)S(1)}, u32[]{:S(2)}, u32[]{:S(2)}) collective-permute-start(bf16[64,768]{1,0:T(8,128)(2,1)S(1)} %fusion.5), channel_id=1, source_target_pairs={{0,2},{1,3},{2,0},{3,1},{4,6},{5,7},{6,4},{7,5},{8,10},{9,11},{10,... | collective-permute-start | bytes 294920 | tf_op jit(solution)/shard_map/ppermute | solution.py:454
  52.7 4.0 %collective-permute-start.16 = (bf16[128,128]{1,0:T(8,128)(2,1)S(1)}, bf16[128,128]{1,0:T(8,128)(2,1)S(1)}, u32[]{:S(2)}, u32[]{:S(2)}) collective-permute-start(bf16[128,128]{1,0:T(8,128)(2,1)S(1)} %get-tuple-element.82), channel_id=1, source_target_pairs={{0,16},{8,24},{16,0},{24,8},{1,17},{9,25},{17,1},{25,9},{2,18},{10... | collective-permute-start | bytes 98312 | tf_op jit(solution)/shard_map/ppermute | solution.py:454
  58.0 5.7 %collective-permute-start.20 = (bf16[1,64,768]{2,1,0:T(8,128)(2,1)S(1)}, bf16[1,64,768]{2,1,0:T(8,128)(2,1)S(1)}, u32[]{:S(2)}, u32[]{:S(2)}) collective-permute-start(bf16[1,64,768]{2,1,0:T(8,128)(2,1)S(1)} %get-tuple-element.65), channel_id=1, source_target_pairs={{0,2},{1,3},{2,0},{3,1},{4,6},{5,7},{6,4},{7,5},{8,10},{9,11},{10,... | collective-permute-start | bytes 294920 | tf_op jit(solution)/shard_map/ppermute | solution.py:454
  62.2 5.5 %collective-permute-start.17 = (bf16[1,64,768]{2,1,0:T(8,128)(2,1)S(1)}, bf16[1,64,768]{2,1,0:T(8,128)(2,1)S(1)}, u32[]{:S(2)}, u32[]{:S(2)}) collective-permute-start(bf16[1,64,768]{2,1,0:T(8,128)(2,1)S(1)} %get-tuple-element.64), channel_id=1, source_target_pairs={{0,2},{1,3},{2,0},{3,1},{4,6},{5,7},{6,4},{7,5},{8,10},{9,11},{10,... | collective-permute-start | bytes 294920 | tf_op jit(solution)/shard_map/ppermute | solution.py:454
  62.2 8.5 %collective-permute-start.21 = (bf16[2,64,768]{2,1,0:T(8,128)(2,1)S(1)}, bf16[2,64,768]{2,1,0:T(8,128)(2,1)S(1)}, u32[]{:S(2)}, u32[]{:S(2)}) collective-permute-start(bf16[2,64,768]{2,1,0:T(8,128)(2,1)S(1)} %pad_maximum_fusion.6), channel_id=1, source_target_pairs={{4,0},{5,1},{6,2},{7,3},{12,8},{13,9},{14,10},{15,11},{20,16},{21,... | collective-permute-start | bytes 589832 | tf_op jit(solution)/shard_map/ppermute | solution.py:469
  63.7 8.4 %collective-permute-start.25 = (bf16[2,64,768]{2,1,0:T(8,128)(2,1)S(1)}, bf16[2,64,768]{2,1,0:T(8,128)(2,1)S(1)}, u32[]{:S(2)}, u32[]{:S(2)}) collective-permute-start(bf16[2,64,768]{2,1,0:T(8,128)(2,1)S(1)} %pad_maximum_fusion.9), channel_id=1, source_target_pairs={{0,16},{8,24},{16,0},{24,8},{1,17},{9,25},{17,1},{25,9},{2,18},{10... | collective-permute-start | bytes 589832 | tf_op jit(solution)/shard_map/ppermute | solution.py:454
  67.7 7.9 %collective-permute-start.23 = (bf16[2,64,768]{2,1,0:T(8,128)(2,1)S(1)}, bf16[2,64,768]{2,1,0:T(8,128)(2,1)S(1)}, u32[]{:S(2)}, u32[]{:S(2)}) collective-permute-start(bf16[2,64,768]{2,1,0:T(8,128)(2,1)S(1)} %pad_maximum_fusion.8), channel_id=1, source_target_pairs={{0,1},{1,0},{2,3},{3,2},{4,5},{5,4},{6,7},{7,6},{8,9},{9,8},{10,11... | collective-permute-start | bytes 589832 | tf_op jit(solution)/shard_map/ppermute | solution.py:454
  70.8 10.7 %collective-permute-start.22 = (bf16[2,64,768]{2,1,0:T(8,128)(2,1)S(1)}, bf16[2,64,768]{2,1,0:T(8,128)(2,1)S(1)}, u32[]{:S(2)}, u32[]{:S(2)}) collective-permute-start(bf16[2,64,768]{2,1,0:T(8,128)(2,1)S(1)} %pad_maximum_fusion.7), channel_id=1, source_target_pairs={{4,0},{5,1},{6,2},{7,3},{12,8},{13,9},{14,10},{15,11},{20,16},{21,... | collective-permute-start | bytes 589832 | tf_op jit(solution)/shard_map/ppermute | solution.py:469
  75.6 8.2 %collective-permute-start.26 = (bf16[4,64,768]{2,1,0:T(8,128)(2,1)S(1)}, bf16[4,64,768]{2,1,0:T(8,128)(2,1)S(1)}, u32[]{:S(2)}, u32[]{:S(2)}) collective-permute-start(bf16[4,64,768]{2,1,0:T(8,128)(2,1)S(1)} %pad_maximum_fusion.1), channel_id=1, source_target_pairs={{0,1},{1,0},{2,3},{3,2},{4,5},{5,4},{6,7},{7,6},{8,9},{9,8},{10,11... | collective-permute-start | bytes 1179656 | tf_op jit(solution)/shard_map/ppermute | solution.py:454
  78.1 7.8 %collective-permute-start.24 = (bf16[4,64,768]{2,1,0:T(8,128)(2,1)S(1)}, bf16[4,64,768]{2,1,0:T(8,128)(2,1)S(1)}, u32[]{:S(2)}, u32[]{:S(2)}) collective-permute-start(bf16[4,64,768]{2,1,0:T(8,128)(2,1)S(1)} %pad_maximum_fusion), channel_id=1, source_target_pairs={{0,16},{8,24},{16,0},{24,8},{1,17},{9,25},{17,1},{25,9},{2,18},{10... | collective-permute-start | bytes 1179656 | tf_op jit(solution)/shard_map/ppermute | solution.py:454
  80.0 11.8 %collective-permute-start.27 = (bf16[4,64,768]{2,1,0:T(8,128)(2,1)S(1)}, bf16[4,64,768]{2,1,0:T(8,128)(2,1)S(1)}, u32[]{:S(2)}, u32[]{:S(2)}) collective-permute-start(bf16[4,64,768]{2,1,0:T(8,128)(2,1)S(1)} %pad_maximum_fusion.2), channel_id=1, source_target_pairs={{4,0},{5,1},{6,2},{7,3},{12,8},{13,9},{14,10},{15,11},{20,16},{21,... | collective-permute-start | bytes 1179656 | tf_op jit(solution)/shard_map/ppermute | solution.py:469
  81.4 18.0 %collective-permute-start.32 = (bf16[8,64,768]{2,1,0:T(8,128)(2,1)S(1)}, bf16[8,64,768]{2,1,0:T(8,128)(2,1)S(1)}, u32[]{:S(2)}, u32[]{:S(2)}) collective-permute-start(bf16[8,64,768]{2,1,0:T(8,128)(2,1)S(1)} %constant_dynamic-update-slice_fusion.3.refs_0_), channel_id=1, source_target_pairs={{0,8},{8,0},{16,24},{24,16},{1,9},{9,1},{17,25},{25,17},{2,10},{10... | collective-permute-start | bytes 2359304 | tf_op jit(solution)/shard_map/ppermute | solution.py:454
  86.0 13.0 %collective-permute-start.30 = (bf16[2,64,768]{2,1,0:T(8,128)(2,1)S(1)}, bf16[2,64,768]{2,1,0:T(8,128)(2,1)S(1)}, u32[]{:S(2)}, u32[]{:S(2)}) collective-permute-start(bf16[2,64,768]{2,1,0:T(8,128)(2,1)S(1)} %pad_maximum_fusion.10), channel_id=1, source_target_pairs={{4,0},{5,1},{6,2},{7,3},{12,8},{13,9},{14,10},{15,11},{20,16},{21,... | collective-permute-start | bytes 589832 | tf_op jit(solution)/shard_map/ppermute | solution.py:469
  91.9 6.8 %collective-permute-start.28 = (bf16[3,64,768]{2,1,0:T(8,128)(2,1)S(1)}, bf16[3,64,768]{2,1,0:T(8,128)(2,1)S(1)}, u32[]{:S(2)}, u32[]{:S(2)}) collective-permute-start(bf16[3,64,768]{2,1,0:T(8,128)(2,1)S(1)} %pad_maximum_fusion.3), channel_id=1, source_target_pairs={{0,16},{8,24},{16,0},{24,8},{1,17},{9,25},{17,1},{25,9},{2,18},{10... | collective-permute-start | bytes 884744 | tf_op jit(solution)/shard_map/ppermute | solution.py:454
  92.1 6.8 %collective-permute-start.29 = (bf16[3,64,768]{2,1,0:T(8,128)(2,1)S(1)}, bf16[3,64,768]{2,1,0:T(8,128)(2,1)S(1)}, u32[]{:S(2)}, u32[]{:S(2)}) collective-permute-start(bf16[3,64,768]{2,1,0:T(8,128)(2,1)S(1)} %pad_maximum_fusion.4), channel_id=1, source_target_pairs={{0,1},{1,0},{2,3},{3,2},{4,5},{5,4},{6,7},{7,6},{8,9},{9,8},{10,11... | collective-permute-start | bytes 884744 | tf_op jit(solution)/shard_map/ppermute | solution.py:454
  92.5 6.9 %collective-permute-start.33 = (bf16[8,64,768]{2,1,0:T(8,128)(2,1)S(1)}, bf16[8,64,768]{2,1,0:T(8,128)(2,1)S(1)}, u32[]{:S(2)}, u32[]{:S(2)}) collective-permute-start(bf16[8,64,768]{2,1,0:T(8,128)(2,1)S(1)} %constant_dynamic-update-slice_fusion.9.refs_2_), channel_id=1, source_target_pairs={{0,8},{8,0},{16,24},{24,16},{1,9},{9,1},{17,25},{25,17},{2,10},{10... | collective-permute-start | bytes 2359304 | tf_op jit(solution)/shard_map/ppermute | solution.py:454
  98.7 2.3 %collective-permute-start.34 = (bf16[8,64,768]{2,1,0:T(8,128)(2,1)S(1)}, bf16[8,64,768]{2,1,0:T(8,128)(2,1)S(1)}, u32[]{:S(2)}, u32[]{:S(2)}) collective-permute-start(bf16[8,64,768]{2,1,0:T(8,128)(2,1)S(1)} %constant_dynamic-update-slice_fusion.11.refs_4_), channel_id=1, source_target_pairs={{0,8},{8,0},{16,24},{24,16},{1,9},{9,1},{17,25},{25,17},{2,10},{10... | collective-permute-start | bytes 2359304 | tf_op jit(solution)/shard_map/ppermute | solution.py:454
  99.0 4.3 %collective-permute-start.31 = (bf16[8,64,768]{2,1,0:T(8,128)(2,1)S(1)}, bf16[8,64,768]{2,1,0:T(8,128)(2,1)S(1)}, u32[]{:S(2)}, u32[]{:S(2)}) collective-permute-start(bf16[8,64,768]{2,1,0:T(8,128)(2,1)S(1)} %constant_dynamic-update-slice_fusion.refs_0_), channel_id=1, source_target_pairs={{0,8},{8,0},{16,24},{24,16},{1,9},{9,1},{17,25},{25,17},{2,10},{10... | collective-permute-start | bytes 2359304 | tf_op jit(solution)/shard_map/ppermute | solution.py:454

commit v9 on v8

--- a/solution.py
+++ b/solution.py
@@ -492,15 +492,15 @@
     down_one = swapped(part(0, whole), "replica", 2)
     up_one = swapped(part(1, whole), "tensor", 1)
     near, kept = halves(0)
+    mixed = added("tensor", 1)
     mixed = added("replica", 1)
-    mixed = added("tensor", 1)
+    mixed = added("tensor", 2)
     down_one, up_one, mixed = lax.optimization_barrier((down_one, up_one, mixed))
     down_two = swapped(part(0, low, down_one[2:]), "tensor", 1)
     up_two = swapped(part(1, low, up_one[2:]), "replica", 2)
     down_last = swapped(part(0, 1, down_one[1], down_two[1]), "tensor", 2)
     kept, near = lax.optimization_barrier((kept, near))
     up_last = swapped(part(1, 1, up_one[1], up_two[1]), "tensor", 2)
-    mixed = added("tensor", 2)
     other = swapped(mixed.astype(bf16), "replica", 2)
     down = (kept, near, down_one, down_two, down_last, mixed, other)
     return down, (kept, near, up_one, up_two, up_last, mixed, other)
@@ -546,8 +546,7 @@
     down_two = crossed(downs, "tensor", 1)
     up_two = crossed(ups, "replica", 2)
     next_one = fetched(one)
-    twos = lax.optimization_barrier((down_two[1], up_two[1]))
-    two = joined((down_two[0], twos[0]), (up_two[0], twos[1]))
+    two = joined(down_two, up_two)
     down_three = crossed(joined(downs, down_two), "replica", 2)
     up_three = crossed(joined(ups, up_two), "tensor", 1)
     next_two = fetched(two)

time: 105 us -> 105 us (level)
  starting transfers between devices: 43.2 us -> 37.2 us
  waiting for transfers between devices: 41.2 us -> 46.8 us
    ppermute x4, waiting for transfers between devices: 4.58 us -> 11.3 us  [following_layer(): return lax.ppermute(block, 'section', [(i + 1, i) for i in range(size - 1)])]
    ppermute x29, starting transfers between devices: 34.3 us -> 28.4 us  [swapped(): return lax.ppermute(block, axis, route)]
    ppermute x29, waiting for transfers between devices: 36.6 us -> 35.5 us  [swapped(): return lax.ppermute(block, axis, route)]
where the time goes in v9:
time: 105 us; the launch traced here: 104 us
  waiting for transfers between devices  46.8 us (45%)
  starting transfers between devices  37.2 us (35%)
  Pallas kernels  16.9 us (16%)
  other arithmetic  1.85 us (2%)
  between operations  1.12 us (1%)
    ppermute x29, waiting for transfers between devices, swapped(): return lax.ppermute(block, axis, route)  35.5 us
    ppermute x29, starting transfers between devices, swapped(): return lax.ppermute(block, axis, route)  28.4 us
    ppermute x4, waiting for transfers between devices, following_layer(): return lax.ppermute(block, 'section', [(i + 1, i) for i in range(size - 1)])  11.3 us
    pallas_call x1, Pallas kernels, project(): pl.pallas_call(functools.partial(project_kernel, steps), in_specs=[in_hbm...  5.99 us
    ppermute x4, starting transfers between devices, following_layer(): return lax.ppermute(block, 'section', [(i + 1, i) for i in range(size - 1)])  5.17 us
    ppermute x2, starting transfers between devices, from_next(): return lax.ppermute(block, 'section', route)  3.69 us
    pallas_call x2, Pallas kernels, place(): pl.pallas_call(functools.partial(place_kernel, layout, not before), in_sp...  3.56 us
    pallas_call x2, Pallas kernels, update(): pl.pallas_call(functools.partial(update_kernel, which), in_specs=[in_vmem...  2.5 us
  transfers between devices with their start and end apart: 35, of which 21 were waited for; matrix products, arithmetic and copies ran while one was open for 1% of the time, Pallas kernels for 13%

profile of v9, /device:TPU:0, one launch (start us, length us, event | category | flops | bytes accessed | tf_op | source)
XLA Modules:
  0.0 104.3 jit_solution(8843805226264669646)
XLA Ops:
  0.6 1.0 %convert_bitcast_fusion = (bf16[64,768]{1,0:T(8,128)(2,1)S(1)}, bf16[64,768]{1,0:T(8,128)(2,1)S(1)}) fusion(f32[1,64,768]{2,1,0:T(8,128)} %refs_0_.3, f32[1,64,768]{2,1,0:T(8,128)} %refs_0_.2), kind=kLoop, calls=%fused_computation.27 | loop fusion | flops 98304 | bytes 589824 | tf_op jit(solution)/shard_map/squeeze | solution.py:596
  1.7 3.0 %collective-permute-start = (bf16[128,768]{1,0:T(8,128)(2,1)S(1)}, bf16[128,768]{1,0:T(8,128)(2,1)S(1)}, u32[]{:S(2)}, u32[]{:S(2)}) collective-permute-start(bf16[128,768]{1,0:T(8,128)(2,1)S(1)} %pad_maximum_fusion.5.refs_0_), channel_id=1, source_target_pairs={{4,0},{0,4},{5,1},{1,5},{6,2},{2,6},{7,3},{3,7},{12,8},{8,12},{13,... | collective-permute-start | bytes 589832 | tf_op jit(solution)/shard_map/ppermute | solution.py:464
  4.7 6.0 %project.1 = (f32[128,256]{1,0:T(8,128)S(1)}, f32[128,128]{1,0:T(8,128)S(1)}, bf16[128,12288]{1,0:T(8,128)(2,1)S(1)}, bf16[128,12288]{1,0:T(8,128)(2,1)S(1)}) custom-call(bf16[128,12288]{1,0:T(8,128)(2,1)} %bitcast.52, bf16[2,64,12288]{2,1,0:T(8,128)(2,1)} %bitcast.53, bf16[2,64,12288]{2,1,0:T(8,128)(2,1)} %bitcast.54), custom_call_target="tpu_custom_call" | custom-call | flops 805306368 | bytes 9437184 | tf_op jit(solution)/shard_map/project/pallas_call | solution.py:98
  10.9 0.7 collective-permute-start.4
  11.7 0.9 collective-permute-start.3
  12.8 1.0 project_back.1.refs_0_
  14.6 1.3 %collective-permute-done.3 = f32[64,128]{1,0:T(8,128)S(1)} collective-permute-done((f32[64,128]{1,0:T(8,128)S(1)}, f32[64,128]{1,0:T(8,128)S(1)}, u32[]{:S(2)}, u32[]{:S(2)}) %collective-permute-start.3) | collective-permute-done | bytes 32800 | tf_op jit(solution)/shard_map/ppermute | solution.py:454
  15.9 1.6 %collective-permute-start.5 = (f32[64,128]{1,0:T(8,128)S(1)}, f32[64,128]{1,0:T(8,128)S(1)}, u32[]{:S(2)}, u32[]{:S(2)}) collective-permute-start(f32[64,128]{1,0:T(8,128)S(1)} %add_add_fusion), channel_id=1, source_target_pairs={{0,1},{1,0},{2,3},{3,2},{4,5},{5,4},{6,7},{7,6},{8,9},{9,8},{10,11... | collective-permute-start | bytes 98312 | tf_op jit(solution)/shard_map/ppermute | solution.py:454
  17.6 2.3 %collective-permute-done.5 = f32[64,128]{1,0:T(8,128)S(1)} collective-permute-done((f32[64,128]{1,0:T(8,128)S(1)}, f32[64,128]{1,0:T(8,128)S(1)}, u32[]{:S(2)}, u32[]{:S(2)}) %collective-permute-start.5) | collective-permute-done | bytes 32800 | tf_op jit(solution)/shard_map/ppermute | solution.py:454
  19.9 2.6 %collective-permute-start.6 = (f32[64,128]{1,0:T(8,128)S(1)}, f32[64,128]{1,0:T(8,128)S(1)}, u32[]{:S(2)}, u32[]{:S(2)}) collective-permute-start(f32[64,128]{1,0:T(8,128)S(1)} %add.74.refs_2_), channel_id=1, source_target_pairs={{0,2},{1,3},{2,0},{3,1},{4,6},{5,7},{6,4},{7,5},{8,10},{9,11},{10,... | collective-permute-start | bytes 98312 | tf_op jit(solution)/shard_map/ppermute | solution.py:454
  22.5 2.2 %collective-permute-done.6.refs_3_ = f32[64,128]{1,0:T(8,128)S(1)} collective-permute-done((f32[64,128]{1,0:T(8,128)S(1)}, f32[64,128]{1,0:T(8,128)S(1)}, u32[]{:S(2)}, u32[]{:S(2)}) %collective-permute-start.6) | collective-permute-done | bytes 32800 | tf_op jit(solution)/shard_map/ppermute | solution.py:454
  24.7 1.7 %chain.1 = (bf16[128,256]{1,0:T(8,128)(2,1)S(1)}, f32[128,128]{1,0:T(8,128)S(1)}) custom-call(s32[4,3]{1,0:T(4,128)S(1)} %copy-done.7, s32[1,4]{1,0:T(1,128)S(1)} %bitcast.49, f32[128,384]{1,0:T(8,128)S(1)} %project_back.1.refs_0_, f32[128,384]{1,0:T(8,128)S(1)} %collective-permute-done.1.refs_1_, f32[64,128]{1,0:T(8,128)S(1)} %add.74.refs_2_, ...), custom_call_target="tpu_custom_call" | custom-call | tf_op jit(solution)/shard_map/chain/pallas_call | solution.py:298
  27.1 1.6 %collective-permute-start.11 = (bf16[128,128]{1,0:T(8,128)(2,1)S(1)}, bf16[128,128]{1,0:T(8,128)(2,1)S(1)}, u32[]{:S(2)}, u32[]{:S(2)}) collective-permute-start(bf16[128,128]{1,0:T(8,128)(2,1)S(1)} %convert_element_type.132), channel_id=1, source_target_pairs={{0,1},{1,0},{2,3},{3,2},{4,5},{5,4},{6,7},{7,6},{8,9},{9,8},{10,11... | collective-permute-start | bytes 98312 | tf_op jit(solution)/shard_map/ppermute | solution.py:454
  29.9 1.1 %collective-permute-done.11 = bf16[128,128]{1,0:T(8,128)(2,1)S(1)} collective-permute-done((bf16[128,128]{1,0:T(8,128)(2,1)S(1)}, bf16[128,128]{1,0:T(8,128)(2,1)S(1)}, u32[]{:S(2)}, u32[]{:S(2)}) %collective-permute-start.11) | collective-permute-done | bytes 32800 | tf_op jit(solution)/shard_map/ppermute | solution.py:454
  31.3 1.6 %collective-permute-start.10 = (bf16[4,64,768]{2,1,0:T(8,128)(2,1)S(1)}, bf16[4,64,768]{2,1,0:T(8,128)(2,1)S(1)}, u32[]{:S(2)}, u32[]{:S(2)}) collective-permute-start(bf16[4,64,768]{2,1,0:T(8,128)(2,1)S(1)} %get-tuple-element.80), channel_id=1, source_target_pairs={{0,1},{1,0},{2,3},{3,2},{4,5},{5,4},{6,7},{7,6},{8,9},{9,8},{10,11... | collective-permute-start | bytes 1179656 | tf_op jit(solution)/shard_map/ppermute | solution.py:454
  33.8 2.9 %collective-permute-start.13 = (bf16[128,128]{1,0:T(8,128)(2,1)S(1)}, bf16[128,128]{1,0:T(8,128)(2,1)S(1)}, u32[]{:S(2)}, u32[]{:S(2)}) collective-permute-start(bf16[128,128]{1,0:T(8,128)(2,1)S(1)} %fusion.7), channel_id=1, source_target_pairs={{0,2},{1,3},{2,0},{3,1},{4,6},{5,7},{6,4},{7,5},{8,10},{9,11},{10,... | collective-permute-start | bytes 98312 | tf_op jit(solution)/shard_map/ppermute | solution.py:454
  37.2 5.5 %collective-permute-done.13 = bf16[128,128]{1,0:T(8,128)(2,1)S(1)} collective-permute-done((bf16[128,128]{1,0:T(8,128)(2,1)S(1)}, bf16[128,128]{1,0:T(8,128)(2,1)S(1)}, u32[]{:S(2)}, u32[]{:S(2)}) %collective-permute-start.13) | collective-permute-done | bytes 32800 | tf_op jit(solution)/shard_map/ppermute | solution.py:454
  42.7 0.9 collective-permute-done.10.one
  44.4 0.8 collective-permute-start.18
  45.1 2.1 %collective-permute-start.14 = (bf16[2,64,768]{2,1,0:T(8,128)(2,1)S(1)}, bf16[2,64,768]{2,1,0:T(8,128)(2,1)S(1)}, u32[]{:S(2)}, u32[]{:S(2)}) collective-permute-start(bf16[2,64,768]{2,1,0:T(8,128)(2,1)S(1)} %get-tuple-element.79), channel_id=1, source_target_pairs={{0,1},{1,0},{2,3},{3,2},{4,5},{5,4},{6,7},{7,6},{8,9},{9,8},{10,11... | collective-permute-start | bytes 589832 | tf_op jit(solution)/shard_map/ppermute | solution.py:454
  47.3 3.3 %collective-permute-done.18.two = bf16[2,64,768]{2,1,0:T(8,128)(2,1)S(1)} collective-permute-done((bf16[2,64,768]{2,1,0:T(8,128)(2,1)S(1)}, bf16[2,64,768]{2,1,0:T(8,128)(2,1)S(1)}, u32[]{:S(2)}, u32[]{:S(2)}) %collective-permute-start.18) | collective-permute-done | bytes 196640 | tf_op jit(solution)/shard_map/ppermute | solution.py:454
  50.7 2.9 %collective-permute-start.19 = (bf16[64,768]{1,0:T(8,128)(2,1)S(1)}, bf16[64,768]{1,0:T(8,128)(2,1)S(1)}, u32[]{:S(2)}, u32[]{:S(2)}) collective-permute-start(bf16[64,768]{1,0:T(8,128)(2,1)S(1)} %fusion.4), channel_id=1, source_target_pairs={{0,2},{1,3},{2,0},{3,1},{4,6},{5,7},{6,4},{7,5},{8,10},{9,11},{10,... | collective-permute-start | bytes 294920 | tf_op jit(solution)/shard_map/ppermute | solution.py:454
  54.0 1.3 %collective-permute-start.16 = (bf16[128,128]{1,0:T(8,128)(2,1)S(1)}, bf16[128,128]{1,0:T(8,128)(2,1)S(1)}, u32[]{:S(2)}, u32[]{:S(2)}) collective-permute-start(bf16[128,128]{1,0:T(8,128)(2,1)S(1)} %convert_element_type.149), channel_id=1, source_target_pairs={{0,16},{8,24},{16,0},{24,8},{1,17},{9,25},{17,1},{25,9},{2,18},{10... | collective-permute-start | bytes 98312 | tf_op jit(solution)/shard_map/ppermute | solution.py:454
  55.3 2.6 %collective-permute-done.16.other_ref = bf16[128,128]{1,0:T(8,128)(2,1)S(1)} collective-permute-done((bf16[128,128]{1,0:T(8,128)(2,1)S(1)}, bf16[128,128]{1,0:T(8,128)(2,1)S(1)}, u32[]{:S(2)}, u32[]{:S(2)}) %collective-permute-start.16) | collective-permute-done | bytes 32800 | tf_op jit(solution)/shard_map/ppermute | solution.py:454
  57.9 3.5 %collective-permute-done.19.last = bf16[64,768]{1,0:T(8,128)(2,1)S(1)} collective-permute-done((bf16[64,768]{1,0:T(8,128)(2,1)S(1)}, bf16[64,768]{1,0:T(8,128)(2,1)S(1)}, u32[]{:S(2)}, u32[]{:S(2)}) %collective-permute-start.19) | collective-permute-done | bytes 98336 | tf_op jit(solution)/shard_map/ppermute | solution.py:454
  61.4 1.3 %update.3 = (f32[1,64,768]{2,1,0:T(8,128)}, f32[1,64,768]{2,1,0:T(8,128)}, f32[1,64,768]{2,1,0:T(8,128)}, bf16[1,64,768]{2,1,0:T(8,128)(2,1)S(1)}) custom-call(bf16[2,4,64,768]{3,2,1,0:T(8,128)(2,1)S(1)} %gradient.4.kept, bf16[2,4,64,768]{3,2,1,0:T(8,128)(2,1)S(1)} %collective-permute-done.7.near, bf16[4,64,768]{2,1,0:T(8,128)(2,1)S(1)} %collective-permute-done.10.one, ...), custom_call_target="tpu_custom_call" | custom-call | tf_op jit(solution)/shard_map/update/pallas_call | solution.py:374
  62.6 0.8 collective-permute-done.15.last
  63.5 1.3 %update.2 = (f32[1,64,768]{2,1,0:T(8,128)}, f32[1,64,768]{2,1,0:T(8,128)}, f32[1,64,768]{2,1,0:T(8,128)}, bf16[1,64,768]{2,1,0:T(8,128)(2,1)S(1)}) custom-call(bf16[2,4,64,768]{3,2,1,0:T(8,128)(2,1)S(1)} %gradient.4.kept, bf16[2,4,64,768]{3,2,1,0:T(8,128)(2,1)S(1)} %collective-permute-done.7.near, bf16[4,64,768]{2,1,0:T(8,128)(2,1)S(1)} %collective-permute-done.9.one, ...), custom_call_target="tpu_custom_call" | custom-call | tf_op jit(solution)/shard_map/update/pallas_call | solution.py:374
  64.7 2.1 %collective-permute-start.17 = (bf16[1,64,768]{2,1,0:T(8,128)(2,1)S(1)}, bf16[1,64,768]{2,1,0:T(8,128)(2,1)S(1)}, u32[]{:S(2)}, u32[]{:S(2)}) collective-permute-start(bf16[1,64,768]{2,1,0:T(8,128)(2,1)S(1)} %get-tuple-element.62), channel_id=1, source_target_pairs={{0,2},{1,3},{2,0},{3,1},{4,6},{5,7},{6,4},{7,5},{8,10},{9,11},{10,... | collective-permute-start | bytes 294920 | tf_op jit(solution)/shard_map/ppermute | solution.py:454
  66.9 1.3 %collective-permute-start.21 = (bf16[2,64,768]{2,1,0:T(8,128)(2,1)S(1)}, bf16[2,64,768]{2,1,0:T(8,128)(2,1)S(1)}, u32[]{:S(2)}, u32[]{:S(2)}) collective-permute-start(bf16[2,64,768]{2,1,0:T(8,128)(2,1)S(1)} %pad_maximum_fusion.6), channel_id=1, source_target_pairs={{4,0},{5,1},{6,2},{7,3},{12,8},{13,9},{14,10},{15,11},{20,16},{21,... | collective-permute-start | bytes 589832 | tf_op jit(solution)/shard_map/ppermute | solution.py:469
  68.2 1.8 %collective-permute-done.20 = bf16[1,64,768]{2,1,0:T(8,128)(2,1)S(1)} collective-permute-done((bf16[1,64,768]{2,1,0:T(8,128)(2,1)S(1)}, bf16[1,64,768]{2,1,0:T(8,128)(2,1)S(1)}, u32[]{:S(2)}, u32[]{:S(2)}) %collective-permute-start.20) | collective-permute-done | bytes 98336 | tf_op jit(solution)/shard_map/ppermute | solution.py:454
  70.0 0.8 collective-permute-start.25
  70.8 1.3 %collective-permute-done.17 = bf16[1,64,768]{2,1,0:T(8,128)(2,1)S(1)} collective-permute-done((bf16[1,64,768]{2,1,0:T(8,128)(2,1)S(1)}, bf16[1,64,768]{2,1,0:T(8,128)(2,1)S(1)}, u32[]{:S(2)}, u32[]{:S(2)}) %collective-permute-start.17) | collective-permute-done | bytes 98336 | tf_op jit(solution)/shard_map/ppermute | solution.py:454
  72.2 2.2 %collective-permute-done.21 = bf16[2,64,768]{2,1,0:T(8,128)(2,1)S(1)} collective-permute-done((bf16[2,64,768]{2,1,0:T(8,128)(2,1)S(1)}, bf16[2,64,768]{2,1,0:T(8,128)(2,1)S(1)}, u32[]{:S(2)}, u32[]{:S(2)}) %collective-permute-start.21) | collective-permute-done | bytes 196640 | tf_op jit(solution)/shard_map/ppermute | solution.py:469
  74.4 1.3 %collective-permute-start.22 = (bf16[2,64,768]{2,1,0:T(8,128)(2,1)S(1)}, bf16[2,64,768]{2,1,0:T(8,128)(2,1)S(1)}, u32[]{:S(2)}, u32[]{:S(2)}) collective-permute-start(bf16[2,64,768]{2,1,0:T(8,128)(2,1)S(1)} %pad_maximum_fusion.7), channel_id=1, source_target_pairs={{4,0},{5,1},{6,2},{7,3},{12,8},{13,9},{14,10},{15,11},{20,16},{21,... | collective-permute-start | bytes 589832 | tf_op jit(solution)/shard_map/ppermute | solution.py:469
  75.8 2.0 %collective-permute-done.23 = bf16[2,64,768]{2,1,0:T(8,128)(2,1)S(1)} collective-permute-done((bf16[2,64,768]{2,1,0:T(8,128)(2,1)S(1)}, bf16[2,64,768]{2,1,0:T(8,128)(2,1)S(1)}, u32[]{:S(2)}, u32[]{:S(2)}) %collective-permute-start.23) | collective-permute-done | bytes 196640 | tf_op jit(solution)/shard_map/ppermute | solution.py:454
  78.0 1.3 %collective-permute-start.27 = (bf16[4,64,768]{2,1,0:T(8,128)(2,1)S(1)}, bf16[4,64,768]{2,1,0:T(8,128)(2,1)S(1)}, u32[]{:S(2)}, u32[]{:S(2)}) collective-permute-start(bf16[4,64,768]{2,1,0:T(8,128)(2,1)S(1)} %get-tuple-element.88), channel_id=1, source_target_pairs={{4,0},{5,1},{6,2},{7,3},{12,8},{13,9},{14,10},{15,11},{20,16},{21,... | collective-permute-start | bytes 1179656 | tf_op jit(solution)/shard_map/ppermute | solution.py:469
  79.3 0.8 collective-permute-start.24
  80.1 0.9 collective-permute-start.26
  81.0 3.1 %collective-permute-done.22 = bf16[2,64,768]{2,1,0:T(8,128)(2,1)S(1)} collective-permute-done((bf16[2,64,768]{2,1,0:T(8,128)(2,1)S(1)}, bf16[2,64,768]{2,1,0:T(8,128)(2,1)S(1)}, u32[]{:S(2)}, u32[]{:S(2)}) %collective-permute-start.22) | collective-permute-done | bytes 196640 | tf_op jit(solution)/shard_map/ppermute | solution.py:469
  84.2 6.0 %collective-permute-done.27 = bf16[4,64,768]{2,1,0:T(8,128)(2,1)S(1)} collective-permute-done((bf16[4,64,768]{2,1,0:T(8,128)(2,1)S(1)}, bf16[4,64,768]{2,1,0:T(8,128)(2,1)S(1)}, u32[]{:S(2)}, u32[]{:S(2)}) %collective-permute-start.27) | collective-permute-done | bytes 393248 | tf_op jit(solution)/shard_map/ppermute | solution.py:469
  90.3 1.3 %collective-permute-start.30 = (bf16[2,64,768]{2,1,0:T(8,128)(2,1)S(1)}, bf16[2,64,768]{2,1,0:T(8,128)(2,1)S(1)}, u32[]{:S(2)}, u32[]{:S(2)}) collective-permute-start(bf16[2,64,768]{2,1,0:T(8,128)(2,1)S(1)} %pad_maximum_fusion.10), channel_id=1, source_target_pairs={{4,0},{5,1},{6,2},{7,3},{12,8},{13,9},{14,10},{15,11},{20,16},{21,... | collective-permute-start | bytes 589832 | tf_op jit(solution)/shard_map/ppermute | solution.py:469
  91.6 0.8 collective-permute-start.28
  92.4 1.9 %collective-permute-start.29 = (bf16[3,64,768]{2,1,0:T(8,128)(2,1)S(1)}, bf16[3,64,768]{2,1,0:T(8,128)(2,1)S(1)}, u32[]{:S(2)}, u32[]{:S(2)}) collective-permute-start(bf16[3,64,768]{2,1,0:T(8,128)(2,1)S(1)} %pad_maximum_fusion.4), channel_id=1, source_target_pairs={{0,1},{1,0},{2,3},{3,2},{4,5},{5,4},{6,7},{7,6},{8,9},{9,8},{10,11... | collective-permute-start | bytes 884744 | tf_op jit(solution)/shard_map/ppermute | solution.py:454
  94.5 3.9 %collective-permute-done.28 = bf16[3,64,768]{2,1,0:T(8,128)(2,1)S(1)} collective-permute-done((bf16[3,64,768]{2,1,0:T(8,128)(2,1)S(1)}, bf16[3,64,768]{2,1,0:T(8,128)(2,1)S(1)}, u32[]{:S(2)}, u32[]{:S(2)}) %collective-permute-start.28) | collective-permute-done | bytes 294944 | tf_op jit(solution)/shard_map/ppermute | solution.py:454
  98.4 1.4 %collective-permute-done.29 = bf16[3,64,768]{2,1,0:T(8,128)(2,1)S(1)} collective-permute-done((bf16[3,64,768]{2,1,0:T(8,128)(2,1)S(1)}, bf16[3,64,768]{2,1,0:T(8,128)(2,1)S(1)}, u32[]{:S(2)}, u32[]{:S(2)}) %collective-permute-start.29) | collective-permute-done | bytes 294944 | tf_op jit(solution)/shard_map/ppermute | solution.py:454
  100.7 2.3 %place.2 = (bf16[2,64,12288]{2,1,0:T(8,128)(2,1)}, bf16[2,64,12288]{2,1,0:T(8,128)(2,1)}) custom-call(s32[4,3]{1,0:T(4,128)S(1)} %copy-done.7, bf16[8,64,768]{2,1,0:T(8,128)(2,1)S(1)} %constant_dynamic-update-slice_fusion.3.refs_0_, bf16[8,64,768]{2,1,0:T(8,128)(2,1)S(1)} %collective-permute-done.32.refs_1_, ...), custom_call_target="tpu_custom_call" | custom-call | bytes 9437184 | tf_op jit(solution)/shard_map/place/pallas_call | solution.py:435
  103.0 1.3 %place.3 = (bf16[2,64,12288]{2,1,0:T(8,128)(2,1)}, bf16[2,64,12288]{2,1,0:T(8,128)(2,1)}) custom-call(s32[4,3]{1,0:T(4,128)S(1)} %copy-done.7, bf16[8,64,768]{2,1,0:T(8,128)(2,1)S(1)} %constant_dynamic-update-slice_fusion.refs_0_, bf16[8,64,768]{2,1,0:T(8,128)(2,1)S(1)} %collective-permute-done.31.refs_1_, ...), custom_call_target="tpu_custom_call", output_to_operand_aliasing={{0}: (3, {}), {1}: (4, {})} | custom-call | bytes 3145728 | tf_op jit(solution)/shard_map/place/pallas_call | solution.py:435
  (92 shorter events, 7.4 us)
Async XLA Ops:
  1.7 9.0 %collective-permute-start = (bf16[128,768]{1,0:T(8,128)(2,1)S(1)}, bf16[128,768]{1,0:T(8,128)(2,1)S(1)}, u32[]{:S(2)}, u32[]{:S(2)}) collective-permute-start(bf16[128,768]{1,0:T(8,128)(2,1)S(1)} %pad_maximum_fusion.5.refs_0_), channel_id=1, source_target_pairs={{4,0},{0,4},{5,1},{1,5},{6,2},{2,6},{7,3},{3,7},{12,8},{8,12},{13,... | collective-permute-start | bytes 589832 | tf_op jit(solution)/shard_map/ppermute | solution.py:464
  4.7 8.1 %copy-start = (bf16[1,4,32,12288]{3,2,1,0:T(8,128)(2,1)S(1)}, bf16[1,4,32,12288]{3,2,1,0:T(8,128)(2,1)}, u32[]{:S(2)}) copy-start(bf16[1,4,32,12288]{3,2,1,0:T(8,128)(2,1)} %param.13) | copy-start | bytes 9437188
  4.7 8.1 %copy-start.8 = (s32[4]{0:T(128)S(1)}, s32[4]{0:T(128)}, u32[]{:S(2)}) copy-start(s32[4]{0:T(128)} %param.14) | copy-start | bytes 52
  10.9 3.7 %collective-permute-start.4 = (f32[64,128]{1,0:T(8,128)S(1)}, f32[64,128]{1,0:T(8,128)S(1)}, u32[]{:S(2)}, u32[]{:S(2)}) collective-permute-start(f32[64,128]{1,0:T(8,128)S(1)} %get-tuple-element.49), channel_id=1, source_target_pairs={{0,24},{8,16},{16,8},{24,0},{1,25},{9,17},{17,9},{25,1},{2,26},{10... | collective-permute-start | bytes 98312 | tf_op jit(solution)/shard_map/ppermute | solution.py:454
  11.7 4.2 %collective-permute-start.3 = (f32[64,128]{1,0:T(8,128)S(1)}, f32[64,128]{1,0:T(8,128)S(1)}, u32[]{:S(2)}, u32[]{:S(2)}) collective-permute-start(f32[64,128]{1,0:T(8,128)S(1)} %get-tuple-element.49), channel_id=1, source_target_pairs={{0,16},{8,24},{16,0},{24,8},{1,17},{9,25},{17,1},{25,9},{2,18},{10... | collective-permute-start | bytes 98312 | tf_op jit(solution)/shard_map/ppermute | solution.py:454
  12.6 3.3 %collective-permute-start.2 = (f32[64,128]{1,0:T(8,128)S(1)}, f32[64,128]{1,0:T(8,128)S(1)}, u32[]{:S(2)}, u32[]{:S(2)}) collective-permute-start(f32[64,128]{1,0:T(8,128)S(1)} %get-tuple-element.49), channel_id=1, source_target_pairs={{0,8},{8,0},{16,24},{24,16},{1,9},{9,1},{17,25},{25,17},{2,10},{10... | collective-permute-start | bytes 98312 | tf_op jit(solution)/shard_map/ppermute | solution.py:454
  12.8 11.9 %copy-start.7 = (s32[4,3]{1,0:T(4,128)S(1)}, s32[4,3]{1,0:T(4,128)}, u32[]{:S(2)}) copy-start(s32[4,3]{1,0:T(4,128)} %bounds.5) | copy-start | bytes 148
  13.8 10.9 %collective-permute-start.1 = (f32[128,384]{1,0:T(8,128)S(1)}, f32[128,384]{1,0:T(8,128)S(1)}, u32[]{:S(2)}, u32[]{:S(2)}) collective-permute-start(f32[128,384]{1,0:T(8,128)S(1)} %project_back.1.refs_0_), channel_id=1, source_target_pairs={{4,0},{0,4},{5,1},{1,5},{6,2},{2,6},{7,3},{3,7},{12,8},{8,12},{13,... | collective-permute-start | bytes 589832 | tf_op jit(solution)/shard_map/ppermute | solution.py:464
  15.9 4.0 %collective-permute-start.5 = (f32[64,128]{1,0:T(8,128)S(1)}, f32[64,128]{1,0:T(8,128)S(1)}, u32[]{:S(2)}, u32[]{:S(2)}) collective-permute-start(f32[64,128]{1,0:T(8,128)S(1)} %add_add_fusion), channel_id=1, source_target_pairs={{0,1},{1,0},{2,3},{3,2},{4,5},{5,4},{6,7},{7,6},{8,9},{9,8},{10,11... | collective-permute-start | bytes 98312 | tf_op jit(solution)/shard_map/ppermute | solution.py:454
  19.9 4.8 %collective-permute-start.6 = (f32[64,128]{1,0:T(8,128)S(1)}, f32[64,128]{1,0:T(8,128)S(1)}, u32[]{:S(2)}, u32[]{:S(2)}) collective-permute-start(f32[64,128]{1,0:T(8,128)S(1)} %add.74.refs_2_), channel_id=1, source_target_pairs={{0,2},{1,3},{2,0},{3,1},{4,6},{5,7},{6,4},{7,5},{8,10},{9,11},{10,... | collective-permute-start | bytes 98312 | tf_op jit(solution)/shard_map/ppermute | solution.py:454
  27.0 4.2 %collective-permute-start.8 = (bf16[2,4,64,768]{3,2,1,0:T(8,128)(2,1)S(1)}, bf16[2,4,64,768]{3,2,1,0:T(8,128)(2,1)S(1)}, u32[]{:S(2)}, u32[]{:S(2)}) collective-permute-start(bf16[2,4,64,768]{3,2,1,0:T(8,128)(2,1)S(1)} %gradient.7), channel_id=1, source_target_pairs={{0,8},{8,0},{16,24},{24,16},{1,9},{9,1},{17,25},{25,17},{2,10},{10... | collective-permute-start | bytes 2359304 | tf_op jit(solution)/shard_map/ppermute | solution.py:454
  27.1 4.0 %collective-permute-start.11 = (bf16[128,128]{1,0:T(8,128)(2,1)S(1)}, bf16[128,128]{1,0:T(8,128)(2,1)S(1)}, u32[]{:S(2)}, u32[]{:S(2)}) collective-permute-start(bf16[128,128]{1,0:T(8,128)(2,1)S(1)} %convert_element_type.132), channel_id=1, source_target_pairs={{0,1},{1,0},{2,3},{3,2},{4,5},{5,4},{6,7},{7,6},{8,9},{9,8},{10,11... | collective-permute-start | bytes 98312 | tf_op jit(solution)/shard_map/ppermute | solution.py:454
  29.2 15.0 %collective-permute-start.7 = (bf16[2,4,64,768]{3,2,1,0:T(8,128)(2,1)S(1)}, bf16[2,4,64,768]{3,2,1,0:T(8,128)(2,1)S(1)}, u32[]{:S(2)}, u32[]{:S(2)}) collective-permute-start(bf16[2,4,64,768]{3,2,1,0:T(8,128)(2,1)S(1)} %gradient.5), channel_id=1, source_target_pairs={{0,8},{8,0},{16,24},{24,16},{1,9},{9,1},{17,25},{25,17},{2,10},{10... | collective-permute-start | bytes 2359304 | tf_op jit(solution)/shard_map/ppermute | solution.py:454
  31.0 2.6 %collective-permute-start.12 = (bf16[128,128]{1,0:T(8,128)(2,1)S(1)}, bf16[128,128]{1,0:T(8,128)(2,1)S(1)}, u32[]{:S(2)}, u32[]{:S(2)}) collective-permute-start(bf16[128,128]{1,0:T(8,128)(2,1)S(1)} %fusion.6), channel_id=1, source_target_pairs={{0,8},{8,0},{16,24},{24,16},{1,9},{9,1},{17,25},{25,17},{2,10},{10... | collective-permute-start | bytes 98312 | tf_op jit(solution)/shard_map/ppermute | solution.py:454
  31.3 12.3 %collective-permute-start.10 = (bf16[4,64,768]{2,1,0:T(8,128)(2,1)S(1)}, bf16[4,64,768]{2,1,0:T(8,128)(2,1)S(1)}, u32[]{:S(2)}, u32[]{:S(2)}) collective-permute-start(bf16[4,64,768]{2,1,0:T(8,128)(2,1)S(1)} %get-tuple-element.80), channel_id=1, source_target_pairs={{0,1},{1,0},{2,3},{3,2},{4,5},{5,4},{6,7},{7,6},{8,9},{9,8},{10,11... | collective-permute-start | bytes 1179656 | tf_op jit(solution)/shard_map/ppermute | solution.py:454
  33.0 11.2 %collective-permute-start.9 = (bf16[4,64,768]{2,1,0:T(8,128)(2,1)S(1)}, bf16[4,64,768]{2,1,0:T(8,128)(2,1)S(1)}, u32[]{:S(2)}, u32[]{:S(2)}) collective-permute-start(bf16[4,64,768]{2,1,0:T(8,128)(2,1)S(1)} %get-tuple-element.81), channel_id=1, source_target_pairs={{0,16},{8,24},{16,0},{24,8},{1,17},{9,25},{17,1},{25,9},{2,18},{10... | collective-permute-start | bytes 1179656 | tf_op jit(solution)/shard_map/ppermute | solution.py:454
  33.7 27.6 %copy-start.1 = (f32[1,64,768]{2,1,0:T(8,128)S(1)}, f32[1,64,768]{2,1,0:T(8,128)}, u32[]{:S(2)}) copy-start(f32[1,64,768]{2,1,0:T(8,128)} %refs_0_.3) | copy-start | bytes 589828
  33.7 27.6 %copy-start.3 = (f32[1,64,768]{2,1,0:T(8,128)S(1)}, f32[1,64,768]{2,1,0:T(8,128)}, u32[]{:S(2)}) copy-start(f32[1,64,768]{2,1,0:T(8,128)} %refs_1_.3) | copy-start | bytes 589828
  33.7 27.6 %copy-start.4 = (f32[1,64,768]{2,1,0:T(8,128)S(1)}, f32[1,64,768]{2,1,0:T(8,128)}, u32[]{:S(2)}) copy-start(f32[1,64,768]{2,1,0:T(8,128)} %refs_2_.3) | copy-start | bytes 589828
  33.8 8.9 %collective-permute-start.13 = (bf16[128,128]{1,0:T(8,128)(2,1)S(1)}, bf16[128,128]{1,0:T(8,128)(2,1)S(1)}, u32[]{:S(2)}, u32[]{:S(2)}) collective-permute-start(bf16[128,128]{1,0:T(8,128)(2,1)S(1)} %fusion.7), channel_id=1, source_target_pairs={{0,2},{1,3},{2,0},{3,1},{4,6},{5,7},{6,4},{7,5},{8,10},{9,11},{10,... | collective-permute-start | bytes 98312 | tf_op jit(solution)/shard_map/ppermute | solution.py:454
  37.1 26.3 %copy-start.2 = (f32[1,64,768]{2,1,0:T(8,128)S(1)}, f32[1,64,768]{2,1,0:T(8,128)}, u32[]{:S(2)}) copy-start(f32[1,64,768]{2,1,0:T(8,128)} %refs_0_.2) | copy-start | bytes 589828
  37.2 26.3 %copy-start.5 = (f32[1,64,768]{2,1,0:T(8,128)S(1)}, f32[1,64,768]{2,1,0:T(8,128)}, u32[]{:S(2)}) copy-start(f32[1,64,768]{2,1,0:T(8,128)} %refs_1_.2) | copy-start | bytes 589828
  37.2 26.3 %copy-start.6 = (f32[1,64,768]{2,1,0:T(8,128)S(1)}, f32[1,64,768]{2,1,0:T(8,128)}, u32[]{:S(2)}) copy-start(f32[1,64,768]{2,1,0:T(8,128)} %refs_2_.2) | copy-start | bytes 589828
  44.4 6.3 %collective-permute-start.18 = (bf16[2,64,768]{2,1,0:T(8,128)(2,1)S(1)}, bf16[2,64,768]{2,1,0:T(8,128)(2,1)S(1)}, u32[]{:S(2)}, u32[]{:S(2)}) collective-permute-start(bf16[2,64,768]{2,1,0:T(8,128)(2,1)S(1)} %get-tuple-element.78), channel_id=1, source_target_pairs={{0,16},{8,24},{16,0},{24,8},{1,17},{9,25},{17,1},{25,9},{2,18},{10... | collective-permute-start | bytes 589832 | tf_op jit(solution)/shard_map/ppermute | solution.py:454
  45.1 8.4 %collective-permute-start.14 = (bf16[2,64,768]{2,1,0:T(8,128)(2,1)S(1)}, bf16[2,64,768]{2,1,0:T(8,128)(2,1)S(1)}, u32[]{:S(2)}, u32[]{:S(2)}) collective-permute-start(bf16[2,64,768]{2,1,0:T(8,128)(2,1)S(1)} %get-tuple-element.79), channel_id=1, source_target_pairs={{0,1},{1,0},{2,3},{3,2},{4,5},{5,4},{6,7},{7,6},{8,9},{9,8},{10,11... | collective-permute-start | bytes 589832 | tf_op jit(solution)/shard_map/ppermute | solution.py:454
  50.7 10.7 %collective-permute-start.19 = (bf16[64,768]{1,0:T(8,128)(2,1)S(1)}, bf16[64,768]{1,0:T(8,128)(2,1)S(1)}, u32[]{:S(2)}, u32[]{:S(2)}) collective-permute-start(bf16[64,768]{1,0:T(8,128)(2,1)S(1)} %fusion.4), channel_id=1, source_target_pairs={{0,2},{1,3},{2,0},{3,1},{4,6},{5,7},{6,4},{7,5},{8,10},{9,11},{10,... | collective-permute-start | bytes 294920 | tf_op jit(solution)/shard_map/ppermute | solution.py:454
  53.6 9.9 %collective-permute-start.15 = (bf16[64,768]{1,0:T(8,128)(2,1)S(1)}, bf16[64,768]{1,0:T(8,128)(2,1)S(1)}, u32[]{:S(2)}, u32[]{:S(2)}) collective-permute-start(bf16[64,768]{1,0:T(8,128)(2,1)S(1)} %fusion.5), channel_id=1, source_target_pairs={{0,2},{1,3},{2,0},{3,1},{4,6},{5,7},{6,4},{7,5},{8,10},{9,11},{10,... | collective-permute-start | bytes 294920 | tf_op jit(solution)/shard_map/ppermute | solution.py:454
  54.0 3.9 %collective-permute-start.16 = (bf16[128,128]{1,0:T(8,128)(2,1)S(1)}, bf16[128,128]{1,0:T(8,128)(2,1)S(1)}, u32[]{:S(2)}, u32[]{:S(2)}) collective-permute-start(bf16[128,128]{1,0:T(8,128)(2,1)S(1)} %convert_element_type.149), channel_id=1, source_target_pairs={{0,16},{8,24},{16,0},{24,8},{1,17},{9,25},{17,1},{25,9},{2,18},{10... | collective-permute-start | bytes 98312 | tf_op jit(solution)/shard_map/ppermute | solution.py:454
  62.6 7.4 %collective-permute-start.20 = (bf16[1,64,768]{2,1,0:T(8,128)(2,1)S(1)}, bf16[1,64,768]{2,1,0:T(8,128)(2,1)S(1)}, u32[]{:S(2)}, u32[]{:S(2)}) collective-permute-start(bf16[1,64,768]{2,1,0:T(8,128)(2,1)S(1)} %get-tuple-element.63), channel_id=1, source_target_pairs={{0,2},{1,3},{2,0},{3,1},{4,6},{5,7},{6,4},{7,5},{8,10},{9,11},{10,... | collective-permute-start | bytes 294920 | tf_op jit(solution)/shard_map/ppermute | solution.py:454
  64.7 7.4 %collective-permute-start.17 = (bf16[1,64,768]{2,1,0:T(8,128)(2,1)S(1)}, bf16[1,64,768]{2,1,0:T(8,128)(2,1)S(1)}, u32[]{:S(2)}, u32[]{:S(2)}) collective-permute-start(bf16[1,64,768]{2,1,0:T(8,128)(2,1)S(1)} %get-tuple-element.62), channel_id=1, source_target_pairs={{0,2},{1,3},{2,0},{3,1},{4,6},{5,7},{6,4},{7,5},{8,10},{9,11},{10,... | collective-permute-start | bytes 294920 | tf_op jit(solution)/shard_map/ppermute | solution.py:454
  66.9 7.6 %collective-permute-start.21 = (bf16[2,64,768]{2,1,0:T(8,128)(2,1)S(1)}, bf16[2,64,768]{2,1,0:T(8,128)(2,1)S(1)}, u32[]{:S(2)}, u32[]{:S(2)}) collective-permute-start(bf16[2,64,768]{2,1,0:T(8,128)(2,1)S(1)} %pad_maximum_fusion.6), channel_id=1, source_target_pairs={{4,0},{5,1},{6,2},{7,3},{12,8},{13,9},{14,10},{15,11},{20,16},{21,... | collective-permute-start | bytes 589832 | tf_op jit(solution)/shard_map/ppermute | solution.py:469
  70.0 5.8 %collective-permute-start.25 = (bf16[2,64,768]{2,1,0:T(8,128)(2,1)S(1)}, bf16[2,64,768]{2,1,0:T(8,128)(2,1)S(1)}, u32[]{:S(2)}, u32[]{:S(2)}) collective-permute-start(bf16[2,64,768]{2,1,0:T(8,128)(2,1)S(1)} %pad_maximum_fusion.9), channel_id=1, source_target_pairs={{0,16},{8,24},{16,0},{24,8},{1,17},{9,25},{17,1},{25,9},{2,18},{10... | collective-permute-start | bytes 589832 | tf_op jit(solution)/shard_map/ppermute | solution.py:454
  72.1 5.7 %collective-permute-start.23 = (bf16[2,64,768]{2,1,0:T(8,128)(2,1)S(1)}, bf16[2,64,768]{2,1,0:T(8,128)(2,1)S(1)}, u32[]{:S(2)}, u32[]{:S(2)}) collective-permute-start(bf16[2,64,768]{2,1,0:T(8,128)(2,1)S(1)} %pad_maximum_fusion.8), channel_id=1, source_target_pairs={{0,1},{1,0},{2,3},{3,2},{4,5},{5,4},{6,7},{7,6},{8,9},{9,8},{10,11... | collective-permute-start | bytes 589832 | tf_op jit(solution)/shard_map/ppermute | solution.py:454
  74.4 9.7 %collective-permute-start.22 = (bf16[2,64,768]{2,1,0:T(8,128)(2,1)S(1)}, bf16[2,64,768]{2,1,0:T(8,128)(2,1)S(1)}, u32[]{:S(2)}, u32[]{:S(2)}) collective-permute-start(bf16[2,64,768]{2,1,0:T(8,128)(2,1)S(1)} %pad_maximum_fusion.7), channel_id=1, source_target_pairs={{4,0},{5,1},{6,2},{7,3},{12,8},{13,9},{14,10},{15,11},{20,16},{21,... | collective-permute-start | bytes 589832 | tf_op jit(solution)/shard_map/ppermute | solution.py:469
  78.0 12.2 %collective-permute-start.27 = (bf16[4,64,768]{2,1,0:T(8,128)(2,1)S(1)}, bf16[4,64,768]{2,1,0:T(8,128)(2,1)S(1)}, u32[]{:S(2)}, u32[]{:S(2)}) collective-permute-start(bf16[4,64,768]{2,1,0:T(8,128)(2,1)S(1)} %get-tuple-element.88), channel_id=1, source_target_pairs={{4,0},{5,1},{6,2},{7,3},{12,8},{13,9},{14,10},{15,11},{20,16},{21,... | collective-permute-start | bytes 1179656 | tf_op jit(solution)/shard_map/ppermute | solution.py:469
  79.3 10.9 %collective-permute-start.24 = (bf16[4,64,768]{2,1,0:T(8,128)(2,1)S(1)}, bf16[4,64,768]{2,1,0:T(8,128)(2,1)S(1)}, u32[]{:S(2)}, u32[]{:S(2)}) collective-permute-start(bf16[4,64,768]{2,1,0:T(8,128)(2,1)S(1)} %get-tuple-element.89), channel_id=1, source_target_pairs={{0,16},{8,24},{16,0},{24,8},{1,17},{9,25},{17,1},{25,9},{2,18},{10... | collective-permute-start | bytes 1179656 | tf_op jit(solution)/shard_map/ppermute | solution.py:454
  80.1 10.1 %collective-permute-start.26 = (bf16[4,64,768]{2,1,0:T(8,128)(2,1)S(1)}, bf16[4,64,768]{2,1,0:T(8,128)(2,1)S(1)}, u32[]{:S(2)}, u32[]{:S(2)}) collective-permute-start(bf16[4,64,768]{2,1,0:T(8,128)(2,1)S(1)} %get-tuple-element.90), channel_id=1, source_target_pairs={{0,1},{1,0},{2,3},{3,2},{4,5},{5,4},{6,7},{7,6},{8,9},{9,8},{10,11... | collective-permute-start | bytes 1179656 | tf_op jit(solution)/shard_map/ppermute | solution.py:454
  81.0 19.0 %collective-permute-start.32 = (bf16[8,64,768]{2,1,0:T(8,128)(2,1)S(1)}, bf16[8,64,768]{2,1,0:T(8,128)(2,1)S(1)}, u32[]{:S(2)}, u32[]{:S(2)}) collective-permute-start(bf16[8,64,768]{2,1,0:T(8,128)(2,1)S(1)} %constant_dynamic-update-slice_fusion.3.refs_0_), channel_id=1, source_target_pairs={{0,8},{8,0},{16,24},{24,16},{1,9},{9,1},{17,25},{25,17},{2,10},{10... | collective-permute-start | bytes 2359304 | tf_op jit(solution)/shard_map/ppermute | solution.py:454
  90.3 9.6 %collective-permute-start.30 = (bf16[2,64,768]{2,1,0:T(8,128)(2,1)S(1)}, bf16[2,64,768]{2,1,0:T(8,128)(2,1)S(1)}, u32[]{:S(2)}, u32[]{:S(2)}) collective-permute-start(bf16[2,64,768]{2,1,0:T(8,128)(2,1)S(1)} %pad_maximum_fusion.10), channel_id=1, source_target_pairs={{4,0},{5,1},{6,2},{7,3},{12,8},{13,9},{14,10},{15,11},{20,16},{21,... | collective-permute-start | bytes 589832 | tf_op jit(solution)/shard_map/ppermute | solution.py:469
  91.6 6.8 %collective-permute-start.28 = (bf16[3,64,768]{2,1,0:T(8,128)(2,1)S(1)}, bf16[3,64,768]{2,1,0:T(8,128)(2,1)S(1)}, u32[]{:S(2)}, u32[]{:S(2)}) collective-permute-start(bf16[3,64,768]{2,1,0:T(8,128)(2,1)S(1)} %pad_maximum_fusion.3), channel_id=1, source_target_pairs={{0,16},{8,24},{16,0},{24,8},{1,17},{9,25},{17,1},{25,9},{2,18},{10... | collective-permute-start | bytes 884744 | tf_op jit(solution)/shard_map/ppermute | solution.py:454
  92.4 7.4 %collective-permute-start.29 = (bf16[3,64,768]{2,1,0:T(8,128)(2,1)S(1)}, bf16[3,64,768]{2,1,0:T(8,128)(2,1)S(1)}, u32[]{:S(2)}, u32[]{:S(2)}) collective-permute-start(bf16[3,64,768]{2,1,0:T(8,128)(2,1)S(1)} %pad_maximum_fusion.4), channel_id=1, source_target_pairs={{0,1},{1,0},{2,3},{3,2},{4,5},{5,4},{6,7},{7,6},{8,9},{9,8},{10,11... | collective-permute-start | bytes 884744 | tf_op jit(solution)/shard_map/ppermute | solution.py:454
  94.4 5.6 %collective-permute-start.33 = (bf16[8,64,768]{2,1,0:T(8,128)(2,1)S(1)}, bf16[8,64,768]{2,1,0:T(8,128)(2,1)S(1)}, u32[]{:S(2)}, u32[]{:S(2)}) collective-permute-start(bf16[8,64,768]{2,1,0:T(8,128)(2,1)S(1)} %constant_dynamic-update-slice_fusion.9.refs_2_), channel_id=1, source_target_pairs={{0,8},{8,0},{16,24},{24,16},{1,9},{9,1},{17,25},{25,17},{2,10},{10... | collective-permute-start | bytes 2359304 | tf_op jit(solution)/shard_map/ppermute | solution.py:454
  98.4 2.3 %collective-permute-start.34 = (bf16[8,64,768]{2,1,0:T(8,128)(2,1)S(1)}, bf16[8,64,768]{2,1,0:T(8,128)(2,1)S(1)}, u32[]{:S(2)}, u32[]{:S(2)}) collective-permute-start(bf16[8,64,768]{2,1,0:T(8,128)(2,1)S(1)} %constant_dynamic-update-slice_fusion.11.refs_4_), channel_id=1, source_target_pairs={{0,8},{8,0},{16,24},{24,16},{1,9},{9,1},{17,25},{25,17},{2,10},{10... | collective-permute-start | bytes 2359304 | tf_op jit(solution)/shard_map/ppermute | solution.py:454
  99.9 3.1 %collective-permute-start.31 = (bf16[8,64,768]{2,1,0:T(8,128)(2,1)S(1)}, bf16[8,64,768]{2,1,0:T(8,128)(2,1)S(1)}, u32[]{:S(2)}, u32[]{:S(2)}) collective-permute-start(bf16[8,64,768]{2,1,0:T(8,128)(2,1)S(1)} %constant_dynamic-update-slice_fusion.refs_0_), channel_id=1, source_target_pairs={{0,8},{8,0},{16,24},{24,16},{1,9},{9,1},{17,25},{25,17},{2,10},{10... | collective-permute-start | bytes 2359304 | tf_op jit(solution)/shard_map/ppermute | solution.py:454

commit v10 on v9

--- a/solution.py
+++ b/solution.py
@@ -47,6 +47,16 @@
     return lax.dot_general(
         x, y, (((0,), (0,)), ((), ())), preferred_element_type=f32, precision=precision
     )
+
+
+def in_parts(product, wide, parts):
+    total = None
+    for _ in range(parts):
+        piece = wide.astype(bf16)
+        wide = wide - piece.astype(f32)
+        term = product(piece)
+        total = term if total is None else total + term
+    return total
 
 
 def row_sum(x):
@@ -213,21 +223,14 @@
     def up_down(i, layer):
         return table[i * ranks : (i + 1) * ranks, (layer - 1) * ranks : layer * ranks]
 
-    def up_up(i, j):
-        at_column = (layers - 1 + j) * ranks
-        return table[i * ranks : (i + 1) * ranks, at_column : at_column + ranks]
-
-    def times(x, y):
-        return jnp.dot(x, y, preferred_element_type=f32, precision=exact)
-
     square = sq_ref[:, 0:1]
-    inverses, inners, actives, sigmoids = [], [], [], []
+    inverses, inners, actives, sigmoids, products = [], [], [], [], []
     on_up = [[part(l, 1) for l in range(layers - 1)]]
     for layer in range(layers):
         inverse = lax.rsqrt(jnp.maximum(square, 0.0) * (1.0 / features) + norm_eps)
         on_down = part(layer, 0)
         for i in range(layer):
-            on_down = on_down + scale_r * times(actives[i], up_down(i, layer))
+            on_down = on_down + products[i][:, (layer - 1) * ranks : layer * ranks]
         inner = on_down * (inverse * scale_d)
         sigmoid = jax.nn.sigmoid(inner)
         active = (inner * sigmoid).astype(bf16).astype(f32)
@@ -237,7 +240,16 @@
         actives.append(active)
         if layer < layers - 1:
             now = on_up[-1]
-            grown = [now[l] + scale_r * times(active, up_up(layer, l)) for l in range(layers - 1)]
+            product = in_parts(
+                lambda part: jnp.dot(active.astype(bf16), part, preferred_element_type=f32),
+                table[layer * ranks : (layer + 1) * ranks],
+                3,
+            )
+            products.append(scale_r * product)
+            grown = [
+                now[l] + products[layer][:, (layers - 1 + l) * ranks : (layers + l) * ranks]
+                for l in range(layers - 1)
+            ]
             square = square + scale_r * row_sum(active * (now[layer] + grown[layer]))
             on_up.append(grown)
     scaled = [None] * layers
@@ -353,8 +365,8 @@
     ranks = last.shape[0]
     rows = slice(which * ranks, (which + 1) * ranks)
     mixed = mixed_ref[rows] + other_ref[rows].astype(f32)
-    right = right_ref[...].astype(f32)
-    own = jnp.dot(mixed, right, preferred_element_type=f32, precision=exact)
+    right = right_ref[...]
+    own = in_parts(lambda part: jnp.dot(part, right, preferred_element_type=f32), mixed, 3)
     for block in (kept[which, 0], near[which, 0], one[0], two[0], last[...]):
         own = own + block.astype(f32)
     moment = beta_one * moment_ref[0] + (1.0 - beta_one) * own
@@ -492,7 +504,6 @@
     down_one = swapped(part(0, whole), "replica", 2)
     up_one = swapped(part(1, whole), "tensor", 1)
     near, kept = halves(0)
-    mixed = added("tensor", 1)
     mixed = added("replica", 1)
     mixed = added("tensor", 2)
     down_one, up_one, mixed = lax.optimization_barrier((down_one, up_one, mixed))
@@ -501,6 +512,7 @@
     down_last = swapped(part(0, 1, down_one[1], down_two[1]), "tensor", 2)
     kept, near = lax.optimization_barrier((kept, near))
     up_last = swapped(part(1, 1, up_one[1], up_two[1]), "tensor", 2)
+    mixed = added("tensor", 1)
     other = swapped(mixed.astype(bf16), "replica", 2)
     down = (kept, near, down_one, down_two, down_last, mixed, other)
     return down, (kept, near, up_one, up_two, up_last, mixed, other)

time: 105 us -> 99.9 us (0.951)
  waiting for transfers between devices: 46.8 us -> 37.7 us
  starting transfers between devices: 37.2 us -> 41.9 us
    ppermute x4, waiting for transfers between devices: 11.3 us -> 6.4 us  [following_layer(): return lax.ppermute(block, 'section', [(i + 1, i) for i in range(size - 1)])]
    ppermute x29, starting transfers between devices: 28.4 us -> 33.1 us  [swapped(): return lax.ppermute(block, axis, route)]
    ppermute x29, waiting for transfers between devices: 35.5 us -> 31.2 us  [swapped(): return lax.ppermute(block, axis, route)]
  transfers between devices with their start and end apart: 35 -> 35, of which waited for: 21 -> 22; matrix products, arithmetic and copies ran while one was open for 1% -> 1% of each run, Pallas kernels for 13% -> 13%
where the time goes in v10:
time: 99.9 us; the launch traced here: 99.6 us
  starting transfers between devices  41.9 us (42%)
  waiting for transfers between devices  37.7 us (38%)
  Pallas kernels  16.8 us (17%)
  other arithmetic  1.83 us (2%)
  between operations  1.1 us (1%)
    ppermute x29, starting transfers between devices, swapped(): return lax.ppermute(block, axis, route)  33.1 us
    ppermute x29, waiting for transfers between devices, swapped(): return lax.ppermute(block, axis, route)  31.2 us
    ppermute x4, waiting for transfers between devices, following_layer(): return lax.ppermute(block, 'section', [(i + 1, i) for i in range(size - 1)])  6.4 us
    pallas_call x1, Pallas kernels, project(): pl.pallas_call(functools.partial(project_kernel, steps), in_specs=[in_hbm...  5.99 us
    ppermute x4, starting transfers between devices, following_layer(): return lax.ppermute(block, 'section', [(i + 1, i) for i in range(size - 1)])  5.17 us
    ppermute x2, starting transfers between devices, from_next(): return lax.ppermute(block, 'section', route)  3.69 us
    pallas_call x2, Pallas kernels, place(): pl.pallas_call(functools.partial(place_kernel, layout, not before), in_sp...  3.56 us
    pallas_call x2, Pallas kernels, update(): pl.pallas_call(functools.partial(update_kernel, which), in_specs=[in_vmem...  2.45 us
  transfers between devices with their start and end apart: 35, of which 22 were waited for; matrix products, arithmetic and copies ran while one was open for 1% of the time, Pallas kernels for 13%

profile of v10, /device:TPU:0, one launch (start us, length us, event | category | flops | bytes accessed | tf_op | source)
XLA Modules:
  0.0 99.6 jit_solution(12516105393427382596)
XLA Ops:
  0.6 1.0 %convert_bitcast_fusion = (bf16[64,768]{1,0:T(8,128)(2,1)S(1)}, bf16[64,768]{1,0:T(8,128)(2,1)S(1)}) fusion(f32[1,64,768]{2,1,0:T(8,128)} %refs_0_.3, f32[1,64,768]{2,1,0:T(8,128)} %refs_0_.2), kind=kLoop, calls=%fused_computation.27 | loop fusion | flops 98304 | bytes 589824 | tf_op jit(solution)/shard_map/squeeze | solution.py:608
  1.7 3.0 %collective-permute-start = (bf16[128,768]{1,0:T(8,128)(2,1)S(1)}, bf16[128,768]{1,0:T(8,128)(2,1)S(1)}, u32[]{:S(2)}, u32[]{:S(2)}) collective-permute-start(bf16[128,768]{1,0:T(8,128)(2,1)S(1)} %pad_maximum_fusion.5.refs_0_), channel_id=1, source_target_pairs={{4,0},{0,4},{5,1},{1,5},{6,2},{2,6},{7,3},{3,7},{12,8},{8,12},{13,... | collective-permute-start | bytes 589832 | tf_op jit(solution)/shard_map/ppermute | solution.py:476
  4.7 6.0 %project.1 = (f32[128,256]{1,0:T(8,128)S(1)}, f32[128,128]{1,0:T(8,128)S(1)}, bf16[128,12288]{1,0:T(8,128)(2,1)S(1)}, bf16[128,12288]{1,0:T(8,128)(2,1)S(1)}) custom-call(bf16[128,12288]{1,0:T(8,128)(2,1)} %bitcast.52, bf16[2,64,12288]{2,1,0:T(8,128)(2,1)} %bitcast.53, bf16[2,64,12288]{2,1,0:T(8,128)(2,1)} %bitcast.54), custom_call_target="tpu_custom_call" | custom-call | flops 805306368 | bytes 9437184 | tf_op jit(solution)/shard_map/project/pallas_call | solution.py:108
  10.9 0.7 collective-permute-start.4
  11.7 0.9 collective-permute-start.3
  12.8 1.0 project_back.1.refs_0_
  13.8 0.7 collective-permute-start.1
  14.6 1.3 %collective-permute-done.3 = f32[64,128]{1,0:T(8,128)S(1)} collective-permute-done((f32[64,128]{1,0:T(8,128)S(1)}, f32[64,128]{1,0:T(8,128)S(1)}, u32[]{:S(2)}, u32[]{:S(2)}) %collective-permute-start.3) | collective-permute-done | bytes 32800 | tf_op jit(solution)/shard_map/ppermute | solution.py:466
  15.9 1.6 %collective-permute-start.5 = (f32[64,128]{1,0:T(8,128)S(1)}, f32[64,128]{1,0:T(8,128)S(1)}, u32[]{:S(2)}, u32[]{:S(2)}) collective-permute-start(f32[64,128]{1,0:T(8,128)S(1)} %add_add_fusion), channel_id=1, source_target_pairs={{0,1},{1,0},{2,3},{3,2},{4,5},{5,4},{6,7},{7,6},{8,9},{9,8},{10,11... | collective-permute-start | bytes 98312 | tf_op jit(solution)/shard_map/ppermute | solution.py:466
  17.6 2.3 %collective-permute-done.5 = f32[64,128]{1,0:T(8,128)S(1)} collective-permute-done((f32[64,128]{1,0:T(8,128)S(1)}, f32[64,128]{1,0:T(8,128)S(1)}, u32[]{:S(2)}, u32[]{:S(2)}) %collective-permute-start.5) | collective-permute-done | bytes 32800 | tf_op jit(solution)/shard_map/ppermute | solution.py:466
  19.9 2.6 %collective-permute-start.6 = (f32[64,128]{1,0:T(8,128)S(1)}, f32[64,128]{1,0:T(8,128)S(1)}, u32[]{:S(2)}, u32[]{:S(2)}) collective-permute-start(f32[64,128]{1,0:T(8,128)S(1)} %add.74.refs_2_), channel_id=1, source_target_pairs={{0,2},{1,3},{2,0},{3,1},{4,6},{5,7},{6,4},{7,5},{8,10},{9,11},{10,... | collective-permute-start | bytes 98312 | tf_op jit(solution)/shard_map/ppermute | solution.py:466
  22.5 2.2 %collective-permute-done.6.refs_3_ = f32[64,128]{1,0:T(8,128)S(1)} collective-permute-done((f32[64,128]{1,0:T(8,128)S(1)}, f32[64,128]{1,0:T(8,128)S(1)}, u32[]{:S(2)}, u32[]{:S(2)}) %collective-permute-start.6) | collective-permute-done | bytes 32800 | tf_op jit(solution)/shard_map/ppermute | solution.py:466
  24.7 1.6 %chain.1 = (bf16[128,256]{1,0:T(8,128)(2,1)S(1)}, f32[128,128]{1,0:T(8,128)S(1)}) custom-call(s32[4,3]{1,0:T(4,128)S(1)} %copy-done.7, s32[1,4]{1,0:T(1,128)S(1)} %bitcast.49, f32[128,384]{1,0:T(8,128)S(1)} %project_back.1.refs_0_, f32[128,384]{1,0:T(8,128)S(1)} %collective-permute-done.1.refs_1_, f32[64,128]{1,0:T(8,128)S(1)} %add.74.refs_2_, ...), custom_call_target="tpu_custom_call" | custom-call | tf_op jit(solution)/shard_map/chain/pallas_call | solution.py:310
  29.4 1.6 %collective-permute-start.10 = (bf16[4,64,768]{2,1,0:T(8,128)(2,1)S(1)}, bf16[4,64,768]{2,1,0:T(8,128)(2,1)S(1)}, u32[]{:S(2)}, u32[]{:S(2)}) collective-permute-start(bf16[4,64,768]{2,1,0:T(8,128)(2,1)S(1)} %get-tuple-element.82), channel_id=1, source_target_pairs={{0,1},{1,0},{2,3},{3,2},{4,5},{5,4},{6,7},{7,6},{8,9},{9,8},{10,11... | collective-permute-start | bytes 1179656 | tf_op jit(solution)/shard_map/ppermute | solution.py:466
  31.0 0.7 collective-permute-start.9
  31.8 2.9 %collective-permute-start.12 = (bf16[128,128]{1,0:T(8,128)(2,1)S(1)}, bf16[128,128]{1,0:T(8,128)(2,1)S(1)}, u32[]{:S(2)}, u32[]{:S(2)}) collective-permute-start(bf16[128,128]{1,0:T(8,128)(2,1)S(1)} %fusion.6), channel_id=1, source_target_pairs={{0,2},{1,3},{2,0},{3,1},{4,6},{5,7},{6,4},{7,5},{8,10},{9,11},{10,... | collective-permute-start | bytes 98312 | tf_op jit(solution)/shard_map/ppermute | solution.py:466
  35.2 5.2 %collective-permute-done.12 = bf16[128,128]{1,0:T(8,128)(2,1)S(1)} collective-permute-done((bf16[128,128]{1,0:T(8,128)(2,1)S(1)}, bf16[128,128]{1,0:T(8,128)(2,1)S(1)}, u32[]{:S(2)}, u32[]{:S(2)}) %collective-permute-start.12) | collective-permute-done | bytes 32800 | tf_op jit(solution)/shard_map/ppermute | solution.py:466
  40.4 0.9 collective-permute-done.10.one
  42.1 0.8 collective-permute-start.18
  42.9 2.1 %collective-permute-start.15 = (bf16[128,128]{1,0:T(8,128)(2,1)S(1)}, bf16[128,128]{1,0:T(8,128)(2,1)S(1)}, u32[]{:S(2)}, u32[]{:S(2)}) collective-permute-start(bf16[128,128]{1,0:T(8,128)(2,1)S(1)} %convert_element_type.147), channel_id=1, source_target_pairs={{0,1},{1,0},{2,3},{3,2},{4,5},{5,4},{6,7},{7,6},{8,9},{9,8},{10,11... | collective-permute-start | bytes 98312 | tf_op jit(solution)/shard_map/ppermute | solution.py:466
  45.0 2.9 %collective-permute-done.18.two = bf16[2,64,768]{2,1,0:T(8,128)(2,1)S(1)} collective-permute-done((bf16[2,64,768]{2,1,0:T(8,128)(2,1)S(1)}, bf16[2,64,768]{2,1,0:T(8,128)(2,1)S(1)}, u32[]{:S(2)}, u32[]{:S(2)}) %collective-permute-start.18) | collective-permute-done | bytes 196640 | tf_op jit(solution)/shard_map/ppermute | solution.py:466
  48.0 2.9 %collective-permute-start.19 = (bf16[64,768]{1,0:T(8,128)(2,1)S(1)}, bf16[64,768]{1,0:T(8,128)(2,1)S(1)}, u32[]{:S(2)}, u32[]{:S(2)}) collective-permute-start(bf16[64,768]{1,0:T(8,128)(2,1)S(1)} %fusion.4), channel_id=1, source_target_pairs={{0,2},{1,3},{2,0},{3,1},{4,6},{5,7},{6,4},{7,5},{8,10},{9,11},{10,... | collective-permute-start | bytes 294920 | tf_op jit(solution)/shard_map/ppermute | solution.py:466
  50.9 0.8 collective-permute-done.13.two
  51.8 1.5 %collective-permute-start.14 = (bf16[64,768]{1,0:T(8,128)(2,1)S(1)}, bf16[64,768]{1,0:T(8,128)(2,1)S(1)}, u32[]{:S(2)}, u32[]{:S(2)}) collective-permute-start(bf16[64,768]{1,0:T(8,128)(2,1)S(1)} %fusion.5), channel_id=1, source_target_pairs={{0,2},{1,3},{2,0},{3,1},{4,6},{5,7},{6,4},{7,5},{8,10},{9,11},{10,... | collective-permute-start | bytes 294920 | tf_op jit(solution)/shard_map/ppermute | solution.py:466
  53.3 2.0 %collective-permute-start.16 = (bf16[128,128]{1,0:T(8,128)(2,1)S(1)}, bf16[128,128]{1,0:T(8,128)(2,1)S(1)}, u32[]{:S(2)}, u32[]{:S(2)}) collective-permute-start(bf16[128,128]{1,0:T(8,128)(2,1)S(1)} %get-tuple-element.78), channel_id=1, source_target_pairs={{0,16},{8,24},{16,0},{24,8},{1,17},{9,25},{17,1},{25,9},{2,18},{10... | collective-permute-start | bytes 98312 | tf_op jit(solution)/shard_map/ppermute | solution.py:466
  55.3 1.9 %collective-permute-done.16.other_ref = bf16[128,128]{1,0:T(8,128)(2,1)S(1)} collective-permute-done((bf16[128,128]{1,0:T(8,128)(2,1)S(1)}, bf16[128,128]{1,0:T(8,128)(2,1)S(1)}, u32[]{:S(2)}, u32[]{:S(2)}) %collective-permute-start.16) | collective-permute-done | bytes 32800 | tf_op jit(solution)/shard_map/ppermute | solution.py:466
  57.3 0.9 collective-permute-done.19.last
  58.2 1.2 %update.3 = (f32[1,64,768]{2,1,0:T(8,128)}, f32[1,64,768]{2,1,0:T(8,128)}, f32[1,64,768]{2,1,0:T(8,128)}, bf16[1,64,768]{2,1,0:T(8,128)(2,1)S(1)}) custom-call(bf16[2,4,64,768]{3,2,1,0:T(8,128)(2,1)S(1)} %gradient.4.kept, bf16[2,4,64,768]{3,2,1,0:T(8,128)(2,1)S(1)} %collective-permute-done.7.near, bf16[4,64,768]{2,1,0:T(8,128)(2,1)S(1)} %collective-permute-done.10.one, ...), custom_call_target="tpu_custom_call" | custom-call | tf_op jit(solution)/shard_map/update/pallas_call | solution.py:386
  60.0 0.9 collective-permute-done.14.last
  60.9 1.2 %update.2 = (f32[1,64,768]{2,1,0:T(8,128)}, f32[1,64,768]{2,1,0:T(8,128)}, f32[1,64,768]{2,1,0:T(8,128)}, bf16[1,64,768]{2,1,0:T(8,128)(2,1)S(1)}) custom-call(bf16[2,4,64,768]{3,2,1,0:T(8,128)(2,1)S(1)} %gradient.4.kept, bf16[2,4,64,768]{3,2,1,0:T(8,128)(2,1)S(1)} %collective-permute-done.7.near, bf16[4,64,768]{2,1,0:T(8,128)(2,1)S(1)} %collective-permute-done.9.one, ...), custom_call_target="tpu_custom_call" | custom-call | tf_op jit(solution)/shard_map/update/pallas_call | solution.py:386
  62.2 1.4 %collective-permute-start.17 = (bf16[1,64,768]{2,1,0:T(8,128)(2,1)S(1)}, bf16[1,64,768]{2,1,0:T(8,128)(2,1)S(1)}, u32[]{:S(2)}, u32[]{:S(2)}) collective-permute-start(bf16[1,64,768]{2,1,0:T(8,128)(2,1)S(1)} %get-tuple-element.62), channel_id=1, source_target_pairs={{0,2},{1,3},{2,0},{3,1},{4,6},{5,7},{6,4},{7,5},{8,10},{9,11},{10,... | collective-permute-start | bytes 294920 | tf_op jit(solution)/shard_map/ppermute | solution.py:466
  63.6 1.3 %collective-permute-start.21 = (bf16[2,64,768]{2,1,0:T(8,128)(2,1)S(1)}, bf16[2,64,768]{2,1,0:T(8,128)(2,1)S(1)}, u32[]{:S(2)}, u32[]{:S(2)}) collective-permute-start(bf16[2,64,768]{2,1,0:T(8,128)(2,1)S(1)} %pad_maximum_fusion.6), channel_id=1, source_target_pairs={{4,0},{5,1},{6,2},{7,3},{12,8},{13,9},{14,10},{15,11},{20,16},{21,... | collective-permute-start | bytes 589832 | tf_op jit(solution)/shard_map/ppermute | solution.py:481
  64.9 2.2 %collective-permute-done.20 = bf16[1,64,768]{2,1,0:T(8,128)(2,1)S(1)} collective-permute-done((bf16[1,64,768]{2,1,0:T(8,128)(2,1)S(1)}, bf16[1,64,768]{2,1,0:T(8,128)(2,1)S(1)}, u32[]{:S(2)}, u32[]{:S(2)}) %collective-permute-start.20) | collective-permute-done | bytes 98336 | tf_op jit(solution)/shard_map/ppermute | solution.py:466
  67.2 1.0 %collective-permute-done.17 = bf16[1,64,768]{2,1,0:T(8,128)(2,1)S(1)} collective-permute-done((bf16[1,64,768]{2,1,0:T(8,128)(2,1)S(1)}, bf16[1,64,768]{2,1,0:T(8,128)(2,1)S(1)}, u32[]{:S(2)}, u32[]{:S(2)}) %collective-permute-start.17) | collective-permute-done | bytes 98336 | tf_op jit(solution)/shard_map/ppermute | solution.py:466
  68.3 2.9 %collective-permute-start.23 = (bf16[2,64,768]{2,1,0:T(8,128)(2,1)S(1)}, bf16[2,64,768]{2,1,0:T(8,128)(2,1)S(1)}, u32[]{:S(2)}, u32[]{:S(2)}) collective-permute-start(bf16[2,64,768]{2,1,0:T(8,128)(2,1)S(1)} %pad_maximum_fusion.8), channel_id=1, source_target_pairs={{0,1},{1,0},{2,3},{3,2},{4,5},{5,4},{6,7},{7,6},{8,9},{9,8},{10,11... | collective-permute-start | bytes 589832 | tf_op jit(solution)/shard_map/ppermute | solution.py:466
  71.6 1.3 %collective-permute-start.22 = (bf16[2,64,768]{2,1,0:T(8,128)(2,1)S(1)}, bf16[2,64,768]{2,1,0:T(8,128)(2,1)S(1)}, u32[]{:S(2)}, u32[]{:S(2)}) collective-permute-start(bf16[2,64,768]{2,1,0:T(8,128)(2,1)S(1)} %pad_maximum_fusion.7), channel_id=1, source_target_pairs={{4,0},{5,1},{6,2},{7,3},{12,8},{13,9},{14,10},{15,11},{20,16},{21,... | collective-permute-start | bytes 589832 | tf_op jit(solution)/shard_map/ppermute | solution.py:481
  73.0 2.3 %collective-permute-done.23 = bf16[2,64,768]{2,1,0:T(8,128)(2,1)S(1)} collective-permute-done((bf16[2,64,768]{2,1,0:T(8,128)(2,1)S(1)}, bf16[2,64,768]{2,1,0:T(8,128)(2,1)S(1)}, u32[]{:S(2)}, u32[]{:S(2)}) %collective-permute-start.23) | collective-permute-done | bytes 196640 | tf_op jit(solution)/shard_map/ppermute | solution.py:466
  75.5 1.3 %collective-permute-start.27 = (bf16[4,64,768]{2,1,0:T(8,128)(2,1)S(1)}, bf16[4,64,768]{2,1,0:T(8,128)(2,1)S(1)}, u32[]{:S(2)}, u32[]{:S(2)}) collective-permute-start(bf16[4,64,768]{2,1,0:T(8,128)(2,1)S(1)} %get-tuple-element.90), channel_id=1, source_target_pairs={{4,0},{5,1},{6,2},{7,3},{12,8},{13,9},{14,10},{15,11},{20,16},{21,... | collective-permute-start | bytes 1179656 | tf_op jit(solution)/shard_map/ppermute | solution.py:481
  76.8 2.5 %collective-permute-start.26 = (bf16[4,64,768]{2,1,0:T(8,128)(2,1)S(1)}, bf16[4,64,768]{2,1,0:T(8,128)(2,1)S(1)}, u32[]{:S(2)}, u32[]{:S(2)}) collective-permute-start(bf16[4,64,768]{2,1,0:T(8,128)(2,1)S(1)} %get-tuple-element.92), channel_id=1, source_target_pairs={{0,1},{1,0},{2,3},{3,2},{4,5},{5,4},{6,7},{7,6},{8,9},{9,8},{10,11... | collective-permute-start | bytes 1179656 | tf_op jit(solution)/shard_map/ppermute | solution.py:466
  79.5 1.8 %collective-permute-done.22 = bf16[2,64,768]{2,1,0:T(8,128)(2,1)S(1)} collective-permute-done((bf16[2,64,768]{2,1,0:T(8,128)(2,1)S(1)}, bf16[2,64,768]{2,1,0:T(8,128)(2,1)S(1)}, u32[]{:S(2)}, u32[]{:S(2)}) %collective-permute-start.22) | collective-permute-done | bytes 196640 | tf_op jit(solution)/shard_map/ppermute | solution.py:481
  81.3 4.2 %collective-permute-done.27 = bf16[4,64,768]{2,1,0:T(8,128)(2,1)S(1)} collective-permute-done((bf16[4,64,768]{2,1,0:T(8,128)(2,1)S(1)}, bf16[4,64,768]{2,1,0:T(8,128)(2,1)S(1)}, u32[]{:S(2)}, u32[]{:S(2)}) %collective-permute-start.27) | collective-permute-done | bytes 393248 | tf_op jit(solution)/shard_map/ppermute | solution.py:481
  85.6 1.3 %collective-permute-start.30 = (bf16[2,64,768]{2,1,0:T(8,128)(2,1)S(1)}, bf16[2,64,768]{2,1,0:T(8,128)(2,1)S(1)}, u32[]{:S(2)}, u32[]{:S(2)}) collective-permute-start(bf16[2,64,768]{2,1,0:T(8,128)(2,1)S(1)} %pad_maximum_fusion.10), channel_id=1, source_target_pairs={{4,0},{5,1},{6,2},{7,3},{12,8},{13,9},{14,10},{15,11},{20,16},{21,... | collective-permute-start | bytes 589832 | tf_op jit(solution)/shard_map/ppermute | solution.py:481
  87.0 1.6 %collective-permute-start.28 = (bf16[3,64,768]{2,1,0:T(8,128)(2,1)S(1)}, bf16[3,64,768]{2,1,0:T(8,128)(2,1)S(1)}, u32[]{:S(2)}, u32[]{:S(2)}) collective-permute-start(bf16[3,64,768]{2,1,0:T(8,128)(2,1)S(1)} %pad_maximum_fusion.3), channel_id=1, source_target_pairs={{0,16},{8,24},{16,0},{24,8},{1,17},{9,25},{17,1},{25,9},{2,18},{10... | collective-permute-start | bytes 884744 | tf_op jit(solution)/shard_map/ppermute | solution.py:466
  88.6 2.1 %collective-permute-start.29 = (bf16[3,64,768]{2,1,0:T(8,128)(2,1)S(1)}, bf16[3,64,768]{2,1,0:T(8,128)(2,1)S(1)}, u32[]{:S(2)}, u32[]{:S(2)}) collective-permute-start(bf16[3,64,768]{2,1,0:T(8,128)(2,1)S(1)} %pad_maximum_fusion.4), channel_id=1, source_target_pairs={{0,1},{1,0},{2,3},{3,2},{4,5},{5,4},{6,7},{7,6},{8,9},{9,8},{10,11... | collective-permute-start | bytes 884744 | tf_op jit(solution)/shard_map/ppermute | solution.py:466
  90.9 2.9 %collective-permute-done.28 = bf16[3,64,768]{2,1,0:T(8,128)(2,1)S(1)} collective-permute-done((bf16[3,64,768]{2,1,0:T(8,128)(2,1)S(1)}, bf16[3,64,768]{2,1,0:T(8,128)(2,1)S(1)}, u32[]{:S(2)}, u32[]{:S(2)}) %collective-permute-start.28) | collective-permute-done | bytes 294944 | tf_op jit(solution)/shard_map/ppermute | solution.py:466
  93.8 1.6 %collective-permute-done.29 = bf16[3,64,768]{2,1,0:T(8,128)(2,1)S(1)} collective-permute-done((bf16[3,64,768]{2,1,0:T(8,128)(2,1)S(1)}, bf16[3,64,768]{2,1,0:T(8,128)(2,1)S(1)}, u32[]{:S(2)}, u32[]{:S(2)}) %collective-permute-start.29) | collective-permute-done | bytes 294944 | tf_op jit(solution)/shard_map/ppermute | solution.py:466
  96.0 2.3 %place.2 = (bf16[2,64,12288]{2,1,0:T(8,128)(2,1)}, bf16[2,64,12288]{2,1,0:T(8,128)(2,1)}) custom-call(s32[4,3]{1,0:T(4,128)S(1)} %copy-done.7, bf16[8,64,768]{2,1,0:T(8,128)(2,1)S(1)} %constant_dynamic-update-slice_fusion.3.refs_0_, bf16[8,64,768]{2,1,0:T(8,128)(2,1)S(1)} %collective-permute-done.32.refs_1_, ...), custom_call_target="tpu_custom_call" | custom-call | bytes 9437184 | tf_op jit(solution)/shard_map/place/pallas_call | solution.py:447
  98.3 1.3 %place.3 = (bf16[2,64,12288]{2,1,0:T(8,128)(2,1)}, bf16[2,64,12288]{2,1,0:T(8,128)(2,1)}) custom-call(s32[4,3]{1,0:T(4,128)S(1)} %copy-done.7, bf16[8,64,768]{2,1,0:T(8,128)(2,1)S(1)} %constant_dynamic-update-slice_fusion.refs_0_, bf16[8,64,768]{2,1,0:T(8,128)(2,1)S(1)} %collective-permute-done.31.refs_1_, ...), custom_call_target="tpu_custom_call", output_to_operand_aliasing={{0}: (3, {}), {1}: (4, {})} | custom-call | bytes 3145728 | tf_op jit(solution)/shard_map/place/pallas_call | solution.py:447
  (92 shorter events, 7.5 us)
Async XLA Ops:
  1.7 9.0 %collective-permute-start = (bf16[128,768]{1,0:T(8,128)(2,1)S(1)}, bf16[128,768]{1,0:T(8,128)(2,1)S(1)}, u32[]{:S(2)}, u32[]{:S(2)}) collective-permute-start(bf16[128,768]{1,0:T(8,128)(2,1)S(1)} %pad_maximum_fusion.5.refs_0_), channel_id=1, source_target_pairs={{4,0},{0,4},{5,1},{1,5},{6,2},{2,6},{7,3},{3,7},{12,8},{8,12},{13,... | collective-permute-start | bytes 589832 | tf_op jit(solution)/shard_map/ppermute | solution.py:476
  4.7 8.1 %copy-start = (bf16[1,4,32,12288]{3,2,1,0:T(8,128)(2,1)S(1)}, bf16[1,4,32,12288]{3,2,1,0:T(8,128)(2,1)}, u32[]{:S(2)}) copy-start(bf16[1,4,32,12288]{3,2,1,0:T(8,128)(2,1)} %param.13) | copy-start | bytes 9437188
  4.7 8.1 %copy-start.8 = (s32[4]{0:T(128)S(1)}, s32[4]{0:T(128)}, u32[]{:S(2)}) copy-start(s32[4]{0:T(128)} %param.14) | copy-start | bytes 52
  10.9 3.7 %collective-permute-start.4 = (f32[64,128]{1,0:T(8,128)S(1)}, f32[64,128]{1,0:T(8,128)S(1)}, u32[]{:S(2)}, u32[]{:S(2)}) collective-permute-start(f32[64,128]{1,0:T(8,128)S(1)} %get-tuple-element.49), channel_id=1, source_target_pairs={{0,24},{8,16},{16,8},{24,0},{1,25},{9,17},{17,9},{25,1},{2,26},{10... | collective-permute-start | bytes 98312 | tf_op jit(solution)/shard_map/ppermute | solution.py:466
  11.7 4.2 %collective-permute-start.3 = (f32[64,128]{1,0:T(8,128)S(1)}, f32[64,128]{1,0:T(8,128)S(1)}, u32[]{:S(2)}, u32[]{:S(2)}) collective-permute-start(f32[64,128]{1,0:T(8,128)S(1)} %get-tuple-element.49), channel_id=1, source_target_pairs={{0,16},{8,24},{16,0},{24,8},{1,17},{9,25},{17,1},{25,9},{2,18},{10... | collective-permute-start | bytes 98312 | tf_op jit(solution)/shard_map/ppermute | solution.py:466
  12.6 3.3 %collective-permute-start.2 = (f32[64,128]{1,0:T(8,128)S(1)}, f32[64,128]{1,0:T(8,128)S(1)}, u32[]{:S(2)}, u32[]{:S(2)}) collective-permute-start(f32[64,128]{1,0:T(8,128)S(1)} %get-tuple-element.49), channel_id=1, source_target_pairs={{0,8},{8,0},{16,24},{24,16},{1,9},{9,1},{17,25},{25,17},{2,10},{10... | collective-permute-start | bytes 98312 | tf_op jit(solution)/shard_map/ppermute | solution.py:466
  12.8 11.9 %copy-start.7 = (s32[4,3]{1,0:T(4,128)S(1)}, s32[4,3]{1,0:T(4,128)}, u32[]{:S(2)}) copy-start(s32[4,3]{1,0:T(4,128)} %bounds.5) | copy-start | bytes 148
  13.8 10.9 %collective-permute-start.1 = (f32[128,384]{1,0:T(8,128)S(1)}, f32[128,384]{1,0:T(8,128)S(1)}, u32[]{:S(2)}, u32[]{:S(2)}) collective-permute-start(f32[128,384]{1,0:T(8,128)S(1)} %project_back.1.refs_0_), channel_id=1, source_target_pairs={{4,0},{0,4},{5,1},{1,5},{6,2},{2,6},{7,3},{3,7},{12,8},{8,12},{13,... | collective-permute-start | bytes 589832 | tf_op jit(solution)/shard_map/ppermute | solution.py:476
  15.9 4.0 %collective-permute-start.5 = (f32[64,128]{1,0:T(8,128)S(1)}, f32[64,128]{1,0:T(8,128)S(1)}, u32[]{:S(2)}, u32[]{:S(2)}) collective-permute-start(f32[64,128]{1,0:T(8,128)S(1)} %add_add_fusion), channel_id=1, source_target_pairs={{0,1},{1,0},{2,3},{3,2},{4,5},{5,4},{6,7},{7,6},{8,9},{9,8},{10,11... | collective-permute-start | bytes 98312 | tf_op jit(solution)/shard_map/ppermute | solution.py:466
  19.9 4.8 %collective-permute-start.6 = (f32[64,128]{1,0:T(8,128)S(1)}, f32[64,128]{1,0:T(8,128)S(1)}, u32[]{:S(2)}, u32[]{:S(2)}) collective-permute-start(f32[64,128]{1,0:T(8,128)S(1)} %add.74.refs_2_), channel_id=1, source_target_pairs={{0,2},{1,3},{2,0},{3,1},{4,6},{5,7},{6,4},{7,5},{8,10},{9,11},{10,... | collective-permute-start | bytes 98312 | tf_op jit(solution)/shard_map/ppermute | solution.py:466
  26.8 2.4 %collective-permute-start.8 = (bf16[2,4,64,768]{3,2,1,0:T(8,128)(2,1)S(1)}, bf16[2,4,64,768]{3,2,1,0:T(8,128)(2,1)S(1)}, u32[]{:S(2)}, u32[]{:S(2)}) collective-permute-start(bf16[2,4,64,768]{3,2,1,0:T(8,128)(2,1)S(1)} %gradient.7), channel_id=1, source_target_pairs={{0,8},{8,0},{16,24},{24,16},{1,9},{9,1},{17,25},{25,17},{2,10},{10... | collective-permute-start | bytes 2359304 | tf_op jit(solution)/shard_map/ppermute | solution.py:466
  27.4 14.5 %collective-permute-start.7 = (bf16[2,4,64,768]{3,2,1,0:T(8,128)(2,1)S(1)}, bf16[2,4,64,768]{3,2,1,0:T(8,128)(2,1)S(1)}, u32[]{:S(2)}, u32[]{:S(2)}) collective-permute-start(bf16[2,4,64,768]{3,2,1,0:T(8,128)(2,1)S(1)} %gradient.5), channel_id=1, source_target_pairs={{0,8},{8,0},{16,24},{24,16},{1,9},{9,1},{17,25},{25,17},{2,10},{10... | collective-permute-start | bytes 2359304 | tf_op jit(solution)/shard_map/ppermute | solution.py:466
  28.0 3.8 %collective-permute-start.11 = (bf16[128,128]{1,0:T(8,128)(2,1)S(1)}, bf16[128,128]{1,0:T(8,128)(2,1)S(1)}, u32[]{:S(2)}, u32[]{:S(2)}) collective-permute-start(bf16[128,128]{1,0:T(8,128)(2,1)S(1)} %convert_element_type.132), channel_id=1, source_target_pairs={{0,8},{8,0},{16,24},{24,16},{1,9},{9,1},{17,25},{25,17},{2,10},{10... | collective-permute-start | bytes 98312 | tf_op jit(solution)/shard_map/ppermute | solution.py:466
  29.4 11.9 %collective-permute-start.10 = (bf16[4,64,768]{2,1,0:T(8,128)(2,1)S(1)}, bf16[4,64,768]{2,1,0:T(8,128)(2,1)S(1)}, u32[]{:S(2)}, u32[]{:S(2)}) collective-permute-start(bf16[4,64,768]{2,1,0:T(8,128)(2,1)S(1)} %get-tuple-element.82), channel_id=1, source_target_pairs={{0,1},{1,0},{2,3},{3,2},{4,5},{5,4},{6,7},{7,6},{8,9},{9,8},{10,11... | collective-permute-start | bytes 1179656 | tf_op jit(solution)/shard_map/ppermute | solution.py:466
  31.0 10.9 %collective-permute-start.9 = (bf16[4,64,768]{2,1,0:T(8,128)(2,1)S(1)}, bf16[4,64,768]{2,1,0:T(8,128)(2,1)S(1)}, u32[]{:S(2)}, u32[]{:S(2)}) collective-permute-start(bf16[4,64,768]{2,1,0:T(8,128)(2,1)S(1)} %get-tuple-element.83), channel_id=1, source_target_pairs={{0,16},{8,24},{16,0},{24,8},{1,17},{9,25},{17,1},{25,9},{2,18},{10... | collective-permute-start | bytes 1179656 | tf_op jit(solution)/shard_map/ppermute | solution.py:466
  31.8 8.6 %collective-permute-start.12 = (bf16[128,128]{1,0:T(8,128)(2,1)S(1)}, bf16[128,128]{1,0:T(8,128)(2,1)S(1)}, u32[]{:S(2)}, u32[]{:S(2)}) collective-permute-start(bf16[128,128]{1,0:T(8,128)(2,1)S(1)} %fusion.6), channel_id=1, source_target_pairs={{0,2},{1,3},{2,0},{3,1},{4,6},{5,7},{6,4},{7,5},{8,10},{9,11},{10,... | collective-permute-start | bytes 98312 | tf_op jit(solution)/shard_map/ppermute | solution.py:466
  35.2 23.0 %copy-start.1 = (f32[1,64,768]{2,1,0:T(8,128)S(1)}, f32[1,64,768]{2,1,0:T(8,128)}, u32[]{:S(2)}) copy-start(f32[1,64,768]{2,1,0:T(8,128)} %refs_0_.3) | copy-start | bytes 589828
  35.2 23.0 %copy-start.3 = (f32[1,64,768]{2,1,0:T(8,128)S(1)}, f32[1,64,768]{2,1,0:T(8,128)}, u32[]{:S(2)}) copy-start(f32[1,64,768]{2,1,0:T(8,128)} %refs_1_.3) | copy-start | bytes 589828
  35.2 23.0 %copy-start.4 = (f32[1,64,768]{2,1,0:T(8,128)S(1)}, f32[1,64,768]{2,1,0:T(8,128)}, u32[]{:S(2)}) copy-start(f32[1,64,768]{2,1,0:T(8,128)} %refs_2_.3) | copy-start | bytes 589828
  35.2 25.7 %copy-start.2 = (f32[1,64,768]{2,1,0:T(8,128)S(1)}, f32[1,64,768]{2,1,0:T(8,128)}, u32[]{:S(2)}) copy-start(f32[1,64,768]{2,1,0:T(8,128)} %refs_0_.2) | copy-start | bytes 589828
  35.2 25.7 %copy-start.5 = (f32[1,64,768]{2,1,0:T(8,128)S(1)}, f32[1,64,768]{2,1,0:T(8,128)}, u32[]{:S(2)}) copy-start(f32[1,64,768]{2,1,0:T(8,128)} %refs_1_.2) | copy-start | bytes 589828
  35.2 25.7 %copy-start.6 = (f32[1,64,768]{2,1,0:T(8,128)S(1)}, f32[1,64,768]{2,1,0:T(8,128)}, u32[]{:S(2)}) copy-start(f32[1,64,768]{2,1,0:T(8,128)} %refs_2_.2) | copy-start | bytes 589828
  42.1 5.9 %collective-permute-start.18 = (bf16[2,64,768]{2,1,0:T(8,128)(2,1)S(1)}, bf16[2,64,768]{2,1,0:T(8,128)(2,1)S(1)}, u32[]{:S(2)}, u32[]{:S(2)}) collective-permute-start(bf16[2,64,768]{2,1,0:T(8,128)(2,1)S(1)} %get-tuple-element.80), channel_id=1, source_target_pairs={{0,16},{8,24},{16,0},{24,8},{1,17},{9,25},{17,1},{25,9},{2,18},{10... | collective-permute-start | bytes 589832 | tf_op jit(solution)/shard_map/ppermute | solution.py:466
  42.9 10.4 %collective-permute-start.15 = (bf16[128,128]{1,0:T(8,128)(2,1)S(1)}, bf16[128,128]{1,0:T(8,128)(2,1)S(1)}, u32[]{:S(2)}, u32[]{:S(2)}) collective-permute-start(bf16[128,128]{1,0:T(8,128)(2,1)S(1)} %convert_element_type.147), channel_id=1, source_target_pairs={{0,1},{1,0},{2,3},{3,2},{4,5},{5,4},{6,7},{7,6},{8,9},{9,8},{10,11... | collective-permute-start | bytes 98312 | tf_op jit(solution)/shard_map/ppermute | solution.py:466
  45.0 6.7 %collective-permute-start.13 = (bf16[2,64,768]{2,1,0:T(8,128)(2,1)S(1)}, bf16[2,64,768]{2,1,0:T(8,128)(2,1)S(1)}, u32[]{:S(2)}, u32[]{:S(2)}) collective-permute-start(bf16[2,64,768]{2,1,0:T(8,128)(2,1)S(1)} %get-tuple-element.81), channel_id=1, source_target_pairs={{0,1},{1,0},{2,3},{3,2},{4,5},{5,4},{6,7},{7,6},{8,9},{9,8},{10,11... | collective-permute-start | bytes 589832 | tf_op jit(solution)/shard_map/ppermute | solution.py:466
  48.0 10.2 %collective-permute-start.19 = (bf16[64,768]{1,0:T(8,128)(2,1)S(1)}, bf16[64,768]{1,0:T(8,128)(2,1)S(1)}, u32[]{:S(2)}, u32[]{:S(2)}) collective-permute-start(bf16[64,768]{1,0:T(8,128)(2,1)S(1)} %fusion.4), channel_id=1, source_target_pairs={{0,2},{1,3},{2,0},{3,1},{4,6},{5,7},{6,4},{7,5},{8,10},{9,11},{10,... | collective-permute-start | bytes 294920 | tf_op jit(solution)/shard_map/ppermute | solution.py:466
  51.8 9.2 %collective-permute-start.14 = (bf16[64,768]{1,0:T(8,128)(2,1)S(1)}, bf16[64,768]{1,0:T(8,128)(2,1)S(1)}, u32[]{:S(2)}, u32[]{:S(2)}) collective-permute-start(bf16[64,768]{1,0:T(8,128)(2,1)S(1)} %fusion.5), channel_id=1, source_target_pairs={{0,2},{1,3},{2,0},{3,1},{4,6},{5,7},{6,4},{7,5},{8,10},{9,11},{10,... | collective-permute-start | bytes 294920 | tf_op jit(solution)/shard_map/ppermute | solution.py:466
  53.3 4.0 %collective-permute-start.16 = (bf16[128,128]{1,0:T(8,128)(2,1)S(1)}, bf16[128,128]{1,0:T(8,128)(2,1)S(1)}, u32[]{:S(2)}, u32[]{:S(2)}) collective-permute-start(bf16[128,128]{1,0:T(8,128)(2,1)S(1)} %get-tuple-element.78), channel_id=1, source_target_pairs={{0,16},{8,24},{16,0},{24,8},{1,17},{9,25},{17,1},{25,9},{2,18},{10... | collective-permute-start | bytes 98312 | tf_op jit(solution)/shard_map/ppermute | solution.py:466
  59.4 7.7 %collective-permute-start.20 = (bf16[1,64,768]{2,1,0:T(8,128)(2,1)S(1)}, bf16[1,64,768]{2,1,0:T(8,128)(2,1)S(1)}, u32[]{:S(2)}, u32[]{:S(2)}) collective-permute-start(bf16[1,64,768]{2,1,0:T(8,128)(2,1)S(1)} %get-tuple-element.63), channel_id=1, source_target_pairs={{0,2},{1,3},{2,0},{3,1},{4,6},{5,7},{6,4},{7,5},{8,10},{9,11},{10,... | collective-permute-start | bytes 294920 | tf_op jit(solution)/shard_map/ppermute | solution.py:466
  62.2 6.1 %collective-permute-start.17 = (bf16[1,64,768]{2,1,0:T(8,128)(2,1)S(1)}, bf16[1,64,768]{2,1,0:T(8,128)(2,1)S(1)}, u32[]{:S(2)}, u32[]{:S(2)}) collective-permute-start(bf16[1,64,768]{2,1,0:T(8,128)(2,1)S(1)} %get-tuple-element.62), channel_id=1, source_target_pairs={{0,2},{1,3},{2,0},{3,1},{4,6},{5,7},{6,4},{7,5},{8,10},{9,11},{10,... | collective-permute-start | bytes 294920 | tf_op jit(solution)/shard_map/ppermute | solution.py:466
  63.6 8.0 %collective-permute-start.21 = (bf16[2,64,768]{2,1,0:T(8,128)(2,1)S(1)}, bf16[2,64,768]{2,1,0:T(8,128)(2,1)S(1)}, u32[]{:S(2)}, u32[]{:S(2)}) collective-permute-start(bf16[2,64,768]{2,1,0:T(8,128)(2,1)S(1)} %pad_maximum_fusion.6), channel_id=1, source_target_pairs={{4,0},{5,1},{6,2},{7,3},{12,8},{13,9},{14,10},{15,11},{20,16},{21,... | collective-permute-start | bytes 589832 | tf_op jit(solution)/shard_map/ppermute | solution.py:481
  67.1 5.9 %collective-permute-start.25 = (bf16[2,64,768]{2,1,0:T(8,128)(2,1)S(1)}, bf16[2,64,768]{2,1,0:T(8,128)(2,1)S(1)}, u32[]{:S(2)}, u32[]{:S(2)}) collective-permute-start(bf16[2,64,768]{2,1,0:T(8,128)(2,1)S(1)} %pad_maximum_fusion.9), channel_id=1, source_target_pairs={{0,16},{8,24},{16,0},{24,8},{1,17},{9,25},{17,1},{25,9},{2,18},{10... | collective-permute-start | bytes 589832 | tf_op jit(solution)/shard_map/ppermute | solution.py:466
  68.3 7.1 %collective-permute-start.23 = (bf16[2,64,768]{2,1,0:T(8,128)(2,1)S(1)}, bf16[2,64,768]{2,1,0:T(8,128)(2,1)S(1)}, u32[]{:S(2)}, u32[]{:S(2)}) collective-permute-start(bf16[2,64,768]{2,1,0:T(8,128)(2,1)S(1)} %pad_maximum_fusion.8), channel_id=1, source_target_pairs={{0,1},{1,0},{2,3},{3,2},{4,5},{5,4},{6,7},{7,6},{8,9},{9,8},{10,11... | collective-permute-start | bytes 589832 | tf_op jit(solution)/shard_map/ppermute | solution.py:466
  71.6 9.7 %collective-permute-start.22 = (bf16[2,64,768]{2,1,0:T(8,128)(2,1)S(1)}, bf16[2,64,768]{2,1,0:T(8,128)(2,1)S(1)}, u32[]{:S(2)}, u32[]{:S(2)}) collective-permute-start(bf16[2,64,768]{2,1,0:T(8,128)(2,1)S(1)} %pad_maximum_fusion.7), channel_id=1, source_target_pairs={{4,0},{5,1},{6,2},{7,3},{12,8},{13,9},{14,10},{15,11},{20,16},{21,... | collective-permute-start | bytes 589832 | tf_op jit(solution)/shard_map/ppermute | solution.py:481
  75.5 10.1 %collective-permute-start.27 = (bf16[4,64,768]{2,1,0:T(8,128)(2,1)S(1)}, bf16[4,64,768]{2,1,0:T(8,128)(2,1)S(1)}, u32[]{:S(2)}, u32[]{:S(2)}) collective-permute-start(bf16[4,64,768]{2,1,0:T(8,128)(2,1)S(1)} %get-tuple-element.90), channel_id=1, source_target_pairs={{4,0},{5,1},{6,2},{7,3},{12,8},{13,9},{14,10},{15,11},{20,16},{21,... | collective-permute-start | bytes 1179656 | tf_op jit(solution)/shard_map/ppermute | solution.py:481
  76.8 8.8 %collective-permute-start.24 = (bf16[4,64,768]{2,1,0:T(8,128)(2,1)S(1)}, bf16[4,64,768]{2,1,0:T(8,128)(2,1)S(1)}, u32[]{:S(2)}, u32[]{:S(2)}) collective-permute-start(bf16[4,64,768]{2,1,0:T(8,128)(2,1)S(1)} %get-tuple-element.91), channel_id=1, source_target_pairs={{0,16},{8,24},{16,0},{24,8},{1,17},{9,25},{17,1},{25,9},{2,18},{10... | collective-permute-start | bytes 1179656 | tf_op jit(solution)/shard_map/ppermute | solution.py:466
  76.8 8.7 %collective-permute-start.26 = (bf16[4,64,768]{2,1,0:T(8,128)(2,1)S(1)}, bf16[4,64,768]{2,1,0:T(8,128)(2,1)S(1)}, u32[]{:S(2)}, u32[]{:S(2)}) collective-permute-start(bf16[4,64,768]{2,1,0:T(8,128)(2,1)S(1)} %get-tuple-element.92), channel_id=1, source_target_pairs={{0,1},{1,0},{2,3},{3,2},{4,5},{5,4},{6,7},{7,6},{8,9},{9,8},{10,11... | collective-permute-start | bytes 1179656 | tf_op jit(solution)/shard_map/ppermute | solution.py:466
  79.4 16.1 %collective-permute-start.32 = (bf16[8,64,768]{2,1,0:T(8,128)(2,1)S(1)}, bf16[8,64,768]{2,1,0:T(8,128)(2,1)S(1)}, u32[]{:S(2)}, u32[]{:S(2)}) collective-permute-start(bf16[8,64,768]{2,1,0:T(8,128)(2,1)S(1)} %constant_dynamic-update-slice_fusion.3.refs_0_), channel_id=1, source_target_pairs={{0,8},{8,0},{16,24},{24,16},{1,9},{9,1},{17,25},{25,17},{2,10},{10... | collective-permute-start | bytes 2359304 | tf_op jit(solution)/shard_map/ppermute | solution.py:466
  85.6 9.8 %collective-permute-start.30 = (bf16[2,64,768]{2,1,0:T(8,128)(2,1)S(1)}, bf16[2,64,768]{2,1,0:T(8,128)(2,1)S(1)}, u32[]{:S(2)}, u32[]{:S(2)}) collective-permute-start(bf16[2,64,768]{2,1,0:T(8,128)(2,1)S(1)} %pad_maximum_fusion.10), channel_id=1, source_target_pairs={{4,0},{5,1},{6,2},{7,3},{12,8},{13,9},{14,10},{15,11},{20,16},{21,... | collective-permute-start | bytes 589832 | tf_op jit(solution)/shard_map/ppermute | solution.py:481
  87.0 6.8 %collective-permute-start.28 = (bf16[3,64,768]{2,1,0:T(8,128)(2,1)S(1)}, bf16[3,64,768]{2,1,0:T(8,128)(2,1)S(1)}, u32[]{:S(2)}, u32[]{:S(2)}) collective-permute-start(bf16[3,64,768]{2,1,0:T(8,128)(2,1)S(1)} %pad_maximum_fusion.3), channel_id=1, source_target_pairs={{0,16},{8,24},{16,0},{24,8},{1,17},{9,25},{17,1},{25,9},{2,18},{10... | collective-permute-start | bytes 884744 | tf_op jit(solution)/shard_map/ppermute | solution.py:466
  88.6 6.8 %collective-permute-start.29 = (bf16[3,64,768]{2,1,0:T(8,128)(2,1)S(1)}, bf16[3,64,768]{2,1,0:T(8,128)(2,1)S(1)}, u32[]{:S(2)}, u32[]{:S(2)}) collective-permute-start(bf16[3,64,768]{2,1,0:T(8,128)(2,1)S(1)} %pad_maximum_fusion.4), channel_id=1, source_target_pairs={{0,1},{1,0},{2,3},{3,2},{4,5},{5,4},{6,7},{7,6},{8,9},{9,8},{10,11... | collective-permute-start | bytes 884744 | tf_op jit(solution)/shard_map/ppermute | solution.py:466
  90.8 4.8 %collective-permute-start.33 = (bf16[8,64,768]{2,1,0:T(8,128)(2,1)S(1)}, bf16[8,64,768]{2,1,0:T(8,128)(2,1)S(1)}, u32[]{:S(2)}, u32[]{:S(2)}) collective-permute-start(bf16[8,64,768]{2,1,0:T(8,128)(2,1)S(1)} %constant_dynamic-update-slice_fusion.9.refs_2_), channel_id=1, source_target_pairs={{0,8},{8,0},{16,24},{24,16},{1,9},{9,1},{17,25},{25,17},{2,10},{10... | collective-permute-start | bytes 2359304 | tf_op jit(solution)/shard_map/ppermute | solution.py:466
  93.7 2.3 %collective-permute-start.34 = (bf16[8,64,768]{2,1,0:T(8,128)(2,1)S(1)}, bf16[8,64,768]{2,1,0:T(8,128)(2,1)S(1)}, u32[]{:S(2)}, u32[]{:S(2)}) collective-permute-start(bf16[8,64,768]{2,1,0:T(8,128)(2,1)S(1)} %constant_dynamic-update-slice_fusion.11.refs_4_), channel_id=1, source_target_pairs={{0,8},{8,0},{16,24},{24,16},{1,9},{9,1},{17,25},{25,17},{2,10},{10... | collective-permute-start | bytes 2359304 | tf_op jit(solution)/shard_map/ppermute | solution.py:466
  95.5 2.9 %collective-permute-start.31 = (bf16[8,64,768]{2,1,0:T(8,128)(2,1)S(1)}, bf16[8,64,768]{2,1,0:T(8,128)(2,1)S(1)}, u32[]{:S(2)}, u32[]{:S(2)}) collective-permute-start(bf16[8,64,768]{2,1,0:T(8,128)(2,1)S(1)} %constant_dynamic-update-slice_fusion.refs_0_), channel_id=1, source_target_pairs={{0,8},{8,0},{16,24},{24,16},{1,9},{9,1},{17,25},{25,17},{2,10},{10... | collective-permute-start | bytes 2359304 | tf_op jit(solution)/shard_map/ppermute | solution.py:466

commit v11 on v10

--- a/solution.py
+++ b/solution.py
@@ -63,8 +63,7 @@
     return jnp.sum(x, axis=-1, keepdims=True)
 
 
-def project_kernel(steps, h_in, down_in, up_in, *refs):
-    out_ref, sq_ref, h_ref, up_ref, down_ref, sems = refs
+def project_down_kernel(steps, h_in, down_in, out_ref, sq_ref, h_ref, down_ref, sems):
     slots, ranks, features = down_in.shape
     tokens = h_ref.shape[0]
     width = features // steps
@@ -75,7 +74,6 @@
         for slot in range(slots):
             rows = pl.ds(slot * ranks, ranks)
             moves.append((down_in.at[slot, :, cut], down_ref.at[rows, cut]))
-            moves.append((up_in.at[slot, :, cut], up_ref.at[rows, cut]))
         copies.append(
             [
                 pltpu.make_async_copy(source, target, sems.at[step, i])
@@ -84,75 +82,75 @@
         )
         for copy in copies[-1]:
             copy.start()
-    ph = jnp.zeros((tokens, 2 * slots * ranks), f32)
+    total = jnp.zeros((tokens, slots * ranks), f32)
     square = jnp.zeros((tokens, 128), f32)
     for step in range(steps):
         for copy in copies[step]:
             copy.wait()
         cut = pl.ds(step * width, width)
         h = h_ref[:, cut]
-        ph = ph + dot_last(h, jnp.concatenate([down_ref[:, cut], up_ref[:, cut]], axis=0))
+        total = total + dot_last(h, down_ref[:, cut])
         wide = h.astype(f32)
         wide = wide * wide
         for lane in range(0, width, 128):
             square = square + wide[:, lane : lane + 128]
     sq_ref[...] = jnp.broadcast_to(row_sum(square), square.shape)
-    out_ref[...] = ph
-
-
-def project(hidden, downs, ups):
+    out_ref[...] = total
+
+
+def project_down(hidden, downs):
     tokens, features = hidden.shape
     slots, ranks, _ = downs.shape
     steps = 8
-    sources = [pltpu.with_memory_space_constraint(x, pltpu.HBM) for x in (hidden, downs, ups)]
+    sources = [pltpu.with_memory_space_constraint(x, pltpu.HBM) for x in (hidden, downs)]
     return pl.pallas_call(
-        functools.partial(project_kernel, steps),
-        in_specs=[in_hbm] * 3,
-        out_specs=[in_vmem] * 4,
+        functools.partial(project_down_kernel, steps),
+        in_specs=[in_hbm] * 2,
+        out_specs=[in_vmem] * 3,
         out_shape=[
-            jax.ShapeDtypeStruct((tokens, 2 * slots * ranks), f32),
+            jax.ShapeDtypeStruct((tokens, slots * ranks), f32),
             jax.ShapeDtypeStruct((tokens, 128), f32),
             jax.ShapeDtypeStruct((tokens, features), bf16),
-            jax.ShapeDtypeStruct((slots * ranks, features), bf16),
         ],
         scratch_shapes=[
             pltpu.VMEM((slots * ranks, features), bf16),
-            pltpu.SemaphoreType.DMA((steps, 1 + 2 * slots)),
+            pltpu.SemaphoreType.DMA((steps, 1 + slots)),
         ],
         compiler_params=limited,
         cost_estimate=pl.CostEstimate(
-            flops=4 * tokens * slots * ranks * features,
-            bytes_accessed=2 * (tokens + 2 * slots * ranks) * features,
+            flops=2 * tokens * slots * ranks * features,
+            bytes_accessed=2 * (tokens + slots * ranks) * features,
             transcendentals=0,
         ),
-        name="project",
+        name="project_down",
     )(*sources)
 
 
-def project_back_kernel(per_micro, counts, by_hidden, g_ref, up_ref, out_ref):
-    pg = dot_last(g_ref[...], up_ref[...])
-    pg = jnp.where(counted_rows(counts, pg.shape[0], per_micro), pg, 0.0)
-    ahead = by_hidden.shape[1]
-    out_ref[:, :ahead] = by_hidden[...]
-    out_ref[:, ahead:] = pg
-
-
-def project_back(counts, by_hidden, cot, ups, per_micro):
-    tokens, features = cot.shape
-    columns = by_hidden.shape[1] + ups.shape[0]
+def project_up_kernel(per_micro, counts, by_down, h_ref, g_ref, up_ref, out_ref):
+    tokens, columns = by_down.shape
+    ups = up_ref[...].reshape(columns, up_ref.shape[2])
+    out_ref[:, :columns] = by_down[...]
+    out_ref[:, columns : 2 * columns] = dot_last(h_ref[...], ups)
+    by_cot = dot_last(g_ref[...], ups)
+    out_ref[:, 2 * columns :] = jnp.where(counted_rows(counts, tokens, per_micro), by_cot, 0.0)
+
+
+def project_up(counts, by_down, hidden, cot, ups, per_micro):
+    tokens, features = hidden.shape
+    columns = by_down.shape[1]
     return pl.pallas_call(
-        functools.partial(project_back_kernel, per_micro),
-        in_specs=[in_vmem] * 4,
+        functools.partial(project_up_kernel, per_micro),
+        in_specs=[in_vmem] * 5,
         out_specs=in_vmem,
-        out_shape=jax.ShapeDtypeStruct((tokens, columns), f32),
+        out_shape=jax.ShapeDtypeStruct((tokens, 3 * columns), f32),
         compiler_params=limited,
         cost_estimate=pl.CostEstimate(
-            flops=2 * tokens * ups.shape[0] * features,
-            bytes_accessed=2 * (tokens + ups.shape[0]) * features,
+            flops=4 * tokens * columns * features,
+            bytes_accessed=2 * (2 * tokens + columns) * features,
             transcendentals=0,
         ),
-        name="project_back",
-    )(counts, by_hidden, cot, ups)
+        name="project_up",
+    )(counts, by_down, hidden, cot, ups)
 
 
 def gram_kernel(sections, *refs):
@@ -160,15 +158,21 @@
     gram_ref, right_ref = refs[sections:]
     section_at = lax.axis_index("section")
     ranks = around[0].shape[0] // 2
-    layers = []
-    for layer in range(sections):
-        distance = lax.rem(layer - section_at + sections, sections)
-        chosen = around[0][...]
-        for step in range(1, sections):
-            chosen = jnp.where(distance == step, around[step][...], chosen)
-        layers.append(chosen)
-    lefts = [chosen[ranks:] for chosen in layers[:-1]]
-    right = jnp.concatenate([chosen[:ranks] for chosen in layers[1:]] + lefts, axis=0)
+    if sections == 2:
+        own, other = around[0][...], around[1][...]
+        downs = [jnp.where(section_at == 0, other, own[:ranks])]
+        lefts = [jnp.where(section_at == 0, own[ranks:], other)]
+    else:
+        layers = []
+        for layer in range(sections):
+            distance = lax.rem(layer - section_at + sections, sections)
+            chosen = around[0][...]
+            for step in range(1, sections):
+                chosen = jnp.where(distance == step, around[step][...], chosen)
+            layers.append(chosen)
+        downs = [chosen[:ranks] for chosen in layers[1:]]
+        lefts = [chosen[ranks:] for chosen in layers[:-1]]
+    right = jnp.concatenate(downs + lefts, axis=0)
     right_ref[...] = right
     gram_ref[...] = dot_last(jnp.concatenate(lefts, axis=0), right)
 
@@ -606,12 +610,17 @@
     cot = cotangent.reshape(micros * per_micro, features)
 
     owned = jnp.concatenate([master_down[0], master_up[0]], axis=0).astype(bf16)
-    around = [from_next(owned, d) for d in range(1, sections)]
-    by_hidden, square, hidden, ups = project(hidden, holder_down[0, 0], holder_up[0, 0])
-    around, by_hidden = lax.optimization_barrier((around, by_hidden))
+    if sections == 2:
+        first = lax.axis_index("section") == 0
+        needed = jnp.where(first, master_up[0], master_down[0]).astype(bf16)
+    else:
+        needed = owned
+    around = [from_next(needed, d) for d in range(1, sections)]
+    by_down, square, hidden = project_down(hidden, holder_down[0, 0])
+    around, by_down = lax.optimization_barrier((around, by_down))
     table, right = gram([owned, *around])
-    table, ups = lax.optimization_barrier((table, ups))
-    projected = project_back(micro_counts, by_hidden, cot, ups, per_micro)
+    table, hidden = lax.optimization_barrier((table, hidden))
+    projected = project_up(micro_counts, by_down, hidden, cot, holder_up[0, 0], per_micro)
     table = table + sum(swaps(table, "replica"))
     projections = [projected] + [from_next(projected, d) for d in range(1, sections)]
     table = table + swapped(table, "tensor", 1)

time: 99.9 us -> 101 us (1.011)
  starting transfers between devices: 41.9 us -> 43.3 us
  Pallas kernels: 16.8 us -> 15.5 us
    ppermute x29, starting transfers between devices: 33.1 us -> 34.8 us  [swapped(): return lax.ppermute(block, axis, route)]
    pallas_call x2, Pallas kernels: 6.97 us -> 5.68 us  [the longest x1 3.87 us: project_down(): pl.pallas_call(functools.partial(project_down_kernel, steps), in_specs=[i...]
    squeeze x1 -> x0, other arithmetic: 1.05 us -> none  [on_device(): owned = jnp.concatenate([master_down[0], master_up[0]], axis=0).astype(bf16)]
    another operation x0 -> x1, other arithmetic: none -> 1.04 us
  transfers between devices with their start and end apart: 35 -> 35, of which waited for: 22 -> 20; matrix products, arithmetic and copies ran while one was open for 1% -> 2% of each run, Pallas kernels for 13% -> 12%
where the time goes in v11:
time: 101 us; the launch traced here: 100 us
  starting transfers between devices  43.3 us (43%)
  waiting for transfers between devices  37.2 us (37%)
  Pallas kernels  15.5 us (15%)
  other arithmetic  2.8 us (3%)
  between operations  1.14 us (1%)
    ppermute x29, starting transfers between devices, swapped(): return lax.ppermute(block, axis, route)  34.8 us
    ppermute x29, waiting for transfers between devices, swapped(): return lax.ppermute(block, axis, route)  31.5 us
    ppermute x4, waiting for transfers between devices, following_layer(): return lax.ppermute(block, 'section', [(i + 1, i) for i in range(size - 1)])  5.72 us
    ppermute x4, starting transfers between devices, following_layer(): return lax.ppermute(block, 'section', [(i + 1, i) for i in range(size - 1)])  5.17 us
    pallas_call x1, Pallas kernels, project_down(): pl.pallas_call(functools.partial(project_down_kernel, steps), in_specs=[i...  3.87 us
    pallas_call x2, Pallas kernels, place(): pl.pallas_call(functools.partial(place_kernel, layout, not before), in_sp...  3.57 us
    ppermute x2, starting transfers between devices, from_next(): return lax.ppermute(block, 'section', route)  3.36 us
    pallas_call x2, Pallas kernels, update(): pl.pallas_call(functools.partial(update_kernel, which), in_specs=[in_vmem...  2.45 us
  transfers between devices with their start and end apart: 35, of which 20 were waited for; matrix products, arithmetic and copies ran while one was open for 2% of the time, Pallas kernels for 12%

profile of v11, /device:TPU:0, one launch (start us, length us, event | category | flops | bytes accessed | tf_op | source)
XLA Modules:
  0.0 100.3 jit_solution(14937260227209243322)
XLA Ops:
  0.6 1.0 fusion.6
  1.6 3.0 %collective-permute-start = (bf16[64,768]{1,0:T(8,128)(2,1)S(1)}, bf16[64,768]{1,0:T(8,128)(2,1)S(1)}, u32[]{:S(2)}, u32[]{:S(2)}) collective-permute-start(bf16[64,768]{1,0:T(8,128)(2,1)S(1)} %fusion.6), channel_id=1, source_target_pairs={{4,0},{0,4},{5,1},{1,5},{6,2},{2,6},{7,3},{3,7},{12,8},{8,12},{13,... | collective-permute-start | bytes 294920 | tf_op jit(solution)/shard_map/ppermute | solution.py:480
  4.6 1.0 %convert_bitcast_fusion = (bf16[64,768]{1,0:T(8,128)(2,1)S(1)}, bf16[64,768]{1,0:T(8,128)(2,1)S(1)}) fusion(f32[1,64,768]{2,1,0:T(8,128)} %refs_0_.3, f32[1,64,768]{2,1,0:T(8,128)} %refs_0_.2), kind=kLoop, calls=%fused_computation.29 | loop fusion | flops 98304 | bytes 589824 | tf_op jit(solution)/shard_map/convert.5
  5.7 3.9 %project_down.1 = (f32[128,128]{1,0:T(8,128)S(1)}, f32[128,128]{1,0:T(8,128)S(1)}, bf16[128,12288]{1,0:T(8,128)(2,1)S(1)}) custom-call(bf16[128,12288]{1,0:T(8,128)(2,1)} %bitcast.53, bf16[2,64,12288]{2,1,0:T(8,128)(2,1)} %bitcast.54), custom_call_target="tpu_custom_call" | custom-call | flops 402653184 | bytes 6291456 | tf_op jit(solution)/shard_map/project_down/pallas_call | solution.py:106
  9.8 0.7 collective-permute-start.4
  10.5 0.9 collective-permute-start.3
  11.7 1.8 %project_up.1.refs_0_ = f32[128,384]{1,0:T(8,128)S(1)} custom-call(s32[1,4]{1,0:T(1,128)S(1)} %bitcast.51, f32[128,128]{1,0:T(8,128)S(1)} %get-tuple-element.43.by_down, bf16[128,12288]{1,0:T(8,128)(2,1)S(1)} %get-tuple-element.47.h_ref, bf16[128,12288]{1,0:T(8,128)(2,1)S(1)} %bitcast.45, bf16[2,64,12288]{2,1,0:T(8,128)(2,1)S(1)} %bitcast.50), custom_call_target="tpu_custom_call" | custom-call | flops 805306368 | bytes 9437184 | tf_op jit(solution)/shard_map/project_up/pallas_call | solution.py:141
  13.9 0.9 collective-permute-done.3
  14.8 1.6 %collective-permute-start.5 = (f32[64,128]{1,0:T(8,128)S(1)}, f32[64,128]{1,0:T(8,128)S(1)}, u32[]{:S(2)}, u32[]{:S(2)}) collective-permute-start(f32[64,128]{1,0:T(8,128)S(1)} %add_add_fusion), channel_id=1, source_target_pairs={{0,1},{1,0},{2,3},{3,2},{4,5},{5,4},{6,7},{7,6},{8,9},{9,8},{10,11... | collective-permute-start | bytes 98312 | tf_op jit(solution)/shard_map/ppermute | solution.py:470
  16.4 2.3 %collective-permute-done.5 = f32[64,128]{1,0:T(8,128)S(1)} collective-permute-done((f32[64,128]{1,0:T(8,128)S(1)}, f32[64,128]{1,0:T(8,128)S(1)}, u32[]{:S(2)}, u32[]{:S(2)}) %collective-permute-start.5) | collective-permute-done | bytes 32800 | tf_op jit(solution)/shard_map/ppermute | solution.py:470
  18.8 2.6 %collective-permute-start.6 = (f32[64,128]{1,0:T(8,128)S(1)}, f32[64,128]{1,0:T(8,128)S(1)}, u32[]{:S(2)}, u32[]{:S(2)}) collective-permute-start(f32[64,128]{1,0:T(8,128)S(1)} %add.74.refs_2_), channel_id=1, source_target_pairs={{0,2},{1,3},{2,0},{3,1},{4,6},{5,7},{6,4},{7,5},{8,10},{9,11},{10,... | collective-permute-start | bytes 98312 | tf_op jit(solution)/shard_map/ppermute | solution.py:470
  21.4 2.2 %collective-permute-done.6.refs_3_ = f32[64,128]{1,0:T(8,128)S(1)} collective-permute-done((f32[64,128]{1,0:T(8,128)S(1)}, f32[64,128]{1,0:T(8,128)S(1)}, u32[]{:S(2)}, u32[]{:S(2)}) %collective-permute-start.6) | collective-permute-done | bytes 32800 | tf_op jit(solution)/shard_map/ppermute | solution.py:470
  23.6 1.6 %chain.1 = (bf16[128,256]{1,0:T(8,128)(2,1)S(1)}, f32[128,128]{1,0:T(8,128)S(1)}) custom-call(s32[4,3]{1,0:T(4,128)S(1)} %copy-done.8, s32[1,4]{1,0:T(1,128)S(1)} %bitcast.52, f32[128,384]{1,0:T(8,128)S(1)} %project_up.1.refs_0_, f32[128,384]{1,0:T(8,128)S(1)} %collective-permute-done.1.refs_1_, f32[64,128]{1,0:T(8,128)S(1)} %add.74.refs_2_, ...), custom_call_target="tpu_custom_call" | custom-call | tf_op jit(solution)/shard_map/chain/pallas_call | solution.py:314
  28.3 1.6 %collective-permute-start.10 = (bf16[4,64,768]{2,1,0:T(8,128)(2,1)S(1)}, bf16[4,64,768]{2,1,0:T(8,128)(2,1)S(1)}, u32[]{:S(2)}, u32[]{:S(2)}) collective-permute-start(bf16[4,64,768]{2,1,0:T(8,128)(2,1)S(1)} %get-tuple-element.80), channel_id=1, source_target_pairs={{0,1},{1,0},{2,3},{3,2},{4,5},{5,4},{6,7},{7,6},{8,9},{9,8},{10,11... | collective-permute-start | bytes 1179656 | tf_op jit(solution)/shard_map/ppermute | solution.py:470
  29.9 0.9 collective-permute-start.9
  30.8 2.9 %collective-permute-start.12 = (bf16[128,128]{1,0:T(8,128)(2,1)S(1)}, bf16[128,128]{1,0:T(8,128)(2,1)S(1)}, u32[]{:S(2)}, u32[]{:S(2)}) collective-permute-start(bf16[128,128]{1,0:T(8,128)(2,1)S(1)} %fusion.7), channel_id=1, source_target_pairs={{0,2},{1,3},{2,0},{3,1},{4,6},{5,7},{6,4},{7,5},{8,10},{9,11},{10,... | collective-permute-start | bytes 98312 | tf_op jit(solution)/shard_map/ppermute | solution.py:470
  34.3 5.0 %collective-permute-done.12 = bf16[128,128]{1,0:T(8,128)(2,1)S(1)} collective-permute-done((bf16[128,128]{1,0:T(8,128)(2,1)S(1)}, bf16[128,128]{1,0:T(8,128)(2,1)S(1)}, u32[]{:S(2)}, u32[]{:S(2)}) %collective-permute-start.12) | collective-permute-done | bytes 32800 | tf_op jit(solution)/shard_map/ppermute | solution.py:470
  39.3 0.9 collective-permute-done.10.one
  41.0 0.9 collective-permute-start.18
  41.9 2.1 %collective-permute-start.15 = (bf16[128,128]{1,0:T(8,128)(2,1)S(1)}, bf16[128,128]{1,0:T(8,128)(2,1)S(1)}, u32[]{:S(2)}, u32[]{:S(2)}) collective-permute-start(bf16[128,128]{1,0:T(8,128)(2,1)S(1)} %convert_element_type.151), channel_id=1, source_target_pairs={{0,1},{1,0},{2,3},{3,2},{4,5},{5,4},{6,7},{7,6},{8,9},{9,8},{10,11... | collective-permute-start | bytes 98312 | tf_op jit(solution)/shard_map/ppermute | solution.py:470
  44.1 2.7 %collective-permute-done.18.two = bf16[2,64,768]{2,1,0:T(8,128)(2,1)S(1)} collective-permute-done((bf16[2,64,768]{2,1,0:T(8,128)(2,1)S(1)}, bf16[2,64,768]{2,1,0:T(8,128)(2,1)S(1)}, u32[]{:S(2)}, u32[]{:S(2)}) %collective-permute-start.18) | collective-permute-done | bytes 196640 | tf_op jit(solution)/shard_map/ppermute | solution.py:470
  46.9 2.9 %collective-permute-start.19 = (bf16[64,768]{1,0:T(8,128)(2,1)S(1)}, bf16[64,768]{1,0:T(8,128)(2,1)S(1)}, u32[]{:S(2)}, u32[]{:S(2)}) collective-permute-start(bf16[64,768]{1,0:T(8,128)(2,1)S(1)} %fusion.4), channel_id=1, source_target_pairs={{0,2},{1,3},{2,0},{3,1},{4,6},{5,7},{6,4},{7,5},{8,10},{9,11},{10,... | collective-permute-start | bytes 294920 | tf_op jit(solution)/shard_map/ppermute | solution.py:470
  49.8 1.0 collective-permute-done.13.two
  50.8 1.7 %collective-permute-start.14 = (bf16[64,768]{1,0:T(8,128)(2,1)S(1)}, bf16[64,768]{1,0:T(8,128)(2,1)S(1)}, u32[]{:S(2)}, u32[]{:S(2)}) collective-permute-start(bf16[64,768]{1,0:T(8,128)(2,1)S(1)} %fusion.5), channel_id=1, source_target_pairs={{0,2},{1,3},{2,0},{3,1},{4,6},{5,7},{6,4},{7,5},{8,10},{9,11},{10,... | collective-permute-start | bytes 294920 | tf_op jit(solution)/shard_map/ppermute | solution.py:470
  52.5 1.6 %collective-permute-start.16 = (bf16[128,128]{1,0:T(8,128)(2,1)S(1)}, bf16[128,128]{1,0:T(8,128)(2,1)S(1)}, u32[]{:S(2)}, u32[]{:S(2)}) collective-permute-start(bf16[128,128]{1,0:T(8,128)(2,1)S(1)} %get-tuple-element.76), channel_id=1, source_target_pairs={{0,16},{8,24},{16,0},{24,8},{1,17},{9,25},{17,1},{25,9},{2,18},{10... | collective-permute-start | bytes 98312 | tf_op jit(solution)/shard_map/ppermute | solution.py:470
  54.1 2.4 %collective-permute-done.16.other_ref = bf16[128,128]{1,0:T(8,128)(2,1)S(1)} collective-permute-done((bf16[128,128]{1,0:T(8,128)(2,1)S(1)}, bf16[128,128]{1,0:T(8,128)(2,1)S(1)}, u32[]{:S(2)}, u32[]{:S(2)}) %collective-permute-start.16) | collective-permute-done | bytes 32800 | tf_op jit(solution)/shard_map/ppermute | solution.py:470
  57.1 1.2 %update.3 = (f32[1,64,768]{2,1,0:T(8,128)}, f32[1,64,768]{2,1,0:T(8,128)}, f32[1,64,768]{2,1,0:T(8,128)}, bf16[1,64,768]{2,1,0:T(8,128)(2,1)S(1)}) custom-call(bf16[2,4,64,768]{3,2,1,0:T(8,128)(2,1)S(1)} %gradient.4.kept, bf16[2,4,64,768]{3,2,1,0:T(8,128)(2,1)S(1)} %collective-permute-done.7.near, bf16[4,64,768]{2,1,0:T(8,128)(2,1)S(1)} %collective-permute-done.10.one, ...), custom_call_target="tpu_custom_call" | custom-call | tf_op jit(solution)/shard_map/update/pallas_call | solution.py:390
  58.3 0.8 collective-permute-start.20
  59.0 0.8 collective-permute-done.14.last
  59.9 1.2 %update.2 = (f32[1,64,768]{2,1,0:T(8,128)}, f32[1,64,768]{2,1,0:T(8,128)}, f32[1,64,768]{2,1,0:T(8,128)}, bf16[1,64,768]{2,1,0:T(8,128)(2,1)S(1)}) custom-call(bf16[2,4,64,768]{3,2,1,0:T(8,128)(2,1)S(1)} %gradient.4.kept, bf16[2,4,64,768]{3,2,1,0:T(8,128)(2,1)S(1)} %collective-permute-done.7.near, bf16[4,64,768]{2,1,0:T(8,128)(2,1)S(1)} %collective-permute-done.9.one, ...), custom_call_target="tpu_custom_call" | custom-call | tf_op jit(solution)/shard_map/update/pallas_call | solution.py:390
  61.1 1.3 %collective-permute-start.17 = (bf16[1,64,768]{2,1,0:T(8,128)(2,1)S(1)}, bf16[1,64,768]{2,1,0:T(8,128)(2,1)S(1)}, u32[]{:S(2)}, u32[]{:S(2)}) collective-permute-start(bf16[1,64,768]{2,1,0:T(8,128)(2,1)S(1)} %get-tuple-element.60), channel_id=1, source_target_pairs={{0,2},{1,3},{2,0},{3,1},{4,6},{5,7},{6,4},{7,5},{8,10},{9,11},{10,... | collective-permute-start | bytes 294920 | tf_op jit(solution)/shard_map/ppermute | solution.py:470
  62.5 1.3 %collective-permute-start.21 = (bf16[2,64,768]{2,1,0:T(8,128)(2,1)S(1)}, bf16[2,64,768]{2,1,0:T(8,128)(2,1)S(1)}, u32[]{:S(2)}, u32[]{:S(2)}) collective-permute-start(bf16[2,64,768]{2,1,0:T(8,128)(2,1)S(1)} %pad_maximum_fusion.6), channel_id=1, source_target_pairs={{4,0},{5,1},{6,2},{7,3},{12,8},{13,9},{14,10},{15,11},{20,16},{21,... | collective-permute-start | bytes 589832 | tf_op jit(solution)/shard_map/ppermute | solution.py:485
  63.8 2.2 %collective-permute-done.20 = bf16[1,64,768]{2,1,0:T(8,128)(2,1)S(1)} collective-permute-done((bf16[1,64,768]{2,1,0:T(8,128)(2,1)S(1)}, bf16[1,64,768]{2,1,0:T(8,128)(2,1)S(1)}, u32[]{:S(2)}, u32[]{:S(2)}) %collective-permute-start.20) | collective-permute-done | bytes 98336 | tf_op jit(solution)/shard_map/ppermute | solution.py:470
  66.1 0.9 collective-permute-done.17
  67.1 3.4 %collective-permute-start.23 = (bf16[2,64,768]{2,1,0:T(8,128)(2,1)S(1)}, bf16[2,64,768]{2,1,0:T(8,128)(2,1)S(1)}, u32[]{:S(2)}, u32[]{:S(2)}) collective-permute-start(bf16[2,64,768]{2,1,0:T(8,128)(2,1)S(1)} %pad_maximum_fusion.8), channel_id=1, source_target_pairs={{0,1},{1,0},{2,3},{3,2},{4,5},{5,4},{6,7},{7,6},{8,9},{9,8},{10,11... | collective-permute-start | bytes 589832 | tf_op jit(solution)/shard_map/ppermute | solution.py:470
  70.4 1.3 %collective-permute-start.22 = (bf16[2,64,768]{2,1,0:T(8,128)(2,1)S(1)}, bf16[2,64,768]{2,1,0:T(8,128)(2,1)S(1)}, u32[]{:S(2)}, u32[]{:S(2)}) collective-permute-start(bf16[2,64,768]{2,1,0:T(8,128)(2,1)S(1)} %pad_maximum_fusion.7), channel_id=1, source_target_pairs={{4,0},{5,1},{6,2},{7,3},{12,8},{13,9},{14,10},{15,11},{20,16},{21,... | collective-permute-start | bytes 589832 | tf_op jit(solution)/shard_map/ppermute | solution.py:485
  71.8 3.4 %collective-permute-done.23 = bf16[2,64,768]{2,1,0:T(8,128)(2,1)S(1)} collective-permute-done((bf16[2,64,768]{2,1,0:T(8,128)(2,1)S(1)}, bf16[2,64,768]{2,1,0:T(8,128)(2,1)S(1)}, u32[]{:S(2)}, u32[]{:S(2)}) %collective-permute-start.23) | collective-permute-done | bytes 196640 | tf_op jit(solution)/shard_map/ppermute | solution.py:470
  75.4 1.3 %collective-permute-start.27 = (bf16[4,64,768]{2,1,0:T(8,128)(2,1)S(1)}, bf16[4,64,768]{2,1,0:T(8,128)(2,1)S(1)}, u32[]{:S(2)}, u32[]{:S(2)}) collective-permute-start(bf16[4,64,768]{2,1,0:T(8,128)(2,1)S(1)} %get-tuple-element.88), channel_id=1, source_target_pairs={{4,0},{5,1},{6,2},{7,3},{12,8},{13,9},{14,10},{15,11},{20,16},{21,... | collective-permute-start | bytes 1179656 | tf_op jit(solution)/shard_map/ppermute | solution.py:485
  76.8 2.5 %collective-permute-start.26 = (bf16[4,64,768]{2,1,0:T(8,128)(2,1)S(1)}, bf16[4,64,768]{2,1,0:T(8,128)(2,1)S(1)}, u32[]{:S(2)}, u32[]{:S(2)}) collective-permute-start(bf16[4,64,768]{2,1,0:T(8,128)(2,1)S(1)} %get-tuple-element.90), channel_id=1, source_target_pairs={{0,1},{1,0},{2,3},{3,2},{4,5},{5,4},{6,7},{7,6},{8,9},{9,8},{10,11... | collective-permute-start | bytes 1179656 | tf_op jit(solution)/shard_map/ppermute | solution.py:470
  79.4 0.7 collective-permute-done.22
  80.2 5.0 %collective-permute-done.27 = bf16[4,64,768]{2,1,0:T(8,128)(2,1)S(1)} collective-permute-done((bf16[4,64,768]{2,1,0:T(8,128)(2,1)S(1)}, bf16[4,64,768]{2,1,0:T(8,128)(2,1)S(1)}, u32[]{:S(2)}, u32[]{:S(2)}) %collective-permute-start.27) | collective-permute-done | bytes 393248 | tf_op jit(solution)/shard_map/ppermute | solution.py:485
  85.6 1.3 %collective-permute-start.30 = (bf16[2,64,768]{2,1,0:T(8,128)(2,1)S(1)}, bf16[2,64,768]{2,1,0:T(8,128)(2,1)S(1)}, u32[]{:S(2)}, u32[]{:S(2)}) collective-permute-start(bf16[2,64,768]{2,1,0:T(8,128)(2,1)S(1)} %pad_maximum_fusion.10), channel_id=1, source_target_pairs={{4,0},{5,1},{6,2},{7,3},{12,8},{13,9},{14,10},{15,11},{20,16},{21,... | collective-permute-start | bytes 589832 | tf_op jit(solution)/shard_map/ppermute | solution.py:485
  86.9 2.4 %collective-permute-start.28 = (bf16[3,64,768]{2,1,0:T(8,128)(2,1)S(1)}, bf16[3,64,768]{2,1,0:T(8,128)(2,1)S(1)}, u32[]{:S(2)}, u32[]{:S(2)}) collective-permute-start(bf16[3,64,768]{2,1,0:T(8,128)(2,1)S(1)} %pad_maximum_fusion.3), channel_id=1, source_target_pairs={{0,16},{8,24},{16,0},{24,8},{1,17},{9,25},{17,1},{25,9},{2,18},{10... | collective-permute-start | bytes 884744 | tf_op jit(solution)/shard_map/ppermute | solution.py:470
  89.3 2.5 %collective-permute-start.29 = (bf16[3,64,768]{2,1,0:T(8,128)(2,1)S(1)}, bf16[3,64,768]{2,1,0:T(8,128)(2,1)S(1)}, u32[]{:S(2)}, u32[]{:S(2)}) collective-permute-start(bf16[3,64,768]{2,1,0:T(8,128)(2,1)S(1)} %pad_maximum_fusion.4), channel_id=1, source_target_pairs={{0,1},{1,0},{2,3},{3,2},{4,5},{5,4},{6,7},{7,6},{8,9},{9,8},{10,11... | collective-permute-start | bytes 884744 | tf_op jit(solution)/shard_map/ppermute | solution.py:470
  92.0 1.9 %collective-permute-done.28 = bf16[3,64,768]{2,1,0:T(8,128)(2,1)S(1)} collective-permute-done((bf16[3,64,768]{2,1,0:T(8,128)(2,1)S(1)}, bf16[3,64,768]{2,1,0:T(8,128)(2,1)S(1)}, u32[]{:S(2)}, u32[]{:S(2)}) %collective-permute-start.28) | collective-permute-done | bytes 294944 | tf_op jit(solution)/shard_map/ppermute | solution.py:470
  94.0 2.6 %collective-permute-done.29 = bf16[3,64,768]{2,1,0:T(8,128)(2,1)S(1)} collective-permute-done((bf16[3,64,768]{2,1,0:T(8,128)(2,1)S(1)}, bf16[3,64,768]{2,1,0:T(8,128)(2,1)S(1)}, u32[]{:S(2)}, u32[]{:S(2)}) %collective-permute-start.29) | collective-permute-done | bytes 294944 | tf_op jit(solution)/shard_map/ppermute | solution.py:470
  96.7 2.3 %place.2 = (bf16[2,64,12288]{2,1,0:T(8,128)(2,1)}, bf16[2,64,12288]{2,1,0:T(8,128)(2,1)}) custom-call(s32[4,3]{1,0:T(4,128)S(1)} %copy-done.8, bf16[8,64,768]{2,1,0:T(8,128)(2,1)S(1)} %constant_dynamic-update-slice_fusion.3.refs_0_, bf16[8,64,768]{2,1,0:T(8,128)(2,1)S(1)} %collective-permute-done.32.refs_1_, ...), custom_call_target="tpu_custom_call" | custom-call | bytes 9437184 | tf_op jit(solution)/shard_map/place/pallas_call | solution.py:451
  99.0 1.3 %place.3 = (bf16[2,64,12288]{2,1,0:T(8,128)(2,1)}, bf16[2,64,12288]{2,1,0:T(8,128)(2,1)}) custom-call(s32[4,3]{1,0:T(4,128)S(1)} %copy-done.8, bf16[8,64,768]{2,1,0:T(8,128)(2,1)S(1)} %constant_dynamic-update-slice_fusion.refs_0_, bf16[8,64,768]{2,1,0:T(8,128)(2,1)S(1)} %collective-permute-done.31.refs_1_, ...), custom_call_target="tpu_custom_call", output_to_operand_aliasing={{0}: (3, {}), {1}: (4, {})} | custom-call | bytes 3145728 | tf_op jit(solution)/shard_map/place/pallas_call | solution.py:451
  (95 shorter events, 7.1 us)
Async XLA Ops:
  1.6 8.0 %collective-permute-start = (bf16[64,768]{1,0:T(8,128)(2,1)S(1)}, bf16[64,768]{1,0:T(8,128)(2,1)S(1)}, u32[]{:S(2)}, u32[]{:S(2)}) collective-permute-start(bf16[64,768]{1,0:T(8,128)(2,1)S(1)} %fusion.6), channel_id=1, source_target_pairs={{4,0},{0,4},{5,1},{1,5},{6,2},{2,6},{7,3},{3,7},{12,8},{8,12},{13,... | collective-permute-start | bytes 294920 | tf_op jit(solution)/shard_map/ppermute | solution.py:480
  5.7 6.1 %copy-start = (bf16[1,4,32,12288]{3,2,1,0:T(8,128)(2,1)S(1)}, bf16[1,4,32,12288]{3,2,1,0:T(8,128)(2,1)}, u32[]{:S(2)}) copy-start(bf16[1,4,32,12288]{3,2,1,0:T(8,128)(2,1)} %param.13) | copy-start | bytes 9437188
  5.7 6.0 %copy-start.1 = (bf16[1,1,2,64,12288]{4,3,2,1,0:T(8,128)(2,1)S(1)}, bf16[1,1,2,64,12288]{4,3,2,1,0:T(8,128)(2,1)}, u32[]{:S(2)}) copy-start(bf16[1,1,2,64,12288]{4,3,2,1,0:T(8,128)(2,1)} %param.17) | copy-start | bytes 9437188
  5.7 6.0 %copy-start.9 = (s32[4]{0:T(128)S(1)}, s32[4]{0:T(128)}, u32[]{:S(2)}) copy-start(s32[4]{0:T(128)} %param.14) | copy-start | bytes 52
  9.8 4.1 %collective-permute-start.4 = (f32[64,128]{1,0:T(8,128)S(1)}, f32[64,128]{1,0:T(8,128)S(1)}, u32[]{:S(2)}, u32[]{:S(2)}) collective-permute-start(f32[64,128]{1,0:T(8,128)S(1)} %get-tuple-element.48), channel_id=1, source_target_pairs={{0,24},{8,16},{16,8},{24,0},{1,25},{9,17},{17,9},{25,1},{2,26},{10... | collective-permute-start | bytes 98312 | tf_op jit(solution)/shard_map/ppermute | solution.py:470
  10.5 4.3 %collective-permute-start.3 = (f32[64,128]{1,0:T(8,128)S(1)}, f32[64,128]{1,0:T(8,128)S(1)}, u32[]{:S(2)}, u32[]{:S(2)}) collective-permute-start(f32[64,128]{1,0:T(8,128)S(1)} %get-tuple-element.48), channel_id=1, source_target_pairs={{0,16},{8,24},{16,0},{24,8},{1,17},{9,25},{17,1},{25,9},{2,18},{10... | collective-permute-start | bytes 98312 | tf_op jit(solution)/shard_map/ppermute | solution.py:470
  11.4 3.3 %collective-permute-start.2 = (f32[64,128]{1,0:T(8,128)S(1)}, f32[64,128]{1,0:T(8,128)S(1)}, u32[]{:S(2)}, u32[]{:S(2)}) collective-permute-start(f32[64,128]{1,0:T(8,128)S(1)} %get-tuple-element.48), channel_id=1, source_target_pairs={{0,8},{8,0},{16,24},{24,16},{1,9},{9,1},{17,25},{25,17},{2,10},{10... | collective-permute-start | bytes 98312 | tf_op jit(solution)/shard_map/ppermute | solution.py:470
  11.7 11.9 %copy-start.8 = (s32[4,3]{1,0:T(4,128)S(1)}, s32[4,3]{1,0:T(4,128)}, u32[]{:S(2)}) copy-start(s32[4,3]{1,0:T(4,128)} %bounds.5) | copy-start | bytes 148
  13.5 10.1 %collective-permute-start.1 = (f32[128,384]{1,0:T(8,128)S(1)}, f32[128,384]{1,0:T(8,128)S(1)}, u32[]{:S(2)}, u32[]{:S(2)}) collective-permute-start(f32[128,384]{1,0:T(8,128)S(1)} %project_up.1.refs_0_), channel_id=1, source_target_pairs={{4,0},{0,4},{5,1},{1,5},{6,2},{2,6},{7,3},{3,7},{12,8},{8,12},{13,... | collective-permute-start | bytes 589832 | tf_op jit(solution)/shard_map/ppermute | solution.py:480
  14.8 4.0 %collective-permute-start.5 = (f32[64,128]{1,0:T(8,128)S(1)}, f32[64,128]{1,0:T(8,128)S(1)}, u32[]{:S(2)}, u32[]{:S(2)}) collective-permute-start(f32[64,128]{1,0:T(8,128)S(1)} %add_add_fusion), channel_id=1, source_target_pairs={{0,1},{1,0},{2,3},{3,2},{4,5},{5,4},{6,7},{7,6},{8,9},{9,8},{10,11... | collective-permute-start | bytes 98312 | tf_op jit(solution)/shard_map/ppermute | solution.py:470
  18.8 4.8 %collective-permute-start.6 = (f32[64,128]{1,0:T(8,128)S(1)}, f32[64,128]{1,0:T(8,128)S(1)}, u32[]{:S(2)}, u32[]{:S(2)}) collective-permute-start(f32[64,128]{1,0:T(8,128)S(1)} %add.74.refs_2_), channel_id=1, source_target_pairs={{0,2},{1,3},{2,0},{3,1},{4,6},{5,7},{6,4},{7,5},{8,10},{9,11},{10,... | collective-permute-start | bytes 98312 | tf_op jit(solution)/shard_map/ppermute | solution.py:470
  25.7 2.4 %collective-permute-start.8 = (bf16[2,4,64,768]{3,2,1,0:T(8,128)(2,1)S(1)}, bf16[2,4,64,768]{3,2,1,0:T(8,128)(2,1)S(1)}, u32[]{:S(2)}, u32[]{:S(2)}) collective-permute-start(bf16[2,4,64,768]{3,2,1,0:T(8,128)(2,1)S(1)} %gradient.7), channel_id=1, source_target_pairs={{0,8},{8,0},{16,24},{24,16},{1,9},{9,1},{17,25},{25,17},{2,10},{10... | collective-permute-start | bytes 2359304 | tf_op jit(solution)/shard_map/ppermute | solution.py:470
  26.3 14.5 %collective-permute-start.7 = (bf16[2,4,64,768]{3,2,1,0:T(8,128)(2,1)S(1)}, bf16[2,4,64,768]{3,2,1,0:T(8,128)(2,1)S(1)}, u32[]{:S(2)}, u32[]{:S(2)}) collective-permute-start(bf16[2,4,64,768]{3,2,1,0:T(8,128)(2,1)S(1)} %gradient.5), channel_id=1, source_target_pairs={{0,8},{8,0},{16,24},{24,16},{1,9},{9,1},{17,25},{25,17},{2,10},{10... | collective-permute-start | bytes 2359304 | tf_op jit(solution)/shard_map/ppermute | solution.py:470
  26.9 3.9 %collective-permute-start.11 = (bf16[128,128]{1,0:T(8,128)(2,1)S(1)}, bf16[128,128]{1,0:T(8,128)(2,1)S(1)}, u32[]{:S(2)}, u32[]{:S(2)}) collective-permute-start(bf16[128,128]{1,0:T(8,128)(2,1)S(1)} %convert_element_type.136), channel_id=1, source_target_pairs={{0,8},{8,0},{16,24},{24,16},{1,9},{9,1},{17,25},{25,17},{2,10},{10... | collective-permute-start | bytes 98312 | tf_op jit(solution)/shard_map/ppermute | solution.py:470
  28.3 11.9 %collective-permute-start.10 = (bf16[4,64,768]{2,1,0:T(8,128)(2,1)S(1)}, bf16[4,64,768]{2,1,0:T(8,128)(2,1)S(1)}, u32[]{:S(2)}, u32[]{:S(2)}) collective-permute-start(bf16[4,64,768]{2,1,0:T(8,128)(2,1)S(1)} %get-tuple-element.80), channel_id=1, source_target_pairs={{0,1},{1,0},{2,3},{3,2},{4,5},{5,4},{6,7},{7,6},{8,9},{9,8},{10,11... | collective-permute-start | bytes 1179656 | tf_op jit(solution)/shard_map/ppermute | solution.py:470
  29.9 10.9 %collective-permute-start.9 = (bf16[4,64,768]{2,1,0:T(8,128)(2,1)S(1)}, bf16[4,64,768]{2,1,0:T(8,128)(2,1)S(1)}, u32[]{:S(2)}, u32[]{:S(2)}) collective-permute-start(bf16[4,64,768]{2,1,0:T(8,128)(2,1)S(1)} %get-tuple-element.81), channel_id=1, source_target_pairs={{0,16},{8,24},{16,0},{24,8},{1,17},{9,25},{17,1},{25,9},{2,18},{10... | collective-permute-start | bytes 1179656 | tf_op jit(solution)/shard_map/ppermute | solution.py:470
  30.8 8.5 %collective-permute-start.12 = (bf16[128,128]{1,0:T(8,128)(2,1)S(1)}, bf16[128,128]{1,0:T(8,128)(2,1)S(1)}, u32[]{:S(2)}, u32[]{:S(2)}) collective-permute-start(bf16[128,128]{1,0:T(8,128)(2,1)S(1)} %fusion.7), channel_id=1, source_target_pairs={{0,2},{1,3},{2,0},{3,1},{4,6},{5,7},{6,4},{7,5},{8,10},{9,11},{10,... | collective-permute-start | bytes 98312 | tf_op jit(solution)/shard_map/ppermute | solution.py:470
  34.2 22.8 %copy-start.2 = (f32[1,64,768]{2,1,0:T(8,128)S(1)}, f32[1,64,768]{2,1,0:T(8,128)}, u32[]{:S(2)}) copy-start(f32[1,64,768]{2,1,0:T(8,128)} %refs_0_.3) | copy-start | bytes 589828
  34.2 22.8 %copy-start.4 = (f32[1,64,768]{2,1,0:T(8,128)S(1)}, f32[1,64,768]{2,1,0:T(8,128)}, u32[]{:S(2)}) copy-start(f32[1,64,768]{2,1,0:T(8,128)} %refs_1_.3) | copy-start | bytes 589828
  34.2 22.8 %copy-start.5 = (f32[1,64,768]{2,1,0:T(8,128)S(1)}, f32[1,64,768]{2,1,0:T(8,128)}, u32[]{:S(2)}) copy-start(f32[1,64,768]{2,1,0:T(8,128)} %refs_2_.3) | copy-start | bytes 589828
  34.2 25.6 %copy-start.3 = (f32[1,64,768]{2,1,0:T(8,128)S(1)}, f32[1,64,768]{2,1,0:T(8,128)}, u32[]{:S(2)}) copy-start(f32[1,64,768]{2,1,0:T(8,128)} %refs_0_.2) | copy-start | bytes 589828
  34.3 25.6 %copy-start.6 = (f32[1,64,768]{2,1,0:T(8,128)S(1)}, f32[1,64,768]{2,1,0:T(8,128)}, u32[]{:S(2)}) copy-start(f32[1,64,768]{2,1,0:T(8,128)} %refs_1_.2) | copy-start | bytes 589828
  34.3 25.6 %copy-start.7 = (f32[1,64,768]{2,1,0:T(8,128)S(1)}, f32[1,64,768]{2,1,0:T(8,128)}, u32[]{:S(2)}) copy-start(f32[1,64,768]{2,1,0:T(8,128)} %refs_2_.2) | copy-start | bytes 589828
  41.0 5.9 %collective-permute-start.18 = (bf16[2,64,768]{2,1,0:T(8,128)(2,1)S(1)}, bf16[2,64,768]{2,1,0:T(8,128)(2,1)S(1)}, u32[]{:S(2)}, u32[]{:S(2)}) collective-permute-start(bf16[2,64,768]{2,1,0:T(8,128)(2,1)S(1)} %get-tuple-element.78), channel_id=1, source_target_pairs={{0,16},{8,24},{16,0},{24,8},{1,17},{9,25},{17,1},{25,9},{2,18},{10... | collective-permute-start | bytes 589832 | tf_op jit(solution)/shard_map/ppermute | solution.py:470
  41.9 10.6 %collective-permute-start.15 = (bf16[128,128]{1,0:T(8,128)(2,1)S(1)}, bf16[128,128]{1,0:T(8,128)(2,1)S(1)}, u32[]{:S(2)}, u32[]{:S(2)}) collective-permute-start(bf16[128,128]{1,0:T(8,128)(2,1)S(1)} %convert_element_type.151), channel_id=1, source_target_pairs={{0,1},{1,0},{2,3},{3,2},{4,5},{5,4},{6,7},{7,6},{8,9},{9,8},{10,11... | collective-permute-start | bytes 98312 | tf_op jit(solution)/shard_map/ppermute | solution.py:470
  44.0 6.7 %collective-permute-start.13 = (bf16[2,64,768]{2,1,0:T(8,128)(2,1)S(1)}, bf16[2,64,768]{2,1,0:T(8,128)(2,1)S(1)}, u32[]{:S(2)}, u32[]{:S(2)}) collective-permute-start(bf16[2,64,768]{2,1,0:T(8,128)(2,1)S(1)} %get-tuple-element.79), channel_id=1, source_target_pairs={{0,1},{1,0},{2,3},{3,2},{4,5},{5,4},{6,7},{7,6},{8,9},{9,8},{10,11... | collective-permute-start | bytes 589832 | tf_op jit(solution)/shard_map/ppermute | solution.py:470
  46.9 10.2 %collective-permute-start.19 = (bf16[64,768]{1,0:T(8,128)(2,1)S(1)}, bf16[64,768]{1,0:T(8,128)(2,1)S(1)}, u32[]{:S(2)}, u32[]{:S(2)}) collective-permute-start(bf16[64,768]{1,0:T(8,128)(2,1)S(1)} %fusion.4), channel_id=1, source_target_pairs={{0,2},{1,3},{2,0},{3,1},{4,6},{5,7},{6,4},{7,5},{8,10},{9,11},{10,... | collective-permute-start | bytes 294920 | tf_op jit(solution)/shard_map/ppermute | solution.py:470
  50.8 9.1 %collective-permute-start.14 = (bf16[64,768]{1,0:T(8,128)(2,1)S(1)}, bf16[64,768]{1,0:T(8,128)(2,1)S(1)}, u32[]{:S(2)}, u32[]{:S(2)}) collective-permute-start(bf16[64,768]{1,0:T(8,128)(2,1)S(1)} %fusion.5), channel_id=1, source_target_pairs={{0,2},{1,3},{2,0},{3,1},{4,6},{5,7},{6,4},{7,5},{8,10},{9,11},{10,... | collective-permute-start | bytes 294920 | tf_op jit(solution)/shard_map/ppermute | solution.py:470
  52.5 4.0 %collective-permute-start.16 = (bf16[128,128]{1,0:T(8,128)(2,1)S(1)}, bf16[128,128]{1,0:T(8,128)(2,1)S(1)}, u32[]{:S(2)}, u32[]{:S(2)}) collective-permute-start(bf16[128,128]{1,0:T(8,128)(2,1)S(1)} %get-tuple-element.76), channel_id=1, source_target_pairs={{0,16},{8,24},{16,0},{24,8},{1,17},{9,25},{17,1},{25,9},{2,18},{10... | collective-permute-start | bytes 98312 | tf_op jit(solution)/shard_map/ppermute | solution.py:470
  58.3 7.7 %collective-permute-start.20 = (bf16[1,64,768]{2,1,0:T(8,128)(2,1)S(1)}, bf16[1,64,768]{2,1,0:T(8,128)(2,1)S(1)}, u32[]{:S(2)}, u32[]{:S(2)}) collective-permute-start(bf16[1,64,768]{2,1,0:T(8,128)(2,1)S(1)} %get-tuple-element.61), channel_id=1, source_target_pairs={{0,2},{1,3},{2,0},{3,1},{4,6},{5,7},{6,4},{7,5},{8,10},{9,11},{10,... | collective-permute-start | bytes 294920 | tf_op jit(solution)/shard_map/ppermute | solution.py:470
  61.1 5.9 %collective-permute-start.17 = (bf16[1,64,768]{2,1,0:T(8,128)(2,1)S(1)}, bf16[1,64,768]{2,1,0:T(8,128)(2,1)S(1)}, u32[]{:S(2)}, u32[]{:S(2)}) collective-permute-start(bf16[1,64,768]{2,1,0:T(8,128)(2,1)S(1)} %get-tuple-element.60), channel_id=1, source_target_pairs={{0,2},{1,3},{2,0},{3,1},{4,6},{5,7},{6,4},{7,5},{8,10},{9,11},{10,... | collective-permute-start | bytes 294920 | tf_op jit(solution)/shard_map/ppermute | solution.py:470
  62.5 7.9 %collective-permute-start.21 = (bf16[2,64,768]{2,1,0:T(8,128)(2,1)S(1)}, bf16[2,64,768]{2,1,0:T(8,128)(2,1)S(1)}, u32[]{:S(2)}, u32[]{:S(2)}) collective-permute-start(bf16[2,64,768]{2,1,0:T(8,128)(2,1)S(1)} %pad_maximum_fusion.6), channel_id=1, source_target_pairs={{4,0},{5,1},{6,2},{7,3},{12,8},{13,9},{14,10},{15,11},{20,16},{21,... | collective-permute-start | bytes 589832 | tf_op jit(solution)/shard_map/ppermute | solution.py:485
  66.0 5.8 %collective-permute-start.25 = (bf16[2,64,768]{2,1,0:T(8,128)(2,1)S(1)}, bf16[2,64,768]{2,1,0:T(8,128)(2,1)S(1)}, u32[]{:S(2)}, u32[]{:S(2)}) collective-permute-start(bf16[2,64,768]{2,1,0:T(8,128)(2,1)S(1)} %pad_maximum_fusion.9), channel_id=1, source_target_pairs={{0,16},{8,24},{16,0},{24,8},{1,17},{9,25},{17,1},{25,9},{2,18},{10... | collective-permute-start | bytes 589832 | tf_op jit(solution)/shard_map/ppermute | solution.py:470
  67.1 8.2 %collective-permute-start.23 = (bf16[2,64,768]{2,1,0:T(8,128)(2,1)S(1)}, bf16[2,64,768]{2,1,0:T(8,128)(2,1)S(1)}, u32[]{:S(2)}, u32[]{:S(2)}) collective-permute-start(bf16[2,64,768]{2,1,0:T(8,128)(2,1)S(1)} %pad_maximum_fusion.8), channel_id=1, source_target_pairs={{0,1},{1,0},{2,3},{3,2},{4,5},{5,4},{6,7},{7,6},{8,9},{9,8},{10,11... | collective-permute-start | bytes 589832 | tf_op jit(solution)/shard_map/ppermute | solution.py:470
  70.4 9.7 %collective-permute-start.22 = (bf16[2,64,768]{2,1,0:T(8,128)(2,1)S(1)}, bf16[2,64,768]{2,1,0:T(8,128)(2,1)S(1)}, u32[]{:S(2)}, u32[]{:S(2)}) collective-permute-start(bf16[2,64,768]{2,1,0:T(8,128)(2,1)S(1)} %pad_maximum_fusion.7), channel_id=1, source_target_pairs={{4,0},{5,1},{6,2},{7,3},{12,8},{13,9},{14,10},{15,11},{20,16},{21,... | collective-permute-start | bytes 589832 | tf_op jit(solution)/shard_map/ppermute | solution.py:485
  75.4 9.8 %collective-permute-start.27 = (bf16[4,64,768]{2,1,0:T(8,128)(2,1)S(1)}, bf16[4,64,768]{2,1,0:T(8,128)(2,1)S(1)}, u32[]{:S(2)}, u32[]{:S(2)}) collective-permute-start(bf16[4,64,768]{2,1,0:T(8,128)(2,1)S(1)} %get-tuple-element.88), channel_id=1, source_target_pairs={{4,0},{5,1},{6,2},{7,3},{12,8},{13,9},{14,10},{15,11},{20,16},{21,... | collective-permute-start | bytes 1179656 | tf_op jit(solution)/shard_map/ppermute | solution.py:485
  76.7 8.5 %collective-permute-start.24 = (bf16[4,64,768]{2,1,0:T(8,128)(2,1)S(1)}, bf16[4,64,768]{2,1,0:T(8,128)(2,1)S(1)}, u32[]{:S(2)}, u32[]{:S(2)}) collective-permute-start(bf16[4,64,768]{2,1,0:T(8,128)(2,1)S(1)} %get-tuple-element.89), channel_id=1, source_target_pairs={{0,16},{8,24},{16,0},{24,8},{1,17},{9,25},{17,1},{25,9},{2,18},{10... | collective-permute-start | bytes 1179656 | tf_op jit(solution)/shard_map/ppermute | solution.py:470
  76.8 8.7 %collective-permute-start.26 = (bf16[4,64,768]{2,1,0:T(8,128)(2,1)S(1)}, bf16[4,64,768]{2,1,0:T(8,128)(2,1)S(1)}, u32[]{:S(2)}, u32[]{:S(2)}) collective-permute-start(bf16[4,64,768]{2,1,0:T(8,128)(2,1)S(1)} %get-tuple-element.90), channel_id=1, source_target_pairs={{0,1},{1,0},{2,3},{3,2},{4,5},{5,4},{6,7},{7,6},{8,9},{9,8},{10,11... | collective-permute-start | bytes 1179656 | tf_op jit(solution)/shard_map/ppermute | solution.py:470
  79.4 17.3 %collective-permute-start.32 = (bf16[8,64,768]{2,1,0:T(8,128)(2,1)S(1)}, bf16[8,64,768]{2,1,0:T(8,128)(2,1)S(1)}, u32[]{:S(2)}, u32[]{:S(2)}) collective-permute-start(bf16[8,64,768]{2,1,0:T(8,128)(2,1)S(1)} %constant_dynamic-update-slice_fusion.3.refs_0_), channel_id=1, source_target_pairs={{0,8},{8,0},{16,24},{24,16},{1,9},{9,1},{17,25},{25,17},{2,10},{10... | collective-permute-start | bytes 2359304 | tf_op jit(solution)/shard_map/ppermute | solution.py:470
  85.6 11.0 %collective-permute-start.30 = (bf16[2,64,768]{2,1,0:T(8,128)(2,1)S(1)}, bf16[2,64,768]{2,1,0:T(8,128)(2,1)S(1)}, u32[]{:S(2)}, u32[]{:S(2)}) collective-permute-start(bf16[2,64,768]{2,1,0:T(8,128)(2,1)S(1)} %pad_maximum_fusion.10), channel_id=1, source_target_pairs={{4,0},{5,1},{6,2},{7,3},{12,8},{13,9},{14,10},{15,11},{20,16},{21,... | collective-permute-start | bytes 589832 | tf_op jit(solution)/shard_map/ppermute | solution.py:485
  86.9 7.1 %collective-permute-start.28 = (bf16[3,64,768]{2,1,0:T(8,128)(2,1)S(1)}, bf16[3,64,768]{2,1,0:T(8,128)(2,1)S(1)}, u32[]{:S(2)}, u32[]{:S(2)}) collective-permute-start(bf16[3,64,768]{2,1,0:T(8,128)(2,1)S(1)} %pad_maximum_fusion.3), channel_id=1, source_target_pairs={{0,16},{8,24},{16,0},{24,8},{1,17},{9,25},{17,1},{25,9},{2,18},{10... | collective-permute-start | bytes 884744 | tf_op jit(solution)/shard_map/ppermute | solution.py:470
  89.3 7.2 %collective-permute-start.29 = (bf16[3,64,768]{2,1,0:T(8,128)(2,1)S(1)}, bf16[3,64,768]{2,1,0:T(8,128)(2,1)S(1)}, u32[]{:S(2)}, u32[]{:S(2)}) collective-permute-start(bf16[3,64,768]{2,1,0:T(8,128)(2,1)S(1)} %pad_maximum_fusion.4), channel_id=1, source_target_pairs={{0,1},{1,0},{2,3},{3,2},{4,5},{5,4},{6,7},{7,6},{8,9},{9,8},{10,11... | collective-permute-start | bytes 884744 | tf_op jit(solution)/shard_map/ppermute | solution.py:470
  91.9 4.8 %collective-permute-start.33 = (bf16[8,64,768]{2,1,0:T(8,128)(2,1)S(1)}, bf16[8,64,768]{2,1,0:T(8,128)(2,1)S(1)}, u32[]{:S(2)}, u32[]{:S(2)}) collective-permute-start(bf16[8,64,768]{2,1,0:T(8,128)(2,1)S(1)} %constant_dynamic-update-slice_fusion.9.refs_2_), channel_id=1, source_target_pairs={{0,8},{8,0},{16,24},{24,16},{1,9},{9,1},{17,25},{25,17},{2,10},{10... | collective-permute-start | bytes 2359304 | tf_op jit(solution)/shard_map/ppermute | solution.py:470
  94.0 2.7 %collective-permute-start.34 = (bf16[8,64,768]{2,1,0:T(8,128)(2,1)S(1)}, bf16[8,64,768]{2,1,0:T(8,128)(2,1)S(1)}, u32[]{:S(2)}, u32[]{:S(2)}) collective-permute-start(bf16[8,64,768]{2,1,0:T(8,128)(2,1)S(1)} %constant_dynamic-update-slice_fusion.11.refs_4_), channel_id=1, source_target_pairs={{0,8},{8,0},{16,24},{24,16},{1,9},{9,1},{17,25},{25,17},{2,10},{10... | collective-permute-start | bytes 2359304 | tf_op jit(solution)/shard_map/ppermute | solution.py:470
  96.6 2.4 %collective-permute-start.31 = (bf16[8,64,768]{2,1,0:T(8,128)(2,1)S(1)}, bf16[8,64,768]{2,1,0:T(8,128)(2,1)S(1)}, u32[]{:S(2)}, u32[]{:S(2)}) collective-permute-start(bf16[8,64,768]{2,1,0:T(8,128)(2,1)S(1)} %constant_dynamic-update-slice_fusion.refs_0_), channel_id=1, source_target_pairs={{0,8},{8,0},{16,24},{24,16},{1,9},{9,1},{17,25},{25,17},{2,10},{10... | collective-permute-start | bytes 2359304 | tf_op jit(solution)/shard_map/ppermute | solution.py:470

commit v12 on v11

--- a/solution.py
+++ b/solution.py
@@ -480,11 +480,6 @@
     return lax.ppermute(block, "section", route)
 
 
-def following_layer(block):
-    size = lax.axis_size("section")
-    return lax.ppermute(block, "section", [(i + 1, i) for i in range(size - 1)])
-
-
 def summed(*blocks):
     total = blocks[0].astype(f32)
     for block in blocks[1:]:
@@ -535,7 +530,7 @@
 
 def fetched(piece):
     blocks, array = piece
-    return [(1, *block[1:]) for block in blocks], following_layer(array)
+    return [(1, *block[1:]) for block in blocks], from_next(array)
 
 
 def picked(piece, at):

time: 101 us -> 102 us (level)
  waiting for transfers between devices: 37.2 us -> 38.5 us
    ppermute x2 -> x6, starting transfers between devices: 3.36 us -> 9.55 us  [from_next(): return lax.ppermute(block, 'section', route)]
    ppermute x4 -> x0, waiting for transfers between devices: 5.72 us -> none  [following_layer(): return lax.ppermute(block, 'section', [(i + 1, i) for i in range(size - 1)])]
    ppermute x4 -> x0, starting transfers between devices: 5.17 us -> none  [following_layer(): return lax.ppermute(block, 'section', [(i + 1, i) for i in range(size - 1)])]
    ppermute x2 -> x6, waiting for transfers between devices: 0.01 us -> 4.98 us  [from_next(): return lax.ppermute(block, 'section', route)]
    ppermute x29, waiting for transfers between devices: 31.5 us -> 33.5 us  [swapped(): return lax.ppermute(block, axis, route)]
where the time goes in v12:
time: 102 us
  starting transfers between devices  43.5 us (43%)
  waiting for transfers between devices  38.5 us (38%)
  Pallas kernels  15.5 us (15%)
  other arithmetic  2.8 us (3%)
  between operations  1.11 us (1%)
    ppermute x29, starting transfers between devices, swapped(): return lax.ppermute(block, axis, route)  33.9 us
    ppermute x29, waiting for transfers between devices, swapped(): return lax.ppermute(block, axis, route)  33.5 us
    ppermute x6, starting transfers between devices, from_next(): return lax.ppermute(block, 'section', route)  9.55 us
    ppermute x6, waiting for transfers between devices, from_next(): return lax.ppermute(block, 'section', route)  4.98 us
    pallas_call x1, Pallas kernels, project_down(): pl.pallas_call(functools.partial(project_down_kernel, steps), in_specs=[i...  3.87 us
    pallas_call x2, Pallas kernels, place(): pl.pallas_call(functools.partial(place_kernel, layout, not before), in_sp...  3.56 us
    pallas_call x2, Pallas kernels, update(): pl.pallas_call(functools.partial(update_kernel, which), in_specs=[in_vmem...  2.45 us
  transfers between devices with their start and end apart: 35, of which 20 were waited for; matrix products, arithmetic and copies ran while one was open for 2% of the time, Pallas kernels for 12%

profile of v12, /device:TPU:0, one launch (start us, length us, event | category | flops | bytes accessed | tf_op | source)
XLA Modules:
  0.0 101.7 jit_solution(7560228567860002877)
XLA Ops:
  0.6 1.0 fusion.6
  1.6 3.0 %collective-permute-start = (bf16[64,768]{1,0:T(8,128)(2,1)S(1)}, bf16[64,768]{1,0:T(8,128)(2,1)S(1)}, u32[]{:S(2)}, u32[]{:S(2)}) collective-permute-start(bf16[64,768]{1,0:T(8,128)(2,1)S(1)} %fusion.6), channel_id=1, source_target_pairs={{4,0},{0,4},{5,1},{1,5},{6,2},{2,6},{7,3},{3,7},{12,8},{8,12},{13,... | collective-permute-start | bytes 294920 | tf_op jit(solution)/shard_map/ppermute | solution.py:480
  4.6 1.0 %convert_bitcast_fusion = (bf16[64,768]{1,0:T(8,128)(2,1)S(1)}, bf16[64,768]{1,0:T(8,128)(2,1)S(1)}) fusion(f32[1,64,768]{2,1,0:T(8,128)} %refs_0_.3, f32[1,64,768]{2,1,0:T(8,128)} %refs_0_.2), kind=kLoop, calls=%fused_computation.29 | loop fusion | flops 98304 | bytes 589824 | tf_op jit(solution)/shard_map/convert.5
  5.7 3.9 %project_down.1 = (f32[128,128]{1,0:T(8,128)S(1)}, f32[128,128]{1,0:T(8,128)S(1)}, bf16[128,12288]{1,0:T(8,128)(2,1)S(1)}) custom-call(bf16[128,12288]{1,0:T(8,128)(2,1)} %bitcast.53, bf16[2,64,12288]{2,1,0:T(8,128)(2,1)} %bitcast.54), custom_call_target="tpu_custom_call" | custom-call | flops 402653184 | bytes 6291456 | tf_op jit(solution)/shard_map/project_down/pallas_call | solution.py:106
  9.8 0.7 collective-permute-start.4
  10.5 0.9 collective-permute-start.3
  11.7 1.8 %project_up.1.refs_0_ = f32[128,384]{1,0:T(8,128)S(1)} custom-call(s32[1,4]{1,0:T(1,128)S(1)} %bitcast.51, f32[128,128]{1,0:T(8,128)S(1)} %get-tuple-element.43.by_down, bf16[128,12288]{1,0:T(8,128)(2,1)S(1)} %get-tuple-element.47.h_ref, bf16[128,12288]{1,0:T(8,128)(2,1)S(1)} %bitcast.45, bf16[2,64,12288]{2,1,0:T(8,128)(2,1)S(1)} %bitcast.50), custom_call_target="tpu_custom_call" | custom-call | flops 805306368 | bytes 9437184 | tf_op jit(solution)/shard_map/project_up/pallas_call | solution.py:141
  13.9 0.9 collective-permute-done.3
  14.8 1.6 %collective-permute-start.5 = (f32[64,128]{1,0:T(8,128)S(1)}, f32[64,128]{1,0:T(8,128)S(1)}, u32[]{:S(2)}, u32[]{:S(2)}) collective-permute-start(f32[64,128]{1,0:T(8,128)S(1)} %add_add_fusion), channel_id=1, source_target_pairs={{0,1},{1,0},{2,3},{3,2},{4,5},{5,4},{6,7},{7,6},{8,9},{9,8},{10,11... | collective-permute-start | bytes 98312 | tf_op jit(solution)/shard_map/ppermute | solution.py:470
  16.4 2.3 %collective-permute-done.5 = f32[64,128]{1,0:T(8,128)S(1)} collective-permute-done((f32[64,128]{1,0:T(8,128)S(1)}, f32[64,128]{1,0:T(8,128)S(1)}, u32[]{:S(2)}, u32[]{:S(2)}) %collective-permute-start.5) | collective-permute-done | bytes 32800 | tf_op jit(solution)/shard_map/ppermute | solution.py:470
  18.8 2.6 %collective-permute-start.6 = (f32[64,128]{1,0:T(8,128)S(1)}, f32[64,128]{1,0:T(8,128)S(1)}, u32[]{:S(2)}, u32[]{:S(2)}) collective-permute-start(f32[64,128]{1,0:T(8,128)S(1)} %add.74.refs_2_), channel_id=1, source_target_pairs={{0,2},{1,3},{2,0},{3,1},{4,6},{5,7},{6,4},{7,5},{8,10},{9,11},{10,... | collective-permute-start | bytes 98312 | tf_op jit(solution)/shard_map/ppermute | solution.py:470
  21.4 2.2 %collective-permute-done.6.refs_3_ = f32[64,128]{1,0:T(8,128)S(1)} collective-permute-done((f32[64,128]{1,0:T(8,128)S(1)}, f32[64,128]{1,0:T(8,128)S(1)}, u32[]{:S(2)}, u32[]{:S(2)}) %collective-permute-start.6) | collective-permute-done | bytes 32800 | tf_op jit(solution)/shard_map/ppermute | solution.py:470
  23.6 1.6 %chain.1 = (bf16[128,256]{1,0:T(8,128)(2,1)S(1)}, f32[128,128]{1,0:T(8,128)S(1)}) custom-call(s32[4,3]{1,0:T(4,128)S(1)} %copy-done.8, s32[1,4]{1,0:T(1,128)S(1)} %bitcast.52, f32[128,384]{1,0:T(8,128)S(1)} %project_up.1.refs_0_, f32[128,384]{1,0:T(8,128)S(1)} %collective-permute-done.1.refs_1_, f32[64,128]{1,0:T(8,128)S(1)} %add.74.refs_2_, ...), custom_call_target="tpu_custom_call" | custom-call | tf_op jit(solution)/shard_map/chain/pallas_call | solution.py:314
  27.4 0.6 collective-permute-done.8
  28.3 1.6 %collective-permute-start.10 = (bf16[4,64,768]{2,1,0:T(8,128)(2,1)S(1)}, bf16[4,64,768]{2,1,0:T(8,128)(2,1)S(1)}, u32[]{:S(2)}, u32[]{:S(2)}) collective-permute-start(bf16[4,64,768]{2,1,0:T(8,128)(2,1)S(1)} %get-tuple-element.80), channel_id=1, source_target_pairs={{0,1},{1,0},{2,3},{3,2},{4,5},{5,4},{6,7},{7,6},{8,9},{9,8},{10,11... | collective-permute-start | bytes 1179656 | tf_op jit(solution)/shard_map/ppermute | solution.py:470
  29.9 0.9 collective-permute-start.9
  30.8 2.9 %collective-permute-start.12 = (bf16[128,128]{1,0:T(8,128)(2,1)S(1)}, bf16[128,128]{1,0:T(8,128)(2,1)S(1)}, u32[]{:S(2)}, u32[]{:S(2)}) collective-permute-start(bf16[128,128]{1,0:T(8,128)(2,1)S(1)} %fusion.7), channel_id=1, source_target_pairs={{0,2},{1,3},{2,0},{3,1},{4,6},{5,7},{6,4},{7,5},{8,10},{9,11},{10,... | collective-permute-start | bytes 98312 | tf_op jit(solution)/shard_map/ppermute | solution.py:470
  34.3 5.0 %collective-permute-done.12 = bf16[128,128]{1,0:T(8,128)(2,1)S(1)} collective-permute-done((bf16[128,128]{1,0:T(8,128)(2,1)S(1)}, bf16[128,128]{1,0:T(8,128)(2,1)S(1)}, u32[]{:S(2)}, u32[]{:S(2)}) %collective-permute-start.12) | collective-permute-done | bytes 32800 | tf_op jit(solution)/shard_map/ppermute | solution.py:470
  39.3 0.9 collective-permute-done.10.one
  41.0 0.9 collective-permute-start.18
  41.9 2.1 %collective-permute-start.15 = (bf16[128,128]{1,0:T(8,128)(2,1)S(1)}, bf16[128,128]{1,0:T(8,128)(2,1)S(1)}, u32[]{:S(2)}, u32[]{:S(2)}) collective-permute-start(bf16[128,128]{1,0:T(8,128)(2,1)S(1)} %convert_element_type.151), channel_id=1, source_target_pairs={{0,1},{1,0},{2,3},{3,2},{4,5},{5,4},{6,7},{7,6},{8,9},{9,8},{10,11... | collective-permute-start | bytes 98312 | tf_op jit(solution)/shard_map/ppermute | solution.py:470
  44.1 2.7 %collective-permute-done.18.two = bf16[2,64,768]{2,1,0:T(8,128)(2,1)S(1)} collective-permute-done((bf16[2,64,768]{2,1,0:T(8,128)(2,1)S(1)}, bf16[2,64,768]{2,1,0:T(8,128)(2,1)S(1)}, u32[]{:S(2)}, u32[]{:S(2)}) %collective-permute-start.18) | collective-permute-done | bytes 196640 | tf_op jit(solution)/shard_map/ppermute | solution.py:470
  46.9 2.9 %collective-permute-start.19 = (bf16[64,768]{1,0:T(8,128)(2,1)S(1)}, bf16[64,768]{1,0:T(8,128)(2,1)S(1)}, u32[]{:S(2)}, u32[]{:S(2)}) collective-permute-start(bf16[64,768]{1,0:T(8,128)(2,1)S(1)} %fusion.4), channel_id=1, source_target_pairs={{0,2},{1,3},{2,0},{3,1},{4,6},{5,7},{6,4},{7,5},{8,10},{9,11},{10,... | collective-permute-start | bytes 294920 | tf_op jit(solution)/shard_map/ppermute | solution.py:470
  49.8 1.0 collective-permute-done.13.two
  50.8 1.7 %collective-permute-start.14 = (bf16[64,768]{1,0:T(8,128)(2,1)S(1)}, bf16[64,768]{1,0:T(8,128)(2,1)S(1)}, u32[]{:S(2)}, u32[]{:S(2)}) collective-permute-start(bf16[64,768]{1,0:T(8,128)(2,1)S(1)} %fusion.5), channel_id=1, source_target_pairs={{0,2},{1,3},{2,0},{3,1},{4,6},{5,7},{6,4},{7,5},{8,10},{9,11},{10,... | collective-permute-start | bytes 294920 | tf_op jit(solution)/shard_map/ppermute | solution.py:470
  52.5 1.6 %collective-permute-start.16 = (bf16[128,128]{1,0:T(8,128)(2,1)S(1)}, bf16[128,128]{1,0:T(8,128)(2,1)S(1)}, u32[]{:S(2)}, u32[]{:S(2)}) collective-permute-start(bf16[128,128]{1,0:T(8,128)(2,1)S(1)} %get-tuple-element.76), channel_id=1, source_target_pairs={{0,16},{8,24},{16,0},{24,8},{1,17},{9,25},{17,1},{25,9},{2,18},{10... | collective-permute-start | bytes 98312 | tf_op jit(solution)/shard_map/ppermute | solution.py:470
  54.1 2.4 %collective-permute-done.16.other_ref = bf16[128,128]{1,0:T(8,128)(2,1)S(1)} collective-permute-done((bf16[128,128]{1,0:T(8,128)(2,1)S(1)}, bf16[128,128]{1,0:T(8,128)(2,1)S(1)}, u32[]{:S(2)}, u32[]{:S(2)}) %collective-permute-start.16) | collective-permute-done | bytes 32800 | tf_op jit(solution)/shard_map/ppermute | solution.py:470
  57.1 1.2 %update.3 = (f32[1,64,768]{2,1,0:T(8,128)}, f32[1,64,768]{2,1,0:T(8,128)}, f32[1,64,768]{2,1,0:T(8,128)}, bf16[1,64,768]{2,1,0:T(8,128)(2,1)S(1)}) custom-call(bf16[2,4,64,768]{3,2,1,0:T(8,128)(2,1)S(1)} %gradient.4.kept, bf16[2,4,64,768]{3,2,1,0:T(8,128)(2,1)S(1)} %collective-permute-done.7.near, bf16[4,64,768]{2,1,0:T(8,128)(2,1)S(1)} %collective-permute-done.10.one, ...), custom_call_target="tpu_custom_call" | custom-call | tf_op jit(solution)/shard_map/update/pallas_call | solution.py:390
  58.3 0.8 collective-permute-start.20
  59.0 0.8 collective-permute-done.14.last
  59.9 1.2 %update.2 = (f32[1,64,768]{2,1,0:T(8,128)}, f32[1,64,768]{2,1,0:T(8,128)}, f32[1,64,768]{2,1,0:T(8,128)}, bf16[1,64,768]{2,1,0:T(8,128)(2,1)S(1)}) custom-call(bf16[2,4,64,768]{3,2,1,0:T(8,128)(2,1)S(1)} %gradient.4.kept, bf16[2,4,64,768]{3,2,1,0:T(8,128)(2,1)S(1)} %collective-permute-done.7.near, bf16[4,64,768]{2,1,0:T(8,128)(2,1)S(1)} %collective-permute-done.9.one, ...), custom_call_target="tpu_custom_call" | custom-call | tf_op jit(solution)/shard_map/update/pallas_call | solution.py:390
  61.1 1.3 %collective-permute-start.17 = (bf16[1,64,768]{2,1,0:T(8,128)(2,1)S(1)}, bf16[1,64,768]{2,1,0:T(8,128)(2,1)S(1)}, u32[]{:S(2)}, u32[]{:S(2)}) collective-permute-start(bf16[1,64,768]{2,1,0:T(8,128)(2,1)S(1)} %get-tuple-element.60), channel_id=1, source_target_pairs={{0,2},{1,3},{2,0},{3,1},{4,6},{5,7},{6,4},{7,5},{8,10},{9,11},{10,... | collective-permute-start | bytes 294920 | tf_op jit(solution)/shard_map/ppermute | solution.py:470
  62.5 1.8 %collective-permute-start.21 = (bf16[2,64,768]{2,1,0:T(8,128)(2,1)S(1)}, bf16[2,64,768]{2,1,0:T(8,128)(2,1)S(1)}, u32[]{:S(2)}, u32[]{:S(2)}) collective-permute-start(bf16[2,64,768]{2,1,0:T(8,128)(2,1)S(1)} %pad_maximum_fusion.6), channel_id=1, source_target_pairs={{4,0},{0,4},{5,1},{1,5},{6,2},{2,6},{7,3},{3,7},{12,8},{8,12},{13,... | collective-permute-start | bytes 589832 | tf_op jit(solution)/shard_map/ppermute | solution.py:480
  64.3 1.7 %collective-permute-done.20 = bf16[1,64,768]{2,1,0:T(8,128)(2,1)S(1)} collective-permute-done((bf16[1,64,768]{2,1,0:T(8,128)(2,1)S(1)}, bf16[1,64,768]{2,1,0:T(8,128)(2,1)S(1)}, u32[]{:S(2)}, u32[]{:S(2)}) %collective-permute-start.20) | collective-permute-done | bytes 98336 | tf_op jit(solution)/shard_map/ppermute | solution.py:470
  66.1 0.9 collective-permute-done.17
  67.1 3.4 %collective-permute-start.23 = (bf16[2,64,768]{2,1,0:T(8,128)(2,1)S(1)}, bf16[2,64,768]{2,1,0:T(8,128)(2,1)S(1)}, u32[]{:S(2)}, u32[]{:S(2)}) collective-permute-start(bf16[2,64,768]{2,1,0:T(8,128)(2,1)S(1)} %pad_maximum_fusion.8), channel_id=1, source_target_pairs={{0,1},{1,0},{2,3},{3,2},{4,5},{5,4},{6,7},{7,6},{8,9},{9,8},{10,11... | collective-permute-start | bytes 589832 | tf_op jit(solution)/shard_map/ppermute | solution.py:470
  70.4 1.3 %collective-permute-start.22 = (bf16[2,64,768]{2,1,0:T(8,128)(2,1)S(1)}, bf16[2,64,768]{2,1,0:T(8,128)(2,1)S(1)}, u32[]{:S(2)}, u32[]{:S(2)}) collective-permute-start(bf16[2,64,768]{2,1,0:T(8,128)(2,1)S(1)} %pad_maximum_fusion.7), channel_id=1, source_target_pairs={{4,0},{0,4},{5,1},{1,5},{6,2},{2,6},{7,3},{3,7},{12,8},{8,12},{13,... | collective-permute-start | bytes 589832 | tf_op jit(solution)/shard_map/ppermute | solution.py:480
  71.8 2.7 %collective-permute-done.23 = bf16[2,64,768]{2,1,0:T(8,128)(2,1)S(1)} collective-permute-done((bf16[2,64,768]{2,1,0:T(8,128)(2,1)S(1)}, bf16[2,64,768]{2,1,0:T(8,128)(2,1)S(1)}, u32[]{:S(2)}, u32[]{:S(2)}) %collective-permute-start.23) | collective-permute-done | bytes 196640 | tf_op jit(solution)/shard_map/ppermute | solution.py:470
  74.7 1.5 %collective-permute-start.24 = (bf16[4,64,768]{2,1,0:T(8,128)(2,1)S(1)}, bf16[4,64,768]{2,1,0:T(8,128)(2,1)S(1)}, u32[]{:S(2)}, u32[]{:S(2)}) collective-permute-start(bf16[4,64,768]{2,1,0:T(8,128)(2,1)S(1)} %get-tuple-element.89), channel_id=1, source_target_pairs={{0,16},{8,24},{16,0},{24,8},{1,17},{9,25},{17,1},{25,9},{2,18},{10... | collective-permute-start | bytes 1179656 | tf_op jit(solution)/shard_map/ppermute | solution.py:470
  76.2 2.5 %collective-permute-start.26 = (bf16[4,64,768]{2,1,0:T(8,128)(2,1)S(1)}, bf16[4,64,768]{2,1,0:T(8,128)(2,1)S(1)}, u32[]{:S(2)}, u32[]{:S(2)}) collective-permute-start(bf16[4,64,768]{2,1,0:T(8,128)(2,1)S(1)} %get-tuple-element.90), channel_id=1, source_target_pairs={{0,1},{1,0},{2,3},{3,2},{4,5},{5,4},{6,7},{7,6},{8,9},{9,8},{10,11... | collective-permute-start | bytes 1179656 | tf_op jit(solution)/shard_map/ppermute | solution.py:470
  78.9 5.0 %collective-permute-done.27 = bf16[4,64,768]{2,1,0:T(8,128)(2,1)S(1)} collective-permute-done((bf16[4,64,768]{2,1,0:T(8,128)(2,1)S(1)}, bf16[4,64,768]{2,1,0:T(8,128)(2,1)S(1)}, u32[]{:S(2)}, u32[]{:S(2)}) %collective-permute-start.27) | collective-permute-done | bytes 393248 | tf_op jit(solution)/shard_map/ppermute | solution.py:480
  83.8 2.1 %collective-permute-done.26 = bf16[4,64,768]{2,1,0:T(8,128)(2,1)S(1)} collective-permute-done((bf16[4,64,768]{2,1,0:T(8,128)(2,1)S(1)}, bf16[4,64,768]{2,1,0:T(8,128)(2,1)S(1)}, u32[]{:S(2)}, u32[]{:S(2)}) %collective-permute-start.26) | collective-permute-done | bytes 393248 | tf_op jit(solution)/shard_map/ppermute | solution.py:470
  86.0 3.1 %collective-permute-start.30 = (bf16[2,64,768]{2,1,0:T(8,128)(2,1)S(1)}, bf16[2,64,768]{2,1,0:T(8,128)(2,1)S(1)}, u32[]{:S(2)}, u32[]{:S(2)}) collective-permute-start(bf16[2,64,768]{2,1,0:T(8,128)(2,1)S(1)} %pad_maximum_fusion.10), channel_id=1, source_target_pairs={{4,0},{0,4},{5,1},{1,5},{6,2},{2,6},{7,3},{3,7},{12,8},{8,12},{13,... | collective-permute-start | bytes 589832 | tf_op jit(solution)/shard_map/ppermute | solution.py:480
  89.2 2.5 %collective-permute-start.29 = (bf16[3,64,768]{2,1,0:T(8,128)(2,1)S(1)}, bf16[3,64,768]{2,1,0:T(8,128)(2,1)S(1)}, u32[]{:S(2)}, u32[]{:S(2)}) collective-permute-start(bf16[3,64,768]{2,1,0:T(8,128)(2,1)S(1)} %pad_maximum_fusion.4), channel_id=1, source_target_pairs={{0,1},{1,0},{2,3},{3,2},{4,5},{5,4},{6,7},{7,6},{8,9},{9,8},{10,11... | collective-permute-start | bytes 884744 | tf_op jit(solution)/shard_map/ppermute | solution.py:470
  91.9 3.9 %collective-permute-done.28 = bf16[3,64,768]{2,1,0:T(8,128)(2,1)S(1)} collective-permute-done((bf16[3,64,768]{2,1,0:T(8,128)(2,1)S(1)}, bf16[3,64,768]{2,1,0:T(8,128)(2,1)S(1)}, u32[]{:S(2)}, u32[]{:S(2)}) %collective-permute-start.28) | collective-permute-done | bytes 294944 | tf_op jit(solution)/shard_map/ppermute | solution.py:470
  96.6 1.5 %collective-permute-done.34.refs_5_ = bf16[8,64,768]{2,1,0:T(8,128)(2,1)S(1)} collective-permute-done((bf16[8,64,768]{2,1,0:T(8,128)(2,1)S(1)}, bf16[8,64,768]{2,1,0:T(8,128)(2,1)S(1)}, u32[]{:S(2)}, u32[]{:S(2)}) %collective-permute-start.34) | collective-permute-done | bytes 786464 | tf_op jit(solution)/shard_map/ppermute | solution.py:470
  98.1 2.3 %place.2 = (bf16[2,64,12288]{2,1,0:T(8,128)(2,1)}, bf16[2,64,12288]{2,1,0:T(8,128)(2,1)}) custom-call(s32[4,3]{1,0:T(4,128)S(1)} %copy-done.8, bf16[8,64,768]{2,1,0:T(8,128)(2,1)S(1)} %constant_dynamic-update-slice_fusion.3.refs_0_, bf16[8,64,768]{2,1,0:T(8,128)(2,1)S(1)} %collective-permute-done.32.refs_1_, ...), custom_call_target="tpu_custom_call" | custom-call | bytes 9437184 | tf_op jit(solution)/shard_map/place/pallas_call | solution.py:451
  100.4 1.3 %place.3 = (bf16[2,64,12288]{2,1,0:T(8,128)(2,1)}, bf16[2,64,12288]{2,1,0:T(8,128)(2,1)}) custom-call(s32[4,3]{1,0:T(4,128)S(1)} %copy-done.8, bf16[8,64,768]{2,1,0:T(8,128)(2,1)S(1)} %constant_dynamic-update-slice_fusion.refs_0_, bf16[8,64,768]{2,1,0:T(8,128)(2,1)S(1)} %collective-permute-done.31.refs_1_, ...), custom_call_target="tpu_custom_call", output_to_operand_aliasing={{0}: (3, {}), {1}: (4, {})} | custom-call | bytes 3145728 | tf_op jit(solution)/shard_map/place/pallas_call | solution.py:451
  (95 shorter events, 6.9 us)
Async XLA Ops:
  1.6 8.0 %collective-permute-start = (bf16[64,768]{1,0:T(8,128)(2,1)S(1)}, bf16[64,768]{1,0:T(8,128)(2,1)S(1)}, u32[]{:S(2)}, u32[]{:S(2)}) collective-permute-start(bf16[64,768]{1,0:T(8,128)(2,1)S(1)} %fusion.6), channel_id=1, source_target_pairs={{4,0},{0,4},{5,1},{1,5},{6,2},{2,6},{7,3},{3,7},{12,8},{8,12},{13,... | collective-permute-start | bytes 294920 | tf_op jit(solution)/shard_map/ppermute | solution.py:480
  5.7 6.1 %copy-start = (bf16[1,4,32,12288]{3,2,1,0:T(8,128)(2,1)S(1)}, bf16[1,4,32,12288]{3,2,1,0:T(8,128)(2,1)}, u32[]{:S(2)}) copy-start(bf16[1,4,32,12288]{3,2,1,0:T(8,128)(2,1)} %param.13) | copy-start | bytes 9437188
  5.7 6.0 %copy-start.1 = (bf16[1,1,2,64,12288]{4,3,2,1,0:T(8,128)(2,1)S(1)}, bf16[1,1,2,64,12288]{4,3,2,1,0:T(8,128)(2,1)}, u32[]{:S(2)}) copy-start(bf16[1,1,2,64,12288]{4,3,2,1,0:T(8,128)(2,1)} %param.17) | copy-start | bytes 9437188
  5.7 6.0 %copy-start.9 = (s32[4]{0:T(128)S(1)}, s32[4]{0:T(128)}, u32[]{:S(2)}) copy-start(s32[4]{0:T(128)} %param.14) | copy-start | bytes 52
  9.8 4.1 %collective-permute-start.4 = (f32[64,128]{1,0:T(8,128)S(1)}, f32[64,128]{1,0:T(8,128)S(1)}, u32[]{:S(2)}, u32[]{:S(2)}) collective-permute-start(f32[64,128]{1,0:T(8,128)S(1)} %get-tuple-element.48), channel_id=1, source_target_pairs={{0,24},{8,16},{16,8},{24,0},{1,25},{9,17},{17,9},{25,1},{2,26},{10... | collective-permute-start | bytes 98312 | tf_op jit(solution)/shard_map/ppermute | solution.py:470
  10.5 4.3 %collective-permute-start.3 = (f32[64,128]{1,0:T(8,128)S(1)}, f32[64,128]{1,0:T(8,128)S(1)}, u32[]{:S(2)}, u32[]{:S(2)}) collective-permute-start(f32[64,128]{1,0:T(8,128)S(1)} %get-tuple-element.48), channel_id=1, source_target_pairs={{0,16},{8,24},{16,0},{24,8},{1,17},{9,25},{17,1},{25,9},{2,18},{10... | collective-permute-start | bytes 98312 | tf_op jit(solution)/shard_map/ppermute | solution.py:470
  11.4 3.3 %collective-permute-start.2 = (f32[64,128]{1,0:T(8,128)S(1)}, f32[64,128]{1,0:T(8,128)S(1)}, u32[]{:S(2)}, u32[]{:S(2)}) collective-permute-start(f32[64,128]{1,0:T(8,128)S(1)} %get-tuple-element.48), channel_id=1, source_target_pairs={{0,8},{8,0},{16,24},{24,16},{1,9},{9,1},{17,25},{25,17},{2,10},{10... | collective-permute-start | bytes 98312 | tf_op jit(solution)/shard_map/ppermute | solution.py:470
  11.7 11.9 %copy-start.8 = (s32[4,3]{1,0:T(4,128)S(1)}, s32[4,3]{1,0:T(4,128)}, u32[]{:S(2)}) copy-start(s32[4,3]{1,0:T(4,128)} %bounds.5) | copy-start | bytes 148
  13.5 10.1 %collective-permute-start.1 = (f32[128,384]{1,0:T(8,128)S(1)}, f32[128,384]{1,0:T(8,128)S(1)}, u32[]{:S(2)}, u32[]{:S(2)}) collective-permute-start(f32[128,384]{1,0:T(8,128)S(1)} %project_up.1.refs_0_), channel_id=1, source_target_pairs={{4,0},{0,4},{5,1},{1,5},{6,2},{2,6},{7,3},{3,7},{12,8},{8,12},{13,... | collective-permute-start | bytes 589832 | tf_op jit(solution)/shard_map/ppermute | solution.py:480
  14.8 4.0 %collective-permute-start.5 = (f32[64,128]{1,0:T(8,128)S(1)}, f32[64,128]{1,0:T(8,128)S(1)}, u32[]{:S(2)}, u32[]{:S(2)}) collective-permute-start(f32[64,128]{1,0:T(8,128)S(1)} %add_add_fusion), channel_id=1, source_target_pairs={{0,1},{1,0},{2,3},{3,2},{4,5},{5,4},{6,7},{7,6},{8,9},{9,8},{10,11... | collective-permute-start | bytes 98312 | tf_op jit(solution)/shard_map/ppermute | solution.py:470
  18.8 4.8 %collective-permute-start.6 = (f32[64,128]{1,0:T(8,128)S(1)}, f32[64,128]{1,0:T(8,128)S(1)}, u32[]{:S(2)}, u32[]{:S(2)}) collective-permute-start(f32[64,128]{1,0:T(8,128)S(1)} %add.74.refs_2_), channel_id=1, source_target_pairs={{0,2},{1,3},{2,0},{3,1},{4,6},{5,7},{6,4},{7,5},{8,10},{9,11},{10,... | collective-permute-start | bytes 98312 | tf_op jit(solution)/shard_map/ppermute | solution.py:470
  25.7 2.4 %collective-permute-start.8 = (bf16[2,4,64,768]{3,2,1,0:T(8,128)(2,1)S(1)}, bf16[2,4,64,768]{3,2,1,0:T(8,128)(2,1)S(1)}, u32[]{:S(2)}, u32[]{:S(2)}) collective-permute-start(bf16[2,4,64,768]{3,2,1,0:T(8,128)(2,1)S(1)} %gradient.7), channel_id=1, source_target_pairs={{0,8},{8,0},{16,24},{24,16},{1,9},{9,1},{17,25},{25,17},{2,10},{10... | collective-permute-start | bytes 2359304 | tf_op jit(solution)/shard_map/ppermute | solution.py:470
  26.3 14.5 %collective-permute-start.7 = (bf16[2,4,64,768]{3,2,1,0:T(8,128)(2,1)S(1)}, bf16[2,4,64,768]{3,2,1,0:T(8,128)(2,1)S(1)}, u32[]{:S(2)}, u32[]{:S(2)}) collective-permute-start(bf16[2,4,64,768]{3,2,1,0:T(8,128)(2,1)S(1)} %gradient.5), channel_id=1, source_target_pairs={{0,8},{8,0},{16,24},{24,16},{1,9},{9,1},{17,25},{25,17},{2,10},{10... | collective-permute-start | bytes 2359304 | tf_op jit(solution)/shard_map/ppermute | solution.py:470
  26.9 3.9 %collective-permute-start.11 = (bf16[128,128]{1,0:T(8,128)(2,1)S(1)}, bf16[128,128]{1,0:T(8,128)(2,1)S(1)}, u32[]{:S(2)}, u32[]{:S(2)}) collective-permute-start(bf16[128,128]{1,0:T(8,128)(2,1)S(1)} %convert_element_type.136), channel_id=1, source_target_pairs={{0,8},{8,0},{16,24},{24,16},{1,9},{9,1},{17,25},{25,17},{2,10},{10... | collective-permute-start | bytes 98312 | tf_op jit(solution)/shard_map/ppermute | solution.py:470
  28.3 11.9 %collective-permute-start.10 = (bf16[4,64,768]{2,1,0:T(8,128)(2,1)S(1)}, bf16[4,64,768]{2,1,0:T(8,128)(2,1)S(1)}, u32[]{:S(2)}, u32[]{:S(2)}) collective-permute-start(bf16[4,64,768]{2,1,0:T(8,128)(2,1)S(1)} %get-tuple-element.80), channel_id=1, source_target_pairs={{0,1},{1,0},{2,3},{3,2},{4,5},{5,4},{6,7},{7,6},{8,9},{9,8},{10,11... | collective-permute-start | bytes 1179656 | tf_op jit(solution)/shard_map/ppermute | solution.py:470
  29.9 10.9 %collective-permute-start.9 = (bf16[4,64,768]{2,1,0:T(8,128)(2,1)S(1)}, bf16[4,64,768]{2,1,0:T(8,128)(2,1)S(1)}, u32[]{:S(2)}, u32[]{:S(2)}) collective-permute-start(bf16[4,64,768]{2,1,0:T(8,128)(2,1)S(1)} %get-tuple-element.81), channel_id=1, source_target_pairs={{0,16},{8,24},{16,0},{24,8},{1,17},{9,25},{17,1},{25,9},{2,18},{10... | collective-permute-start | bytes 1179656 | tf_op jit(solution)/shard_map/ppermute | solution.py:470
  30.8 8.5 %collective-permute-start.12 = (bf16[128,128]{1,0:T(8,128)(2,1)S(1)}, bf16[128,128]{1,0:T(8,128)(2,1)S(1)}, u32[]{:S(2)}, u32[]{:S(2)}) collective-permute-start(bf16[128,128]{1,0:T(8,128)(2,1)S(1)} %fusion.7), channel_id=1, source_target_pairs={{0,2},{1,3},{2,0},{3,1},{4,6},{5,7},{6,4},{7,5},{8,10},{9,11},{10,... | collective-permute-start | bytes 98312 | tf_op jit(solution)/shard_map/ppermute | solution.py:470
  34.2 22.8 %copy-start.2 = (f32[1,64,768]{2,1,0:T(8,128)S(1)}, f32[1,64,768]{2,1,0:T(8,128)}, u32[]{:S(2)}) copy-start(f32[1,64,768]{2,1,0:T(8,128)} %refs_0_.3) | copy-start | bytes 589828
  34.2 22.8 %copy-start.4 = (f32[1,64,768]{2,1,0:T(8,128)S(1)}, f32[1,64,768]{2,1,0:T(8,128)}, u32[]{:S(2)}) copy-start(f32[1,64,768]{2,1,0:T(8,128)} %refs_1_.3) | copy-start | bytes 589828
  34.2 22.8 %copy-start.5 = (f32[1,64,768]{2,1,0:T(8,128)S(1)}, f32[1,64,768]{2,1,0:T(8,128)}, u32[]{:S(2)}) copy-start(f32[1,64,768]{2,1,0:T(8,128)} %refs_2_.3) | copy-start | bytes 589828
  34.2 25.6 %copy-start.3 = (f32[1,64,768]{2,1,0:T(8,128)S(1)}, f32[1,64,768]{2,1,0:T(8,128)}, u32[]{:S(2)}) copy-start(f32[1,64,768]{2,1,0:T(8,128)} %refs_0_.2) | copy-start | bytes 589828
  34.3 25.6 %copy-start.6 = (f32[1,64,768]{2,1,0:T(8,128)S(1)}, f32[1,64,768]{2,1,0:T(8,128)}, u32[]{:S(2)}) copy-start(f32[1,64,768]{2,1,0:T(8,128)} %refs_1_.2) | copy-start | bytes 589828
  34.3 25.6 %copy-start.7 = (f32[1,64,768]{2,1,0:T(8,128)S(1)}, f32[1,64,768]{2,1,0:T(8,128)}, u32[]{:S(2)}) copy-start(f32[1,64,768]{2,1,0:T(8,128)} %refs_2_.2) | copy-start | bytes 589828
  41.0 5.9 %collective-permute-start.18 = (bf16[2,64,768]{2,1,0:T(8,128)(2,1)S(1)}, bf16[2,64,768]{2,1,0:T(8,128)(2,1)S(1)}, u32[]{:S(2)}, u32[]{:S(2)}) collective-permute-start(bf16[2,64,768]{2,1,0:T(8,128)(2,1)S(1)} %get-tuple-element.78), channel_id=1, source_target_pairs={{0,16},{8,24},{16,0},{24,8},{1,17},{9,25},{17,1},{25,9},{2,18},{10... | collective-permute-start | bytes 589832 | tf_op jit(solution)/shard_map/ppermute | solution.py:470
  41.9 10.6 %collective-permute-start.15 = (bf16[128,128]{1,0:T(8,128)(2,1)S(1)}, bf16[128,128]{1,0:T(8,128)(2,1)S(1)}, u32[]{:S(2)}, u32[]{:S(2)}) collective-permute-start(bf16[128,128]{1,0:T(8,128)(2,1)S(1)} %convert_element_type.151), channel_id=1, source_target_pairs={{0,1},{1,0},{2,3},{3,2},{4,5},{5,4},{6,7},{7,6},{8,9},{9,8},{10,11... | collective-permute-start | bytes 98312 | tf_op jit(solution)/shard_map/ppermute | solution.py:470
  44.0 6.7 %collective-permute-start.13 = (bf16[2,64,768]{2,1,0:T(8,128)(2,1)S(1)}, bf16[2,64,768]{2,1,0:T(8,128)(2,1)S(1)}, u32[]{:S(2)}, u32[]{:S(2)}) collective-permute-start(bf16[2,64,768]{2,1,0:T(8,128)(2,1)S(1)} %get-tuple-element.79), channel_id=1, source_target_pairs={{0,1},{1,0},{2,3},{3,2},{4,5},{5,4},{6,7},{7,6},{8,9},{9,8},{10,11... | collective-permute-start | bytes 589832 | tf_op jit(solution)/shard_map/ppermute | solution.py:470
  46.9 10.2 %collective-permute-start.19 = (bf16[64,768]{1,0:T(8,128)(2,1)S(1)}, bf16[64,768]{1,0:T(8,128)(2,1)S(1)}, u32[]{:S(2)}, u32[]{:S(2)}) collective-permute-start(bf16[64,768]{1,0:T(8,128)(2,1)S(1)} %fusion.4), channel_id=1, source_target_pairs={{0,2},{1,3},{2,0},{3,1},{4,6},{5,7},{6,4},{7,5},{8,10},{9,11},{10,... | collective-permute-start | bytes 294920 | tf_op jit(solution)/shard_map/ppermute | solution.py:470
  50.8 9.1 %collective-permute-start.14 = (bf16[64,768]{1,0:T(8,128)(2,1)S(1)}, bf16[64,768]{1,0:T(8,128)(2,1)S(1)}, u32[]{:S(2)}, u32[]{:S(2)}) collective-permute-start(bf16[64,768]{1,0:T(8,128)(2,1)S(1)} %fusion.5), channel_id=1, source_target_pairs={{0,2},{1,3},{2,0},{3,1},{4,6},{5,7},{6,4},{7,5},{8,10},{9,11},{10,... | collective-permute-start | bytes 294920 | tf_op jit(solution)/shard_map/ppermute | solution.py:470
  52.5 4.0 %collective-permute-start.16 = (bf16[128,128]{1,0:T(8,128)(2,1)S(1)}, bf16[128,128]{1,0:T(8,128)(2,1)S(1)}, u32[]{:S(2)}, u32[]{:S(2)}) collective-permute-start(bf16[128,128]{1,0:T(8,128)(2,1)S(1)} %get-tuple-element.76), channel_id=1, source_target_pairs={{0,16},{8,24},{16,0},{24,8},{1,17},{9,25},{17,1},{25,9},{2,18},{10... | collective-permute-start | bytes 98312 | tf_op jit(solution)/shard_map/ppermute | solution.py:470
  58.3 7.7 %collective-permute-start.20 = (bf16[1,64,768]{2,1,0:T(8,128)(2,1)S(1)}, bf16[1,64,768]{2,1,0:T(8,128)(2,1)S(1)}, u32[]{:S(2)}, u32[]{:S(2)}) collective-permute-start(bf16[1,64,768]{2,1,0:T(8,128)(2,1)S(1)} %get-tuple-element.61), channel_id=1, source_target_pairs={{0,2},{1,3},{2,0},{3,1},{4,6},{5,7},{6,4},{7,5},{8,10},{9,11},{10,... | collective-permute-start | bytes 294920 | tf_op jit(solution)/shard_map/ppermute | solution.py:470
  61.1 5.9 %collective-permute-start.17 = (bf16[1,64,768]{2,1,0:T(8,128)(2,1)S(1)}, bf16[1,64,768]{2,1,0:T(8,128)(2,1)S(1)}, u32[]{:S(2)}, u32[]{:S(2)}) collective-permute-start(bf16[1,64,768]{2,1,0:T(8,128)(2,1)S(1)} %get-tuple-element.60), channel_id=1, source_target_pairs={{0,2},{1,3},{2,0},{3,1},{4,6},{5,7},{6,4},{7,5},{8,10},{9,11},{10,... | collective-permute-start | bytes 294920 | tf_op jit(solution)/shard_map/ppermute | solution.py:470
  62.5 7.9 %collective-permute-start.21 = (bf16[2,64,768]{2,1,0:T(8,128)(2,1)S(1)}, bf16[2,64,768]{2,1,0:T(8,128)(2,1)S(1)}, u32[]{:S(2)}, u32[]{:S(2)}) collective-permute-start(bf16[2,64,768]{2,1,0:T(8,128)(2,1)S(1)} %pad_maximum_fusion.6), channel_id=1, source_target_pairs={{4,0},{0,4},{5,1},{1,5},{6,2},{2,6},{7,3},{3,7},{12,8},{8,12},{13,... | collective-permute-start | bytes 589832 | tf_op jit(solution)/shard_map/ppermute | solution.py:480
  66.0 5.8 %collective-permute-start.25 = (bf16[2,64,768]{2,1,0:T(8,128)(2,1)S(1)}, bf16[2,64,768]{2,1,0:T(8,128)(2,1)S(1)}, u32[]{:S(2)}, u32[]{:S(2)}) collective-permute-start(bf16[2,64,768]{2,1,0:T(8,128)(2,1)S(1)} %pad_maximum_fusion.9), channel_id=1, source_target_pairs={{0,16},{8,24},{16,0},{24,8},{1,17},{9,25},{17,1},{25,9},{2,18},{10... | collective-permute-start | bytes 589832 | tf_op jit(solution)/shard_map/ppermute | solution.py:470
  67.1 7.4 %collective-permute-start.23 = (bf16[2,64,768]{2,1,0:T(8,128)(2,1)S(1)}, bf16[2,64,768]{2,1,0:T(8,128)(2,1)S(1)}, u32[]{:S(2)}, u32[]{:S(2)}) collective-permute-start(bf16[2,64,768]{2,1,0:T(8,128)(2,1)S(1)} %pad_maximum_fusion.8), channel_id=1, source_target_pairs={{0,1},{1,0},{2,3},{3,2},{4,5},{5,4},{6,7},{7,6},{8,9},{9,8},{10,11... | collective-permute-start | bytes 589832 | tf_op jit(solution)/shard_map/ppermute | solution.py:470
  70.4 8.4 %collective-permute-start.22 = (bf16[2,64,768]{2,1,0:T(8,128)(2,1)S(1)}, bf16[2,64,768]{2,1,0:T(8,128)(2,1)S(1)}, u32[]{:S(2)}, u32[]{:S(2)}) collective-permute-start(bf16[2,64,768]{2,1,0:T(8,128)(2,1)S(1)} %pad_maximum_fusion.7), channel_id=1, source_target_pairs={{4,0},{0,4},{5,1},{1,5},{6,2},{2,6},{7,3},{3,7},{12,8},{8,12},{13,... | collective-permute-start | bytes 589832 | tf_op jit(solution)/shard_map/ppermute | solution.py:480
  74.6 9.2 %collective-permute-start.27 = (bf16[4,64,768]{2,1,0:T(8,128)(2,1)S(1)}, bf16[4,64,768]{2,1,0:T(8,128)(2,1)S(1)}, u32[]{:S(2)}, u32[]{:S(2)}) collective-permute-start(bf16[4,64,768]{2,1,0:T(8,128)(2,1)S(1)} %get-tuple-element.88), channel_id=1, source_target_pairs={{4,0},{0,4},{5,1},{1,5},{6,2},{2,6},{7,3},{3,7},{12,8},{8,12},{13,... | collective-permute-start | bytes 1179656 | tf_op jit(solution)/shard_map/ppermute | solution.py:480
  74.7 9.2 %collective-permute-start.24 = (bf16[4,64,768]{2,1,0:T(8,128)(2,1)S(1)}, bf16[4,64,768]{2,1,0:T(8,128)(2,1)S(1)}, u32[]{:S(2)}, u32[]{:S(2)}) collective-permute-start(bf16[4,64,768]{2,1,0:T(8,128)(2,1)S(1)} %get-tuple-element.89), channel_id=1, source_target_pairs={{0,16},{8,24},{16,0},{24,8},{1,17},{9,25},{17,1},{25,9},{2,18},{10... | collective-permute-start | bytes 1179656 | tf_op jit(solution)/shard_map/ppermute | solution.py:470
  76.2 9.7 %collective-permute-start.26 = (bf16[4,64,768]{2,1,0:T(8,128)(2,1)S(1)}, bf16[4,64,768]{2,1,0:T(8,128)(2,1)S(1)}, u32[]{:S(2)}, u32[]{:S(2)}) collective-permute-start(bf16[4,64,768]{2,1,0:T(8,128)(2,1)S(1)} %get-tuple-element.90), channel_id=1, source_target_pairs={{0,1},{1,0},{2,3},{3,2},{4,5},{5,4},{6,7},{7,6},{8,9},{9,8},{10,11... | collective-permute-start | bytes 1179656 | tf_op jit(solution)/shard_map/ppermute | solution.py:470
  78.7 17.9 %collective-permute-start.32 = (bf16[8,64,768]{2,1,0:T(8,128)(2,1)S(1)}, bf16[8,64,768]{2,1,0:T(8,128)(2,1)S(1)}, u32[]{:S(2)}, u32[]{:S(2)}) collective-permute-start(bf16[8,64,768]{2,1,0:T(8,128)(2,1)S(1)} %constant_dynamic-update-slice_fusion.3.refs_0_), channel_id=1, source_target_pairs={{0,8},{8,0},{16,24},{24,16},{1,9},{9,1},{17,25},{25,17},{2,10},{10... | collective-permute-start | bytes 2359304 | tf_op jit(solution)/shard_map/ppermute | solution.py:470
  86.0 10.5 %collective-permute-start.30 = (bf16[2,64,768]{2,1,0:T(8,128)(2,1)S(1)}, bf16[2,64,768]{2,1,0:T(8,128)(2,1)S(1)}, u32[]{:S(2)}, u32[]{:S(2)}) collective-permute-start(bf16[2,64,768]{2,1,0:T(8,128)(2,1)S(1)} %pad_maximum_fusion.10), channel_id=1, source_target_pairs={{4,0},{0,4},{5,1},{1,5},{6,2},{2,6},{7,3},{3,7},{12,8},{8,12},{13,... | collective-permute-start | bytes 589832 | tf_op jit(solution)/shard_map/ppermute | solution.py:480
  89.1 6.8 %collective-permute-start.28 = (bf16[3,64,768]{2,1,0:T(8,128)(2,1)S(1)}, bf16[3,64,768]{2,1,0:T(8,128)(2,1)S(1)}, u32[]{:S(2)}, u32[]{:S(2)}) collective-permute-start(bf16[3,64,768]{2,1,0:T(8,128)(2,1)S(1)} %pad_maximum_fusion.3), channel_id=1, source_target_pairs={{0,16},{8,24},{16,0},{24,8},{1,17},{9,25},{17,1},{25,9},{2,18},{10... | collective-permute-start | bytes 884744 | tf_op jit(solution)/shard_map/ppermute | solution.py:470
  89.2 7.2 %collective-permute-start.29 = (bf16[3,64,768]{2,1,0:T(8,128)(2,1)S(1)}, bf16[3,64,768]{2,1,0:T(8,128)(2,1)S(1)}, u32[]{:S(2)}, u32[]{:S(2)}) collective-permute-start(bf16[3,64,768]{2,1,0:T(8,128)(2,1)S(1)} %pad_maximum_fusion.4), channel_id=1, source_target_pairs={{0,1},{1,0},{2,3},{3,2},{4,5},{5,4},{6,7},{7,6},{8,9},{9,8},{10,11... | collective-permute-start | bytes 884744 | tf_op jit(solution)/shard_map/ppermute | solution.py:470
  91.8 4.8 %collective-permute-start.33 = (bf16[8,64,768]{2,1,0:T(8,128)(2,1)S(1)}, bf16[8,64,768]{2,1,0:T(8,128)(2,1)S(1)}, u32[]{:S(2)}, u32[]{:S(2)}) collective-permute-start(bf16[8,64,768]{2,1,0:T(8,128)(2,1)S(1)} %constant_dynamic-update-slice_fusion.9.refs_2_), channel_id=1, source_target_pairs={{0,8},{8,0},{16,24},{24,16},{1,9},{9,1},{17,25},{25,17},{2,10},{10... | collective-permute-start | bytes 2359304 | tf_op jit(solution)/shard_map/ppermute | solution.py:470
  95.9 2.3 %collective-permute-start.34 = (bf16[8,64,768]{2,1,0:T(8,128)(2,1)S(1)}, bf16[8,64,768]{2,1,0:T(8,128)(2,1)S(1)}, u32[]{:S(2)}, u32[]{:S(2)}) collective-permute-start(bf16[8,64,768]{2,1,0:T(8,128)(2,1)S(1)} %constant_dynamic-update-slice_fusion.11.refs_4_), channel_id=1, source_target_pairs={{0,8},{8,0},{16,24},{24,16},{1,9},{9,1},{17,25},{25,17},{2,10},{10... | collective-permute-start | bytes 2359304 | tf_op jit(solution)/shard_map/ppermute | solution.py:470
  96.5 3.9 %collective-permute-start.31 = (bf16[8,64,768]{2,1,0:T(8,128)(2,1)S(1)}, bf16[8,64,768]{2,1,0:T(8,128)(2,1)S(1)}, u32[]{:S(2)}, u32[]{:S(2)}) collective-permute-start(bf16[8,64,768]{2,1,0:T(8,128)(2,1)S(1)} %constant_dynamic-update-slice_fusion.refs_0_), channel_id=1, source_target_pairs={{0,8},{8,0},{16,24},{24,16},{1,9},{9,1},{17,25},{25,17},{2,10},{10... | collective-permute-start | bytes 2359304 | tf_op jit(solution)/shard_map/ppermute | solution.py:470

commit v13 on v11

--- a/solution.py
+++ b/solution.py
@@ -533,9 +533,9 @@
     return blocks, swapped(array, axis, distance)
 
 
-def fetched(piece):
+def fetched(piece, fetch):
     blocks, array = piece
-    return [(1, *block[1:]) for block in blocks], following_layer(array)
+    return [(1, *block[1:]) for block in blocks], fetch(array)
 
 
 def picked(piece, at):
@@ -555,18 +555,19 @@
     downs, ups = joined(down_own, down_one), joined(up_own, up_one)
     owns = lax.optimization_barrier((down, up))
     own = joined((down_own[0], owns[0]), (up_own[0], owns[1]))
-    next_own = fetched(own)
+    next_own = fetched(own, from_next)
     *ones, next_array = lax.optimization_barrier((down_one[1], up_one[1], next_own[1]))
     one = joined((down_one[0], ones[0]), (up_one[0], ones[1]))
     next_own = (next_own[0], next_array)
     down_two = crossed(downs, "tensor", 1)
     up_two = crossed(ups, "replica", 2)
-    next_one = fetched(one)
+    next_one = fetched(one, from_next)
     two = joined(down_two, up_two)
     down_three = crossed(joined(downs, down_two), "replica", 2)
     up_three = crossed(joined(ups, up_two), "tensor", 1)
-    next_two = fetched(two)
-    next_end = fetched(joined(picked(down_three, 3), picked(up_three, 3)))
+    next_two = fetched(two, from_next)
+    ends = joined(picked(down_three, 3), picked(up_three, 3))
+    next_end = fetched(ends, following_layer)
     _, _, next_array = lax.optimization_barrier((down_three[1], up_three[1], next_two[1]))
     next_two = (next_two[0], next_array)
     down_end = joined(picked(next_own, 0), picked(next_one, 0), picked(next_two, 0))

time: 101 us -> 100 us (0.990)
  starting transfers between devices: 43.3 us -> 41.7 us
    ppermute x4 -> x1, waiting for transfers between devices: 5.72 us -> 0.01 us  [following_layer(): return lax.ppermute(block, 'section', [(i + 1, i) for i in range(size - 1)])]
    ppermute x2 -> x5, waiting for transfers between devices: 0.01 us -> 4.51 us  [from_next(): return lax.ppermute(block, 'section', route)]
    ppermute x4 -> x1, starting transfers between devices: 5.17 us -> 1.29 us  [following_layer(): return lax.ppermute(block, 'section', [(i + 1, i) for i in range(size - 1)])]
    ppermute x2 -> x5, starting transfers between devices: 3.36 us -> 6.48 us  [from_next(): return lax.ppermute(block, 'section', route)]
    ppermute x29, waiting for transfers between devices: 31.5 us -> 33.6 us  [swapped(): return lax.ppermute(block, axis, route)]
where the time goes in v13:
time: 100 us; the launch traced here: 99.5 us
  starting transfers between devices  41.7 us (42%)
  waiting for transfers between devices  38.1 us (38%)
  Pallas kernels  15.5 us (16%)
  other arithmetic  2.81 us (3%)
  between operations  1.13 us (1%)
    ppermute x29, starting transfers between devices, swapped(): return lax.ppermute(block, axis, route)  33.9 us
    ppermute x29, waiting for transfers between devices, swapped(): return lax.ppermute(block, axis, route)  33.6 us
    ppermute x5, starting transfers between devices, from_next(): return lax.ppermute(block, 'section', route)  6.48 us
    ppermute x5, waiting for transfers between devices, from_next(): return lax.ppermute(block, 'section', route)  4.51 us
    pallas_call x1, Pallas kernels, project_down(): pl.pallas_call(functools.partial(project_down_kernel, steps), in_specs=[i...  3.87 us
    pallas_call x2, Pallas kernels, place(): pl.pallas_call(functools.partial(place_kernel, layout, not before), in_sp...  3.56 us
    pallas_call x2, Pallas kernels, update(): pl.pallas_call(functools.partial(update_kernel, which), in_specs=[in_vmem...  2.45 us
  transfers between devices with their start and end apart: 35, of which 20 were waited for; matrix products, arithmetic and copies ran while one was open for 2% of the time, Pallas kernels for 12%

profile of v13, /device:TPU:0, one launch (start us, length us, event | category | flops | bytes accessed | tf_op | source)
XLA Modules:
  0.0 99.5 jit_solution(3538010454263349125)
XLA Ops:
  0.6 1.0 fusion.6
  1.6 3.0 %collective-permute-start = (bf16[64,768]{1,0:T(8,128)(2,1)S(1)}, bf16[64,768]{1,0:T(8,128)(2,1)S(1)}, u32[]{:S(2)}, u32[]{:S(2)}) collective-permute-start(bf16[64,768]{1,0:T(8,128)(2,1)S(1)} %fusion.6), channel_id=1, source_target_pairs={{4,0},{0,4},{5,1},{1,5},{6,2},{2,6},{7,3},{3,7},{12,8},{8,12},{13,... | collective-permute-start | bytes 294920 | tf_op jit(solution)/shard_map/ppermute | solution.py:480
  4.6 1.0 %convert_bitcast_fusion = (bf16[64,768]{1,0:T(8,128)(2,1)S(1)}, bf16[64,768]{1,0:T(8,128)(2,1)S(1)}) fusion(f32[1,64,768]{2,1,0:T(8,128)} %refs_0_.3, f32[1,64,768]{2,1,0:T(8,128)} %refs_0_.2), kind=kLoop, calls=%fused_computation.29 | loop fusion | flops 98304 | bytes 589824 | tf_op jit(solution)/shard_map/convert.5
  5.7 3.9 %project_down.1 = (f32[128,128]{1,0:T(8,128)S(1)}, f32[128,128]{1,0:T(8,128)S(1)}, bf16[128,12288]{1,0:T(8,128)(2,1)S(1)}) custom-call(bf16[128,12288]{1,0:T(8,128)(2,1)} %bitcast.53, bf16[2,64,12288]{2,1,0:T(8,128)(2,1)} %bitcast.54), custom_call_target="tpu_custom_call" | custom-call | flops 402653184 | bytes 6291456 | tf_op jit(solution)/shard_map/project_down/pallas_call | solution.py:106
  9.8 0.7 collective-permute-start.4
  10.5 0.9 collective-permute-start.3
  11.7 1.8 %project_up.1.refs_0_ = f32[128,384]{1,0:T(8,128)S(1)} custom-call(s32[1,4]{1,0:T(1,128)S(1)} %bitcast.51, f32[128,128]{1,0:T(8,128)S(1)} %get-tuple-element.43.by_down, bf16[128,12288]{1,0:T(8,128)(2,1)S(1)} %get-tuple-element.47.h_ref, bf16[128,12288]{1,0:T(8,128)(2,1)S(1)} %bitcast.45, bf16[2,64,12288]{2,1,0:T(8,128)(2,1)S(1)} %bitcast.50), custom_call_target="tpu_custom_call" | custom-call | flops 805306368 | bytes 9437184 | tf_op jit(solution)/shard_map/project_up/pallas_call | solution.py:141
  13.9 0.9 collective-permute-done.3
  14.8 1.6 %collective-permute-start.5 = (f32[64,128]{1,0:T(8,128)S(1)}, f32[64,128]{1,0:T(8,128)S(1)}, u32[]{:S(2)}, u32[]{:S(2)}) collective-permute-start(f32[64,128]{1,0:T(8,128)S(1)} %add_add_fusion), channel_id=1, source_target_pairs={{0,1},{1,0},{2,3},{3,2},{4,5},{5,4},{6,7},{7,6},{8,9},{9,8},{10,11... | collective-permute-start | bytes 98312 | tf_op jit(solution)/shard_map/ppermute | solution.py:470
  16.4 2.3 %collective-permute-done.5 = f32[64,128]{1,0:T(8,128)S(1)} collective-permute-done((f32[64,128]{1,0:T(8,128)S(1)}, f32[64,128]{1,0:T(8,128)S(1)}, u32[]{:S(2)}, u32[]{:S(2)}) %collective-permute-start.5) | collective-permute-done | bytes 32800 | tf_op jit(solution)/shard_map/ppermute | solution.py:470
  18.8 2.6 %collective-permute-start.6 = (f32[64,128]{1,0:T(8,128)S(1)}, f32[64,128]{1,0:T(8,128)S(1)}, u32[]{:S(2)}, u32[]{:S(2)}) collective-permute-start(f32[64,128]{1,0:T(8,128)S(1)} %add.74.refs_2_), channel_id=1, source_target_pairs={{0,2},{1,3},{2,0},{3,1},{4,6},{5,7},{6,4},{7,5},{8,10},{9,11},{10,... | collective-permute-start | bytes 98312 | tf_op jit(solution)/shard_map/ppermute | solution.py:470
  21.4 2.2 %collective-permute-done.6.refs_3_ = f32[64,128]{1,0:T(8,128)S(1)} collective-permute-done((f32[64,128]{1,0:T(8,128)S(1)}, f32[64,128]{1,0:T(8,128)S(1)}, u32[]{:S(2)}, u32[]{:S(2)}) %collective-permute-start.6) | collective-permute-done | bytes 32800 | tf_op jit(solution)/shard_map/ppermute | solution.py:470
  23.6 1.6 %chain.1 = (bf16[128,256]{1,0:T(8,128)(2,1)S(1)}, f32[128,128]{1,0:T(8,128)S(1)}) custom-call(s32[4,3]{1,0:T(4,128)S(1)} %copy-done.8, s32[1,4]{1,0:T(1,128)S(1)} %bitcast.52, f32[128,384]{1,0:T(8,128)S(1)} %project_up.1.refs_0_, f32[128,384]{1,0:T(8,128)S(1)} %collective-permute-done.1.refs_1_, f32[64,128]{1,0:T(8,128)S(1)} %add.74.refs_2_, ...), custom_call_target="tpu_custom_call" | custom-call | tf_op jit(solution)/shard_map/chain/pallas_call | solution.py:314
  27.4 0.6 collective-permute-done.8
  28.3 1.6 %collective-permute-start.10 = (bf16[4,64,768]{2,1,0:T(8,128)(2,1)S(1)}, bf16[4,64,768]{2,1,0:T(8,128)(2,1)S(1)}, u32[]{:S(2)}, u32[]{:S(2)}) collective-permute-start(bf16[4,64,768]{2,1,0:T(8,128)(2,1)S(1)} %get-tuple-element.80), channel_id=1, source_target_pairs={{0,1},{1,0},{2,3},{3,2},{4,5},{5,4},{6,7},{7,6},{8,9},{9,8},{10,11... | collective-permute-start | bytes 1179656 | tf_op jit(solution)/shard_map/ppermute | solution.py:470
  29.9 0.9 collective-permute-start.9
  30.8 2.9 %collective-permute-start.12 = (bf16[128,128]{1,0:T(8,128)(2,1)S(1)}, bf16[128,128]{1,0:T(8,128)(2,1)S(1)}, u32[]{:S(2)}, u32[]{:S(2)}) collective-permute-start(bf16[128,128]{1,0:T(8,128)(2,1)S(1)} %fusion.7), channel_id=1, source_target_pairs={{0,2},{1,3},{2,0},{3,1},{4,6},{5,7},{6,4},{7,5},{8,10},{9,11},{10,... | collective-permute-start | bytes 98312 | tf_op jit(solution)/shard_map/ppermute | solution.py:470
  34.3 5.0 %collective-permute-done.12 = bf16[128,128]{1,0:T(8,128)(2,1)S(1)} collective-permute-done((bf16[128,128]{1,0:T(8,128)(2,1)S(1)}, bf16[128,128]{1,0:T(8,128)(2,1)S(1)}, u32[]{:S(2)}, u32[]{:S(2)}) %collective-permute-start.12) | collective-permute-done | bytes 32800 | tf_op jit(solution)/shard_map/ppermute | solution.py:470
  39.3 0.9 collective-permute-done.10.one
  41.0 0.9 collective-permute-start.18
  41.9 2.1 %collective-permute-start.15 = (bf16[128,128]{1,0:T(8,128)(2,1)S(1)}, bf16[128,128]{1,0:T(8,128)(2,1)S(1)}, u32[]{:S(2)}, u32[]{:S(2)}) collective-permute-start(bf16[128,128]{1,0:T(8,128)(2,1)S(1)} %convert_element_type.151), channel_id=1, source_target_pairs={{0,1},{1,0},{2,3},{3,2},{4,5},{5,4},{6,7},{7,6},{8,9},{9,8},{10,11... | collective-permute-start | bytes 98312 | tf_op jit(solution)/shard_map/ppermute | solution.py:470
  44.1 2.7 %collective-permute-done.18.two = bf16[2,64,768]{2,1,0:T(8,128)(2,1)S(1)} collective-permute-done((bf16[2,64,768]{2,1,0:T(8,128)(2,1)S(1)}, bf16[2,64,768]{2,1,0:T(8,128)(2,1)S(1)}, u32[]{:S(2)}, u32[]{:S(2)}) %collective-permute-start.18) | collective-permute-done | bytes 196640 | tf_op jit(solution)/shard_map/ppermute | solution.py:470
  46.9 2.9 %collective-permute-start.19 = (bf16[64,768]{1,0:T(8,128)(2,1)S(1)}, bf16[64,768]{1,0:T(8,128)(2,1)S(1)}, u32[]{:S(2)}, u32[]{:S(2)}) collective-permute-start(bf16[64,768]{1,0:T(8,128)(2,1)S(1)} %fusion.4), channel_id=1, source_target_pairs={{0,2},{1,3},{2,0},{3,1},{4,6},{5,7},{6,4},{7,5},{8,10},{9,11},{10,... | collective-permute-start | bytes 294920 | tf_op jit(solution)/shard_map/ppermute | solution.py:470
  49.8 1.0 collective-permute-done.13.two
  50.8 1.7 %collective-permute-start.14 = (bf16[64,768]{1,0:T(8,128)(2,1)S(1)}, bf16[64,768]{1,0:T(8,128)(2,1)S(1)}, u32[]{:S(2)}, u32[]{:S(2)}) collective-permute-start(bf16[64,768]{1,0:T(8,128)(2,1)S(1)} %fusion.5), channel_id=1, source_target_pairs={{0,2},{1,3},{2,0},{3,1},{4,6},{5,7},{6,4},{7,5},{8,10},{9,11},{10,... | collective-permute-start | bytes 294920 | tf_op jit(solution)/shard_map/ppermute | solution.py:470
  52.5 1.6 %collective-permute-start.16 = (bf16[128,128]{1,0:T(8,128)(2,1)S(1)}, bf16[128,128]{1,0:T(8,128)(2,1)S(1)}, u32[]{:S(2)}, u32[]{:S(2)}) collective-permute-start(bf16[128,128]{1,0:T(8,128)(2,1)S(1)} %get-tuple-element.76), channel_id=1, source_target_pairs={{0,16},{8,24},{16,0},{24,8},{1,17},{9,25},{17,1},{25,9},{2,18},{10... | collective-permute-start | bytes 98312 | tf_op jit(solution)/shard_map/ppermute | solution.py:470
  54.1 2.4 %collective-permute-done.16.other_ref = bf16[128,128]{1,0:T(8,128)(2,1)S(1)} collective-permute-done((bf16[128,128]{1,0:T(8,128)(2,1)S(1)}, bf16[128,128]{1,0:T(8,128)(2,1)S(1)}, u32[]{:S(2)}, u32[]{:S(2)}) %collective-permute-start.16) | collective-permute-done | bytes 32800 | tf_op jit(solution)/shard_map/ppermute | solution.py:470
  57.1 1.2 %update.3 = (f32[1,64,768]{2,1,0:T(8,128)}, f32[1,64,768]{2,1,0:T(8,128)}, f32[1,64,768]{2,1,0:T(8,128)}, bf16[1,64,768]{2,1,0:T(8,128)(2,1)S(1)}) custom-call(bf16[2,4,64,768]{3,2,1,0:T(8,128)(2,1)S(1)} %gradient.4.kept, bf16[2,4,64,768]{3,2,1,0:T(8,128)(2,1)S(1)} %collective-permute-done.7.near, bf16[4,64,768]{2,1,0:T(8,128)(2,1)S(1)} %collective-permute-done.10.one, ...), custom_call_target="tpu_custom_call" | custom-call | tf_op jit(solution)/shard_map/update/pallas_call | solution.py:390
  58.3 0.8 collective-permute-start.20
  59.0 0.8 collective-permute-done.14.last
  59.9 1.2 %update.2 = (f32[1,64,768]{2,1,0:T(8,128)}, f32[1,64,768]{2,1,0:T(8,128)}, f32[1,64,768]{2,1,0:T(8,128)}, bf16[1,64,768]{2,1,0:T(8,128)(2,1)S(1)}) custom-call(bf16[2,4,64,768]{3,2,1,0:T(8,128)(2,1)S(1)} %gradient.4.kept, bf16[2,4,64,768]{3,2,1,0:T(8,128)(2,1)S(1)} %collective-permute-done.7.near, bf16[4,64,768]{2,1,0:T(8,128)(2,1)S(1)} %collective-permute-done.9.one, ...), custom_call_target="tpu_custom_call" | custom-call | tf_op jit(solution)/shard_map/update/pallas_call | solution.py:390
  61.1 1.3 %collective-permute-start.17 = (bf16[1,64,768]{2,1,0:T(8,128)(2,1)S(1)}, bf16[1,64,768]{2,1,0:T(8,128)(2,1)S(1)}, u32[]{:S(2)}, u32[]{:S(2)}) collective-permute-start(bf16[1,64,768]{2,1,0:T(8,128)(2,1)S(1)} %get-tuple-element.60), channel_id=1, source_target_pairs={{0,2},{1,3},{2,0},{3,1},{4,6},{5,7},{6,4},{7,5},{8,10},{9,11},{10,... | collective-permute-start | bytes 294920 | tf_op jit(solution)/shard_map/ppermute | solution.py:470
  62.5 1.8 %collective-permute-start.21 = (bf16[2,64,768]{2,1,0:T(8,128)(2,1)S(1)}, bf16[2,64,768]{2,1,0:T(8,128)(2,1)S(1)}, u32[]{:S(2)}, u32[]{:S(2)}) collective-permute-start(bf16[2,64,768]{2,1,0:T(8,128)(2,1)S(1)} %pad_maximum_fusion.6), channel_id=1, source_target_pairs={{4,0},{0,4},{5,1},{1,5},{6,2},{2,6},{7,3},{3,7},{12,8},{8,12},{13,... | collective-permute-start | bytes 589832 | tf_op jit(solution)/shard_map/ppermute | solution.py:480
  64.3 1.7 %collective-permute-done.20 = bf16[1,64,768]{2,1,0:T(8,128)(2,1)S(1)} collective-permute-done((bf16[1,64,768]{2,1,0:T(8,128)(2,1)S(1)}, bf16[1,64,768]{2,1,0:T(8,128)(2,1)S(1)}, u32[]{:S(2)}, u32[]{:S(2)}) %collective-permute-start.20) | collective-permute-done | bytes 98336 | tf_op jit(solution)/shard_map/ppermute | solution.py:470
  66.1 0.9 collective-permute-done.17
  67.1 3.4 %collective-permute-start.23 = (bf16[2,64,768]{2,1,0:T(8,128)(2,1)S(1)}, bf16[2,64,768]{2,1,0:T(8,128)(2,1)S(1)}, u32[]{:S(2)}, u32[]{:S(2)}) collective-permute-start(bf16[2,64,768]{2,1,0:T(8,128)(2,1)S(1)} %pad_maximum_fusion.8), channel_id=1, source_target_pairs={{0,1},{1,0},{2,3},{3,2},{4,5},{5,4},{6,7},{7,6},{8,9},{9,8},{10,11... | collective-permute-start | bytes 589832 | tf_op jit(solution)/shard_map/ppermute | solution.py:470
  70.4 1.3 %collective-permute-start.22 = (bf16[2,64,768]{2,1,0:T(8,128)(2,1)S(1)}, bf16[2,64,768]{2,1,0:T(8,128)(2,1)S(1)}, u32[]{:S(2)}, u32[]{:S(2)}) collective-permute-start(bf16[2,64,768]{2,1,0:T(8,128)(2,1)S(1)} %pad_maximum_fusion.7), channel_id=1, source_target_pairs={{4,0},{0,4},{5,1},{1,5},{6,2},{2,6},{7,3},{3,7},{12,8},{8,12},{13,... | collective-permute-start | bytes 589832 | tf_op jit(solution)/shard_map/ppermute | solution.py:480
  71.8 2.7 %collective-permute-done.23 = bf16[2,64,768]{2,1,0:T(8,128)(2,1)S(1)} collective-permute-done((bf16[2,64,768]{2,1,0:T(8,128)(2,1)S(1)}, bf16[2,64,768]{2,1,0:T(8,128)(2,1)S(1)}, u32[]{:S(2)}, u32[]{:S(2)}) %collective-permute-start.23) | collective-permute-done | bytes 196640 | tf_op jit(solution)/shard_map/ppermute | solution.py:470
  74.7 1.5 %collective-permute-start.24 = (bf16[4,64,768]{2,1,0:T(8,128)(2,1)S(1)}, bf16[4,64,768]{2,1,0:T(8,128)(2,1)S(1)}, u32[]{:S(2)}, u32[]{:S(2)}) collective-permute-start(bf16[4,64,768]{2,1,0:T(8,128)(2,1)S(1)} %get-tuple-element.89), channel_id=1, source_target_pairs={{0,16},{8,24},{16,0},{24,8},{1,17},{9,25},{17,1},{25,9},{2,18},{10... | collective-permute-start | bytes 1179656 | tf_op jit(solution)/shard_map/ppermute | solution.py:470
  76.2 2.5 %collective-permute-start.26 = (bf16[4,64,768]{2,1,0:T(8,128)(2,1)S(1)}, bf16[4,64,768]{2,1,0:T(8,128)(2,1)S(1)}, u32[]{:S(2)}, u32[]{:S(2)}) collective-permute-start(bf16[4,64,768]{2,1,0:T(8,128)(2,1)S(1)} %get-tuple-element.90), channel_id=1, source_target_pairs={{0,1},{1,0},{2,3},{3,2},{4,5},{5,4},{6,7},{7,6},{8,9},{9,8},{10,11... | collective-permute-start | bytes 1179656 | tf_op jit(solution)/shard_map/ppermute | solution.py:470
  78.9 4.5 %collective-permute-done.27 = bf16[4,64,768]{2,1,0:T(8,128)(2,1)S(1)} collective-permute-done((bf16[4,64,768]{2,1,0:T(8,128)(2,1)S(1)}, bf16[4,64,768]{2,1,0:T(8,128)(2,1)S(1)}, u32[]{:S(2)}, u32[]{:S(2)}) %collective-permute-start.27) | collective-permute-done | bytes 393248 | tf_op jit(solution)/shard_map/ppermute | solution.py:480
  83.4 2.1 %collective-permute-done.26 = bf16[4,64,768]{2,1,0:T(8,128)(2,1)S(1)} collective-permute-done((bf16[4,64,768]{2,1,0:T(8,128)(2,1)S(1)}, bf16[4,64,768]{2,1,0:T(8,128)(2,1)S(1)}, u32[]{:S(2)}, u32[]{:S(2)}) %collective-permute-start.26) | collective-permute-done | bytes 393248 | tf_op jit(solution)/shard_map/ppermute | solution.py:470
  85.5 1.3 %collective-permute-start.30 = (bf16[2,64,768]{2,1,0:T(8,128)(2,1)S(1)}, bf16[2,64,768]{2,1,0:T(8,128)(2,1)S(1)}, u32[]{:S(2)}, u32[]{:S(2)}) collective-permute-start(bf16[2,64,768]{2,1,0:T(8,128)(2,1)S(1)} %pad_maximum_fusion.10), channel_id=1, source_target_pairs={{4,0},{5,1},{6,2},{7,3},{12,8},{13,9},{14,10},{15,11},{20,16},{21,... | collective-permute-start | bytes 589832 | tf_op jit(solution)/shard_map/ppermute | solution.py:485
  87.0 2.5 %collective-permute-start.29 = (bf16[3,64,768]{2,1,0:T(8,128)(2,1)S(1)}, bf16[3,64,768]{2,1,0:T(8,128)(2,1)S(1)}, u32[]{:S(2)}, u32[]{:S(2)}) collective-permute-start(bf16[3,64,768]{2,1,0:T(8,128)(2,1)S(1)} %pad_maximum_fusion.4), channel_id=1, source_target_pairs={{0,1},{1,0},{2,3},{3,2},{4,5},{5,4},{6,7},{7,6},{8,9},{9,8},{10,11... | collective-permute-start | bytes 884744 | tf_op jit(solution)/shard_map/ppermute | solution.py:470
  89.7 3.9 %collective-permute-done.28 = bf16[3,64,768]{2,1,0:T(8,128)(2,1)S(1)} collective-permute-done((bf16[3,64,768]{2,1,0:T(8,128)(2,1)S(1)}, bf16[3,64,768]{2,1,0:T(8,128)(2,1)S(1)}, u32[]{:S(2)}, u32[]{:S(2)}) %collective-permute-start.28) | collective-permute-done | bytes 294944 | tf_op jit(solution)/shard_map/ppermute | solution.py:470
  94.4 1.5 %collective-permute-done.34.refs_5_ = bf16[8,64,768]{2,1,0:T(8,128)(2,1)S(1)} collective-permute-done((bf16[8,64,768]{2,1,0:T(8,128)(2,1)S(1)}, bf16[8,64,768]{2,1,0:T(8,128)(2,1)S(1)}, u32[]{:S(2)}, u32[]{:S(2)}) %collective-permute-start.34) | collective-permute-done | bytes 786464 | tf_op jit(solution)/shard_map/ppermute | solution.py:470
  96.0 2.3 %place.2 = (bf16[2,64,12288]{2,1,0:T(8,128)(2,1)}, bf16[2,64,12288]{2,1,0:T(8,128)(2,1)}) custom-call(s32[4,3]{1,0:T(4,128)S(1)} %copy-done.8, bf16[8,64,768]{2,1,0:T(8,128)(2,1)S(1)} %constant_dynamic-update-slice_fusion.3.refs_0_, bf16[8,64,768]{2,1,0:T(8,128)(2,1)S(1)} %collective-permute-done.32.refs_1_, ...), custom_call_target="tpu_custom_call" | custom-call | bytes 9437184 | tf_op jit(solution)/shard_map/place/pallas_call | solution.py:451
  98.3 1.3 %place.3 = (bf16[2,64,12288]{2,1,0:T(8,128)(2,1)}, bf16[2,64,12288]{2,1,0:T(8,128)(2,1)}) custom-call(s32[4,3]{1,0:T(4,128)S(1)} %copy-done.8, bf16[8,64,768]{2,1,0:T(8,128)(2,1)S(1)} %constant_dynamic-update-slice_fusion.refs_0_, bf16[8,64,768]{2,1,0:T(8,128)(2,1)S(1)} %collective-permute-done.31.refs_1_, ...), custom_call_target="tpu_custom_call", output_to_operand_aliasing={{0}: (3, {}), {1}: (4, {})} | custom-call | bytes 3145728 | tf_op jit(solution)/shard_map/place/pallas_call | solution.py:451
  (95 shorter events, 6.9 us)
Async XLA Ops:
  1.6 8.0 %collective-permute-start = (bf16[64,768]{1,0:T(8,128)(2,1)S(1)}, bf16[64,768]{1,0:T(8,128)(2,1)S(1)}, u32[]{:S(2)}, u32[]{:S(2)}) collective-permute-start(bf16[64,768]{1,0:T(8,128)(2,1)S(1)} %fusion.6), channel_id=1, source_target_pairs={{4,0},{0,4},{5,1},{1,5},{6,2},{2,6},{7,3},{3,7},{12,8},{8,12},{13,... | collective-permute-start | bytes 294920 | tf_op jit(solution)/shard_map/ppermute | solution.py:480
  5.7 6.1 %copy-start = (bf16[1,4,32,12288]{3,2,1,0:T(8,128)(2,1)S(1)}, bf16[1,4,32,12288]{3,2,1,0:T(8,128)(2,1)}, u32[]{:S(2)}) copy-start(bf16[1,4,32,12288]{3,2,1,0:T(8,128)(2,1)} %param.13) | copy-start | bytes 9437188
  5.7 6.0 %copy-start.1 = (bf16[1,1,2,64,12288]{4,3,2,1,0:T(8,128)(2,1)S(1)}, bf16[1,1,2,64,12288]{4,3,2,1,0:T(8,128)(2,1)}, u32[]{:S(2)}) copy-start(bf16[1,1,2,64,12288]{4,3,2,1,0:T(8,128)(2,1)} %param.17) | copy-start | bytes 9437188
  5.7 6.0 %copy-start.9 = (s32[4]{0:T(128)S(1)}, s32[4]{0:T(128)}, u32[]{:S(2)}) copy-start(s32[4]{0:T(128)} %param.14) | copy-start | bytes 52
  9.8 4.1 %collective-permute-start.4 = (f32[64,128]{1,0:T(8,128)S(1)}, f32[64,128]{1,0:T(8,128)S(1)}, u32[]{:S(2)}, u32[]{:S(2)}) collective-permute-start(f32[64,128]{1,0:T(8,128)S(1)} %get-tuple-element.48), channel_id=1, source_target_pairs={{0,24},{8,16},{16,8},{24,0},{1,25},{9,17},{17,9},{25,1},{2,26},{10... | collective-permute-start | bytes 98312 | tf_op jit(solution)/shard_map/ppermute | solution.py:470
  10.5 4.3 %collective-permute-start.3 = (f32[64,128]{1,0:T(8,128)S(1)}, f32[64,128]{1,0:T(8,128)S(1)}, u32[]{:S(2)}, u32[]{:S(2)}) collective-permute-start(f32[64,128]{1,0:T(8,128)S(1)} %get-tuple-element.48), channel_id=1, source_target_pairs={{0,16},{8,24},{16,0},{24,8},{1,17},{9,25},{17,1},{25,9},{2,18},{10... | collective-permute-start | bytes 98312 | tf_op jit(solution)/shard_map/ppermute | solution.py:470
  11.4 3.3 %collective-permute-start.2 = (f32[64,128]{1,0:T(8,128)S(1)}, f32[64,128]{1,0:T(8,128)S(1)}, u32[]{:S(2)}, u32[]{:S(2)}) collective-permute-start(f32[64,128]{1,0:T(8,128)S(1)} %get-tuple-element.48), channel_id=1, source_target_pairs={{0,8},{8,0},{16,24},{24,16},{1,9},{9,1},{17,25},{25,17},{2,10},{10... | collective-permute-start | bytes 98312 | tf_op jit(solution)/shard_map/ppermute | solution.py:470
  11.7 11.9 %copy-start.8 = (s32[4,3]{1,0:T(4,128)S(1)}, s32[4,3]{1,0:T(4,128)}, u32[]{:S(2)}) copy-start(s32[4,3]{1,0:T(4,128)} %bounds.5) | copy-start | bytes 148
  13.5 10.1 %collective-permute-start.1 = (f32[128,384]{1,0:T(8,128)S(1)}, f32[128,384]{1,0:T(8,128)S(1)}, u32[]{:S(2)}, u32[]{:S(2)}) collective-permute-start(f32[128,384]{1,0:T(8,128)S(1)} %project_up.1.refs_0_), channel_id=1, source_target_pairs={{4,0},{0,4},{5,1},{1,5},{6,2},{2,6},{7,3},{3,7},{12,8},{8,12},{13,... | collective-permute-start | bytes 589832 | tf_op jit(solution)/shard_map/ppermute | solution.py:480
  14.8 4.0 %collective-permute-start.5 = (f32[64,128]{1,0:T(8,128)S(1)}, f32[64,128]{1,0:T(8,128)S(1)}, u32[]{:S(2)}, u32[]{:S(2)}) collective-permute-start(f32[64,128]{1,0:T(8,128)S(1)} %add_add_fusion), channel_id=1, source_target_pairs={{0,1},{1,0},{2,3},{3,2},{4,5},{5,4},{6,7},{7,6},{8,9},{9,8},{10,11... | collective-permute-start | bytes 98312 | tf_op jit(solution)/shard_map/ppermute | solution.py:470
  18.8 4.8 %collective-permute-start.6 = (f32[64,128]{1,0:T(8,128)S(1)}, f32[64,128]{1,0:T(8,128)S(1)}, u32[]{:S(2)}, u32[]{:S(2)}) collective-permute-start(f32[64,128]{1,0:T(8,128)S(1)} %add.74.refs_2_), channel_id=1, source_target_pairs={{0,2},{1,3},{2,0},{3,1},{4,6},{5,7},{6,4},{7,5},{8,10},{9,11},{10,... | collective-permute-start | bytes 98312 | tf_op jit(solution)/shard_map/ppermute | solution.py:470
  25.7 2.4 %collective-permute-start.8 = (bf16[2,4,64,768]{3,2,1,0:T(8,128)(2,1)S(1)}, bf16[2,4,64,768]{3,2,1,0:T(8,128)(2,1)S(1)}, u32[]{:S(2)}, u32[]{:S(2)}) collective-permute-start(bf16[2,4,64,768]{3,2,1,0:T(8,128)(2,1)S(1)} %gradient.7), channel_id=1, source_target_pairs={{0,8},{8,0},{16,24},{24,16},{1,9},{9,1},{17,25},{25,17},{2,10},{10... | collective-permute-start | bytes 2359304 | tf_op jit(solution)/shard_map/ppermute | solution.py:470
  26.3 14.5 %collective-permute-start.7 = (bf16[2,4,64,768]{3,2,1,0:T(8,128)(2,1)S(1)}, bf16[2,4,64,768]{3,2,1,0:T(8,128)(2,1)S(1)}, u32[]{:S(2)}, u32[]{:S(2)}) collective-permute-start(bf16[2,4,64,768]{3,2,1,0:T(8,128)(2,1)S(1)} %gradient.5), channel_id=1, source_target_pairs={{0,8},{8,0},{16,24},{24,16},{1,9},{9,1},{17,25},{25,17},{2,10},{10... | collective-permute-start | bytes 2359304 | tf_op jit(solution)/shard_map/ppermute | solution.py:470
  26.9 3.9 %collective-permute-start.11 = (bf16[128,128]{1,0:T(8,128)(2,1)S(1)}, bf16[128,128]{1,0:T(8,128)(2,1)S(1)}, u32[]{:S(2)}, u32[]{:S(2)}) collective-permute-start(bf16[128,128]{1,0:T(8,128)(2,1)S(1)} %convert_element_type.136), channel_id=1, source_target_pairs={{0,8},{8,0},{16,24},{24,16},{1,9},{9,1},{17,25},{25,17},{2,10},{10... | collective-permute-start | bytes 98312 | tf_op jit(solution)/shard_map/ppermute | solution.py:470
  28.3 11.9 %collective-permute-start.10 = (bf16[4,64,768]{2,1,0:T(8,128)(2,1)S(1)}, bf16[4,64,768]{2,1,0:T(8,128)(2,1)S(1)}, u32[]{:S(2)}, u32[]{:S(2)}) collective-permute-start(bf16[4,64,768]{2,1,0:T(8,128)(2,1)S(1)} %get-tuple-element.80), channel_id=1, source_target_pairs={{0,1},{1,0},{2,3},{3,2},{4,5},{5,4},{6,7},{7,6},{8,9},{9,8},{10,11... | collective-permute-start | bytes 1179656 | tf_op jit(solution)/shard_map/ppermute | solution.py:470
  29.9 10.9 %collective-permute-start.9 = (bf16[4,64,768]{2,1,0:T(8,128)(2,1)S(1)}, bf16[4,64,768]{2,1,0:T(8,128)(2,1)S(1)}, u32[]{:S(2)}, u32[]{:S(2)}) collective-permute-start(bf16[4,64,768]{2,1,0:T(8,128)(2,1)S(1)} %get-tuple-element.81), channel_id=1, source_target_pairs={{0,16},{8,24},{16,0},{24,8},{1,17},{9,25},{17,1},{25,9},{2,18},{10... | collective-permute-start | bytes 1179656 | tf_op jit(solution)/shard_map/ppermute | solution.py:470
  30.8 8.5 %collective-permute-start.12 = (bf16[128,128]{1,0:T(8,128)(2,1)S(1)}, bf16[128,128]{1,0:T(8,128)(2,1)S(1)}, u32[]{:S(2)}, u32[]{:S(2)}) collective-permute-start(bf16[128,128]{1,0:T(8,128)(2,1)S(1)} %fusion.7), channel_id=1, source_target_pairs={{0,2},{1,3},{2,0},{3,1},{4,6},{5,7},{6,4},{7,5},{8,10},{9,11},{10,... | collective-permute-start | bytes 98312 | tf_op jit(solution)/shard_map/ppermute | solution.py:470
  34.2 22.8 %copy-start.2 = (f32[1,64,768]{2,1,0:T(8,128)S(1)}, f32[1,64,768]{2,1,0:T(8,128)}, u32[]{:S(2)}) copy-start(f32[1,64,768]{2,1,0:T(8,128)} %refs_0_.3) | copy-start | bytes 589828
  34.2 22.8 %copy-start.4 = (f32[1,64,768]{2,1,0:T(8,128)S(1)}, f32[1,64,768]{2,1,0:T(8,128)}, u32[]{:S(2)}) copy-start(f32[1,64,768]{2,1,0:T(8,128)} %refs_1_.3) | copy-start | bytes 589828
  34.2 22.8 %copy-start.5 = (f32[1,64,768]{2,1,0:T(8,128)S(1)}, f32[1,64,768]{2,1,0:T(8,128)}, u32[]{:S(2)}) copy-start(f32[1,64,768]{2,1,0:T(8,128)} %refs_2_.3) | copy-start | bytes 589828
  34.2 25.6 %copy-start.3 = (f32[1,64,768]{2,1,0:T(8,128)S(1)}, f32[1,64,768]{2,1,0:T(8,128)}, u32[]{:S(2)}) copy-start(f32[1,64,768]{2,1,0:T(8,128)} %refs_0_.2) | copy-start | bytes 589828
  34.3 25.6 %copy-start.6 = (f32[1,64,768]{2,1,0:T(8,128)S(1)}, f32[1,64,768]{2,1,0:T(8,128)}, u32[]{:S(2)}) copy-start(f32[1,64,768]{2,1,0:T(8,128)} %refs_1_.2) | copy-start | bytes 589828
  34.3 25.6 %copy-start.7 = (f32[1,64,768]{2,1,0:T(8,128)S(1)}, f32[1,64,768]{2,1,0:T(8,128)}, u32[]{:S(2)}) copy-start(f32[1,64,768]{2,1,0:T(8,128)} %refs_2_.2) | copy-start | bytes 589828
  41.0 5.9 %collective-permute-start.18 = (bf16[2,64,768]{2,1,0:T(8,128)(2,1)S(1)}, bf16[2,64,768]{2,1,0:T(8,128)(2,1)S(1)}, u32[]{:S(2)}, u32[]{:S(2)}) collective-permute-start(bf16[2,64,768]{2,1,0:T(8,128)(2,1)S(1)} %get-tuple-element.78), channel_id=1, source_target_pairs={{0,16},{8,24},{16,0},{24,8},{1,17},{9,25},{17,1},{25,9},{2,18},{10... | collective-permute-start | bytes 589832 | tf_op jit(solution)/shard_map/ppermute | solution.py:470
  41.9 10.6 %collective-permute-start.15 = (bf16[128,128]{1,0:T(8,128)(2,1)S(1)}, bf16[128,128]{1,0:T(8,128)(2,1)S(1)}, u32[]{:S(2)}, u32[]{:S(2)}) collective-permute-start(bf16[128,128]{1,0:T(8,128)(2,1)S(1)} %convert_element_type.151), channel_id=1, source_target_pairs={{0,1},{1,0},{2,3},{3,2},{4,5},{5,4},{6,7},{7,6},{8,9},{9,8},{10,11... | collective-permute-start | bytes 98312 | tf_op jit(solution)/shard_map/ppermute | solution.py:470
  44.0 6.7 %collective-permute-start.13 = (bf16[2,64,768]{2,1,0:T(8,128)(2,1)S(1)}, bf16[2,64,768]{2,1,0:T(8,128)(2,1)S(1)}, u32[]{:S(2)}, u32[]{:S(2)}) collective-permute-start(bf16[2,64,768]{2,1,0:T(8,128)(2,1)S(1)} %get-tuple-element.79), channel_id=1, source_target_pairs={{0,1},{1,0},{2,3},{3,2},{4,5},{5,4},{6,7},{7,6},{8,9},{9,8},{10,11... | collective-permute-start | bytes 589832 | tf_op jit(solution)/shard_map/ppermute | solution.py:470
  46.9 10.2 %collective-permute-start.19 = (bf16[64,768]{1,0:T(8,128)(2,1)S(1)}, bf16[64,768]{1,0:T(8,128)(2,1)S(1)}, u32[]{:S(2)}, u32[]{:S(2)}) collective-permute-start(bf16[64,768]{1,0:T(8,128)(2,1)S(1)} %fusion.4), channel_id=1, source_target_pairs={{0,2},{1,3},{2,0},{3,1},{4,6},{5,7},{6,4},{7,5},{8,10},{9,11},{10,... | collective-permute-start | bytes 294920 | tf_op jit(solution)/shard_map/ppermute | solution.py:470
  50.8 9.1 %collective-permute-start.14 = (bf16[64,768]{1,0:T(8,128)(2,1)S(1)}, bf16[64,768]{1,0:T(8,128)(2,1)S(1)}, u32[]{:S(2)}, u32[]{:S(2)}) collective-permute-start(bf16[64,768]{1,0:T(8,128)(2,1)S(1)} %fusion.5), channel_id=1, source_target_pairs={{0,2},{1,3},{2,0},{3,1},{4,6},{5,7},{6,4},{7,5},{8,10},{9,11},{10,... | collective-permute-start | bytes 294920 | tf_op jit(solution)/shard_map/ppermute | solution.py:470
  52.5 4.0 %collective-permute-start.16 = (bf16[128,128]{1,0:T(8,128)(2,1)S(1)}, bf16[128,128]{1,0:T(8,128)(2,1)S(1)}, u32[]{:S(2)}, u32[]{:S(2)}) collective-permute-start(bf16[128,128]{1,0:T(8,128)(2,1)S(1)} %get-tuple-element.76), channel_id=1, source_target_pairs={{0,16},{8,24},{16,0},{24,8},{1,17},{9,25},{17,1},{25,9},{2,18},{10... | collective-permute-start | bytes 98312 | tf_op jit(solution)/shard_map/ppermute | solution.py:470
  58.3 7.7 %collective-permute-start.20 = (bf16[1,64,768]{2,1,0:T(8,128)(2,1)S(1)}, bf16[1,64,768]{2,1,0:T(8,128)(2,1)S(1)}, u32[]{:S(2)}, u32[]{:S(2)}) collective-permute-start(bf16[1,64,768]{2,1,0:T(8,128)(2,1)S(1)} %get-tuple-element.61), channel_id=1, source_target_pairs={{0,2},{1,3},{2,0},{3,1},{4,6},{5,7},{6,4},{7,5},{8,10},{9,11},{10,... | collective-permute-start | bytes 294920 | tf_op jit(solution)/shard_map/ppermute | solution.py:470
  61.1 5.9 %collective-permute-start.17 = (bf16[1,64,768]{2,1,0:T(8,128)(2,1)S(1)}, bf16[1,64,768]{2,1,0:T(8,128)(2,1)S(1)}, u32[]{:S(2)}, u32[]{:S(2)}) collective-permute-start(bf16[1,64,768]{2,1,0:T(8,128)(2,1)S(1)} %get-tuple-element.60), channel_id=1, source_target_pairs={{0,2},{1,3},{2,0},{3,1},{4,6},{5,7},{6,4},{7,5},{8,10},{9,11},{10,... | collective-permute-start | bytes 294920 | tf_op jit(solution)/shard_map/ppermute | solution.py:470
  62.5 7.9 %collective-permute-start.21 = (bf16[2,64,768]{2,1,0:T(8,128)(2,1)S(1)}, bf16[2,64,768]{2,1,0:T(8,128)(2,1)S(1)}, u32[]{:S(2)}, u32[]{:S(2)}) collective-permute-start(bf16[2,64,768]{2,1,0:T(8,128)(2,1)S(1)} %pad_maximum_fusion.6), channel_id=1, source_target_pairs={{4,0},{0,4},{5,1},{1,5},{6,2},{2,6},{7,3},{3,7},{12,8},{8,12},{13,... | collective-permute-start | bytes 589832 | tf_op jit(solution)/shard_map/ppermute | solution.py:480
  66.0 5.8 %collective-permute-start.25 = (bf16[2,64,768]{2,1,0:T(8,128)(2,1)S(1)}, bf16[2,64,768]{2,1,0:T(8,128)(2,1)S(1)}, u32[]{:S(2)}, u32[]{:S(2)}) collective-permute-start(bf16[2,64,768]{2,1,0:T(8,128)(2,1)S(1)} %pad_maximum_fusion.9), channel_id=1, source_target_pairs={{0,16},{8,24},{16,0},{24,8},{1,17},{9,25},{17,1},{25,9},{2,18},{10... | collective-permute-start | bytes 589832 | tf_op jit(solution)/shard_map/ppermute | solution.py:470
  67.1 7.4 %collective-permute-start.23 = (bf16[2,64,768]{2,1,0:T(8,128)(2,1)S(1)}, bf16[2,64,768]{2,1,0:T(8,128)(2,1)S(1)}, u32[]{:S(2)}, u32[]{:S(2)}) collective-permute-start(bf16[2,64,768]{2,1,0:T(8,128)(2,1)S(1)} %pad_maximum_fusion.8), channel_id=1, source_target_pairs={{0,1},{1,0},{2,3},{3,2},{4,5},{5,4},{6,7},{7,6},{8,9},{9,8},{10,11... | collective-permute-start | bytes 589832 | tf_op jit(solution)/shard_map/ppermute | solution.py:470
  70.4 8.4 %collective-permute-start.22 = (bf16[2,64,768]{2,1,0:T(8,128)(2,1)S(1)}, bf16[2,64,768]{2,1,0:T(8,128)(2,1)S(1)}, u32[]{:S(2)}, u32[]{:S(2)}) collective-permute-start(bf16[2,64,768]{2,1,0:T(8,128)(2,1)S(1)} %pad_maximum_fusion.7), channel_id=1, source_target_pairs={{4,0},{0,4},{5,1},{1,5},{6,2},{2,6},{7,3},{3,7},{12,8},{8,12},{13,... | collective-permute-start | bytes 589832 | tf_op jit(solution)/shard_map/ppermute | solution.py:480
  74.6 8.8 %collective-permute-start.27 = (bf16[4,64,768]{2,1,0:T(8,128)(2,1)S(1)}, bf16[4,64,768]{2,1,0:T(8,128)(2,1)S(1)}, u32[]{:S(2)}, u32[]{:S(2)}) collective-permute-start(bf16[4,64,768]{2,1,0:T(8,128)(2,1)S(1)} %get-tuple-element.88), channel_id=1, source_target_pairs={{4,0},{0,4},{5,1},{1,5},{6,2},{2,6},{7,3},{3,7},{12,8},{8,12},{13,... | collective-permute-start | bytes 1179656 | tf_op jit(solution)/shard_map/ppermute | solution.py:480
  74.7 8.7 %collective-permute-start.24 = (bf16[4,64,768]{2,1,0:T(8,128)(2,1)S(1)}, bf16[4,64,768]{2,1,0:T(8,128)(2,1)S(1)}, u32[]{:S(2)}, u32[]{:S(2)}) collective-permute-start(bf16[4,64,768]{2,1,0:T(8,128)(2,1)S(1)} %get-tuple-element.89), channel_id=1, source_target_pairs={{0,16},{8,24},{16,0},{24,8},{1,17},{9,25},{17,1},{25,9},{2,18},{10... | collective-permute-start | bytes 1179656 | tf_op jit(solution)/shard_map/ppermute | solution.py:470
  76.2 9.3 %collective-permute-start.26 = (bf16[4,64,768]{2,1,0:T(8,128)(2,1)S(1)}, bf16[4,64,768]{2,1,0:T(8,128)(2,1)S(1)}, u32[]{:S(2)}, u32[]{:S(2)}) collective-permute-start(bf16[4,64,768]{2,1,0:T(8,128)(2,1)S(1)} %get-tuple-element.90), channel_id=1, source_target_pairs={{0,1},{1,0},{2,3},{3,2},{4,5},{5,4},{6,7},{7,6},{8,9},{9,8},{10,11... | collective-permute-start | bytes 1179656 | tf_op jit(solution)/shard_map/ppermute | solution.py:470
  78.7 15.7 %collective-permute-start.32 = (bf16[8,64,768]{2,1,0:T(8,128)(2,1)S(1)}, bf16[8,64,768]{2,1,0:T(8,128)(2,1)S(1)}, u32[]{:S(2)}, u32[]{:S(2)}) collective-permute-start(bf16[8,64,768]{2,1,0:T(8,128)(2,1)S(1)} %constant_dynamic-update-slice_fusion.3.refs_0_), channel_id=1, source_target_pairs={{0,8},{8,0},{16,24},{24,16},{1,9},{9,1},{17,25},{25,17},{2,10},{10... | collective-permute-start | bytes 2359304 | tf_op jit(solution)/shard_map/ppermute | solution.py:470
  85.5 8.7 %collective-permute-start.30 = (bf16[2,64,768]{2,1,0:T(8,128)(2,1)S(1)}, bf16[2,64,768]{2,1,0:T(8,128)(2,1)S(1)}, u32[]{:S(2)}, u32[]{:S(2)}) collective-permute-start(bf16[2,64,768]{2,1,0:T(8,128)(2,1)S(1)} %pad_maximum_fusion.10), channel_id=1, source_target_pairs={{4,0},{5,1},{6,2},{7,3},{12,8},{13,9},{14,10},{15,11},{20,16},{21,... | collective-permute-start | bytes 589832 | tf_op jit(solution)/shard_map/ppermute | solution.py:485
  86.9 6.8 %collective-permute-start.28 = (bf16[3,64,768]{2,1,0:T(8,128)(2,1)S(1)}, bf16[3,64,768]{2,1,0:T(8,128)(2,1)S(1)}, u32[]{:S(2)}, u32[]{:S(2)}) collective-permute-start(bf16[3,64,768]{2,1,0:T(8,128)(2,1)S(1)} %pad_maximum_fusion.3), channel_id=1, source_target_pairs={{0,16},{8,24},{16,0},{24,8},{1,17},{9,25},{17,1},{25,9},{2,18},{10... | collective-permute-start | bytes 884744 | tf_op jit(solution)/shard_map/ppermute | solution.py:470
  87.0 7.2 %collective-permute-start.29 = (bf16[3,64,768]{2,1,0:T(8,128)(2,1)S(1)}, bf16[3,64,768]{2,1,0:T(8,128)(2,1)S(1)}, u32[]{:S(2)}, u32[]{:S(2)}) collective-permute-start(bf16[3,64,768]{2,1,0:T(8,128)(2,1)S(1)} %pad_maximum_fusion.4), channel_id=1, source_target_pairs={{0,1},{1,0},{2,3},{3,2},{4,5},{5,4},{6,7},{7,6},{8,9},{9,8},{10,11... | collective-permute-start | bytes 884744 | tf_op jit(solution)/shard_map/ppermute | solution.py:470
  89.6 4.8 %collective-permute-start.33 = (bf16[8,64,768]{2,1,0:T(8,128)(2,1)S(1)}, bf16[8,64,768]{2,1,0:T(8,128)(2,1)S(1)}, u32[]{:S(2)}, u32[]{:S(2)}) collective-permute-start(bf16[8,64,768]{2,1,0:T(8,128)(2,1)S(1)} %constant_dynamic-update-slice_fusion.9.refs_2_), channel_id=1, source_target_pairs={{0,8},{8,0},{16,24},{24,16},{1,9},{9,1},{17,25},{25,17},{2,10},{10... | collective-permute-start | bytes 2359304 | tf_op jit(solution)/shard_map/ppermute | solution.py:470
  93.7 2.3 %collective-permute-start.34 = (bf16[8,64,768]{2,1,0:T(8,128)(2,1)S(1)}, bf16[8,64,768]{2,1,0:T(8,128)(2,1)S(1)}, u32[]{:S(2)}, u32[]{:S(2)}) collective-permute-start(bf16[8,64,768]{2,1,0:T(8,128)(2,1)S(1)} %constant_dynamic-update-slice_fusion.11.refs_4_), channel_id=1, source_target_pairs={{0,8},{8,0},{16,24},{24,16},{1,9},{9,1},{17,25},{25,17},{2,10},{10... | collective-permute-start | bytes 2359304 | tf_op jit(solution)/shard_map/ppermute | solution.py:470
  94.3 3.9 %collective-permute-start.31 = (bf16[8,64,768]{2,1,0:T(8,128)(2,1)S(1)}, bf16[8,64,768]{2,1,0:T(8,128)(2,1)S(1)}, u32[]{:S(2)}, u32[]{:S(2)}) collective-permute-start(bf16[8,64,768]{2,1,0:T(8,128)(2,1)S(1)} %constant_dynamic-update-slice_fusion.refs_0_), channel_id=1, source_target_pairs={{0,8},{8,0},{16,24},{24,16},{1,9},{9,1},{17,25},{25,17},{2,10},{10... | collective-permute-start | bytes 2359304 | tf_op jit(solution)/shard_map/ppermute | solution.py:470

commit v14 on v13

--- a/solution.py
+++ b/solution.py
@@ -568,16 +568,19 @@
     next_two = fetched(two, from_next)
     ends = joined(picked(down_three, 3), picked(up_three, 3))
     next_end = fetched(ends, following_layer)
-    _, _, next_array = lax.optimization_barrier((down_three[1], up_three[1], next_two[1]))
-    next_two = (next_two[0], next_array)
+    near = joined(own, one, two)
+    core_blocks, core_array = crossed(near, "replica", 1)
+    _, _, next_array, core_array = lax.optimization_barrier(
+        (down_three[1], up_three[1], next_two[1], core_array)
+    )
+    next_two, near_core = (next_two[0], next_array), (core_blocks, core_array)
     down_end = joined(picked(next_own, 0), picked(next_one, 0), picked(next_two, 0))
     up_end = joined(picked(next_own, 1), picked(next_one, 1), picked(next_two, 2))
     end = joined(crossed(down_end, "replica", 2), crossed(up_end, "tensor", 1), next_end)
-    near = joined(own, one, two)
     far = joined(down_three, up_three)
     next_near = joined(next_own, next_one, next_two)
-    near_core, far_core, next_core, end_core = (
-        crossed(piece, "replica", 1) for piece in (near, far, next_near, end)
+    far_core, next_core, end_core = (
+        crossed(piece, "replica", 1) for piece in (far, next_near, end)
     )
     placed = place(
         bounds, [near, near_core, far, far_core, next_near, next_core], [], slots, ranks, features

time: 100 us -> 102 us (1.020)
  waiting for transfers between devices: 38.1 us -> 40.4 us
    ppermute x29, waiting for transfers between devices: 33.6 us -> 40.2 us  [swapped(): return lax.ppermute(block, axis, route)]
    ppermute x5, waiting for transfers between devices: 4.51 us -> 0.18 us  [from_next(): return lax.ppermute(block, 'section', route)]
where the time goes in v14:
time: 102 us
  starting transfers between devices  41.6 us (41%)
  waiting for transfers between devices  40.4 us (40%)
  Pallas kernels  15.5 us (15%)
  other arithmetic  2.83 us (3%)
  between operations  1.08 us (1%)
    ppermute x29, waiting for transfers between devices, swapped(): return lax.ppermute(block, axis, route)  40.2 us
    ppermute x29, starting transfers between devices, swapped(): return lax.ppermute(block, axis, route)  33.7 us
    ppermute x5, starting transfers between devices, from_next(): return lax.ppermute(block, 'section', route)  6.61 us
    pallas_call x1, Pallas kernels, project_down(): pl.pallas_call(functools.partial(project_down_kernel, steps), in_specs=[i...  3.87 us
    pallas_call x2, Pallas kernels, place(): pl.pallas_call(functools.partial(place_kernel, layout, not before), in_sp...  3.57 us
    pallas_call x2, Pallas kernels, update(): pl.pallas_call(functools.partial(update_kernel, which), in_specs=[in_vmem...  2.45 us
  transfers between devices with their start and end apart: 35, of which 20 were waited for; matrix products, arithmetic and copies ran while one was open for 2% of the time, Pallas kernels for 12%

profile of v14, /device:TPU:0, one launch (start us, length us, event | category | flops | bytes accessed | tf_op | source)
XLA Modules:
  0.0 101.7 jit_solution(8468561132515575078)
XLA Ops:
  0.6 1.0 fusion.6
  1.6 3.0 %collective-permute-start = (bf16[64,768]{1,0:T(8,128)(2,1)S(1)}, bf16[64,768]{1,0:T(8,128)(2,1)S(1)}, u32[]{:S(2)}, u32[]{:S(2)}) collective-permute-start(bf16[64,768]{1,0:T(8,128)(2,1)S(1)} %fusion.6), channel_id=1, source_target_pairs={{4,0},{0,4},{5,1},{1,5},{6,2},{2,6},{7,3},{3,7},{12,8},{8,12},{13,... | collective-permute-start | bytes 294920 | tf_op jit(solution)/shard_map/ppermute | solution.py:480
  4.6 1.0 %convert_bitcast_fusion = (bf16[64,768]{1,0:T(8,128)(2,1)S(1)}, bf16[64,768]{1,0:T(8,128)(2,1)S(1)}) fusion(f32[1,64,768]{2,1,0:T(8,128)} %refs_0_.3, f32[1,64,768]{2,1,0:T(8,128)} %refs_0_.2), kind=kLoop, calls=%fused_computation.29 | loop fusion | flops 98304 | bytes 589824 | tf_op jit(solution)/shard_map/convert.5
  5.7 3.9 %project_down.1 = (f32[128,128]{1,0:T(8,128)S(1)}, f32[128,128]{1,0:T(8,128)S(1)}, bf16[128,12288]{1,0:T(8,128)(2,1)S(1)}) custom-call(bf16[128,12288]{1,0:T(8,128)(2,1)} %bitcast.53, bf16[2,64,12288]{2,1,0:T(8,128)(2,1)} %bitcast.54), custom_call_target="tpu_custom_call" | custom-call | flops 402653184 | bytes 6291456 | tf_op jit(solution)/shard_map/project_down/pallas_call | solution.py:106
  9.8 0.7 collective-permute-start.4
  10.5 0.9 collective-permute-start.3
  11.7 1.8 %project_up.1.refs_0_ = f32[128,384]{1,0:T(8,128)S(1)} custom-call(s32[1,4]{1,0:T(1,128)S(1)} %bitcast.51, f32[128,128]{1,0:T(8,128)S(1)} %get-tuple-element.44.by_down, bf16[128,12288]{1,0:T(8,128)(2,1)S(1)} %get-tuple-element.48.h_ref, bf16[128,12288]{1,0:T(8,128)(2,1)S(1)} %bitcast.45, bf16[2,64,12288]{2,1,0:T(8,128)(2,1)S(1)} %bitcast.50), custom_call_target="tpu_custom_call" | custom-call | flops 805306368 | bytes 9437184 | tf_op jit(solution)/shard_map/project_up/pallas_call | solution.py:141
  13.9 0.9 collective-permute-done.3
  14.8 1.6 %collective-permute-start.5 = (f32[64,128]{1,0:T(8,128)S(1)}, f32[64,128]{1,0:T(8,128)S(1)}, u32[]{:S(2)}, u32[]{:S(2)}) collective-permute-start(f32[64,128]{1,0:T(8,128)S(1)} %add_add_fusion), channel_id=1, source_target_pairs={{0,1},{1,0},{2,3},{3,2},{4,5},{5,4},{6,7},{7,6},{8,9},{9,8},{10,11... | collective-permute-start | bytes 98312 | tf_op jit(solution)/shard_map/ppermute | solution.py:470
  16.4 2.3 %collective-permute-done.5 = f32[64,128]{1,0:T(8,128)S(1)} collective-permute-done((f32[64,128]{1,0:T(8,128)S(1)}, f32[64,128]{1,0:T(8,128)S(1)}, u32[]{:S(2)}, u32[]{:S(2)}) %collective-permute-start.5) | collective-permute-done | bytes 32800 | tf_op jit(solution)/shard_map/ppermute | solution.py:470
  18.8 2.6 %collective-permute-start.6 = (f32[64,128]{1,0:T(8,128)S(1)}, f32[64,128]{1,0:T(8,128)S(1)}, u32[]{:S(2)}, u32[]{:S(2)}) collective-permute-start(f32[64,128]{1,0:T(8,128)S(1)} %add.74.refs_2_), channel_id=1, source_target_pairs={{0,2},{1,3},{2,0},{3,1},{4,6},{5,7},{6,4},{7,5},{8,10},{9,11},{10,... | collective-permute-start | bytes 98312 | tf_op jit(solution)/shard_map/ppermute | solution.py:470
  21.4 2.2 %collective-permute-done.6.refs_3_ = f32[64,128]{1,0:T(8,128)S(1)} collective-permute-done((f32[64,128]{1,0:T(8,128)S(1)}, f32[64,128]{1,0:T(8,128)S(1)}, u32[]{:S(2)}, u32[]{:S(2)}) %collective-permute-start.6) | collective-permute-done | bytes 32800 | tf_op jit(solution)/shard_map/ppermute | solution.py:470
  23.6 1.6 %chain.1 = (bf16[128,256]{1,0:T(8,128)(2,1)S(1)}, f32[128,128]{1,0:T(8,128)S(1)}) custom-call(s32[4,3]{1,0:T(4,128)S(1)} %copy-done.8, s32[1,4]{1,0:T(1,128)S(1)} %bitcast.52, f32[128,384]{1,0:T(8,128)S(1)} %project_up.1.refs_0_, f32[128,384]{1,0:T(8,128)S(1)} %collective-permute-done.1.refs_1_, f32[64,128]{1,0:T(8,128)S(1)} %add.74.refs_2_, ...), custom_call_target="tpu_custom_call" | custom-call | tf_op jit(solution)/shard_map/chain/pallas_call | solution.py:314
  28.3 1.6 %collective-permute-start.10 = (bf16[4,64,768]{2,1,0:T(8,128)(2,1)S(1)}, bf16[4,64,768]{2,1,0:T(8,128)(2,1)S(1)}, u32[]{:S(2)}, u32[]{:S(2)}) collective-permute-start(bf16[4,64,768]{2,1,0:T(8,128)(2,1)S(1)} %get-tuple-element.82), channel_id=1, source_target_pairs={{0,1},{1,0},{2,3},{3,2},{4,5},{5,4},{6,7},{7,6},{8,9},{9,8},{10,11... | collective-permute-start | bytes 1179656 | tf_op jit(solution)/shard_map/ppermute | solution.py:470
  29.9 0.9 collective-permute-start.9
  30.8 2.9 %collective-permute-start.12 = (bf16[128,128]{1,0:T(8,128)(2,1)S(1)}, bf16[128,128]{1,0:T(8,128)(2,1)S(1)}, u32[]{:S(2)}, u32[]{:S(2)}) collective-permute-start(bf16[128,128]{1,0:T(8,128)(2,1)S(1)} %fusion.7), channel_id=1, source_target_pairs={{0,2},{1,3},{2,0},{3,1},{4,6},{5,7},{6,4},{7,5},{8,10},{9,11},{10,... | collective-permute-start | bytes 98312 | tf_op jit(solution)/shard_map/ppermute | solution.py:470
  34.3 5.0 %collective-permute-done.12 = bf16[128,128]{1,0:T(8,128)(2,1)S(1)} collective-permute-done((bf16[128,128]{1,0:T(8,128)(2,1)S(1)}, bf16[128,128]{1,0:T(8,128)(2,1)S(1)}, u32[]{:S(2)}, u32[]{:S(2)}) %collective-permute-start.12) | collective-permute-done | bytes 32800 | tf_op jit(solution)/shard_map/ppermute | solution.py:470
  39.3 0.9 collective-permute-done.10.one
  41.0 0.9 collective-permute-start.18
  41.9 2.1 %collective-permute-start.15 = (bf16[128,128]{1,0:T(8,128)(2,1)S(1)}, bf16[128,128]{1,0:T(8,128)(2,1)S(1)}, u32[]{:S(2)}, u32[]{:S(2)}) collective-permute-start(bf16[128,128]{1,0:T(8,128)(2,1)S(1)} %convert_element_type.151), channel_id=1, source_target_pairs={{0,1},{1,0},{2,3},{3,2},{4,5},{5,4},{6,7},{7,6},{8,9},{9,8},{10,11... | collective-permute-start | bytes 98312 | tf_op jit(solution)/shard_map/ppermute | solution.py:470
  44.1 2.7 %collective-permute-done.18.two = bf16[2,64,768]{2,1,0:T(8,128)(2,1)S(1)} collective-permute-done((bf16[2,64,768]{2,1,0:T(8,128)(2,1)S(1)}, bf16[2,64,768]{2,1,0:T(8,128)(2,1)S(1)}, u32[]{:S(2)}, u32[]{:S(2)}) %collective-permute-start.18) | collective-permute-done | bytes 196640 | tf_op jit(solution)/shard_map/ppermute | solution.py:470
  46.9 2.9 %collective-permute-start.19 = (bf16[64,768]{1,0:T(8,128)(2,1)S(1)}, bf16[64,768]{1,0:T(8,128)(2,1)S(1)}, u32[]{:S(2)}, u32[]{:S(2)}) collective-permute-start(bf16[64,768]{1,0:T(8,128)(2,1)S(1)} %fusion.4), channel_id=1, source_target_pairs={{0,2},{1,3},{2,0},{3,1},{4,6},{5,7},{6,4},{7,5},{8,10},{9,11},{10,... | collective-permute-start | bytes 294920 | tf_op jit(solution)/shard_map/ppermute | solution.py:470
  49.8 1.0 collective-permute-done.13.two
  50.8 1.7 %collective-permute-start.14 = (bf16[64,768]{1,0:T(8,128)(2,1)S(1)}, bf16[64,768]{1,0:T(8,128)(2,1)S(1)}, u32[]{:S(2)}, u32[]{:S(2)}) collective-permute-start(bf16[64,768]{1,0:T(8,128)(2,1)S(1)} %fusion.5), channel_id=1, source_target_pairs={{0,2},{1,3},{2,0},{3,1},{4,6},{5,7},{6,4},{7,5},{8,10},{9,11},{10,... | collective-permute-start | bytes 294920 | tf_op jit(solution)/shard_map/ppermute | solution.py:470
  52.5 1.6 %collective-permute-start.16 = (bf16[128,128]{1,0:T(8,128)(2,1)S(1)}, bf16[128,128]{1,0:T(8,128)(2,1)S(1)}, u32[]{:S(2)}, u32[]{:S(2)}) collective-permute-start(bf16[128,128]{1,0:T(8,128)(2,1)S(1)} %get-tuple-element.78), channel_id=1, source_target_pairs={{0,16},{8,24},{16,0},{24,8},{1,17},{9,25},{17,1},{25,9},{2,18},{10... | collective-permute-start | bytes 98312 | tf_op jit(solution)/shard_map/ppermute | solution.py:470
  54.1 2.4 %collective-permute-done.16.other_ref = bf16[128,128]{1,0:T(8,128)(2,1)S(1)} collective-permute-done((bf16[128,128]{1,0:T(8,128)(2,1)S(1)}, bf16[128,128]{1,0:T(8,128)(2,1)S(1)}, u32[]{:S(2)}, u32[]{:S(2)}) %collective-permute-start.16) | collective-permute-done | bytes 32800 | tf_op jit(solution)/shard_map/ppermute | solution.py:470
  57.1 1.2 %update.3 = (f32[1,64,768]{2,1,0:T(8,128)}, f32[1,64,768]{2,1,0:T(8,128)}, f32[1,64,768]{2,1,0:T(8,128)}, bf16[1,64,768]{2,1,0:T(8,128)(2,1)S(1)}) custom-call(bf16[2,4,64,768]{3,2,1,0:T(8,128)(2,1)S(1)} %gradient.4.kept, bf16[2,4,64,768]{3,2,1,0:T(8,128)(2,1)S(1)} %collective-permute-done.7.near, bf16[4,64,768]{2,1,0:T(8,128)(2,1)S(1)} %collective-permute-done.10.one, ...), custom_call_target="tpu_custom_call" | custom-call | tf_op jit(solution)/shard_map/update/pallas_call | solution.py:390
  58.3 0.8 collective-permute-start.20
  59.0 0.8 collective-permute-done.14.last
  59.9 1.2 %update.2 = (f32[1,64,768]{2,1,0:T(8,128)}, f32[1,64,768]{2,1,0:T(8,128)}, f32[1,64,768]{2,1,0:T(8,128)}, bf16[1,64,768]{2,1,0:T(8,128)(2,1)S(1)}) custom-call(bf16[2,4,64,768]{3,2,1,0:T(8,128)(2,1)S(1)} %gradient.4.kept, bf16[2,4,64,768]{3,2,1,0:T(8,128)(2,1)S(1)} %collective-permute-done.7.near, bf16[4,64,768]{2,1,0:T(8,128)(2,1)S(1)} %collective-permute-done.9.one, ...), custom_call_target="tpu_custom_call" | custom-call | tf_op jit(solution)/shard_map/update/pallas_call | solution.py:390
  61.1 1.3 %collective-permute-start.17 = (bf16[1,64,768]{2,1,0:T(8,128)(2,1)S(1)}, bf16[1,64,768]{2,1,0:T(8,128)(2,1)S(1)}, u32[]{:S(2)}, u32[]{:S(2)}) collective-permute-start(bf16[1,64,768]{2,1,0:T(8,128)(2,1)S(1)} %get-tuple-element.61), channel_id=1, source_target_pairs={{0,2},{1,3},{2,0},{3,1},{4,6},{5,7},{6,4},{7,5},{8,10},{9,11},{10,... | collective-permute-start | bytes 294920 | tf_op jit(solution)/shard_map/ppermute | solution.py:470
  62.5 1.8 %collective-permute-start.21 = (bf16[2,64,768]{2,1,0:T(8,128)(2,1)S(1)}, bf16[2,64,768]{2,1,0:T(8,128)(2,1)S(1)}, u32[]{:S(2)}, u32[]{:S(2)}) collective-permute-start(bf16[2,64,768]{2,1,0:T(8,128)(2,1)S(1)} %pad_maximum_fusion.6), channel_id=1, source_target_pairs={{4,0},{0,4},{5,1},{1,5},{6,2},{2,6},{7,3},{3,7},{12,8},{8,12},{13,... | collective-permute-start | bytes 589832 | tf_op jit(solution)/shard_map/ppermute | solution.py:480
  64.3 1.7 %collective-permute-done.20 = bf16[1,64,768]{2,1,0:T(8,128)(2,1)S(1)} collective-permute-done((bf16[1,64,768]{2,1,0:T(8,128)(2,1)S(1)}, bf16[1,64,768]{2,1,0:T(8,128)(2,1)S(1)}, u32[]{:S(2)}, u32[]{:S(2)}) %collective-permute-start.20) | collective-permute-done | bytes 98336 | tf_op jit(solution)/shard_map/ppermute | solution.py:470
  66.1 0.9 collective-permute-done.17
  67.1 3.4 %collective-permute-start.23 = (bf16[2,64,768]{2,1,0:T(8,128)(2,1)S(1)}, bf16[2,64,768]{2,1,0:T(8,128)(2,1)S(1)}, u32[]{:S(2)}, u32[]{:S(2)}) collective-permute-start(bf16[2,64,768]{2,1,0:T(8,128)(2,1)S(1)} %pad_maximum_fusion.8), channel_id=1, source_target_pairs={{0,1},{1,0},{2,3},{3,2},{4,5},{5,4},{6,7},{7,6},{8,9},{9,8},{10,11... | collective-permute-start | bytes 589832 | tf_op jit(solution)/shard_map/ppermute | solution.py:470
  70.5 1.2 %collective-permute-start.22 = (bf16[2,64,768]{2,1,0:T(8,128)(2,1)S(1)}, bf16[2,64,768]{2,1,0:T(8,128)(2,1)S(1)}, u32[]{:S(2)}, u32[]{:S(2)}) collective-permute-start(bf16[2,64,768]{2,1,0:T(8,128)(2,1)S(1)} %pad_maximum_fusion.7), channel_id=1, source_target_pairs={{4,0},{0,4},{5,1},{1,5},{6,2},{2,6},{7,3},{3,7},{12,8},{8,12},{13,... | collective-permute-start | bytes 589832 | tf_op jit(solution)/shard_map/ppermute | solution.py:480
  71.7 2.3 %collective-permute-done.23 = bf16[2,64,768]{2,1,0:T(8,128)(2,1)S(1)} collective-permute-done((bf16[2,64,768]{2,1,0:T(8,128)(2,1)S(1)}, bf16[2,64,768]{2,1,0:T(8,128)(2,1)S(1)}, u32[]{:S(2)}, u32[]{:S(2)}) %collective-permute-start.23) | collective-permute-done | bytes 196640 | tf_op jit(solution)/shard_map/ppermute | solution.py:470
  74.3 0.9 collective-permute-start.24
  75.3 2.0 %collective-permute-start.26 = (bf16[4,64,768]{2,1,0:T(8,128)(2,1)S(1)}, bf16[4,64,768]{2,1,0:T(8,128)(2,1)S(1)}, u32[]{:S(2)}, u32[]{:S(2)}) collective-permute-start(bf16[4,64,768]{2,1,0:T(8,128)(2,1)S(1)} %get-tuple-element.92), channel_id=1, source_target_pairs={{0,1},{1,0},{2,3},{3,2},{4,5},{5,4},{6,7},{7,6},{8,9},{9,8},{10,11... | collective-permute-start | bytes 1179656 | tf_op jit(solution)/shard_map/ppermute | solution.py:470
  77.6 8.3 %collective-permute-done.24 = bf16[4,64,768]{2,1,0:T(8,128)(2,1)S(1)} collective-permute-done((bf16[4,64,768]{2,1,0:T(8,128)(2,1)S(1)}, bf16[4,64,768]{2,1,0:T(8,128)(2,1)S(1)}, u32[]{:S(2)}, u32[]{:S(2)}) %collective-permute-start.24) | collective-permute-done | bytes 393248 | tf_op jit(solution)/shard_map/ppermute | solution.py:470
  85.9 0.9 collective-permute-done.26
  86.8 1.3 %collective-permute-start.31 = (bf16[2,64,768]{2,1,0:T(8,128)(2,1)S(1)}, bf16[2,64,768]{2,1,0:T(8,128)(2,1)S(1)}, u32[]{:S(2)}, u32[]{:S(2)}) collective-permute-start(bf16[2,64,768]{2,1,0:T(8,128)(2,1)S(1)} %pad_maximum_fusion.10), channel_id=1, source_target_pairs={{4,0},{5,1},{6,2},{7,3},{12,8},{13,9},{14,10},{15,11},{20,16},{21,... | collective-permute-start | bytes 589832 | tf_op jit(solution)/shard_map/ppermute | solution.py:485
  88.4 1.2 %collective-permute-start.29 = (bf16[3,64,768]{2,1,0:T(8,128)(2,1)S(1)}, bf16[3,64,768]{2,1,0:T(8,128)(2,1)S(1)}, u32[]{:S(2)}, u32[]{:S(2)}) collective-permute-start(bf16[3,64,768]{2,1,0:T(8,128)(2,1)S(1)} %pad_maximum_fusion.3), channel_id=1, source_target_pairs={{0,16},{8,24},{16,0},{24,8},{1,17},{9,25},{17,1},{25,9},{2,18},{10... | collective-permute-start | bytes 884744 | tf_op jit(solution)/shard_map/ppermute | solution.py:470
  89.7 1.7 %collective-permute-start.30 = (bf16[3,64,768]{2,1,0:T(8,128)(2,1)S(1)}, bf16[3,64,768]{2,1,0:T(8,128)(2,1)S(1)}, u32[]{:S(2)}, u32[]{:S(2)}) collective-permute-start(bf16[3,64,768]{2,1,0:T(8,128)(2,1)S(1)} %pad_maximum_fusion.4), channel_id=1, source_target_pairs={{0,1},{1,0},{2,3},{3,2},{4,5},{5,4},{6,7},{7,6},{8,9},{9,8},{10,11... | collective-permute-start | bytes 884744 | tf_op jit(solution)/shard_map/ppermute | solution.py:470
  92.0 4.9 %collective-permute-done.29 = bf16[3,64,768]{2,1,0:T(8,128)(2,1)S(1)} collective-permute-done((bf16[3,64,768]{2,1,0:T(8,128)(2,1)S(1)}, bf16[3,64,768]{2,1,0:T(8,128)(2,1)S(1)}, u32[]{:S(2)}, u32[]{:S(2)}) %collective-permute-start.29) | collective-permute-done | bytes 294944 | tf_op jit(solution)/shard_map/ppermute | solution.py:470
  97.0 1.0 collective-permute-done.30
  98.1 2.3 %place.2 = (bf16[2,64,12288]{2,1,0:T(8,128)(2,1)}, bf16[2,64,12288]{2,1,0:T(8,128)(2,1)}) custom-call(s32[4,3]{1,0:T(4,128)S(1)} %copy-done.8, bf16[8,64,768]{2,1,0:T(8,128)(2,1)S(1)} %constant_dynamic-update-slice_fusion.refs_0_, bf16[8,64,768]{2,1,0:T(8,128)(2,1)S(1)} %collective-permute-done.28.refs_1_, ...), custom_call_target="tpu_custom_call" | custom-call | bytes 9437184 | tf_op jit(solution)/shard_map/place/pallas_call | solution.py:451
  100.4 1.3 %place.3 = (bf16[2,64,12288]{2,1,0:T(8,128)(2,1)}, bf16[2,64,12288]{2,1,0:T(8,128)(2,1)}) custom-call(s32[4,3]{1,0:T(4,128)S(1)} %copy-done.8, bf16[8,64,768]{2,1,0:T(8,128)(2,1)S(1)} %constant_dynamic-update-slice_fusion.6.refs_0_, bf16[8,64,768]{2,1,0:T(8,128)(2,1)S(1)} %collective-permute-done.32.refs_1_, ...), custom_call_target="tpu_custom_call", output_to_operand_aliasing={{0}: (3, {}), {1}: (4, {})} | custom-call | bytes 3145728 | tf_op jit(solution)/shard_map/place/pallas_call | solution.py:451
  (95 shorter events, 7.7 us)
Async XLA Ops:
  1.6 8.0 %collective-permute-start = (bf16[64,768]{1,0:T(8,128)(2,1)S(1)}, bf16[64,768]{1,0:T(8,128)(2,1)S(1)}, u32[]{:S(2)}, u32[]{:S(2)}) collective-permute-start(bf16[64,768]{1,0:T(8,128)(2,1)S(1)} %fusion.6), channel_id=1, source_target_pairs={{4,0},{0,4},{5,1},{1,5},{6,2},{2,6},{7,3},{3,7},{12,8},{8,12},{13,... | collective-permute-start | bytes 294920 | tf_op jit(solution)/shard_map/ppermute | solution.py:480
  5.7 6.1 %copy-start = (bf16[1,4,32,12288]{3,2,1,0:T(8,128)(2,1)S(1)}, bf16[1,4,32,12288]{3,2,1,0:T(8,128)(2,1)}, u32[]{:S(2)}) copy-start(bf16[1,4,32,12288]{3,2,1,0:T(8,128)(2,1)} %param.13) | copy-start | bytes 9437188
  5.7 6.0 %copy-start.1 = (bf16[1,1,2,64,12288]{4,3,2,1,0:T(8,128)(2,1)S(1)}, bf16[1,1,2,64,12288]{4,3,2,1,0:T(8,128)(2,1)}, u32[]{:S(2)}) copy-start(bf16[1,1,2,64,12288]{4,3,2,1,0:T(8,128)(2,1)} %param.17) | copy-start | bytes 9437188
  5.7 6.0 %copy-start.9 = (s32[4]{0:T(128)S(1)}, s32[4]{0:T(128)}, u32[]{:S(2)}) copy-start(s32[4]{0:T(128)} %param.14) | copy-start | bytes 52
  9.8 4.1 %collective-permute-start.4 = (f32[64,128]{1,0:T(8,128)S(1)}, f32[64,128]{1,0:T(8,128)S(1)}, u32[]{:S(2)}, u32[]{:S(2)}) collective-permute-start(f32[64,128]{1,0:T(8,128)S(1)} %get-tuple-element.49), channel_id=1, source_target_pairs={{0,24},{8,16},{16,8},{24,0},{1,25},{9,17},{17,9},{25,1},{2,26},{10... | collective-permute-start | bytes 98312 | tf_op jit(solution)/shard_map/ppermute | solution.py:470
  10.5 4.3 %collective-permute-start.3 = (f32[64,128]{1,0:T(8,128)S(1)}, f32[64,128]{1,0:T(8,128)S(1)}, u32[]{:S(2)}, u32[]{:S(2)}) collective-permute-start(f32[64,128]{1,0:T(8,128)S(1)} %get-tuple-element.49), channel_id=1, source_target_pairs={{0,16},{8,24},{16,0},{24,8},{1,17},{9,25},{17,1},{25,9},{2,18},{10... | collective-permute-start | bytes 98312 | tf_op jit(solution)/shard_map/ppermute | solution.py:470
  11.4 3.3 %collective-permute-start.2 = (f32[64,128]{1,0:T(8,128)S(1)}, f32[64,128]{1,0:T(8,128)S(1)}, u32[]{:S(2)}, u32[]{:S(2)}) collective-permute-start(f32[64,128]{1,0:T(8,128)S(1)} %get-tuple-element.49), channel_id=1, source_target_pairs={{0,8},{8,0},{16,24},{24,16},{1,9},{9,1},{17,25},{25,17},{2,10},{10... | collective-permute-start | bytes 98312 | tf_op jit(solution)/shard_map/ppermute | solution.py:470
  11.7 11.9 %copy-start.8 = (s32[4,3]{1,0:T(4,128)S(1)}, s32[4,3]{1,0:T(4,128)}, u32[]{:S(2)}) copy-start(s32[4,3]{1,0:T(4,128)} %bounds.5) | copy-start | bytes 148
  13.5 10.1 %collective-permute-start.1 = (f32[128,384]{1,0:T(8,128)S(1)}, f32[128,384]{1,0:T(8,128)S(1)}, u32[]{:S(2)}, u32[]{:S(2)}) collective-permute-start(f32[128,384]{1,0:T(8,128)S(1)} %project_up.1.refs_0_), channel_id=1, source_target_pairs={{4,0},{0,4},{5,1},{1,5},{6,2},{2,6},{7,3},{3,7},{12,8},{8,12},{13,... | collective-permute-start | bytes 589832 | tf_op jit(solution)/shard_map/ppermute | solution.py:480
  14.8 4.0 %collective-permute-start.5 = (f32[64,128]{1,0:T(8,128)S(1)}, f32[64,128]{1,0:T(8,128)S(1)}, u32[]{:S(2)}, u32[]{:S(2)}) collective-permute-start(f32[64,128]{1,0:T(8,128)S(1)} %add_add_fusion), channel_id=1, source_target_pairs={{0,1},{1,0},{2,3},{3,2},{4,5},{5,4},{6,7},{7,6},{8,9},{9,8},{10,11... | collective-permute-start | bytes 98312 | tf_op jit(solution)/shard_map/ppermute | solution.py:470
  18.8 4.8 %collective-permute-start.6 = (f32[64,128]{1,0:T(8,128)S(1)}, f32[64,128]{1,0:T(8,128)S(1)}, u32[]{:S(2)}, u32[]{:S(2)}) collective-permute-start(f32[64,128]{1,0:T(8,128)S(1)} %add.74.refs_2_), channel_id=1, source_target_pairs={{0,2},{1,3},{2,0},{3,1},{4,6},{5,7},{6,4},{7,5},{8,10},{9,11},{10,... | collective-permute-start | bytes 98312 | tf_op jit(solution)/shard_map/ppermute | solution.py:470
  25.7 2.4 %collective-permute-start.8 = (bf16[2,4,64,768]{3,2,1,0:T(8,128)(2,1)S(1)}, bf16[2,4,64,768]{3,2,1,0:T(8,128)(2,1)S(1)}, u32[]{:S(2)}, u32[]{:S(2)}) collective-permute-start(bf16[2,4,64,768]{3,2,1,0:T(8,128)(2,1)S(1)} %gradient.7), channel_id=1, source_target_pairs={{0,8},{8,0},{16,24},{24,16},{1,9},{9,1},{17,25},{25,17},{2,10},{10... | collective-permute-start | bytes 2359304 | tf_op jit(solution)/shard_map/ppermute | solution.py:470
  26.3 14.5 %collective-permute-start.7 = (bf16[2,4,64,768]{3,2,1,0:T(8,128)(2,1)S(1)}, bf16[2,4,64,768]{3,2,1,0:T(8,128)(2,1)S(1)}, u32[]{:S(2)}, u32[]{:S(2)}) collective-permute-start(bf16[2,4,64,768]{3,2,1,0:T(8,128)(2,1)S(1)} %gradient.5), channel_id=1, source_target_pairs={{0,8},{8,0},{16,24},{24,16},{1,9},{9,1},{17,25},{25,17},{2,10},{10... | collective-permute-start | bytes 2359304 | tf_op jit(solution)/shard_map/ppermute | solution.py:470
  26.9 3.9 %collective-permute-start.11 = (bf16[128,128]{1,0:T(8,128)(2,1)S(1)}, bf16[128,128]{1,0:T(8,128)(2,1)S(1)}, u32[]{:S(2)}, u32[]{:S(2)}) collective-permute-start(bf16[128,128]{1,0:T(8,128)(2,1)S(1)} %convert_element_type.136), channel_id=1, source_target_pairs={{0,8},{8,0},{16,24},{24,16},{1,9},{9,1},{17,25},{25,17},{2,10},{10... | collective-permute-start | bytes 98312 | tf_op jit(solution)/shard_map/ppermute | solution.py:470
  28.3 11.9 %collective-permute-start.10 = (bf16[4,64,768]{2,1,0:T(8,128)(2,1)S(1)}, bf16[4,64,768]{2,1,0:T(8,128)(2,1)S(1)}, u32[]{:S(2)}, u32[]{:S(2)}) collective-permute-start(bf16[4,64,768]{2,1,0:T(8,128)(2,1)S(1)} %get-tuple-element.82), channel_id=1, source_target_pairs={{0,1},{1,0},{2,3},{3,2},{4,5},{5,4},{6,7},{7,6},{8,9},{9,8},{10,11... | collective-permute-start | bytes 1179656 | tf_op jit(solution)/shard_map/ppermute | solution.py:470
  29.9 10.9 %collective-permute-start.9 = (bf16[4,64,768]{2,1,0:T(8,128)(2,1)S(1)}, bf16[4,64,768]{2,1,0:T(8,128)(2,1)S(1)}, u32[]{:S(2)}, u32[]{:S(2)}) collective-permute-start(bf16[4,64,768]{2,1,0:T(8,128)(2,1)S(1)} %get-tuple-element.83), channel_id=1, source_target_pairs={{0,16},{8,24},{16,0},{24,8},{1,17},{9,25},{17,1},{25,9},{2,18},{10... | collective-permute-start | bytes 1179656 | tf_op jit(solution)/shard_map/ppermute | solution.py:470
  30.8 8.5 %collective-permute-start.12 = (bf16[128,128]{1,0:T(8,128)(2,1)S(1)}, bf16[128,128]{1,0:T(8,128)(2,1)S(1)}, u32[]{:S(2)}, u32[]{:S(2)}) collective-permute-start(bf16[128,128]{1,0:T(8,128)(2,1)S(1)} %fusion.7), channel_id=1, source_target_pairs={{0,2},{1,3},{2,0},{3,1},{4,6},{5,7},{6,4},{7,5},{8,10},{9,11},{10,... | collective-permute-start | bytes 98312 | tf_op jit(solution)/shard_map/ppermute | solution.py:470
  34.2 22.8 %copy-start.2 = (f32[1,64,768]{2,1,0:T(8,128)S(1)}, f32[1,64,768]{2,1,0:T(8,128)}, u32[]{:S(2)}) copy-start(f32[1,64,768]{2,1,0:T(8,128)} %refs_0_.3) | copy-start | bytes 589828
  34.2 22.8 %copy-start.4 = (f32[1,64,768]{2,1,0:T(8,128)S(1)}, f32[1,64,768]{2,1,0:T(8,128)}, u32[]{:S(2)}) copy-start(f32[1,64,768]{2,1,0:T(8,128)} %refs_1_.3) | copy-start | bytes 589828
  34.2 22.8 %copy-start.5 = (f32[1,64,768]{2,1,0:T(8,128)S(1)}, f32[1,64,768]{2,1,0:T(8,128)}, u32[]{:S(2)}) copy-start(f32[1,64,768]{2,1,0:T(8,128)} %refs_2_.3) | copy-start | bytes 589828
  34.2 25.6 %copy-start.3 = (f32[1,64,768]{2,1,0:T(8,128)S(1)}, f32[1,64,768]{2,1,0:T(8,128)}, u32[]{:S(2)}) copy-start(f32[1,64,768]{2,1,0:T(8,128)} %refs_0_.2) | copy-start | bytes 589828
  34.3 25.6 %copy-start.6 = (f32[1,64,768]{2,1,0:T(8,128)S(1)}, f32[1,64,768]{2,1,0:T(8,128)}, u32[]{:S(2)}) copy-start(f32[1,64,768]{2,1,0:T(8,128)} %refs_1_.2) | copy-start | bytes 589828
  34.3 25.6 %copy-start.7 = (f32[1,64,768]{2,1,0:T(8,128)S(1)}, f32[1,64,768]{2,1,0:T(8,128)}, u32[]{:S(2)}) copy-start(f32[1,64,768]{2,1,0:T(8,128)} %refs_2_.2) | copy-start | bytes 589828
  41.0 5.9 %collective-permute-start.18 = (bf16[2,64,768]{2,1,0:T(8,128)(2,1)S(1)}, bf16[2,64,768]{2,1,0:T(8,128)(2,1)S(1)}, u32[]{:S(2)}, u32[]{:S(2)}) collective-permute-start(bf16[2,64,768]{2,1,0:T(8,128)(2,1)S(1)} %get-tuple-element.80), channel_id=1, source_target_pairs={{0,16},{8,24},{16,0},{24,8},{1,17},{9,25},{17,1},{25,9},{2,18},{10... | collective-permute-start | bytes 589832 | tf_op jit(solution)/shard_map/ppermute | solution.py:470
  41.9 10.6 %collective-permute-start.15 = (bf16[128,128]{1,0:T(8,128)(2,1)S(1)}, bf16[128,128]{1,0:T(8,128)(2,1)S(1)}, u32[]{:S(2)}, u32[]{:S(2)}) collective-permute-start(bf16[128,128]{1,0:T(8,128)(2,1)S(1)} %convert_element_type.151), channel_id=1, source_target_pairs={{0,1},{1,0},{2,3},{3,2},{4,5},{5,4},{6,7},{7,6},{8,9},{9,8},{10,11... | collective-permute-start | bytes 98312 | tf_op jit(solution)/shard_map/ppermute | solution.py:470
  44.0 6.7 %collective-permute-start.13 = (bf16[2,64,768]{2,1,0:T(8,128)(2,1)S(1)}, bf16[2,64,768]{2,1,0:T(8,128)(2,1)S(1)}, u32[]{:S(2)}, u32[]{:S(2)}) collective-permute-start(bf16[2,64,768]{2,1,0:T(8,128)(2,1)S(1)} %get-tuple-element.81), channel_id=1, source_target_pairs={{0,1},{1,0},{2,3},{3,2},{4,5},{5,4},{6,7},{7,6},{8,9},{9,8},{10,11... | collective-permute-start | bytes 589832 | tf_op jit(solution)/shard_map/ppermute | solution.py:470
  46.9 10.2 %collective-permute-start.19 = (bf16[64,768]{1,0:T(8,128)(2,1)S(1)}, bf16[64,768]{1,0:T(8,128)(2,1)S(1)}, u32[]{:S(2)}, u32[]{:S(2)}) collective-permute-start(bf16[64,768]{1,0:T(8,128)(2,1)S(1)} %fusion.4), channel_id=1, source_target_pairs={{0,2},{1,3},{2,0},{3,1},{4,6},{5,7},{6,4},{7,5},{8,10},{9,11},{10,... | collective-permute-start | bytes 294920 | tf_op jit(solution)/shard_map/ppermute | solution.py:470
  50.8 9.1 %collective-permute-start.14 = (bf16[64,768]{1,0:T(8,128)(2,1)S(1)}, bf16[64,768]{1,0:T(8,128)(2,1)S(1)}, u32[]{:S(2)}, u32[]{:S(2)}) collective-permute-start(bf16[64,768]{1,0:T(8,128)(2,1)S(1)} %fusion.5), channel_id=1, source_target_pairs={{0,2},{1,3},{2,0},{3,1},{4,6},{5,7},{6,4},{7,5},{8,10},{9,11},{10,... | collective-permute-start | bytes 294920 | tf_op jit(solution)/shard_map/ppermute | solution.py:470
  52.5 4.0 %collective-permute-start.16 = (bf16[128,128]{1,0:T(8,128)(2,1)S(1)}, bf16[128,128]{1,0:T(8,128)(2,1)S(1)}, u32[]{:S(2)}, u32[]{:S(2)}) collective-permute-start(bf16[128,128]{1,0:T(8,128)(2,1)S(1)} %get-tuple-element.78), channel_id=1, source_target_pairs={{0,16},{8,24},{16,0},{24,8},{1,17},{9,25},{17,1},{25,9},{2,18},{10... | collective-permute-start | bytes 98312 | tf_op jit(solution)/shard_map/ppermute | solution.py:470
  58.3 7.7 %collective-permute-start.20 = (bf16[1,64,768]{2,1,0:T(8,128)(2,1)S(1)}, bf16[1,64,768]{2,1,0:T(8,128)(2,1)S(1)}, u32[]{:S(2)}, u32[]{:S(2)}) collective-permute-start(bf16[1,64,768]{2,1,0:T(8,128)(2,1)S(1)} %get-tuple-element.62), channel_id=1, source_target_pairs={{0,2},{1,3},{2,0},{3,1},{4,6},{5,7},{6,4},{7,5},{8,10},{9,11},{10,... | collective-permute-start | bytes 294920 | tf_op jit(solution)/shard_map/ppermute | solution.py:470
  61.1 5.9 %collective-permute-start.17 = (bf16[1,64,768]{2,1,0:T(8,128)(2,1)S(1)}, bf16[1,64,768]{2,1,0:T(8,128)(2,1)S(1)}, u32[]{:S(2)}, u32[]{:S(2)}) collective-permute-start(bf16[1,64,768]{2,1,0:T(8,128)(2,1)S(1)} %get-tuple-element.61), channel_id=1, source_target_pairs={{0,2},{1,3},{2,0},{3,1},{4,6},{5,7},{6,4},{7,5},{8,10},{9,11},{10,... | collective-permute-start | bytes 294920 | tf_op jit(solution)/shard_map/ppermute | solution.py:470
  62.5 7.9 %collective-permute-start.21 = (bf16[2,64,768]{2,1,0:T(8,128)(2,1)S(1)}, bf16[2,64,768]{2,1,0:T(8,128)(2,1)S(1)}, u32[]{:S(2)}, u32[]{:S(2)}) collective-permute-start(bf16[2,64,768]{2,1,0:T(8,128)(2,1)S(1)} %pad_maximum_fusion.6), channel_id=1, source_target_pairs={{4,0},{0,4},{5,1},{1,5},{6,2},{2,6},{7,3},{3,7},{12,8},{8,12},{13,... | collective-permute-start | bytes 589832 | tf_op jit(solution)/shard_map/ppermute | solution.py:480
  66.0 8.1 %collective-permute-start.25 = (bf16[2,64,768]{2,1,0:T(8,128)(2,1)S(1)}, bf16[2,64,768]{2,1,0:T(8,128)(2,1)S(1)}, u32[]{:S(2)}, u32[]{:S(2)}) collective-permute-start(bf16[2,64,768]{2,1,0:T(8,128)(2,1)S(1)} %pad_maximum_fusion.9), channel_id=1, source_target_pairs={{0,16},{8,24},{16,0},{24,8},{1,17},{9,25},{17,1},{25,9},{2,18},{10... | collective-permute-start | bytes 589832 | tf_op jit(solution)/shard_map/ppermute | solution.py:470
  67.1 7.0 %collective-permute-start.23 = (bf16[2,64,768]{2,1,0:T(8,128)(2,1)S(1)}, bf16[2,64,768]{2,1,0:T(8,128)(2,1)S(1)}, u32[]{:S(2)}, u32[]{:S(2)}) collective-permute-start(bf16[2,64,768]{2,1,0:T(8,128)(2,1)S(1)} %pad_maximum_fusion.8), channel_id=1, source_target_pairs={{0,1},{1,0},{2,3},{3,2},{4,5},{5,4},{6,7},{7,6},{8,9},{9,8},{10,11... | collective-permute-start | bytes 589832 | tf_op jit(solution)/shard_map/ppermute | solution.py:470
  70.5 7.1 %collective-permute-start.22 = (bf16[2,64,768]{2,1,0:T(8,128)(2,1)S(1)}, bf16[2,64,768]{2,1,0:T(8,128)(2,1)S(1)}, u32[]{:S(2)}, u32[]{:S(2)}) collective-permute-start(bf16[2,64,768]{2,1,0:T(8,128)(2,1)S(1)} %pad_maximum_fusion.7), channel_id=1, source_target_pairs={{4,0},{0,4},{5,1},{1,5},{6,2},{2,6},{7,3},{3,7},{12,8},{8,12},{13,... | collective-permute-start | bytes 589832 | tf_op jit(solution)/shard_map/ppermute | solution.py:480
  74.1 14.2 %collective-permute-start.28 = (bf16[8,64,768]{2,1,0:T(8,128)(2,1)S(1)}, bf16[8,64,768]{2,1,0:T(8,128)(2,1)S(1)}, u32[]{:S(2)}, u32[]{:S(2)}) collective-permute-start(bf16[8,64,768]{2,1,0:T(8,128)(2,1)S(1)} %constant_dynamic-update-slice_fusion.refs_0_), channel_id=1, source_target_pairs={{0,8},{8,0},{16,24},{24,16},{1,9},{9,1},{17,25},{25,17},{2,10},{10... | collective-permute-start | bytes 2359304 | tf_op jit(solution)/shard_map/ppermute | solution.py:470
  74.3 11.6 %collective-permute-start.24 = (bf16[4,64,768]{2,1,0:T(8,128)(2,1)S(1)}, bf16[4,64,768]{2,1,0:T(8,128)(2,1)S(1)}, u32[]{:S(2)}, u32[]{:S(2)}) collective-permute-start(bf16[4,64,768]{2,1,0:T(8,128)(2,1)S(1)} %get-tuple-element.91), channel_id=1, source_target_pairs={{0,16},{8,24},{16,0},{24,8},{1,17},{9,25},{17,1},{25,9},{2,18},{10... | collective-permute-start | bytes 1179656 | tf_op jit(solution)/shard_map/ppermute | solution.py:470
  75.3 11.5 %collective-permute-start.26 = (bf16[4,64,768]{2,1,0:T(8,128)(2,1)S(1)}, bf16[4,64,768]{2,1,0:T(8,128)(2,1)S(1)}, u32[]{:S(2)}, u32[]{:S(2)}) collective-permute-start(bf16[4,64,768]{2,1,0:T(8,128)(2,1)S(1)} %get-tuple-element.92), channel_id=1, source_target_pairs={{0,1},{1,0},{2,3},{3,2},{4,5},{5,4},{6,7},{7,6},{8,9},{9,8},{10,11... | collective-permute-start | bytes 1179656 | tf_op jit(solution)/shard_map/ppermute | solution.py:470
  77.3 11.0 %collective-permute-start.27 = (bf16[4,64,768]{2,1,0:T(8,128)(2,1)S(1)}, bf16[4,64,768]{2,1,0:T(8,128)(2,1)S(1)}, u32[]{:S(2)}, u32[]{:S(2)}) collective-permute-start(bf16[4,64,768]{2,1,0:T(8,128)(2,1)S(1)} %get-tuple-element.90), channel_id=1, source_target_pairs={{4,0},{0,4},{5,1},{1,5},{6,2},{2,6},{7,3},{3,7},{12,8},{8,12},{13,... | collective-permute-start | bytes 1179656 | tf_op jit(solution)/shard_map/ppermute | solution.py:480
  86.8 11.1 %collective-permute-start.31 = (bf16[2,64,768]{2,1,0:T(8,128)(2,1)S(1)}, bf16[2,64,768]{2,1,0:T(8,128)(2,1)S(1)}, u32[]{:S(2)}, u32[]{:S(2)}) collective-permute-start(bf16[2,64,768]{2,1,0:T(8,128)(2,1)S(1)} %pad_maximum_fusion.10), channel_id=1, source_target_pairs={{4,0},{5,1},{6,2},{7,3},{12,8},{13,9},{14,10},{15,11},{20,16},{21,... | collective-permute-start | bytes 589832 | tf_op jit(solution)/shard_map/ppermute | solution.py:485
  88.4 8.5 %collective-permute-start.29 = (bf16[3,64,768]{2,1,0:T(8,128)(2,1)S(1)}, bf16[3,64,768]{2,1,0:T(8,128)(2,1)S(1)}, u32[]{:S(2)}, u32[]{:S(2)}) collective-permute-start(bf16[3,64,768]{2,1,0:T(8,128)(2,1)S(1)} %pad_maximum_fusion.3), channel_id=1, source_target_pairs={{0,16},{8,24},{16,0},{24,8},{1,17},{9,25},{17,1},{25,9},{2,18},{10... | collective-permute-start | bytes 884744 | tf_op jit(solution)/shard_map/ppermute | solution.py:470
  89.7 8.3 %collective-permute-start.30 = (bf16[3,64,768]{2,1,0:T(8,128)(2,1)S(1)}, bf16[3,64,768]{2,1,0:T(8,128)(2,1)S(1)}, u32[]{:S(2)}, u32[]{:S(2)}) collective-permute-start(bf16[3,64,768]{2,1,0:T(8,128)(2,1)S(1)} %pad_maximum_fusion.4), channel_id=1, source_target_pairs={{0,1},{1,0},{2,3},{3,2},{4,5},{5,4},{6,7},{7,6},{8,9},{9,8},{10,11... | collective-permute-start | bytes 884744 | tf_op jit(solution)/shard_map/ppermute | solution.py:470
  91.3 6.7 %collective-permute-start.33 = (bf16[8,64,768]{2,1,0:T(8,128)(2,1)S(1)}, bf16[8,64,768]{2,1,0:T(8,128)(2,1)S(1)}, u32[]{:S(2)}, u32[]{:S(2)}) collective-permute-start(bf16[8,64,768]{2,1,0:T(8,128)(2,1)S(1)} %constant_dynamic-update-slice_fusion.9.refs_2_), channel_id=1, source_target_pairs={{0,8},{8,0},{16,24},{24,16},{1,9},{9,1},{17,25},{25,17},{2,10},{10... | collective-permute-start | bytes 2359304 | tf_op jit(solution)/shard_map/ppermute | solution.py:470
  91.5 6.6 %collective-permute-start.34 = (bf16[8,64,768]{2,1,0:T(8,128)(2,1)S(1)}, bf16[8,64,768]{2,1,0:T(8,128)(2,1)S(1)}, u32[]{:S(2)}, u32[]{:S(2)}) collective-permute-start(bf16[8,64,768]{2,1,0:T(8,128)(2,1)S(1)} %constant_dynamic-update-slice_fusion.11.refs_4_), channel_id=1, source_target_pairs={{0,8},{8,0},{16,24},{24,16},{1,9},{9,1},{17,25},{25,17},{2,10},{10... | collective-permute-start | bytes 2359304 | tf_op jit(solution)/shard_map/ppermute | solution.py:470
  98.0 2.4 %collective-permute-start.32 = (bf16[8,64,768]{2,1,0:T(8,128)(2,1)S(1)}, bf16[8,64,768]{2,1,0:T(8,128)(2,1)S(1)}, u32[]{:S(2)}, u32[]{:S(2)}) collective-permute-start(bf16[8,64,768]{2,1,0:T(8,128)(2,1)S(1)} %constant_dynamic-update-slice_fusion.6.refs_0_), channel_id=1, source_target_pairs={{0,8},{8,0},{16,24},{24,16},{1,9},{9,1},{17,25},{25,17},{2,10},{10... | collective-permute-start | bytes 2359304 | tf_op jit(solution)/shard_map/ppermute | solution.py:470

commit v15 on v13

--- a/solution.py
+++ b/solution.py
@@ -573,15 +573,13 @@
     down_end = joined(picked(next_own, 0), picked(next_one, 0), picked(next_two, 0))
     up_end = joined(picked(next_own, 1), picked(next_one, 1), picked(next_two, 2))
     end = joined(crossed(down_end, "replica", 2), crossed(up_end, "tensor", 1), next_end)
-    near = joined(own, one, two)
-    far = joined(down_three, up_three)
+    owned = joined(own, one, two, down_three, up_three)
     next_near = joined(next_own, next_one, next_two)
-    near_core, far_core, next_core, end_core = (
-        crossed(piece, "replica", 1) for piece in (near, far, next_near, end)
-    )
-    placed = place(
-        bounds, [near, near_core, far, far_core, next_near, next_core], [], slots, ranks, features
-    )
+    owned_core, next_core, end_core = (
+        crossed(piece, "replica", 1) for piece in (owned, next_near, end)
+    )
+    early = [owned, owned_core, next_near, next_core]
+    placed = place(bounds, early, [], slots, ranks, features)
     placed = place(bounds, [end, end_core], placed, slots, ranks, features)
     return placed
 

time: 100 us -> 100 us (level)
    ppermute x1, waiting for transfers between devices: 0.01 us -> 1.27 us  [following_layer(): return lax.ppermute(block, 'section', [(i + 1, i) for i in range(size - 1)])]
    ppermute x29 -> x28, waiting for transfers between devices: 33.6 us -> 32.5 us  [swapped(): return lax.ppermute(block, axis, route)]
    ppermute x29 -> x28, starting transfers between devices: 33.9 us -> 34.1 us  [swapped(): return lax.ppermute(block, axis, route)]
  transfers between devices with their start and end apart: 35 -> 34, of which waited for: 20 -> 20; matrix products, arithmetic and copies ran while one was open for 2% -> 2% of each run, Pallas kernels for 12% -> 12%
where the time goes in v15:
time: 100 us; the launch traced here: 99.8 us
  starting transfers between devices  42 us (42%)
  waiting for transfers between devices  38.1 us (38%)
  Pallas kernels  15.5 us (16%)
  other arithmetic  2.8 us (3%)
  between operations  1.09 us (1%)
    ppermute x28, starting transfers between devices, swapped(): return lax.ppermute(block, axis, route)  34.1 us
    ppermute x28, waiting for transfers between devices, swapped(): return lax.ppermute(block, axis, route)  32.5 us
    ppermute x5, starting transfers between devices, from_next(): return lax.ppermute(block, 'section', route)  6.58 us
    ppermute x5, waiting for transfers between devices, from_next(): return lax.ppermute(block, 'section', route)  4.41 us
    pallas_call x1, Pallas kernels, project_down(): pl.pallas_call(functools.partial(project_down_kernel, steps), in_specs=[i...  3.87 us
    pallas_call x2, Pallas kernels, place(): pl.pallas_call(functools.partial(place_kernel, layout, not before), in_sp...  3.57 us
    pallas_call x2, Pallas kernels, update(): pl.pallas_call(functools.partial(update_kernel, which), in_specs=[in_vmem...  2.45 us
  transfers between devices with their start and end apart: 34, of which 20 were waited for; matrix products, arithmetic and copies ran while one was open for 2% of the time, Pallas kernels for 12%

profile of v15, /device:TPU:0, one launch (start us, length us, event | category | flops | bytes accessed | tf_op | source)
XLA Modules:
  0.0 99.8 jit_solution(16715545956983949738)
XLA Ops:
  0.6 1.0 fusion.6
  1.6 3.0 %collective-permute-start = (bf16[64,768]{1,0:T(8,128)(2,1)S(1)}, bf16[64,768]{1,0:T(8,128)(2,1)S(1)}, u32[]{:S(2)}, u32[]{:S(2)}) collective-permute-start(bf16[64,768]{1,0:T(8,128)(2,1)S(1)} %fusion.6), channel_id=1, source_target_pairs={{4,0},{0,4},{5,1},{1,5},{6,2},{2,6},{7,3},{3,7},{12,8},{8,12},{13,... | collective-permute-start | bytes 294920 | tf_op jit(solution)/shard_map/ppermute | solution.py:480
  4.6 1.0 %convert_bitcast_fusion = (bf16[64,768]{1,0:T(8,128)(2,1)S(1)}, bf16[64,768]{1,0:T(8,128)(2,1)S(1)}) fusion(f32[1,64,768]{2,1,0:T(8,128)} %refs_0_.3, f32[1,64,768]{2,1,0:T(8,128)} %refs_0_.2), kind=kLoop, calls=%fused_computation.29 | loop fusion | flops 98304 | bytes 589824 | tf_op jit(solution)/shard_map/convert.5
  5.7 3.9 %project_down.1 = (f32[128,128]{1,0:T(8,128)S(1)}, f32[128,128]{1,0:T(8,128)S(1)}, bf16[128,12288]{1,0:T(8,128)(2,1)S(1)}) custom-call(bf16[128,12288]{1,0:T(8,128)(2,1)} %bitcast.53, bf16[2,64,12288]{2,1,0:T(8,128)(2,1)} %bitcast.54), custom_call_target="tpu_custom_call" | custom-call | flops 402653184 | bytes 6291456 | tf_op jit(solution)/shard_map/project_down/pallas_call | solution.py:106
  9.8 0.7 collective-permute-start.4
  10.5 0.9 collective-permute-start.3
  11.7 1.8 %project_up.1.refs_0_ = f32[128,384]{1,0:T(8,128)S(1)} custom-call(s32[1,4]{1,0:T(1,128)S(1)} %bitcast.51, f32[128,128]{1,0:T(8,128)S(1)} %get-tuple-element.43.by_down, bf16[128,12288]{1,0:T(8,128)(2,1)S(1)} %get-tuple-element.47.h_ref, bf16[128,12288]{1,0:T(8,128)(2,1)S(1)} %bitcast.45, bf16[2,64,12288]{2,1,0:T(8,128)(2,1)S(1)} %bitcast.50), custom_call_target="tpu_custom_call" | custom-call | flops 805306368 | bytes 9437184 | tf_op jit(solution)/shard_map/project_up/pallas_call | solution.py:141
  13.9 0.9 collective-permute-done.3
  14.8 1.6 %collective-permute-start.5 = (f32[64,128]{1,0:T(8,128)S(1)}, f32[64,128]{1,0:T(8,128)S(1)}, u32[]{:S(2)}, u32[]{:S(2)}) collective-permute-start(f32[64,128]{1,0:T(8,128)S(1)} %add_add_fusion), channel_id=1, source_target_pairs={{0,1},{1,0},{2,3},{3,2},{4,5},{5,4},{6,7},{7,6},{8,9},{9,8},{10,11... | collective-permute-start | bytes 98312 | tf_op jit(solution)/shard_map/ppermute | solution.py:470
  16.4 2.3 %collective-permute-done.5 = f32[64,128]{1,0:T(8,128)S(1)} collective-permute-done((f32[64,128]{1,0:T(8,128)S(1)}, f32[64,128]{1,0:T(8,128)S(1)}, u32[]{:S(2)}, u32[]{:S(2)}) %collective-permute-start.5) | collective-permute-done | bytes 32800 | tf_op jit(solution)/shard_map/ppermute | solution.py:470
  18.8 2.6 %collective-permute-start.6 = (f32[64,128]{1,0:T(8,128)S(1)}, f32[64,128]{1,0:T(8,128)S(1)}, u32[]{:S(2)}, u32[]{:S(2)}) collective-permute-start(f32[64,128]{1,0:T(8,128)S(1)} %add.74.refs_2_), channel_id=1, source_target_pairs={{0,2},{1,3},{2,0},{3,1},{4,6},{5,7},{6,4},{7,5},{8,10},{9,11},{10,... | collective-permute-start | bytes 98312 | tf_op jit(solution)/shard_map/ppermute | solution.py:470
  21.4 2.2 %collective-permute-done.6.refs_3_ = f32[64,128]{1,0:T(8,128)S(1)} collective-permute-done((f32[64,128]{1,0:T(8,128)S(1)}, f32[64,128]{1,0:T(8,128)S(1)}, u32[]{:S(2)}, u32[]{:S(2)}) %collective-permute-start.6) | collective-permute-done | bytes 32800 | tf_op jit(solution)/shard_map/ppermute | solution.py:470
  23.6 1.6 %chain.1 = (bf16[128,256]{1,0:T(8,128)(2,1)S(1)}, f32[128,128]{1,0:T(8,128)S(1)}) custom-call(s32[4,3]{1,0:T(4,128)S(1)} %copy-done.8, s32[1,4]{1,0:T(1,128)S(1)} %bitcast.52, f32[128,384]{1,0:T(8,128)S(1)} %project_up.1.refs_0_, f32[128,384]{1,0:T(8,128)S(1)} %collective-permute-done.1.refs_1_, f32[64,128]{1,0:T(8,128)S(1)} %add.74.refs_2_, ...), custom_call_target="tpu_custom_call" | custom-call | tf_op jit(solution)/shard_map/chain/pallas_call | solution.py:314
  27.4 0.6 collective-permute-done.8
  28.3 1.6 %collective-permute-start.10 = (bf16[4,64,768]{2,1,0:T(8,128)(2,1)S(1)}, bf16[4,64,768]{2,1,0:T(8,128)(2,1)S(1)}, u32[]{:S(2)}, u32[]{:S(2)}) collective-permute-start(bf16[4,64,768]{2,1,0:T(8,128)(2,1)S(1)} %get-tuple-element.80), channel_id=1, source_target_pairs={{0,1},{1,0},{2,3},{3,2},{4,5},{5,4},{6,7},{7,6},{8,9},{9,8},{10,11... | collective-permute-start | bytes 1179656 | tf_op jit(solution)/shard_map/ppermute | solution.py:470
  29.9 0.9 collective-permute-start.9
  30.8 2.9 %collective-permute-start.12 = (bf16[128,128]{1,0:T(8,128)(2,1)S(1)}, bf16[128,128]{1,0:T(8,128)(2,1)S(1)}, u32[]{:S(2)}, u32[]{:S(2)}) collective-permute-start(bf16[128,128]{1,0:T(8,128)(2,1)S(1)} %fusion.7), channel_id=1, source_target_pairs={{0,2},{1,3},{2,0},{3,1},{4,6},{5,7},{6,4},{7,5},{8,10},{9,11},{10,... | collective-permute-start | bytes 98312 | tf_op jit(solution)/shard_map/ppermute | solution.py:470
  34.2 5.1 %collective-permute-done.12 = bf16[128,128]{1,0:T(8,128)(2,1)S(1)} collective-permute-done((bf16[128,128]{1,0:T(8,128)(2,1)S(1)}, bf16[128,128]{1,0:T(8,128)(2,1)S(1)}, u32[]{:S(2)}, u32[]{:S(2)}) %collective-permute-start.12) | collective-permute-done | bytes 32800 | tf_op jit(solution)/shard_map/ppermute | solution.py:470
  39.3 0.9 collective-permute-done.10.one
  41.0 0.9 collective-permute-start.18
  41.9 2.1 %collective-permute-start.15 = (bf16[128,128]{1,0:T(8,128)(2,1)S(1)}, bf16[128,128]{1,0:T(8,128)(2,1)S(1)}, u32[]{:S(2)}, u32[]{:S(2)}) collective-permute-start(bf16[128,128]{1,0:T(8,128)(2,1)S(1)} %convert_element_type.151), channel_id=1, source_target_pairs={{0,1},{1,0},{2,3},{3,2},{4,5},{5,4},{6,7},{7,6},{8,9},{9,8},{10,11... | collective-permute-start | bytes 98312 | tf_op jit(solution)/shard_map/ppermute | solution.py:470
  44.1 2.7 %collective-permute-done.18.two = bf16[2,64,768]{2,1,0:T(8,128)(2,1)S(1)} collective-permute-done((bf16[2,64,768]{2,1,0:T(8,128)(2,1)S(1)}, bf16[2,64,768]{2,1,0:T(8,128)(2,1)S(1)}, u32[]{:S(2)}, u32[]{:S(2)}) %collective-permute-start.18) | collective-permute-done | bytes 196640 | tf_op jit(solution)/shard_map/ppermute | solution.py:470
  46.9 2.9 %collective-permute-start.19 = (bf16[64,768]{1,0:T(8,128)(2,1)S(1)}, bf16[64,768]{1,0:T(8,128)(2,1)S(1)}, u32[]{:S(2)}, u32[]{:S(2)}) collective-permute-start(bf16[64,768]{1,0:T(8,128)(2,1)S(1)} %fusion.4), channel_id=1, source_target_pairs={{0,2},{1,3},{2,0},{3,1},{4,6},{5,7},{6,4},{7,5},{8,10},{9,11},{10,... | collective-permute-start | bytes 294920 | tf_op jit(solution)/shard_map/ppermute | solution.py:470
  49.8 1.0 collective-permute-done.13.two
  50.8 1.7 %collective-permute-start.14 = (bf16[64,768]{1,0:T(8,128)(2,1)S(1)}, bf16[64,768]{1,0:T(8,128)(2,1)S(1)}, u32[]{:S(2)}, u32[]{:S(2)}) collective-permute-start(bf16[64,768]{1,0:T(8,128)(2,1)S(1)} %fusion.5), channel_id=1, source_target_pairs={{0,2},{1,3},{2,0},{3,1},{4,6},{5,7},{6,4},{7,5},{8,10},{9,11},{10,... | collective-permute-start | bytes 294920 | tf_op jit(solution)/shard_map/ppermute | solution.py:470
  52.5 1.6 %collective-permute-start.16 = (bf16[128,128]{1,0:T(8,128)(2,1)S(1)}, bf16[128,128]{1,0:T(8,128)(2,1)S(1)}, u32[]{:S(2)}, u32[]{:S(2)}) collective-permute-start(bf16[128,128]{1,0:T(8,128)(2,1)S(1)} %get-tuple-element.76), channel_id=1, source_target_pairs={{0,16},{8,24},{16,0},{24,8},{1,17},{9,25},{17,1},{25,9},{2,18},{10... | collective-permute-start | bytes 98312 | tf_op jit(solution)/shard_map/ppermute | solution.py:470
  54.1 2.4 %collective-permute-done.16.other_ref = bf16[128,128]{1,0:T(8,128)(2,1)S(1)} collective-permute-done((bf16[128,128]{1,0:T(8,128)(2,1)S(1)}, bf16[128,128]{1,0:T(8,128)(2,1)S(1)}, u32[]{:S(2)}, u32[]{:S(2)}) %collective-permute-start.16) | collective-permute-done | bytes 32800 | tf_op jit(solution)/shard_map/ppermute | solution.py:470
  57.1 1.2 %update.3 = (f32[1,64,768]{2,1,0:T(8,128)}, f32[1,64,768]{2,1,0:T(8,128)}, f32[1,64,768]{2,1,0:T(8,128)}, bf16[1,64,768]{2,1,0:T(8,128)(2,1)S(1)}) custom-call(bf16[2,4,64,768]{3,2,1,0:T(8,128)(2,1)S(1)} %gradient.4.kept, bf16[2,4,64,768]{3,2,1,0:T(8,128)(2,1)S(1)} %collective-permute-done.7.near, bf16[4,64,768]{2,1,0:T(8,128)(2,1)S(1)} %collective-permute-done.10.one, ...), custom_call_target="tpu_custom_call" | custom-call | tf_op jit(solution)/shard_map/update/pallas_call | solution.py:390
  58.3 0.8 collective-permute-start.20
  59.1 0.8 collective-permute-done.14.last
  59.8 1.2 %update.2 = (f32[1,64,768]{2,1,0:T(8,128)}, f32[1,64,768]{2,1,0:T(8,128)}, f32[1,64,768]{2,1,0:T(8,128)}, bf16[1,64,768]{2,1,0:T(8,128)(2,1)S(1)}) custom-call(bf16[2,4,64,768]{3,2,1,0:T(8,128)(2,1)S(1)} %gradient.4.kept, bf16[2,4,64,768]{3,2,1,0:T(8,128)(2,1)S(1)} %collective-permute-done.7.near, bf16[4,64,768]{2,1,0:T(8,128)(2,1)S(1)} %collective-permute-done.9.one, ...), custom_call_target="tpu_custom_call" | custom-call | tf_op jit(solution)/shard_map/update/pallas_call | solution.py:390
  61.1 1.4 %collective-permute-start.17 = (bf16[1,64,768]{2,1,0:T(8,128)(2,1)S(1)}, bf16[1,64,768]{2,1,0:T(8,128)(2,1)S(1)}, u32[]{:S(2)}, u32[]{:S(2)}) collective-permute-start(bf16[1,64,768]{2,1,0:T(8,128)(2,1)S(1)} %get-tuple-element.60), channel_id=1, source_target_pairs={{0,2},{1,3},{2,0},{3,1},{4,6},{5,7},{6,4},{7,5},{8,10},{9,11},{10,... | collective-permute-start | bytes 294920 | tf_op jit(solution)/shard_map/ppermute | solution.py:470
  62.5 1.8 %collective-permute-start.21 = (bf16[2,64,768]{2,1,0:T(8,128)(2,1)S(1)}, bf16[2,64,768]{2,1,0:T(8,128)(2,1)S(1)}, u32[]{:S(2)}, u32[]{:S(2)}) collective-permute-start(bf16[2,64,768]{2,1,0:T(8,128)(2,1)S(1)} %pad_maximum_fusion.6), channel_id=1, source_target_pairs={{4,0},{0,4},{5,1},{1,5},{6,2},{2,6},{7,3},{3,7},{12,8},{8,12},{13,... | collective-permute-start | bytes 589832 | tf_op jit(solution)/shard_map/ppermute | solution.py:480
  64.3 1.7 %collective-permute-done.20 = bf16[1,64,768]{2,1,0:T(8,128)(2,1)S(1)} collective-permute-done((bf16[1,64,768]{2,1,0:T(8,128)(2,1)S(1)}, bf16[1,64,768]{2,1,0:T(8,128)(2,1)S(1)}, u32[]{:S(2)}, u32[]{:S(2)}) %collective-permute-start.20) | collective-permute-done | bytes 98336 | tf_op jit(solution)/shard_map/ppermute | solution.py:470
  66.1 0.9 collective-permute-done.17
  67.1 3.4 %collective-permute-start.23 = (bf16[2,64,768]{2,1,0:T(8,128)(2,1)S(1)}, bf16[2,64,768]{2,1,0:T(8,128)(2,1)S(1)}, u32[]{:S(2)}, u32[]{:S(2)}) collective-permute-start(bf16[2,64,768]{2,1,0:T(8,128)(2,1)S(1)} %pad_maximum_fusion.8), channel_id=1, source_target_pairs={{0,1},{1,0},{2,3},{3,2},{4,5},{5,4},{6,7},{7,6},{8,9},{9,8},{10,11... | collective-permute-start | bytes 589832 | tf_op jit(solution)/shard_map/ppermute | solution.py:470
  70.5 1.4 %collective-permute-start.22 = (bf16[2,64,768]{2,1,0:T(8,128)(2,1)S(1)}, bf16[2,64,768]{2,1,0:T(8,128)(2,1)S(1)}, u32[]{:S(2)}, u32[]{:S(2)}) collective-permute-start(bf16[2,64,768]{2,1,0:T(8,128)(2,1)S(1)} %pad_maximum_fusion.7), channel_id=1, source_target_pairs={{4,0},{0,4},{5,1},{1,5},{6,2},{2,6},{7,3},{3,7},{12,8},{8,12},{13,... | collective-permute-start | bytes 589832 | tf_op jit(solution)/shard_map/ppermute | solution.py:480
  71.9 2.6 %collective-permute-done.23 = bf16[2,64,768]{2,1,0:T(8,128)(2,1)S(1)} collective-permute-done((bf16[2,64,768]{2,1,0:T(8,128)(2,1)S(1)}, bf16[2,64,768]{2,1,0:T(8,128)(2,1)S(1)}, u32[]{:S(2)}, u32[]{:S(2)}) %collective-permute-start.23) | collective-permute-done | bytes 196640 | tf_op jit(solution)/shard_map/ppermute | solution.py:470
  74.7 1.6 %collective-permute-start.24 = (bf16[4,64,768]{2,1,0:T(8,128)(2,1)S(1)}, bf16[4,64,768]{2,1,0:T(8,128)(2,1)S(1)}, u32[]{:S(2)}, u32[]{:S(2)}) collective-permute-start(bf16[4,64,768]{2,1,0:T(8,128)(2,1)S(1)} %get-tuple-element.89), channel_id=1, source_target_pairs={{0,16},{8,24},{16,0},{24,8},{1,17},{9,25},{17,1},{25,9},{2,18},{10... | collective-permute-start | bytes 1179656 | tf_op jit(solution)/shard_map/ppermute | solution.py:470
  76.3 2.5 %collective-permute-start.26 = (bf16[4,64,768]{2,1,0:T(8,128)(2,1)S(1)}, bf16[4,64,768]{2,1,0:T(8,128)(2,1)S(1)}, u32[]{:S(2)}, u32[]{:S(2)}) collective-permute-start(bf16[4,64,768]{2,1,0:T(8,128)(2,1)S(1)} %get-tuple-element.90), channel_id=1, source_target_pairs={{0,1},{1,0},{2,3},{3,2},{4,5},{5,4},{6,7},{7,6},{8,9},{9,8},{10,11... | collective-permute-start | bytes 1179656 | tf_op jit(solution)/shard_map/ppermute | solution.py:470
  78.9 4.4 %collective-permute-done.27 = bf16[4,64,768]{2,1,0:T(8,128)(2,1)S(1)} collective-permute-done((bf16[4,64,768]{2,1,0:T(8,128)(2,1)S(1)}, bf16[4,64,768]{2,1,0:T(8,128)(2,1)S(1)}, u32[]{:S(2)}, u32[]{:S(2)}) %collective-permute-start.27) | collective-permute-done | bytes 393248 | tf_op jit(solution)/shard_map/ppermute | solution.py:480
  83.3 1.3 %collective-permute-done.26 = bf16[4,64,768]{2,1,0:T(8,128)(2,1)S(1)} collective-permute-done((bf16[4,64,768]{2,1,0:T(8,128)(2,1)S(1)}, bf16[4,64,768]{2,1,0:T(8,128)(2,1)S(1)}, u32[]{:S(2)}, u32[]{:S(2)}) %collective-permute-start.26) | collective-permute-done | bytes 393248 | tf_op jit(solution)/shard_map/ppermute | solution.py:470
  85.3 2.1 %collective-permute-start.29 = (bf16[3,64,768]{2,1,0:T(8,128)(2,1)S(1)}, bf16[3,64,768]{2,1,0:T(8,128)(2,1)S(1)}, u32[]{:S(2)}, u32[]{:S(2)}) collective-permute-start(bf16[3,64,768]{2,1,0:T(8,128)(2,1)S(1)} %pad_maximum_fusion.4), channel_id=1, source_target_pairs={{0,1},{1,0},{2,3},{3,2},{4,5},{5,4},{6,7},{7,6},{8,9},{9,8},{10,11... | collective-permute-start | bytes 884744 | tf_op jit(solution)/shard_map/ppermute | solution.py:470
  87.5 1.3 %collective-permute-start.30 = (bf16[2,64,768]{2,1,0:T(8,128)(2,1)S(1)}, bf16[2,64,768]{2,1,0:T(8,128)(2,1)S(1)}, u32[]{:S(2)}, u32[]{:S(2)}) collective-permute-start(bf16[2,64,768]{2,1,0:T(8,128)(2,1)S(1)} %pad_maximum_fusion.10), channel_id=1, source_target_pairs={{4,0},{5,1},{6,2},{7,3},{12,8},{13,9},{14,10},{15,11},{20,16},{21,... | collective-permute-start | bytes 589832 | tf_op jit(solution)/shard_map/ppermute | solution.py:485
  88.9 5.4 %collective-permute-done.28 = bf16[3,64,768]{2,1,0:T(8,128)(2,1)S(1)} collective-permute-done((bf16[3,64,768]{2,1,0:T(8,128)(2,1)S(1)}, bf16[3,64,768]{2,1,0:T(8,128)(2,1)S(1)}, u32[]{:S(2)}, u32[]{:S(2)}) %collective-permute-start.28) | collective-permute-done | bytes 294944 | tf_op jit(solution)/shard_map/ppermute | solution.py:470
  94.8 1.3 %collective-permute-done.30 = bf16[2,64,768]{2,1,0:T(8,128)(2,1)S(1)} collective-permute-done((bf16[2,64,768]{2,1,0:T(8,128)(2,1)S(1)}, bf16[2,64,768]{2,1,0:T(8,128)(2,1)S(1)}, u32[]{:S(2)}, u32[]{:S(2)}) %collective-permute-start.30) | collective-permute-done | bytes 196640 | tf_op jit(solution)/shard_map/ppermute | solution.py:485
  96.2 2.3 %place.2 = (bf16[2,64,12288]{2,1,0:T(8,128)(2,1)}, bf16[2,64,12288]{2,1,0:T(8,128)(2,1)}) custom-call(s32[4,3]{1,0:T(4,128)S(1)} %copy-done.8, bf16[16,64,768]{2,1,0:T(8,128)(2,1)S(1)} %constant_dynamic-update-slice_fusion.3.refs_0_, bf16[16,64,768]{2,1,0:T(8,128)(2,1)S(1)} %collective-permute-done.32.refs_1_, ...), custom_call_target="tpu_custom_call" | custom-call | bytes 9437184 | tf_op jit(solution)/shard_map/place/pallas_call | solution.py:451
  98.5 1.3 %place.3 = (bf16[2,64,12288]{2,1,0:T(8,128)(2,1)}, bf16[2,64,12288]{2,1,0:T(8,128)(2,1)}) custom-call(s32[4,3]{1,0:T(4,128)S(1)} %copy-done.8, bf16[8,64,768]{2,1,0:T(8,128)(2,1)S(1)} %constant_dynamic-update-slice_fusion.refs_0_, bf16[8,64,768]{2,1,0:T(8,128)(2,1)S(1)} %collective-permute-done.31.refs_1_, ...), custom_call_target="tpu_custom_call", output_to_operand_aliasing={{0}: (3, {}), {1}: (4, {})} | custom-call | bytes 3145728 | tf_op jit(solution)/shard_map/place/pallas_call | solution.py:451
  (93 shorter events, 7.3 us)
Async XLA Ops:
  1.6 8.0 %collective-permute-start = (bf16[64,768]{1,0:T(8,128)(2,1)S(1)}, bf16[64,768]{1,0:T(8,128)(2,1)S(1)}, u32[]{:S(2)}, u32[]{:S(2)}) collective-permute-start(bf16[64,768]{1,0:T(8,128)(2,1)S(1)} %fusion.6), channel_id=1, source_target_pairs={{4,0},{0,4},{5,1},{1,5},{6,2},{2,6},{7,3},{3,7},{12,8},{8,12},{13,... | collective-permute-start | bytes 294920 | tf_op jit(solution)/shard_map/ppermute | solution.py:480
  5.7 6.1 %copy-start = (bf16[1,4,32,12288]{3,2,1,0:T(8,128)(2,1)S(1)}, bf16[1,4,32,12288]{3,2,1,0:T(8,128)(2,1)}, u32[]{:S(2)}) copy-start(bf16[1,4,32,12288]{3,2,1,0:T(8,128)(2,1)} %param.13) | copy-start | bytes 9437188
  5.7 6.0 %copy-start.1 = (bf16[1,1,2,64,12288]{4,3,2,1,0:T(8,128)(2,1)S(1)}, bf16[1,1,2,64,12288]{4,3,2,1,0:T(8,128)(2,1)}, u32[]{:S(2)}) copy-start(bf16[1,1,2,64,12288]{4,3,2,1,0:T(8,128)(2,1)} %param.17) | copy-start | bytes 9437188
  5.7 6.0 %copy-start.9 = (s32[4]{0:T(128)S(1)}, s32[4]{0:T(128)}, u32[]{:S(2)}) copy-start(s32[4]{0:T(128)} %param.14) | copy-start | bytes 52
  9.8 4.1 %collective-permute-start.4 = (f32[64,128]{1,0:T(8,128)S(1)}, f32[64,128]{1,0:T(8,128)S(1)}, u32[]{:S(2)}, u32[]{:S(2)}) collective-permute-start(f32[64,128]{1,0:T(8,128)S(1)} %get-tuple-element.48), channel_id=1, source_target_pairs={{0,24},{8,16},{16,8},{24,0},{1,25},{9,17},{17,9},{25,1},{2,26},{10... | collective-permute-start | bytes 98312 | tf_op jit(solution)/shard_map/ppermute | solution.py:470
  10.5 4.3 %collective-permute-start.3 = (f32[64,128]{1,0:T(8,128)S(1)}, f32[64,128]{1,0:T(8,128)S(1)}, u32[]{:S(2)}, u32[]{:S(2)}) collective-permute-start(f32[64,128]{1,0:T(8,128)S(1)} %get-tuple-element.48), channel_id=1, source_target_pairs={{0,16},{8,24},{16,0},{24,8},{1,17},{9,25},{17,1},{25,9},{2,18},{10... | collective-permute-start | bytes 98312 | tf_op jit(solution)/shard_map/ppermute | solution.py:470
  11.4 3.3 %collective-permute-start.2 = (f32[64,128]{1,0:T(8,128)S(1)}, f32[64,128]{1,0:T(8,128)S(1)}, u32[]{:S(2)}, u32[]{:S(2)}) collective-permute-start(f32[64,128]{1,0:T(8,128)S(1)} %get-tuple-element.48), channel_id=1, source_target_pairs={{0,8},{8,0},{16,24},{24,16},{1,9},{9,1},{17,25},{25,17},{2,10},{10... | collective-permute-start | bytes 98312 | tf_op jit(solution)/shard_map/ppermute | solution.py:470
  11.7 11.9 %copy-start.8 = (s32[4,3]{1,0:T(4,128)S(1)}, s32[4,3]{1,0:T(4,128)}, u32[]{:S(2)}) copy-start(s32[4,3]{1,0:T(4,128)} %bounds.5) | copy-start | bytes 148
  13.5 10.1 %collective-permute-start.1 = (f32[128,384]{1,0:T(8,128)S(1)}, f32[128,384]{1,0:T(8,128)S(1)}, u32[]{:S(2)}, u32[]{:S(2)}) collective-permute-start(f32[128,384]{1,0:T(8,128)S(1)} %project_up.1.refs_0_), channel_id=1, source_target_pairs={{4,0},{0,4},{5,1},{1,5},{6,2},{2,6},{7,3},{3,7},{12,8},{8,12},{13,... | collective-permute-start | bytes 589832 | tf_op jit(solution)/shard_map/ppermute | solution.py:480
  14.8 4.0 %collective-permute-start.5 = (f32[64,128]{1,0:T(8,128)S(1)}, f32[64,128]{1,0:T(8,128)S(1)}, u32[]{:S(2)}, u32[]{:S(2)}) collective-permute-start(f32[64,128]{1,0:T(8,128)S(1)} %add_add_fusion), channel_id=1, source_target_pairs={{0,1},{1,0},{2,3},{3,2},{4,5},{5,4},{6,7},{7,6},{8,9},{9,8},{10,11... | collective-permute-start | bytes 98312 | tf_op jit(solution)/shard_map/ppermute | solution.py:470
  18.8 4.8 %collective-permute-start.6 = (f32[64,128]{1,0:T(8,128)S(1)}, f32[64,128]{1,0:T(8,128)S(1)}, u32[]{:S(2)}, u32[]{:S(2)}) collective-permute-start(f32[64,128]{1,0:T(8,128)S(1)} %add.74.refs_2_), channel_id=1, source_target_pairs={{0,2},{1,3},{2,0},{3,1},{4,6},{5,7},{6,4},{7,5},{8,10},{9,11},{10,... | collective-permute-start | bytes 98312 | tf_op jit(solution)/shard_map/ppermute | solution.py:470
  25.7 2.4 %collective-permute-start.8 = (bf16[2,4,64,768]{3,2,1,0:T(8,128)(2,1)S(1)}, bf16[2,4,64,768]{3,2,1,0:T(8,128)(2,1)S(1)}, u32[]{:S(2)}, u32[]{:S(2)}) collective-permute-start(bf16[2,4,64,768]{3,2,1,0:T(8,128)(2,1)S(1)} %gradient.7), channel_id=1, source_target_pairs={{0,8},{8,0},{16,24},{24,16},{1,9},{9,1},{17,25},{25,17},{2,10},{10... | collective-permute-start | bytes 2359304 | tf_op jit(solution)/shard_map/ppermute | solution.py:470
  26.3 14.5 %collective-permute-start.7 = (bf16[2,4,64,768]{3,2,1,0:T(8,128)(2,1)S(1)}, bf16[2,4,64,768]{3,2,1,0:T(8,128)(2,1)S(1)}, u32[]{:S(2)}, u32[]{:S(2)}) collective-permute-start(bf16[2,4,64,768]{3,2,1,0:T(8,128)(2,1)S(1)} %gradient.5), channel_id=1, source_target_pairs={{0,8},{8,0},{16,24},{24,16},{1,9},{9,1},{17,25},{25,17},{2,10},{10... | collective-permute-start | bytes 2359304 | tf_op jit(solution)/shard_map/ppermute | solution.py:470
  26.9 3.9 %collective-permute-start.11 = (bf16[128,128]{1,0:T(8,128)(2,1)S(1)}, bf16[128,128]{1,0:T(8,128)(2,1)S(1)}, u32[]{:S(2)}, u32[]{:S(2)}) collective-permute-start(bf16[128,128]{1,0:T(8,128)(2,1)S(1)} %convert_element_type.136), channel_id=1, source_target_pairs={{0,8},{8,0},{16,24},{24,16},{1,9},{9,1},{17,25},{25,17},{2,10},{10... | collective-permute-start | bytes 98312 | tf_op jit(solution)/shard_map/ppermute | solution.py:470
  28.3 11.9 %collective-permute-start.10 = (bf16[4,64,768]{2,1,0:T(8,128)(2,1)S(1)}, bf16[4,64,768]{2,1,0:T(8,128)(2,1)S(1)}, u32[]{:S(2)}, u32[]{:S(2)}) collective-permute-start(bf16[4,64,768]{2,1,0:T(8,128)(2,1)S(1)} %get-tuple-element.80), channel_id=1, source_target_pairs={{0,1},{1,0},{2,3},{3,2},{4,5},{5,4},{6,7},{7,6},{8,9},{9,8},{10,11... | collective-permute-start | bytes 1179656 | tf_op jit(solution)/shard_map/ppermute | solution.py:470
  29.9 10.9 %collective-permute-start.9 = (bf16[4,64,768]{2,1,0:T(8,128)(2,1)S(1)}, bf16[4,64,768]{2,1,0:T(8,128)(2,1)S(1)}, u32[]{:S(2)}, u32[]{:S(2)}) collective-permute-start(bf16[4,64,768]{2,1,0:T(8,128)(2,1)S(1)} %get-tuple-element.81), channel_id=1, source_target_pairs={{0,16},{8,24},{16,0},{24,8},{1,17},{9,25},{17,1},{25,9},{2,18},{10... | collective-permute-start | bytes 1179656 | tf_op jit(solution)/shard_map/ppermute | solution.py:470
  30.8 8.5 %collective-permute-start.12 = (bf16[128,128]{1,0:T(8,128)(2,1)S(1)}, bf16[128,128]{1,0:T(8,128)(2,1)S(1)}, u32[]{:S(2)}, u32[]{:S(2)}) collective-permute-start(bf16[128,128]{1,0:T(8,128)(2,1)S(1)} %fusion.7), channel_id=1, source_target_pairs={{0,2},{1,3},{2,0},{3,1},{4,6},{5,7},{6,4},{7,5},{8,10},{9,11},{10,... | collective-permute-start | bytes 98312 | tf_op jit(solution)/shard_map/ppermute | solution.py:470
  34.2 22.8 %copy-start.2 = (f32[1,64,768]{2,1,0:T(8,128)S(1)}, f32[1,64,768]{2,1,0:T(8,128)}, u32[]{:S(2)}) copy-start(f32[1,64,768]{2,1,0:T(8,128)} %refs_0_.3) | copy-start | bytes 589828
  34.2 22.8 %copy-start.4 = (f32[1,64,768]{2,1,0:T(8,128)S(1)}, f32[1,64,768]{2,1,0:T(8,128)}, u32[]{:S(2)}) copy-start(f32[1,64,768]{2,1,0:T(8,128)} %refs_1_.3) | copy-start | bytes 589828
  34.2 22.8 %copy-start.5 = (f32[1,64,768]{2,1,0:T(8,128)S(1)}, f32[1,64,768]{2,1,0:T(8,128)}, u32[]{:S(2)}) copy-start(f32[1,64,768]{2,1,0:T(8,128)} %refs_2_.3) | copy-start | bytes 589828
  41.0 5.9 %collective-permute-start.18 = (bf16[2,64,768]{2,1,0:T(8,128)(2,1)S(1)}, bf16[2,64,768]{2,1,0:T(8,128)(2,1)S(1)}, u32[]{:S(2)}, u32[]{:S(2)}) collective-permute-start(bf16[2,64,768]{2,1,0:T(8,128)(2,1)S(1)} %get-tuple-element.78), channel_id=1, source_target_pairs={{0,16},{8,24},{16,0},{24,8},{1,17},{9,25},{17,1},{25,9},{2,18},{10... | collective-permute-start | bytes 589832 | tf_op jit(solution)/shard_map/ppermute | solution.py:470
  41.9 10.6 %collective-permute-start.15 = (bf16[128,128]{1,0:T(8,128)(2,1)S(1)}, bf16[128,128]{1,0:T(8,128)(2,1)S(1)}, u32[]{:S(2)}, u32[]{:S(2)}) collective-permute-start(bf16[128,128]{1,0:T(8,128)(2,1)S(1)} %convert_element_type.151), channel_id=1, source_target_pairs={{0,1},{1,0},{2,3},{3,2},{4,5},{5,4},{6,7},{7,6},{8,9},{9,8},{10,11... | collective-permute-start | bytes 98312 | tf_op jit(solution)/shard_map/ppermute | solution.py:470
  44.0 6.7 %collective-permute-start.13 = (bf16[2,64,768]{2,1,0:T(8,128)(2,1)S(1)}, bf16[2,64,768]{2,1,0:T(8,128)(2,1)S(1)}, u32[]{:S(2)}, u32[]{:S(2)}) collective-permute-start(bf16[2,64,768]{2,1,0:T(8,128)(2,1)S(1)} %get-tuple-element.79), channel_id=1, source_target_pairs={{0,1},{1,0},{2,3},{3,2},{4,5},{5,4},{6,7},{7,6},{8,9},{9,8},{10,11... | collective-permute-start | bytes 589832 | tf_op jit(solution)/shard_map/ppermute | solution.py:470
  46.9 10.2 %collective-permute-start.19 = (bf16[64,768]{1,0:T(8,128)(2,1)S(1)}, bf16[64,768]{1,0:T(8,128)(2,1)S(1)}, u32[]{:S(2)}, u32[]{:S(2)}) collective-permute-start(bf16[64,768]{1,0:T(8,128)(2,1)S(1)} %fusion.4), channel_id=1, source_target_pairs={{0,2},{1,3},{2,0},{3,1},{4,6},{5,7},{6,4},{7,5},{8,10},{9,11},{10,... | collective-permute-start | bytes 294920 | tf_op jit(solution)/shard_map/ppermute | solution.py:470
  50.8 9.0 %collective-permute-start.14 = (bf16[64,768]{1,0:T(8,128)(2,1)S(1)}, bf16[64,768]{1,0:T(8,128)(2,1)S(1)}, u32[]{:S(2)}, u32[]{:S(2)}) collective-permute-start(bf16[64,768]{1,0:T(8,128)(2,1)S(1)} %fusion.5), channel_id=1, source_target_pairs={{0,2},{1,3},{2,0},{3,1},{4,6},{5,7},{6,4},{7,5},{8,10},{9,11},{10,... | collective-permute-start | bytes 294920 | tf_op jit(solution)/shard_map/ppermute | solution.py:470
  52.5 4.0 %collective-permute-start.16 = (bf16[128,128]{1,0:T(8,128)(2,1)S(1)}, bf16[128,128]{1,0:T(8,128)(2,1)S(1)}, u32[]{:S(2)}, u32[]{:S(2)}) collective-permute-start(bf16[128,128]{1,0:T(8,128)(2,1)S(1)} %get-tuple-element.76), channel_id=1, source_target_pairs={{0,16},{8,24},{16,0},{24,8},{1,17},{9,25},{17,1},{25,9},{2,18},{10... | collective-permute-start | bytes 98312 | tf_op jit(solution)/shard_map/ppermute | solution.py:470
  57.1 2.8 %copy-start.3 = (f32[1,64,768]{2,1,0:T(8,128)S(1)}, f32[1,64,768]{2,1,0:T(8,128)}, u32[]{:S(2)}) copy-start(f32[1,64,768]{2,1,0:T(8,128)} %refs_0_.2) | copy-start | bytes 589828
  57.1 2.8 %copy-start.6 = (f32[1,64,768]{2,1,0:T(8,128)S(1)}, f32[1,64,768]{2,1,0:T(8,128)}, u32[]{:S(2)}) copy-start(f32[1,64,768]{2,1,0:T(8,128)} %refs_1_.2) | copy-start | bytes 589828
  57.1 2.8 %copy-start.7 = (f32[1,64,768]{2,1,0:T(8,128)S(1)}, f32[1,64,768]{2,1,0:T(8,128)}, u32[]{:S(2)}) copy-start(f32[1,64,768]{2,1,0:T(8,128)} %refs_2_.2) | copy-start | bytes 589828
  58.3 7.7 %collective-permute-start.20 = (bf16[1,64,768]{2,1,0:T(8,128)(2,1)S(1)}, bf16[1,64,768]{2,1,0:T(8,128)(2,1)S(1)}, u32[]{:S(2)}, u32[]{:S(2)}) collective-permute-start(bf16[1,64,768]{2,1,0:T(8,128)(2,1)S(1)} %get-tuple-element.61), channel_id=1, source_target_pairs={{0,2},{1,3},{2,0},{3,1},{4,6},{5,7},{6,4},{7,5},{8,10},{9,11},{10,... | collective-permute-start | bytes 294920 | tf_op jit(solution)/shard_map/ppermute | solution.py:470
  61.1 6.0 %collective-permute-start.17 = (bf16[1,64,768]{2,1,0:T(8,128)(2,1)S(1)}, bf16[1,64,768]{2,1,0:T(8,128)(2,1)S(1)}, u32[]{:S(2)}, u32[]{:S(2)}) collective-permute-start(bf16[1,64,768]{2,1,0:T(8,128)(2,1)S(1)} %get-tuple-element.60), channel_id=1, source_target_pairs={{0,2},{1,3},{2,0},{3,1},{4,6},{5,7},{6,4},{7,5},{8,10},{9,11},{10,... | collective-permute-start | bytes 294920 | tf_op jit(solution)/shard_map/ppermute | solution.py:470
  62.5 7.9 %collective-permute-start.21 = (bf16[2,64,768]{2,1,0:T(8,128)(2,1)S(1)}, bf16[2,64,768]{2,1,0:T(8,128)(2,1)S(1)}, u32[]{:S(2)}, u32[]{:S(2)}) collective-permute-start(bf16[2,64,768]{2,1,0:T(8,128)(2,1)S(1)} %pad_maximum_fusion.6), channel_id=1, source_target_pairs={{4,0},{0,4},{5,1},{1,5},{6,2},{2,6},{7,3},{3,7},{12,8},{8,12},{13,... | collective-permute-start | bytes 589832 | tf_op jit(solution)/shard_map/ppermute | solution.py:480
  66.0 5.9 %collective-permute-start.25 = (bf16[2,64,768]{2,1,0:T(8,128)(2,1)S(1)}, bf16[2,64,768]{2,1,0:T(8,128)(2,1)S(1)}, u32[]{:S(2)}, u32[]{:S(2)}) collective-permute-start(bf16[2,64,768]{2,1,0:T(8,128)(2,1)S(1)} %pad_maximum_fusion.9), channel_id=1, source_target_pairs={{0,16},{8,24},{16,0},{24,8},{1,17},{9,25},{17,1},{25,9},{2,18},{10... | collective-permute-start | bytes 589832 | tf_op jit(solution)/shard_map/ppermute | solution.py:470
  67.1 7.5 %collective-permute-start.23 = (bf16[2,64,768]{2,1,0:T(8,128)(2,1)S(1)}, bf16[2,64,768]{2,1,0:T(8,128)(2,1)S(1)}, u32[]{:S(2)}, u32[]{:S(2)}) collective-permute-start(bf16[2,64,768]{2,1,0:T(8,128)(2,1)S(1)} %pad_maximum_fusion.8), channel_id=1, source_target_pairs={{0,1},{1,0},{2,3},{3,2},{4,5},{5,4},{6,7},{7,6},{8,9},{9,8},{10,11... | collective-permute-start | bytes 589832 | tf_op jit(solution)/shard_map/ppermute | solution.py:470
  70.5 8.4 %collective-permute-start.22 = (bf16[2,64,768]{2,1,0:T(8,128)(2,1)S(1)}, bf16[2,64,768]{2,1,0:T(8,128)(2,1)S(1)}, u32[]{:S(2)}, u32[]{:S(2)}) collective-permute-start(bf16[2,64,768]{2,1,0:T(8,128)(2,1)S(1)} %pad_maximum_fusion.7), channel_id=1, source_target_pairs={{4,0},{0,4},{5,1},{1,5},{6,2},{2,6},{7,3},{3,7},{12,8},{8,12},{13,... | collective-permute-start | bytes 589832 | tf_op jit(solution)/shard_map/ppermute | solution.py:480
  74.6 8.7 %collective-permute-start.27 = (bf16[4,64,768]{2,1,0:T(8,128)(2,1)S(1)}, bf16[4,64,768]{2,1,0:T(8,128)(2,1)S(1)}, u32[]{:S(2)}, u32[]{:S(2)}) collective-permute-start(bf16[4,64,768]{2,1,0:T(8,128)(2,1)S(1)} %get-tuple-element.88), channel_id=1, source_target_pairs={{4,0},{0,4},{5,1},{1,5},{6,2},{2,6},{7,3},{3,7},{12,8},{8,12},{13,... | collective-permute-start | bytes 1179656 | tf_op jit(solution)/shard_map/ppermute | solution.py:480
  74.7 8.6 %collective-permute-start.24 = (bf16[4,64,768]{2,1,0:T(8,128)(2,1)S(1)}, bf16[4,64,768]{2,1,0:T(8,128)(2,1)S(1)}, u32[]{:S(2)}, u32[]{:S(2)}) collective-permute-start(bf16[4,64,768]{2,1,0:T(8,128)(2,1)S(1)} %get-tuple-element.89), channel_id=1, source_target_pairs={{0,16},{8,24},{16,0},{24,8},{1,17},{9,25},{17,1},{25,9},{2,18},{10... | collective-permute-start | bytes 1179656 | tf_op jit(solution)/shard_map/ppermute | solution.py:470
  76.3 8.2 %collective-permute-start.26 = (bf16[4,64,768]{2,1,0:T(8,128)(2,1)S(1)}, bf16[4,64,768]{2,1,0:T(8,128)(2,1)S(1)}, u32[]{:S(2)}, u32[]{:S(2)}) collective-permute-start(bf16[4,64,768]{2,1,0:T(8,128)(2,1)S(1)} %get-tuple-element.90), channel_id=1, source_target_pairs={{0,1},{1,0},{2,3},{3,2},{4,5},{5,4},{6,7},{7,6},{8,9},{9,8},{10,11... | collective-permute-start | bytes 1179656 | tf_op jit(solution)/shard_map/ppermute | solution.py:470
  84.7 11.6 %collective-permute-start.32 = (bf16[16,64,768]{2,1,0:T(8,128)(2,1)S(1)}, bf16[16,64,768]{2,1,0:T(8,128)(2,1)S(1)}, u32[]{:S(2)}, u32[]{:S(2)}) collective-permute-start(bf16[16,64,768]{2,1,0:T(8,128)(2,1)S(1)} %constant_dynamic-update-slice_fusion.3.refs_0_), channel_id=1, source_target_pairs={{0,8},{8,0},{16,24},{24,16},{1,9},{9,1},{17,25},{25,17},{2,10},{10... | collective-permute-start | bytes 4718600 | tf_op jit(solution)/shard_map/ppermute | solution.py:470
  84.8 9.5 %collective-permute-start.28 = (bf16[3,64,768]{2,1,0:T(8,128)(2,1)S(1)}, bf16[3,64,768]{2,1,0:T(8,128)(2,1)S(1)}, u32[]{:S(2)}, u32[]{:S(2)}) collective-permute-start(bf16[3,64,768]{2,1,0:T(8,128)(2,1)S(1)} %pad_maximum_fusion.3), channel_id=1, source_target_pairs={{0,16},{8,24},{16,0},{24,8},{1,17},{9,25},{17,1},{25,9},{2,18},{10... | collective-permute-start | bytes 884744 | tf_op jit(solution)/shard_map/ppermute | solution.py:470
  85.3 9.5 %collective-permute-start.29 = (bf16[3,64,768]{2,1,0:T(8,128)(2,1)S(1)}, bf16[3,64,768]{2,1,0:T(8,128)(2,1)S(1)}, u32[]{:S(2)}, u32[]{:S(2)}) collective-permute-start(bf16[3,64,768]{2,1,0:T(8,128)(2,1)S(1)} %pad_maximum_fusion.4), channel_id=1, source_target_pairs={{0,1},{1,0},{2,3},{3,2},{4,5},{5,4},{6,7},{7,6},{8,9},{9,8},{10,11... | collective-permute-start | bytes 884744 | tf_op jit(solution)/shard_map/ppermute | solution.py:470
  87.5 8.6 %collective-permute-start.30 = (bf16[2,64,768]{2,1,0:T(8,128)(2,1)S(1)}, bf16[2,64,768]{2,1,0:T(8,128)(2,1)S(1)}, u32[]{:S(2)}, u32[]{:S(2)}) collective-permute-start(bf16[2,64,768]{2,1,0:T(8,128)(2,1)S(1)} %pad_maximum_fusion.10), channel_id=1, source_target_pairs={{4,0},{5,1},{6,2},{7,3},{12,8},{13,9},{14,10},{15,11},{20,16},{21,... | collective-permute-start | bytes 589832 | tf_op jit(solution)/shard_map/ppermute | solution.py:485
  88.8 7.4 %collective-permute-start.33 = (bf16[8,64,768]{2,1,0:T(8,128)(2,1)S(1)}, bf16[8,64,768]{2,1,0:T(8,128)(2,1)S(1)}, u32[]{:S(2)}, u32[]{:S(2)}) collective-permute-start(bf16[8,64,768]{2,1,0:T(8,128)(2,1)S(1)} %constant_dynamic-update-slice_fusion.11.refs_2_), channel_id=1, source_target_pairs={{0,8},{8,0},{16,24},{24,16},{1,9},{9,1},{17,25},{25,17},{2,10},{10... | collective-permute-start | bytes 2359304 | tf_op jit(solution)/shard_map/ppermute | solution.py:470
  96.1 2.4 %collective-permute-start.31 = (bf16[8,64,768]{2,1,0:T(8,128)(2,1)S(1)}, bf16[8,64,768]{2,1,0:T(8,128)(2,1)S(1)}, u32[]{:S(2)}, u32[]{:S(2)}) collective-permute-start(bf16[8,64,768]{2,1,0:T(8,128)(2,1)S(1)} %constant_dynamic-update-slice_fusion.refs_0_), channel_id=1, source_target_pairs={{0,8},{8,0},{16,24},{24,16},{1,9},{9,1},{17,25},{25,17},{2,10},{10... | collective-permute-start | bytes 2359304 | tf_op jit(solution)/shard_map/ppermute | solution.py:470
